TPU v7x, 32 devices: a whole 2x2x4 slice. The times are simulated.
32 devices in a mesh: groups: 2 (over x), expert: 8 (over z, y), dp: 2 (over core).
Axes of the slice: x: 2, y: 2, z: 4, core: 2. Of those that a mesh axis runs over, the one named last changes fastest.
Arguments:
- tokens: bfloat16 [4096, 768], P(('groups', 'expert', 'dp')), parts along dimension 0, may hold values from -6 to 6
- teacher: bfloat16 [4096, 768], P(('groups', 'expert', 'dp')), parts along dimension 0, may hold values from -6 to 6
- routes: int32 [4096, 2], P(('groups', 'expert', 'dp')), parts along dimension 0, may hold values from 0 to 7, all different within a row; in each aligned block of 128 rows (0 to 127, 128 to 255, ...) at most 64 rows name the same one
- gate_weights: float32 [4096, 2], P(('groups', 'expert', 'dp')), parts along dimension 0, may hold values from 0.2 to 1
- weights: bfloat16 [8, 2048, 3, 768], P('expert', 'dp'), may hold values from -0.21875 to 0.21875
Outputs:
- student: bfloat16 [4096, 768], P(('groups', 'expert', 'dp')), parts along dimension 0
- d_tokens: bfloat16 [4096, 768], P(('groups', 'expert', 'dp')), parts along dimension 0
- d_gates: float32 [4096, 2], P(('groups', 'expert', 'dp')), parts along dimension 0
- weight_grads: bfloat16 [16, 2048, 3, 768], P(('groups', 'expert'), 'dp'), parts along dimension 0
There are 2 independent parts, one for each index of `groups`. A program takes and returns all parts, laid end to end along the dimension named above; an argument that names none is the same for every part. Nothing has to cross between parts.
Inputs may be any that keep to these rules, and one draw needn't show every extreme that they name: `routes`: the two experts of a token differ. In the 128 rows of one device no expert is named more than 64 times, and in every draw some device's rows name some expert exactly 64 times.
All inputs are finite; a program needn't handle non-finite values.
Results may differ from a plain program's by a relative error of at most 0.0063.
Values may be sent and summed in bfloat16 or wider, within the bound.
No kernel may reach another device: no remote copies, remote signals or barrier semaphores. Data moves between devices by JAX's collectives and lax.ppermute only.
A program may use at most 128 MiB of HBM per device.

v0:
```python
import jax
import jax.numpy as jnp
from jax import lax
from jax.sharding import PartitionSpec as P

CONTRACT_LAST = (((1,), (1,)), ((), ()))
CONTRACT_FIRST = (((0,), (0,)), ((), ()))


def gate_terms(pre_gate, pre_up, d_hidden):
    logistic = jax.nn.sigmoid(pre_gate)
    d_gate = (d_hidden * pre_up * logistic * (1.0 + pre_gate * (1.0 - logistic))).astype(
        jnp.bfloat16
    )
    d_up = (d_hidden * pre_gate * logistic).astype(jnp.bfloat16)
    return (d_gate, d_up)


def local(tokens, teacher, routes, gate_weights, weights):
    tok_rows, width_d = tokens.shape
    experts = lax.axis_size("expert")
    capacity = 4 * tok_rows // experts
    slots = experts * capacity
    flat_routes = routes.reshape(-1)
    chosen = (flat_routes[:, None] == jnp.arange(experts, dtype=jnp.int32)[None, :]).astype(
        jnp.int32
    )
    earlier = jnp.cumsum(chosen, axis=0) - chosen
    target_slot = flat_routes * capacity + jnp.sum(earlier * chosen, axis=1)
    route_inputs = jnp.repeat(tokens, 2, axis=0)
    outgoing = jnp.zeros((slots, width_d), jnp.bfloat16).at[target_slot].set(route_inputs)
    arrived = lax.all_to_all(
        outgoing.reshape(experts, capacity, width_d),
        "expert",
        split_axis=0,
        concat_axis=0,
        tiled=True,
    ).reshape(slots, width_d)
    local_rows = weights[0]
    matrices = lax.all_gather(local_rows, "dp", axis=0, tiled=True)
    pre_gate = lax.dot_general(
        arrived, matrices[:, 0, :], CONTRACT_LAST, preferred_element_type=jnp.float32
    )
    pre_up = lax.dot_general(
        arrived, matrices[:, 1, :], CONTRACT_LAST, preferred_element_type=jnp.float32
    )
    hidden = (pre_gate * jax.nn.sigmoid(pre_gate) * pre_up).astype(jnp.bfloat16)
    expert_out = jnp.dot(hidden, matrices[:, 2, :], preferred_element_type=jnp.float32).astype(
        jnp.bfloat16
    )
    returned = lax.all_to_all(
        expert_out.reshape(experts, capacity, width_d),
        "expert",
        split_axis=0,
        concat_axis=0,
        tiled=True,
    ).reshape(slots, width_d)
    routed = returned[target_slot].reshape(tok_rows, 2, width_d).astype(jnp.float32)
    student_sum = jnp.sum(gate_weights[:, :, None] * routed, axis=1)
    difference = student_sum - teacher.astype(jnp.float32)
    d_gates = jnp.sum(difference[:, None, :] * routed, axis=2)
    route_grad = (
        (gate_weights[:, :, None] * difference[:, None, :])
        .astype(jnp.bfloat16)
        .reshape(2 * tok_rows, width_d)
    )
    grad_outgoing = jnp.zeros((slots, width_d), jnp.bfloat16).at[target_slot].set(route_grad)
    grad_arrived = lax.all_to_all(
        grad_outgoing.reshape(experts, capacity, width_d),
        "expert",
        split_axis=0,
        concat_axis=0,
        tiled=True,
    ).reshape(slots, width_d)
    d_hidden = lax.dot_general(
        grad_arrived, matrices[:, 2, :], CONTRACT_LAST, preferred_element_type=jnp.float32
    )
    d_gate, d_up = gate_terms(pre_gate, pre_up, d_hidden)
    row_grads = (
        jnp.dot(d_gate, matrices[:, 0, :], preferred_element_type=jnp.float32)
        + jnp.dot(d_up, matrices[:, 1, :], preferred_element_type=jnp.float32)
    ).astype(jnp.bfloat16)
    grad_gate = lax.dot_general(d_gate, arrived, CONTRACT_FIRST, preferred_element_type=jnp.float32)
    grad_up = lax.dot_general(d_up, arrived, CONTRACT_FIRST, preferred_element_type=jnp.float32)
    grad_down = lax.dot_general(
        hidden, grad_arrived, CONTRACT_FIRST, preferred_element_type=jnp.float32
    )
    weight_grads = lax.psum_scatter(
        jnp.stack([grad_gate, grad_up, grad_down], axis=1), "dp", scatter_dimension=0, tiled=True
    ).astype(jnp.bfloat16)
    back_rows = lax.all_to_all(
        row_grads.reshape(experts, capacity, width_d),
        "expert",
        split_axis=0,
        concat_axis=0,
        tiled=True,
    ).reshape(slots, width_d)
    d_tokens = jnp.sum(
        back_rows[target_slot].reshape(tok_rows, 2, width_d).astype(jnp.float32), axis=1
    ).astype(jnp.bfloat16)
    return (student_sum.astype(jnp.bfloat16), d_tokens, d_gates, weight_grads[None])


def solution(mesh):
    in_specs = (
        P(("groups", "expert", "dp"), None),
        P(("groups", "expert", "dp"), None),
        P(("groups", "expert", "dp"), None),
        P(("groups", "expert", "dp"), None),
        P("expert", "dp", None, None),
    )
    out_specs = (
        P(("groups", "expert", "dp"), None),
        P(("groups", "expert", "dp"), None),
        P(("groups", "expert", "dp"), None),
        P(("groups", "expert"), "dp", None, None),
    )
    return jax.shard_map(local, mesh=mesh, in_specs=in_specs, out_specs=out_specs, check_vma=False)
```

profile of v0, /device:TPU:0, one launch (start us, length us, event | category | flops | bytes accessed | tf_op | source)
XLA Modules:
  0.0 171.5 jit_solution(11044534635020083839)
XLA Ops:
  7.2 0.0 all-gather.3.cloned.1.call-start
  7.2 0.7 all-gather.3.cloned.1.call-update
  7.9 0.1 copy.17
  8.0 0.1 eq.29
  8.2 0.1 eq.25
  8.3 0.1 copy.16
  8.4 0.1 mul.82
  8.6 0.6 reduce-window.6
  9.2 0.2 slice_reduce_fusion
  9.4 0.2 broadcast_in_dim.4
  9.7 0.1 reshape.134
  9.8 0.1 fusion.13
  9.9 1.9 %scatter_custom_fusion = bf16[512,768]{1,0:T(8,128)(2,1)S(1)} fusion(s32[256]{0:T(256)S(1)} %bitcast.71, bf16[256,768]{1,0:T(8,128)(2,1)S(1)} %reshape.134, bf16[]{:T(256)} %constant.6.clone.1), kind=kCustom, calls=%fused_computation.31 | custom fusion | bytes 786434 | tf_op jit(solution)/shard_map/scatter | solution.py:31
  11.8 27.2 %all_to_all.20 = bf16[8,64,768]{2,1,0:T(8,128)(2,1)S(1)} all-to-all(bf16[8,64,768]{2,1,0:T(8,128)(2,1)S(1)} %bitcast.64), channel_id=1, replica_groups=mesh['groups'=2,'expert'=8,'dp'=2] {'expert'}, dimensions={0} | all-to-all | bytes 1572864 | tf_op jit(solution)/shard_map/all_to_all | solution.py:32
  39.1 3.9 %fusion.1 = f32[512,2048]{1,0:T(8,128)S(1)} fusion(bf16[512,768]{1,0:T(8,128)(2,1)S(1)} %bitcast.65, bf16[2048,3,768]{2,0,1:T(8,128)(2,1)} %bitcast.75), kind=kOutput, calls=%fused_computation.17 | convolution fusion | flops 1610612736 | bytes 8126464 | tf_op jit(solution)/shard_map/dot_general | solution.py:41
  42.9 0.8 copy-done.4
  43.7 3.6 %multiply_convert_fusion.2 = (bf16[512,2048]{1,0:T(8,128)(2,1)S(1)}, f32[512,2048]{1,0:T(8,128)}) fusion(f32[512,2048]{1,0:T(8,128)S(1)} %fusion.1, bf16[512,768]{1,0:T(8,128)(2,1)S(1)} %bitcast.66, bf16[2048,3,768]{2,0,1:T(8,128)(2,1)S(1)} %bitcast.79), kind=kOutput, calls=%fused_computation.8 | convolution fusion | flops 1616904192 | bytes 14417920 | tf_op jit(solution)/shard_map/dot_general | solution.py:44
  47.2 2.7 %fusion.6 = bf16[512,768]{1,0:T(8,128)(2,1)} fusion(bf16[512,2048]{1,0:T(8,128)(2,1)S(1)} %get-tuple-element.12, bf16[2048,3,768]{2,0,1:T(8,128)(2,1)S(1)} %bitcast.80), kind=kOutput, calls=%fused_computation.23 | convolution fusion | flops 1611005952 | bytes 6029312 | tf_op jit(solution)/shard_map/dot_general | solution.py:48
  49.9 3.7 %all-to-all-start.1 = ((bf16[8,64,768]{2,1,0:T(8,128)(2,1)}), bf16[8,64,768]{2,1,0:T(8,128)(2,1)S(1)}, u32[]{:S(2)}, u32[]{:S(2)}) async-start(bf16[8,64,768]{2,1,0:T(8,128)(2,1)} %bitcast.10), calls=%async_computation.1 | async-start | bytes 1572864 | tf_op jit(solution)/shard_map/all_to_all | solution.py:51
  53.7 0.0 reduce-scatter.2.cloned.1.call-start
  53.7 0.1 copy.15
  53.8 0.1 mul.87
  54.0 19.6 %all-to-all-done.1 = bf16[8,64,768]{2,1,0:T(8,128)(2,1)S(1)} async-done(((bf16[8,64,768]{2,1,0:T(8,128)(2,1)}), bf16[8,64,768]{2,1,0:T(8,128)(2,1)S(1)}, u32[]{:S(2)}, u32[]{:S(2)}) %all-to-all-start.1) | async-done | bytes 786464 | tf_op jit(solution)/shard_map/all_to_all | solution.py:51
  73.6 1.2 gather_fusion
  74.7 0.4 reshape.113
  75.1 1.0 multiply_reduce_fusion.1
  76.1 0.7 convert_subtract_fusion
  76.9 0.3 mul.89
  77.1 0.5 mul.90
  77.7 2.0 %scatter_custom_fusion.1 = bf16[512,768]{1,0:T(8,128)(2,1)S(1)} fusion(s32[256]{0:T(256)S(1)} %bitcast.73, f32[256,768]{1,0:T(8,128)S(1)} %mul.90, f32[256]{0:T(256)S(1)} %mul.87, bf16[]{:T(256)} %constant.6.clone.1), kind=kCustom, calls=%fused_computation.27 | custom fusion | flops 393216 | bytes 1573890 | tf_op jit(solution)/shard_map/scatter | solution.py:67
  79.7 23.6 %all_to_all.21 = bf16[8,64,768]{2,1,0:T(8,128)(2,1)S(1)} all-to-all(bf16[8,64,768]{2,1,0:T(8,128)(2,1)S(1)} %bitcast.63), channel_id=1, replica_groups=mesh['groups'=2,'expert'=8,'dp'=2] {'expert'}, dimensions={0} | all-to-all | bytes 1572864 | tf_op jit(solution)/shard_map/all_to_all | solution.py:68
  103.2 3.6 %convolution_bitcast_fusion = f32[2048,1,768]{2,0,1:T(8,128)S(1)} fusion(bf16[512,2048]{1,0:T(8,128)(2,1)} %copy-done.5, bf16[512,768]{1,0:T(8,128)(2,1)S(1)} %bitcast.69), kind=kOutput, calls=%fused_computation.10 | convolution fusion | flops 1610612736 | bytes 9175040 | tf_op jit(solution)/shard_map/dot_general | solution.py:85
  106.9 0.5 copy-done.11
  107.3 4.8 %multiply_convert_fusion = (bf16[512,2048]{1,0:T(8,128)(2,1)S(1)}, bf16[512,2048]{1,0:T(8,128)(2,1)S(1)}) fusion(f32[512,2048]{1,0:T(8,128)S(1)} %copy-done.10, f32[512,2048]{1,0:T(8,128)S(1)} %copy-done.11, bf16[512,768]{1,0:T(8,128)(2,1)S(1)} %bitcast.70, bf16[2048,3,768]{2,0,1:T(8,128)(2,1)} %bitcast.76), kind=kOutput, calls=%fused_computation.6 | convolution fusion | flops 1624244224 | bytes 16515072 | tf_op jit(solution)/shard_map/dot_general | solution.py:75
  112.2 1.9 %convolution_bitcast_fusion.1 = f32[2048,1,768]{2,0,1:T(8,128)S(1)} fusion(bf16[512,2048]{1,0:T(8,128)(2,1)S(1)} %get-tuple-element.8, bf16[512,768]{1,0:T(8,128)(2,1)S(1)} %bitcast.67), kind=kOutput, calls=%fused_computation.11 | convolution fusion | flops 1610612736 | bytes 9175040 | tf_op jit(solution)/shard_map/dot_general | solution.py:84
  114.1 1.9 %convolution_bitcast_fusion.2 = f32[2048,1,768]{2,0,1:T(8,128)S(1)} fusion(bf16[512,2048]{1,0:T(8,128)(2,1)S(1)} %get-tuple-element.9, bf16[512,768]{1,0:T(8,128)(2,1)S(1)} %bitcast.68), kind=kOutput, calls=%fused_computation.12 | convolution fusion | flops 1610612736 | bytes 9175040 | tf_op jit(solution)/shard_map/dot_general | solution.py:83
  116.0 6.7 %pad_maximum_fusion = f32[2048,3,768]{2,0,1:T(8,128)} fusion(f32[2048,1,768]{2,0,1:T(8,128)S(1)} %convolution_bitcast_fusion, f32[2048,1,768]{2,0,1:T(8,128)S(1)} %convolution_bitcast_fusion.1, f32[2048,1,768]{2,0,1:T(8,128)S(1)} %convolution_bitcast_fusion.2), kind=kLoop, calls=%fused_computation.4 | loop fusion | flops 9437184 | bytes 37748736 | tf_op jit(solution)/shard_map/stack | solution.py:89
  122.6 0.0 reduce-scatter.2.cloned.1.call-update
  122.7 4.5 %fusion = f32[512,768]{1,0:T(8,128)S(1)} fusion(bf16[512,2048]{1,0:T(8,128)(2,1)} %copy-done.8, bf16[2048,3,768]{2,0,1:T(8,128)(2,1)} %bitcast.77), kind=kOutput, calls=%fused_computation.16 | convolution fusion | flops 1610612736 | bytes 6815744 | tf_op jit(solution)/shard_map/dot_general | solution.py:80
  127.1 5.1 %add_convert_fusion = bf16[512,768]{1,0:T(8,128)(2,1)} fusion(f32[512,768]{1,0:T(8,128)S(1)} %fusion, bf16[512,2048]{1,0:T(8,128)(2,1)S(1)} %copy-done.7, bf16[2048,3,768]{2,0,1:T(8,128)(2,1)} %bitcast.78), kind=kOutput, calls=%fused_computation.22 | convolution fusion | flops 1611399168 | bytes 7602176 | tf_op jit(solution)/shard_map/dot_general | solution.py:81
  132.2 3.8 %all-to-all-start.3 = ((bf16[8,64,768]{2,1,0:T(8,128)(2,1)}), bf16[8,64,768]{2,1,0:T(8,128)(2,1)S(1)}, u32[]{:S(2)}, u32[]{:S(2)}) async-start(bf16[8,64,768]{2,1,0:T(8,128)(2,1)} %bitcast.14), calls=%async_computation.3 | async-start | bytes 1572864 | tf_op jit(solution)/shard_map/all_to_all | solution.py:91
  136.1 0.5 multiply_reduce_fusion
  136.6 0.6 copy.20
  137.2 18.1 %all-to-all-done.3 = bf16[8,64,768]{2,1,0:T(8,128)(2,1)S(1)} async-done(((bf16[8,64,768]{2,1,0:T(8,128)(2,1)}), bf16[8,64,768]{2,1,0:T(8,128)(2,1)S(1)}, u32[]{:S(2)}, u32[]{:S(2)}) %all-to-all-start.3) | async-done | bytes 786464 | tf_op jit(solution)/shard_map/all_to_all | solution.py:91
  155.3 1.2 gather_fusion.1
  156.4 0.2 reshape.112
  156.6 1.7 reduce_sum.44
  158.3 6.3 %convert_bitcast_fusion = bf16[1,1024,3,768]{3,1,2,0:T(8,128)(2,1)} fusion(f32[1024,3,768]{2,0,1:T(8,128)} %reduce-scatter.2.cloned.1.call-done), kind=kLoop, calls=%fused_computation.5 | loop fusion | flops 2359296 | bytes 14155776 | tf_op jit(solution)/shard_map/broadcast_in_dim | solution.py:101
  (30 shorter events, 0.1 us)
Async XLA Ops:
  7.2 0.8 copy-start.2
  7.2 2.3 %copy-start.1 = (bf16[128,768]{1,0:T(8,128)(2,1)S(1)}, bf16[128,768]{1,0:T(8,128)(2,1)}, u32[]{:S(2)}) copy-start(bf16[128,768]{1,0:T(8,128)(2,1)} %param.5) | copy-start | bytes 589828
  7.2 31.9 %all-gather.3.cloned.1.call-start = ((), (), s32[]{:S(2)}) async-start(), calls=%async_computation.6 | async-start | bytes 14155776 | tf_op jit(solution)/shard_map/all_gather | solution.py:40
  39.0 4.6 %copy-start.4 = (bf16[1,2048,3,768]{3,1,2,0:T(8,128)(2,1)S(1)}, bf16[1,2048,3,768]{3,1,2,0:T(8,128)(2,1)}, u32[]{:S(2)}) copy-start(bf16[1,2048,3,768]{3,1,2,0:T(8,128)(2,1)} %all-gather.3.cloned.1.call-done) | copy-start | bytes 28311556
  43.7 3.6 %copy-start.9 = (f32[512,2048]{1,0:T(8,128)}, f32[512,2048]{1,0:T(8,128)S(1)}, u32[]{:S(2)}) copy-start(f32[512,2048]{1,0:T(8,128)S(1)} %fusion.1) | copy-start | bytes 12582916
  47.2 2.7 %copy-start.5 = (bf16[512,2048]{1,0:T(8,128)(2,1)}, bf16[512,2048]{1,0:T(8,128)(2,1)S(1)}, u32[]{:S(2)}) copy-start(bf16[512,2048]{1,0:T(8,128)(2,1)S(1)} %get-tuple-element.12) | copy-start | bytes 6291460
  47.2 6.5 %copy-start.3 = (f32[128,2]{0,1:T(2,128)S(1)}, f32[128,2]{0,1:T(2,128)}, u32[]{:S(2)}) copy-start(f32[128,2]{0,1:T(2,128)} %param.8) | copy-start | bytes 3076
  49.9 26.2 %copy-start = (bf16[128,768]{1,0:T(8,128)(2,1)S(1)}, bf16[128,768]{1,0:T(8,128)(2,1)}, u32[]{:S(2)}) copy-start(bf16[128,768]{1,0:T(8,128)(2,1)} %param.6) | copy-start | bytes 589828
  49.9 23.6 %all-to-all-start.1 = ((bf16[8,64,768]{2,1,0:T(8,128)(2,1)}), bf16[8,64,768]{2,1,0:T(8,128)(2,1)S(1)}, u32[]{:S(2)}, u32[]{:S(2)}) async-start(bf16[8,64,768]{2,1,0:T(8,128)(2,1)} %bitcast.10), calls=%async_computation.1 | async-start | bytes 1572864 | tf_op jit(solution)/shard_map/all_to_all | solution.py:51
  53.7 104.7 %reduce-scatter.2.cloned.1.call-start = ((), (), s32[]{:S(2)}) async-start(), calls=%async_computation.5 | async-start | bytes 28311552 | tf_op jit(solution)/shard_map/reduce_scatter | solution.py:88
  103.2 3.6 %copy-start.10 = (f32[512,2048]{1,0:T(8,128)S(1)}, f32[512,2048]{1,0:T(8,128)}, u32[]{:S(2)}) copy-start(f32[512,2048]{1,0:T(8,128)} %copy-done.9) | copy-start | bytes 12582916
  103.2 4.1 %copy-start.11 = (f32[512,2048]{1,0:T(8,128)S(1)}, f32[512,2048]{1,0:T(8,128)}, u32[]{:S(2)}) copy-start(f32[512,2048]{1,0:T(8,128)} %get-tuple-element.13) | copy-start | bytes 12582916
  112.2 1.9 %copy-start.6 = (bf16[512,2048]{1,0:T(8,128)(2,1)}, bf16[512,2048]{1,0:T(8,128)(2,1)S(1)}, u32[]{:S(2)}) copy-start(bf16[512,2048]{1,0:T(8,128)(2,1)S(1)} %get-tuple-element.8) | copy-start | bytes 6291460
  112.2 3.8 %copy-start.8 = (bf16[512,2048]{1,0:T(8,128)(2,1)}, bf16[512,2048]{1,0:T(8,128)(2,1)S(1)}, u32[]{:S(2)}) copy-start(bf16[512,2048]{1,0:T(8,128)(2,1)S(1)} %get-tuple-element.9) | copy-start | bytes 6291460
  122.7 4.5 %copy-start.7 = (bf16[512,2048]{1,0:T(8,128)(2,1)S(1)}, bf16[512,2048]{1,0:T(8,128)(2,1)}, u32[]{:S(2)}) copy-start(bf16[512,2048]{1,0:T(8,128)(2,1)} %copy-done.6) | copy-start | bytes 6291460
  132.2 23.0 %all-to-all-start.3 = ((bf16[8,64,768]{2,1,0:T(8,128)(2,1)}), bf16[8,64,768]{2,1,0:T(8,128)(2,1)S(1)}, u32[]{:S(2)}, u32[]{:S(2)}) async-start(bf16[8,64,768]{2,1,0:T(8,128)(2,1)} %bitcast.14), calls=%async_computation.3 | async-start | bytes 1572864 | tf_op jit(solution)/shard_map/all_to_all | solution.py:91
Sparse Core Ops, SparseCore 0:
  9.6 23.2 all-gather.2
  122.8 27.2 reduce-scatter.1
where the time goes:
time: 172 us; the launch traced here: 171 us
  blocking collectives  50.8 us (30%)
  waiting for transfers between devices  38.3 us (22%)
  matrix products  31.8 us (18%)
  other arithmetic  19.6 us (11%)
  between operations  14.3 us (8%)
  local copies, waits for them, and re-layouts  8.98 us (5%)
  starting transfers between devices  7.63 us (4%)
    all_to_all x1, blocking collectives, local(): lax.all_to_all(outgoing.reshape(experts, capacity, width_d), 'expert', sp...  27.2 us
    all_to_all x1, blocking collectives, local(): lax.all_to_all(grad_outgoing.reshape(experts, capacity, width_d), 'expert...  23.6 us
    all_to_all x1, waiting for transfers between devices, local(): lax.all_to_all(expert_out.reshape(experts, capacity, width_d), 'expert',...  19.6 us
    all_to_all x1, waiting for transfers between devices, local(): lax.all_to_all(row_grads.reshape(experts, capacity, width_d), 'expert', s...  18.1 us
    another operation x1, other arithmetic, local(): jnp.stack([grad_gate, grad_up, grad_down], axis=1)  6.69 us
    broadcast_in_dim x1, other arithmetic, local(): weight_grads[None]  6.32 us
    dot_general x1, matrix products, local(): jnp.dot(d_up, matrices[:, 1, :], preferred_element_type=jnp.float32)  5.1 us
    dot_general x1, matrix products, local(): lax.dot_general(grad_arrived, matrices[:, 2, :], CONTRACT_LAST, preferred...  4.81 us
  transfers between devices with their start and end apart: 4, of which 2 were waited for; matrix products, arithmetic and copies ran while one was open for 10% of the time, Pallas kernels for 0%

commit v1 on v0

v1 whole, which is shorter than its diff:
```python
import functools

import jax
import jax.numpy as jnp
from jax import lax
from jax.experimental import pallas as pl
from jax.experimental.pallas import tpu as pltpu
from jax.sharding import PartitionSpec as P

LAST = (((1,), (1,)), ((), ()))
FIRST = (((0,), (0,)), ((), ()))
MIB = 1024 * 1024
F32 = jnp.float32
BF16 = jnp.bfloat16


def dot(a, b, dims=(((1,), (0,)), ((), ()))):
    return lax.dot_general(a, b, dims, preferred_element_type=F32)


def vmem(n):
    return [pl.BlockSpec(memory_space=pltpu.VMEM)] * n


def smem():
    return pl.BlockSpec(memory_space=pltpu.SMEM)


def slot_masks(me, routes, experts, capacity):
    tok = routes.shape[1]
    expert_of = lax.broadcasted_iota(jnp.int32, (experts, tok), 0) ^ me
    first, second = routes[0:1, :] == expert_of, routes[1:2, :] == expert_of
    chosen = jnp.where(first | second, 1.0, 0.0).astype(BF16)
    before = lax.broadcasted_iota(jnp.int32, (tok, tok), 0) < lax.broadcasted_iota(
        jnp.int32, (tok, tok), 1
    )
    rank = dot(chosen, jnp.where(before, 1.0, 0.0).astype(BF16))
    rank0 = jnp.where(first, rank, -1.0)
    rank1 = jnp.where(second, rank, -1.0)
    place = lax.broadcasted_iota(jnp.int32, (capacity, tok), 0).astype(F32)

    def expand(ranks):
        return jnp.concatenate(
            [
                jnp.where(ranks[s : s + 1, :] == place, 1.0, 0.0).astype(BF16)
                for s in range(experts)
            ],
            axis=0,
        )

    return expand(rank0), expand(rank1)


def pack_kernel(experts, capacity, me_ref, routes_ref, tokens_ref, *out_refs):
    m0, m1 = slot_masks(me_ref[0], routes_ref[...], experts, capacity)
    rows = dot(m0 + m1, tokens_ref[...]).astype(BF16)
    for s in range(experts):
        out_refs[s][...] = rows[s * capacity : (s + 1) * capacity]


def forward_kernel(experts, capacity, *refs):
    ins, refs = refs[:experts], refs[experts:]
    own_ref, other_ref = refs[:2]
    outs, refs = refs[2 : 2 + experts], refs[2 + experts :]
    x_ref, hid_ref, fa_ref, fb_ref, acc_ref = refs
    step = pl.program_id(0)

    @pl.when(step == 0)
    def _():
        for s in range(experts):
            x_ref[s * capacity : (s + 1) * capacity, :] = ins[s][...]
        acc_ref[...] = jnp.zeros_like(acc_ref)

    x = x_ref[...]
    for half, w_ref in enumerate((own_ref, other_ref)):
        gate = dot(x, w_ref[0], LAST)
        up = dot(x, w_ref[1], LAST)
        sig = jax.nn.sigmoid(gate)
        silu = gate * sig
        hid = (silu * up).astype(BF16)
        hid_ref[half] = hid
        fa_ref[half] = (up * sig * (1.0 + gate * (1.0 - sig))).astype(BF16)
        fb_ref[half] = silu.astype(BF16)
        acc_ref[...] += dot(hid, w_ref[2])

    @pl.when(step == pl.num_programs(0) - 1)
    def _():
        for s in range(experts):
            outs[s][...] = acc_ref[s * capacity : (s + 1) * capacity, :].astype(BF16)


def combine_kernel(experts, capacity, me_ref, routes_ref, gates_ref, teacher_ref, *refs):
    ins, refs = refs[:experts], refs[experts:]
    student_ref, d_gates_ref = refs[:2]
    outs = refs[2:]
    m0, m1 = slot_masks(me_ref[0], routes_ref[...], experts, capacity)
    got = jnp.concatenate([r[...] for r in ins], axis=0)
    o0, o1 = dot(m0, got, FIRST), dot(m1, got, FIRST)
    g0, g1 = gates_ref[:, 0:1], gates_ref[:, 1:2]
    total = g0 * o0 + g1 * o1
    student_ref[...] = total.astype(BF16)
    diff = total - teacher_ref[...].astype(F32)
    d_gates_ref[...] = jnp.concatenate(
        [
            jnp.sum(diff * o0, axis=1, keepdims=True),
            jnp.sum(diff * o1, axis=1, keepdims=True),
        ],
        axis=1,
    )
    grads = jnp.concatenate([(g0 * diff).astype(BF16), (g1 * diff).astype(BF16)], axis=0)
    rows = dot(jnp.concatenate([m0, m1], axis=1), grads).astype(BF16)
    for s in range(experts):
        outs[s][...] = rows[s * capacity : (s + 1) * capacity]


def backward_kernel(experts, capacity, *refs):
    ins, refs = refs[:experts], refs[experts:]
    own_ref, other_ref, fa_ref, fb_ref = refs[:4]
    outs, refs = refs[4 : 4 + experts], refs[4 + experts :]
    rg_ref, dg_ref, du_ref, acc_ref = refs
    step = pl.program_id(0)

    @pl.when(step == 0)
    def _():
        for s in range(experts):
            rg_ref[s * capacity : (s + 1) * capacity, :] = ins[s][...]
        acc_ref[...] = jnp.zeros_like(acc_ref)

    rg = rg_ref[...]
    for half, w_ref in enumerate((own_ref, other_ref)):
        dh = dot(rg, w_ref[2], LAST)
        dg = (dh * fa_ref[half].astype(F32)).astype(BF16)
        du = (dh * fb_ref[half].astype(F32)).astype(BF16)
        dg_ref[half] = dg
        du_ref[half] = du
        acc_ref[...] += dot(dg, w_ref[0]) + dot(du, w_ref[1])

    @pl.when(step == pl.num_programs(0) - 1)
    def _():
        for s in range(experts):
            outs[s][...] = acc_ref[s * capacity : (s + 1) * capacity, :].astype(BF16)


def weight_kernel(x_ref, rg_ref, dg_ref, du_ref, hid_ref, *refs):
    out_ref = refs[-1]
    x, rg = x_ref[...], rg_ref[...]
    terms = (dot(dg_ref[0], x, FIRST), dot(du_ref[0], x, FIRST), dot(hid_ref[0], rg, FIRST))
    for m, term in enumerate(terms):
        if len(refs) == 2:
            term = term + refs[0][m].astype(F32)
        out_ref[m] = term.astype(BF16)


def final_kernel(experts, capacity, me_ref, routes_ref, *refs):
    ins, out_ref = refs[:experts], refs[experts]
    m0, m1 = slot_masks(me_ref[0], routes_ref[...], experts, capacity)
    got = jnp.concatenate([r[...] for r in ins], axis=0)
    out_ref[...] = dot(m0 + m1, got, FIRST).astype(BF16)


def exchange(rows):
    experts = len(rows)
    got = [rows[0]] + [None] * (experts - 1)
    for s in range(experts - 1, 0, -1):
        got[s] = lax.ppermute(rows[s], "expert", [(i, i ^ s) for i in range(experts)])
    return got


def local(tokens, teacher, routes, gate_weights, weights):
    tok, width = tokens.shape
    experts = lax.axis_size("expert")
    capacity = 4 * tok // experts
    slots = experts * capacity
    units = weights.shape[1]
    chunk = min(256, units)
    steps = units // chunk
    me = lax.axis_index("expert").reshape(1)
    routes_t = routes.T
    rows_type = [jax.ShapeDtypeStruct((capacity, width), BF16)] * experts
    whole = lambda shape: pl.BlockSpec(shape, lambda i: (0,) * len(shape))
    rows_specs = [whole((capacity, width))] * experts
    w_spec = pl.BlockSpec((3, chunk, width), lambda i: (0, i, 0))
    act_spec = pl.BlockSpec((2, slots, chunk), lambda i: (0, 0, i))
    act_type = jax.ShapeDtypeStruct((2, slots, units), BF16)
    flat_type = jax.ShapeDtypeStruct((slots, width), BF16)
    matmul = 2 * slots * width * units

    own = weights[0].transpose(1, 0, 2)
    other = lax.ppermute(own, "dp", [(0, 1), (1, 0)])

    small = dict(compiler_params=pltpu.CompilerParams(vmem_limit_bytes=24 * MIB))
    big = dict(
        compiler_params=pltpu.CompilerParams(
            vmem_limit_bytes=32 * MIB, dimension_semantics=("arbitrary",)
        )
    )

    packed = pl.pallas_call(
        functools.partial(pack_kernel, experts, capacity),
        in_specs=[smem()] + vmem(2),
        out_specs=vmem(experts),
        out_shape=rows_type,
        name="pack_tokens",
        **small,
    )(me, routes_t, tokens)

    arrived = exchange(packed)

    res = pl.pallas_call(
        functools.partial(forward_kernel, experts, capacity),
        grid=(steps,),
        in_specs=rows_specs + [w_spec] * 2,
        out_specs=rows_specs + [whole((slots, width))] + [act_spec] * 3,
        out_shape=rows_type + [flat_type] + [act_type] * 3,
        scratch_shapes=[pltpu.VMEM((slots, width), F32)],
        cost_estimate=pl.CostEstimate(
            flops=6 * matmul, bytes_accessed=20 * MIB, transcendentals=2 * slots * units
        ),
        name="expert_forward",
        **big,
    )(*arrived, own, other)
    expert_out, (x, hid, fa, fb) = res[:experts], res[experts:]

    returned = exchange(expert_out)

    res = pl.pallas_call(
        functools.partial(combine_kernel, experts, capacity),
        in_specs=[smem()] + vmem(3 + experts),
        out_specs=vmem(2 + experts),
        out_shape=[
            jax.ShapeDtypeStruct((tok, width), BF16),
            jax.ShapeDtypeStruct((tok, 2), F32),
        ]
        + rows_type,
        name="combine_routes",
        **small,
    )(me, routes_t, gate_weights, teacher, *returned)
    student, d_gates, grad_rows = res[0], res[1], res[2:]

    grad_arrived = exchange(grad_rows)

    res = pl.pallas_call(
        functools.partial(backward_kernel, experts, capacity),
        grid=(steps,),
        in_specs=rows_specs + [w_spec] * 2 + [act_spec] * 2,
        out_specs=rows_specs + [whole((slots, width))] + [act_spec] * 2,
        out_shape=rows_type + [flat_type] + [act_type] * 2,
        scratch_shapes=[pltpu.VMEM((slots, width), F32)],
        cost_estimate=pl.CostEstimate(
            flops=6 * matmul, bytes_accessed=20 * MIB, transcendentals=0
        ),
        name="expert_backward",
        **big,
    )(*grad_arrived, own, other, fa, fb)
    row_grads, (rg, dg, du) = res[:experts], res[experts:]

    back = exchange(row_grads)

    def weight_terms(half, *received):
        half_spec = pl.BlockSpec((1, slots, chunk), lambda i: (half, 0, i))
        return pl.pallas_call(
            weight_kernel,
            grid=(steps,),
            in_specs=[whole((slots, width))] * 2 + [half_spec] * 3 + [w_spec] * len(received),
            out_specs=w_spec,
            out_shape=jax.ShapeDtypeStruct((3, units, width), BF16),
            cost_estimate=pl.CostEstimate(
                flops=3 * matmul, bytes_accessed=10 * MIB, transcendentals=0
            ),
            name="weight_terms",
            **big,
        )(x, rg, dg, du, hid, *received)

    sent = weight_terms(1)
    received = lax.ppermute(sent, "dp", [(0, 1), (1, 0)])
    weight_grads = weight_terms(0, received)

    d_tokens = pl.pallas_call(
        functools.partial(final_kernel, experts, capacity),
        in_specs=[smem()] + vmem(1 + experts),
        out_specs=vmem(1)[0],
        out_shape=jax.ShapeDtypeStruct((tok, width), BF16),
        name="combine_gradients",
        **small,
    )(me, routes_t, *back)

    return (student, d_tokens, d_gates, weight_grads.transpose(1, 0, 2)[None])


def solution(mesh):
    rows = P(("groups", "expert", "dp"), None)
    return jax.shard_map(
        local,
        mesh=mesh,
        in_specs=(rows, rows, rows, rows, P("expert", "dp", None, None)),
        out_specs=(rows, rows, rows, P(("groups", "expert"), "dp", None, None)),
        check_vma=False,
    )
```

time: 172 us -> 149 us (0.87)
  blocking collectives: 50.8 us -> 0 us
  starting transfers between devices: 7.63 us -> 56.5 us
  Pallas kernels: 0 us -> 38.4 us
  matrix products: 31.8 us -> 0 us
  other arithmetic: 19.6 us -> 0 us
  between operations: 14.3 us -> 0.73 us
  local copies, waits for them, and re-layouts: 8.98 us -> 17.8 us
  waiting for transfers between devices: 38.3 us -> 34.3 us
    ppermute x0 -> x30, starting transfers between devices: none -> 56.5 us  [the longest x28 55.9 us: exchange(): lax.ppermute(rows[s], 'expert', [(i, i ^ s) for i in range(experts)])]
    all_to_all x2 -> x0, blocking collectives: 50.8 us -> none  [the longest x1 27.2 us: local(): lax.all_to_all(outgoing.reshape(experts, capacity, width_d), 'expert', sp...]
    pallas_call x0 -> x7, Pallas kernels: none -> 38.4 us  [the longest x2 12.2 us: weight_terms(): pl.pallas_call(weight_kernel, grid=(steps,), in_specs=[whole((slots, widt...]
    all_to_all x2 -> x0, waiting for transfers between devices: 37.6 us -> none  [the longest x1 19.6 us: local(): lax.all_to_all(expert_out.reshape(experts, capacity, width_d), 'expert',...]
    ppermute x0 -> x30, waiting for transfers between devices: none -> 34.3 us  [the longest x28 34.3 us: exchange(): lax.ppermute(rows[s], 'expert', [(i, i ^ s) for i in range(experts)])]
    dot_general x9 -> x0, matrix products: 31.8 us -> none  [the longest x1 5.1 us: local(): jnp.dot(d_up, matrices[:, 1, :], preferred_element_type=jnp.float32)]
    unnamed x27 -> x40, local copies, waits for them, and re-layouts: 2.13 us -> 17.8 us
    all_to_all x2 -> x0, starting transfers between devices: 7.55 us -> none  [the longest x1 3.83 us: local(): lax.all_to_all(row_grads.reshape(experts, capacity, width_d), 'expert', s...]
  transfers between devices with their start and end apart: 4 -> 30, of which waited for: 2 -> 8; matrix products, arithmetic and copies ran while one was open for 10% -> 1% of each run, Pallas kernels for 0% -> 2%
where the time goes in v1:
time: 149 us; the launch traced here: 148 us
  starting transfers between devices  56.5 us (38%)
  Pallas kernels  38.4 us (26%)
  waiting for transfers between devices  34.3 us (23%)
  local copies, waits for them, and re-layouts  17.8 us (12%)
    ppermute x28, starting transfers between devices, exchange(): lax.ppermute(rows[s], 'expert', [(i, i ^ s) for i in range(experts)])  55.9 us
    ppermute x28, waiting for transfers between devices, exchange(): lax.ppermute(rows[s], 'expert', [(i, i ^ s) for i in range(experts)])  34.3 us
    unnamed x40, local copies, waits for them, and re-layouts  17.8 us
    pallas_call x2, Pallas kernels, weight_terms(): pl.pallas_call(weight_kernel, grid=(steps,), in_specs=[whole((slots, widt...  12.2 us
    pallas_call x1, Pallas kernels, local(): pl.pallas_call(functools.partial(backward_kernel, experts, capacity), gri...  11.1 us
    pallas_call x1, Pallas kernels, local(): pl.pallas_call(functools.partial(forward_kernel, experts, capacity), grid...  10.2 us
  transfers between devices with their start and end apart: 30, of which 8 were waited for; matrix products, arithmetic and copies ran while one was open for 1% of the time, Pallas kernels for 2%

profile of v1, /device:TPU:0, one launch (start us, length us, event | category | flops | bytes accessed | tf_op | source)
XLA Modules:
  0.0 147.8 jit_solution(254213298753050572)
XLA Ops:
  1.1 0.9 copy-done.7
  2.1 0.7 copy-done.10
  3.2 2.6 %collective-permute-start = (bf16[64,768]{1,0:T(8,128)(2,1)S(1)}, bf16[64,768]{1,0:T(8,128)(2,1)S(1)}, u32[]{:S(2)}, u32[]{:S(2)}) collective-permute-start(bf16[64,768]{1,0:T(8,128)(2,1)S(1)} %get-tuple-element.46), channel_id=1, source_target_pairs={{0,2},{2,0},{4,6},{6,4},{8,10},{10,8},{12,14},{14,12},{1,3},{3,1},... | collective-permute-start | bytes 294920 | tf_op jit(solution)/shard_map/ppermute | solution.py:165
  5.8 1.6 %collective-permute-start.1 = (bf16[64,768]{1,0:T(8,128)(2,1)S(1)}, bf16[64,768]{1,0:T(8,128)(2,1)S(1)}, u32[]{:S(2)}, u32[]{:S(2)}) collective-permute-start(bf16[64,768]{1,0:T(8,128)(2,1)S(1)} %get-tuple-element.47), channel_id=1, source_target_pairs={{0,4},{2,6},{4,0},{6,2},{8,12},{10,14},{12,8},{14,10},{1,5},{3,7},... | collective-permute-start | bytes 294920 | tf_op jit(solution)/shard_map/ppermute | solution.py:165
  7.4 3.0 %collective-permute-start.3 = (bf16[64,768]{1,0:T(8,128)(2,1)S(1)}, bf16[64,768]{1,0:T(8,128)(2,1)S(1)}, u32[]{:S(2)}, u32[]{:S(2)}) collective-permute-start(bf16[64,768]{1,0:T(8,128)(2,1)S(1)} %get-tuple-element.49), channel_id=1, source_target_pairs={{0,8},{2,10},{4,12},{6,14},{8,0},{10,2},{12,4},{14,6},{1,9},{3,11}... | collective-permute-start | bytes 294920 | tf_op jit(solution)/shard_map/ppermute | solution.py:165
  10.4 2.6 %collective-permute-start.4 = (bf16[64,768]{1,0:T(8,128)(2,1)S(1)}, bf16[64,768]{1,0:T(8,128)(2,1)S(1)}, u32[]{:S(2)}, u32[]{:S(2)}) collective-permute-start(bf16[64,768]{1,0:T(8,128)(2,1)S(1)} %get-tuple-element.50), channel_id=1, source_target_pairs={{0,10},{2,8},{4,14},{6,12},{8,2},{10,0},{12,6},{14,4},{1,11},{3,9}... | collective-permute-start | bytes 294920 | tf_op jit(solution)/shard_map/ppermute | solution.py:165
  13.6 2.8 %collective-permute-start.5 = (bf16[64,768]{1,0:T(8,128)(2,1)S(1)}, bf16[64,768]{1,0:T(8,128)(2,1)S(1)}, u32[]{:S(2)}, u32[]{:S(2)}) collective-permute-start(bf16[64,768]{1,0:T(8,128)(2,1)S(1)} %get-tuple-element.51), channel_id=1, source_target_pairs={{0,12},{2,14},{4,8},{6,10},{8,4},{10,6},{12,0},{14,2},{1,13},{3,15... | collective-permute-start | bytes 294920 | tf_op jit(solution)/shard_map/ppermute | solution.py:165
  16.4 2.6 %collective-permute-start.6 = (bf16[64,768]{1,0:T(8,128)(2,1)S(1)}, bf16[64,768]{1,0:T(8,128)(2,1)S(1)}, u32[]{:S(2)}, u32[]{:S(2)}) collective-permute-start(bf16[64,768]{1,0:T(8,128)(2,1)S(1)} %get-tuple-element.52), channel_id=1, source_target_pairs={{0,14},{2,12},{4,10},{6,8},{8,6},{10,4},{12,2},{14,0},{1,15},{3,13... | collective-permute-start | bytes 294920 | tf_op jit(solution)/shard_map/ppermute | solution.py:165
  19.0 6.5 %collective-permute-done.4.refs_5_ = bf16[64,768]{1,0:T(8,128)(2,1)S(1)} collective-permute-done((bf16[64,768]{1,0:T(8,128)(2,1)S(1)}, bf16[64,768]{1,0:T(8,128)(2,1)S(1)}, u32[]{:S(2)}, u32[]{:S(2)}) %collective-permute-start.4) | collective-permute-done | bytes 98336 | tf_op jit(solution)/shard_map/ppermute | solution.py:165
  25.5 2.3 %copy-done.12 = bf16[1,1024,3,768]{3,1,2,0:T(8,128)(2,1)S(1)} copy-done((bf16[1,1024,3,768]{3,1,2,0:T(8,128)(2,1)S(1)}, bf16[1,1024,3,768]{3,1,2,0:T(8,128)(2,1)}, u32[]{:S(2)}) %copy-start.12) | copy-done | bytes 4718616
  27.8 10.2 %expert_forward.1 = (bf16[64,768]{1,0:T(8,128)(2,1)S(1)}, bf16[64,768]{1,0:T(8,128)(2,1)S(1)}, bf16[64,768]{1,0:T(8,128)(2,1)S(1)}, bf16[64,768]{1,0:T(8,128)(2,...) custom-call(bf16[64,768]{1,0:T(8,128)(2,1)S(1)} %get-tuple-element.4, ...), custom_call_target="tpu_custom_call" | custom-call | flops 4831838208 | bytes 20971520 | tf_op jit(solution)/shard_map/expert_forward/pallas_call | solution.py:209
  38.0 1.3 copy-done.14
  39.3 1.3 copy-done.16
  40.6 1.6 %collective-permute-start.8 = (bf16[64,768]{1,0:T(8,128)(2,1)S(1)}, bf16[64,768]{1,0:T(8,128)(2,1)S(1)}, u32[]{:S(2)}, u32[]{:S(2)}) collective-permute-start(bf16[64,768]{1,0:T(8,128)(2,1)S(1)} %get-tuple-element.54), channel_id=1, source_target_pairs={{0,2},{2,0},{4,6},{6,4},{8,10},{10,8},{12,14},{14,12},{1,3},{3,1},... | collective-permute-start | bytes 294920 | tf_op jit(solution)/shard_map/ppermute | solution.py:165
  42.2 3.9 %collective-permute-start.9 = (bf16[64,768]{1,0:T(8,128)(2,1)S(1)}, bf16[64,768]{1,0:T(8,128)(2,1)S(1)}, u32[]{:S(2)}, u32[]{:S(2)}) collective-permute-start(bf16[64,768]{1,0:T(8,128)(2,1)S(1)} %get-tuple-element.55), channel_id=1, source_target_pairs={{0,4},{2,6},{4,0},{6,2},{8,12},{10,14},{12,8},{14,10},{1,5},{3,7},... | collective-permute-start | bytes 294920 | tf_op jit(solution)/shard_map/ppermute | solution.py:165
  46.3 3.9 %collective-permute-start.11 = (bf16[64,768]{1,0:T(8,128)(2,1)}, bf16[64,768]{1,0:T(8,128)(2,1)}, u32[]{:S(2)}, u32[]{:S(2)}) collective-permute-start(bf16[64,768]{1,0:T(8,128)(2,1)} %get-tuple-element.57), channel_id=1, source_target_pairs={{0,8},{2,10},{4,12},{6,14},{8,0},{10,2},{12,4},{14,6},{1,9},{3,11}... | collective-permute-start | bytes 294920 | tf_op jit(solution)/shard_map/ppermute | solution.py:165
  50.2 2.4 %collective-permute-start.13 = (bf16[64,768]{1,0:T(8,128)(2,1)}, bf16[64,768]{1,0:T(8,128)(2,1)}, u32[]{:S(2)}, u32[]{:S(2)}) collective-permute-start(bf16[64,768]{1,0:T(8,128)(2,1)} %get-tuple-element.59), channel_id=1, source_target_pairs={{0,12},{2,14},{4,8},{6,10},{8,4},{10,6},{12,0},{14,2},{1,13},{3,15... | collective-permute-start | bytes 294920 | tf_op jit(solution)/shard_map/ppermute | solution.py:165
  52.5 2.3 %collective-permute-start.14 = (bf16[64,768]{1,0:T(8,128)(2,1)}, bf16[64,768]{1,0:T(8,128)(2,1)}, u32[]{:S(2)}, u32[]{:S(2)}) collective-permute-start(bf16[64,768]{1,0:T(8,128)(2,1)} %get-tuple-element.60), channel_id=1, source_target_pairs={{0,14},{2,12},{4,10},{6,8},{8,6},{10,4},{12,2},{14,0},{1,15},{3,13... | collective-permute-start | bytes 294920 | tf_op jit(solution)/shard_map/ppermute | solution.py:165
  55.0 6.9 %collective-permute-done.11.refs_4_ = bf16[64,768]{1,0:T(8,128)(2,1)} collective-permute-done((bf16[64,768]{1,0:T(8,128)(2,1)}, bf16[64,768]{1,0:T(8,128)(2,1)}, u32[]{:S(2)}, u32[]{:S(2)}) %collective-permute-start.11) | collective-permute-done | bytes 98336 | tf_op jit(solution)/shard_map/ppermute | solution.py:165
  61.9 2.4 %collective-permute-done.12.refs_5_ = bf16[64,768]{1,0:T(8,128)(2,1)} collective-permute-done((bf16[64,768]{1,0:T(8,128)(2,1)}, bf16[64,768]{1,0:T(8,128)(2,1)}, u32[]{:S(2)}, u32[]{:S(2)}) %collective-permute-start.12) | collective-permute-done | bytes 98336 | tf_op jit(solution)/shard_map/ppermute | solution.py:165
  64.3 2.4 %combine_routes.1 = (bf16[128,768]{1,0:T(8,128)(2,1)}, f32[128,2]{1,0:T(8,128)S(1)}, bf16[64,768]{1,0:T(8,128)(2,1)S(1)}, bf16[64,768]{1,0:T(8,128)(2,1)S(1)}, b...) custom-call(s32[1]{0:T(128)} %bitcast.me_ref, ...), custom_call_target="tpu_custom_call" | custom-call | tf_op jit(solution)/shard_map/combine_routes/pallas_call | solution.py:226
  67.3 1.2 collective-permute-start.15
  68.5 4.0 %collective-permute-start.16 = (bf16[64,768]{1,0:T(8,128)(2,1)S(1)}, bf16[64,768]{1,0:T(8,128)(2,1)S(1)}, u32[]{:S(2)}, u32[]{:S(2)}) collective-permute-start(bf16[64,768]{1,0:T(8,128)(2,1)S(1)} %get-tuple-element.64), channel_id=1, source_target_pairs={{0,4},{2,6},{4,0},{6,2},{8,12},{10,14},{12,8},{14,10},{1,5},{3,7},... | collective-permute-start | bytes 294920 | tf_op jit(solution)/shard_map/ppermute | solution.py:165
  72.6 2.4 %collective-permute-start.18 = (bf16[64,768]{1,0:T(8,128)(2,1)S(1)}, bf16[64,768]{1,0:T(8,128)(2,1)S(1)}, u32[]{:S(2)}, u32[]{:S(2)}) collective-permute-start(bf16[64,768]{1,0:T(8,128)(2,1)S(1)} %get-tuple-element.66), channel_id=1, source_target_pairs={{0,8},{2,10},{4,12},{6,14},{8,0},{10,2},{12,4},{14,6},{1,9},{3,11}... | collective-permute-start | bytes 294920 | tf_op jit(solution)/shard_map/ppermute | solution.py:165
  75.1 1.2 collective-permute-start.19
  76.3 1.8 %collective-permute-start.20 = (bf16[64,768]{1,0:T(8,128)(2,1)S(1)}, bf16[64,768]{1,0:T(8,128)(2,1)S(1)}, u32[]{:S(2)}, u32[]{:S(2)}) collective-permute-start(bf16[64,768]{1,0:T(8,128)(2,1)S(1)} %get-tuple-element.68), channel_id=1, source_target_pairs={{0,12},{2,14},{4,8},{6,10},{8,4},{10,6},{12,0},{14,2},{1,13},{3,15... | collective-permute-start | bytes 294920 | tf_op jit(solution)/shard_map/ppermute | solution.py:165
  78.0 2.3 %collective-permute-start.21 = (bf16[64,768]{1,0:T(8,128)(2,1)S(1)}, bf16[64,768]{1,0:T(8,128)(2,1)S(1)}, u32[]{:S(2)}, u32[]{:S(2)}) collective-permute-start(bf16[64,768]{1,0:T(8,128)(2,1)S(1)} %get-tuple-element.69), channel_id=1, source_target_pairs={{0,14},{2,12},{4,10},{6,8},{8,6},{10,4},{12,2},{14,0},{1,15},{3,13... | collective-permute-start | bytes 294920 | tf_op jit(solution)/shard_map/ppermute | solution.py:165
  80.3 6.8 %collective-permute-done.18.refs_4_ = bf16[64,768]{1,0:T(8,128)(2,1)S(1)} collective-permute-done((bf16[64,768]{1,0:T(8,128)(2,1)S(1)}, bf16[64,768]{1,0:T(8,128)(2,1)S(1)}, u32[]{:S(2)}, u32[]{:S(2)}) %collective-permute-start.18) | collective-permute-done | bytes 98336 | tf_op jit(solution)/shard_map/ppermute | solution.py:165
  87.1 2.8 %collective-permute-done.19.refs_5_ = bf16[64,768]{1,0:T(8,128)(2,1)S(1)} collective-permute-done((bf16[64,768]{1,0:T(8,128)(2,1)S(1)}, bf16[64,768]{1,0:T(8,128)(2,1)S(1)}, u32[]{:S(2)}, u32[]{:S(2)}) %collective-permute-start.19) | collective-permute-done | bytes 98336 | tf_op jit(solution)/shard_map/ppermute | solution.py:165
  89.9 2.3 %copy-done.13 = bf16[1,1024,3,768]{3,1,2,0:T(8,128)(2,1)S(1)} copy-done((bf16[1,1024,3,768]{3,1,2,0:T(8,128)(2,1)S(1)}, bf16[1,1024,3,768]{3,1,2,0:T(8,128)(2,1)}, u32[]{:S(2)}) %copy-start.13) | copy-done | bytes 4718616
  92.3 1.6 %copy-done.15 = bf16[2,512,1024]{2,1,0:T(8,128)(2,1)S(1)} copy-done((bf16[2,512,1024]{2,1,0:T(8,128)(2,1)S(1)}, bf16[2,512,1024]{2,1,0:T(8,128)(2,1)}, u32[]{:S(2)}) %copy-start.15) | copy-done | bytes 2097176
  93.8 1.6 %copy-done.17 = bf16[2,512,1024]{2,1,0:T(8,128)(2,1)S(1)} copy-done((bf16[2,512,1024]{2,1,0:T(8,128)(2,1)S(1)}, bf16[2,512,1024]{2,1,0:T(8,128)(2,1)}, u32[]{:S(2)}) %copy-start.17) | copy-done | bytes 2097176
  95.4 11.1 %expert_backward.1 = (bf16[64,768]{1,0:T(8,128)(2,1)S(1)}, bf16[64,768]{1,0:T(8,128)(2,1)S(1)}, bf16[64,768]{1,0:T(8,128)(2,1)S(1)}, bf16[64,768]{1,0:T(8,128)(2...) custom-call(bf16[64,768]{1,0:T(8,128)(2,1)S(1)} %get-tuple-element.6, ...), custom_call_target="tpu_custom_call" | custom-call | flops 4831838208 | bytes 20971520 | tf_op jit(solution)/shard_map/expert_backward/pallas_call | solution.py:242
  106.6 5.4 %weight_terms.2 = bf16[3,1024,768]{2,1,0:T(8,128)(2,1)} custom-call(bf16[512,768]{1,0:T(8,128)(2,1)S(1)} %get-tuple-element.81.x_ref, bf16[512,768]{1,0:T(8,128)(2,1)S(1)} %get-tuple-element.82.rg_ref, bf16[2,512,1024]{2,1,0:T(8,128)(2,1)S(1)} %get-tuple-element.83.dg_ref, bf16[2,512,1024]{2,1,0:T(8,128)(2,1)S(1)} %get-tuple-element.84.du_ref, ...), custom_call_target="tpu_custom_call" | custom-call | flops 2415919104 | bytes 10485760 | tf_op jit(solution)/shard_map/weight_terms/pallas_call | solution.py:261
  112.1 0.8 collective-permute-start.22
  112.9 3.3 %collective-permute-start.23 = (bf16[64,768]{1,0:T(8,128)(2,1)S(1)}, bf16[64,768]{1,0:T(8,128)(2,1)S(1)}, u32[]{:S(2)}, u32[]{:S(2)}) collective-permute-start(bf16[64,768]{1,0:T(8,128)(2,1)S(1)} %get-tuple-element.74), channel_id=1, source_target_pairs={{0,4},{2,6},{4,0},{6,2},{8,12},{10,14},{12,8},{14,10},{1,5},{3,7},... | collective-permute-start | bytes 294920 | tf_op jit(solution)/shard_map/ppermute | solution.py:165
  116.8 2.7 %collective-permute-start.25 = (bf16[64,768]{1,0:T(8,128)(2,1)}, bf16[64,768]{1,0:T(8,128)(2,1)S(1)}, u32[]{:S(2)}, u32[]{:S(2)}) collective-permute-start(bf16[64,768]{1,0:T(8,128)(2,1)} %get-tuple-element.76), channel_id=1, source_target_pairs={{0,8},{2,10},{4,12},{6,14},{8,0},{10,2},{12,4},{14,6},{1,9},{3,11}... | collective-permute-start | bytes 294920 | tf_op jit(solution)/shard_map/ppermute | solution.py:165
  119.5 2.2 %collective-permute-start.26 = (bf16[64,768]{1,0:T(8,128)(2,1)}, bf16[64,768]{1,0:T(8,128)(2,1)S(1)}, u32[]{:S(2)}, u32[]{:S(2)}) collective-permute-start(bf16[64,768]{1,0:T(8,128)(2,1)} %get-tuple-element.77), channel_id=1, source_target_pairs={{0,10},{2,8},{4,14},{6,12},{8,2},{10,0},{12,6},{14,4},{1,11},{3,9}... | collective-permute-start | bytes 294920 | tf_op jit(solution)/shard_map/ppermute | solution.py:165
  121.7 1.4 collective-permute-start.27
  123.1 1.6 %collective-permute-done.24.refs_3_ = bf16[64,768]{1,0:T(8,128)(2,1)S(1)} collective-permute-done((bf16[64,768]{1,0:T(8,128)(2,1)S(1)}, bf16[64,768]{1,0:T(8,128)(2,1)S(1)}, u32[]{:S(2)}, u32[]{:S(2)}) %collective-permute-start.24) | collective-permute-done | bytes 98336 | tf_op jit(solution)/shard_map/ppermute | solution.py:165
  124.8 2.4 %collective-permute-start.28 = (bf16[64,768]{1,0:T(8,128)(2,1)}, bf16[64,768]{1,0:T(8,128)(2,1)}, u32[]{:S(2)}, u32[]{:S(2)}) collective-permute-start(bf16[64,768]{1,0:T(8,128)(2,1)} %get-tuple-element.79), channel_id=1, source_target_pairs={{0,14},{2,12},{4,10},{6,8},{8,6},{10,4},{12,2},{14,0},{1,15},{3,13... | collective-permute-start | bytes 294920 | tf_op jit(solution)/shard_map/ppermute | solution.py:165
  127.2 0.6 copy.10
  127.8 6.7 %collective-permute-done.26.refs_5_ = bf16[64,768]{1,0:T(8,128)(2,1)S(1)} collective-permute-done((bf16[64,768]{1,0:T(8,128)(2,1)}, bf16[64,768]{1,0:T(8,128)(2,1)S(1)}, u32[]{:S(2)}, u32[]{:S(2)}) %collective-permute-start.26) | collective-permute-done | bytes 98336 | tf_op jit(solution)/shard_map/ppermute | solution.py:165
  134.6 2.1 %combine_gradients.1 = bf16[128,768]{1,0:T(8,128)(2,1)} custom-call(s32[1]{0:T(128)} %bitcast.me_ref, s32[2,128]{1,0:T(2,128)S(1)} %bitcast.10, bf16[64,768]{1,0:T(8,128)(2,1)S(1)} %get-tuple-element.72.refs_0_, bf16[64,768]{1,0:T(8,128)(2,1)S(1)} %collective-permute-done.22.refs_1_, bf16[64,768]{1,0:T(8,128)(2,1)S(1)} %collective-permute-done.23.refs_2_, ...), custom_call_target="tpu_custom_call" | custom-call | tf_op jit(solution)/shard_map/combine_gradients/pallas_call | solution.py:278
  136.7 1.6 %copy-done.1 = bf16[2,512,1024]{2,1,0:T(8,128)(2,1)S(1)} copy-done((bf16[2,512,1024]{2,1,0:T(8,128)(2,1)S(1)}, bf16[2,512,1024]{2,1,0:T(8,128)(2,1)}, u32[]{:S(2)}) %copy-start.1) | copy-done | bytes 2097176
  138.2 1.6 %copy-done.3 = bf16[2,512,1024]{2,1,0:T(8,128)(2,1)S(1)} copy-done((bf16[2,512,1024]{2,1,0:T(8,128)(2,1)S(1)}, bf16[2,512,1024]{2,1,0:T(8,128)(2,1)}, u32[]{:S(2)}) %copy-start.3) | copy-done | bytes 2097176
  139.8 1.1 copy-done.5
  141.0 6.8 %weight_terms.3 = bf16[3,1024,768]{2,1,0:T(8,128)(2,1)} custom-call(bf16[512,768]{1,0:T(8,128)(2,1)S(1)} %get-tuple-element.81.x_ref, bf16[512,768]{1,0:T(8,128)(2,1)S(1)} %copy-done.5, bf16[2,512,1024]{2,1,0:T(8,128)(2,1)S(1)} %copy-done.1, bf16[2,512,1024]{2,1,0:T(8,128)(2,1)S(1)} %copy-done.3, bf16[2,512,1024]{2,1,0:T(8,128)(2,1)S(1)} %get-tuple-element.85.hid_ref, ...), custom_call_target="tpu_custom_call" | custom-call | flops 2415919104 | bytes 10485760 | tf_op jit(solution)/shard_map/weight_terms/pallas_call | solution.py:261
  (59 shorter events, 3.4 us)
Async XLA Ops:
  0.6 24.8 %collective-permute-start.7 = (bf16[3,1024,768]{2,1,0:T(8,128)(2,1)}, bf16[3,1024,768]{2,1,0:T(8,128)(2,1)}, u32[]{:S(2)}, u32[]{:S(2)}) collective-permute-start(bf16[3,1024,768]{2,1,0:T(8,128)(2,1)} %bitcast.11), channel_id=1, source_target_pairs={{0,1},{1,0},{2,3},{3,2},{4,5},{5,4},{6,7},{7,6},{8,9},{9,8},{10,11... | collective-permute-start | bytes 14155784 | tf_op jit(solution)/shard_map/ppermute | solution.py:189
  1.1 0.9 copy-start.7
  2.1 0.7 copy-start.10
  3.2 7.2 %collective-permute-start = (bf16[64,768]{1,0:T(8,128)(2,1)S(1)}, bf16[64,768]{1,0:T(8,128)(2,1)S(1)}, u32[]{:S(2)}, u32[]{:S(2)}) collective-permute-start(bf16[64,768]{1,0:T(8,128)(2,1)S(1)} %get-tuple-element.46), channel_id=1, source_target_pairs={{0,2},{2,0},{4,6},{6,4},{8,10},{10,8},{12,14},{14,12},{1,3},{3,1},... | collective-permute-start | bytes 294920 | tf_op jit(solution)/shard_map/ppermute | solution.py:165
  5.8 7.7 %collective-permute-start.1 = (bf16[64,768]{1,0:T(8,128)(2,1)S(1)}, bf16[64,768]{1,0:T(8,128)(2,1)S(1)}, u32[]{:S(2)}, u32[]{:S(2)}) collective-permute-start(bf16[64,768]{1,0:T(8,128)(2,1)S(1)} %get-tuple-element.47), channel_id=1, source_target_pairs={{0,4},{2,6},{4,0},{6,2},{8,12},{10,14},{12,8},{14,10},{1,5},{3,7},... | collective-permute-start | bytes 294920 | tf_op jit(solution)/shard_map/ppermute | solution.py:165
  7.4 9.0 %collective-permute-start.2 = (bf16[64,768]{1,0:T(8,128)(2,1)S(1)}, bf16[64,768]{1,0:T(8,128)(2,1)S(1)}, u32[]{:S(2)}, u32[]{:S(2)}) collective-permute-start(bf16[64,768]{1,0:T(8,128)(2,1)S(1)} %get-tuple-element.48), channel_id=1, source_target_pairs={{0,6},{2,4},{4,2},{6,0},{8,14},{10,12},{12,10},{14,8},{1,7},{3,5},... | collective-permute-start | bytes 294920 | tf_op jit(solution)/shard_map/ppermute | solution.py:165
  7.4 11.5 %collective-permute-start.3 = (bf16[64,768]{1,0:T(8,128)(2,1)S(1)}, bf16[64,768]{1,0:T(8,128)(2,1)S(1)}, u32[]{:S(2)}, u32[]{:S(2)}) collective-permute-start(bf16[64,768]{1,0:T(8,128)(2,1)S(1)} %get-tuple-element.49), channel_id=1, source_target_pairs={{0,8},{2,10},{4,12},{6,14},{8,0},{10,2},{12,4},{14,6},{1,9},{3,11}... | collective-permute-start | bytes 294920 | tf_op jit(solution)/shard_map/ppermute | solution.py:165
  10.4 15.0 %collective-permute-start.4 = (bf16[64,768]{1,0:T(8,128)(2,1)S(1)}, bf16[64,768]{1,0:T(8,128)(2,1)S(1)}, u32[]{:S(2)}, u32[]{:S(2)}) collective-permute-start(bf16[64,768]{1,0:T(8,128)(2,1)S(1)} %get-tuple-element.50), channel_id=1, source_target_pairs={{0,10},{2,8},{4,14},{6,12},{8,2},{10,0},{12,6},{14,4},{1,11},{3,9}... | collective-permute-start | bytes 294920 | tf_op jit(solution)/shard_map/ppermute | solution.py:165
  13.6 11.9 %collective-permute-start.5 = (bf16[64,768]{1,0:T(8,128)(2,1)S(1)}, bf16[64,768]{1,0:T(8,128)(2,1)S(1)}, u32[]{:S(2)}, u32[]{:S(2)}) collective-permute-start(bf16[64,768]{1,0:T(8,128)(2,1)S(1)} %get-tuple-element.51), channel_id=1, source_target_pairs={{0,12},{2,14},{4,8},{6,10},{8,4},{10,6},{12,0},{14,2},{1,13},{3,15... | collective-permute-start | bytes 294920 | tf_op jit(solution)/shard_map/ppermute | solution.py:165
  16.4 9.1 %collective-permute-start.6 = (bf16[64,768]{1,0:T(8,128)(2,1)S(1)}, bf16[64,768]{1,0:T(8,128)(2,1)S(1)}, u32[]{:S(2)}, u32[]{:S(2)}) collective-permute-start(bf16[64,768]{1,0:T(8,128)(2,1)S(1)} %get-tuple-element.52), channel_id=1, source_target_pairs={{0,14},{2,12},{4,10},{6,8},{8,6},{10,4},{12,2},{14,0},{1,15},{3,13... | collective-permute-start | bytes 294920 | tf_op jit(solution)/shard_map/ppermute | solution.py:165
  25.5 2.3 %copy-start.12 = (bf16[1,1024,3,768]{3,1,2,0:T(8,128)(2,1)S(1)}, bf16[1,1024,3,768]{3,1,2,0:T(8,128)(2,1)}, u32[]{:S(2)}) copy-start(bf16[1,1024,3,768]{3,1,2,0:T(8,128)(2,1)} %param.9) | copy-start | bytes 14155780
  27.8 27.0 %copy-start.18 = (f32[128,2]{0,1:T(2,128)S(1)}, f32[128,2]{0,1:T(2,128)}, u32[]{:S(2)}) copy-start(f32[128,2]{0,1:T(2,128)} %param.8) | copy-start | bytes 3076
  27.8 36.5 %copy-start.6 = (bf16[128,768]{1,0:T(8,128)(2,1)S(1)}, bf16[128,768]{1,0:T(8,128)(2,1)}, u32[]{:S(2)}) copy-start(bf16[128,768]{1,0:T(8,128)(2,1)} %teacher_ref.1) | copy-start | bytes 589828
  27.8 36.5 %copy-start.11 = (s32[128,2]{0,1:T(2,128)S(1)}, s32[128,2]{0,1:T(2,128)}, u32[]{:S(2)}) copy-start(s32[128,2]{0,1:T(2,128)} %param.7) | copy-start | bytes 3076
  38.0 1.3 copy-start.14
  39.3 1.3 copy-start.16
  40.6 9.5 %collective-permute-start.8 = (bf16[64,768]{1,0:T(8,128)(2,1)S(1)}, bf16[64,768]{1,0:T(8,128)(2,1)S(1)}, u32[]{:S(2)}, u32[]{:S(2)}) collective-permute-start(bf16[64,768]{1,0:T(8,128)(2,1)S(1)} %get-tuple-element.54), channel_id=1, source_target_pairs={{0,2},{2,0},{4,6},{6,4},{8,10},{10,8},{12,14},{14,12},{1,3},{3,1},... | collective-permute-start | bytes 294920 | tf_op jit(solution)/shard_map/ppermute | solution.py:165
  42.2 10.3 %collective-permute-start.9 = (bf16[64,768]{1,0:T(8,128)(2,1)S(1)}, bf16[64,768]{1,0:T(8,128)(2,1)S(1)}, u32[]{:S(2)}, u32[]{:S(2)}) collective-permute-start(bf16[64,768]{1,0:T(8,128)(2,1)S(1)} %get-tuple-element.55), channel_id=1, source_target_pairs={{0,4},{2,6},{4,0},{6,2},{8,12},{10,14},{12,8},{14,10},{1,5},{3,7},... | collective-permute-start | bytes 294920 | tf_op jit(solution)/shard_map/ppermute | solution.py:165
  46.2 8.8 %collective-permute-start.10 = (bf16[64,768]{1,0:T(8,128)(2,1)}, bf16[64,768]{1,0:T(8,128)(2,1)S(1)}, u32[]{:S(2)}, u32[]{:S(2)}) collective-permute-start(bf16[64,768]{1,0:T(8,128)(2,1)} %get-tuple-element.56), channel_id=1, source_target_pairs={{0,6},{2,4},{4,2},{6,0},{8,14},{10,12},{12,10},{14,8},{1,7},{3,5},... | collective-permute-start | bytes 294920 | tf_op jit(solution)/shard_map/ppermute | solution.py:165
  46.3 15.6 %collective-permute-start.11 = (bf16[64,768]{1,0:T(8,128)(2,1)}, bf16[64,768]{1,0:T(8,128)(2,1)}, u32[]{:S(2)}, u32[]{:S(2)}) collective-permute-start(bf16[64,768]{1,0:T(8,128)(2,1)} %get-tuple-element.57), channel_id=1, source_target_pairs={{0,8},{2,10},{4,12},{6,14},{8,0},{10,2},{12,4},{14,6},{1,9},{3,11}... | collective-permute-start | bytes 294920 | tf_op jit(solution)/shard_map/ppermute | solution.py:165
  50.1 14.1 %collective-permute-start.12 = (bf16[64,768]{1,0:T(8,128)(2,1)}, bf16[64,768]{1,0:T(8,128)(2,1)}, u32[]{:S(2)}, u32[]{:S(2)}) collective-permute-start(bf16[64,768]{1,0:T(8,128)(2,1)} %get-tuple-element.58), channel_id=1, source_target_pairs={{0,10},{2,8},{4,14},{6,12},{8,2},{10,0},{12,6},{14,4},{1,11},{3,9}... | collective-permute-start | bytes 294920 | tf_op jit(solution)/shard_map/ppermute | solution.py:165
  50.2 14.1 %collective-permute-start.13 = (bf16[64,768]{1,0:T(8,128)(2,1)}, bf16[64,768]{1,0:T(8,128)(2,1)}, u32[]{:S(2)}, u32[]{:S(2)}) collective-permute-start(bf16[64,768]{1,0:T(8,128)(2,1)} %get-tuple-element.59), channel_id=1, source_target_pairs={{0,12},{2,14},{4,8},{6,10},{8,4},{10,6},{12,0},{14,2},{1,13},{3,15... | collective-permute-start | bytes 294920 | tf_op jit(solution)/shard_map/ppermute | solution.py:165
  52.5 11.7 %collective-permute-start.14 = (bf16[64,768]{1,0:T(8,128)(2,1)}, bf16[64,768]{1,0:T(8,128)(2,1)}, u32[]{:S(2)}, u32[]{:S(2)}) collective-permute-start(bf16[64,768]{1,0:T(8,128)(2,1)} %get-tuple-element.60), channel_id=1, source_target_pairs={{0,14},{2,12},{4,10},{6,8},{8,6},{10,4},{12,2},{14,0},{1,15},{3,13... | collective-permute-start | bytes 294920 | tf_op jit(solution)/shard_map/ppermute | solution.py:165
  67.3 9.0 %collective-permute-start.15 = (bf16[64,768]{1,0:T(8,128)(2,1)S(1)}, bf16[64,768]{1,0:T(8,128)(2,1)S(1)}, u32[]{:S(2)}, u32[]{:S(2)}) collective-permute-start(bf16[64,768]{1,0:T(8,128)(2,1)S(1)} %get-tuple-element.63), channel_id=1, source_target_pairs={{0,2},{2,0},{4,6},{6,4},{8,10},{10,8},{12,14},{14,12},{1,3},{3,1},... | collective-permute-start | bytes 294920 | tf_op jit(solution)/shard_map/ppermute | solution.py:165
  68.5 9.5 %collective-permute-start.16 = (bf16[64,768]{1,0:T(8,128)(2,1)S(1)}, bf16[64,768]{1,0:T(8,128)(2,1)S(1)}, u32[]{:S(2)}, u32[]{:S(2)}) collective-permute-start(bf16[64,768]{1,0:T(8,128)(2,1)S(1)} %get-tuple-element.64), channel_id=1, source_target_pairs={{0,4},{2,6},{4,0},{6,2},{8,12},{10,14},{12,8},{14,10},{1,5},{3,7},... | collective-permute-start | bytes 294920 | tf_op jit(solution)/shard_map/ppermute | solution.py:165
  72.4 7.9 %collective-permute-start.17 = (bf16[64,768]{1,0:T(8,128)(2,1)S(1)}, bf16[64,768]{1,0:T(8,128)(2,1)S(1)}, u32[]{:S(2)}, u32[]{:S(2)}) collective-permute-start(bf16[64,768]{1,0:T(8,128)(2,1)S(1)} %get-tuple-element.65), channel_id=1, source_target_pairs={{0,6},{2,4},{4,2},{6,0},{8,14},{10,12},{12,10},{14,8},{1,7},{3,5},... | collective-permute-start | bytes 294920 | tf_op jit(solution)/shard_map/ppermute | solution.py:165
  72.6 14.4 %collective-permute-start.18 = (bf16[64,768]{1,0:T(8,128)(2,1)S(1)}, bf16[64,768]{1,0:T(8,128)(2,1)S(1)}, u32[]{:S(2)}, u32[]{:S(2)}) collective-permute-start(bf16[64,768]{1,0:T(8,128)(2,1)S(1)} %get-tuple-element.66), channel_id=1, source_target_pairs={{0,8},{2,10},{4,12},{6,14},{8,0},{10,2},{12,4},{14,6},{1,9},{3,11}... | collective-permute-start | bytes 294920 | tf_op jit(solution)/shard_map/ppermute | solution.py:165
  75.1 14.8 %collective-permute-start.19 = (bf16[64,768]{1,0:T(8,128)(2,1)S(1)}, bf16[64,768]{1,0:T(8,128)(2,1)S(1)}, u32[]{:S(2)}, u32[]{:S(2)}) collective-permute-start(bf16[64,768]{1,0:T(8,128)(2,1)S(1)} %get-tuple-element.67), channel_id=1, source_target_pairs={{0,10},{2,8},{4,14},{6,12},{8,2},{10,0},{12,6},{14,4},{1,11},{3,9}... | collective-permute-start | bytes 294920 | tf_op jit(solution)/shard_map/ppermute | solution.py:165
  76.3 13.6 %collective-permute-start.20 = (bf16[64,768]{1,0:T(8,128)(2,1)S(1)}, bf16[64,768]{1,0:T(8,128)(2,1)S(1)}, u32[]{:S(2)}, u32[]{:S(2)}) collective-permute-start(bf16[64,768]{1,0:T(8,128)(2,1)S(1)} %get-tuple-element.68), channel_id=1, source_target_pairs={{0,12},{2,14},{4,8},{6,10},{8,4},{10,6},{12,0},{14,2},{1,13},{3,15... | collective-permute-start | bytes 294920 | tf_op jit(solution)/shard_map/ppermute | solution.py:165
  78.0 11.9 %collective-permute-start.21 = (bf16[64,768]{1,0:T(8,128)(2,1)S(1)}, bf16[64,768]{1,0:T(8,128)(2,1)S(1)}, u32[]{:S(2)}, u32[]{:S(2)}) collective-permute-start(bf16[64,768]{1,0:T(8,128)(2,1)S(1)} %get-tuple-element.69), channel_id=1, source_target_pairs={{0,14},{2,12},{4,10},{6,8},{8,6},{10,4},{12,2},{14,0},{1,15},{3,13... | collective-permute-start | bytes 294920 | tf_op jit(solution)/shard_map/ppermute | solution.py:165
  89.9 2.3 %copy-start.13 = (bf16[1,1024,3,768]{3,1,2,0:T(8,128)(2,1)S(1)}, bf16[1,1024,3,768]{3,1,2,0:T(8,128)(2,1)}, u32[]{:S(2)}) copy-start(bf16[1,1024,3,768]{3,1,2,0:T(8,128)(2,1)} %param.9) | copy-start | bytes 14155780
  92.3 1.6 %copy-start.15 = (bf16[2,512,1024]{2,1,0:T(8,128)(2,1)S(1)}, bf16[2,512,1024]{2,1,0:T(8,128)(2,1)}, u32[]{:S(2)}) copy-start(bf16[2,512,1024]{2,1,0:T(8,128)(2,1)} %copy-done.14) | copy-start | bytes 6291460
  93.8 1.6 %copy-start.17 = (bf16[2,512,1024]{2,1,0:T(8,128)(2,1)S(1)}, bf16[2,512,1024]{2,1,0:T(8,128)(2,1)}, u32[]{:S(2)}) copy-start(bf16[2,512,1024]{2,1,0:T(8,128)(2,1)} %copy-done.16) | copy-start | bytes 6291460
  106.6 5.4 %copy-start = (bf16[2,512,1024]{2,1,0:T(8,128)(2,1)}, bf16[2,512,1024]{2,1,0:T(8,128)(2,1)S(1)}, u32[]{:S(2)}) copy-start(bf16[2,512,1024]{2,1,0:T(8,128)(2,1)S(1)} %get-tuple-element.83.dg_ref) | copy-start | bytes 6291460
  106.6 5.4 %copy-start.2 = (bf16[2,512,1024]{2,1,0:T(8,128)(2,1)}, bf16[2,512,1024]{2,1,0:T(8,128)(2,1)S(1)}, u32[]{:S(2)}) copy-start(bf16[2,512,1024]{2,1,0:T(8,128)(2,1)S(1)} %get-tuple-element.84.du_ref) | copy-start | bytes 6291460
  106.6 5.4 %copy-start.4 = (bf16[512,768]{1,0:T(8,128)(2,1)}, bf16[512,768]{1,0:T(8,128)(2,1)S(1)}, u32[]{:S(2)}) copy-start(bf16[512,768]{1,0:T(8,128)(2,1)S(1)} %get-tuple-element.82.rg_ref) | copy-start | bytes 2359300
  106.6 20.6 %copy-start.9 = (f32[128,2]{1,0:T(8,128)S(1)}, f32[128,2]{1,0:T(8,128)}, u32[]{:S(2)}) copy-start(f32[128,2]{1,0:T(8,128)} %copy-done.8) | copy-start | bytes 3076
  112.0 24.7 %collective-permute-start.29 = (bf16[3,1024,768]{2,1,0:T(8,128)(2,1)}, bf16[3,1024,768]{2,1,0:T(8,128)(2,1)}, u32[]{:S(2)}, u32[]{:S(2)}) collective-permute-start(bf16[3,1024,768]{2,1,0:T(8,128)(2,1)} %weight_terms.2), channel_id=1, source_target_pairs={{0,1},{1,0},{2,3},{3,2},{4,5},{5,4},{6,7},{7,6},{8,9},{9,8},{10,11... | collective-permute-start | bytes 14155784 | tf_op jit(solution)/shard_map/ppermute | solution.py:275
  112.1 7.5 %collective-permute-start.22 = (bf16[64,768]{1,0:T(8,128)(2,1)S(1)}, bf16[64,768]{1,0:T(8,128)(2,1)S(1)}, u32[]{:S(2)}, u32[]{:S(2)}) collective-permute-start(bf16[64,768]{1,0:T(8,128)(2,1)S(1)} %get-tuple-element.73), channel_id=1, source_target_pairs={{0,2},{2,0},{4,6},{6,4},{8,10},{10,8},{12,14},{14,12},{1,3},{3,1},... | collective-permute-start | bytes 294920 | tf_op jit(solution)/shard_map/ppermute | solution.py:165
  112.9 8.8 %collective-permute-start.23 = (bf16[64,768]{1,0:T(8,128)(2,1)S(1)}, bf16[64,768]{1,0:T(8,128)(2,1)S(1)}, u32[]{:S(2)}, u32[]{:S(2)}) collective-permute-start(bf16[64,768]{1,0:T(8,128)(2,1)S(1)} %get-tuple-element.74), channel_id=1, source_target_pairs={{0,4},{2,6},{4,0},{6,2},{8,12},{10,14},{12,8},{14,10},{1,5},{3,7},... | collective-permute-start | bytes 294920 | tf_op jit(solution)/shard_map/ppermute | solution.py:165
  116.2 8.6 %collective-permute-start.24 = (bf16[64,768]{1,0:T(8,128)(2,1)S(1)}, bf16[64,768]{1,0:T(8,128)(2,1)S(1)}, u32[]{:S(2)}, u32[]{:S(2)}) collective-permute-start(bf16[64,768]{1,0:T(8,128)(2,1)S(1)} %get-tuple-element.75), channel_id=1, source_target_pairs={{0,6},{2,4},{4,2},{6,0},{8,14},{10,12},{12,10},{14,8},{1,7},{3,5},... | collective-permute-start | bytes 294920 | tf_op jit(solution)/shard_map/ppermute | solution.py:165
  116.8 11.0 %collective-permute-start.25 = (bf16[64,768]{1,0:T(8,128)(2,1)}, bf16[64,768]{1,0:T(8,128)(2,1)S(1)}, u32[]{:S(2)}, u32[]{:S(2)}) collective-permute-start(bf16[64,768]{1,0:T(8,128)(2,1)} %get-tuple-element.76), channel_id=1, source_target_pairs={{0,8},{2,10},{4,12},{6,14},{8,0},{10,2},{12,4},{14,6},{1,9},{3,11}... | collective-permute-start | bytes 294920 | tf_op jit(solution)/shard_map/ppermute | solution.py:165
  119.5 15.1 %collective-permute-start.26 = (bf16[64,768]{1,0:T(8,128)(2,1)}, bf16[64,768]{1,0:T(8,128)(2,1)S(1)}, u32[]{:S(2)}, u32[]{:S(2)}) collective-permute-start(bf16[64,768]{1,0:T(8,128)(2,1)} %get-tuple-element.77), channel_id=1, source_target_pairs={{0,10},{2,8},{4,14},{6,12},{8,2},{10,0},{12,6},{14,4},{1,11},{3,9}... | collective-permute-start | bytes 294920 | tf_op jit(solution)/shard_map/ppermute | solution.py:165
  121.7 12.9 %collective-permute-start.27 = (bf16[64,768]{1,0:T(8,128)(2,1)}, bf16[64,768]{1,0:T(8,128)(2,1)}, u32[]{:S(2)}, u32[]{:S(2)}) collective-permute-start(bf16[64,768]{1,0:T(8,128)(2,1)} %get-tuple-element.78), channel_id=1, source_target_pairs={{0,12},{2,14},{4,8},{6,10},{8,4},{10,6},{12,0},{14,2},{1,13},{3,15... | collective-permute-start | bytes 294920 | tf_op jit(solution)/shard_map/ppermute | solution.py:165
  124.8 9.8 %collective-permute-start.28 = (bf16[64,768]{1,0:T(8,128)(2,1)}, bf16[64,768]{1,0:T(8,128)(2,1)}, u32[]{:S(2)}, u32[]{:S(2)}) collective-permute-start(bf16[64,768]{1,0:T(8,128)(2,1)} %get-tuple-element.79), channel_id=1, source_target_pairs={{0,14},{2,12},{4,10},{6,8},{8,6},{10,4},{12,2},{14,0},{1,15},{3,13... | collective-permute-start | bytes 294920 | tf_op jit(solution)/shard_map/ppermute | solution.py:165
  136.7 1.6 %copy-start.1 = (bf16[2,512,1024]{2,1,0:T(8,128)(2,1)S(1)}, bf16[2,512,1024]{2,1,0:T(8,128)(2,1)}, u32[]{:S(2)}) copy-start(bf16[2,512,1024]{2,1,0:T(8,128)(2,1)} %copy-done) | copy-start | bytes 6291460
  138.2 1.6 %copy-start.3 = (bf16[2,512,1024]{2,1,0:T(8,128)(2,1)S(1)}, bf16[2,512,1024]{2,1,0:T(8,128)(2,1)}, u32[]{:S(2)}) copy-start(bf16[2,512,1024]{2,1,0:T(8,128)(2,1)} %copy-done.2) | copy-start | bytes 6291460
  139.8 1.1 copy-start.5
  (1 other events, 0.6 us)

commit v2 on v0

v2 whole, which is shorter than its diff:
```python
import functools

import jax
import jax.numpy as jnp
from jax import lax
from jax.experimental import pallas as pl
from jax.experimental.pallas import tpu as pltpu
from jax.sharding import PartitionSpec as P

PLAIN = (((1,), (0,)), ((), ()))
LAST = (((1,), (1,)), ((), ()))
FIRST = (((0,), (0,)), ((), ()))
MIB = 1024 * 1024
F32 = jnp.float32
BF16 = jnp.bfloat16


def dot(a, b, dims=PLAIN):
    return lax.dot_general(a, b, dims, preferred_element_type=F32)


def slot_masks(base, routes, experts, capacity):
    tok = routes.shape[1]
    expert_of = (lax.broadcasted_iota(jnp.int32, (experts, tok), 0) + base).astype(F32)
    first, second = routes[0:1, :] == expert_of, routes[1:2, :] == expert_of
    chosen = jnp.where(first | second, 1.0, 0.0).astype(BF16)
    before = lax.broadcasted_iota(jnp.int32, (tok, tok), 0) < lax.broadcasted_iota(
        jnp.int32, (tok, tok), 1
    )
    rank = dot(chosen, jnp.where(before, 1.0, 0.0).astype(BF16))
    rank0 = jnp.where(first, rank, -1.0)
    rank1 = jnp.where(second, rank, -1.0)
    place = lax.broadcasted_iota(jnp.int32, (capacity, tok), 0).astype(F32)

    def expand(ranks):
        return jnp.concatenate(
            [
                jnp.where(ranks[s : s + 1, :] == place, 1.0, 0.0).astype(BF16)
                for s in range(experts)
            ],
            axis=0,
        )

    return expand(rank0), expand(rank1)


def put_blocks(ref, rows):
    experts, capacity = ref.shape[:2]
    for s in range(experts):
        ref[s] = rows[s * capacity : (s + 1) * capacity].astype(ref.dtype)


def get_blocks(ref):
    return jnp.concatenate([ref[s] for s in range(ref.shape[0])], axis=0)


def gate_columns(meta):
    columns = meta.T
    return columns[:, 2:3], columns[:, 3:4]


def pack_kernel(base_ref, meta_ref, tokens_ref, rows_ref):
    m0, m1 = slot_masks(base_ref[0], meta_ref[0:2, :], *rows_ref.shape[:2])
    put_blocks(rows_ref, dot(m0 + m1, tokens_ref[...]))


def forward_kernel(chunk, w_ref, xa_ref, xb_ref, pa_ref, pb_ref, hid_ref, fa_ref, fb_ref):
    x = jnp.concatenate([get_blocks(xa_ref), get_blocks(xb_ref)], axis=0)
    units = w_ref.shape[1]
    for j in range(0, units, chunk):
        sl = slice(j, j + chunk)
        gate = dot(x, w_ref[0, sl, :], LAST)
        up = dot(x, w_ref[1, sl, :], LAST)
        sig = 0.5 * jnp.tanh(0.5 * gate) + 0.5
        silu = gate * sig
        hid_ref[:, sl] = (silu * up).astype(BF16)
        fa_ref[:, sl] = (up * (sig + silu * (1.0 - sig))).astype(BF16)
        fb_ref[:, sl] = silu.astype(BF16)
    out = dot(hid_ref[...], w_ref[2])
    rows = out.shape[0] // 2
    put_blocks(pa_ref, out[:rows])
    put_blocks(pb_ref, out[rows:])


def backward_kernel(chunk, w_ref, ra_ref, rb_ref, fa_ref, fb_ref, pa_ref, pb_ref, dgu_ref):
    rg = jnp.concatenate([get_blocks(ra_ref), get_blocks(rb_ref)], axis=0)
    units, width = w_ref.shape[1:]
    for j in range(0, units, chunk):
        sl = slice(j, j + chunk)
        dh = dot(rg, w_ref[2, sl, :], LAST)
        dgu_ref[:, sl] = (dh * fa_ref[:, sl].astype(F32)).astype(BF16)
        dgu_ref[:, units + j : units + j + chunk] = (dh * fb_ref[:, sl].astype(F32)).astype(BF16)
    out = dot(dgu_ref[...], w_ref[0:2].reshape(2 * units, width))
    rows = out.shape[0] // 2
    put_blocks(pa_ref, out[:rows])
    put_blocks(pb_ref, out[rows:])


def add_kernel(a_ref, b_ref, out_ref):
    out_ref[...] = (a_ref[...] + b_ref[...].astype(F32)).astype(BF16)


def relay_forward_kernel(base_ref, meta_ref, got_ref, part_ref):
    meta = meta_ref[...]
    m0, m1 = slot_masks(base_ref[0], meta[0:2, :], *got_ref.shape[:2])
    got = get_blocks(got_ref)
    g0, g1 = gate_columns(meta)
    part_ref[...] = (g0 * dot(m0, got, FIRST) + g1 * dot(m1, got, FIRST)).astype(BF16)


def combine_kernel(
    base_ref, meta_ref, teacher_ref, got_ref, part_ref, student_ref, d_gates_ref, diff_ref, rows_ref
):
    meta = meta_ref[...]
    m0, m1 = slot_masks(base_ref[0], meta[0:2, :], *got_ref.shape[:2])
    got = get_blocks(got_ref)
    g0, g1 = gate_columns(meta)
    o0, o1 = dot(m0, got, FIRST), dot(m1, got, FIRST)
    total = g0 * o0 + g1 * o1 + part_ref[...].astype(F32)
    student_ref[...] = total.astype(BF16)
    diff = total - teacher_ref[...].astype(F32)
    diff_ref[...] = diff.astype(BF16)
    put_d_gates(d_gates_ref, diff, o0, o1)
    put_route_grads(rows_ref, m0, m1, g0, g1, diff)


def put_d_gates(ref, diff, o0, o1):
    ref[...] = jnp.concatenate(
        [
            jnp.sum(diff * o0, axis=1, keepdims=True),
            jnp.sum(diff * o1, axis=1, keepdims=True),
        ],
        axis=1,
    )


def put_route_grads(ref, m0, m1, g0, g1, diff):
    grads = jnp.concatenate([(g0 * diff).astype(BF16), (g1 * diff).astype(BF16)], axis=0)
    put_blocks(ref, dot(jnp.concatenate([m0, m1], axis=1), grads))


def relay_backward_kernel(base_ref, meta_ref, got_ref, diff_ref, d_gates_ref, rows_ref):
    meta = meta_ref[...]
    m0, m1 = slot_masks(base_ref[0], meta[0:2, :], *got_ref.shape[:2])
    got = get_blocks(got_ref)
    g0, g1 = gate_columns(meta)
    diff = diff_ref[...].astype(F32)
    put_route_grads(rows_ref, m0, m1, g0, g1, diff)
    put_d_gates(d_gates_ref, diff, dot(m0, got, FIRST), dot(m1, got, FIRST))


def relay_sum_kernel(base_ref, meta_ref, got_ref, part_ref):
    m0, m1 = slot_masks(base_ref[0], meta_ref[0:2, :], *got_ref.shape[:2])
    part_ref[...] = dot(m0 + m1, get_blocks(got_ref), FIRST).astype(BF16)


def final_kernel(base_ref, meta_ref, got_ref, part_ref, out_ref):
    m0, m1 = slot_masks(base_ref[0], meta_ref[0:2, :], *got_ref.shape[:2])
    total = dot(m0 + m1, get_blocks(got_ref), FIRST) + part_ref[...].astype(F32)
    out_ref[...] = total.astype(BF16)


def weight_kernel(*refs):
    xs, rgs, acts, out_ref = refs[0:4], refs[4:8], refs[8:14], refs[14]
    x_near = jnp.concatenate([get_blocks(r) for r in xs[:2]], axis=0)
    x_far = jnp.concatenate([get_blocks(r) for r in xs[2:]], axis=0)
    rg_near = jnp.concatenate([get_blocks(r) for r in rgs[:2]], axis=0)
    rg_far = jnp.concatenate([get_blocks(r) for r in rgs[2:]], axis=0)
    for m, (near, far) in enumerate(((x_near, x_far), (x_near, x_far), (rg_near, rg_far))):
        term = dot(acts[m][...], near, FIRST) + dot(acts[3 + m][...], far, FIRST)
        out_ref[m] = term.astype(BF16)


def local(tokens, teacher, routes, gate_weights, weights):
    tok, width = tokens.shape
    experts = lax.axis_size("expert")
    half = experts // 2
    capacity = 4 * tok // experts
    rows = 2 * half * capacity
    units = weights.shape[1]
    chunk = min(256, units)
    base = (lax.axis_index("expert") // half * half).reshape(1)
    groups = [list(range(half)), list(range(half, experts))]
    mirror = [(i, i ^ half) for i in range(experts)]

    blocks = jax.ShapeDtypeStruct((half, capacity, width), BF16)
    blocks_f32 = jax.ShapeDtypeStruct((half, capacity, width), F32)
    dense = jax.ShapeDtypeStruct((tok, width), BF16)
    pair = jax.ShapeDtypeStruct((tok, 2), F32)
    acts = jax.ShapeDtypeStruct((rows, units), BF16)
    acts2 = jax.ShapeDtypeStruct((rows, 2 * units), BF16)
    vspec = pl.BlockSpec(memory_space=pltpu.VMEM)
    sspec = pl.BlockSpec(memory_space=pltpu.SMEM)
    matmul = 2 * rows * width * units

    def call(kernel, name, out_shape, scalars, *args, flops=0, limit=16):
        many = isinstance(out_shape, list)
        return pl.pallas_call(
            kernel,
            in_specs=[sspec] * scalars + [vspec] * (len(args) - scalars),
            out_specs=[vspec] * len(out_shape) if many else vspec,
            out_shape=out_shape,
            cost_estimate=pl.CostEstimate(
                flops=flops or 10**8, bytes_accessed=4 * MIB, transcendentals=0
            ),
            compiler_params=pltpu.CompilerParams(vmem_limit_bytes=limit * MIB),
            name=name,
        )(*args)

    def within_half(x):
        return lax.all_to_all(
            x, "expert", split_axis=0, concat_axis=0, axis_index_groups=groups, tiled=True
        )

    def to_mirror(x):
        return lax.ppermute(x, "expert", mirror)

    def to_sibling(x):
        return lax.ppermute(x, "dp", [(0, 1), (1, 0)])

    own = weights[0].transpose(1, 0, 2)
    meta = jnp.concatenate(
        [routes.T.astype(F32), gate_weights.T, jnp.zeros((4, tok), F32)], axis=0
    )

    def forward(x, name):
        x_sib = to_sibling(x)
        pa, pb, hid, fa, fb = call(
            functools.partial(forward_kernel, chunk),
            name,
            [blocks_f32, blocks, acts, acts, acts],
            0,
            own,
            x,
            x_sib,
            flops=3 * matmul,
            limit=24,
        )
        out = call(add_kernel, "add_halves", blocks, 0, pa, to_sibling(pb))
        return out, (x, x_sib, hid, fa, fb)

    def backward(rg, saved, name):
        fa, fb = saved[3:]
        rg_sib = to_sibling(rg)
        pa, pb, dgu = call(
            functools.partial(backward_kernel, chunk),
            name,
            [blocks_f32, blocks, acts2],
            0,
            own,
            rg,
            rg_sib,
            fa,
            fb,
            flops=3 * matmul,
            limit=24,
        )
        out = call(add_kernel, "add_halves", blocks, 0, pa, to_sibling(pb))
        return out, (rg, rg_sib, dgu)

    far_tokens = to_mirror(tokens)
    far_meta = to_mirror(meta)
    x_near = within_half(call(pack_kernel, "pack_near", blocks, 1, base, meta, tokens))
    x_far = within_half(call(pack_kernel, "pack_far", blocks, 1, base, far_meta, far_tokens))

    out_near, saved_near = forward(x_near, "forward_near")
    out_far, saved_far = forward(x_far, "forward_far")

    got_far = within_half(out_far)
    part = to_mirror(
        call(relay_forward_kernel, "relay_forward", dense, 1, base, far_meta, got_far)
    )
    got_near = within_half(out_near)
    student, d_gates, diff, rows_near = call(
        combine_kernel,
        "combine_routes",
        [dense, pair, dense, blocks],
        1,
        base,
        meta,
        teacher,
        got_near,
        part,
    )

    far_diff = to_mirror(diff)
    rg_near = within_half(rows_near)
    far_d_gates, rows_far = call(
        relay_backward_kernel,
        "relay_backward",
        [pair, blocks],
        1,
        base,
        far_meta,
        got_far,
        far_diff,
    )
    rg_far = within_half(rows_far)
    d_gates = d_gates + to_mirror(far_d_gates)

    grad_near, more_near = backward(rg_near, saved_near, "backward_near")
    grad_far, more_far = backward(rg_far, saved_far, "backward_far")

    back_far = within_half(grad_far)
    part = to_mirror(call(relay_sum_kernel, "relay_sum", dense, 1, base, far_meta, back_far))
    back_near = within_half(grad_near)

    whole = pl.BlockSpec((half, capacity, width), lambda i: (0, 0, 0))
    steps = units // chunk
    column = lambda first: pl.BlockSpec((rows, chunk), lambda i: (0, first + i))
    weight_grads = pl.pallas_call(
        weight_kernel,
        grid=(steps,),
        in_specs=[whole] * 8 + [column(0), column(steps), column(0)] * 2,
        out_specs=pl.BlockSpec((3, chunk, width), lambda i: (0, i, 0)),
        out_shape=jax.ShapeDtypeStruct((3, units, width), BF16),
        cost_estimate=pl.CostEstimate(
            flops=6 * matmul, bytes_accessed=20 * MIB, transcendentals=0
        ),
        compiler_params=pltpu.CompilerParams(vmem_limit_bytes=24 * MIB),
        name="weight_gradients",
    )(
        *saved_near[:2],
        *saved_far[:2],
        *more_near[:2],
        *more_far[:2],
        more_near[2],
        more_near[2],
        saved_near[2],
        more_far[2],
        more_far[2],
        saved_far[2],
    )

    d_tokens = call(
        final_kernel, "combine_gradients", dense, 1, base, meta, back_near, part
    )
    return (student, d_tokens, d_gates, weight_grads.transpose(1, 0, 2)[None])


def solution(mesh):
    rows = P(("groups", "expert", "dp"), None)
    return jax.shard_map(
        local,
        mesh=mesh,
        in_specs=(rows, rows, rows, rows, P("expert", "dp", None, None)),
        out_specs=(rows, rows, rows, P(("groups", "expert"), "dp", None, None)),
        check_vma=False,
    )
```

time: 172 us -> 164 us (0.953)
  starting transfers between devices: 7.63 us -> 40.2 us
  Pallas kernels: 0 us -> 32.3 us
  matrix products: 31.8 us -> 0 us
  blocking collectives: 50.8 us -> 19 us
  local copies, waits for them, and re-layouts: 8.98 us -> 34.5 us
  other arithmetic: 19.6 us -> 1.44 us
  between operations: 14.3 us -> 0.83 us
  waiting for transfers between devices: 38.3 us -> 34.4 us
    unnamed x27 -> x65, local copies, waits for them, and re-layouts: 2.13 us -> 34.4 us
    pallas_call x0 -> x16, Pallas kernels: none -> 32.3 us  [the longest x15 23.7 us: call(): pl.pallas_call(kernel, in_specs=[sspec] * scalars + [vspec] * (len(args)...]
    dot_general x9 -> x0, matrix products: 31.8 us -> none  [the longest x1 5.1 us: local(): jnp.dot(d_up, matrices[:, 1, :], preferred_element_type=jnp.float32)]
    all_to_all x2, blocking collectives: 50.8 us -> 19 us  [within_half(): lax.all_to_all(x, 'expert', split_axis=0, concat_axis=0, axis_index_group...]
    all_to_all x2 -> x6, waiting for transfers between devices: 37.6 us -> 7.24 us  [within_half(): lax.all_to_all(x, 'expert', split_axis=0, concat_axis=0, axis_index_group...]
    ppermute x0 -> x14, waiting for transfers between devices: none -> 27.2 us  [the longest x6 20.9 us: to_mirror(): return lax.ppermute(x, 'expert', mirror)]
    ppermute x0 -> x14, starting transfers between devices: none -> 16.4 us  [the longest x6 15.1 us: to_mirror(): return lax.ppermute(x, 'expert', mirror)]
    all_to_all x2 -> x6, starting transfers between devices: 7.55 us -> 23.8 us  [within_half(): lax.all_to_all(x, 'expert', split_axis=0, concat_axis=0, axis_index_group...]
  transfers between devices with their start and end apart: 4 -> 20, of which waited for: 2 -> 8; matrix products, arithmetic and copies ran while one was open for 10% -> 1% of each run, Pallas kernels for 0% -> 18%
where the time goes in v2:
time: 164 us; the launch traced here: 163 us
  starting transfers between devices  40.2 us (25%)
  local copies, waits for them, and re-layouts  34.5 us (21%)
  waiting for transfers between devices  34.4 us (21%)
  Pallas kernels  32.3 us (20%)
  blocking collectives  19 us (12%)
    unnamed x65, local copies, waits for them, and re-layouts  34.4 us
    all_to_all x6, starting transfers between devices, within_half(): lax.all_to_all(x, 'expert', split_axis=0, concat_axis=0, axis_index_group...  23.8 us
    pallas_call x15, Pallas kernels, call(): pl.pallas_call(kernel, in_specs=[sspec] * scalars + [vspec] * (len(args)...  23.7 us
    ppermute x6, waiting for transfers between devices, to_mirror(): return lax.ppermute(x, 'expert', mirror)  20.9 us
    all_to_all x2, blocking collectives, within_half(): lax.all_to_all(x, 'expert', split_axis=0, concat_axis=0, axis_index_group...  19 us
    ppermute x6, starting transfers between devices, to_mirror(): return lax.ppermute(x, 'expert', mirror)  15.1 us
    pallas_call x1, Pallas kernels, local(): pl.pallas_call(weight_kernel, grid=(steps,), in_specs=[whole] * 8 + [colu...  8.58 us
    all_to_all x6, waiting for transfers between devices, within_half(): lax.all_to_all(x, 'expert', split_axis=0, concat_axis=0, axis_index_group...  7.24 us
  transfers between devices with their start and end apart: 20, of which 8 were waited for; matrix products, arithmetic and copies ran while one was open for 1% of the time, Pallas kernels for 18%

profile of v2, /device:TPU:0, one launch (start us, length us, event | category | flops | bytes accessed | tf_op | source)
XLA Modules:
  0.0 162.7 jit_solution(6275754249816006467)
XLA Ops:
  0.6 4.1 %collective-permute-start.3 = (bf16[128,768]{1,0:T(8,128)(2,1)}, bf16[128,768]{1,0:T(8,128)(2,1)S(1)}, u32[]{:S(2)}, u32[]{:S(2)}) collective-permute-start(bf16[128,768]{1,0:T(8,128)(2,1)} %tokens_ref.1), channel_id=1, source_target_pairs={{0,8},{2,10},{4,12},{6,14},{8,0},{10,2},{12,4},{14,6},{1,9},{3,11}... | collective-permute-start | bytes 589832 | tf_op jit(solution)/shard_map/ppermute | solution.py:216
  6.3 8.0 %collective-permute-done.2.meta_ref = f32[8,128]{1,0:T(8,128)S(1)} collective-permute-done((f32[8,128]{1,0:T(8,128)S(1)}, f32[8,128]{1,0:T(8,128)S(1)}, u32[]{:S(2)}, u32[]{:S(2)}) %collective-permute-start.2) | collective-permute-done | bytes 4128 | tf_op jit(solution)/shard_map/ppermute | solution.py:216
  14.6 10.1 %all_to_all.40.xa_ref.refs_2_ = bf16[4,64,768]{2,1,0:T(8,128)(2,1)S(1)} all-to-all(bf16[4,64,768]{2,1,0:T(8,128)(2,1)S(1)} %pack_far.1), channel_id=1, replica_groups={{0,2,4,6},{8,10,12,14},{1,3,5,7},{9,11,13,15},{16,18,20,22},{24,26,28,3..., dimensions={0} | all-to-all | bytes 786432 | tf_op jit(solution)/shard_map/all_to_all | solution.py:211
  25.6 1.1 pack_near.1
  26.7 3.5 %all-to-all-start = ((bf16[4,64,768]{2,1,0:T(8,128)(2,1)}), bf16[4,64,768]{2,1,0:T(8,128)(2,1)S(1)}, u32[]{:S(2)}, u32[]{:S(2)}) async-start(bf16[4,64,768]{2,1,0:T(8,128)(2,1)} %pack_near.1), calls=%async_computation | async-start | bytes 786432 | tf_op jit(solution)/shard_map/all_to_all | solution.py:211
  30.2 2.5 %copy-done.20 = bf16[1,1024,3,768]{3,1,2,0:T(8,128)(2,1)S(1)} copy-done((bf16[1,1024,3,768]{3,1,2,0:T(8,128)(2,1)S(1)}, bf16[1,1024,3,768]{3,1,2,0:T(8,128)(2,1)}, u32[]{:S(2)}) %copy-start.20) | copy-done | bytes 4718616
  32.7 2.8 %forward_far.1 = (f32[4,64,768]{2,1,0:T(8,128)S(1)}, bf16[4,64,768]{2,1,0:T(8,128)(2,1)S(1)}, bf16[512,1024]{1,0:T(8,128)(2,1)S(1)}, bf16[512,1024]{1,0:T(8,128)(2,1)S(1)}, bf16[512,1024]{1,0:T(8,128)(2,1)S(1)}) custom-call(bf16[3,1024,768]{2,1,0:T(8,128)(2,1)S(1)} %bitcast.10, bf16[4,64,768]{2,1,0:T(8,128)(2,1)S(1)} %all_to_all.40.xa_ref.refs_2_, ...), custom_call_target="tpu_custom_call" | custom-call | flops 2415919104 | bytes 4194304 | tf_op jit(solution)/shard_map/forward_far/pallas_call | solution.py:198
  35.5 1.0 copy-done.6
  37.5 1.0 copy-done.26
  39.1 1.3 collective-permute-done.5.b_ref
  41.2 4.0 %all-to-all-start.3 = ((bf16[4,64,768]{2,1,0:T(8,128)(2,1)}), bf16[4,64,768]{2,1,0:T(8,128)(2,1)S(1)}, u32[]{:S(2)}, u32[]{:S(2)}) async-start(bf16[4,64,768]{2,1,0:T(8,128)(2,1)} %add_halves.5), calls=%async_computation.3 | async-start | bytes 786432 | tf_op jit(solution)/shard_map/all_to_all | solution.py:211
  45.2 2.4 %copy-done.21 = bf16[1,1024,3,768]{3,1,2,0:T(8,128)(2,1)S(1)} copy-done((bf16[1,1024,3,768]{3,1,2,0:T(8,128)(2,1)S(1)}, bf16[1,1024,3,768]{3,1,2,0:T(8,128)(2,1)}, u32[]{:S(2)}) %copy-start.21) | copy-done | bytes 4718616
  47.6 2.8 %forward_near.1 = (f32[4,64,768]{2,1,0:T(8,128)S(1)}, bf16[4,64,768]{2,1,0:T(8,128)(2,1)S(1)}, bf16[512,1024]{1,0:T(8,128)(2,1)S(1)}, bf16[512,1024]{1,0:T(8,128)(2,1)S(1)}, bf16[512,1024]{1,0:T(8,128)(2,1)S(1)}) custom-call(bf16[3,1024,768]{2,1,0:T(8,128)(2,1)S(1)} %bitcast.11, bf16[4,64,768]{2,1,0:T(8,128)(2,1)S(1)} %all-to-all-done.xa_ref.refs_0_, ...), custom_call_target="tpu_custom_call" | custom-call | flops 2415919104 | bytes 4194304 | tf_op jit(solution)/shard_map/forward_near/pallas_call | solution.py:198
  53.4 1.7 %collective-permute-done.1.b_ref = bf16[4,64,768]{2,1,0:T(8,128)(2,1)S(1)} collective-permute-done((bf16[4,64,768]{2,1,0:T(8,128)(2,1)S(1)}, bf16[4,64,768]{2,1,0:T(8,128)(2,1)S(1)}, u32[]{:S(2)}, u32[]{:S(2)}) %collective-permute-start.1) | collective-permute-done | bytes 393248 | tf_op jit(solution)/shard_map/ppermute | solution.py:219
  55.9 4.2 %all-to-all-start.1 = ((bf16[4,64,768]{2,1,0:T(8,128)(2,1)}), bf16[4,64,768]{2,1,0:T(8,128)(2,1)S(1)}, u32[]{:S(2)}, u32[]{:S(2)}) async-start(bf16[4,64,768]{2,1,0:T(8,128)(2,1)} %add_halves.4), calls=%async_computation.1 | async-start | bytes 786432 | tf_op jit(solution)/shard_map/all_to_all | solution.py:211
  60.6 3.4 %collective-permute-start.6 = (bf16[128,768]{1,0:T(8,128)(2,1)S(1)}, bf16[128,768]{1,0:T(8,128)(2,1)S(1)}, u32[]{:S(2)}, u32[]{:S(2)}) collective-permute-start(bf16[128,768]{1,0:T(8,128)(2,1)S(1)} %relay_forward.1), channel_id=1, source_target_pairs={{0,8},{2,10},{4,12},{6,14},{8,0},{10,2},{12,4},{14,6},{1,9},{3,11}... | collective-permute-start | bytes 589832 | tf_op jit(solution)/shard_map/ppermute | solution.py:216
  64.0 7.2 %all-to-all-done.1.got_ref = bf16[4,64,768]{2,1,0:T(8,128)(2,1)S(1)} async-done(((bf16[4,64,768]{2,1,0:T(8,128)(2,1)}), bf16[4,64,768]{2,1,0:T(8,128)(2,1)S(1)}, u32[]{:S(2)}, u32[]{:S(2)}) %all-to-all-start.1) | async-done | bytes 393248 | tf_op jit(solution)/shard_map/all_to_all | solution.py:211
  71.2 1.6 combine_routes.1
  72.8 1.2 collective-permute-start.9
  74.1 9.7 %collective-permute-done.9.diff_ref = bf16[128,768]{1,0:T(8,128)(2,1)S(1)} collective-permute-done((bf16[128,768]{1,0:T(8,128)(2,1)S(1)}, bf16[128,768]{1,0:T(8,128)(2,1)S(1)}, u32[]{:S(2)}, u32[]{:S(2)}) %collective-permute-start.9) | collective-permute-done | bytes 196640 | tf_op jit(solution)/shard_map/ppermute | solution.py:216
  84.4 8.9 %all_to_all.41.ra_ref.refs_6_ = bf16[4,64,768]{2,1,0:T(8,128)(2,1)S(1)} all-to-all(bf16[4,64,768]{2,1,0:T(8,128)(2,1)S(1)} %get-tuple-element.37), channel_id=1, replica_groups={{0,2,4,6},{8,10,12,14},{1,3,5,7},{9,11,13,15},{16,18,20,22},{24,26,28,3..., dimensions={0} | all-to-all | bytes 786432 | tf_op jit(solution)/shard_map/all_to_all | solution.py:211
  93.4 4.1 %all-to-all-start.4 = ((bf16[4,64,768]{2,1,0:T(8,128)(2,1)}), bf16[4,64,768]{2,1,0:T(8,128)(2,1)}, u32[]{:S(2)}, u32[]{:S(2)}) async-start(bf16[4,64,768]{2,1,0:T(8,128)(2,1)} %get-tuple-element.31), calls=%async_computation.4 | async-start | bytes 786432 | tf_op jit(solution)/shard_map/all_to_all | solution.py:211
  97.5 2.5 %copy-done.22 = bf16[1,1024,3,768]{3,1,2,0:T(8,128)(2,1)S(1)} copy-done((bf16[1,1024,3,768]{3,1,2,0:T(8,128)(2,1)S(1)}, bf16[1,1024,3,768]{3,1,2,0:T(8,128)(2,1)}, u32[]{:S(2)}) %copy-start.22) | copy-done | bytes 4718616
  100.0 1.2 copy-done.25
  101.2 1.2 copy-done.27
  102.4 4.1 %backward_far.1 = (f32[4,64,768]{2,1,0:T(8,128)S(1)}, bf16[4,64,768]{2,1,0:T(8,128)(2,1)}, bf16[512,2048]{1,0:T(8,128)(2,1)S(1)}) custom-call(bf16[3,1024,768]{2,1,0:T(8,128)(2,1)S(1)} %bitcast.12, bf16[4,64,768]{2,1,0:T(8,128)(2,1)S(1)} %all_to_all.41.ra_ref.refs_6_, bf16[4,64,768]{2,1,0:T(8,128)(2,1)S(1)} %collective-permute-done.10.rb_ref.refs_7_, ...), custom_call_target="tpu_custom_call" | custom-call | flops 2415919104 | bytes 4194304 | tf_op jit(solution)/shard_map/backward_far/pallas_call | solution.py:198
  107.9 1.7 %collective-permute-done.11.b_ref = bf16[4,64,768]{2,1,0:T(8,128)(2,1)S(1)} collective-permute-done((bf16[4,64,768]{2,1,0:T(8,128)(2,1)}, bf16[4,64,768]{2,1,0:T(8,128)(2,1)S(1)}, u32[]{:S(2)}, u32[]{:S(2)}) %collective-permute-start.11) | collective-permute-done | bytes 393248 | tf_op jit(solution)/shard_map/ppermute | solution.py:219
  109.7 1.1 copy-done.11
  111.6 3.8 %all-to-all-start.7 = ((bf16[4,64,768]{2,1,0:T(8,128)(2,1)}), bf16[4,64,768]{2,1,0:T(8,128)(2,1)S(1)}, u32[]{:S(2)}, u32[]{:S(2)}) async-start(bf16[4,64,768]{2,1,0:T(8,128)(2,1)} %add_halves.7), calls=%async_computation.7 | async-start | bytes 786432 | tf_op jit(solution)/shard_map/all_to_all | solution.py:211
  115.4 2.3 %copy-done.23 = bf16[1,1024,3,768]{3,1,2,0:T(8,128)(2,1)S(1)} copy-done((bf16[1,1024,3,768]{3,1,2,0:T(8,128)(2,1)S(1)}, bf16[1,1024,3,768]{3,1,2,0:T(8,128)(2,1)}, u32[]{:S(2)}) %copy-start.23) | copy-done | bytes 4718616
  117.8 1.2 copy-done.29
  119.0 1.2 copy-done.31
  120.2 4.4 %backward_near.1 = (f32[4,64,768]{2,1,0:T(8,128)S(1)}, bf16[4,64,768]{2,1,0:T(8,128)(2,1)S(1)}, bf16[512,2048]{1,0:T(8,128)(2,1)S(1)}) custom-call(bf16[3,1024,768]{2,1,0:T(8,128)(2,1)S(1)} %bitcast.13, bf16[4,64,768]{2,1,0:T(8,128)(2,1)} %all-to-all-done.4.ra_ref.refs_4_, bf16[4,64,768]{2,1,0:T(8,128)(2,1)} %collective-permute-done.7.rb_ref.refs_5_, ...), custom_call_target="tpu_custom_call" | custom-call | flops 2415919104 | bytes 4194304 | tf_op jit(solution)/shard_map/backward_near/pallas_call | solution.py:198
  124.7 1.3 copy-done
  126.2 1.5 collective-permute-done.8.b_ref
  128.5 4.2 %all-to-all-start.5 = ((bf16[4,64,768]{2,1,0:T(8,128)(2,1)}), bf16[4,64,768]{2,1,0:T(8,128)(2,1)S(1)}, u32[]{:S(2)}, u32[]{:S(2)}) async-start(bf16[4,64,768]{2,1,0:T(8,128)(2,1)} %add_halves.6), calls=%async_computation.5 | async-start | bytes 786432 | tf_op jit(solution)/shard_map/all_to_all | solution.py:211
  132.7 2.9 %collective-permute-start.13 = (f32[128,2]{1,0:T(8,128)S(1)}, f32[128,2]{1,0:T(8,128)S(1)}, u32[]{:S(2)}, u32[]{:S(2)}) collective-permute-start(f32[128,2]{1,0:T(8,128)S(1)} %get-tuple-element.43), channel_id=1, source_target_pairs={{0,8},{2,10},{4,12},{6,14},{8,0},{10,2},{12,4},{14,6},{1,9},{3,11}... | collective-permute-start | bytes 3080 | tf_op jit(solution)/shard_map/ppermute | solution.py:216
  135.6 3.2 %collective-permute-done.13 = f32[128,2]{1,0:T(8,128)S(1)} collective-permute-done((f32[128,2]{1,0:T(8,128)S(1)}, f32[128,2]{1,0:T(8,128)S(1)}, u32[]{:S(2)}, u32[]{:S(2)}) %collective-permute-start.13) | collective-permute-done | bytes 1056 | tf_op jit(solution)/shard_map/ppermute | solution.py:216
  139.4 1.1 relay_sum.1
  140.5 3.5 %collective-permute-start.12 = (bf16[128,768]{1,0:T(8,128)(2,1)}, bf16[128,768]{1,0:T(8,128)(2,1)S(1)}, u32[]{:S(2)}, u32[]{:S(2)}) collective-permute-start(bf16[128,768]{1,0:T(8,128)(2,1)} %relay_sum.1), channel_id=1, source_target_pairs={{0,8},{2,10},{4,12},{6,14},{8,0},{10,2},{12,4},{14,6},{1,9},{3,11}... | collective-permute-start | bytes 589832 | tf_op jit(solution)/shard_map/ppermute | solution.py:216
  144.0 1.6 copy-done.1
  145.6 1.0 copy-done.3
  146.6 1.0 copy-done.5
  147.6 1.2 copy-done.7
  148.8 1.2 copy-done.9
  150.0 1.0 copy-done.13
  153.0 8.6 %weight_gradients.1 = bf16[3,1024,768]{2,1,0:T(8,128)(2,1)} custom-call(bf16[4,64,768]{2,1,0:T(8,128)(2,1)S(1)} %copy-done.3, bf16[4,64,768]{2,1,0:T(8,128)(2,1)S(1)} %copy-done.15, bf16[4,64,768]{2,1,0:T(8,128)(2,1)S(1)} %all_to_all.40.xa_ref.refs_2_, bf16[4,64,768]{2,1,0:T(8,128)(2,1)S(1)} %copy-done.13, ...), custom_call_target="tpu_custom_call" | custom-call | flops 4831838208 | bytes 20971520 | tf_op jit(solution)/shard_map/weight_gradients/pallas_call | solution.py:311
  161.6 1.1 combine_gradients.1
  (80 shorter events, 16.0 us)
Async XLA Ops:
  0.6 13.6 %collective-permute-start.3 = (bf16[128,768]{1,0:T(8,128)(2,1)}, bf16[128,768]{1,0:T(8,128)(2,1)S(1)}, u32[]{:S(2)}, u32[]{:S(2)}) collective-permute-start(bf16[128,768]{1,0:T(8,128)(2,1)} %tokens_ref.1), channel_id=1, source_target_pairs={{0,8},{2,10},{4,12},{6,14},{8,0},{10,2},{12,4},{14,6},{1,9},{3,11}... | collective-permute-start | bytes 589832 | tf_op jit(solution)/shard_map/ppermute | solution.py:216
  6.2 8.0 %collective-permute-start.2 = (f32[8,128]{1,0:T(8,128)S(1)}, f32[8,128]{1,0:T(8,128)S(1)}, u32[]{:S(2)}, u32[]{:S(2)}) collective-permute-start(f32[8,128]{1,0:T(8,128)S(1)} %maximum_maximum_fusion.meta_ref), channel_id=1, source_target_pairs={{0,8},{2,10},{4,12},{6,14},{8,0},{10,2},{12,4},{14,6},{1,9},{3,11}... | collective-permute-start | bytes 12296 | tf_op jit(solution)/shard_map/ppermute | solution.py:216
  24.7 5.5 %collective-permute-start.4 = (bf16[4,64,768]{2,1,0:T(8,128)(2,1)S(1)}, bf16[4,64,768]{2,1,0:T(8,128)(2,1)S(1)}, u32[]{:S(2)}, u32[]{:S(2)}) collective-permute-start(bf16[4,64,768]{2,1,0:T(8,128)(2,1)S(1)} %all_to_all.40.xa_ref.refs_2_), channel_id=1, source_target_pairs={{0,1},{1,0},{2,3},{3,2},{4,5},{5,4},{6,7},{7,6},{8,9},{9,8},{10,11... | collective-permute-start | bytes 1179656 | tf_op jit(solution)/shard_map/ppermute | solution.py:219
  26.7 12.3 %all-to-all-start = ((bf16[4,64,768]{2,1,0:T(8,128)(2,1)}), bf16[4,64,768]{2,1,0:T(8,128)(2,1)S(1)}, u32[]{:S(2)}, u32[]{:S(2)}) async-start(bf16[4,64,768]{2,1,0:T(8,128)(2,1)} %pack_near.1), calls=%async_computation | async-start | bytes 786432 | tf_op jit(solution)/shard_map/all_to_all | solution.py:211
  30.2 5.3 %copy-start.12 = (bf16[4,64,768]{2,1,0:T(8,128)(2,1)}, bf16[4,64,768]{2,1,0:T(8,128)(2,1)S(1)}, u32[]{:S(2)}) copy-start(bf16[4,64,768]{2,1,0:T(8,128)(2,1)S(1)} %collective-permute-done.4.xb_ref.refs_3_) | copy-start | bytes 1179652
  30.2 2.5 %copy-start.20 = (bf16[1,1024,3,768]{3,1,2,0:T(8,128)(2,1)S(1)}, bf16[1,1024,3,768]{3,1,2,0:T(8,128)(2,1)}, u32[]{:S(2)}) copy-start(bf16[1,1024,3,768]{3,1,2,0:T(8,128)(2,1)} %param.9) | copy-start | bytes 14155780
  35.5 1.0 copy-start.6
  37.5 1.0 copy-start.26
  38.6 1.9 %collective-permute-start.5 = (bf16[4,64,768]{2,1,0:T(8,128)(2,1)S(1)}, bf16[4,64,768]{2,1,0:T(8,128)(2,1)S(1)}, u32[]{:S(2)}, u32[]{:S(2)}) collective-permute-start(bf16[4,64,768]{2,1,0:T(8,128)(2,1)S(1)} %get-tuple-element.29), channel_id=1, source_target_pairs={{0,1},{1,0},{2,3},{3,2},{4,5},{5,4},{6,7},{7,6},{8,9},{9,8},{10,11... | collective-permute-start | bytes 1179656 | tf_op jit(solution)/shard_map/ppermute | solution.py:219
  39.1 11.4 %copy-start.2 = (bf16[4,64,768]{2,1,0:T(8,128)(2,1)}, bf16[4,64,768]{2,1,0:T(8,128)(2,1)S(1)}, u32[]{:S(2)}) copy-start(bf16[4,64,768]{2,1,0:T(8,128)(2,1)S(1)} %all-to-all-done.xa_ref.refs_0_) | copy-start | bytes 1179652
  39.1 6.2 %collective-permute-start = (bf16[4,64,768]{2,1,0:T(8,128)(2,1)S(1)}, bf16[4,64,768]{2,1,0:T(8,128)(2,1)S(1)}, u32[]{:S(2)}, u32[]{:S(2)}) collective-permute-start(bf16[4,64,768]{2,1,0:T(8,128)(2,1)S(1)} %all-to-all-done.xa_ref.refs_0_), channel_id=1, source_target_pairs={{0,1},{1,0},{2,3},{3,2},{4,5},{5,4},{6,7},{7,6},{8,9},{9,8},{10,11... | collective-permute-start | bytes 1179656 | tf_op jit(solution)/shard_map/ppermute | solution.py:219
  41.2 14.7 %all-to-all-start.3 = ((bf16[4,64,768]{2,1,0:T(8,128)(2,1)}), bf16[4,64,768]{2,1,0:T(8,128)(2,1)S(1)}, u32[]{:S(2)}, u32[]{:S(2)}) async-start(bf16[4,64,768]{2,1,0:T(8,128)(2,1)} %add_halves.5), calls=%async_computation.3 | async-start | bytes 786432 | tf_op jit(solution)/shard_map/all_to_all | solution.py:211
  45.2 26.0 %copy-start.19 = (bf16[128,768]{1,0:T(8,128)(2,1)S(1)}, bf16[128,768]{1,0:T(8,128)(2,1)}, u32[]{:S(2)}) copy-start(bf16[128,768]{1,0:T(8,128)(2,1)} %teacher_ref.1) | copy-start | bytes 589828
  45.2 2.4 %copy-start.21 = (bf16[1,1024,3,768]{3,1,2,0:T(8,128)(2,1)S(1)}, bf16[1,1024,3,768]{3,1,2,0:T(8,128)(2,1)}, u32[]{:S(2)}) copy-start(bf16[1,1024,3,768]{3,1,2,0:T(8,128)(2,1)} %param.9) | copy-start | bytes 14155780
  47.6 8.3 %copy-start.14 = (bf16[4,64,768]{2,1,0:T(8,128)(2,1)}, bf16[4,64,768]{2,1,0:T(8,128)(2,1)S(1)}, u32[]{:S(2)}) copy-start(bf16[4,64,768]{2,1,0:T(8,128)(2,1)S(1)} %collective-permute-done.xb_ref.refs_1_) | copy-start | bytes 1179652
  50.4 1.0 copy-start.8
  52.4 1.0 copy-start.30
  53.4 1.7 %collective-permute-start.1 = (bf16[4,64,768]{2,1,0:T(8,128)(2,1)S(1)}, bf16[4,64,768]{2,1,0:T(8,128)(2,1)S(1)}, u32[]{:S(2)}, u32[]{:S(2)}) collective-permute-start(bf16[4,64,768]{2,1,0:T(8,128)(2,1)S(1)} %get-tuple-element.27), channel_id=1, source_target_pairs={{0,1},{1,0},{2,3},{3,2},{4,5},{5,4},{6,7},{7,6},{8,9},{9,8},{10,11... | collective-permute-start | bytes 1179656 | tf_op jit(solution)/shard_map/ppermute | solution.py:219
  55.9 15.3 %all-to-all-start.1 = ((bf16[4,64,768]{2,1,0:T(8,128)(2,1)}), bf16[4,64,768]{2,1,0:T(8,128)(2,1)S(1)}, u32[]{:S(2)}, u32[]{:S(2)}) async-start(bf16[4,64,768]{2,1,0:T(8,128)(2,1)} %add_halves.4), calls=%async_computation.1 | async-start | bytes 786432 | tf_op jit(solution)/shard_map/all_to_all | solution.py:211
  60.6 10.7 %collective-permute-start.6 = (bf16[128,768]{1,0:T(8,128)(2,1)S(1)}, bf16[128,768]{1,0:T(8,128)(2,1)S(1)}, u32[]{:S(2)}, u32[]{:S(2)}) collective-permute-start(bf16[128,768]{1,0:T(8,128)(2,1)S(1)} %relay_forward.1), channel_id=1, source_target_pairs={{0,8},{2,10},{4,12},{6,14},{8,0},{10,2},{12,4},{14,6},{1,9},{3,11}... | collective-permute-start | bytes 589832 | tf_op jit(solution)/shard_map/ppermute | solution.py:216
  72.8 11.0 %collective-permute-start.9 = (bf16[128,768]{1,0:T(8,128)(2,1)S(1)}, bf16[128,768]{1,0:T(8,128)(2,1)S(1)}, u32[]{:S(2)}, u32[]{:S(2)}) collective-permute-start(bf16[128,768]{1,0:T(8,128)(2,1)S(1)} %get-tuple-element.36), channel_id=1, source_target_pairs={{0,8},{2,10},{4,12},{6,14},{8,0},{10,2},{12,4},{14,6},{1,9},{3,11}... | collective-permute-start | bytes 589832 | tf_op jit(solution)/shard_map/ppermute | solution.py:216
  93.4 13.2 %copy-start.4 = (bf16[4,64,768]{2,1,0:T(8,128)(2,1)}, bf16[4,64,768]{2,1,0:T(8,128)(2,1)S(1)}, u32[]{:S(2)}) copy-start(bf16[4,64,768]{2,1,0:T(8,128)(2,1)S(1)} %all_to_all.41.ra_ref.refs_6_) | copy-start | bytes 1179652
  93.4 4.1 %collective-permute-start.10 = (bf16[4,64,768]{2,1,0:T(8,128)(2,1)S(1)}, bf16[4,64,768]{2,1,0:T(8,128)(2,1)S(1)}, u32[]{:S(2)}, u32[]{:S(2)}) collective-permute-start(bf16[4,64,768]{2,1,0:T(8,128)(2,1)S(1)} %all_to_all.41.ra_ref.refs_6_), channel_id=1, source_target_pairs={{0,1},{1,0},{2,3},{3,2},{4,5},{5,4},{6,7},{7,6},{8,9},{9,8},{10,11... | collective-permute-start | bytes 1179656 | tf_op jit(solution)/shard_map/ppermute | solution.py:219
  93.4 14.5 %all-to-all-start.4 = ((bf16[4,64,768]{2,1,0:T(8,128)(2,1)}), bf16[4,64,768]{2,1,0:T(8,128)(2,1)}, u32[]{:S(2)}, u32[]{:S(2)}) async-start(bf16[4,64,768]{2,1,0:T(8,128)(2,1)} %get-tuple-element.31), calls=%async_computation.4 | async-start | bytes 786432 | tf_op jit(solution)/shard_map/all_to_all | solution.py:211
  97.5 14.1 %copy-start.16 = (bf16[4,64,768]{2,1,0:T(8,128)(2,1)}, bf16[4,64,768]{2,1,0:T(8,128)(2,1)S(1)}, u32[]{:S(2)}) copy-start(bf16[4,64,768]{2,1,0:T(8,128)(2,1)S(1)} %collective-permute-done.10.rb_ref.refs_7_) | copy-start | bytes 1179652
  97.5 2.5 %copy-start.22 = (bf16[1,1024,3,768]{3,1,2,0:T(8,128)(2,1)S(1)}, bf16[1,1024,3,768]{3,1,2,0:T(8,128)(2,1)}, u32[]{:S(2)}) copy-start(bf16[1,1024,3,768]{3,1,2,0:T(8,128)(2,1)} %param.9) | copy-start | bytes 14155780
  100.0 1.2 copy-start.25
  101.2 1.2 copy-start.27
  107.4 2.3 %collective-permute-start.11 = (bf16[4,64,768]{2,1,0:T(8,128)(2,1)}, bf16[4,64,768]{2,1,0:T(8,128)(2,1)S(1)}, u32[]{:S(2)}, u32[]{:S(2)}) collective-permute-start(bf16[4,64,768]{2,1,0:T(8,128)(2,1)} %get-tuple-element.41), channel_id=1, source_target_pairs={{0,1},{1,0},{2,3},{3,2},{4,5},{5,4},{6,7},{7,6},{8,9},{9,8},{10,11... | collective-permute-start | bytes 1179656 | tf_op jit(solution)/shard_map/ppermute | solution.py:219
  107.9 7.5 %collective-permute-start.7 = (bf16[4,64,768]{2,1,0:T(8,128)(2,1)}, bf16[4,64,768]{2,1,0:T(8,128)(2,1)}, u32[]{:S(2)}, u32[]{:S(2)}) collective-permute-start(bf16[4,64,768]{2,1,0:T(8,128)(2,1)} %all-to-all-done.4.ra_ref.refs_4_), channel_id=1, source_target_pairs={{0,1},{1,0},{2,3},{3,2},{4,5},{5,4},{6,7},{7,6},{8,9},{9,8},{10,11... | collective-permute-start | bytes 1179656 | tf_op jit(solution)/shard_map/ppermute | solution.py:219
  109.7 1.1 copy-start.11
  111.6 16.9 %all-to-all-start.7 = ((bf16[4,64,768]{2,1,0:T(8,128)(2,1)}), bf16[4,64,768]{2,1,0:T(8,128)(2,1)S(1)}, u32[]{:S(2)}, u32[]{:S(2)}) async-start(bf16[4,64,768]{2,1,0:T(8,128)(2,1)} %add_halves.7), calls=%async_computation.7 | async-start | bytes 786432 | tf_op jit(solution)/shard_map/all_to_all | solution.py:211
  115.4 2.3 %copy-start.23 = (bf16[1,1024,3,768]{3,1,2,0:T(8,128)(2,1)S(1)}, bf16[1,1024,3,768]{3,1,2,0:T(8,128)(2,1)}, u32[]{:S(2)}) copy-start(bf16[1,1024,3,768]{3,1,2,0:T(8,128)(2,1)} %param.9) | copy-start | bytes 14155780
  117.8 1.2 copy-start.29
  119.0 1.2 copy-start.31
  124.6 1.3 copy-start
  126.0 1.7 %collective-permute-start.8 = (bf16[4,64,768]{2,1,0:T(8,128)(2,1)S(1)}, bf16[4,64,768]{2,1,0:T(8,128)(2,1)S(1)}, u32[]{:S(2)}, u32[]{:S(2)}) collective-permute-start(bf16[4,64,768]{2,1,0:T(8,128)(2,1)S(1)} %get-tuple-element.35), channel_id=1, source_target_pairs={{0,1},{1,0},{2,3},{3,2},{4,5},{5,4},{6,7},{7,6},{8,9},{9,8},{10,11... | collective-permute-start | bytes 1179656 | tf_op jit(solution)/shard_map/ppermute | solution.py:219
  128.5 33.1 %all-to-all-start.5 = ((bf16[4,64,768]{2,1,0:T(8,128)(2,1)}), bf16[4,64,768]{2,1,0:T(8,128)(2,1)S(1)}, u32[]{:S(2)}, u32[]{:S(2)}) async-start(bf16[4,64,768]{2,1,0:T(8,128)(2,1)} %add_halves.6), calls=%async_computation.5 | async-start | bytes 786432 | tf_op jit(solution)/shard_map/all_to_all | solution.py:211
  132.7 6.1 %collective-permute-start.13 = (f32[128,2]{1,0:T(8,128)S(1)}, f32[128,2]{1,0:T(8,128)S(1)}, u32[]{:S(2)}, u32[]{:S(2)}) collective-permute-start(f32[128,2]{1,0:T(8,128)S(1)} %get-tuple-element.43), channel_id=1, source_target_pairs={{0,8},{2,10},{4,12},{6,14},{8,0},{10,2},{12,4},{14,6},{1,9},{3,11}... | collective-permute-start | bytes 3080 | tf_op jit(solution)/shard_map/ppermute | solution.py:216
  140.5 21.1 %collective-permute-start.12 = (bf16[128,768]{1,0:T(8,128)(2,1)}, bf16[128,768]{1,0:T(8,128)(2,1)S(1)}, u32[]{:S(2)}, u32[]{:S(2)}) collective-permute-start(bf16[128,768]{1,0:T(8,128)(2,1)} %relay_sum.1), channel_id=1, source_target_pairs={{0,8},{2,10},{4,12},{6,14},{8,0},{10,2},{12,4},{14,6},{1,9},{3,11}... | collective-permute-start | bytes 589832 | tf_op jit(solution)/shard_map/ppermute | solution.py:216
  144.0 1.6 copy-start.1
  145.6 1.0 copy-start.3
  146.6 1.0 copy-start.5
  147.6 1.2 copy-start.7
  148.8 1.2 copy-start.9
  150.0 1.0 copy-start.13
  151.0 1.0 copy-start.15
  152.0 1.0 copy-start.17
  (4 other events, 3.8 us)

commit v3 on v2

v3 whole, which is shorter than its diff:
```python
import functools

import jax
import jax.numpy as jnp
from jax import lax
from jax.experimental import pallas as pl
from jax.experimental.pallas import tpu as pltpu
from jax.sharding import PartitionSpec as P

PLAIN = (((1,), (0,)), ((), ()))
LAST = (((1,), (1,)), ((), ()))
FIRST = (((0,), (0,)), ((), ()))
MIB = 1024 * 1024
F32 = jnp.float32
BF16 = jnp.bfloat16


def dot(a, b, dims=PLAIN):
    return lax.dot_general(a, b, dims, preferred_element_type=F32)


def slot_masks(me, meta, pieces, capacity):
    tok = meta.shape[1]
    expert_of = (lax.broadcasted_iota(jnp.int32, (pieces, tok), 0) ^ me).astype(F32)
    first, second = meta[0:1, :] == expert_of, meta[1:2, :] == expert_of
    chosen = jnp.where(first | second, 1.0, 0.0).astype(BF16)
    before = lax.broadcasted_iota(jnp.int32, (tok, tok), 0) < lax.broadcasted_iota(
        jnp.int32, (tok, tok), 1
    )
    rank = dot(chosen, jnp.where(before, 1.0, 0.0).astype(BF16))
    rank0 = jnp.where(first, rank, -1.0)
    rank1 = jnp.where(second, rank, -1.0)
    place = lax.broadcasted_iota(jnp.int32, (capacity, tok), 0).astype(F32)

    def expand(ranks):
        return jnp.concatenate(
            [
                jnp.where(ranks[s : s + 1, :] == place, 1.0, 0.0).astype(BF16)
                for s in range(pieces)
            ],
            axis=0,
        )

    return expand(rank0), expand(rank1)


def put(refs, rows):
    capacity = refs[0].shape[0]
    for s, ref in enumerate(refs):
        ref[...] = rows[s * capacity : (s + 1) * capacity].astype(ref.dtype)


def get(refs):
    return jnp.concatenate([ref[...] for ref in refs], axis=0)


def masks_of(me_ref, meta, refs):
    return slot_masks(me_ref[0], meta, len(refs), refs[0].shape[0])


def gate_columns(meta):
    columns = meta.T
    return columns[:, 2:3], columns[:, 3:4]


def route_sums(me_ref, meta, refs):
    m0, m1 = masks_of(me_ref, meta, refs)
    got = get(refs)
    g0, g1 = gate_columns(meta)
    o0, o1 = dot(m0, got, FIRST), dot(m1, got, FIRST)
    return m0, m1, g0, g1, o0, o1, g0 * o0 + g1 * o1


def put_d_gates(ref, diff, o0, o1):
    tok = diff.shape[0]
    lane = lax.broadcasted_iota(jnp.int32, (tok, 128), 1)
    d0 = jnp.sum(diff * o0, axis=1, keepdims=True)
    d1 = jnp.sum(diff * o1, axis=1, keepdims=True)
    ref[...] = jnp.where(lane == 0, d0, jnp.where(lane == 1, d1, 0.0)).T[0:2, :]


def put_route_grads(refs, m0, m1, g0, g1, diff):
    grads = jnp.concatenate([(g0 * diff).astype(BF16), (g1 * diff).astype(BF16)], axis=0)
    put(refs, dot(jnp.concatenate([m0, m1], axis=1), grads))


def pack_near_kernel(me_ref, routes_ref, gates_ref, tokens_ref, meta_ref, *rows_refs):
    meta = jnp.concatenate(
        [
            routes_ref[...].astype(F32),
            gates_ref[...],
            jnp.zeros((4, routes_ref.shape[1]), F32),
        ],
        axis=0,
    )
    meta_ref[...] = meta
    m0, m1 = masks_of(me_ref, meta, rows_refs)
    put(rows_refs, dot(m0 + m1, tokens_ref[...]))


def pack_far_kernel(me_ref, meta_ref, tokens_ref, *rows_refs):
    m0, m1 = masks_of(me_ref, meta_ref[...], rows_refs)
    put(rows_refs, dot(m0 + m1, tokens_ref[...]))


def forward_kernel(pieces, chunk, own_ref, other_ref, *refs):
    ins, outs, refs = refs[:pieces], refs[pieces : 2 * pieces], refs[2 * pieces :]
    x_ref, hid_own_ref, hid_other_ref, fa_ref, fb_ref = refs
    x = get(ins)
    x_ref[...] = x
    units = own_ref.shape[1]
    for w_ref, hid_ref, first in ((own_ref, hid_own_ref, 0), (other_ref, hid_other_ref, units)):
        for j in range(0, units, chunk):
            sl = slice(j, j + chunk)
            to = slice(first + j, first + j + chunk)
            gate = dot(x, w_ref[0, sl, :], LAST)
            up = dot(x, w_ref[1, sl, :], LAST)
            sig = 0.5 * jnp.tanh(0.5 * gate) + 0.5
            silu = gate * sig
            hid_ref[:, sl] = (silu * up).astype(BF16)
            fa_ref[:, to] = (up * (sig + silu * (1.0 - sig))).astype(BF16)
            fb_ref[:, to] = silu.astype(BF16)
    put(outs, dot(hid_own_ref[...], own_ref[2]) + dot(hid_other_ref[...], other_ref[2]))


def backward_kernel(pieces, chunk, own_ref, other_ref, fa_ref, fb_ref, *refs):
    ins, outs, refs = refs[:pieces], refs[pieces : 2 * pieces], refs[2 * pieces :]
    rg_ref, dgu_own_ref, dgu_other_ref = refs
    rg = get(ins)
    rg_ref[...] = rg
    units, width = own_ref.shape[1:]
    for w_ref, dgu_ref, first in ((own_ref, dgu_own_ref, 0), (other_ref, dgu_other_ref, units)):
        for j in range(0, units, chunk):
            sl = slice(j, j + chunk)
            at = slice(first + j, first + j + chunk)
            dh = dot(rg, w_ref[2, sl, :], LAST)
            dgu_ref[:, sl] = (dh * fa_ref[:, at].astype(F32)).astype(BF16)
            dgu_ref[:, units + j : units + j + chunk] = (dh * fb_ref[:, at].astype(F32)).astype(BF16)
    put(
        outs,
        dot(dgu_own_ref[...], own_ref[0:2].reshape(2 * units, width))
        + dot(dgu_other_ref[...], other_ref[0:2].reshape(2 * units, width)),
    )


def near_sum_kernel(me_ref, meta_ref, teacher_ref, *refs):
    ins, out_ref = refs[:-1], refs[-1]
    total = route_sums(me_ref, meta_ref[...], ins)[-1]
    out_ref[...] = (total - teacher_ref[...].astype(F32)).astype(BF16)


def far_sum_kernel(me_ref, meta_ref, *refs):
    ins, out_ref = refs[:-1], refs[-1]
    out_ref[...] = route_sums(me_ref, meta_ref[...], ins)[-1].astype(BF16)


def far_grad_kernel(pieces, me_ref, meta_ref, rest_ref, *refs):
    ins, d_gates_ref, outs = refs[:pieces], refs[pieces], refs[pieces + 1 :]
    m0, m1, g0, g1, o0, o1, total = route_sums(me_ref, meta_ref[...], ins)
    diff = total + rest_ref[...].astype(F32)
    put_route_grads(outs, m0, m1, g0, g1, diff)
    put_d_gates(d_gates_ref, diff, o0, o1)


def near_grad_kernel(pieces, me_ref, meta_ref, teacher_ref, part_ref, *refs):
    ins, student_ref, d_gates_ref, outs = (
        refs[:pieces],
        refs[pieces],
        refs[pieces + 1],
        refs[pieces + 2 :],
    )
    m0, m1, g0, g1, o0, o1, total = route_sums(me_ref, meta_ref[...], ins)
    total = total + part_ref[...].astype(F32)
    student_ref[...] = total.astype(BF16)
    diff = total - teacher_ref[...].astype(F32)
    put_route_grads(outs, m0, m1, g0, g1, diff)
    put_d_gates(d_gates_ref, diff, o0, o1)


def far_back_kernel(me_ref, meta_ref, *refs):
    ins, out_ref = refs[:-1], refs[-1]
    m0, m1 = masks_of(me_ref, meta_ref[...], ins)
    out_ref[...] = dot(m0 + m1, get(ins), FIRST).astype(BF16)


def final_kernel(pieces, me_ref, meta_ref, part_ref, near_ref, far_ref, *refs):
    ins, out_ref, d_gates_ref = refs[:pieces], refs[pieces], refs[pieces + 1]
    m0, m1 = masks_of(me_ref, meta_ref[...], ins)
    total = dot(m0 + m1, get(ins), FIRST) + part_ref[...].astype(F32)
    out_ref[...] = total.astype(BF16)
    d_gates_ref[...] = near_ref[...] + far_ref[...]


def weight_kernel(*refs):
    xs, rgs, gates, ups, hids, out_ref = (
        refs[0:4],
        refs[4:8],
        refs[8:12],
        refs[12:16],
        refs[16:20],
        refs[20],
    )
    for m, (acts, rows) in enumerate(((gates, xs), (ups, xs), (hids, rgs))):
        term = dot(acts[0][...], rows[0][...], FIRST)
        for i in range(1, 4):
            term = term + dot(acts[i][...], rows[i][...], FIRST)
        out_ref[m] = term.astype(BF16)


def local(tokens, teacher, routes, gate_weights, weights):
    tok, width = tokens.shape
    experts = lax.axis_size("expert")
    half = experts // 2
    capacity = 4 * tok // experts
    rows = half * capacity
    units = weights.shape[1]
    chunk = min(256, units)
    me = lax.axis_index("expert").reshape(1)

    pieces = [jax.ShapeDtypeStruct((capacity, width), BF16)] * half
    dense = jax.ShapeDtypeStruct((tok, width), BF16)
    pair = jax.ShapeDtypeStruct((2, tok), F32)
    flat = jax.ShapeDtypeStruct((rows, width), BF16)
    acts = jax.ShapeDtypeStruct((rows, units), BF16)
    acts2 = jax.ShapeDtypeStruct((rows, 2 * units), BF16)
    vspec = pl.BlockSpec(memory_space=pltpu.VMEM)
    sspec = pl.BlockSpec(memory_space=pltpu.SMEM)
    matmul = 4 * rows * width * units

    def call(kernel, name, out_shape, scalars, *args, flops=10**8, limit=8):
        many = isinstance(out_shape, list)
        return pl.pallas_call(
            kernel,
            in_specs=[sspec] * scalars + [vspec] * (len(args) - scalars),
            out_specs=[vspec] * len(out_shape) if many else vspec,
            out_shape=out_shape,
            cost_estimate=pl.CostEstimate(
                flops=flops, bytes_accessed=2 * MIB, transcendentals=0
            ),
            compiler_params=pltpu.CompilerParams(vmem_limit_bytes=limit * MIB),
            name=name,
        )(*args)

    def within_half(rows_of):
        got = [rows_of[0]] + [None] * (half - 1)
        for s in range(half - 1, 0, -1):
            got[s] = lax.ppermute(rows_of[s], "expert", [(i, i ^ s) for i in range(experts)])
        return got

    def to_mirror(x):
        return lax.ppermute(x, "expert", [(i, i ^ half) for i in range(experts)])

    def to_sibling(x):
        return lax.ppermute(x, "dp", [(0, 1), (1, 0)])

    far_tokens = to_mirror(tokens)
    own = weights[0].transpose(1, 0, 2)
    other = to_sibling(own)

    def forward(x_pieces, name):
        res = call(
            functools.partial(forward_kernel, half, chunk),
            name,
            pieces + [flat] + [acts] * 2 + [acts2] * 2,
            0,
            own,
            other,
            *x_pieces,
            flops=3 * matmul,
            limit=20,
        )
        return res[:half], res[half:]

    def backward(rg_pieces, fa, fb, name):
        res = call(
            functools.partial(backward_kernel, half, chunk),
            name,
            pieces + [flat] + [acts2] * 2,
            0,
            own,
            other,
            fa,
            fb,
            *rg_pieces,
            flops=3 * matmul,
            limit=20,
        )
        return res[:half], res[half:]

    res = call(
        pack_near_kernel,
        "pack_near",
        [jax.ShapeDtypeStruct((8, tok), F32)] + pieces,
        1,
        me,
        routes.T,
        gate_weights.T,
        tokens,
    )
    meta, x_near = res[0], within_half(res[1:])
    far_meta = to_mirror(meta)
    x_far = within_half(call(pack_far_kernel, "pack_far", pieces, 1, me, far_meta, far_tokens))

    out_near, (xn, hn, hn_other, fan, fbn) = forward(x_near, "forward_near")
    got_near = within_half(out_near)
    rest = to_mirror(
        call(near_sum_kernel, "near_sum", dense, 1, me, meta, teacher, *got_near)
    )
    out_far, (xf, hf, hf_other, faf, fbf) = forward(x_far, "forward_far")
    got_far = within_half(out_far)
    part = to_mirror(call(far_sum_kernel, "far_sum", dense, 1, me, far_meta, *got_far))

    res = call(
        functools.partial(far_grad_kernel, half),
        "far_grad",
        [pair] + pieces,
        1,
        me,
        far_meta,
        rest,
        *got_far,
    )
    d_gates_far, rg_far = to_mirror(res[0]), within_half(res[1:])
    res = call(
        functools.partial(near_grad_kernel, half),
        "near_grad",
        [dense, pair] + pieces,
        1,
        me,
        meta,
        teacher,
        part,
        *got_near,
    )
    student, d_gates_near, rg_near = res[0], res[1], within_half(res[2:])

    grad_far, (rf, df, df_other) = backward(rg_far, faf, fbf, "backward_far")
    back_far = within_half(grad_far)
    part = to_mirror(call(far_back_kernel, "far_back", dense, 1, me, far_meta, *back_far))
    grad_near, (rn, dn, dn_other) = backward(rg_near, fan, fbn, "backward_near")
    back_near = within_half(grad_near)

    whole = pl.BlockSpec((rows, width), lambda i: (0, 0))
    steps = units // chunk
    column = lambda first: pl.BlockSpec((rows, chunk), lambda i: (0, first + i))
    xs = [xf, xn, to_sibling(xf), to_sibling(xn)]
    rgs = [rf, rn, to_sibling(rf), to_sibling(rn)]
    dgus = [df, dn, to_sibling(df_other), to_sibling(dn_other)]
    hids = [hf, hn, to_sibling(hf_other), to_sibling(hn_other)]
    weight_grads = pl.pallas_call(
        weight_kernel,
        grid=(steps,),
        in_specs=[whole] * 8 + [column(0)] * 4 + [column(steps)] * 4 + [column(0)] * 4,
        out_specs=pl.BlockSpec((3, chunk, width), lambda i: (0, i, 0)),
        out_shape=jax.ShapeDtypeStruct((3, units, width), BF16),
        cost_estimate=pl.CostEstimate(
            flops=3 * matmul * 2, bytes_accessed=16 * MIB, transcendentals=0
        ),
        compiler_params=pltpu.CompilerParams(vmem_limit_bytes=20 * MIB),
        name="weight_gradients",
    )(*xs, *rgs, *dgus, *dgus, *hids)

    d_tokens, d_gates = call(
        functools.partial(final_kernel, half),
        "combine_gradients",
        [dense, pair],
        1,
        me,
        meta,
        part,
        d_gates_near,
        d_gates_far,
        *back_near,
    )
    return (student, d_tokens, d_gates.T, weight_grads.transpose(1, 0, 2)[None])


def solution(mesh):
    rows = P(("groups", "expert", "dp"), None)
    return jax.shard_map(
        local,
        mesh=mesh,
        in_specs=(rows, rows, rows, rows, P("expert", "dp", None, None)),
        out_specs=(rows, rows, rows, P(("groups", "expert"), "dp", None, None)),
        check_vma=False,
    )
```

time: 164 us -> 120 us (0.73)
  local copies, waits for them, and re-layouts: 34.5 us -> 4.67 us
  blocking collectives: 19 us -> 0 us
  starting transfers between devices: 40.2 us -> 46.2 us
  Pallas kernels: 32.3 us -> 36 us
  waiting for transfers between devices: 34.4 us -> 32.4 us
    unnamed x65 -> x14, local copies, waits for them, and re-layouts: 34.4 us -> 4.67 us
    ppermute x6 -> x30, starting transfers between devices: 15.1 us -> 44 us  [the longest x24 29.6 us: within_half(): lax.ppermute(rows_of[s], 'expert', [(i, i ^ s) for i in range(experts)])]
    all_to_all x6 -> x0, starting transfers between devices: 23.8 us -> none  [within_half(): lax.all_to_all(x, 'expert', split_axis=0, concat_axis=0, axis_index_group...]
    all_to_all x2 -> x0, blocking collectives: 19 us -> none  [within_half(): lax.all_to_all(x, 'expert', split_axis=0, concat_axis=0, axis_index_group...]
    ppermute x6 -> x30, waiting for transfers between devices: 20.9 us -> 31.7 us  [the longest x6 18.5 us: to_mirror(): return lax.ppermute(x, 'expert', [(i, i ^ half) for i in range(experts)])]
    all_to_all x6 -> x0, waiting for transfers between devices: 7.24 us -> none  [within_half(): lax.all_to_all(x, 'expert', split_axis=0, concat_axis=0, axis_index_group...]
    ppermute x8 -> x9, waiting for transfers between devices: 6.25 us -> 0.67 us  [to_sibling(): return lax.ppermute(x, 'dp', [(0, 1), (1, 0)])]
    pallas_call x15 -> x12, Pallas kernels: 23.7 us -> 28.1 us  [call(): pl.pallas_call(kernel, in_specs=[sspec] * scalars + [vspec] * (len(args)...]
  transfers between devices with their start and end apart: 20 -> 39, of which waited for: 8 -> 13; matrix products, arithmetic and copies ran while one was open for 1% -> 0% of each run, Pallas kernels for 18% -> 23%
where the time goes in v3:
time: 120 us
  starting transfers between devices  46.2 us (38%)
  Pallas kernels  36 us (30%)
  waiting for transfers between devices  32.4 us (27%)
  local copies, waits for them, and re-layouts  4.67 us (4%)
    ppermute x24, starting transfers between devices, within_half(): lax.ppermute(rows_of[s], 'expert', [(i, i ^ s) for i in range(experts)])  29.6 us
    pallas_call x12, Pallas kernels, call(): pl.pallas_call(kernel, in_specs=[sspec] * scalars + [vspec] * (len(args)...  28.1 us
    ppermute x6, waiting for transfers between devices, to_mirror(): return lax.ppermute(x, 'expert', [(i, i ^ half) for i in range(experts)])  18.5 us
    ppermute x6, starting transfers between devices, to_mirror(): return lax.ppermute(x, 'expert', [(i, i ^ half) for i in range(experts)])  14.5 us
    ppermute x24, waiting for transfers between devices, within_half(): lax.ppermute(rows_of[s], 'expert', [(i, i ^ s) for i in range(experts)])  13.3 us
    pallas_call x1, Pallas kernels, local(): pl.pallas_call(weight_kernel, grid=(steps,), in_specs=[whole] * 8 + [colu...  7.87 us
    unnamed x14, local copies, waits for them, and re-layouts  4.67 us
  transfers between devices with their start and end apart: 39, of which 13 were waited for; matrix products, arithmetic and copies ran while one was open for 0% of the time, Pallas kernels for 23%

profile of v3, /device:TPU:0, one launch (start us, length us, event | category | flops | bytes accessed | tf_op | source)
XLA Modules:
  0.0 120.1 jit_solution(15153068764995444175)
XLA Ops:
  1.1 3.7 %collective-permute-start.2 = (bf16[128,768]{1,0:T(8,128)(2,1)}, bf16[128,768]{1,0:T(8,128)(2,1)S(1)}, u32[]{:S(2)}, u32[]{:S(2)}) collective-permute-start(bf16[128,768]{1,0:T(8,128)(2,1)} %tokens_ref.1), channel_id=1, source_target_pairs={{0,8},{2,10},{4,12},{6,14},{8,0},{10,2},{12,4},{14,6},{1,9},{3,11}... | collective-permute-start | bytes 589832 | tf_op jit(solution)/shard_map/ppermute | solution.py:251
  4.8 1.0 copy-done.2
  5.8 0.7 copy-done.3
  6.5 0.7 copy-done.4
  7.6 1.8 %collective-permute-start.10 = (bf16[64,768]{1,0:T(8,128)(2,1)S(1)}, bf16[64,768]{1,0:T(8,128)(2,1)S(1)}, u32[]{:S(2)}, u32[]{:S(2)}) collective-permute-start(bf16[64,768]{1,0:T(8,128)(2,1)S(1)} %get-tuple-element.68), channel_id=1, source_target_pairs={{0,2},{2,0},{4,6},{6,4},{8,10},{10,8},{12,14},{14,12},{1,3},{3,1},... | collective-permute-start | bytes 294920 | tf_op jit(solution)/shard_map/ppermute | solution.py:247
  9.4 1.6 %collective-permute-start.11 = (bf16[64,768]{1,0:T(8,128)(2,1)S(1)}, bf16[64,768]{1,0:T(8,128)(2,1)S(1)}, u32[]{:S(2)}, u32[]{:S(2)}) collective-permute-start(bf16[64,768]{1,0:T(8,128)(2,1)S(1)} %get-tuple-element.69), channel_id=1, source_target_pairs={{0,4},{2,6},{4,0},{6,2},{8,12},{10,14},{12,8},{14,10},{1,5},{3,7},... | collective-permute-start | bytes 294920 | tf_op jit(solution)/shard_map/ppermute | solution.py:247
  11.0 4.0 %collective-permute-done.meta_ref = f32[8,128]{1,0:T(8,128)S(1)} collective-permute-done((f32[8,128]{1,0:T(8,128)S(1)}, f32[8,128]{1,0:T(8,128)S(1)}, u32[]{:S(2)}, u32[]{:S(2)}) %collective-permute-start) | collective-permute-done | bytes 4128 | tf_op jit(solution)/shard_map/ppermute | solution.py:251
  15.0 1.7 %collective-permute-start.12 = (bf16[64,768]{1,0:T(8,128)(2,1)S(1)}, bf16[64,768]{1,0:T(8,128)(2,1)S(1)}, u32[]{:S(2)}, u32[]{:S(2)}) collective-permute-start(bf16[64,768]{1,0:T(8,128)(2,1)S(1)} %get-tuple-element.70), channel_id=1, source_target_pairs={{0,6},{2,4},{4,2},{6,0},{8,14},{10,12},{12,10},{14,8},{1,7},{3,5},... | collective-permute-start | bytes 294920 | tf_op jit(solution)/shard_map/ppermute | solution.py:247
  17.7 1.2 %collective-permute-start.4 = (bf16[64,768]{1,0:T(8,128)(2,1)S(1)}, bf16[64,768]{1,0:T(8,128)(2,1)S(1)}, u32[]{:S(2)}, u32[]{:S(2)}) collective-permute-start(bf16[64,768]{1,0:T(8,128)(2,1)S(1)} %get-tuple-element.61), channel_id=1, source_target_pairs={{0,4},{2,6},{4,0},{6,2},{8,12},{10,14},{12,8},{14,10},{1,5},{3,7},... | collective-permute-start | bytes 294920 | tf_op jit(solution)/shard_map/ppermute | solution.py:247
  18.9 1.7 %collective-permute-start.5 = (bf16[64,768]{1,0:T(8,128)(2,1)S(1)}, bf16[64,768]{1,0:T(8,128)(2,1)S(1)}, u32[]{:S(2)}, u32[]{:S(2)}) collective-permute-start(bf16[64,768]{1,0:T(8,128)(2,1)S(1)} %get-tuple-element.62), channel_id=1, source_target_pairs={{0,6},{2,4},{4,2},{6,0},{8,14},{10,12},{12,10},{14,8},{1,7},{3,5},... | collective-permute-start | bytes 294920 | tf_op jit(solution)/shard_map/ppermute | solution.py:247
  20.7 2.3 %copy-done = bf16[1,1024,3,768]{3,1,2,0:T(8,128)(2,1)S(1)} copy-done((bf16[1,1024,3,768]{3,1,2,0:T(8,128)(2,1)S(1)}, bf16[1,1024,3,768]{3,1,2,0:T(8,128)(2,1)}, u32[]{:S(2)}) %copy-start) | copy-done | bytes 4718616
  23.0 5.4 %forward_near.1 = (bf16[64,768]{1,0:T(8,128)(2,1)S(1)}, bf16[64,768]{1,0:T(8,128)(2,1)S(1)}, bf16[64,768]{1,0:T(8,128)(2,1)S(1)}, bf16[64,768]{1,0:T(8,128)(2,1)...) custom-call(bf16[3,1024,768]{2,1,0:T(8,128)(2,1)S(1)} %bitcast.11, ...), custom_call_target="tpu_custom_call" | custom-call | flops 2415919104 | bytes 2097152 | tf_op jit(solution)/shard_map/forward_near/pallas_call | solution.py:232
  28.4 2.4 %collective-permute-start.13 = (bf16[64,768]{1,0:T(8,128)(2,1)S(1)}, bf16[64,768]{1,0:T(8,128)(2,1)S(1)}, u32[]{:S(2)}, u32[]{:S(2)}) collective-permute-start(bf16[64,768]{1,0:T(8,128)(2,1)S(1)} %get-tuple-element.72), channel_id=1, source_target_pairs={{0,2},{2,0},{4,6},{6,4},{8,10},{10,8},{12,14},{14,12},{1,3},{3,1},... | collective-permute-start | bytes 294920 | tf_op jit(solution)/shard_map/ppermute | solution.py:247
  30.8 0.7 collective-permute-start.14
  31.5 0.8 collective-permute-start.15
  32.3 5.6 %forward_far.1 = (bf16[64,768]{1,0:T(8,128)(2,1)S(1)}, bf16[64,768]{1,0:T(8,128)(2,1)S(1)}, bf16[64,768]{1,0:T(8,128)(2,1)S(1)}, bf16[64,768]{1,0:T(8,128)(2,1)S...) custom-call(bf16[3,1024,768]{2,1,0:T(8,128)(2,1)S(1)} %bitcast.12, ...), custom_call_target="tpu_custom_call" | custom-call | flops 2415919104 | bytes 2097152 | tf_op jit(solution)/shard_map/forward_far/pallas_call | solution.py:232
  37.9 2.0 %collective-permute-start.6 = (bf16[64,768]{1,0:T(8,128)(2,1)S(1)}, bf16[64,768]{1,0:T(8,128)(2,1)S(1)}, u32[]{:S(2)}, u32[]{:S(2)}) collective-permute-start(bf16[64,768]{1,0:T(8,128)(2,1)S(1)} %get-tuple-element.64), channel_id=1, source_target_pairs={{0,2},{2,0},{4,6},{6,4},{8,10},{10,8},{12,14},{14,12},{1,3},{3,1},... | collective-permute-start | bytes 294920 | tf_op jit(solution)/shard_map/ppermute | solution.py:247
  39.9 0.7 collective-permute-start.7
  40.6 0.8 collective-permute-start.8
  42.0 3.1 %collective-permute-start.16 = (bf16[128,768]{1,0:T(8,128)(2,1)S(1)}, bf16[128,768]{1,0:T(8,128)(2,1)S(1)}, u32[]{:S(2)}, u32[]{:S(2)}) collective-permute-start(bf16[128,768]{1,0:T(8,128)(2,1)S(1)} %near_sum.1), channel_id=1, source_target_pairs={{0,8},{2,10},{4,12},{6,14},{8,0},{10,2},{12,4},{14,6},{1,9},{3,11}... | collective-permute-start | bytes 589832 | tf_op jit(solution)/shard_map/ppermute | solution.py:251
  45.2 2.4 %collective-permute-done.8.refs_3_ = bf16[64,768]{1,0:T(8,128)(2,1)S(1)} collective-permute-done((bf16[64,768]{1,0:T(8,128)(2,1)S(1)}, bf16[64,768]{1,0:T(8,128)(2,1)S(1)}, u32[]{:S(2)}, u32[]{:S(2)}) %collective-permute-start.8) | collective-permute-done | bytes 98336 | tf_op jit(solution)/shard_map/ppermute | solution.py:247
  48.1 3.3 %collective-permute-start.9 = (bf16[128,768]{1,0:T(8,128)(2,1)S(1)}, bf16[128,768]{1,0:T(8,128)(2,1)S(1)}, u32[]{:S(2)}, u32[]{:S(2)}) collective-permute-start(bf16[128,768]{1,0:T(8,128)(2,1)S(1)} %far_sum.1), channel_id=1, source_target_pairs={{0,8},{2,10},{4,12},{6,14},{8,0},{10,2},{12,4},{14,6},{1,9},{3,11}... | collective-permute-start | bytes 589832 | tf_op jit(solution)/shard_map/ppermute | solution.py:251
  51.4 6.2 %collective-permute-done.16.rest_ref = bf16[128,768]{1,0:T(8,128)(2,1)S(1)} collective-permute-done((bf16[128,768]{1,0:T(8,128)(2,1)S(1)}, bf16[128,768]{1,0:T(8,128)(2,1)S(1)}, u32[]{:S(2)}, u32[]{:S(2)}) %collective-permute-start.16) | collective-permute-done | bytes 196640 | tf_op jit(solution)/shard_map/ppermute | solution.py:251
  57.6 0.8 far_grad.1
  58.4 1.4 %collective-permute-start.17 = (bf16[64,768]{1,0:T(8,128)(2,1)S(1)}, bf16[64,768]{1,0:T(8,128)(2,1)S(1)}, u32[]{:S(2)}, u32[]{:S(2)}) collective-permute-start(bf16[64,768]{1,0:T(8,128)(2,1)S(1)} %get-tuple-element.79), channel_id=1, source_target_pairs={{0,2},{2,0},{4,6},{6,4},{8,10},{10,8},{12,14},{14,12},{1,3},{3,1},... | collective-permute-start | bytes 294920 | tf_op jit(solution)/shard_map/ppermute | solution.py:247
  59.8 2.1 %collective-permute-start.19 = (bf16[64,768]{1,0:T(8,128)(2,1)S(1)}, bf16[64,768]{1,0:T(8,128)(2,1)S(1)}, u32[]{:S(2)}, u32[]{:S(2)}) collective-permute-start(bf16[64,768]{1,0:T(8,128)(2,1)S(1)} %get-tuple-element.81), channel_id=1, source_target_pairs={{0,6},{2,4},{4,2},{6,0},{8,14},{10,12},{12,10},{14,8},{1,7},{3,5},... | collective-permute-start | bytes 294920 | tf_op jit(solution)/shard_map/ppermute | solution.py:247
  62.4 1.2 %near_grad.1 = (bf16[128,768]{1,0:T(8,128)(2,1)}, f32[2,128]{1,0:T(2,128)S(1)}, bf16[64,768]{1,0:T(8,128)(2,1)S(1)}, bf16[64,768]{1,0:T(8,128)(2,1)S(1)}, bf16[6...) custom-call(s32[1]{0:T(128)} %bitcast.me_ref, f32[8,128]{1,0:T(8,128)S(1)} %get-tuple-element.58.meta_ref, ...), custom_call_target="tpu_custom_call" | custom-call | flops 100000000 | bytes 2097152 | tf_op jit(solution)/shard_map/near_grad/pallas_call | solution.py:232
  63.7 1.4 %collective-permute-start.25 = (bf16[64,768]{1,0:T(8,128)(2,1)S(1)}, bf16[64,768]{1,0:T(8,128)(2,1)S(1)}, u32[]{:S(2)}, u32[]{:S(2)}) collective-permute-start(bf16[64,768]{1,0:T(8,128)(2,1)S(1)} %get-tuple-element.91), channel_id=1, source_target_pairs={{0,2},{2,0},{4,6},{6,4},{8,10},{10,8},{12,14},{14,12},{1,3},{3,1},... | collective-permute-start | bytes 294920 | tf_op jit(solution)/shard_map/ppermute | solution.py:247
  65.5 1.9 %collective-permute-start.27 = (bf16[64,768]{1,0:T(8,128)(2,1)S(1)}, bf16[64,768]{1,0:T(8,128)(2,1)S(1)}, u32[]{:S(2)}, u32[]{:S(2)}) collective-permute-start(bf16[64,768]{1,0:T(8,128)(2,1)S(1)} %get-tuple-element.93), channel_id=1, source_target_pairs={{0,6},{2,4},{4,2},{6,0},{8,14},{10,12},{12,10},{14,8},{1,7},{3,5},... | collective-permute-start | bytes 294920 | tf_op jit(solution)/shard_map/ppermute | solution.py:247
  67.5 5.9 %backward_far.1 = (bf16[64,768]{1,0:T(8,128)(2,1)S(1)}, bf16[64,768]{1,0:T(8,128)(2,1)S(1)}, bf16[64,768]{1,0:T(8,128)(2,1)S(1)}, bf16[64,768]{1,0:T(8,128)(2,1)...) custom-call(bf16[3,1024,768]{2,1,0:T(8,128)(2,1)S(1)} %bitcast.15, ...), custom_call_target="tpu_custom_call" | custom-call | flops 2415919104 | bytes 2097152 | tf_op jit(solution)/shard_map/backward_far/pallas_call | solution.py:232
  73.5 6.1 %backward_near.1 = (bf16[64,768]{1,0:T(8,128)(2,1)S(1)}, bf16[64,768]{1,0:T(8,128)(2,1)S(1)}, bf16[64,768]{1,0:T(8,128)(2,1)S(1)}, bf16[64,768]{1,0:T(8,128)(2,1...) custom-call(bf16[3,1024,768]{2,1,0:T(8,128)(2,1)S(1)} %bitcast.16, ...), custom_call_target="tpu_custom_call" | custom-call | flops 2415919104 | bytes 2097152 | tf_op jit(solution)/shard_map/backward_near/pallas_call | solution.py:232
  80.2 2.2 %collective-permute-start.24 = (f32[2,128]{1,0:T(2,128)S(1)}, f32[2,128]{1,0:T(2,128)S(1)}, u32[]{:S(2)}, u32[]{:S(2)}) collective-permute-start(f32[2,128]{1,0:T(2,128)S(1)} %get-tuple-element.87), channel_id=1, source_target_pairs={{0,8},{2,10},{4,12},{6,14},{8,0},{10,2},{12,4},{14,6},{1,9},{3,11}... | collective-permute-start | bytes 3080 | tf_op jit(solution)/shard_map/ppermute | solution.py:251
  82.3 2.3 %collective-permute-done.24.far_ref = f32[2,128]{1,0:T(2,128)S(1)} collective-permute-done((f32[2,128]{1,0:T(2,128)S(1)}, f32[2,128]{1,0:T(2,128)S(1)}, u32[]{:S(2)}, u32[]{:S(2)}) %collective-permute-start.24) | collective-permute-done | bytes 1056 | tf_op jit(solution)/shard_map/ppermute | solution.py:251
  84.6 1.4 %collective-permute-start.20 = (bf16[64,768]{1,0:T(8,128)(2,1)S(1)}, bf16[64,768]{1,0:T(8,128)(2,1)S(1)}, u32[]{:S(2)}, u32[]{:S(2)}) collective-permute-start(bf16[64,768]{1,0:T(8,128)(2,1)S(1)} %get-tuple-element.83), channel_id=1, source_target_pairs={{0,2},{2,0},{4,6},{6,4},{8,10},{10,8},{12,14},{14,12},{1,3},{3,1},... | collective-permute-start | bytes 294920 | tf_op jit(solution)/shard_map/ppermute | solution.py:247
  86.4 3.5 %collective-permute-done.20.refs_1_ = bf16[64,768]{1,0:T(8,128)(2,1)S(1)} collective-permute-done((bf16[64,768]{1,0:T(8,128)(2,1)S(1)}, bf16[64,768]{1,0:T(8,128)(2,1)S(1)}, u32[]{:S(2)}, u32[]{:S(2)}) %collective-permute-start.20) | collective-permute-done | bytes 98336 | tf_op jit(solution)/shard_map/ppermute | solution.py:247
  89.8 1.2 collective-permute-start.22
  91.0 1.4 %collective-permute-start.28 = (bf16[64,768]{1,0:T(8,128)(2,1)S(1)}, bf16[64,768]{1,0:T(8,128)(2,1)S(1)}, u32[]{:S(2)}, u32[]{:S(2)}) collective-permute-start(bf16[64,768]{1,0:T(8,128)(2,1)S(1)} %get-tuple-element.95), channel_id=1, source_target_pairs={{0,2},{2,0},{4,6},{6,4},{8,10},{10,8},{12,14},{14,12},{1,3},{3,1},... | collective-permute-start | bytes 294920 | tf_op jit(solution)/shard_map/ppermute | solution.py:247
  92.4 3.0 %collective-permute-done.22.refs_3_ = bf16[64,768]{1,0:T(8,128)(2,1)S(1)} collective-permute-done((bf16[64,768]{1,0:T(8,128)(2,1)S(1)}, bf16[64,768]{1,0:T(8,128)(2,1)S(1)}, u32[]{:S(2)}, u32[]{:S(2)}) %collective-permute-start.22) | collective-permute-done | bytes 98336 | tf_op jit(solution)/shard_map/ppermute | solution.py:247
  95.4 1.1 collective-permute-start.29
  96.5 0.8 collective-permute-done.28.refs_1_
  97.3 1.2 collective-permute-start.30
  98.8 1.2 collective-permute-done.29.refs_2_
  100.0 2.2 %collective-permute-start.23 = (bf16[128,768]{1,0:T(8,128)(2,1)S(1)}, bf16[128,768]{1,0:T(8,128)(2,1)S(1)}, u32[]{:S(2)}, u32[]{:S(2)}) collective-permute-start(bf16[128,768]{1,0:T(8,128)(2,1)S(1)} %far_back.1), channel_id=1, source_target_pairs={{0,8},{2,10},{4,12},{6,14},{8,0},{10,2},{12,4},{14,6},{1,9},{3,11}... | collective-permute-start | bytes 589832 | tf_op jit(solution)/shard_map/ppermute | solution.py:251
  102.2 1.7 %collective-permute-done.30.refs_3_ = bf16[64,768]{1,0:T(8,128)(2,1)S(1)} collective-permute-done((bf16[64,768]{1,0:T(8,128)(2,1)S(1)}, bf16[64,768]{1,0:T(8,128)(2,1)S(1)}, u32[]{:S(2)}, u32[]{:S(2)}) %collective-permute-start.30) | collective-permute-done | bytes 98336 | tf_op jit(solution)/shard_map/ppermute | solution.py:247
  104.4 6.1 %collective-permute-done.23.part_ref = bf16[128,768]{1,0:T(8,128)(2,1)S(1)} collective-permute-done((bf16[128,768]{1,0:T(8,128)(2,1)S(1)}, bf16[128,768]{1,0:T(8,128)(2,1)S(1)}, u32[]{:S(2)}, u32[]{:S(2)}) %collective-permute-start.23) | collective-permute-done | bytes 196640 | tf_op jit(solution)/shard_map/ppermute | solution.py:251
  110.5 1.1 combine_gradients.1
  111.6 0.6 collective-permute-done.34.refs_7_
  112.2 7.9 %weight_gradients.1 = bf16[3,1024,768]{2,1,0:T(8,128)(2,1)} custom-call(bf16[256,768]{1,0:T(8,128)(2,1)S(1)} %get-tuple-element.100.refs_0_, bf16[256,768]{1,0:T(8,128)(2,1)S(1)} %get-tuple-element.101.refs_1_, bf16[256,768]{1,0:T(8,128)(2,1)S(1)} %collective-permute-done.31.refs_2_, bf16[256,768]{1,0:T(8,128)(2,1)S(1)} %collective-permute-done.32.refs_3_, ...), custom_call_target="tpu_custom_call" | custom-call | flops 4831838208 | bytes 16777216 | tf_op jit(solution)/shard_map/weight_gradients/pallas_call | solution.py:350
  (58 shorter events, 5.9 us)
Async XLA Ops:
  0.6 20.0 %collective-permute-start.1 = (bf16[3,1024,768]{2,1,0:T(8,128)(2,1)}, bf16[3,1024,768]{2,1,0:T(8,128)(2,1)}, u32[]{:S(2)}, u32[]{:S(2)}) collective-permute-start(bf16[3,1024,768]{2,1,0:T(8,128)(2,1)} %bitcast.10), channel_id=1, source_target_pairs={{0,1},{1,0},{2,3},{3,2},{4,5},{5,4},{6,7},{7,6},{8,9},{9,8},{10,11... | collective-permute-start | bytes 14155784 | tf_op jit(solution)/shard_map/ppermute | solution.py:254
  1.1 15.6 %collective-permute-start.2 = (bf16[128,768]{1,0:T(8,128)(2,1)}, bf16[128,768]{1,0:T(8,128)(2,1)S(1)}, u32[]{:S(2)}, u32[]{:S(2)}) collective-permute-start(bf16[128,768]{1,0:T(8,128)(2,1)} %tokens_ref.1), channel_id=1, source_target_pairs={{0,8},{2,10},{4,12},{6,14},{8,0},{10,2},{12,4},{14,6},{1,9},{3,11}... | collective-permute-start | bytes 589832 | tf_op jit(solution)/shard_map/ppermute | solution.py:251
  4.8 1.0 copy-start.2
  5.8 0.7 copy-start.3
  6.5 0.7 copy-start.4
  7.5 7.4 %collective-permute-start = (f32[8,128]{1,0:T(8,128)S(1)}, f32[8,128]{1,0:T(8,128)S(1)}, u32[]{:S(2)}, u32[]{:S(2)}) collective-permute-start(f32[8,128]{1,0:T(8,128)S(1)} %get-tuple-element.58.meta_ref), channel_id=1, source_target_pairs={{0,8},{2,10},{4,12},{6,14},{8,0},{10,2},{12,4},{14,6},{1,9},{3,11}... | collective-permute-start | bytes 12296 | tf_op jit(solution)/shard_map/ppermute | solution.py:251
  7.6 10.1 %collective-permute-start.10 = (bf16[64,768]{1,0:T(8,128)(2,1)S(1)}, bf16[64,768]{1,0:T(8,128)(2,1)S(1)}, u32[]{:S(2)}, u32[]{:S(2)}) collective-permute-start(bf16[64,768]{1,0:T(8,128)(2,1)S(1)} %get-tuple-element.68), channel_id=1, source_target_pairs={{0,2},{2,0},{4,6},{6,4},{8,10},{10,8},{12,14},{14,12},{1,3},{3,1},... | collective-permute-start | bytes 294920 | tf_op jit(solution)/shard_map/ppermute | solution.py:247
  9.4 9.5 %collective-permute-start.11 = (bf16[64,768]{1,0:T(8,128)(2,1)S(1)}, bf16[64,768]{1,0:T(8,128)(2,1)S(1)}, u32[]{:S(2)}, u32[]{:S(2)}) collective-permute-start(bf16[64,768]{1,0:T(8,128)(2,1)S(1)} %get-tuple-element.69), channel_id=1, source_target_pairs={{0,4},{2,6},{4,0},{6,2},{8,12},{10,14},{12,8},{14,10},{1,5},{3,7},... | collective-permute-start | bytes 294920 | tf_op jit(solution)/shard_map/ppermute | solution.py:247
  15.0 5.7 %collective-permute-start.12 = (bf16[64,768]{1,0:T(8,128)(2,1)S(1)}, bf16[64,768]{1,0:T(8,128)(2,1)S(1)}, u32[]{:S(2)}, u32[]{:S(2)}) collective-permute-start(bf16[64,768]{1,0:T(8,128)(2,1)S(1)} %get-tuple-element.70), channel_id=1, source_target_pairs={{0,6},{2,4},{4,2},{6,0},{8,14},{10,12},{12,10},{14,8},{1,7},{3,5},... | collective-permute-start | bytes 294920 | tf_op jit(solution)/shard_map/ppermute | solution.py:247
  17.1 14.4 %collective-permute-start.3 = (bf16[64,768]{1,0:T(8,128)(2,1)S(1)}, bf16[64,768]{1,0:T(8,128)(2,1)S(1)}, u32[]{:S(2)}, u32[]{:S(2)}) collective-permute-start(bf16[64,768]{1,0:T(8,128)(2,1)S(1)} %get-tuple-element.60), channel_id=1, source_target_pairs={{0,2},{2,0},{4,6},{6,4},{8,10},{10,8},{12,14},{14,12},{1,3},{3,1},... | collective-permute-start | bytes 294920 | tf_op jit(solution)/shard_map/ppermute | solution.py:247
  17.7 14.6 %collective-permute-start.4 = (bf16[64,768]{1,0:T(8,128)(2,1)S(1)}, bf16[64,768]{1,0:T(8,128)(2,1)S(1)}, u32[]{:S(2)}, u32[]{:S(2)}) collective-permute-start(bf16[64,768]{1,0:T(8,128)(2,1)S(1)} %get-tuple-element.61), channel_id=1, source_target_pairs={{0,4},{2,6},{4,0},{6,2},{8,12},{10,14},{12,8},{14,10},{1,5},{3,7},... | collective-permute-start | bytes 294920 | tf_op jit(solution)/shard_map/ppermute | solution.py:247
  18.9 13.4 %collective-permute-start.5 = (bf16[64,768]{1,0:T(8,128)(2,1)S(1)}, bf16[64,768]{1,0:T(8,128)(2,1)S(1)}, u32[]{:S(2)}, u32[]{:S(2)}) collective-permute-start(bf16[64,768]{1,0:T(8,128)(2,1)S(1)} %get-tuple-element.62), channel_id=1, source_target_pairs={{0,6},{2,4},{4,2},{6,0},{8,14},{10,12},{12,10},{14,8},{1,7},{3,5},... | collective-permute-start | bytes 294920 | tf_op jit(solution)/shard_map/ppermute | solution.py:247
  20.7 2.3 %copy-start = (bf16[1,1024,3,768]{3,1,2,0:T(8,128)(2,1)S(1)}, bf16[1,1024,3,768]{3,1,2,0:T(8,128)(2,1)}, u32[]{:S(2)}) copy-start(bf16[1,1024,3,768]{3,1,2,0:T(8,128)(2,1)} %param.9) | copy-start | bytes 14155780
  28.4 12.3 %collective-permute-start.13 = (bf16[64,768]{1,0:T(8,128)(2,1)S(1)}, bf16[64,768]{1,0:T(8,128)(2,1)S(1)}, u32[]{:S(2)}, u32[]{:S(2)}) collective-permute-start(bf16[64,768]{1,0:T(8,128)(2,1)S(1)} %get-tuple-element.72), channel_id=1, source_target_pairs={{0,2},{2,0},{4,6},{6,4},{8,10},{10,8},{12,14},{14,12},{1,3},{3,1},... | collective-permute-start | bytes 294920 | tf_op jit(solution)/shard_map/ppermute | solution.py:247
  30.8 10.7 %collective-permute-start.14 = (bf16[64,768]{1,0:T(8,128)(2,1)S(1)}, bf16[64,768]{1,0:T(8,128)(2,1)S(1)}, u32[]{:S(2)}, u32[]{:S(2)}) collective-permute-start(bf16[64,768]{1,0:T(8,128)(2,1)S(1)} %get-tuple-element.73), channel_id=1, source_target_pairs={{0,4},{2,6},{4,0},{6,2},{8,12},{10,14},{12,8},{14,10},{1,5},{3,7},... | collective-permute-start | bytes 294920 | tf_op jit(solution)/shard_map/ppermute | solution.py:247
  31.5 10.0 %collective-permute-start.15 = (bf16[64,768]{1,0:T(8,128)(2,1)S(1)}, bf16[64,768]{1,0:T(8,128)(2,1)S(1)}, u32[]{:S(2)}, u32[]{:S(2)}) collective-permute-start(bf16[64,768]{1,0:T(8,128)(2,1)S(1)} %get-tuple-element.74), channel_id=1, source_target_pairs={{0,6},{2,4},{4,2},{6,0},{8,14},{10,12},{12,10},{14,8},{1,7},{3,5},... | collective-permute-start | bytes 294920 | tf_op jit(solution)/shard_map/ppermute | solution.py:247
  32.3 35.2 %slice-start = ((s8[4718592]{0:T(1024)(128)(4,1)}), s8[4194304]{0:T(1024)(128)(4,1)S(1)}, s32[]{:S(2)}) async-start(s8[4718592]{0:T(1024)(128)(4,1)} %bitcast.13), calls=%async_computation | async-start | bytes 8388608
  32.3 9.2 %copy-start.1 = (bf16[128,768]{1,0:T(8,128)(2,1)S(1)}, bf16[128,768]{1,0:T(8,128)(2,1)}, u32[]{:S(2)}) copy-start(bf16[128,768]{1,0:T(8,128)(2,1)} %teacher_ref.3) | copy-start | bytes 589828
  32.3 35.1 %slice-start.1 = ((s8[4718592]{0:T(1024)(128)(4,1)}), s8[524288]{0:T(1024)(128)(4,1)S(1)}, s32[]{:S(2)}) async-start(s8[4718592]{0:T(1024)(128)(4,1)} %bitcast.13), calls=%async_computation.1 | async-start | bytes 1048576
  37.9 7.1 %collective-permute-start.6 = (bf16[64,768]{1,0:T(8,128)(2,1)S(1)}, bf16[64,768]{1,0:T(8,128)(2,1)S(1)}, u32[]{:S(2)}, u32[]{:S(2)}) collective-permute-start(bf16[64,768]{1,0:T(8,128)(2,1)S(1)} %get-tuple-element.64), channel_id=1, source_target_pairs={{0,2},{2,0},{4,6},{6,4},{8,10},{10,8},{12,14},{14,12},{1,3},{3,1},... | collective-permute-start | bytes 294920 | tf_op jit(solution)/shard_map/ppermute | solution.py:247
  39.9 5.3 %collective-permute-start.7 = (bf16[64,768]{1,0:T(8,128)(2,1)S(1)}, bf16[64,768]{1,0:T(8,128)(2,1)S(1)}, u32[]{:S(2)}, u32[]{:S(2)}) collective-permute-start(bf16[64,768]{1,0:T(8,128)(2,1)S(1)} %get-tuple-element.65), channel_id=1, source_target_pairs={{0,4},{2,6},{4,0},{6,2},{8,12},{10,14},{12,8},{14,10},{1,5},{3,7},... | collective-permute-start | bytes 294920 | tf_op jit(solution)/shard_map/ppermute | solution.py:247
  40.6 7.0 %collective-permute-start.8 = (bf16[64,768]{1,0:T(8,128)(2,1)S(1)}, bf16[64,768]{1,0:T(8,128)(2,1)S(1)}, u32[]{:S(2)}, u32[]{:S(2)}) collective-permute-start(bf16[64,768]{1,0:T(8,128)(2,1)S(1)} %get-tuple-element.66), channel_id=1, source_target_pairs={{0,6},{2,4},{4,2},{6,0},{8,14},{10,12},{12,10},{14,8},{1,7},{3,5},... | collective-permute-start | bytes 294920 | tf_op jit(solution)/shard_map/ppermute | solution.py:247
  42.0 15.6 %collective-permute-start.16 = (bf16[128,768]{1,0:T(8,128)(2,1)S(1)}, bf16[128,768]{1,0:T(8,128)(2,1)S(1)}, u32[]{:S(2)}, u32[]{:S(2)}) collective-permute-start(bf16[128,768]{1,0:T(8,128)(2,1)S(1)} %near_sum.1), channel_id=1, source_target_pairs={{0,8},{2,10},{4,12},{6,14},{8,0},{10,2},{12,4},{14,6},{1,9},{3,11}... | collective-permute-start | bytes 589832 | tf_op jit(solution)/shard_map/ppermute | solution.py:251
  48.1 13.8 %collective-permute-start.9 = (bf16[128,768]{1,0:T(8,128)(2,1)S(1)}, bf16[128,768]{1,0:T(8,128)(2,1)S(1)}, u32[]{:S(2)}, u32[]{:S(2)}) collective-permute-start(bf16[128,768]{1,0:T(8,128)(2,1)S(1)} %far_sum.1), channel_id=1, source_target_pairs={{0,8},{2,10},{4,12},{6,14},{8,0},{10,2},{12,4},{14,6},{1,9},{3,11}... | collective-permute-start | bytes 589832 | tf_op jit(solution)/shard_map/ppermute | solution.py:251
  58.4 5.3 %collective-permute-start.17 = (bf16[64,768]{1,0:T(8,128)(2,1)S(1)}, bf16[64,768]{1,0:T(8,128)(2,1)S(1)}, u32[]{:S(2)}, u32[]{:S(2)}) collective-permute-start(bf16[64,768]{1,0:T(8,128)(2,1)S(1)} %get-tuple-element.79), channel_id=1, source_target_pairs={{0,2},{2,0},{4,6},{6,4},{8,10},{10,8},{12,14},{14,12},{1,3},{3,1},... | collective-permute-start | bytes 294920 | tf_op jit(solution)/shard_map/ppermute | solution.py:247
  59.8 5.2 %collective-permute-start.18 = (bf16[64,768]{1,0:T(8,128)(2,1)S(1)}, bf16[64,768]{1,0:T(8,128)(2,1)S(1)}, u32[]{:S(2)}, u32[]{:S(2)}) collective-permute-start(bf16[64,768]{1,0:T(8,128)(2,1)S(1)} %get-tuple-element.80), channel_id=1, source_target_pairs={{0,4},{2,6},{4,0},{6,2},{8,12},{10,14},{12,8},{14,10},{1,5},{3,7},... | collective-permute-start | bytes 294920 | tf_op jit(solution)/shard_map/ppermute | solution.py:247
  59.8 5.7 %collective-permute-start.19 = (bf16[64,768]{1,0:T(8,128)(2,1)S(1)}, bf16[64,768]{1,0:T(8,128)(2,1)S(1)}, u32[]{:S(2)}, u32[]{:S(2)}) collective-permute-start(bf16[64,768]{1,0:T(8,128)(2,1)S(1)} %get-tuple-element.81), channel_id=1, source_target_pairs={{0,6},{2,4},{4,2},{6,0},{8,14},{10,12},{12,10},{14,8},{1,7},{3,5},... | collective-permute-start | bytes 294920 | tf_op jit(solution)/shard_map/ppermute | solution.py:247
  61.9 22.7 %collective-permute-start.31 = (bf16[256,768]{1,0:T(8,128)(2,1)S(1)}, bf16[256,768]{1,0:T(8,128)(2,1)S(1)}, u32[]{:S(2)}, u32[]{:S(2)}) collective-permute-start(bf16[256,768]{1,0:T(8,128)(2,1)S(1)} %get-tuple-element.100.refs_0_), channel_id=1, source_target_pairs={{0,1},{1,0},{2,3},{3,2},{4,5},{5,4},{6,7},{7,6},{8,9},{9,8},{10,11... | collective-permute-start | bytes 1179656 | tf_op jit(solution)/shard_map/ppermute | solution.py:254
  61.9 24.1 %collective-permute-start.32 = (bf16[256,768]{1,0:T(8,128)(2,1)S(1)}, bf16[256,768]{1,0:T(8,128)(2,1)S(1)}, u32[]{:S(2)}, u32[]{:S(2)}) collective-permute-start(bf16[256,768]{1,0:T(8,128)(2,1)S(1)} %get-tuple-element.101.refs_1_), channel_id=1, source_target_pairs={{0,1},{1,0},{2,3},{3,2},{4,5},{5,4},{6,7},{7,6},{8,9},{9,8},{10,11... | collective-permute-start | bytes 1179656 | tf_op jit(solution)/shard_map/ppermute | solution.py:254
  63.7 9.7 %collective-permute-start.25 = (bf16[64,768]{1,0:T(8,128)(2,1)S(1)}, bf16[64,768]{1,0:T(8,128)(2,1)S(1)}, u32[]{:S(2)}, u32[]{:S(2)}) collective-permute-start(bf16[64,768]{1,0:T(8,128)(2,1)S(1)} %get-tuple-element.91), channel_id=1, source_target_pairs={{0,2},{2,0},{4,6},{6,4},{8,10},{10,8},{12,14},{14,12},{1,3},{3,1},... | collective-permute-start | bytes 294920 | tf_op jit(solution)/shard_map/ppermute | solution.py:247
  65.0 8.4 %collective-permute-start.26 = (bf16[64,768]{1,0:T(8,128)(2,1)S(1)}, bf16[64,768]{1,0:T(8,128)(2,1)S(1)}, u32[]{:S(2)}, u32[]{:S(2)}) collective-permute-start(bf16[64,768]{1,0:T(8,128)(2,1)S(1)} %get-tuple-element.92), channel_id=1, source_target_pairs={{0,4},{2,6},{4,0},{6,2},{8,12},{10,14},{12,8},{14,10},{1,5},{3,7},... | collective-permute-start | bytes 294920 | tf_op jit(solution)/shard_map/ppermute | solution.py:247
  65.5 7.9 %collective-permute-start.27 = (bf16[64,768]{1,0:T(8,128)(2,1)S(1)}, bf16[64,768]{1,0:T(8,128)(2,1)S(1)}, u32[]{:S(2)}, u32[]{:S(2)}) collective-permute-start(bf16[64,768]{1,0:T(8,128)(2,1)S(1)} %get-tuple-element.93), channel_id=1, source_target_pairs={{0,6},{2,4},{4,2},{6,0},{8,14},{10,12},{12,10},{14,8},{1,7},{3,5},... | collective-permute-start | bytes 294920 | tf_op jit(solution)/shard_map/ppermute | solution.py:247
  73.4 38.8 %collective-permute-start.35 = (bf16[256,2048]{1,0:T(8,128)(2,1)S(1)}, bf16[256,2048]{1,0:T(8,128)(2,1)S(1)}, u32[]{:S(2)}, u32[]{:S(2)}) collective-permute-start(bf16[256,2048]{1,0:T(8,128)(2,1)S(1)} %get-tuple-element.106), channel_id=1, source_target_pairs={{0,1},{1,0},{2,3},{3,2},{4,5},{5,4},{6,7},{7,6},{8,9},{9,8},{10,11... | collective-permute-start | bytes 3145736 | tf_op jit(solution)/shard_map/ppermute | solution.py:254
  79.6 32.6 %collective-permute-start.36 = (bf16[256,2048]{1,0:T(8,128)(2,1)S(1)}, bf16[256,2048]{1,0:T(8,128)(2,1)S(1)}, u32[]{:S(2)}, u32[]{:S(2)}) collective-permute-start(bf16[256,2048]{1,0:T(8,128)(2,1)S(1)} %get-tuple-element.107), channel_id=1, source_target_pairs={{0,1},{1,0},{2,3},{3,2},{4,5},{5,4},{6,7},{7,6},{8,9},{9,8},{10,11... | collective-permute-start | bytes 3145736 | tf_op jit(solution)/shard_map/ppermute | solution.py:254
  80.2 4.5 %collective-permute-start.24 = (f32[2,128]{1,0:T(2,128)S(1)}, f32[2,128]{1,0:T(2,128)S(1)}, u32[]{:S(2)}, u32[]{:S(2)}) collective-permute-start(f32[2,128]{1,0:T(2,128)S(1)} %get-tuple-element.87), channel_id=1, source_target_pairs={{0,8},{2,10},{4,12},{6,14},{8,0},{10,2},{12,4},{14,6},{1,9},{3,11}... | collective-permute-start | bytes 3080 | tf_op jit(solution)/shard_map/ppermute | solution.py:251
  84.6 19.3 %collective-permute-start.37 = (bf16[256,1024]{1,0:T(8,128)(2,1)S(1)}, bf16[256,1024]{1,0:T(8,128)(2,1)S(1)}, u32[]{:S(2)}, u32[]{:S(2)}) collective-permute-start(bf16[256,1024]{1,0:T(8,128)(2,1)S(1)} %get-tuple-element.110), channel_id=1, source_target_pairs={{0,1},{1,0},{2,3},{3,2},{4,5},{5,4},{6,7},{7,6},{8,9},{9,8},{10,11... | collective-permute-start | bytes 1572872 | tf_op jit(solution)/shard_map/ppermute | solution.py:254
  84.6 5.2 %collective-permute-start.20 = (bf16[64,768]{1,0:T(8,128)(2,1)S(1)}, bf16[64,768]{1,0:T(8,128)(2,1)S(1)}, u32[]{:S(2)}, u32[]{:S(2)}) collective-permute-start(bf16[64,768]{1,0:T(8,128)(2,1)S(1)} %get-tuple-element.83), channel_id=1, source_target_pairs={{0,2},{2,0},{4,6},{6,4},{8,10},{10,8},{12,14},{14,12},{1,3},{3,1},... | collective-permute-start | bytes 294920 | tf_op jit(solution)/shard_map/ppermute | solution.py:247
  86.1 5.0 %collective-permute-start.21 = (bf16[64,768]{1,0:T(8,128)(2,1)S(1)}, bf16[64,768]{1,0:T(8,128)(2,1)S(1)}, u32[]{:S(2)}, u32[]{:S(2)}) collective-permute-start(bf16[64,768]{1,0:T(8,128)(2,1)S(1)} %get-tuple-element.84), channel_id=1, source_target_pairs={{0,4},{2,6},{4,0},{6,2},{8,12},{10,14},{12,8},{14,10},{1,5},{3,7},... | collective-permute-start | bytes 294920 | tf_op jit(solution)/shard_map/ppermute | solution.py:247
  89.8 5.6 %collective-permute-start.22 = (bf16[64,768]{1,0:T(8,128)(2,1)S(1)}, bf16[64,768]{1,0:T(8,128)(2,1)S(1)}, u32[]{:S(2)}, u32[]{:S(2)}) collective-permute-start(bf16[64,768]{1,0:T(8,128)(2,1)S(1)} %get-tuple-element.85), channel_id=1, source_target_pairs={{0,6},{2,4},{4,2},{6,0},{8,14},{10,12},{12,10},{14,8},{1,7},{3,5},... | collective-permute-start | bytes 294920 | tf_op jit(solution)/shard_map/ppermute | solution.py:247
  91.0 6.2 %collective-permute-start.28 = (bf16[64,768]{1,0:T(8,128)(2,1)S(1)}, bf16[64,768]{1,0:T(8,128)(2,1)S(1)}, u32[]{:S(2)}, u32[]{:S(2)}) collective-permute-start(bf16[64,768]{1,0:T(8,128)(2,1)S(1)} %get-tuple-element.95), channel_id=1, source_target_pairs={{0,2},{2,0},{4,6},{6,4},{8,10},{10,8},{12,14},{14,12},{1,3},{3,1},... | collective-permute-start | bytes 294920 | tf_op jit(solution)/shard_map/ppermute | solution.py:247
  95.4 4.6 %collective-permute-start.29 = (bf16[64,768]{1,0:T(8,128)(2,1)S(1)}, bf16[64,768]{1,0:T(8,128)(2,1)S(1)}, u32[]{:S(2)}, u32[]{:S(2)}) collective-permute-start(bf16[64,768]{1,0:T(8,128)(2,1)S(1)} %get-tuple-element.96), channel_id=1, source_target_pairs={{0,4},{2,6},{4,0},{6,2},{8,12},{10,14},{12,8},{14,10},{1,5},{3,7},... | collective-permute-start | bytes 294920 | tf_op jit(solution)/shard_map/ppermute | solution.py:247
  97.3 6.6 %collective-permute-start.30 = (bf16[64,768]{1,0:T(8,128)(2,1)S(1)}, bf16[64,768]{1,0:T(8,128)(2,1)S(1)}, u32[]{:S(2)}, u32[]{:S(2)}) collective-permute-start(bf16[64,768]{1,0:T(8,128)(2,1)S(1)} %get-tuple-element.97), channel_id=1, source_target_pairs={{0,6},{2,4},{4,2},{6,0},{8,14},{10,12},{12,10},{14,8},{1,7},{3,5},... | collective-permute-start | bytes 294920 | tf_op jit(solution)/shard_map/ppermute | solution.py:247
  100.0 10.4 %collective-permute-start.23 = (bf16[128,768]{1,0:T(8,128)(2,1)S(1)}, bf16[128,768]{1,0:T(8,128)(2,1)S(1)}, u32[]{:S(2)}, u32[]{:S(2)}) collective-permute-start(bf16[128,768]{1,0:T(8,128)(2,1)S(1)} %far_back.1), channel_id=1, source_target_pairs={{0,8},{2,10},{4,12},{6,14},{8,0},{10,2},{12,4},{14,6},{1,9},{3,11}... | collective-permute-start | bytes 589832 | tf_op jit(solution)/shard_map/ppermute | solution.py:251
  103.9 7.7 %collective-permute-start.38 = (bf16[256,1024]{1,0:T(8,128)(2,1)S(1)}, bf16[256,1024]{1,0:T(8,128)(2,1)S(1)}, u32[]{:S(2)}, u32[]{:S(2)}) collective-permute-start(bf16[256,1024]{1,0:T(8,128)(2,1)S(1)} %get-tuple-element.111), channel_id=1, source_target_pairs={{0,1},{1,0},{2,3},{3,2},{4,5},{5,4},{6,7},{7,6},{8,9},{9,8},{10,11... | collective-permute-start | bytes 1572872 | tf_op jit(solution)/shard_map/ppermute | solution.py:254
  103.9 7.7 %collective-permute-start.33 = (bf16[256,768]{1,0:T(8,128)(2,1)S(1)}, bf16[256,768]{1,0:T(8,128)(2,1)S(1)}, u32[]{:S(2)}, u32[]{:S(2)}) collective-permute-start(bf16[256,768]{1,0:T(8,128)(2,1)S(1)} %get-tuple-element.102.refs_4_), channel_id=1, source_target_pairs={{0,1},{1,0},{2,3},{3,2},{4,5},{5,4},{6,7},{7,6},{8,9},{9,8},{10,11... | collective-permute-start | bytes 1179656 | tf_op jit(solution)/shard_map/ppermute | solution.py:254
  110.5 1.7 %collective-permute-start.34 = (bf16[256,768]{1,0:T(8,128)(2,1)S(1)}, bf16[256,768]{1,0:T(8,128)(2,1)S(1)}, u32[]{:S(2)}, u32[]{:S(2)}) collective-permute-start(bf16[256,768]{1,0:T(8,128)(2,1)S(1)} %get-tuple-element.103.refs_5_), channel_id=1, source_target_pairs={{0,1},{1,0},{2,3},{3,2},{4,5},{5,4},{6,7},{7,6},{8,9},{9,8},{10,11... | collective-permute-start | bytes 1179656 | tf_op jit(solution)/shard_map/ppermute | solution.py:254

commit v4 on v3

v4 whole, which is shorter than its diff:
```python
import functools

import jax
import jax.numpy as jnp
from jax import lax
from jax.experimental import pallas as pl
from jax.experimental.pallas import tpu as pltpu
from jax.sharding import PartitionSpec as P

PLAIN = (((1,), (0,)), ((), ()))
LAST = (((1,), (1,)), ((), ()))
FIRST = (((0,), (0,)), ((), ()))
MIB = 1024 * 1024
F32 = jnp.float32
BF16 = jnp.bfloat16


def dot(a, b, dims=PLAIN):
    return lax.dot_general(a, b, dims, preferred_element_type=F32)


def slot_masks(me, meta, pieces, capacity):
    tok = meta.shape[1]
    expert_of = (lax.broadcasted_iota(jnp.int32, (pieces, tok), 0) ^ me).astype(F32)
    first, second = meta[0:1, :] == expert_of, meta[1:2, :] == expert_of
    chosen = jnp.where(first | second, 1.0, 0.0).astype(BF16)
    before = lax.broadcasted_iota(jnp.int32, (tok, tok), 0) < lax.broadcasted_iota(
        jnp.int32, (tok, tok), 1
    )
    rank = dot(chosen, jnp.where(before, 1.0, 0.0).astype(BF16))
    rank0 = jnp.where(first, rank, -1.0)
    rank1 = jnp.where(second, rank, -1.0)
    place = lax.broadcasted_iota(jnp.int32, (capacity, tok), 0).astype(F32)

    def expand(ranks):
        return jnp.concatenate(
            [
                jnp.where(ranks[s : s + 1, :] == place, 1.0, 0.0).astype(BF16)
                for s in range(pieces)
            ],
            axis=0,
        )

    return expand(rank0), expand(rank1)


def put(refs, rows):
    capacity = refs[0].shape[0]
    for s, ref in enumerate(refs):
        ref[...] = rows[s * capacity : (s + 1) * capacity].astype(ref.dtype)


def put_columns(ref, rows):
    side = rows.shape[0]
    for i in range(rows.shape[1] // side):
        ref[i] = rows[:, i * side : (i + 1) * side]


def put_rows(ref, first, value):
    side = value.shape[1]
    for i in range(value.shape[0] // side):
        ref[first + i] = value[i * side : (i + 1) * side, :]


def get_columns(ref):
    return jnp.concatenate([ref[i] for i in range(ref.shape[0])], axis=1)


def get(refs):
    return jnp.concatenate([ref[...] for ref in refs], axis=0)


def masks_of(me_ref, meta, refs):
    return slot_masks(me_ref[0], meta, len(refs), refs[0].shape[0])


def gate_columns(meta):
    columns = meta.T
    return columns[:, 2:3], columns[:, 3:4]


def route_sums(me_ref, meta, refs):
    m0, m1 = masks_of(me_ref, meta, refs)
    got = get(refs)
    g0, g1 = gate_columns(meta)
    o0, o1 = dot(m0, got, FIRST), dot(m1, got, FIRST)
    return m0, m1, g0, g1, o0, o1, g0 * o0 + g1 * o1


def put_d_gates(ref, diff, o0, o1):
    tok = diff.shape[0]
    lane = lax.broadcasted_iota(jnp.int32, (tok, 128), 1)
    d0 = jnp.sum(diff * o0, axis=1, keepdims=True)
    d1 = jnp.sum(diff * o1, axis=1, keepdims=True)
    ref[...] = jnp.where(lane == 0, d0, jnp.where(lane == 1, d1, 0.0)).T[0:2, :]


def put_route_grads(refs, m0, m1, g0, g1, diff):
    grads = jnp.concatenate([(g0 * diff).astype(BF16), (g1 * diff).astype(BF16)], axis=0)
    put(refs, dot(jnp.concatenate([m0, m1], axis=1), grads))


def pack_near_kernel(me_ref, own_ref, routes_ref, gates_ref, tokens_ref, meta_ref, *rows_refs):
    del own_ref
    meta = jnp.concatenate(
        [
            routes_ref[...].astype(F32),
            gates_ref[...],
            jnp.zeros((4, routes_ref.shape[1]), F32),
        ],
        axis=0,
    )
    meta_ref[...] = meta
    m0, m1 = masks_of(me_ref, meta, rows_refs)
    put(rows_refs, dot(m0 + m1, tokens_ref[...]))


def pack_far_kernel(me_ref, meta_ref, tokens_ref, *rows_refs):
    m0, m1 = masks_of(me_ref, meta_ref[...], rows_refs)
    put(rows_refs, dot(m0 + m1, tokens_ref[...]))


def forward_kernel(pieces, own_ref, other_ref, *refs):
    ins, outs, refs = refs[:pieces], refs[pieces : 2 * pieces], refs[2 * pieces :]
    sent_ref, hid_own_ref, fa_ref, fb_ref = refs
    x = get(ins)
    put_columns(sent_ref, x)
    units, width = other_ref.shape[1:]
    hidden = []
    for w_ref, first in ((own_ref, 0), (other_ref, units)):
        both = dot(w_ref[0:2].reshape(2 * units, width), x, LAST)
        gate, up = both[:units], both[units:]
        sig = 0.5 * jnp.tanh(0.5 * gate) + 0.5
        silu = gate * sig
        hidden.append((silu * up).astype(BF16))
        fa_ref[first : first + units, :] = (up * (sig + silu * (1.0 - sig))).astype(BF16)
        fb_ref[first : first + units, :] = silu.astype(BF16)
    hid_own_ref[...] = hidden[0]
    put_rows(sent_ref, width // x.shape[0], hidden[1])
    put(outs, dot(hidden[0], own_ref[2], FIRST) + dot(hidden[1], other_ref[2], FIRST))


def backward_kernel(pieces, own_ref, other_ref, fa_ref, fb_ref, *refs):
    ins, outs, refs = refs[:pieces], refs[pieces : 2 * pieces], refs[2 * pieces :]
    sent_ref, dgu_own_ref = refs
    rg = get(ins)
    put_columns(sent_ref, rg)
    units, width = own_ref.shape[1:]
    both = []
    for w_ref, first in ((own_ref, 0), (other_ref, units)):
        at = slice(first, first + units)
        dh = dot(w_ref[2], rg, LAST)
        dg = (dh * fa_ref[at, :].astype(F32)).astype(BF16)
        du = (dh * fb_ref[at, :].astype(F32)).astype(BF16)
        both.append(jnp.concatenate([dg, du], axis=0))
    dgu_own_ref[...] = both[0]
    put_rows(sent_ref, width // rg.shape[0], both[1])
    put(
        outs,
        dot(both[0], own_ref[0:2].reshape(2 * units, width), FIRST)
        + dot(both[1], other_ref[0:2].reshape(2 * units, width), FIRST),
    )


def near_sum_kernel(me_ref, meta_ref, teacher_ref, *refs):
    ins, out_ref = refs[:-1], refs[-1]
    total = route_sums(me_ref, meta_ref[...], ins)[-1]
    out_ref[...] = (total - teacher_ref[...].astype(F32)).astype(BF16)


def far_sum_kernel(me_ref, meta_ref, *refs):
    ins, out_ref = refs[:-1], refs[-1]
    out_ref[...] = route_sums(me_ref, meta_ref[...], ins)[-1].astype(BF16)


def far_grad_kernel(pieces, me_ref, meta_ref, rest_ref, *refs):
    ins, d_gates_ref, outs = refs[:pieces], refs[pieces], refs[pieces + 1 :]
    m0, m1, g0, g1, o0, o1, total = route_sums(me_ref, meta_ref[...], ins)
    diff = total + rest_ref[...].astype(F32)
    put_route_grads(outs, m0, m1, g0, g1, diff)
    put_d_gates(d_gates_ref, diff, o0, o1)


def near_grad_kernel(pieces, me_ref, meta_ref, teacher_ref, part_ref, *refs):
    ins, student_ref, d_gates_ref, outs = (
        refs[:pieces],
        refs[pieces],
        refs[pieces + 1],
        refs[pieces + 2 :],
    )
    m0, m1, g0, g1, o0, o1, total = route_sums(me_ref, meta_ref[...], ins)
    total = total + part_ref[...].astype(F32)
    student_ref[...] = total.astype(BF16)
    diff = total - teacher_ref[...].astype(F32)
    put_route_grads(outs, m0, m1, g0, g1, diff)
    put_d_gates(d_gates_ref, diff, o0, o1)


def far_back_kernel(me_ref, meta_ref, d_gates_ref, *refs):
    ins, out_ref = refs[:-1], refs[-1]
    m0, m1 = masks_of(me_ref, meta_ref[...], ins)
    tok = m0.shape[1]
    out_ref[:tok, :] = dot(m0 + m1, get(ins), FIRST).astype(BF16)
    value = d_gates_ref[...]
    high = value.astype(BF16)
    low = (value - high.astype(F32)).astype(BF16)
    rest = jnp.zeros((out_ref.shape[0] - tok - 4, tok), BF16)
    out_ref[tok:, :tok] = jnp.concatenate([high, low, rest], axis=0)
    out_ref[tok:, tok:] = jnp.zeros((out_ref.shape[0] - tok, out_ref.shape[1] - tok), BF16)


def final_kernel(pieces, me_ref, meta_ref, part_ref, near_ref, *refs):
    ins, out_ref, d_gates_ref = refs[:pieces], refs[pieces], refs[pieces + 1]
    m0, m1 = masks_of(me_ref, meta_ref[...], ins)
    tok = m0.shape[1]
    total = dot(m0 + m1, get(ins), FIRST) + part_ref[:tok, :].astype(F32)
    out_ref[...] = total.astype(BF16)
    far = part_ref[tok:, :tok].astype(F32)
    d_gates_ref[...] = near_ref[...] + (far[0:2] + far[2:4])


def weight_kernel(*refs):
    refs, out_ref, finished_ref = refs[:-2], refs[-2], refs[-1]
    xs, rgs = [get_columns(r) for r in refs[0:4]], [get_columns(r) for r in refs[4:8]]
    finished_ref[...] = jnp.zeros_like(finished_ref)
    for m, rows in enumerate((xs, xs, rgs)):
        term = None
        for ref, row in zip(refs[8 + 4 * m : 12 + 4 * m], rows):
            act = ref[0] if len(ref.shape) == 3 else ref[...]
            term = dot(act, row) if term is None else term + dot(act, row)
        out_ref[m] = term.astype(BF16)


def local(tokens, teacher, routes, gate_weights, weights):
    tok, width = tokens.shape
    experts = lax.axis_size("expert")
    half = experts // 2
    capacity = 4 * tok // experts
    rows = half * capacity
    units = weights.shape[1]
    me = lax.axis_index("expert").reshape(1)

    pieces = [jax.ShapeDtypeStruct((capacity, width), BF16)] * half
    dense = jax.ShapeDtypeStruct((tok, width), BF16)
    longer = jax.ShapeDtypeStruct((tok + 16, width), BF16)
    pair = jax.ShapeDtypeStruct((2, tok), F32)
    acts = jax.ShapeDtypeStruct((units, rows), BF16)
    across, along = width // rows, units // rows
    sent_x = jax.ShapeDtypeStruct((across + along, rows, rows), BF16)
    sent_g = jax.ShapeDtypeStruct((across + 2 * along, rows, rows), BF16)
    acts2 = jax.ShapeDtypeStruct((2 * units, rows), BF16)
    vspec = pl.BlockSpec(memory_space=pltpu.VMEM)
    sspec = pl.BlockSpec(memory_space=pltpu.SMEM)
    aspec = pl.BlockSpec(memory_space=pl.ANY)
    matmul = 4 * rows * width * units

    def call(
        kernel,
        name,
        out_shape,
        specs,
        *args,
        after=(),
        through=(),
        flops=10**8,
        limit=8,
        scratch=(),
    ):
        many = isinstance(out_shape, list)
        specs = list(specs) + [vspec] * (len(args) - len(specs))
        inputs = len(args) + len(after) + len(through)
        outputs = len(out_shape) if many else 1

        def body(*refs):
            kernel(
                *refs[: len(args)],
                *refs[inputs : inputs + outputs],
                *refs[inputs + outputs + len(through) :],
            )

        out_specs = [vspec] * outputs + [aspec] * len(through)
        out_shapes = (out_shape if many else [out_shape]) + [
            jax.ShapeDtypeStruct(a.shape, a.dtype) for a in through
        ]
        single = not many and not through
        return pl.pallas_call(
            body,
            in_specs=specs + [aspec] * (len(after) + len(through)),
            out_specs=out_specs[0] if single else out_specs,
            out_shape=out_shapes[0] if single else out_shapes,
            input_output_aliases={
                len(args) + len(after) + i: outputs + i for i in range(len(through))
            },
            scratch_shapes=scratch,
            cost_estimate=pl.CostEstimate(
                flops=flops, bytes_accessed=2 * MIB, transcendentals=0
            ),
            compiler_params=pltpu.CompilerParams(vmem_limit_bytes=limit * MIB),
            name=name,
        )(*args, *after, *through)

    def within_half(rows_of):
        got = [rows_of[0]] + [None] * (half - 1)
        for s in range(1, half):
            got[s] = lax.ppermute(rows_of[s], "expert", [(i, i ^ s) for i in range(experts)])
        return got

    def to_mirror(x):
        return lax.ppermute(x, "expert", [(i, i ^ half) for i in range(experts)])

    def to_sibling(x):
        return lax.ppermute(x, "dp", [(0, 1), (1, 0)])

    far_tokens = to_mirror(tokens)
    own = weights[0].transpose(1, 0, 2)
    other = to_sibling(own)

    def forward(x_pieces, name, after=()):
        res = call(
            functools.partial(forward_kernel, half),
            name,
            pieces + [sent_x, acts, acts2, acts2],
            [],
            own,
            other,
            *x_pieces,
            after=after,
            flops=3 * matmul,
            limit=20,
        )
        return res[:half], res[half:]

    def backward(rg_pieces, fa, fb, name, after=(), through=()):
        res = call(
            functools.partial(backward_kernel, half),
            name,
            pieces + [sent_g, acts2],
            [],
            own,
            other,
            fa,
            fb,
            *rg_pieces,
            after=after,
            through=through,
            flops=3 * matmul,
            limit=20,
        )
        return res[:half], res[half:]

    res = call(
        pack_near_kernel,
        "pack_near",
        [jax.ShapeDtypeStruct((8, tok), F32)] + pieces,
        [sspec],
        me,
        own,
        routes.T,
        gate_weights.T,
        tokens,
        limit=10,
    )
    meta, x_near = res[0], within_half(res[1:])
    far_meta = to_mirror(meta)
    x_far = within_half(
        call(pack_far_kernel, "pack_far", pieces, [sspec], me, far_meta, far_tokens)
    )

    out_near, (xn, hn, fan, fbn) = forward(x_near, "forward_near")
    got_near = within_half(out_near)
    rest_rows = call(
        near_sum_kernel, "near_sum", dense, [sspec], me, meta, teacher, *got_near
    )
    rest = to_mirror(rest_rows)
    out_far, (xf, hf, faf, fbf) = forward(x_far, "forward_far", after=[rest_rows])
    got_far = within_half(out_far)
    xf_sib, xn_sib = to_sibling(xf), to_sibling(xn)
    part = to_mirror(call(far_sum_kernel, "far_sum", dense, [sspec], me, far_meta, *got_far))

    res = call(
        functools.partial(far_grad_kernel, half),
        "far_grad",
        [pair] + pieces,
        [sspec],
        me,
        far_meta,
        rest,
        *got_far,
    )
    d_gates_far, rg_far = res[0], within_half(res[1:])
    res = call(
        functools.partial(near_grad_kernel, half),
        "near_grad",
        [dense, pair] + pieces,
        [sspec],
        me,
        meta,
        teacher,
        part,
        *got_near,
    )
    student, d_gates_near, rg_near = res[0], res[1], within_half(res[2:])

    grad_far, (gf, df) = backward(rg_far, faf, fbf, "backward_far", after=[xf_sib, xn_sib])
    back_far = within_half(grad_far)
    part_rows = call(
        far_back_kernel,
        "far_back",
        longer,
        [sspec],
        me,
        far_meta,
        d_gates_far,
        *back_far,
    )
    part = to_mirror(part_rows)
    grad_near, (gn, dn) = backward(rg_near, fan, fbn, "backward_near", after=[back_far[1]])
    gf_sib, gn_sib = to_sibling(gf), to_sibling(gn)
    back_near = within_half(grad_near)

    chunk, steps = rows, along
    columns = pl.BlockSpec((across, rows, rows), lambda i: (0, 0, 0))
    part_of = lambda first: pl.BlockSpec((1, rows, rows), lambda i: (across + first + i, 0, 0))
    block = lambda first: pl.BlockSpec((chunk, rows), lambda i: (first + i, 0))
    specs = [columns] * 8
    for first in (0, steps, 0):
        specs += [block(first)] * 2 + [part_of(first)] * 2
    weight_grads, finished = pl.pallas_call(
        weight_kernel,
        grid=(steps,),
        in_specs=specs,
        out_specs=[
            pl.BlockSpec((3, chunk, width), lambda i: (0, i, 0)),
            pl.BlockSpec((8, 128), lambda i: (0, 0)),
        ],
        out_shape=[
            jax.ShapeDtypeStruct((3, units, width), BF16),
            jax.ShapeDtypeStruct((8, 128), F32),
        ],
        cost_estimate=pl.CostEstimate(
            flops=3 * matmul * 2, bytes_accessed=16 * MIB, transcendentals=0
        ),
        compiler_params=pltpu.CompilerParams(vmem_limit_bytes=20 * MIB),
        name="weight_gradients",
    )(
        *(xf, xn, xf_sib, xn_sib),
        *(gf, gn, gf_sib, gn_sib),
        *(df, dn, gf_sib, gn_sib),
        *(df, dn, gf_sib, gn_sib),
        *(hf, hn, xf_sib, xn_sib),
    )

    d_tokens, d_gates = call(
        functools.partial(final_kernel, half),
        "combine_gradients",
        [dense, pair],
        [sspec],
        me,
        meta,
        part,
        d_gates_near,
        *back_near,
        after=[finished],
    )
    return (student, d_tokens, d_gates.T, weight_grads.transpose(1, 0, 2)[None])


def solution(mesh):
    rows = P(("groups", "expert", "dp"), None)
    return jax.shard_map(
        local,
        mesh=mesh,
        in_specs=(rows, rows, rows, rows, P("expert", "dp", None, None)),
        out_specs=(rows, rows, rows, P(("groups", "expert"), "dp", None, None)),
        check_vma=False,
    )
```

time: 120 us -> 117 us (0.975)
  starting transfers between devices: 46.2 us -> 34.4 us
  waiting for transfers between devices: 32.4 us -> 42.1 us
    ppermute x24, waiting for transfers between devices: 13.3 us -> 22.8 us  [within_half(): lax.ppermute(rows_of[s], 'expert', [(i, i ^ s) for i in range(experts)])]
    ppermute x6 -> x5, starting transfers between devices: 14.5 us -> 5.44 us  [to_mirror(): return lax.ppermute(x, 'expert', [(i, i ^ half) for i in range(experts)])]
    ppermute x9 -> x5, starting transfers between devices: 2.16 us -> 0.67 us  [to_sibling(): return lax.ppermute(x, 'dp', [(0, 1), (1, 0)])]
    ppermute x24, starting transfers between devices: 29.6 us -> 28.3 us  [within_half(): lax.ppermute(rows_of[s], 'expert', [(i, i ^ s) for i in range(experts)])]
    unnamed x14 -> x10, local copies, waits for them, and re-layouts: 4.67 us -> 3.7 us
    ppermute x6 -> x5, waiting for transfers between devices: 18.5 us -> 19.3 us  [to_mirror(): return lax.ppermute(x, 'expert', [(i, i ^ half) for i in range(experts)])]
  transfers between devices with their start and end apart: 39 -> 34, of which waited for: 13 -> 15; matrix products, arithmetic and copies ran while one was open for 0% -> 0% of each run, Pallas kernels for 23% -> 30%
where the time goes in v4:
time: 117 us
  waiting for transfers between devices  42.1 us (36%)
  Pallas kernels  36.1 us (31%)
  starting transfers between devices  34.4 us (29%)
  local copies, waits for them, and re-layouts  3.7 us (3%)
    pallas_call x12, Pallas kernels, call(): pl.pallas_call(body, in_specs=specs + [aspec] * (len(after) + len(through...  29.5 us
    ppermute x24, starting transfers between devices, within_half(): lax.ppermute(rows_of[s], 'expert', [(i, i ^ s) for i in range(experts)])  28.3 us
    ppermute x24, waiting for transfers between devices, within_half(): lax.ppermute(rows_of[s], 'expert', [(i, i ^ s) for i in range(experts)])  22.8 us
    ppermute x5, waiting for transfers between devices, to_mirror(): return lax.ppermute(x, 'expert', [(i, i ^ half) for i in range(experts)])  19.3 us
    pallas_call x1, Pallas kernels, local(): pl.pallas_call(weight_kernel, grid=(steps,), in_specs=specs, out_specs=[p...  6.65 us
    ppermute x5, starting transfers between devices, to_mirror(): return lax.ppermute(x, 'expert', [(i, i ^ half) for i in range(experts)])  5.44 us
    unnamed x10, local copies, waits for them, and re-layouts  3.7 us
  transfers between devices with their start and end apart: 34, of which 15 were waited for; matrix products, arithmetic and copies ran while one was open for 0% of the time, Pallas kernels for 30%

profile of v4, /device:TPU:0, one launch (start us, length us, event | category | flops | bytes accessed | tf_op | source)
XLA Modules:
  0.0 117.1 jit_solution(7248940963268287253)
XLA Ops:
  0.6 0.5 collective-permute-start.1
  1.2 2.3 %copy-done = bf16[1,1024,3,768]{3,1,2,0:T(8,128)(2,1)S(1)} copy-done((bf16[1,1024,3,768]{3,1,2,0:T(8,128)(2,1)S(1)}, bf16[1,1024,3,768]{3,1,2,0:T(8,128)(2,1)}, u32[]{:S(2)}) %copy-start) | copy-done | bytes 4718616
  3.5 0.7 copy-done.3
  4.2 0.7 copy-done.4
  4.8 1.5 %pack_near.1 = (f32[8,128]{1,0:T(8,128)S(1)}, bf16[64,768]{1,0:T(8,128)(2,1)S(1)}, bf16[64,768]{1,0:T(8,128)(2,1)S(1)}, bf16[64,768]{1,0:T(8,128)(2,1)S(1)}, bf16[64,768]{1,0:T(8,128)(2,1)S(1)}) custom-call(s32[1]{0:T(128)} %bitcast.refs_0_, bf16[3,1024,768]{2,1,0:T(8,128)(2,1)S(1)} %bitcast.11, s32[2,128]{1,0:T(2,128)S(1)} %bitcast.16, ...), custom_call_target="tpu_custom_call" | custom-call | flops 100000000 | bytes 2097152 | tf_op jit(solution)/shard_map/pack_near/pallas_call | solution.py:286
  6.3 2.6 %collective-permute-start.6 = (bf16[64,768]{1,0:T(8,128)(2,1)S(1)}, bf16[64,768]{1,0:T(8,128)(2,1)S(1)}, u32[]{:S(2)}, u32[]{:S(2)}) collective-permute-start(bf16[64,768]{1,0:T(8,128)(2,1)S(1)} %get-tuple-element.62), channel_id=1, source_target_pairs={{0,2},{2,0},{4,6},{6,4},{8,10},{10,8},{12,14},{14,12},{1,3},{3,1},... | collective-permute-start | bytes 294920 | tf_op jit(solution)/shard_map/ppermute | solution.py:305
  8.9 1.6 %collective-permute-start.7 = (bf16[64,768]{1,0:T(8,128)(2,1)S(1)}, bf16[64,768]{1,0:T(8,128)(2,1)S(1)}, u32[]{:S(2)}, u32[]{:S(2)}) collective-permute-start(bf16[64,768]{1,0:T(8,128)(2,1)S(1)} %get-tuple-element.63), channel_id=1, source_target_pairs={{0,4},{2,6},{4,0},{6,2},{8,12},{10,14},{12,8},{14,10},{1,5},{3,7},... | collective-permute-start | bytes 294920 | tf_op jit(solution)/shard_map/ppermute | solution.py:305
  10.5 3.0 %collective-permute-start.2 = (bf16[128,768]{1,0:T(8,128)(2,1)}, bf16[128,768]{1,0:T(8,128)(2,1)S(1)}, u32[]{:S(2)}, u32[]{:S(2)}) collective-permute-start(bf16[128,768]{1,0:T(8,128)(2,1)} %refs_4_.1), channel_id=1, source_target_pairs={{0,8},{2,10},{4,12},{6,14},{8,0},{10,2},{12,4},{14,6},{1,9},{3,11}... | collective-permute-start | bytes 589832 | tf_op jit(solution)/shard_map/ppermute | solution.py:309
  13.5 4.4 %collective-permute-done.7.refs_4_ = bf16[64,768]{1,0:T(8,128)(2,1)S(1)} collective-permute-done((bf16[64,768]{1,0:T(8,128)(2,1)S(1)}, bf16[64,768]{1,0:T(8,128)(2,1)S(1)}, u32[]{:S(2)}, u32[]{:S(2)}) %collective-permute-start.7) | collective-permute-done | bytes 98336 | tf_op jit(solution)/shard_map/ppermute | solution.py:305
  17.9 0.7 collective-permute-done.8.refs_5_
  18.6 5.7 %forward_near.1 = (bf16[64,768]{1,0:T(8,128)(2,1)S(1)}, bf16[64,768]{1,0:T(8,128)(2,1)S(1)}, bf16[64,768]{1,0:T(8,128)(2,1)S(1)}, bf16[64,768]{1,0:T(8,128)(2,1)...) custom-call(bf16[3,1024,768]{2,1,0:T(8,128)(2,1)S(1)} %bitcast.12, ...), custom_call_target="tpu_custom_call" | custom-call | flops 2415919104 | bytes 2097152 | tf_op jit(solution)/shard_map/forward_near/pallas_call | solution.py:286
  24.2 2.7 %collective-permute-start.9 = (bf16[64,768]{1,0:T(8,128)(2,1)S(1)}, bf16[64,768]{1,0:T(8,128)(2,1)S(1)}, u32[]{:S(2)}, u32[]{:S(2)}) collective-permute-start(bf16[64,768]{1,0:T(8,128)(2,1)S(1)} %get-tuple-element.66), channel_id=1, source_target_pairs={{0,2},{2,0},{4,6},{6,4},{8,10},{10,8},{12,14},{14,12},{1,3},{3,1},... | collective-permute-start | bytes 294920 | tf_op jit(solution)/shard_map/ppermute | solution.py:305
  27.0 1.9 %collective-permute-start.10 = (bf16[64,768]{1,0:T(8,128)(2,1)S(1)}, bf16[64,768]{1,0:T(8,128)(2,1)S(1)}, u32[]{:S(2)}, u32[]{:S(2)}) collective-permute-start(bf16[64,768]{1,0:T(8,128)(2,1)S(1)} %get-tuple-element.67), channel_id=1, source_target_pairs={{0,4},{2,6},{4,0},{6,2},{8,12},{10,14},{12,8},{14,10},{1,5},{3,7},... | collective-permute-start | bytes 294920 | tf_op jit(solution)/shard_map/ppermute | solution.py:305
  28.9 2.7 %collective-permute-done.refs_1_ = f32[8,128]{1,0:T(8,128)S(1)} collective-permute-done((f32[8,128]{1,0:T(8,128)S(1)}, f32[8,128]{1,0:T(8,128)S(1)}, u32[]{:S(2)}, u32[]{:S(2)}) %collective-permute-start) | collective-permute-done | bytes 4128 | tf_op jit(solution)/shard_map/ppermute | solution.py:309
  32.1 0.7 collective-permute-start.4
  32.8 2.7 %collective-permute-start.5 = (bf16[64,768]{1,0:T(8,128)(2,1)S(1)}, bf16[64,768]{1,0:T(8,128)(2,1)S(1)}, u32[]{:S(2)}, u32[]{:S(2)}) collective-permute-start(bf16[64,768]{1,0:T(8,128)(2,1)S(1)} %get-tuple-element.60), channel_id=1, source_target_pairs={{0,6},{2,4},{4,2},{6,0},{8,14},{10,12},{12,10},{14,8},{1,7},{3,5},... | collective-permute-start | bytes 294920 | tf_op jit(solution)/shard_map/ppermute | solution.py:305
  36.0 1.5 %collective-permute-done.3.refs_3_ = bf16[64,768]{1,0:T(8,128)(2,1)S(1)} collective-permute-done((bf16[64,768]{1,0:T(8,128)(2,1)S(1)}, bf16[64,768]{1,0:T(8,128)(2,1)S(1)}, u32[]{:S(2)}, u32[]{:S(2)}) %collective-permute-start.3) | collective-permute-done | bytes 98336 | tf_op jit(solution)/shard_map/ppermute | solution.py:305
  37.6 1.6 %collective-permute-done.5.refs_5_ = bf16[64,768]{1,0:T(8,128)(2,1)S(1)} collective-permute-done((bf16[64,768]{1,0:T(8,128)(2,1)S(1)}, bf16[64,768]{1,0:T(8,128)(2,1)S(1)}, u32[]{:S(2)}, u32[]{:S(2)}) %collective-permute-start.5) | collective-permute-done | bytes 98336 | tf_op jit(solution)/shard_map/ppermute | solution.py:305
  39.1 5.6 %forward_far.1 = (bf16[64,768]{1,0:T(8,128)(2,1)S(1)}, bf16[64,768]{1,0:T(8,128)(2,1)S(1)}, bf16[64,768]{1,0:T(8,128)(2,1)S(1)}, bf16[64,768]{1,0:T(8,128)(2,1)S...) custom-call(bf16[3,1024,768]{2,1,0:T(8,128)(2,1)S(1)} %bitcast.13, ...), custom_call_target="tpu_custom_call" | custom-call | flops 2415919104 | bytes 2097152 | tf_op jit(solution)/shard_map/forward_far/pallas_call | solution.py:286
  45.3 2.0 %collective-permute-start.13 = (bf16[64,768]{1,0:T(8,128)(2,1)S(1)}, bf16[64,768]{1,0:T(8,128)(2,1)S(1)}, u32[]{:S(2)}, u32[]{:S(2)}) collective-permute-start(bf16[64,768]{1,0:T(8,128)(2,1)S(1)} %get-tuple-element.71), channel_id=1, source_target_pairs={{0,4},{2,6},{4,0},{6,2},{8,12},{10,14},{12,8},{14,10},{1,5},{3,7},... | collective-permute-start | bytes 294920 | tf_op jit(solution)/shard_map/ppermute | solution.py:305
  47.4 1.0 collective-permute-start.14
  48.4 1.7 %collective-permute-done.12.refs_3_.refs_4_ = bf16[64,768]{1,0:T(8,128)(2,1)S(1)} collective-permute-done((bf16[64,768]{1,0:T(8,128)(2,1)S(1)}, bf16[64,768]{1,0:T(8,128)(2,1)S(1)}, u32[]{:S(2)}, u32[]{:S(2)}) %collective-permute-start.12) | collective-permute-done | bytes 98336 | tf_op jit(solution)/shard_map/ppermute | solution.py:305
  50.1 0.6 collective-permute-start.16
  50.9 3.9 %collective-permute-done.14.refs_5_.refs_6_ = bf16[64,768]{1,0:T(8,128)(2,1)S(1)} collective-permute-done((bf16[64,768]{1,0:T(8,128)(2,1)S(1)}, bf16[64,768]{1,0:T(8,128)(2,1)S(1)}, u32[]{:S(2)}, u32[]{:S(2)}) %collective-permute-start.14) | collective-permute-done | bytes 98336 | tf_op jit(solution)/shard_map/ppermute | solution.py:305
  55.4 11.0 %collective-permute-done.16.refs_2_ = bf16[128,768]{1,0:T(8,128)(2,1)S(1)} collective-permute-done((bf16[128,768]{1,0:T(8,128)(2,1)S(1)}, bf16[128,768]{1,0:T(8,128)(2,1)S(1)}, u32[]{:S(2)}, u32[]{:S(2)}) %collective-permute-start.16) | collective-permute-done | bytes 196640 | tf_op jit(solution)/shard_map/ppermute | solution.py:309
  66.4 0.8 far_grad.1
  67.2 1.2 %collective-permute-start.17 = (bf16[64,768]{1,0:T(8,128)(2,1)S(1)}, bf16[64,768]{1,0:T(8,128)(2,1)S(1)}, u32[]{:S(2)}, u32[]{:S(2)}) collective-permute-start(bf16[64,768]{1,0:T(8,128)(2,1)S(1)} %get-tuple-element.78), channel_id=1, source_target_pairs={{0,2},{2,0},{4,6},{6,4},{8,10},{10,8},{12,14},{14,12},{1,3},{3,1},... | collective-permute-start | bytes 294920 | tf_op jit(solution)/shard_map/ppermute | solution.py:305
  68.5 1.7 %collective-permute-done.15.refs_3_ = bf16[128,768]{1,0:T(8,128)(2,1)S(1)} collective-permute-done((bf16[128,768]{1,0:T(8,128)(2,1)S(1)}, bf16[128,768]{1,0:T(8,128)(2,1)S(1)}, u32[]{:S(2)}, u32[]{:S(2)}) %collective-permute-start.15) | collective-permute-done | bytes 196640 | tf_op jit(solution)/shard_map/ppermute | solution.py:309
  70.2 0.6 collective-permute-start.19
  70.8 1.2 %near_grad.1 = (bf16[128,768]{1,0:T(8,128)(2,1)}, f32[2,128]{1,0:T(2,128)S(1)}, bf16[64,768]{1,0:T(8,128)(2,1)S(1)}, bf16[64,768]{1,0:T(8,128)(2,1)S(1)}, bf16[6...) custom-call(s32[1]{0:T(128)} %bitcast.refs_0_, f32[8,128]{1,0:T(8,128)S(1)} %get-tuple-element.56.refs_1_, ...), custom_call_target="tpu_custom_call" | custom-call | flops 100000000 | bytes 2097152 | tf_op jit(solution)/shard_map/near_grad/pallas_call | solution.py:286
  72.0 2.0 %collective-permute-start.26 = (bf16[64,768]{1,0:T(8,128)(2,1)S(1)}, bf16[64,768]{1,0:T(8,128)(2,1)S(1)}, u32[]{:S(2)}, u32[]{:S(2)}) collective-permute-start(bf16[64,768]{1,0:T(8,128)(2,1)S(1)} %get-tuple-element.91), channel_id=1, source_target_pairs={{0,2},{2,0},{4,6},{6,4},{8,10},{10,8},{12,14},{14,12},{1,3},{3,1},... | collective-permute-start | bytes 294920 | tf_op jit(solution)/shard_map/ppermute | solution.py:305
  74.1 0.9 collective-permute-start.27
  74.9 1.8 %collective-permute-done.19.refs_7_ = bf16[64,768]{1,0:T(8,128)(2,1)S(1)} collective-permute-done((bf16[64,768]{1,0:T(8,128)(2,1)S(1)}, bf16[64,768]{1,0:T(8,128)(2,1)S(1)}, u32[]{:S(2)}, u32[]{:S(2)}) %collective-permute-start.19) | collective-permute-done | bytes 98336 | tf_op jit(solution)/shard_map/ppermute | solution.py:305
  76.7 6.0 %backward_far.1 = (bf16[64,768]{1,0:T(8,128)(2,1)S(1)}, bf16[64,768]{1,0:T(8,128)(2,1)S(1)}, bf16[64,768]{1,0:T(8,128)(2,1)S(1)}, bf16[64,768]{1,0:T(8,128)(2,1)...) custom-call(bf16[3,1024,768]{2,1,0:T(8,128)(2,1)S(1)} %bitcast.14, ...), custom_call_target="tpu_custom_call" | custom-call | flops 2415919104 | bytes 2097152 | tf_op jit(solution)/shard_map/backward_far/pallas_call | solution.py:286
  82.7 0.9 collective-permute-start.22
  83.7 3.7 %collective-permute-done.22.refs_4_.refs_8_ = bf16[64,768]{1,0:T(8,128)(2,1)S(1)} collective-permute-done((bf16[64,768]{1,0:T(8,128)(2,1)S(1)}, bf16[64,768]{1,0:T(8,128)(2,1)S(1)}, u32[]{:S(2)}, u32[]{:S(2)}) %collective-permute-start.22) | collective-permute-done | bytes 98336 | tf_op jit(solution)/shard_map/ppermute | solution.py:305
  87.4 6.0 %backward_near.1 = (bf16[64,768]{1,0:T(8,128)(2,1)S(1)}, bf16[64,768]{1,0:T(8,128)(2,1)S(1)}, bf16[64,768]{1,0:T(8,128)(2,1)S(1)}, bf16[64,768]{1,0:T(8,128)(2,1...) custom-call(bf16[3,1024,768]{2,1,0:T(8,128)(2,1)S(1)} %bitcast.15, ...), custom_call_target="tpu_custom_call" | custom-call | flops 2415919104 | bytes 2097152 | tf_op jit(solution)/shard_map/backward_near/pallas_call | solution.py:286
  93.5 1.5 %collective-permute-start.23 = (bf16[64,768]{1,0:T(8,128)(2,1)S(1)}, bf16[64,768]{1,0:T(8,128)(2,1)S(1)}, u32[]{:S(2)}, u32[]{:S(2)}) collective-permute-start(bf16[64,768]{1,0:T(8,128)(2,1)S(1)} %get-tuple-element.85), channel_id=1, source_target_pairs={{0,4},{2,6},{4,0},{6,2},{8,12},{10,14},{12,8},{14,10},{1,5},{3,7},... | collective-permute-start | bytes 294920 | tf_op jit(solution)/shard_map/ppermute | solution.py:305
  95.0 1.5 %collective-permute-start.24 = (bf16[64,768]{1,0:T(8,128)(2,1)S(1)}, bf16[64,768]{1,0:T(8,128)(2,1)S(1)}, u32[]{:S(2)}, u32[]{:S(2)}) collective-permute-start(bf16[64,768]{1,0:T(8,128)(2,1)S(1)} %get-tuple-element.86), channel_id=1, source_target_pairs={{0,6},{2,4},{4,2},{6,0},{8,14},{10,12},{12,10},{14,8},{1,7},{3,5},... | collective-permute-start | bytes 294920 | tf_op jit(solution)/shard_map/ppermute | solution.py:305
  96.6 0.5 collective-permute-start.29
  97.1 1.7 %collective-permute-done.23.refs_5_ = bf16[64,768]{1,0:T(8,128)(2,1)S(1)} collective-permute-done((bf16[64,768]{1,0:T(8,128)(2,1)S(1)}, bf16[64,768]{1,0:T(8,128)(2,1)S(1)}, u32[]{:S(2)}, u32[]{:S(2)}) %collective-permute-start.23) | collective-permute-done | bytes 98336 | tf_op jit(solution)/shard_map/ppermute | solution.py:305
  98.7 1.9 %collective-permute-start.30 = (bf16[64,768]{1,0:T(8,128)(2,1)S(1)}, bf16[64,768]{1,0:T(8,128)(2,1)S(1)}, u32[]{:S(2)}, u32[]{:S(2)}) collective-permute-start(bf16[64,768]{1,0:T(8,128)(2,1)S(1)} %get-tuple-element.96), channel_id=1, source_target_pairs={{0,4},{2,6},{4,0},{6,2},{8,12},{10,14},{12,8},{14,10},{1,5},{3,7},... | collective-permute-start | bytes 294920 | tf_op jit(solution)/shard_map/ppermute | solution.py:305
  100.6 1.5 %collective-permute-done.24.refs_6_ = bf16[64,768]{1,0:T(8,128)(2,1)S(1)} collective-permute-done((bf16[64,768]{1,0:T(8,128)(2,1)S(1)}, bf16[64,768]{1,0:T(8,128)(2,1)S(1)}, u32[]{:S(2)}, u32[]{:S(2)}) %collective-permute-start.24) | collective-permute-done | bytes 98336 | tf_op jit(solution)/shard_map/ppermute | solution.py:305
  102.1 1.2 %collective-permute-start.31 = (bf16[64,768]{1,0:T(8,128)(2,1)S(1)}, bf16[64,768]{1,0:T(8,128)(2,1)S(1)}, u32[]{:S(2)}, u32[]{:S(2)}) collective-permute-start(bf16[64,768]{1,0:T(8,128)(2,1)S(1)} %get-tuple-element.97), channel_id=1, source_target_pairs={{0,6},{2,4},{4,2},{6,0},{8,14},{10,12},{12,10},{14,8},{1,7},{3,5},... | collective-permute-start | bytes 294920 | tf_op jit(solution)/shard_map/ppermute | solution.py:305
  103.7 1.8 %collective-permute-start.25 = (bf16[144,768]{1,0:T(8,128)(2,1)S(1)}, bf16[144,768]{1,0:T(8,128)(2,1)S(1)}, u32[]{:S(2)}, u32[]{:S(2)}) collective-permute-start(bf16[144,768]{1,0:T(8,128)(2,1)S(1)} %far_back.1), channel_id=1, source_target_pairs={{0,8},{2,10},{4,12},{6,14},{8,0},{10,2},{12,4},{14,6},{1,9},{3,11}... | collective-permute-start | bytes 663560 | tf_op jit(solution)/shard_map/ppermute | solution.py:309
  105.5 6.7 %weight_gradients.1 = (bf16[3,1024,768]{2,1,0:T(8,128)(2,1)}, f32[8,128]{1,0:T(8,128)S(1)}) custom-call(bf16[7,256,256]{2,1,0:T(8,128)(2,1)S(1)} %get-tuple-element.81.refs_0_, bf16[7,256,256]{2,1,0:T(8,128)(2,1)S(1)} %get-tuple-element.82.refs_1_, bf16[7,256,256]{2,1,0:T(8,128)(2,1)S(1)} %collective-permute-done.20.refs_8_.refs_2_.refs_18_, ...), custom_call_target="tpu_custom_call" | custom-call | flops 4831838208 | bytes 16777216 | tf_op jit(solution)/shard_map/weight_gradients/pallas_call | solution.py:428
  112.2 3.9 %collective-permute-done.25.refs_2_ = bf16[144,768]{1,0:T(8,128)(2,1)S(1)} collective-permute-done((bf16[144,768]{1,0:T(8,128)(2,1)S(1)}, bf16[144,768]{1,0:T(8,128)(2,1)S(1)}, u32[]{:S(2)}, u32[]{:S(2)}) %collective-permute-start.25) | collective-permute-done | bytes 221216 | tf_op jit(solution)/shard_map/ppermute | solution.py:309
  116.0 1.1 combine_gradients.1
  (43 shorter events, 2.9 us)
Async XLA Ops:
  0.6 17.9 %collective-permute-start.1 = (bf16[3,1024,768]{2,1,0:T(8,128)(2,1)}, bf16[3,1024,768]{2,1,0:T(8,128)(2,1)}, u32[]{:S(2)}, u32[]{:S(2)}) collective-permute-start(bf16[3,1024,768]{2,1,0:T(8,128)(2,1)} %bitcast.10), channel_id=1, source_target_pairs={{0,1},{1,0},{2,3},{3,2},{4,5},{5,4},{6,7},{7,6},{8,9},{9,8},{10,11... | collective-permute-start | bytes 14155784 | tf_op jit(solution)/shard_map/ppermute | solution.py:312
  1.1 2.3 %copy-start = (bf16[1,1024,3,768]{3,1,2,0:T(8,128)(2,1)S(1)}, bf16[1,1024,3,768]{3,1,2,0:T(8,128)(2,1)}, u32[]{:S(2)}) copy-start(bf16[1,1024,3,768]{3,1,2,0:T(8,128)(2,1)} %param.9) | copy-start | bytes 14155780
  3.5 0.7 copy-start.3
  4.2 0.7 copy-start.4
  4.8 13.7 %copy-start.1 = (bf16[1,1024,3,768]{3,1,2,0:T(8,128)(2,1)S(1)}, bf16[1,1024,3,768]{3,1,2,0:T(8,128)(2,1)}, u32[]{:S(2)}) copy-start(bf16[1,1024,3,768]{3,1,2,0:T(8,128)(2,1)} %param.9) | copy-start | bytes 14155780
  6.3 7.2 %collective-permute-start.6 = (bf16[64,768]{1,0:T(8,128)(2,1)S(1)}, bf16[64,768]{1,0:T(8,128)(2,1)S(1)}, u32[]{:S(2)}, u32[]{:S(2)}) collective-permute-start(bf16[64,768]{1,0:T(8,128)(2,1)S(1)} %get-tuple-element.62), channel_id=1, source_target_pairs={{0,2},{2,0},{4,6},{6,4},{8,10},{10,8},{12,14},{14,12},{1,3},{3,1},... | collective-permute-start | bytes 294920 | tf_op jit(solution)/shard_map/ppermute | solution.py:305
  8.9 9.0 %collective-permute-start.7 = (bf16[64,768]{1,0:T(8,128)(2,1)S(1)}, bf16[64,768]{1,0:T(8,128)(2,1)S(1)}, u32[]{:S(2)}, u32[]{:S(2)}) collective-permute-start(bf16[64,768]{1,0:T(8,128)(2,1)S(1)} %get-tuple-element.63), channel_id=1, source_target_pairs={{0,4},{2,6},{4,0},{6,2},{8,12},{10,14},{12,8},{14,10},{1,5},{3,7},... | collective-permute-start | bytes 294920 | tf_op jit(solution)/shard_map/ppermute | solution.py:305
  10.5 8.1 %collective-permute-start.8 = (bf16[64,768]{1,0:T(8,128)(2,1)S(1)}, bf16[64,768]{1,0:T(8,128)(2,1)S(1)}, u32[]{:S(2)}, u32[]{:S(2)}) collective-permute-start(bf16[64,768]{1,0:T(8,128)(2,1)S(1)} %get-tuple-element.64), channel_id=1, source_target_pairs={{0,6},{2,4},{4,2},{6,0},{8,14},{10,12},{12,10},{14,8},{1,7},{3,5},... | collective-permute-start | bytes 294920 | tf_op jit(solution)/shard_map/ppermute | solution.py:305
  10.5 21.1 %collective-permute-start.2 = (bf16[128,768]{1,0:T(8,128)(2,1)}, bf16[128,768]{1,0:T(8,128)(2,1)S(1)}, u32[]{:S(2)}, u32[]{:S(2)}) collective-permute-start(bf16[128,768]{1,0:T(8,128)(2,1)} %refs_4_.1), channel_id=1, source_target_pairs={{0,8},{2,10},{4,12},{6,14},{8,0},{10,2},{12,4},{14,6},{1,9},{3,11}... | collective-permute-start | bytes 589832 | tf_op jit(solution)/shard_map/ppermute | solution.py:309
  18.6 17.0 %copy-start.2 = (bf16[128,768]{1,0:T(8,128)(2,1)S(1)}, bf16[128,768]{1,0:T(8,128)(2,1)}, u32[]{:S(2)}) copy-start(bf16[128,768]{1,0:T(8,128)(2,1)} %refs_2_.3) | copy-start | bytes 589828
  24.2 8.6 %collective-permute-start.9 = (bf16[64,768]{1,0:T(8,128)(2,1)S(1)}, bf16[64,768]{1,0:T(8,128)(2,1)S(1)}, u32[]{:S(2)}, u32[]{:S(2)}) collective-permute-start(bf16[64,768]{1,0:T(8,128)(2,1)S(1)} %get-tuple-element.66), channel_id=1, source_target_pairs={{0,2},{2,0},{4,6},{6,4},{8,10},{10,8},{12,14},{14,12},{1,3},{3,1},... | collective-permute-start | bytes 294920 | tf_op jit(solution)/shard_map/ppermute | solution.py:305
  27.0 4.6 %collective-permute-start = (f32[8,128]{1,0:T(8,128)S(1)}, f32[8,128]{1,0:T(8,128)S(1)}, u32[]{:S(2)}, u32[]{:S(2)}) collective-permute-start(f32[8,128]{1,0:T(8,128)S(1)} %get-tuple-element.56.refs_1_), channel_id=1, source_target_pairs={{0,8},{2,10},{4,12},{6,14},{8,0},{10,2},{12,4},{14,6},{1,9},{3,11}... | collective-permute-start | bytes 12296 | tf_op jit(solution)/shard_map/ppermute | solution.py:309
  27.0 8.6 %collective-permute-start.10 = (bf16[64,768]{1,0:T(8,128)(2,1)S(1)}, bf16[64,768]{1,0:T(8,128)(2,1)S(1)}, u32[]{:S(2)}, u32[]{:S(2)}) collective-permute-start(bf16[64,768]{1,0:T(8,128)(2,1)S(1)} %get-tuple-element.67), channel_id=1, source_target_pairs={{0,4},{2,6},{4,0},{6,2},{8,12},{10,14},{12,8},{14,10},{1,5},{3,7},... | collective-permute-start | bytes 294920 | tf_op jit(solution)/shard_map/ppermute | solution.py:305
  28.9 6.6 %collective-permute-start.11 = (bf16[64,768]{1,0:T(8,128)(2,1)S(1)}, bf16[64,768]{1,0:T(8,128)(2,1)S(1)}, u32[]{:S(2)}, u32[]{:S(2)}) collective-permute-start(bf16[64,768]{1,0:T(8,128)(2,1)S(1)} %get-tuple-element.68), channel_id=1, source_target_pairs={{0,6},{2,4},{4,2},{6,0},{8,14},{10,12},{12,10},{14,8},{1,7},{3,5},... | collective-permute-start | bytes 294920 | tf_op jit(solution)/shard_map/ppermute | solution.py:305
  31.9 5.6 %collective-permute-start.3 = (bf16[64,768]{1,0:T(8,128)(2,1)S(1)}, bf16[64,768]{1,0:T(8,128)(2,1)S(1)}, u32[]{:S(2)}, u32[]{:S(2)}) collective-permute-start(bf16[64,768]{1,0:T(8,128)(2,1)S(1)} %get-tuple-element.58), channel_id=1, source_target_pairs={{0,2},{2,0},{4,6},{6,4},{8,10},{10,8},{12,14},{14,12},{1,3},{3,1},... | collective-permute-start | bytes 294920 | tf_op jit(solution)/shard_map/ppermute | solution.py:305
  32.1 5.5 %collective-permute-start.4 = (bf16[64,768]{1,0:T(8,128)(2,1)S(1)}, bf16[64,768]{1,0:T(8,128)(2,1)S(1)}, u32[]{:S(2)}, u32[]{:S(2)}) collective-permute-start(bf16[64,768]{1,0:T(8,128)(2,1)S(1)} %get-tuple-element.59), channel_id=1, source_target_pairs={{0,4},{2,6},{4,0},{6,2},{8,12},{10,14},{12,8},{14,10},{1,5},{3,7},... | collective-permute-start | bytes 294920 | tf_op jit(solution)/shard_map/ppermute | solution.py:305
  32.8 6.3 %collective-permute-start.5 = (bf16[64,768]{1,0:T(8,128)(2,1)S(1)}, bf16[64,768]{1,0:T(8,128)(2,1)S(1)}, u32[]{:S(2)}, u32[]{:S(2)}) collective-permute-start(bf16[64,768]{1,0:T(8,128)(2,1)S(1)} %get-tuple-element.60), channel_id=1, source_target_pairs={{0,6},{2,4},{4,2},{6,0},{8,14},{10,12},{12,10},{14,8},{1,7},{3,5},... | collective-permute-start | bytes 294920 | tf_op jit(solution)/shard_map/ppermute | solution.py:305
  35.5 41.2 %collective-permute-start.21 = (bf16[7,256,256]{2,1,0:T(8,128)(2,1)S(1)}, bf16[7,256,256]{2,1,0:T(8,128)(2,1)S(1)}, u32[]{:S(2)}, u32[]{:S(2)}) collective-permute-start(bf16[7,256,256]{2,1,0:T(8,128)(2,1)S(1)} %get-tuple-element.82.refs_1_), channel_id=1, source_target_pairs={{0,1},{1,0},{2,3},{3,2},{4,5},{5,4},{6,7},{7,6},{8,9},{9,8},{10,11... | collective-permute-start | bytes 2752520 | tf_op jit(solution)/shard_map/ppermute | solution.py:312
  44.8 32.0 %collective-permute-start.20 = (bf16[7,256,256]{2,1,0:T(8,128)(2,1)S(1)}, bf16[7,256,256]{2,1,0:T(8,128)(2,1)S(1)}, u32[]{:S(2)}, u32[]{:S(2)}) collective-permute-start(bf16[7,256,256]{2,1,0:T(8,128)(2,1)S(1)} %get-tuple-element.81.refs_0_), channel_id=1, source_target_pairs={{0,1},{1,0},{2,3},{3,2},{4,5},{5,4},{6,7},{7,6},{8,9},{9,8},{10,11... | collective-permute-start | bytes 2752520 | tf_op jit(solution)/shard_map/ppermute | solution.py:312
  44.9 5.2 %collective-permute-start.12 = (bf16[64,768]{1,0:T(8,128)(2,1)S(1)}, bf16[64,768]{1,0:T(8,128)(2,1)S(1)}, u32[]{:S(2)}, u32[]{:S(2)}) collective-permute-start(bf16[64,768]{1,0:T(8,128)(2,1)S(1)} %get-tuple-element.70), channel_id=1, source_target_pairs={{0,2},{2,0},{4,6},{6,4},{8,10},{10,8},{12,14},{14,12},{1,3},{3,1},... | collective-permute-start | bytes 294920 | tf_op jit(solution)/shard_map/ppermute | solution.py:305
  45.3 5.6 %collective-permute-start.13 = (bf16[64,768]{1,0:T(8,128)(2,1)S(1)}, bf16[64,768]{1,0:T(8,128)(2,1)S(1)}, u32[]{:S(2)}, u32[]{:S(2)}) collective-permute-start(bf16[64,768]{1,0:T(8,128)(2,1)S(1)} %get-tuple-element.71), channel_id=1, source_target_pairs={{0,4},{2,6},{4,0},{6,2},{8,12},{10,14},{12,8},{14,10},{1,5},{3,7},... | collective-permute-start | bytes 294920 | tf_op jit(solution)/shard_map/ppermute | solution.py:305
  47.4 7.5 %collective-permute-start.14 = (bf16[64,768]{1,0:T(8,128)(2,1)S(1)}, bf16[64,768]{1,0:T(8,128)(2,1)S(1)}, u32[]{:S(2)}, u32[]{:S(2)}) collective-permute-start(bf16[64,768]{1,0:T(8,128)(2,1)S(1)} %get-tuple-element.72), channel_id=1, source_target_pairs={{0,6},{2,4},{4,2},{6,0},{8,14},{10,12},{12,10},{14,8},{1,7},{3,5},... | collective-permute-start | bytes 294920 | tf_op jit(solution)/shard_map/ppermute | solution.py:305
  50.1 16.4 %collective-permute-start.16 = (bf16[128,768]{1,0:T(8,128)(2,1)S(1)}, bf16[128,768]{1,0:T(8,128)(2,1)S(1)}, u32[]{:S(2)}, u32[]{:S(2)}) collective-permute-start(bf16[128,768]{1,0:T(8,128)(2,1)S(1)} %near_sum.1.refs_6_), channel_id=1, source_target_pairs={{0,8},{2,10},{4,12},{6,14},{8,0},{10,2},{12,4},{14,6},{1,9},{3,11}... | collective-permute-start | bytes 589832 | tf_op jit(solution)/shard_map/ppermute | solution.py:309
  55.3 14.8 %collective-permute-start.15 = (bf16[128,768]{1,0:T(8,128)(2,1)S(1)}, bf16[128,768]{1,0:T(8,128)(2,1)S(1)}, u32[]{:S(2)}, u32[]{:S(2)}) collective-permute-start(bf16[128,768]{1,0:T(8,128)(2,1)S(1)} %far_sum.1), channel_id=1, source_target_pairs={{0,8},{2,10},{4,12},{6,14},{8,0},{10,2},{12,4},{14,6},{1,9},{3,11}... | collective-permute-start | bytes 589832 | tf_op jit(solution)/shard_map/ppermute | solution.py:309
  67.2 4.8 %collective-permute-start.17 = (bf16[64,768]{1,0:T(8,128)(2,1)S(1)}, bf16[64,768]{1,0:T(8,128)(2,1)S(1)}, u32[]{:S(2)}, u32[]{:S(2)}) collective-permute-start(bf16[64,768]{1,0:T(8,128)(2,1)S(1)} %get-tuple-element.78), channel_id=1, source_target_pairs={{0,2},{2,0},{4,6},{6,4},{8,10},{10,8},{12,14},{14,12},{1,3},{3,1},... | collective-permute-start | bytes 294920 | tf_op jit(solution)/shard_map/ppermute | solution.py:305
  68.5 5.6 %collective-permute-start.18 = (bf16[64,768]{1,0:T(8,128)(2,1)S(1)}, bf16[64,768]{1,0:T(8,128)(2,1)S(1)}, u32[]{:S(2)}, u32[]{:S(2)}) collective-permute-start(bf16[64,768]{1,0:T(8,128)(2,1)S(1)} %get-tuple-element.79), channel_id=1, source_target_pairs={{0,4},{2,6},{4,0},{6,2},{8,12},{10,14},{12,8},{14,10},{1,5},{3,7},... | collective-permute-start | bytes 294920 | tf_op jit(solution)/shard_map/ppermute | solution.py:305
  70.2 6.6 %collective-permute-start.19 = (bf16[64,768]{1,0:T(8,128)(2,1)S(1)}, bf16[64,768]{1,0:T(8,128)(2,1)S(1)}, u32[]{:S(2)}, u32[]{:S(2)}) collective-permute-start(bf16[64,768]{1,0:T(8,128)(2,1)S(1)} %get-tuple-element.80), channel_id=1, source_target_pairs={{0,6},{2,4},{4,2},{6,0},{8,14},{10,12},{12,10},{14,8},{1,7},{3,5},... | collective-permute-start | bytes 294920 | tf_op jit(solution)/shard_map/ppermute | solution.py:305
  72.0 11.6 %collective-permute-start.26 = (bf16[64,768]{1,0:T(8,128)(2,1)S(1)}, bf16[64,768]{1,0:T(8,128)(2,1)S(1)}, u32[]{:S(2)}, u32[]{:S(2)}) collective-permute-start(bf16[64,768]{1,0:T(8,128)(2,1)S(1)} %get-tuple-element.91), channel_id=1, source_target_pairs={{0,2},{2,0},{4,6},{6,4},{8,10},{10,8},{12,14},{14,12},{1,3},{3,1},... | collective-permute-start | bytes 294920 | tf_op jit(solution)/shard_map/ppermute | solution.py:305
  74.1 9.6 %collective-permute-start.27 = (bf16[64,768]{1,0:T(8,128)(2,1)S(1)}, bf16[64,768]{1,0:T(8,128)(2,1)S(1)}, u32[]{:S(2)}, u32[]{:S(2)}) collective-permute-start(bf16[64,768]{1,0:T(8,128)(2,1)S(1)} %get-tuple-element.92), channel_id=1, source_target_pairs={{0,4},{2,6},{4,0},{6,2},{8,12},{10,14},{12,8},{14,10},{1,5},{3,7},... | collective-permute-start | bytes 294920 | tf_op jit(solution)/shard_map/ppermute | solution.py:305
  76.7 6.9 %collective-permute-start.28 = (bf16[64,768]{1,0:T(8,128)(2,1)S(1)}, bf16[64,768]{1,0:T(8,128)(2,1)S(1)}, u32[]{:S(2)}, u32[]{:S(2)}) collective-permute-start(bf16[64,768]{1,0:T(8,128)(2,1)S(1)} %get-tuple-element.93), channel_id=1, source_target_pairs={{0,6},{2,4},{4,2},{6,0},{8,14},{10,12},{12,10},{14,8},{1,7},{3,5},... | collective-permute-start | bytes 294920 | tf_op jit(solution)/shard_map/ppermute | solution.py:305
  82.7 4.7 %collective-permute-start.22 = (bf16[64,768]{1,0:T(8,128)(2,1)S(1)}, bf16[64,768]{1,0:T(8,128)(2,1)S(1)}, u32[]{:S(2)}, u32[]{:S(2)}) collective-permute-start(bf16[64,768]{1,0:T(8,128)(2,1)S(1)} %get-tuple-element.84), channel_id=1, source_target_pairs={{0,2},{2,0},{4,6},{6,4},{8,10},{10,8},{12,14},{14,12},{1,3},{3,1},... | collective-permute-start | bytes 294920 | tf_op jit(solution)/shard_map/ppermute | solution.py:305
  83.7 20.0 %collective-permute-start.32 = (bf16[11,256,256]{2,1,0:T(8,128)(2,1)S(1)}, bf16[11,256,256]{2,1,0:T(8,128)(2,1)S(1)}, u32[]{:S(2)}, u32[]{:S(2)}) collective-permute-start(bf16[11,256,256]{2,1,0:T(8,128)(2,1)S(1)} %get-tuple-element.98.refs_4_), channel_id=1, source_target_pairs={{0,1},{1,0},{2,3},{3,2},{4,5},{5,4},{6,7},{7,6},{8,9},{9,8},{10,11... | collective-permute-start | bytes 4325384 | tf_op jit(solution)/shard_map/ppermute | solution.py:312
  93.4 12.1 %collective-permute-start.33 = (bf16[11,256,256]{2,1,0:T(8,128)(2,1)S(1)}, bf16[11,256,256]{2,1,0:T(8,128)(2,1)S(1)}, u32[]{:S(2)}, u32[]{:S(2)}) collective-permute-start(bf16[11,256,256]{2,1,0:T(8,128)(2,1)S(1)} %get-tuple-element.99.refs_5_), channel_id=1, source_target_pairs={{0,1},{1,0},{2,3},{3,2},{4,5},{5,4},{6,7},{7,6},{8,9},{9,8},{10,11... | collective-permute-start | bytes 4325384 | tf_op jit(solution)/shard_map/ppermute | solution.py:312
  93.5 5.2 %collective-permute-start.23 = (bf16[64,768]{1,0:T(8,128)(2,1)S(1)}, bf16[64,768]{1,0:T(8,128)(2,1)S(1)}, u32[]{:S(2)}, u32[]{:S(2)}) collective-permute-start(bf16[64,768]{1,0:T(8,128)(2,1)S(1)} %get-tuple-element.85), channel_id=1, source_target_pairs={{0,4},{2,6},{4,0},{6,2},{8,12},{10,14},{12,8},{14,10},{1,5},{3,7},... | collective-permute-start | bytes 294920 | tf_op jit(solution)/shard_map/ppermute | solution.py:305
  95.0 7.1 %collective-permute-start.24 = (bf16[64,768]{1,0:T(8,128)(2,1)S(1)}, bf16[64,768]{1,0:T(8,128)(2,1)S(1)}, u32[]{:S(2)}, u32[]{:S(2)}) collective-permute-start(bf16[64,768]{1,0:T(8,128)(2,1)S(1)} %get-tuple-element.86), channel_id=1, source_target_pairs={{0,6},{2,4},{4,2},{6,0},{8,14},{10,12},{12,10},{14,8},{1,7},{3,5},... | collective-permute-start | bytes 294920 | tf_op jit(solution)/shard_map/ppermute | solution.py:305
  96.6 15.6 %collective-permute-start.29 = (bf16[64,768]{1,0:T(8,128)(2,1)S(1)}, bf16[64,768]{1,0:T(8,128)(2,1)S(1)}, u32[]{:S(2)}, u32[]{:S(2)}) collective-permute-start(bf16[64,768]{1,0:T(8,128)(2,1)S(1)} %get-tuple-element.95), channel_id=1, source_target_pairs={{0,2},{2,0},{4,6},{6,4},{8,10},{10,8},{12,14},{14,12},{1,3},{3,1},... | collective-permute-start | bytes 294920 | tf_op jit(solution)/shard_map/ppermute | solution.py:305
  98.7 13.4 %collective-permute-start.30 = (bf16[64,768]{1,0:T(8,128)(2,1)S(1)}, bf16[64,768]{1,0:T(8,128)(2,1)S(1)}, u32[]{:S(2)}, u32[]{:S(2)}) collective-permute-start(bf16[64,768]{1,0:T(8,128)(2,1)S(1)} %get-tuple-element.96), channel_id=1, source_target_pairs={{0,4},{2,6},{4,0},{6,2},{8,12},{10,14},{12,8},{14,10},{1,5},{3,7},... | collective-permute-start | bytes 294920 | tf_op jit(solution)/shard_map/ppermute | solution.py:305
  102.1 10.1 %collective-permute-start.31 = (bf16[64,768]{1,0:T(8,128)(2,1)S(1)}, bf16[64,768]{1,0:T(8,128)(2,1)S(1)}, u32[]{:S(2)}, u32[]{:S(2)}) collective-permute-start(bf16[64,768]{1,0:T(8,128)(2,1)S(1)} %get-tuple-element.97), channel_id=1, source_target_pairs={{0,6},{2,4},{4,2},{6,0},{8,14},{10,12},{12,10},{14,8},{1,7},{3,5},... | collective-permute-start | bytes 294920 | tf_op jit(solution)/shard_map/ppermute | solution.py:305
  103.7 12.4 %collective-permute-start.25 = (bf16[144,768]{1,0:T(8,128)(2,1)S(1)}, bf16[144,768]{1,0:T(8,128)(2,1)S(1)}, u32[]{:S(2)}, u32[]{:S(2)}) collective-permute-start(bf16[144,768]{1,0:T(8,128)(2,1)S(1)} %far_back.1), channel_id=1, source_target_pairs={{0,8},{2,10},{4,12},{6,14},{8,0},{10,2},{12,4},{14,6},{1,9},{3,11}... | collective-permute-start | bytes 663560 | tf_op jit(solution)/shard_map/ppermute | solution.py:309

commit v5 on v4

--- a/solution.py
+++ b/solution.py
@@ -70,8 +70,8 @@
     return jnp.concatenate([ref[...] for ref in refs], axis=0)
 
 
-def masks_of(me_ref, meta, refs):
-    return slot_masks(me_ref[0], meta, len(refs), refs[0].shape[0])
+def masks_of(meta, refs):
+    return slot_masks(lax.axis_index("expert"), meta, len(refs), refs[0].shape[0])
 
 
 def gate_columns(meta):
@@ -79,8 +79,8 @@
     return columns[:, 2:3], columns[:, 3:4]
 
 
-def route_sums(me_ref, meta, refs):
-    m0, m1 = masks_of(me_ref, meta, refs)
+def route_sums(meta, refs):
+    m0, m1 = masks_of(meta, refs)
     got = get(refs)
     g0, g1 = gate_columns(meta)
     o0, o1 = dot(m0, got, FIRST), dot(m1, got, FIRST)
@@ -100,8 +100,7 @@
     put(refs, dot(jnp.concatenate([m0, m1], axis=1), grads))
 
 
-def pack_near_kernel(me_ref, own_ref, routes_ref, gates_ref, tokens_ref, meta_ref, *rows_refs):
-    del own_ref
+def pack_near_kernel(routes_ref, gates_ref, tokens_ref, meta_ref, *rows_refs):
     meta = jnp.concatenate(
         [
             routes_ref[...].astype(F32),
@@ -111,12 +110,12 @@
         axis=0,
     )
     meta_ref[...] = meta
-    m0, m1 = masks_of(me_ref, meta, rows_refs)
+    m0, m1 = masks_of(meta, rows_refs)
     put(rows_refs, dot(m0 + m1, tokens_ref[...]))
 
 
-def pack_far_kernel(me_ref, meta_ref, tokens_ref, *rows_refs):
-    m0, m1 = masks_of(me_ref, meta_ref[...], rows_refs)
+def pack_far_kernel(meta_ref, tokens_ref, *rows_refs):
+    m0, m1 = masks_of(meta_ref[...], rows_refs)
     put(rows_refs, dot(m0 + m1, tokens_ref[...]))
 
 
@@ -162,33 +161,33 @@
     )
 
 
-def near_sum_kernel(me_ref, meta_ref, teacher_ref, *refs):
+def near_sum_kernel(meta_ref, teacher_ref, *refs):
     ins, out_ref = refs[:-1], refs[-1]
-    total = route_sums(me_ref, meta_ref[...], ins)[-1]
+    total = route_sums(meta_ref[...], ins)[-1]
     out_ref[...] = (total - teacher_ref[...].astype(F32)).astype(BF16)
 
 
-def far_sum_kernel(me_ref, meta_ref, *refs):
+def far_sum_kernel(meta_ref, *refs):
     ins, out_ref = refs[:-1], refs[-1]
-    out_ref[...] = route_sums(me_ref, meta_ref[...], ins)[-1].astype(BF16)
-
-
-def far_grad_kernel(pieces, me_ref, meta_ref, rest_ref, *refs):
+    out_ref[...] = route_sums(meta_ref[...], ins)[-1].astype(BF16)
+
+
+def far_grad_kernel(pieces, meta_ref, rest_ref, *refs):
     ins, d_gates_ref, outs = refs[:pieces], refs[pieces], refs[pieces + 1 :]
-    m0, m1, g0, g1, o0, o1, total = route_sums(me_ref, meta_ref[...], ins)
+    m0, m1, g0, g1, o0, o1, total = route_sums(meta_ref[...], ins)
     diff = total + rest_ref[...].astype(F32)
     put_route_grads(outs, m0, m1, g0, g1, diff)
     put_d_gates(d_gates_ref, diff, o0, o1)
 
 
-def near_grad_kernel(pieces, me_ref, meta_ref, teacher_ref, part_ref, *refs):
+def near_grad_kernel(pieces, meta_ref, teacher_ref, part_ref, *refs):
     ins, student_ref, d_gates_ref, outs = (
         refs[:pieces],
         refs[pieces],
         refs[pieces + 1],
         refs[pieces + 2 :],
     )
-    m0, m1, g0, g1, o0, o1, total = route_sums(me_ref, meta_ref[...], ins)
+    m0, m1, g0, g1, o0, o1, total = route_sums(meta_ref[...], ins)
     total = total + part_ref[...].astype(F32)
     student_ref[...] = total.astype(BF16)
     diff = total - teacher_ref[...].astype(F32)
@@ -196,9 +195,9 @@
     put_d_gates(d_gates_ref, diff, o0, o1)
 
 
-def far_back_kernel(me_ref, meta_ref, d_gates_ref, *refs):
+def far_back_kernel(meta_ref, d_gates_ref, *refs):
     ins, out_ref = refs[:-1], refs[-1]
-    m0, m1 = masks_of(me_ref, meta_ref[...], ins)
+    m0, m1 = masks_of(meta_ref[...], ins)
     tok = m0.shape[1]
     out_ref[:tok, :] = dot(m0 + m1, get(ins), FIRST).astype(BF16)
     value = d_gates_ref[...]
@@ -209,9 +208,9 @@
     out_ref[tok:, tok:] = jnp.zeros((out_ref.shape[0] - tok, out_ref.shape[1] - tok), BF16)
 
 
-def final_kernel(pieces, me_ref, meta_ref, part_ref, near_ref, *refs):
+def final_kernel(pieces, meta_ref, part_ref, near_ref, *refs):
     ins, out_ref, d_gates_ref = refs[:pieces], refs[pieces], refs[pieces + 1]
-    m0, m1 = masks_of(me_ref, meta_ref[...], ins)
+    m0, m1 = masks_of(meta_ref[...], ins)
     tok = m0.shape[1]
     total = dot(m0 + m1, get(ins), FIRST) + part_ref[:tok, :].astype(F32)
     out_ref[...] = total.astype(BF16)
@@ -221,14 +220,14 @@
 
 def weight_kernel(*refs):
     refs, out_ref, finished_ref = refs[:-2], refs[-2], refs[-1]
-    xs, rgs = [get_columns(r) for r in refs[0:4]], [get_columns(r) for r in refs[4:8]]
+    xs = jnp.concatenate([get_columns(r) for r in refs[0:4]], axis=0)
+    rgs = jnp.concatenate([get_columns(r) for r in refs[4:8]], axis=0)
     finished_ref[...] = jnp.zeros_like(finished_ref)
     for m, rows in enumerate((xs, xs, rgs)):
-        term = None
-        for ref, row in zip(refs[8 + 4 * m : 12 + 4 * m], rows):
-            act = ref[0] if len(ref.shape) == 3 else ref[...]
-            term = dot(act, row) if term is None else term + dot(act, row)
-        out_ref[m] = term.astype(BF16)
+        acts = [
+            ref[0] if len(ref.shape) == 3 else ref[...] for ref in refs[8 + 4 * m : 12 + 4 * m]
+        ]
+        out_ref[m] = dot(jnp.concatenate(acts, axis=1), rows).astype(BF16)
 
 
 def local(tokens, teacher, routes, gate_weights, weights):
@@ -238,7 +237,6 @@
     capacity = 4 * tok // experts
     rows = half * capacity
     units = weights.shape[1]
-    me = lax.axis_index("expert").reshape(1)
 
     pieces = [jax.ShapeDtypeStruct((capacity, width), BF16)] * half
     dense = jax.ShapeDtypeStruct((tok, width), BF16)
@@ -250,7 +248,6 @@
     sent_g = jax.ShapeDtypeStruct((across + 2 * along, rows, rows), BF16)
     acts2 = jax.ShapeDtypeStruct((2 * units, rows), BF16)
     vspec = pl.BlockSpec(memory_space=pltpu.VMEM)
-    sspec = pl.BlockSpec(memory_space=pltpu.SMEM)
     aspec = pl.BlockSpec(memory_space=pl.ANY)
     matmul = 4 * rows * width * units
 
@@ -352,9 +349,7 @@
         pack_near_kernel,
         "pack_near",
         [jax.ShapeDtypeStruct((8, tok), F32)] + pieces,
-        [sspec],
-        me,
-        own,
+        [],
         routes.T,
         gate_weights.T,
         tokens,
@@ -363,37 +358,37 @@
     meta, x_near = res[0], within_half(res[1:])
     far_meta = to_mirror(meta)
     x_far = within_half(
-        call(pack_far_kernel, "pack_far", pieces, [sspec], me, far_meta, far_tokens)
+        call(pack_far_kernel, "pack_far", pieces, [], far_meta, far_tokens)
     )
 
     out_near, (xn, hn, fan, fbn) = forward(x_near, "forward_near")
     got_near = within_half(out_near)
     rest_rows = call(
-        near_sum_kernel, "near_sum", dense, [sspec], me, meta, teacher, *got_near
+        near_sum_kernel, "near_sum", dense, [], meta, teacher, *got_near
     )
     rest = to_mirror(rest_rows)
-    out_far, (xf, hf, faf, fbf) = forward(x_far, "forward_far", after=[rest_rows])
+    out_far, (xf, hf, faf, fbf) = forward(x_far, "forward_far")
     got_far = within_half(out_far)
     xf_sib, xn_sib = to_sibling(xf), to_sibling(xn)
-    part = to_mirror(call(far_sum_kernel, "far_sum", dense, [sspec], me, far_meta, *got_far))
+    far_rows = call(far_sum_kernel, "far_sum", dense, [], far_meta, *got_far)
+    part = to_mirror(far_rows)
 
     res = call(
         functools.partial(far_grad_kernel, half),
         "far_grad",
         [pair] + pieces,
-        [sspec],
-        me,
+        [],
         far_meta,
         rest,
         *got_far,
+        after=[far_rows],
     )
     d_gates_far, rg_far = res[0], within_half(res[1:])
     res = call(
         functools.partial(near_grad_kernel, half),
         "near_grad",
         [dense, pair] + pieces,
-        [sspec],
-        me,
+        [],
         meta,
         teacher,
         part,
@@ -403,19 +398,19 @@
 
     grad_far, (gf, df) = backward(rg_far, faf, fbf, "backward_far", after=[xf_sib, xn_sib])
     back_far = within_half(grad_far)
-    part_rows = call(
+    grad_near, (gn, dn) = backward(rg_near, fan, fbn, "backward_near", after=back_far[1:])
+    gf_sib, gn_sib = to_sibling(gf), to_sibling(gn)
+    part_rows, *grad_near = call(
         far_back_kernel,
         "far_back",
         longer,
-        [sspec],
-        me,
+        [],
         far_meta,
         d_gates_far,
         *back_far,
+        through=grad_near,
     )
     part = to_mirror(part_rows)
-    grad_near, (gn, dn) = backward(rg_near, fan, fbn, "backward_near", after=[back_far[1]])
-    gf_sib, gn_sib = to_sibling(gf), to_sibling(gn)
     back_near = within_half(grad_near)
 
     chunk, steps = rows, along
@@ -454,8 +449,7 @@
         functools.partial(final_kernel, half),
         "combine_gradients",
         [dense, pair],
-        [sspec],
-        me,
+        [],
         meta,
         part,
         d_gates_near,

time: 117 us -> 102 us (0.87)
  waiting for transfers between devices: 42.1 us -> 25.5 us
  starting transfers between devices: 34.4 us -> 44.9 us
  Pallas kernels: 36.1 us -> 25.7 us
    ppermute x24, waiting for transfers between devices: 22.8 us -> 8.12 us  [within_half(): lax.ppermute(rows_of[s], 'expert', [(i, i ^ s) for i in range(experts)])]
    pallas_call x12, Pallas kernels: 29.5 us -> 19 us  [call(): pl.pallas_call(body, in_specs=specs + [aspec] * (len(after) + len(through...]
    ppermute x5, starting transfers between devices: 5.44 us -> 14.3 us  [to_mirror(): return lax.ppermute(x, 'expert', [(i, i ^ half) for i in range(experts)])]
    ppermute x5, waiting for transfers between devices: 19.3 us -> 17.4 us  [to_mirror(): return lax.ppermute(x, 'expert', [(i, i ^ half) for i in range(experts)])]
    unnamed x10 -> x14, local copies, waits for them, and re-layouts: 3.7 us -> 4.67 us
  transfers between devices with their start and end apart: 34 -> 34, of which waited for: 15 -> 12; matrix products, arithmetic and copies ran while one was open for 0% -> 0% of each run, Pallas kernels for 30% -> 24%
where the time goes in v5:
time: 102 us
  starting transfers between devices  44.9 us (44%)
  Pallas kernels  25.7 us (25%)
  waiting for transfers between devices  25.5 us (25%)
  local copies, waits for them, and re-layouts  4.67 us (5%)
  between operations  1.02 us (1%)
    ppermute x24, starting transfers between devices, within_half(): lax.ppermute(rows_of[s], 'expert', [(i, i ^ s) for i in range(experts)])  29.4 us
    pallas_call x12, Pallas kernels, call(): pl.pallas_call(body, in_specs=specs + [aspec] * (len(after) + len(through...  19 us
    ppermute x5, waiting for transfers between devices, to_mirror(): return lax.ppermute(x, 'expert', [(i, i ^ half) for i in range(experts)])  17.4 us
    ppermute x5, starting transfers between devices, to_mirror(): return lax.ppermute(x, 'expert', [(i, i ^ half) for i in range(experts)])  14.3 us
    ppermute x24, waiting for transfers between devices, within_half(): lax.ppermute(rows_of[s], 'expert', [(i, i ^ s) for i in range(experts)])  8.12 us
    pallas_call x1, Pallas kernels, local(): pl.pallas_call(weight_kernel, grid=(steps,), in_specs=specs, out_specs=[p...  6.65 us
    unnamed x14, local copies, waits for them, and re-layouts  4.67 us
  transfers between devices with their start and end apart: 34, of which 12 were waited for; matrix products, arithmetic and copies ran while one was open for 0% of the time, Pallas kernels for 24%

profile of v5, /device:TPU:0, one launch (start us, length us, event | category | flops | bytes accessed | tf_op | source)
XLA Modules:
  0.0 101.8 jit_solution(8708667508717487378)
XLA Ops:
  1.1 3.7 %collective-permute-start.2 = (bf16[128,768]{1,0:T(8,128)(2,1)}, bf16[128,768]{1,0:T(8,128)(2,1)S(1)}, u32[]{:S(2)}, u32[]{:S(2)}) collective-permute-start(bf16[128,768]{1,0:T(8,128)(2,1)} %refs_2_.1), channel_id=1, source_target_pairs={{0,8},{2,10},{4,12},{6,14},{8,0},{10,2},{12,4},{14,6},{1,9},{3,11}... | collective-permute-start | bytes 589832 | tf_op jit(solution)/shard_map/ppermute | solution.py:306
  4.8 1.0 copy-done.2
  5.8 0.7 copy-done.3
  6.5 0.7 copy-done.4
  7.6 1.8 %collective-permute-start.10 = (bf16[64,768]{1,0:T(8,128)(2,1)S(1)}, bf16[64,768]{1,0:T(8,128)(2,1)S(1)}, u32[]{:S(2)}, u32[]{:S(2)}) collective-permute-start(bf16[64,768]{1,0:T(8,128)(2,1)S(1)} %get-tuple-element.71), channel_id=1, source_target_pairs={{0,2},{2,0},{4,6},{6,4},{8,10},{10,8},{12,14},{14,12},{1,3},{3,1},... | collective-permute-start | bytes 294920 | tf_op jit(solution)/shard_map/ppermute | solution.py:302
  9.4 1.6 %collective-permute-start.11 = (bf16[64,768]{1,0:T(8,128)(2,1)S(1)}, bf16[64,768]{1,0:T(8,128)(2,1)S(1)}, u32[]{:S(2)}, u32[]{:S(2)}) collective-permute-start(bf16[64,768]{1,0:T(8,128)(2,1)S(1)} %get-tuple-element.72), channel_id=1, source_target_pairs={{0,4},{2,6},{4,0},{6,2},{8,12},{10,14},{12,8},{14,10},{1,5},{3,7},... | collective-permute-start | bytes 294920 | tf_op jit(solution)/shard_map/ppermute | solution.py:302
  11.0 4.0 %collective-permute-done.refs_0_ = f32[8,128]{1,0:T(8,128)S(1)} collective-permute-done((f32[8,128]{1,0:T(8,128)S(1)}, f32[8,128]{1,0:T(8,128)S(1)}, u32[]{:S(2)}, u32[]{:S(2)}) %collective-permute-start) | collective-permute-done | bytes 4128 | tf_op jit(solution)/shard_map/ppermute | solution.py:306
  15.0 1.7 %collective-permute-start.12 = (bf16[64,768]{1,0:T(8,128)(2,1)S(1)}, bf16[64,768]{1,0:T(8,128)(2,1)S(1)}, u32[]{:S(2)}, u32[]{:S(2)}) collective-permute-start(bf16[64,768]{1,0:T(8,128)(2,1)S(1)} %get-tuple-element.73), channel_id=1, source_target_pairs={{0,6},{2,4},{4,2},{6,0},{8,14},{10,12},{12,10},{14,8},{1,7},{3,5},... | collective-permute-start | bytes 294920 | tf_op jit(solution)/shard_map/ppermute | solution.py:302
  17.1 0.6 collective-permute-start.3
  17.7 1.2 %collective-permute-start.4 = (bf16[64,768]{1,0:T(8,128)(2,1)S(1)}, bf16[64,768]{1,0:T(8,128)(2,1)S(1)}, u32[]{:S(2)}, u32[]{:S(2)}) collective-permute-start(bf16[64,768]{1,0:T(8,128)(2,1)S(1)} %get-tuple-element.64), channel_id=1, source_target_pairs={{0,4},{2,6},{4,0},{6,2},{8,12},{10,14},{12,8},{14,10},{1,5},{3,7},... | collective-permute-start | bytes 294920 | tf_op jit(solution)/shard_map/ppermute | solution.py:302
  18.9 1.7 %collective-permute-start.5 = (bf16[64,768]{1,0:T(8,128)(2,1)S(1)}, bf16[64,768]{1,0:T(8,128)(2,1)S(1)}, u32[]{:S(2)}, u32[]{:S(2)}) collective-permute-start(bf16[64,768]{1,0:T(8,128)(2,1)S(1)} %get-tuple-element.65), channel_id=1, source_target_pairs={{0,6},{2,4},{4,2},{6,0},{8,14},{10,12},{12,10},{14,8},{1,7},{3,5},... | collective-permute-start | bytes 294920 | tf_op jit(solution)/shard_map/ppermute | solution.py:302
  20.7 2.3 %copy-done = bf16[1,1024,3,768]{3,1,2,0:T(8,128)(2,1)S(1)} copy-done((bf16[1,1024,3,768]{3,1,2,0:T(8,128)(2,1)S(1)}, bf16[1,1024,3,768]{3,1,2,0:T(8,128)(2,1)}, u32[]{:S(2)}) %copy-start) | copy-done | bytes 4718616
  23.0 3.3 %forward_near.1 = (bf16[64,768]{1,0:T(8,128)(2,1)S(1)}, bf16[64,768]{1,0:T(8,128)(2,1)S(1)}, bf16[64,768]{1,0:T(8,128)(2,1)S(1)}, bf16[64,768]{1,0:T(8,128)(2,1)...) custom-call(bf16[3,1024,768]{2,1,0:T(8,128)(2,1)S(1)} %bitcast.10, ...), custom_call_target="tpu_custom_call" | custom-call | flops 2415919104 | bytes 2097152 | tf_op jit(solution)/shard_map/forward_near/pallas_call | solution.py:283
  26.4 3.3 %forward_far.1 = (bf16[64,768]{1,0:T(8,128)(2,1)S(1)}, bf16[64,768]{1,0:T(8,128)(2,1)S(1)}, bf16[64,768]{1,0:T(8,128)(2,1)S(1)}, bf16[64,768]{1,0:T(8,128)(2,1)S...) custom-call(bf16[3,1024,768]{2,1,0:T(8,128)(2,1)S(1)} %bitcast.11, ...), custom_call_target="tpu_custom_call" | custom-call | flops 2415919104 | bytes 2097152 | tf_op jit(solution)/shard_map/forward_far/pallas_call | solution.py:283
  29.7 0.5 collective-permute-start.20
  30.3 2.3 %collective-permute-start.13 = (bf16[64,768]{1,0:T(8,128)(2,1)S(1)}, bf16[64,768]{1,0:T(8,128)(2,1)S(1)}, u32[]{:S(2)}, u32[]{:S(2)}) collective-permute-start(bf16[64,768]{1,0:T(8,128)(2,1)S(1)} %get-tuple-element.75), channel_id=1, source_target_pairs={{0,2},{2,0},{4,6},{6,4},{8,10},{10,8},{12,14},{14,12},{1,3},{3,1},... | collective-permute-start | bytes 294920 | tf_op jit(solution)/shard_map/ppermute | solution.py:302
  32.6 0.7 collective-permute-start.14
  33.3 0.8 collective-permute-start.15
  34.0 1.6 %collective-permute-done.13.refs_4_.refs_3_ = bf16[64,768]{1,0:T(8,128)(2,1)S(1)} collective-permute-done((bf16[64,768]{1,0:T(8,128)(2,1)S(1)}, bf16[64,768]{1,0:T(8,128)(2,1)S(1)}, u32[]{:S(2)}, u32[]{:S(2)}) %collective-permute-start.13) | collective-permute-done | bytes 98336 | tf_op jit(solution)/shard_map/ppermute | solution.py:302
  35.6 1.7 %collective-permute-start.6 = (bf16[64,768]{1,0:T(8,128)(2,1)S(1)}, bf16[64,768]{1,0:T(8,128)(2,1)S(1)}, u32[]{:S(2)}, u32[]{:S(2)}) collective-permute-start(bf16[64,768]{1,0:T(8,128)(2,1)S(1)} %get-tuple-element.67), channel_id=1, source_target_pairs={{0,2},{2,0},{4,6},{6,4},{8,10},{10,8},{12,14},{14,12},{1,3},{3,1},... | collective-permute-start | bytes 294920 | tf_op jit(solution)/shard_map/ppermute | solution.py:302
  37.4 0.8 collective-permute-done.14.refs_5_.refs_4_
  38.1 0.7 collective-permute-start.7
  39.1 1.9 %collective-permute-start.8 = (bf16[64,768]{1,0:T(8,128)(2,1)S(1)}, bf16[64,768]{1,0:T(8,128)(2,1)S(1)}, u32[]{:S(2)}, u32[]{:S(2)}) collective-permute-start(bf16[64,768]{1,0:T(8,128)(2,1)S(1)} %get-tuple-element.69), channel_id=1, source_target_pairs={{0,6},{2,4},{4,2},{6,0},{8,14},{10,12},{12,10},{14,8},{1,7},{3,5},... | collective-permute-start | bytes 294920 | tf_op jit(solution)/shard_map/ppermute | solution.py:302
  41.5 3.7 %collective-permute-start.16 = (bf16[128,768]{1,0:T(8,128)(2,1)S(1)}, bf16[128,768]{1,0:T(8,128)(2,1)S(1)}, u32[]{:S(2)}, u32[]{:S(2)}) collective-permute-start(bf16[128,768]{1,0:T(8,128)(2,1)S(1)} %near_sum.1), channel_id=1, source_target_pairs={{0,8},{2,10},{4,12},{6,14},{8,0},{10,2},{12,4},{14,6},{1,9},{3,11}... | collective-permute-start | bytes 589832 | tf_op jit(solution)/shard_map/ppermute | solution.py:306
  45.6 4.8 %collective-permute-start.9 = (bf16[128,768]{1,0:T(8,128)(2,1)S(1)}, bf16[128,768]{1,0:T(8,128)(2,1)S(1)}, u32[]{:S(2)}, u32[]{:S(2)}) collective-permute-start(bf16[128,768]{1,0:T(8,128)(2,1)S(1)} %far_sum.1.refs_6_), channel_id=1, source_target_pairs={{0,8},{2,10},{4,12},{6,14},{8,0},{10,2},{12,4},{14,6},{1,9},{3,11}... | collective-permute-start | bytes 589832 | tf_op jit(solution)/shard_map/ppermute | solution.py:306
  50.5 8.2 %collective-permute-done.16.refs_1_ = bf16[128,768]{1,0:T(8,128)(2,1)S(1)} collective-permute-done((bf16[128,768]{1,0:T(8,128)(2,1)S(1)}, bf16[128,768]{1,0:T(8,128)(2,1)S(1)}, u32[]{:S(2)}, u32[]{:S(2)}) %collective-permute-start.16) | collective-permute-done | bytes 196640 | tf_op jit(solution)/shard_map/ppermute | solution.py:306
  58.7 0.8 far_grad.1
  59.5 0.8 collective-permute-start.17
  60.2 1.3 %collective-permute-done.9.refs_2_ = bf16[128,768]{1,0:T(8,128)(2,1)S(1)} collective-permute-done((bf16[128,768]{1,0:T(8,128)(2,1)S(1)}, bf16[128,768]{1,0:T(8,128)(2,1)S(1)}, u32[]{:S(2)}, u32[]{:S(2)}) %collective-permute-start.9) | collective-permute-done | bytes 196640 | tf_op jit(solution)/shard_map/ppermute | solution.py:306
  61.5 1.5 %collective-permute-start.19 = (bf16[64,768]{1,0:T(8,128)(2,1)S(1)}, bf16[64,768]{1,0:T(8,128)(2,1)S(1)}, u32[]{:S(2)}, u32[]{:S(2)}) collective-permute-start(bf16[64,768]{1,0:T(8,128)(2,1)S(1)} %get-tuple-element.85), channel_id=1, source_target_pairs={{0,6},{2,4},{4,2},{6,0},{8,14},{10,12},{12,10},{14,8},{1,7},{3,5},... | collective-permute-start | bytes 294920 | tf_op jit(solution)/shard_map/ppermute | solution.py:302
  63.0 1.2 %near_grad.1 = (bf16[128,768]{1,0:T(8,128)(2,1)}, f32[2,128]{1,0:T(2,128)S(1)}, bf16[64,768]{1,0:T(8,128)(2,1)S(1)}, bf16[64,768]{1,0:T(8,128)(2,1)S(1)}, bf16[6...) custom-call(f32[8,128]{1,0:T(8,128)S(1)} %get-tuple-element.61.refs_0_, bf16[128,768]{1,0:T(8,128)(2,1)S(1)} %copy-done.1, ...), custom_call_target="tpu_custom_call" | custom-call | flops 100000000 | bytes 2097152 | tf_op jit(solution)/shard_map/near_grad/pallas_call | solution.py:283
  64.2 0.9 collective-permute-done.17.refs_5_
  65.5 0.7 collective-permute-start.26
  66.2 0.9 collective-permute-done.19.refs_7_
  67.1 2.2 %collective-permute-start.27 = (bf16[64,768]{1,0:T(8,128)(2,1)S(1)}, bf16[64,768]{1,0:T(8,128)(2,1)S(1)}, u32[]{:S(2)}, u32[]{:S(2)}) collective-permute-start(bf16[64,768]{1,0:T(8,128)(2,1)S(1)} %get-tuple-element.97), channel_id=1, source_target_pairs={{0,6},{2,4},{4,2},{6,0},{8,14},{10,12},{12,10},{14,8},{1,7},{3,5},... | collective-permute-start | bytes 294920 | tf_op jit(solution)/shard_map/ppermute | solution.py:302
  69.3 3.7 %backward_far.1 = (bf16[64,768]{1,0:T(8,128)(2,1)S(1)}, bf16[64,768]{1,0:T(8,128)(2,1)S(1)}, bf16[64,768]{1,0:T(8,128)(2,1)S(1)}, bf16[64,768]{1,0:T(8,128)(2,1)...) custom-call(bf16[3,1024,768]{2,1,0:T(8,128)(2,1)S(1)} %bitcast.14, ...), custom_call_target="tpu_custom_call" | custom-call | flops 2415919104 | bytes 2097152 | tf_op jit(solution)/shard_map/backward_far/pallas_call | solution.py:283
  73.6 0.9 collective-permute-start.23
  74.6 2.2 %collective-permute-start.24 = (bf16[64,768]{1,0:T(8,128)(2,1)S(1)}, bf16[64,768]{1,0:T(8,128)(2,1)S(1)}, u32[]{:S(2)}, u32[]{:S(2)}) collective-permute-start(bf16[64,768]{1,0:T(8,128)(2,1)S(1)} %get-tuple-element.91), channel_id=1, source_target_pairs={{0,6},{2,4},{4,2},{6,0},{8,14},{10,12},{12,10},{14,8},{1,7},{3,5},... | collective-permute-start | bytes 294920 | tf_op jit(solution)/shard_map/ppermute | solution.py:302
  76.7 1.1 %collective-permute-done.22.refs_8_.refs_3_ = bf16[64,768]{1,0:T(8,128)(2,1)S(1)} collective-permute-done((bf16[64,768]{1,0:T(8,128)(2,1)S(1)}, bf16[64,768]{1,0:T(8,128)(2,1)S(1)}, u32[]{:S(2)}, u32[]{:S(2)}) %collective-permute-start.22) | collective-permute-done | bytes 98336 | tf_op jit(solution)/shard_map/ppermute | solution.py:302
  78.2 2.1 %collective-permute-done.24.refs_10_.refs_5_ = bf16[64,768]{1,0:T(8,128)(2,1)S(1)} collective-permute-done((bf16[64,768]{1,0:T(8,128)(2,1)S(1)}, bf16[64,768]{1,0:T(8,128)(2,1)S(1)}, u32[]{:S(2)}, u32[]{:S(2)}) %collective-permute-start.24) | collective-permute-done | bytes 98336 | tf_op jit(solution)/shard_map/ppermute | solution.py:302
  80.4 3.7 %backward_near.1 = (bf16[64,768]{1,0:T(8,128)(2,1)S(1)}, bf16[64,768]{1,0:T(8,128)(2,1)S(1)}, bf16[64,768]{1,0:T(8,128)(2,1)S(1)}, bf16[64,768]{1,0:T(8,128)(2,1...) custom-call(bf16[3,1024,768]{2,1,0:T(8,128)(2,1)S(1)} %bitcast.15, ...), custom_call_target="tpu_custom_call" | custom-call | flops 2415919104 | bytes 2097152 | tf_op jit(solution)/shard_map/backward_near/pallas_call | solution.py:283
  84.5 0.7 collective-permute-start.29
  85.2 1.8 %collective-permute-start.30 = (bf16[64,768]{1,0:T(8,128)(2,1)S(1)}, bf16[64,768]{1,0:T(8,128)(2,1)S(1)}, u32[]{:S(2)}, u32[]{:S(2)}) collective-permute-start(bf16[64,768]{1,0:T(8,128)(2,1)S(1)} %get-tuple-element.106), channel_id=1, source_target_pairs={{0,4},{2,6},{4,0},{6,2},{8,12},{10,14},{12,8},{14,10},{1,5},{3,7},... | collective-permute-start | bytes 294920 | tf_op jit(solution)/shard_map/ppermute | solution.py:302
  87.0 1.0 %collective-permute-start.31 = (bf16[64,768]{1,0:T(8,128)(2,1)S(1)}, bf16[64,768]{1,0:T(8,128)(2,1)S(1)}, u32[]{:S(2)}, u32[]{:S(2)}) collective-permute-start(bf16[64,768]{1,0:T(8,128)(2,1)S(1)} %get-tuple-element.107), channel_id=1, source_target_pairs={{0,6},{2,4},{4,2},{6,0},{8,14},{10,12},{12,10},{14,8},{1,7},{3,5},... | collective-permute-start | bytes 294920 | tf_op jit(solution)/shard_map/ppermute | solution.py:302
  88.1 2.0 %collective-permute-start.28 = (bf16[144,768]{1,0:T(8,128)(2,1)S(1)}, bf16[144,768]{1,0:T(8,128)(2,1)S(1)}, u32[]{:S(2)}, u32[]{:S(2)}) collective-permute-start(bf16[144,768]{1,0:T(8,128)(2,1)S(1)} %get-tuple-element.102), channel_id=1, source_target_pairs={{0,8},{2,10},{4,12},{6,14},{8,0},{10,2},{12,4},{14,6},{1,9},{3,11}... | collective-permute-start | bytes 663560 | tf_op jit(solution)/shard_map/ppermute | solution.py:306
  90.1 6.6 %weight_gradients.1 = (bf16[3,1024,768]{2,1,0:T(8,128)(2,1)}, f32[8,128]{1,0:T(8,128)S(1)}) custom-call(bf16[7,256,256]{2,1,0:T(8,128)(2,1)S(1)} %get-tuple-element.86.refs_0_, bf16[7,256,256]{2,1,0:T(8,128)(2,1)S(1)} %get-tuple-element.87.refs_1_, bf16[7,256,256]{2,1,0:T(8,128)(2,1)S(1)} %collective-permute-done.20.refs_8_.refs_2_.refs_18_, ...), custom_call_target="tpu_custom_call" | custom-call | flops 4831838208 | bytes 16777216 | tf_op jit(solution)/shard_map/weight_gradients/pallas_call | solution.py:423
  96.7 4.0 %collective-permute-done.28.refs_1_ = bf16[144,768]{1,0:T(8,128)(2,1)S(1)} collective-permute-done((bf16[144,768]{1,0:T(8,128)(2,1)S(1)}, bf16[144,768]{1,0:T(8,128)(2,1)S(1)}, u32[]{:S(2)}, u32[]{:S(2)}) %collective-permute-start.28) | collective-permute-done | bytes 221216 | tf_op jit(solution)/shard_map/ppermute | solution.py:306
  100.7 1.1 %combine_gradients.1 = (bf16[128,768]{1,0:T(8,128)(2,1)}, f32[2,128]{1,0:T(2,128)}) custom-call(f32[8,128]{1,0:T(8,128)S(1)} %get-tuple-element.61.refs_0_, bf16[144,768]{1,0:T(8,128)(2,1)S(1)} %collective-permute-done.28.refs_1_, f32[2,128]{1,0:T(2,128)S(1)} %get-tuple-element.103.refs_2_, bf16[64,768]{1,0:T(8,128)(2,1)S(1)} %get-tuple-element.104.refs_3_, ...), custom_call_target="tpu_custom_call" | custom-call | flops 100000000 | bytes 2097152 | tf_op jit(solution)/shard_map/combine_gradients/pallas_call | solution.py:283
  (48 shorter events, 4.3 us)
Async XLA Ops:
  0.6 20.0 %collective-permute-start.1 = (bf16[3,1024,768]{2,1,0:T(8,128)(2,1)}, bf16[3,1024,768]{2,1,0:T(8,128)(2,1)S(1)}, u32[]{:S(2)}, u32[]{:S(2)}) collective-permute-start(bf16[3,1024,768]{2,1,0:T(8,128)(2,1)} %bitcast.9), channel_id=1, source_target_pairs={{0,1},{1,0},{2,3},{3,2},{4,5},{5,4},{6,7},{7,6},{8,9},{9,8},{10,11... | collective-permute-start | bytes 14155784 | tf_op jit(solution)/shard_map/ppermute | solution.py:309
  1.1 15.6 %collective-permute-start.2 = (bf16[128,768]{1,0:T(8,128)(2,1)}, bf16[128,768]{1,0:T(8,128)(2,1)S(1)}, u32[]{:S(2)}, u32[]{:S(2)}) collective-permute-start(bf16[128,768]{1,0:T(8,128)(2,1)} %refs_2_.1), channel_id=1, source_target_pairs={{0,8},{2,10},{4,12},{6,14},{8,0},{10,2},{12,4},{14,6},{1,9},{3,11}... | collective-permute-start | bytes 589832 | tf_op jit(solution)/shard_map/ppermute | solution.py:306
  4.8 1.0 copy-start.2
  5.8 0.7 copy-start.3
  6.5 0.7 copy-start.4
  7.5 7.4 %collective-permute-start = (f32[8,128]{1,0:T(8,128)S(1)}, f32[8,128]{1,0:T(8,128)S(1)}, u32[]{:S(2)}, u32[]{:S(2)}) collective-permute-start(f32[8,128]{1,0:T(8,128)S(1)} %get-tuple-element.61.refs_0_), channel_id=1, source_target_pairs={{0,8},{2,10},{4,12},{6,14},{8,0},{10,2},{12,4},{14,6},{1,9},{3,11}... | collective-permute-start | bytes 12296 | tf_op jit(solution)/shard_map/ppermute | solution.py:306
  7.6 10.1 %collective-permute-start.10 = (bf16[64,768]{1,0:T(8,128)(2,1)S(1)}, bf16[64,768]{1,0:T(8,128)(2,1)S(1)}, u32[]{:S(2)}, u32[]{:S(2)}) collective-permute-start(bf16[64,768]{1,0:T(8,128)(2,1)S(1)} %get-tuple-element.71), channel_id=1, source_target_pairs={{0,2},{2,0},{4,6},{6,4},{8,10},{10,8},{12,14},{14,12},{1,3},{3,1},... | collective-permute-start | bytes 294920 | tf_op jit(solution)/shard_map/ppermute | solution.py:302
  9.4 9.5 %collective-permute-start.11 = (bf16[64,768]{1,0:T(8,128)(2,1)S(1)}, bf16[64,768]{1,0:T(8,128)(2,1)S(1)}, u32[]{:S(2)}, u32[]{:S(2)}) collective-permute-start(bf16[64,768]{1,0:T(8,128)(2,1)S(1)} %get-tuple-element.72), channel_id=1, source_target_pairs={{0,4},{2,6},{4,0},{6,2},{8,12},{10,14},{12,8},{14,10},{1,5},{3,7},... | collective-permute-start | bytes 294920 | tf_op jit(solution)/shard_map/ppermute | solution.py:302
  15.0 5.7 %collective-permute-start.12 = (bf16[64,768]{1,0:T(8,128)(2,1)S(1)}, bf16[64,768]{1,0:T(8,128)(2,1)S(1)}, u32[]{:S(2)}, u32[]{:S(2)}) collective-permute-start(bf16[64,768]{1,0:T(8,128)(2,1)S(1)} %get-tuple-element.73), channel_id=1, source_target_pairs={{0,6},{2,4},{4,2},{6,0},{8,14},{10,12},{12,10},{14,8},{1,7},{3,5},... | collective-permute-start | bytes 294920 | tf_op jit(solution)/shard_map/ppermute | solution.py:302
  17.1 9.3 %collective-permute-start.3 = (bf16[64,768]{1,0:T(8,128)(2,1)S(1)}, bf16[64,768]{1,0:T(8,128)(2,1)S(1)}, u32[]{:S(2)}, u32[]{:S(2)}) collective-permute-start(bf16[64,768]{1,0:T(8,128)(2,1)S(1)} %get-tuple-element.63), channel_id=1, source_target_pairs={{0,2},{2,0},{4,6},{6,4},{8,10},{10,8},{12,14},{14,12},{1,3},{3,1},... | collective-permute-start | bytes 294920 | tf_op jit(solution)/shard_map/ppermute | solution.py:302
  17.7 8.7 %collective-permute-start.4 = (bf16[64,768]{1,0:T(8,128)(2,1)S(1)}, bf16[64,768]{1,0:T(8,128)(2,1)S(1)}, u32[]{:S(2)}, u32[]{:S(2)}) collective-permute-start(bf16[64,768]{1,0:T(8,128)(2,1)S(1)} %get-tuple-element.64), channel_id=1, source_target_pairs={{0,4},{2,6},{4,0},{6,2},{8,12},{10,14},{12,8},{14,10},{1,5},{3,7},... | collective-permute-start | bytes 294920 | tf_op jit(solution)/shard_map/ppermute | solution.py:302
  18.9 7.5 %collective-permute-start.5 = (bf16[64,768]{1,0:T(8,128)(2,1)S(1)}, bf16[64,768]{1,0:T(8,128)(2,1)S(1)}, u32[]{:S(2)}, u32[]{:S(2)}) collective-permute-start(bf16[64,768]{1,0:T(8,128)(2,1)S(1)} %get-tuple-element.65), channel_id=1, source_target_pairs={{0,6},{2,4},{4,2},{6,0},{8,14},{10,12},{12,10},{14,8},{1,7},{3,5},... | collective-permute-start | bytes 294920 | tf_op jit(solution)/shard_map/ppermute | solution.py:302
  20.7 2.3 %copy-start = (bf16[1,1024,3,768]{3,1,2,0:T(8,128)(2,1)S(1)}, bf16[1,1024,3,768]{3,1,2,0:T(8,128)(2,1)}, u32[]{:S(2)}) copy-start(bf16[1,1024,3,768]{3,1,2,0:T(8,128)(2,1)} %param.9) | copy-start | bytes 14155780
  26.3 43.0 %collective-permute-start.21 = (bf16[7,256,256]{2,1,0:T(8,128)(2,1)S(1)}, bf16[7,256,256]{2,1,0:T(8,128)(2,1)S(1)}, u32[]{:S(2)}, u32[]{:S(2)}) collective-permute-start(bf16[7,256,256]{2,1,0:T(8,128)(2,1)S(1)} %get-tuple-element.87.refs_1_), channel_id=1, source_target_pairs={{0,1},{1,0},{2,3},{3,2},{4,5},{5,4},{6,7},{7,6},{8,9},{9,8},{10,11... | collective-permute-start | bytes 2752520 | tf_op jit(solution)/shard_map/ppermute | solution.py:309
  26.4 42.9 %slice-start = ((s8[4718592]{0:T(1024)(128)(4,1)}), s8[4194304]{0:T(1024)(128)(4,1)S(1)}, s32[]{:S(2)}) async-start(s8[4718592]{0:T(1024)(128)(4,1)} %bitcast.12), calls=%async_computation | async-start | bytes 8388608
  26.4 14.6 %copy-start.1 = (bf16[128,768]{1,0:T(8,128)(2,1)S(1)}, bf16[128,768]{1,0:T(8,128)(2,1)}, u32[]{:S(2)}) copy-start(bf16[128,768]{1,0:T(8,128)(2,1)} %refs_1_.3) | copy-start | bytes 589828
  26.4 42.9 %slice-start.1 = ((s8[4718592]{0:T(1024)(128)(4,1)}), s8[524288]{0:T(1024)(128)(4,1)S(1)}, s32[]{:S(2)}) async-start(s8[4718592]{0:T(1024)(128)(4,1)} %bitcast.12), calls=%async_computation.1 | async-start | bytes 1048576
  29.7 39.6 %collective-permute-start.20 = (bf16[7,256,256]{2,1,0:T(8,128)(2,1)S(1)}, bf16[7,256,256]{2,1,0:T(8,128)(2,1)S(1)}, u32[]{:S(2)}, u32[]{:S(2)}) collective-permute-start(bf16[7,256,256]{2,1,0:T(8,128)(2,1)S(1)} %get-tuple-element.86.refs_0_), channel_id=1, source_target_pairs={{0,1},{1,0},{2,3},{3,2},{4,5},{5,4},{6,7},{7,6},{8,9},{9,8},{10,11... | collective-permute-start | bytes 2752520 | tf_op jit(solution)/shard_map/ppermute | solution.py:309
  30.3 5.3 %collective-permute-start.13 = (bf16[64,768]{1,0:T(8,128)(2,1)S(1)}, bf16[64,768]{1,0:T(8,128)(2,1)S(1)}, u32[]{:S(2)}, u32[]{:S(2)}) collective-permute-start(bf16[64,768]{1,0:T(8,128)(2,1)S(1)} %get-tuple-element.75), channel_id=1, source_target_pairs={{0,2},{2,0},{4,6},{6,4},{8,10},{10,8},{12,14},{14,12},{1,3},{3,1},... | collective-permute-start | bytes 294920 | tf_op jit(solution)/shard_map/ppermute | solution.py:302
  32.6 5.6 %collective-permute-start.14 = (bf16[64,768]{1,0:T(8,128)(2,1)S(1)}, bf16[64,768]{1,0:T(8,128)(2,1)S(1)}, u32[]{:S(2)}, u32[]{:S(2)}) collective-permute-start(bf16[64,768]{1,0:T(8,128)(2,1)S(1)} %get-tuple-element.76), channel_id=1, source_target_pairs={{0,4},{2,6},{4,0},{6,2},{8,12},{10,14},{12,8},{14,10},{1,5},{3,7},... | collective-permute-start | bytes 294920 | tf_op jit(solution)/shard_map/ppermute | solution.py:302
  33.3 5.8 %collective-permute-start.15 = (bf16[64,768]{1,0:T(8,128)(2,1)S(1)}, bf16[64,768]{1,0:T(8,128)(2,1)S(1)}, u32[]{:S(2)}, u32[]{:S(2)}) collective-permute-start(bf16[64,768]{1,0:T(8,128)(2,1)S(1)} %get-tuple-element.77), channel_id=1, source_target_pairs={{0,6},{2,4},{4,2},{6,0},{8,14},{10,12},{12,10},{14,8},{1,7},{3,5},... | collective-permute-start | bytes 294920 | tf_op jit(solution)/shard_map/ppermute | solution.py:302
  35.6 5.8 %collective-permute-start.6 = (bf16[64,768]{1,0:T(8,128)(2,1)S(1)}, bf16[64,768]{1,0:T(8,128)(2,1)S(1)}, u32[]{:S(2)}, u32[]{:S(2)}) collective-permute-start(bf16[64,768]{1,0:T(8,128)(2,1)S(1)} %get-tuple-element.67), channel_id=1, source_target_pairs={{0,2},{2,0},{4,6},{6,4},{8,10},{10,8},{12,14},{14,12},{1,3},{3,1},... | collective-permute-start | bytes 294920 | tf_op jit(solution)/shard_map/ppermute | solution.py:302
  38.1 7.0 %collective-permute-start.7 = (bf16[64,768]{1,0:T(8,128)(2,1)S(1)}, bf16[64,768]{1,0:T(8,128)(2,1)S(1)}, u32[]{:S(2)}, u32[]{:S(2)}) collective-permute-start(bf16[64,768]{1,0:T(8,128)(2,1)S(1)} %get-tuple-element.68), channel_id=1, source_target_pairs={{0,4},{2,6},{4,0},{6,2},{8,12},{10,14},{12,8},{14,10},{1,5},{3,7},... | collective-permute-start | bytes 294920 | tf_op jit(solution)/shard_map/ppermute | solution.py:302
  39.1 6.1 %collective-permute-start.8 = (bf16[64,768]{1,0:T(8,128)(2,1)S(1)}, bf16[64,768]{1,0:T(8,128)(2,1)S(1)}, u32[]{:S(2)}, u32[]{:S(2)}) collective-permute-start(bf16[64,768]{1,0:T(8,128)(2,1)S(1)} %get-tuple-element.69), channel_id=1, source_target_pairs={{0,6},{2,4},{4,2},{6,0},{8,14},{10,12},{12,10},{14,8},{1,7},{3,5},... | collective-permute-start | bytes 294920 | tf_op jit(solution)/shard_map/ppermute | solution.py:302
  41.5 17.2 %collective-permute-start.16 = (bf16[128,768]{1,0:T(8,128)(2,1)S(1)}, bf16[128,768]{1,0:T(8,128)(2,1)S(1)}, u32[]{:S(2)}, u32[]{:S(2)}) collective-permute-start(bf16[128,768]{1,0:T(8,128)(2,1)S(1)} %near_sum.1), channel_id=1, source_target_pairs={{0,8},{2,10},{4,12},{6,14},{8,0},{10,2},{12,4},{14,6},{1,9},{3,11}... | collective-permute-start | bytes 589832 | tf_op jit(solution)/shard_map/ppermute | solution.py:306
  45.6 15.9 %collective-permute-start.9 = (bf16[128,768]{1,0:T(8,128)(2,1)S(1)}, bf16[128,768]{1,0:T(8,128)(2,1)S(1)}, u32[]{:S(2)}, u32[]{:S(2)}) collective-permute-start(bf16[128,768]{1,0:T(8,128)(2,1)S(1)} %far_sum.1.refs_6_), channel_id=1, source_target_pairs={{0,8},{2,10},{4,12},{6,14},{8,0},{10,2},{12,4},{14,6},{1,9},{3,11}... | collective-permute-start | bytes 589832 | tf_op jit(solution)/shard_map/ppermute | solution.py:306
  59.5 5.7 %collective-permute-start.17 = (bf16[64,768]{1,0:T(8,128)(2,1)S(1)}, bf16[64,768]{1,0:T(8,128)(2,1)S(1)}, u32[]{:S(2)}, u32[]{:S(2)}) collective-permute-start(bf16[64,768]{1,0:T(8,128)(2,1)S(1)} %get-tuple-element.83), channel_id=1, source_target_pairs={{0,2},{2,0},{4,6},{6,4},{8,10},{10,8},{12,14},{14,12},{1,3},{3,1},... | collective-permute-start | bytes 294920 | tf_op jit(solution)/shard_map/ppermute | solution.py:302
  60.2 5.3 %collective-permute-start.18 = (bf16[64,768]{1,0:T(8,128)(2,1)S(1)}, bf16[64,768]{1,0:T(8,128)(2,1)S(1)}, u32[]{:S(2)}, u32[]{:S(2)}) collective-permute-start(bf16[64,768]{1,0:T(8,128)(2,1)S(1)} %get-tuple-element.84), channel_id=1, source_target_pairs={{0,4},{2,6},{4,0},{6,2},{8,12},{10,14},{12,8},{14,10},{1,5},{3,7},... | collective-permute-start | bytes 294920 | tf_op jit(solution)/shard_map/ppermute | solution.py:302
  61.5 5.6 %collective-permute-start.19 = (bf16[64,768]{1,0:T(8,128)(2,1)S(1)}, bf16[64,768]{1,0:T(8,128)(2,1)S(1)}, u32[]{:S(2)}, u32[]{:S(2)}) collective-permute-start(bf16[64,768]{1,0:T(8,128)(2,1)S(1)} %get-tuple-element.85), channel_id=1, source_target_pairs={{0,6},{2,4},{4,2},{6,0},{8,14},{10,12},{12,10},{14,8},{1,7},{3,5},... | collective-permute-start | bytes 294920 | tf_op jit(solution)/shard_map/ppermute | solution.py:302
  65.2 9.4 %collective-permute-start.25 = (bf16[64,768]{1,0:T(8,128)(2,1)S(1)}, bf16[64,768]{1,0:T(8,128)(2,1)S(1)}, u32[]{:S(2)}, u32[]{:S(2)}) collective-permute-start(bf16[64,768]{1,0:T(8,128)(2,1)S(1)} %get-tuple-element.95), channel_id=1, source_target_pairs={{0,2},{2,0},{4,6},{6,4},{8,10},{10,8},{12,14},{14,12},{1,3},{3,1},... | collective-permute-start | bytes 294920 | tf_op jit(solution)/shard_map/ppermute | solution.py:302
  65.5 11.2 %collective-permute-start.26 = (bf16[64,768]{1,0:T(8,128)(2,1)S(1)}, bf16[64,768]{1,0:T(8,128)(2,1)S(1)}, u32[]{:S(2)}, u32[]{:S(2)}) collective-permute-start(bf16[64,768]{1,0:T(8,128)(2,1)S(1)} %get-tuple-element.96), channel_id=1, source_target_pairs={{0,4},{2,6},{4,0},{6,2},{8,12},{10,14},{12,8},{14,10},{1,5},{3,7},... | collective-permute-start | bytes 294920 | tf_op jit(solution)/shard_map/ppermute | solution.py:302
  67.1 9.6 %collective-permute-start.27 = (bf16[64,768]{1,0:T(8,128)(2,1)S(1)}, bf16[64,768]{1,0:T(8,128)(2,1)S(1)}, u32[]{:S(2)}, u32[]{:S(2)}) collective-permute-start(bf16[64,768]{1,0:T(8,128)(2,1)S(1)} %get-tuple-element.97), channel_id=1, source_target_pairs={{0,6},{2,4},{4,2},{6,0},{8,14},{10,12},{12,10},{14,8},{1,7},{3,5},... | collective-permute-start | bytes 294920 | tf_op jit(solution)/shard_map/ppermute | solution.py:302
  73.2 4.7 %collective-permute-start.22 = (bf16[64,768]{1,0:T(8,128)(2,1)S(1)}, bf16[64,768]{1,0:T(8,128)(2,1)S(1)}, u32[]{:S(2)}, u32[]{:S(2)}) collective-permute-start(bf16[64,768]{1,0:T(8,128)(2,1)S(1)} %get-tuple-element.89), channel_id=1, source_target_pairs={{0,2},{2,0},{4,6},{6,4},{8,10},{10,8},{12,14},{14,12},{1,3},{3,1},... | collective-permute-start | bytes 294920 | tf_op jit(solution)/shard_map/ppermute | solution.py:302
  73.6 4.6 %collective-permute-start.23 = (bf16[64,768]{1,0:T(8,128)(2,1)S(1)}, bf16[64,768]{1,0:T(8,128)(2,1)S(1)}, u32[]{:S(2)}, u32[]{:S(2)}) collective-permute-start(bf16[64,768]{1,0:T(8,128)(2,1)S(1)} %get-tuple-element.90), channel_id=1, source_target_pairs={{0,4},{2,6},{4,0},{6,2},{8,12},{10,14},{12,8},{14,10},{1,5},{3,7},... | collective-permute-start | bytes 294920 | tf_op jit(solution)/shard_map/ppermute | solution.py:302
  74.6 5.8 %collective-permute-start.24 = (bf16[64,768]{1,0:T(8,128)(2,1)S(1)}, bf16[64,768]{1,0:T(8,128)(2,1)S(1)}, u32[]{:S(2)}, u32[]{:S(2)}) collective-permute-start(bf16[64,768]{1,0:T(8,128)(2,1)S(1)} %get-tuple-element.91), channel_id=1, source_target_pairs={{0,6},{2,4},{4,2},{6,0},{8,14},{10,12},{12,10},{14,8},{1,7},{3,5},... | collective-permute-start | bytes 294920 | tf_op jit(solution)/shard_map/ppermute | solution.py:302
  76.7 11.3 %collective-permute-start.32 = (bf16[11,256,256]{2,1,0:T(8,128)(2,1)S(1)}, bf16[11,256,256]{2,1,0:T(8,128)(2,1)S(1)}, u32[]{:S(2)}, u32[]{:S(2)}) collective-permute-start(bf16[11,256,256]{2,1,0:T(8,128)(2,1)S(1)} %get-tuple-element.108.refs_4_), channel_id=1, source_target_pairs={{0,1},{1,0},{2,3},{3,2},{4,5},{5,4},{6,7},{7,6},{8,9},{9,8},{10,11... | collective-permute-start | bytes 4325384 | tf_op jit(solution)/shard_map/ppermute | solution.py:309
  84.0 6.1 %collective-permute-start.33 = (bf16[11,256,256]{2,1,0:T(8,128)(2,1)S(1)}, bf16[11,256,256]{2,1,0:T(8,128)(2,1)S(1)}, u32[]{:S(2)}, u32[]{:S(2)}) collective-permute-start(bf16[11,256,256]{2,1,0:T(8,128)(2,1)S(1)} %get-tuple-element.109.refs_5_), channel_id=1, source_target_pairs={{0,1},{1,0},{2,3},{3,2},{4,5},{5,4},{6,7},{7,6},{8,9},{9,8},{10,11... | collective-permute-start | bytes 4325384 | tf_op jit(solution)/shard_map/ppermute | solution.py:309
  84.5 12.2 %collective-permute-start.29 = (bf16[64,768]{1,0:T(8,128)(2,1)S(1)}, bf16[64,768]{1,0:T(8,128)(2,1)S(1)}, u32[]{:S(2)}, u32[]{:S(2)}) collective-permute-start(bf16[64,768]{1,0:T(8,128)(2,1)S(1)} %get-tuple-element.105), channel_id=1, source_target_pairs={{0,2},{2,0},{4,6},{6,4},{8,10},{10,8},{12,14},{14,12},{1,3},{3,1},... | collective-permute-start | bytes 294920 | tf_op jit(solution)/shard_map/ppermute | solution.py:302
  85.2 11.5 %collective-permute-start.30 = (bf16[64,768]{1,0:T(8,128)(2,1)S(1)}, bf16[64,768]{1,0:T(8,128)(2,1)S(1)}, u32[]{:S(2)}, u32[]{:S(2)}) collective-permute-start(bf16[64,768]{1,0:T(8,128)(2,1)S(1)} %get-tuple-element.106), channel_id=1, source_target_pairs={{0,4},{2,6},{4,0},{6,2},{8,12},{10,14},{12,8},{14,10},{1,5},{3,7},... | collective-permute-start | bytes 294920 | tf_op jit(solution)/shard_map/ppermute | solution.py:302
  87.0 9.7 %collective-permute-start.31 = (bf16[64,768]{1,0:T(8,128)(2,1)S(1)}, bf16[64,768]{1,0:T(8,128)(2,1)S(1)}, u32[]{:S(2)}, u32[]{:S(2)}) collective-permute-start(bf16[64,768]{1,0:T(8,128)(2,1)S(1)} %get-tuple-element.107), channel_id=1, source_target_pairs={{0,6},{2,4},{4,2},{6,0},{8,14},{10,12},{12,10},{14,8},{1,7},{3,5},... | collective-permute-start | bytes 294920 | tf_op jit(solution)/shard_map/ppermute | solution.py:302
  88.1 12.7 %collective-permute-start.28 = (bf16[144,768]{1,0:T(8,128)(2,1)S(1)}, bf16[144,768]{1,0:T(8,128)(2,1)S(1)}, u32[]{:S(2)}, u32[]{:S(2)}) collective-permute-start(bf16[144,768]{1,0:T(8,128)(2,1)S(1)} %get-tuple-element.102), channel_id=1, source_target_pairs={{0,8},{2,10},{4,12},{6,14},{8,0},{10,2},{12,4},{14,6},{1,9},{3,11}... | collective-permute-start | bytes 663560 | tf_op jit(solution)/shard_map/ppermute | solution.py:306

commit v6 on v5

--- a/solution.py
+++ b/solution.py
@@ -100,7 +100,8 @@
     put(refs, dot(jnp.concatenate([m0, m1], axis=1), grads))
 
 
-def pack_near_kernel(routes_ref, gates_ref, tokens_ref, meta_ref, *rows_refs):
+def pack_near_kernel(own_ref, routes_ref, gates_ref, tokens_ref, meta_ref, *rows_refs):
+    del own_ref
     meta = jnp.concatenate(
         [
             routes_ref[...].astype(F32),
@@ -167,14 +168,15 @@
     out_ref[...] = (total - teacher_ref[...].astype(F32)).astype(BF16)
 
 
-def far_sum_kernel(meta_ref, *refs):
-    ins, out_ref = refs[:-1], refs[-1]
-    out_ref[...] = route_sums(meta_ref[...], ins)[-1].astype(BF16)
-
-
 def far_grad_kernel(pieces, meta_ref, rest_ref, *refs):
-    ins, d_gates_ref, outs = refs[:pieces], refs[pieces], refs[pieces + 1 :]
+    ins, part_ref, d_gates_ref, outs = (
+        refs[:pieces],
+        refs[pieces],
+        refs[pieces + 1],
+        refs[pieces + 2 :],
+    )
     m0, m1, g0, g1, o0, o1, total = route_sums(meta_ref[...], ins)
+    part_ref[...] = total.astype(BF16)
     diff = total + rest_ref[...].astype(F32)
     put_route_grads(outs, m0, m1, g0, g1, diff)
     put_d_gates(d_gates_ref, diff, o0, o1)
@@ -350,6 +352,7 @@
         "pack_near",
         [jax.ShapeDtypeStruct((8, tok), F32)] + pieces,
         [],
+        own,
         routes.T,
         gate_weights.T,
         tokens,
@@ -363,27 +366,32 @@
 
     out_near, (xn, hn, fan, fbn) = forward(x_near, "forward_near")
     got_near = within_half(out_near)
-    rest_rows = call(
-        near_sum_kernel, "near_sum", dense, [], meta, teacher, *got_near
+    out_far, (xf, hf, faf, fbf) = forward(x_far, "forward_far", after=[xn])
+    rest_rows, *out_far = call(
+        near_sum_kernel,
+        "near_sum",
+        dense,
+        [],
+        meta,
+        teacher,
+        *got_near,
+        through=out_far,
     )
     rest = to_mirror(rest_rows)
-    out_far, (xf, hf, faf, fbf) = forward(x_far, "forward_far")
     got_far = within_half(out_far)
     xf_sib, xn_sib = to_sibling(xf), to_sibling(xn)
-    far_rows = call(far_sum_kernel, "far_sum", dense, [], far_meta, *got_far)
-    part = to_mirror(far_rows)
 
     res = call(
         functools.partial(far_grad_kernel, half),
         "far_grad",
-        [pair] + pieces,
+        [dense, pair] + pieces,
         [],
         far_meta,
         rest,
         *got_far,
-        after=[far_rows],
-    )
-    d_gates_far, rg_far = res[0], within_half(res[1:])
+        after=[xf_sib, xn_sib],
+    )
+    part, d_gates_far, rg_far = to_mirror(res[0]), res[1], within_half(res[2:])
     res = call(
         functools.partial(near_grad_kernel, half),
         "near_grad",
@@ -396,7 +404,7 @@
     )
     student, d_gates_near, rg_near = res[0], res[1], within_half(res[2:])
 
-    grad_far, (gf, df) = backward(rg_far, faf, fbf, "backward_far", after=[xf_sib, xn_sib])
+    grad_far, (gf, df) = backward(rg_far, faf, fbf, "backward_far")
     back_far = within_half(grad_far)
     grad_near, (gn, dn) = backward(rg_near, fan, fbn, "backward_near", after=back_far[1:])
     gf_sib, gn_sib = to_sibling(gf), to_sibling(gn)

time: 102 us -> 98.7 us (0.968)
  starting transfers between devices: 44.9 us -> 41.2 us
  waiting for transfers between devices: 25.5 us -> 26.7 us
    ppermute x24, waiting for transfers between devices: 8.12 us -> 21.4 us  [within_half(): lax.ppermute(rows_of[s], 'expert', [(i, i ^ s) for i in range(experts)])]
    ppermute x5, waiting for transfers between devices: 17.4 us -> 5.3 us  [to_mirror(): return lax.ppermute(x, 'expert', [(i, i ^ half) for i in range(experts)])]
    ppermute x5, starting transfers between devices: 14.3 us -> 9.46 us  [to_mirror(): return lax.ppermute(x, 'expert', [(i, i ^ half) for i in range(experts)])]
    ppermute x24, starting transfers between devices: 29.4 us -> 31 us  [within_half(): lax.ppermute(rows_of[s], 'expert', [(i, i ^ s) for i in range(experts)])]
    pallas_call x12 -> x11, Pallas kernels: 19 us -> 18.6 us  [call(): pl.pallas_call(body, in_specs=specs + [aspec] * (len(after) + len(through...]
    unnamed x14 -> x12, local copies, waits for them, and re-layouts: 4.67 us -> 4.63 us
  transfers between devices with their start and end apart: 34 -> 34, of which waited for: 12 -> 14; matrix products, arithmetic and copies ran while one was open for 0% -> 0% of each run, Pallas kernels for 24% -> 24%
where the time goes in v6:
time: 98.7 us; the launch traced here: 98.5 us
  starting transfers between devices  41.2 us (42%)
  waiting for transfers between devices  26.7 us (27%)
  Pallas kernels  25.2 us (26%)
  local copies, waits for them, and re-layouts  4.63 us (5%)
    ppermute x24, starting transfers between devices, within_half(): lax.ppermute(rows_of[s], 'expert', [(i, i ^ s) for i in range(experts)])  31 us
    ppermute x24, waiting for transfers between devices, within_half(): lax.ppermute(rows_of[s], 'expert', [(i, i ^ s) for i in range(experts)])  21.4 us
    pallas_call x11, Pallas kernels, call(): pl.pallas_call(body, in_specs=specs + [aspec] * (len(after) + len(through...  18.6 us
    ppermute x5, starting transfers between devices, to_mirror(): return lax.ppermute(x, 'expert', [(i, i ^ half) for i in range(experts)])  9.46 us
    pallas_call x1, Pallas kernels, local(): pl.pallas_call(weight_kernel, grid=(steps,), in_specs=specs, out_specs=[p...  6.65 us
    ppermute x5, waiting for transfers between devices, to_mirror(): return lax.ppermute(x, 'expert', [(i, i ^ half) for i in range(experts)])  5.3 us
    unnamed x12, local copies, waits for them, and re-layouts  4.63 us
  transfers between devices with their start and end apart: 34, of which 14 were waited for; matrix products, arithmetic and copies ran while one was open for 0% of the time, Pallas kernels for 24%

profile of v6, /device:TPU:0, one launch (start us, length us, event | category | flops | bytes accessed | tf_op | source)
XLA Modules:
  0.0 98.5 jit_solution(5856603213019956860)
XLA Ops:
  1.1 3.7 %collective-permute-start.8 = (bf16[128,768]{1,0:T(8,128)(2,1)}, bf16[128,768]{1,0:T(8,128)(2,1)S(1)}, u32[]{:S(2)}, u32[]{:S(2)}) collective-permute-start(bf16[128,768]{1,0:T(8,128)(2,1)} %refs_3_.1), channel_id=1, source_target_pairs={{0,8},{2,10},{4,12},{6,14},{8,0},{10,2},{12,4},{14,6},{1,9},{3,11}... | collective-permute-start | bytes 589832 | tf_op jit(solution)/shard_map/ppermute | solution.py:308
  4.8 2.3 %copy-done = bf16[1,1024,3,768]{3,1,2,0:T(8,128)(2,1)S(1)} copy-done((bf16[1,1024,3,768]{3,1,2,0:T(8,128)(2,1)S(1)}, bf16[1,1024,3,768]{3,1,2,0:T(8,128)(2,1)}, u32[]{:S(2)}) %copy-start) | copy-done | bytes 4718616
  7.2 0.9 copy-done.3
  8.1 0.7 copy-done.4
  8.8 0.7 copy-done.5
  9.9 1.8 %collective-permute-start.2 = (bf16[64,768]{1,0:T(8,128)(2,1)S(1)}, bf16[64,768]{1,0:T(8,128)(2,1)S(1)}, u32[]{:S(2)}, u32[]{:S(2)}) collective-permute-start(bf16[64,768]{1,0:T(8,128)(2,1)S(1)} %get-tuple-element.69), channel_id=1, source_target_pairs={{0,2},{2,0},{4,6},{6,4},{8,10},{10,8},{12,14},{14,12},{1,3},{3,1},... | collective-permute-start | bytes 294920 | tf_op jit(solution)/shard_map/ppermute | solution.py:304
  11.7 1.6 %collective-permute-start.3 = (bf16[64,768]{1,0:T(8,128)(2,1)S(1)}, bf16[64,768]{1,0:T(8,128)(2,1)S(1)}, u32[]{:S(2)}, u32[]{:S(2)}) collective-permute-start(bf16[64,768]{1,0:T(8,128)(2,1)S(1)} %get-tuple-element.70), channel_id=1, source_target_pairs={{0,4},{2,6},{4,0},{6,2},{8,12},{10,14},{12,8},{14,10},{1,5},{3,7},... | collective-permute-start | bytes 294920 | tf_op jit(solution)/shard_map/ppermute | solution.py:304
  13.3 1.6 %collective-permute-done.refs_0_ = f32[8,128]{1,0:T(8,128)S(1)} collective-permute-done((f32[8,128]{1,0:T(8,128)S(1)}, f32[8,128]{1,0:T(8,128)S(1)}, u32[]{:S(2)}, u32[]{:S(2)}) %collective-permute-start) | collective-permute-done | bytes 4128 | tf_op jit(solution)/shard_map/ppermute | solution.py:308
  14.9 2.0 %collective-permute-start.4 = (bf16[64,768]{1,0:T(8,128)(2,1)S(1)}, bf16[64,768]{1,0:T(8,128)(2,1)S(1)}, u32[]{:S(2)}, u32[]{:S(2)}) collective-permute-start(bf16[64,768]{1,0:T(8,128)(2,1)S(1)} %get-tuple-element.71), channel_id=1, source_target_pairs={{0,6},{2,4},{4,2},{6,0},{8,14},{10,12},{12,10},{14,8},{1,7},{3,5},... | collective-permute-start | bytes 294920 | tf_op jit(solution)/shard_map/ppermute | solution.py:304
  17.9 1.0 collective-permute-start.10
  18.9 2.0 %collective-permute-start.11 = (bf16[64,768]{1,0:T(8,128)(2,1)S(1)}, bf16[64,768]{1,0:T(8,128)(2,1)S(1)}, u32[]{:S(2)}, u32[]{:S(2)}) collective-permute-start(bf16[64,768]{1,0:T(8,128)(2,1)S(1)} %get-tuple-element.79), channel_id=1, source_target_pairs={{0,6},{2,4},{4,2},{6,0},{8,14},{10,12},{12,10},{14,8},{1,7},{3,5},... | collective-permute-start | bytes 294920 | tf_op jit(solution)/shard_map/ppermute | solution.py:304
  20.9 3.3 %forward_near.1 = (bf16[64,768]{1,0:T(8,128)(2,1)S(1)}, bf16[64,768]{1,0:T(8,128)(2,1)S(1)}, bf16[64,768]{1,0:T(8,128)(2,1)S(1)}, bf16[64,768]{1,0:T(8,128)(2,1)...) custom-call(bf16[3,1024,768]{2,1,0:T(8,128)(2,1)S(1)} %bitcast.11, ...), custom_call_target="tpu_custom_call" | custom-call | flops 2415919104 | bytes 2097152 | tf_op jit(solution)/shard_map/forward_near/pallas_call | solution.py:285
  24.9 3.3 %forward_far.1 = (bf16[64,768]{1,0:T(8,128)(2,1)S(1)}, bf16[64,768]{1,0:T(8,128)(2,1)S(1)}, bf16[64,768]{1,0:T(8,128)(2,1)S(1)}, bf16[64,768]{1,0:T(8,128)(2,1)S...) custom-call(bf16[3,1024,768]{2,1,0:T(8,128)(2,1)S(1)} %bitcast.12, ...), custom_call_target="tpu_custom_call" | custom-call | flops 2415919104 | bytes 2097152 | tf_op jit(solution)/shard_map/forward_far/pallas_call | solution.py:285
  28.3 1.9 %collective-permute-start.5 = (bf16[64,768]{1,0:T(8,128)(2,1)S(1)}, bf16[64,768]{1,0:T(8,128)(2,1)S(1)}, u32[]{:S(2)}, u32[]{:S(2)}) collective-permute-start(bf16[64,768]{1,0:T(8,128)(2,1)S(1)} %get-tuple-element.73), channel_id=1, source_target_pairs={{0,2},{2,0},{4,6},{6,4},{8,10},{10,8},{12,14},{14,12},{1,3},{3,1},... | collective-permute-start | bytes 294920 | tf_op jit(solution)/shard_map/ppermute | solution.py:304
  30.2 1.0 collective-permute-start.6
  31.1 0.7 collective-permute-start.7
  31.8 1.7 %collective-permute-done.5.refs_3_.refs_4_ = bf16[64,768]{1,0:T(8,128)(2,1)S(1)} collective-permute-done((bf16[64,768]{1,0:T(8,128)(2,1)S(1)}, bf16[64,768]{1,0:T(8,128)(2,1)S(1)}, u32[]{:S(2)}, u32[]{:S(2)}) %collective-permute-start.5) | collective-permute-done | bytes 98336 | tf_op jit(solution)/shard_map/ppermute | solution.py:304
  33.5 2.3 %collective-permute-done.6.refs_4_.refs_5_ = bf16[64,768]{1,0:T(8,128)(2,1)S(1)} collective-permute-done((bf16[64,768]{1,0:T(8,128)(2,1)S(1)}, bf16[64,768]{1,0:T(8,128)(2,1)S(1)}, u32[]{:S(2)}, u32[]{:S(2)}) %collective-permute-start.6) | collective-permute-done | bytes 98336 | tf_op jit(solution)/shard_map/ppermute | solution.py:304
  35.7 1.0 %collective-permute-done.7.refs_5_.refs_6_ = bf16[64,768]{1,0:T(8,128)(2,1)S(1)} collective-permute-done((bf16[64,768]{1,0:T(8,128)(2,1)S(1)}, bf16[64,768]{1,0:T(8,128)(2,1)S(1)}, u32[]{:S(2)}, u32[]{:S(2)}) %collective-permute-start.7) | collective-permute-done | bytes 98336 | tf_op jit(solution)/shard_map/ppermute | solution.py:304
  37.2 1.5 %collective-permute-start.13 = (bf16[64,768]{1,0:T(8,128)(2,1)S(1)}, bf16[64,768]{1,0:T(8,128)(2,1)S(1)}, u32[]{:S(2)}, u32[]{:S(2)}) collective-permute-start(bf16[64,768]{1,0:T(8,128)(2,1)S(1)} %get-tuple-element.87), channel_id=1, source_target_pairs={{0,2},{2,0},{4,6},{6,4},{8,10},{10,8},{12,14},{14,12},{1,3},{3,1},... | collective-permute-start | bytes 294920 | tf_op jit(solution)/shard_map/ppermute | solution.py:304
  38.8 2.6 %collective-permute-start.12 = (bf16[128,768]{1,0:T(8,128)(2,1)S(1)}, bf16[128,768]{1,0:T(8,128)(2,1)S(1)}, u32[]{:S(2)}, u32[]{:S(2)}) collective-permute-start(bf16[128,768]{1,0:T(8,128)(2,1)S(1)} %get-tuple-element.85), channel_id=1, source_target_pairs={{0,8},{2,10},{4,12},{6,14},{8,0},{10,2},{12,4},{14,6},{1,9},{3,11}... | collective-permute-start | bytes 589832 | tf_op jit(solution)/shard_map/ppermute | solution.py:308
  41.4 1.7 %collective-permute-start.14 = (bf16[64,768]{1,0:T(8,128)(2,1)S(1)}, bf16[64,768]{1,0:T(8,128)(2,1)S(1)}, u32[]{:S(2)}, u32[]{:S(2)}) collective-permute-start(bf16[64,768]{1,0:T(8,128)(2,1)S(1)} %get-tuple-element.88), channel_id=1, source_target_pairs={{0,4},{2,6},{4,0},{6,2},{8,12},{10,14},{12,8},{14,10},{1,5},{3,7},... | collective-permute-start | bytes 294920 | tf_op jit(solution)/shard_map/ppermute | solution.py:304
  43.1 1.0 %collective-permute-start.15 = (bf16[64,768]{1,0:T(8,128)(2,1)S(1)}, bf16[64,768]{1,0:T(8,128)(2,1)S(1)}, u32[]{:S(2)}, u32[]{:S(2)}) collective-permute-start(bf16[64,768]{1,0:T(8,128)(2,1)S(1)} %get-tuple-element.89), channel_id=1, source_target_pairs={{0,6},{2,4},{4,2},{6,0},{8,14},{10,12},{12,10},{14,8},{1,7},{3,5},... | collective-permute-start | bytes 294920 | tf_op jit(solution)/shard_map/ppermute | solution.py:304
  44.2 4.0 %collective-permute-done.14.refs_4_ = bf16[64,768]{1,0:T(8,128)(2,1)S(1)} collective-permute-done((bf16[64,768]{1,0:T(8,128)(2,1)S(1)}, bf16[64,768]{1,0:T(8,128)(2,1)S(1)}, u32[]{:S(2)}, u32[]{:S(2)}) %collective-permute-start.14) | collective-permute-done | bytes 98336 | tf_op jit(solution)/shard_map/ppermute | solution.py:304
  48.1 3.1 %collective-permute-done.15.refs_5_ = bf16[64,768]{1,0:T(8,128)(2,1)S(1)} collective-permute-done((bf16[64,768]{1,0:T(8,128)(2,1)S(1)}, bf16[64,768]{1,0:T(8,128)(2,1)S(1)}, u32[]{:S(2)}, u32[]{:S(2)}) %collective-permute-start.15) | collective-permute-done | bytes 98336 | tf_op jit(solution)/shard_map/ppermute | solution.py:304
  51.2 0.8 far_grad.1
  52.0 1.0 %collective-permute-start.19 = (bf16[64,768]{1,0:T(8,128)(2,1)S(1)}, bf16[64,768]{1,0:T(8,128)(2,1)S(1)}, u32[]{:S(2)}, u32[]{:S(2)}) collective-permute-start(bf16[64,768]{1,0:T(8,128)(2,1)S(1)} %get-tuple-element.97), channel_id=1, source_target_pairs={{0,2},{2,0},{4,6},{6,4},{8,10},{10,8},{12,14},{14,12},{1,3},{3,1},... | collective-permute-start | bytes 294920 | tf_op jit(solution)/shard_map/ppermute | solution.py:304
  53.0 0.7 collective-permute-start.20
  53.8 1.8 %collective-permute-start.21 = (bf16[64,768]{1,0:T(8,128)(2,1)S(1)}, bf16[64,768]{1,0:T(8,128)(2,1)S(1)}, u32[]{:S(2)}, u32[]{:S(2)}) collective-permute-start(bf16[64,768]{1,0:T(8,128)(2,1)S(1)} %get-tuple-element.99), channel_id=1, source_target_pairs={{0,6},{2,4},{4,2},{6,0},{8,14},{10,12},{12,10},{14,8},{1,7},{3,5},... | collective-permute-start | bytes 294920 | tf_op jit(solution)/shard_map/ppermute | solution.py:304
  55.6 0.8 collective-permute-start.18
  56.9 2.4 %collective-permute-done.20.refs_6_ = bf16[64,768]{1,0:T(8,128)(2,1)S(1)} collective-permute-done((bf16[64,768]{1,0:T(8,128)(2,1)S(1)}, bf16[64,768]{1,0:T(8,128)(2,1)S(1)}, u32[]{:S(2)}, u32[]{:S(2)}) %collective-permute-start.20) | collective-permute-done | bytes 98336 | tf_op jit(solution)/shard_map/ppermute | solution.py:304
  59.2 2.3 %collective-permute-done.21.refs_7_ = bf16[64,768]{1,0:T(8,128)(2,1)S(1)} collective-permute-done((bf16[64,768]{1,0:T(8,128)(2,1)S(1)}, bf16[64,768]{1,0:T(8,128)(2,1)S(1)}, u32[]{:S(2)}, u32[]{:S(2)}) %collective-permute-start.21) | collective-permute-done | bytes 98336 | tf_op jit(solution)/shard_map/ppermute | solution.py:304
  61.5 3.6 %backward_far.1 = (bf16[64,768]{1,0:T(8,128)(2,1)S(1)}, bf16[64,768]{1,0:T(8,128)(2,1)S(1)}, bf16[64,768]{1,0:T(8,128)(2,1)S(1)}, bf16[64,768]{1,0:T(8,128)(2,1)...) custom-call(bf16[3,1024,768]{2,1,0:T(8,128)(2,1)S(1)} %bitcast.13, ...), custom_call_target="tpu_custom_call" | custom-call | flops 2415919104 | bytes 2097152 | tf_op jit(solution)/shard_map/backward_far/pallas_call | solution.py:285
  65.7 1.0 %collective-permute-start.23 = (bf16[64,768]{1,0:T(8,128)(2,1)S(1)}, bf16[64,768]{1,0:T(8,128)(2,1)S(1)}, u32[]{:S(2)}, u32[]{:S(2)}) collective-permute-start(bf16[64,768]{1,0:T(8,128)(2,1)S(1)} %get-tuple-element.102), channel_id=1, source_target_pairs={{0,4},{2,6},{4,0},{6,2},{8,12},{10,14},{12,8},{14,10},{1,5},{3,7},... | collective-permute-start | bytes 294920 | tf_op jit(solution)/shard_map/ppermute | solution.py:304
  66.7 2.0 %collective-permute-start.24 = (bf16[64,768]{1,0:T(8,128)(2,1)S(1)}, bf16[64,768]{1,0:T(8,128)(2,1)S(1)}, u32[]{:S(2)}, u32[]{:S(2)}) collective-permute-start(bf16[64,768]{1,0:T(8,128)(2,1)S(1)} %get-tuple-element.103), channel_id=1, source_target_pairs={{0,6},{2,4},{4,2},{6,0},{8,14},{10,12},{12,10},{14,8},{1,7},{3,5},... | collective-permute-start | bytes 294920 | tf_op jit(solution)/shard_map/ppermute | solution.py:304
  68.7 1.2 %near_grad.1 = (bf16[128,768]{1,0:T(8,128)(2,1)}, f32[2,128]{1,0:T(2,128)S(1)}, bf16[64,768]{1,0:T(8,128)(2,1)S(1)}, bf16[64,768]{1,0:T(8,128)(2,1)S(1)}, bf16[6...) custom-call(f32[8,128]{1,0:T(8,128)S(1)} %get-tuple-element.67.refs_0_, bf16[128,768]{1,0:T(8,128)(2,1)S(1)} %copy-done.2, ...), custom_call_target="tpu_custom_call" | custom-call | flops 100000000 | bytes 2097152 | tf_op jit(solution)/shard_map/near_grad/pallas_call | solution.py:285
  70.4 1.0 collective-permute-start.26
  71.4 2.0 %collective-permute-start.27 = (bf16[64,768]{1,0:T(8,128)(2,1)S(1)}, bf16[64,768]{1,0:T(8,128)(2,1)S(1)}, u32[]{:S(2)}, u32[]{:S(2)}) collective-permute-start(bf16[64,768]{1,0:T(8,128)(2,1)S(1)} %get-tuple-element.109), channel_id=1, source_target_pairs={{0,6},{2,4},{4,2},{6,0},{8,14},{10,12},{12,10},{14,8},{1,7},{3,5},... | collective-permute-start | bytes 294920 | tf_op jit(solution)/shard_map/ppermute | solution.py:304
  73.4 1.1 %collective-permute-done.25.refs_5_ = bf16[64,768]{1,0:T(8,128)(2,1)S(1)} collective-permute-done((bf16[64,768]{1,0:T(8,128)(2,1)S(1)}, bf16[64,768]{1,0:T(8,128)(2,1)S(1)}, u32[]{:S(2)}, u32[]{:S(2)}) %collective-permute-start.25) | collective-permute-done | bytes 98336 | tf_op jit(solution)/shard_map/ppermute | solution.py:304
  75.0 2.0 %collective-permute-done.27.refs_7_ = bf16[64,768]{1,0:T(8,128)(2,1)S(1)} collective-permute-done((bf16[64,768]{1,0:T(8,128)(2,1)S(1)}, bf16[64,768]{1,0:T(8,128)(2,1)S(1)}, u32[]{:S(2)}, u32[]{:S(2)}) %collective-permute-start.27) | collective-permute-done | bytes 98336 | tf_op jit(solution)/shard_map/ppermute | solution.py:304
  77.1 3.7 %backward_near.1 = (bf16[64,768]{1,0:T(8,128)(2,1)S(1)}, bf16[64,768]{1,0:T(8,128)(2,1)S(1)}, bf16[64,768]{1,0:T(8,128)(2,1)S(1)}, bf16[64,768]{1,0:T(8,128)(2,1...) custom-call(bf16[3,1024,768]{2,1,0:T(8,128)(2,1)S(1)} %bitcast.14, ...), custom_call_target="tpu_custom_call" | custom-call | flops 2415919104 | bytes 2097152 | tf_op jit(solution)/shard_map/backward_near/pallas_call | solution.py:285
  81.2 1.0 collective-permute-start.29
  82.2 1.5 %collective-permute-start.30 = (bf16[64,768]{1,0:T(8,128)(2,1)S(1)}, bf16[64,768]{1,0:T(8,128)(2,1)S(1)}, u32[]{:S(2)}, u32[]{:S(2)}) collective-permute-start(bf16[64,768]{1,0:T(8,128)(2,1)S(1)} %get-tuple-element.118), channel_id=1, source_target_pairs={{0,4},{2,6},{4,0},{6,2},{8,12},{10,14},{12,8},{14,10},{1,5},{3,7},... | collective-permute-start | bytes 294920 | tf_op jit(solution)/shard_map/ppermute | solution.py:304
  83.7 1.0 %collective-permute-start.31 = (bf16[64,768]{1,0:T(8,128)(2,1)S(1)}, bf16[64,768]{1,0:T(8,128)(2,1)S(1)}, u32[]{:S(2)}, u32[]{:S(2)}) collective-permute-start(bf16[64,768]{1,0:T(8,128)(2,1)S(1)} %get-tuple-element.119), channel_id=1, source_target_pairs={{0,6},{2,4},{4,2},{6,0},{8,14},{10,12},{12,10},{14,8},{1,7},{3,5},... | collective-permute-start | bytes 294920 | tf_op jit(solution)/shard_map/ppermute | solution.py:304
  84.8 2.3 %collective-permute-start.28 = (bf16[144,768]{1,0:T(8,128)(2,1)S(1)}, bf16[144,768]{1,0:T(8,128)(2,1)S(1)}, u32[]{:S(2)}, u32[]{:S(2)}) collective-permute-start(bf16[144,768]{1,0:T(8,128)(2,1)S(1)} %get-tuple-element.114), channel_id=1, source_target_pairs={{0,8},{2,10},{4,12},{6,14},{8,0},{10,2},{12,4},{14,6},{1,9},{3,11}... | collective-permute-start | bytes 663560 | tf_op jit(solution)/shard_map/ppermute | solution.py:308
  87.1 6.6 %weight_gradients.1 = (bf16[3,1024,768]{2,1,0:T(8,128)(2,1)}, f32[8,128]{1,0:T(8,128)S(1)}) custom-call(bf16[7,256,256]{2,1,0:T(8,128)(2,1)S(1)} %get-tuple-element.90.refs_0_, bf16[7,256,256]{2,1,0:T(8,128)(2,1)S(1)} %get-tuple-element.80.refs_6_.refs_1_, bf16[7,256,256]{2,1,0:T(8,128)(2,1)S(1)} %collective-permute-done.16.refs_6_.refs_2_.refs_18_, ...), custom_call_target="tpu_custom_call" | custom-call | flops 4831838208 | bytes 16777216 | tf_op jit(solution)/shard_map/weight_gradients/pallas_call | solution.py:431
  93.7 3.7 %collective-permute-done.28.refs_1_ = bf16[144,768]{1,0:T(8,128)(2,1)S(1)} collective-permute-done((bf16[144,768]{1,0:T(8,128)(2,1)S(1)}, bf16[144,768]{1,0:T(8,128)(2,1)S(1)}, u32[]{:S(2)}, u32[]{:S(2)}) %collective-permute-start.28) | collective-permute-done | bytes 221216 | tf_op jit(solution)/shard_map/ppermute | solution.py:308
  97.4 1.1 %combine_gradients.1 = (bf16[128,768]{1,0:T(8,128)(2,1)}, f32[2,128]{1,0:T(2,128)}) custom-call(f32[8,128]{1,0:T(8,128)S(1)} %get-tuple-element.67.refs_0_, bf16[144,768]{1,0:T(8,128)(2,1)S(1)} %collective-permute-done.28.refs_1_, f32[2,128]{1,0:T(2,128)S(1)} %get-tuple-element.115.refs_2_, bf16[64,768]{1,0:T(8,128)(2,1)S(1)} %get-tuple-element.116.refs_3_, ...), custom_call_target="tpu_custom_call" | custom-call | flops 100000000 | bytes 2097152 | tf_op jit(solution)/shard_map/combine_gradients/pallas_call | solution.py:285
  (44 shorter events, 5.7 us)
Async XLA Ops:
  0.6 20.2 %collective-permute-start.1 = (bf16[3,1024,768]{2,1,0:T(8,128)(2,1)}, bf16[3,1024,768]{2,1,0:T(8,128)(2,1)S(1)}, u32[]{:S(2)}, u32[]{:S(2)}) collective-permute-start(bf16[3,1024,768]{2,1,0:T(8,128)(2,1)} %bitcast.9), channel_id=1, source_target_pairs={{0,1},{1,0},{2,3},{3,2},{4,5},{5,4},{6,7},{7,6},{8,9},{9,8},{10,11... | collective-permute-start | bytes 14155784 | tf_op jit(solution)/shard_map/ppermute | solution.py:311
  1.1 15.8 %collective-permute-start.8 = (bf16[128,768]{1,0:T(8,128)(2,1)}, bf16[128,768]{1,0:T(8,128)(2,1)S(1)}, u32[]{:S(2)}, u32[]{:S(2)}) collective-permute-start(bf16[128,768]{1,0:T(8,128)(2,1)} %refs_3_.1), channel_id=1, source_target_pairs={{0,8},{2,10},{4,12},{6,14},{8,0},{10,2},{12,4},{14,6},{1,9},{3,11}... | collective-permute-start | bytes 589832 | tf_op jit(solution)/shard_map/ppermute | solution.py:308
  4.8 2.3 %copy-start = (bf16[1,1024,3,768]{3,1,2,0:T(8,128)(2,1)S(1)}, bf16[1,1024,3,768]{3,1,2,0:T(8,128)(2,1)}, u32[]{:S(2)}) copy-start(bf16[1,1024,3,768]{3,1,2,0:T(8,128)(2,1)} %param.9) | copy-start | bytes 14155780
  7.1 0.9 copy-start.3
  8.1 0.7 copy-start.4
  8.8 0.7 copy-start.5
  9.4 11.4 %copy-start.1 = (bf16[1,1024,3,768]{3,1,2,0:T(8,128)(2,1)S(1)}, bf16[1,1024,3,768]{3,1,2,0:T(8,128)(2,1)}, u32[]{:S(2)}) copy-start(bf16[1,1024,3,768]{3,1,2,0:T(8,128)(2,1)} %param.9) | copy-start | bytes 14155780
  9.8 5.1 %collective-permute-start = (f32[8,128]{1,0:T(8,128)S(1)}, f32[8,128]{1,0:T(8,128)S(1)}, u32[]{:S(2)}, u32[]{:S(2)}) collective-permute-start(f32[8,128]{1,0:T(8,128)S(1)} %get-tuple-element.67.refs_0_), channel_id=1, source_target_pairs={{0,8},{2,10},{4,12},{6,14},{8,0},{10,2},{12,4},{14,6},{1,9},{3,11}... | collective-permute-start | bytes 12296 | tf_op jit(solution)/shard_map/ppermute | solution.py:308
  9.9 8.0 %collective-permute-start.2 = (bf16[64,768]{1,0:T(8,128)(2,1)S(1)}, bf16[64,768]{1,0:T(8,128)(2,1)S(1)}, u32[]{:S(2)}, u32[]{:S(2)}) collective-permute-start(bf16[64,768]{1,0:T(8,128)(2,1)S(1)} %get-tuple-element.69), channel_id=1, source_target_pairs={{0,2},{2,0},{4,6},{6,4},{8,10},{10,8},{12,14},{14,12},{1,3},{3,1},... | collective-permute-start | bytes 294920 | tf_op jit(solution)/shard_map/ppermute | solution.py:304
  11.7 7.1 %collective-permute-start.3 = (bf16[64,768]{1,0:T(8,128)(2,1)S(1)}, bf16[64,768]{1,0:T(8,128)(2,1)S(1)}, u32[]{:S(2)}, u32[]{:S(2)}) collective-permute-start(bf16[64,768]{1,0:T(8,128)(2,1)S(1)} %get-tuple-element.70), channel_id=1, source_target_pairs={{0,4},{2,6},{4,0},{6,2},{8,12},{10,14},{12,8},{14,10},{1,5},{3,7},... | collective-permute-start | bytes 294920 | tf_op jit(solution)/shard_map/ppermute | solution.py:304
  14.9 6.0 %collective-permute-start.4 = (bf16[64,768]{1,0:T(8,128)(2,1)S(1)}, bf16[64,768]{1,0:T(8,128)(2,1)S(1)}, u32[]{:S(2)}, u32[]{:S(2)}) collective-permute-start(bf16[64,768]{1,0:T(8,128)(2,1)S(1)} %get-tuple-element.71), channel_id=1, source_target_pairs={{0,6},{2,4},{4,2},{6,0},{8,14},{10,12},{12,10},{14,8},{1,7},{3,5},... | collective-permute-start | bytes 294920 | tf_op jit(solution)/shard_map/ppermute | solution.py:304
  17.3 6.9 %collective-permute-start.9 = (bf16[64,768]{1,0:T(8,128)(2,1)S(1)}, bf16[64,768]{1,0:T(8,128)(2,1)S(1)}, u32[]{:S(2)}, u32[]{:S(2)}) collective-permute-start(bf16[64,768]{1,0:T(8,128)(2,1)S(1)} %get-tuple-element.77), channel_id=1, source_target_pairs={{0,2},{2,0},{4,6},{6,4},{8,10},{10,8},{12,14},{14,12},{1,3},{3,1},... | collective-permute-start | bytes 294920 | tf_op jit(solution)/shard_map/ppermute | solution.py:304
  17.9 6.4 %collective-permute-start.10 = (bf16[64,768]{1,0:T(8,128)(2,1)S(1)}, bf16[64,768]{1,0:T(8,128)(2,1)S(1)}, u32[]{:S(2)}, u32[]{:S(2)}) collective-permute-start(bf16[64,768]{1,0:T(8,128)(2,1)S(1)} %get-tuple-element.78), channel_id=1, source_target_pairs={{0,4},{2,6},{4,0},{6,2},{8,12},{10,14},{12,8},{14,10},{1,5},{3,7},... | collective-permute-start | bytes 294920 | tf_op jit(solution)/shard_map/ppermute | solution.py:304
  18.9 6.0 %collective-permute-start.11 = (bf16[64,768]{1,0:T(8,128)(2,1)S(1)}, bf16[64,768]{1,0:T(8,128)(2,1)S(1)}, u32[]{:S(2)}, u32[]{:S(2)}) collective-permute-start(bf16[64,768]{1,0:T(8,128)(2,1)S(1)} %get-tuple-element.79), channel_id=1, source_target_pairs={{0,6},{2,4},{4,2},{6,0},{8,14},{10,12},{12,10},{14,8},{1,7},{3,5},... | collective-permute-start | bytes 294920 | tf_op jit(solution)/shard_map/ppermute | solution.py:304
  24.2 27.1 %collective-permute-start.17 = (bf16[7,256,256]{2,1,0:T(8,128)(2,1)S(1)}, bf16[7,256,256]{2,1,0:T(8,128)(2,1)S(1)}, u32[]{:S(2)}, u32[]{:S(2)}) collective-permute-start(bf16[7,256,256]{2,1,0:T(8,128)(2,1)S(1)} %get-tuple-element.80.refs_6_.refs_1_), channel_id=1, source_target_pairs={{0,1},{1,0},{2,3},{3,2},{4,5},{5,4},{6,7},{7,6},{8,9},{9,8},{10,11... | collective-permute-start | bytes 2752520 | tf_op jit(solution)/shard_map/ppermute | solution.py:311
  24.9 11.9 %copy-start.2 = (bf16[128,768]{1,0:T(8,128)(2,1)S(1)}, bf16[128,768]{1,0:T(8,128)(2,1)}, u32[]{:S(2)}) copy-start(bf16[128,768]{1,0:T(8,128)(2,1)} %refs_1_.3) | copy-start | bytes 589828
  28.2 23.0 %collective-permute-start.16 = (bf16[7,256,256]{2,1,0:T(8,128)(2,1)S(1)}, bf16[7,256,256]{2,1,0:T(8,128)(2,1)S(1)}, u32[]{:S(2)}, u32[]{:S(2)}) collective-permute-start(bf16[7,256,256]{2,1,0:T(8,128)(2,1)S(1)} %get-tuple-element.90.refs_0_), channel_id=1, source_target_pairs={{0,1},{1,0},{2,3},{3,2},{4,5},{5,4},{6,7},{7,6},{8,9},{9,8},{10,11... | collective-permute-start | bytes 2752520 | tf_op jit(solution)/shard_map/ppermute | solution.py:311
  28.3 5.2 %collective-permute-start.5 = (bf16[64,768]{1,0:T(8,128)(2,1)S(1)}, bf16[64,768]{1,0:T(8,128)(2,1)S(1)}, u32[]{:S(2)}, u32[]{:S(2)}) collective-permute-start(bf16[64,768]{1,0:T(8,128)(2,1)S(1)} %get-tuple-element.73), channel_id=1, source_target_pairs={{0,2},{2,0},{4,6},{6,4},{8,10},{10,8},{12,14},{14,12},{1,3},{3,1},... | collective-permute-start | bytes 294920 | tf_op jit(solution)/shard_map/ppermute | solution.py:304
  30.2 5.6 %collective-permute-start.6 = (bf16[64,768]{1,0:T(8,128)(2,1)S(1)}, bf16[64,768]{1,0:T(8,128)(2,1)S(1)}, u32[]{:S(2)}, u32[]{:S(2)}) collective-permute-start(bf16[64,768]{1,0:T(8,128)(2,1)S(1)} %get-tuple-element.74), channel_id=1, source_target_pairs={{0,4},{2,6},{4,0},{6,2},{8,12},{10,14},{12,8},{14,10},{1,5},{3,7},... | collective-permute-start | bytes 294920 | tf_op jit(solution)/shard_map/ppermute | solution.py:304
  31.1 5.6 %collective-permute-start.7 = (bf16[64,768]{1,0:T(8,128)(2,1)S(1)}, bf16[64,768]{1,0:T(8,128)(2,1)S(1)}, u32[]{:S(2)}, u32[]{:S(2)}) collective-permute-start(bf16[64,768]{1,0:T(8,128)(2,1)S(1)} %get-tuple-element.75), channel_id=1, source_target_pairs={{0,6},{2,4},{4,2},{6,0},{8,14},{10,12},{12,10},{14,8},{1,7},{3,5},... | collective-permute-start | bytes 294920 | tf_op jit(solution)/shard_map/ppermute | solution.py:304
  37.2 5.9 %collective-permute-start.13 = (bf16[64,768]{1,0:T(8,128)(2,1)S(1)}, bf16[64,768]{1,0:T(8,128)(2,1)S(1)}, u32[]{:S(2)}, u32[]{:S(2)}) collective-permute-start(bf16[64,768]{1,0:T(8,128)(2,1)S(1)} %get-tuple-element.87), channel_id=1, source_target_pairs={{0,2},{2,0},{4,6},{6,4},{8,10},{10,8},{12,14},{14,12},{1,3},{3,1},... | collective-permute-start | bytes 294920 | tf_op jit(solution)/shard_map/ppermute | solution.py:304
  38.8 12.4 %collective-permute-start.12 = (bf16[128,768]{1,0:T(8,128)(2,1)S(1)}, bf16[128,768]{1,0:T(8,128)(2,1)S(1)}, u32[]{:S(2)}, u32[]{:S(2)}) collective-permute-start(bf16[128,768]{1,0:T(8,128)(2,1)S(1)} %get-tuple-element.85), channel_id=1, source_target_pairs={{0,8},{2,10},{4,12},{6,14},{8,0},{10,2},{12,4},{14,6},{1,9},{3,11}... | collective-permute-start | bytes 589832 | tf_op jit(solution)/shard_map/ppermute | solution.py:308
  41.4 6.7 %collective-permute-start.14 = (bf16[64,768]{1,0:T(8,128)(2,1)S(1)}, bf16[64,768]{1,0:T(8,128)(2,1)S(1)}, u32[]{:S(2)}, u32[]{:S(2)}) collective-permute-start(bf16[64,768]{1,0:T(8,128)(2,1)S(1)} %get-tuple-element.88), channel_id=1, source_target_pairs={{0,4},{2,6},{4,0},{6,2},{8,12},{10,14},{12,8},{14,10},{1,5},{3,7},... | collective-permute-start | bytes 294920 | tf_op jit(solution)/shard_map/ppermute | solution.py:304
  43.1 8.1 %collective-permute-start.15 = (bf16[64,768]{1,0:T(8,128)(2,1)S(1)}, bf16[64,768]{1,0:T(8,128)(2,1)S(1)}, u32[]{:S(2)}, u32[]{:S(2)}) collective-permute-start(bf16[64,768]{1,0:T(8,128)(2,1)S(1)} %get-tuple-element.89), channel_id=1, source_target_pairs={{0,6},{2,4},{4,2},{6,0},{8,14},{10,12},{12,10},{14,8},{1,7},{3,5},... | collective-permute-start | bytes 294920 | tf_op jit(solution)/shard_map/ppermute | solution.py:304
  52.0 4.8 %collective-permute-start.19 = (bf16[64,768]{1,0:T(8,128)(2,1)S(1)}, bf16[64,768]{1,0:T(8,128)(2,1)S(1)}, u32[]{:S(2)}, u32[]{:S(2)}) collective-permute-start(bf16[64,768]{1,0:T(8,128)(2,1)S(1)} %get-tuple-element.97), channel_id=1, source_target_pairs={{0,2},{2,0},{4,6},{6,4},{8,10},{10,8},{12,14},{14,12},{1,3},{3,1},... | collective-permute-start | bytes 294920 | tf_op jit(solution)/shard_map/ppermute | solution.py:304
  53.0 6.2 %collective-permute-start.20 = (bf16[64,768]{1,0:T(8,128)(2,1)S(1)}, bf16[64,768]{1,0:T(8,128)(2,1)S(1)}, u32[]{:S(2)}, u32[]{:S(2)}) collective-permute-start(bf16[64,768]{1,0:T(8,128)(2,1)S(1)} %get-tuple-element.98), channel_id=1, source_target_pairs={{0,4},{2,6},{4,0},{6,2},{8,12},{10,14},{12,8},{14,10},{1,5},{3,7},... | collective-permute-start | bytes 294920 | tf_op jit(solution)/shard_map/ppermute | solution.py:304
  53.8 7.7 %collective-permute-start.21 = (bf16[64,768]{1,0:T(8,128)(2,1)S(1)}, bf16[64,768]{1,0:T(8,128)(2,1)S(1)}, u32[]{:S(2)}, u32[]{:S(2)}) collective-permute-start(bf16[64,768]{1,0:T(8,128)(2,1)S(1)} %get-tuple-element.99), channel_id=1, source_target_pairs={{0,6},{2,4},{4,2},{6,0},{8,14},{10,12},{12,10},{14,8},{1,7},{3,5},... | collective-permute-start | bytes 294920 | tf_op jit(solution)/shard_map/ppermute | solution.py:304
  55.6 13.1 %collective-permute-start.18 = (bf16[128,768]{1,0:T(8,128)(2,1)S(1)}, bf16[128,768]{1,0:T(8,128)(2,1)S(1)}, u32[]{:S(2)}, u32[]{:S(2)}) collective-permute-start(bf16[128,768]{1,0:T(8,128)(2,1)S(1)} %get-tuple-element.91), channel_id=1, source_target_pairs={{0,8},{2,10},{4,12},{6,14},{8,0},{10,2},{12,4},{14,6},{1,9},{3,11}... | collective-permute-start | bytes 589832 | tf_op jit(solution)/shard_map/ppermute | solution.py:308
  65.1 6.3 %collective-permute-start.22 = (bf16[64,768]{1,0:T(8,128)(2,1)S(1)}, bf16[64,768]{1,0:T(8,128)(2,1)S(1)}, u32[]{:S(2)}, u32[]{:S(2)}) collective-permute-start(bf16[64,768]{1,0:T(8,128)(2,1)S(1)} %get-tuple-element.101), channel_id=1, source_target_pairs={{0,2},{2,0},{4,6},{6,4},{8,10},{10,8},{12,14},{14,12},{1,3},{3,1},... | collective-permute-start | bytes 294920 | tf_op jit(solution)/shard_map/ppermute | solution.py:304
  65.7 7.7 %collective-permute-start.23 = (bf16[64,768]{1,0:T(8,128)(2,1)S(1)}, bf16[64,768]{1,0:T(8,128)(2,1)S(1)}, u32[]{:S(2)}, u32[]{:S(2)}) collective-permute-start(bf16[64,768]{1,0:T(8,128)(2,1)S(1)} %get-tuple-element.102), channel_id=1, source_target_pairs={{0,4},{2,6},{4,0},{6,2},{8,12},{10,14},{12,8},{14,10},{1,5},{3,7},... | collective-permute-start | bytes 294920 | tf_op jit(solution)/shard_map/ppermute | solution.py:304
  66.7 6.8 %collective-permute-start.24 = (bf16[64,768]{1,0:T(8,128)(2,1)S(1)}, bf16[64,768]{1,0:T(8,128)(2,1)S(1)}, u32[]{:S(2)}, u32[]{:S(2)}) collective-permute-start(bf16[64,768]{1,0:T(8,128)(2,1)S(1)} %get-tuple-element.103), channel_id=1, source_target_pairs={{0,6},{2,4},{4,2},{6,0},{8,14},{10,12},{12,10},{14,8},{1,7},{3,5},... | collective-permute-start | bytes 294920 | tf_op jit(solution)/shard_map/ppermute | solution.py:304
  69.9 4.6 %collective-permute-start.25 = (bf16[64,768]{1,0:T(8,128)(2,1)S(1)}, bf16[64,768]{1,0:T(8,128)(2,1)S(1)}, u32[]{:S(2)}, u32[]{:S(2)}) collective-permute-start(bf16[64,768]{1,0:T(8,128)(2,1)S(1)} %get-tuple-element.107), channel_id=1, source_target_pairs={{0,2},{2,0},{4,6},{6,4},{8,10},{10,8},{12,14},{14,12},{1,3},{3,1},... | collective-permute-start | bytes 294920 | tf_op jit(solution)/shard_map/ppermute | solution.py:304
  70.4 4.6 %collective-permute-start.26 = (bf16[64,768]{1,0:T(8,128)(2,1)S(1)}, bf16[64,768]{1,0:T(8,128)(2,1)S(1)}, u32[]{:S(2)}, u32[]{:S(2)}) collective-permute-start(bf16[64,768]{1,0:T(8,128)(2,1)S(1)} %get-tuple-element.108), channel_id=1, source_target_pairs={{0,4},{2,6},{4,0},{6,2},{8,12},{10,14},{12,8},{14,10},{1,5},{3,7},... | collective-permute-start | bytes 294920 | tf_op jit(solution)/shard_map/ppermute | solution.py:304
  71.4 5.7 %collective-permute-start.27 = (bf16[64,768]{1,0:T(8,128)(2,1)S(1)}, bf16[64,768]{1,0:T(8,128)(2,1)S(1)}, u32[]{:S(2)}, u32[]{:S(2)}) collective-permute-start(bf16[64,768]{1,0:T(8,128)(2,1)S(1)} %get-tuple-element.109), channel_id=1, source_target_pairs={{0,6},{2,4},{4,2},{6,0},{8,14},{10,12},{12,10},{14,8},{1,7},{3,5},... | collective-permute-start | bytes 294920 | tf_op jit(solution)/shard_map/ppermute | solution.py:304
  73.4 11.3 %collective-permute-start.32 = (bf16[11,256,256]{2,1,0:T(8,128)(2,1)S(1)}, bf16[11,256,256]{2,1,0:T(8,128)(2,1)S(1)}, u32[]{:S(2)}, u32[]{:S(2)}) collective-permute-start(bf16[11,256,256]{2,1,0:T(8,128)(2,1)S(1)} %get-tuple-element.120.refs_4_), channel_id=1, source_target_pairs={{0,1},{1,0},{2,3},{3,2},{4,5},{5,4},{6,7},{7,6},{8,9},{9,8},{10,11... | collective-permute-start | bytes 4325384 | tf_op jit(solution)/shard_map/ppermute | solution.py:311
  80.7 6.3 %collective-permute-start.33 = (bf16[11,256,256]{2,1,0:T(8,128)(2,1)S(1)}, bf16[11,256,256]{2,1,0:T(8,128)(2,1)S(1)}, u32[]{:S(2)}, u32[]{:S(2)}) collective-permute-start(bf16[11,256,256]{2,1,0:T(8,128)(2,1)S(1)} %get-tuple-element.121.refs_5_), channel_id=1, source_target_pairs={{0,1},{1,0},{2,3},{3,2},{4,5},{5,4},{6,7},{7,6},{8,9},{9,8},{10,11... | collective-permute-start | bytes 4325384 | tf_op jit(solution)/shard_map/ppermute | solution.py:311
  81.2 12.5 %collective-permute-start.29 = (bf16[64,768]{1,0:T(8,128)(2,1)S(1)}, bf16[64,768]{1,0:T(8,128)(2,1)S(1)}, u32[]{:S(2)}, u32[]{:S(2)}) collective-permute-start(bf16[64,768]{1,0:T(8,128)(2,1)S(1)} %get-tuple-element.117), channel_id=1, source_target_pairs={{0,2},{2,0},{4,6},{6,4},{8,10},{10,8},{12,14},{14,12},{1,3},{3,1},... | collective-permute-start | bytes 294920 | tf_op jit(solution)/shard_map/ppermute | solution.py:304
  82.2 11.6 %collective-permute-start.30 = (bf16[64,768]{1,0:T(8,128)(2,1)S(1)}, bf16[64,768]{1,0:T(8,128)(2,1)S(1)}, u32[]{:S(2)}, u32[]{:S(2)}) collective-permute-start(bf16[64,768]{1,0:T(8,128)(2,1)S(1)} %get-tuple-element.118), channel_id=1, source_target_pairs={{0,4},{2,6},{4,0},{6,2},{8,12},{10,14},{12,8},{14,10},{1,5},{3,7},... | collective-permute-start | bytes 294920 | tf_op jit(solution)/shard_map/ppermute | solution.py:304
  83.7 10.0 %collective-permute-start.31 = (bf16[64,768]{1,0:T(8,128)(2,1)S(1)}, bf16[64,768]{1,0:T(8,128)(2,1)S(1)}, u32[]{:S(2)}, u32[]{:S(2)}) collective-permute-start(bf16[64,768]{1,0:T(8,128)(2,1)S(1)} %get-tuple-element.119), channel_id=1, source_target_pairs={{0,6},{2,4},{4,2},{6,0},{8,14},{10,12},{12,10},{14,8},{1,7},{3,5},... | collective-permute-start | bytes 294920 | tf_op jit(solution)/shard_map/ppermute | solution.py:304
  84.8 12.7 %collective-permute-start.28 = (bf16[144,768]{1,0:T(8,128)(2,1)S(1)}, bf16[144,768]{1,0:T(8,128)(2,1)S(1)}, u32[]{:S(2)}, u32[]{:S(2)}) collective-permute-start(bf16[144,768]{1,0:T(8,128)(2,1)S(1)} %get-tuple-element.114), channel_id=1, source_target_pairs={{0,8},{2,10},{4,12},{6,14},{8,0},{10,2},{12,4},{14,6},{1,9},{3,11}... | collective-permute-start | bytes 663560 | tf_op jit(solution)/shard_map/ppermute | solution.py:308

commit v7 on v6

--- a/solution.py
+++ b/solution.py
@@ -13,6 +13,20 @@
 MIB = 1024 * 1024
 F32 = jnp.float32
 BF16 = jnp.bfloat16
+FLOPS = {
+    "pack_near": 30000000000,
+    "pack_far": 30000000000,
+    "forward_near": 100000000,
+    "forward_far": 3000000000,
+    "near_sum": 30000000000,
+    "far_grad": 10000000000,
+    "near_grad": 30000000000,
+    "backward_far": 3000000000,
+    "backward_near": 10000000000,
+    "far_back": 1000000000,
+    "weight_gradients": 30000000000,
+    "combine_gradients": 30000000000,
+}
 
 
 def dot(a, b, dims=PLAIN):
@@ -220,16 +234,45 @@
     d_gates_ref[...] = near_ref[...] + (far[0:2] + far[2:4])
 
 
-def weight_kernel(*refs):
-    refs, out_ref, finished_ref = refs[:-2], refs[-2], refs[-1]
-    xs = jnp.concatenate([get_columns(r) for r in refs[0:4]], axis=0)
-    rgs = jnp.concatenate([get_columns(r) for r in refs[4:8]], axis=0)
-    finished_ref[...] = jnp.zeros_like(finished_ref)
-    for m, rows in enumerate((xs, xs, rgs)):
-        acts = [
-            ref[0] if len(ref.shape) == 3 else ref[...] for ref in refs[8 + 4 * m : 12 + 4 * m]
-        ]
-        out_ref[m] = dot(jnp.concatenate(acts, axis=1), rows).astype(BF16)
+def weight_kernel(across, *refs):
+    (xf, xn, xfs, xns, gf, gn, gfs, gns, df, dn, hf, hn, out_hbm, finished, buf, sems) = refs
+    finished[...] = jnp.zeros_like(finished)
+    units = hf.shape[0]
+    side = hf.shape[1]
+    part = units // 2
+
+    def columns(*sets):
+        return jnp.concatenate(
+            [jnp.concatenate([r[i] for i in range(across)], axis=1) for r in sets], axis=0
+        )
+
+    def acts(own, sent, first):
+        blocks = range(across + first // side, across + (first + part) // side)
+        theirs = [jnp.concatenate([r[i] for i in blocks], axis=0) for r in sent]
+        return jnp.concatenate([r[first : first + part, :] for r in own] + theirs, axis=1)
+
+    x, rg = columns(xf, xn, xfs, xns), columns(gf, gn, gfs, gns)
+    copies = []
+    for m, (own, sent, rows, offset) in enumerate(
+        (
+            ((df, dn), (gfs, gns), x, 0),
+            ((df, dn), (gfs, gns), x, units),
+            ((hf, hn), (xfs, xns), rg, 0),
+        )
+    ):
+        for first in range(0, units, part):
+            slot = len(copies) % 2
+            if len(copies) > 1:
+                copies[-2].wait()
+            buf[slot] = dot(acts(own, sent, offset + first), rows).astype(BF16)
+            copies.append(
+                pltpu.make_async_copy(
+                    buf.at[slot], out_hbm.at[m, pl.ds(first, part)], sems.at[slot]
+                )
+            )
+            copies[-1].start()
+    copies[-2].wait()
+    copies[-1].wait()
 
 
 def local(tokens, teacher, routes, gate_weights, weights):
@@ -251,7 +294,6 @@
     acts2 = jax.ShapeDtypeStruct((2 * units, rows), BF16)
     vspec = pl.BlockSpec(memory_space=pltpu.VMEM)
     aspec = pl.BlockSpec(memory_space=pl.ANY)
-    matmul = 4 * rows * width * units
 
     def call(
         kernel,
@@ -261,9 +303,9 @@
         *args,
         after=(),
         through=(),
-        flops=10**8,
         limit=8,
         scratch=(),
+        in_hbm=0,
     ):
         many = isinstance(out_shape, list)
         specs = list(specs) + [vspec] * (len(args) - len(specs))
@@ -277,7 +319,7 @@
                 *refs[inputs + outputs + len(through) :],
             )
 
-        out_specs = [vspec] * outputs + [aspec] * len(through)
+        out_specs = [aspec] * in_hbm + [vspec] * (outputs - in_hbm) + [aspec] * len(through)
         out_shapes = (out_shape if many else [out_shape]) + [
             jax.ShapeDtypeStruct(a.shape, a.dtype) for a in through
         ]
@@ -292,7 +334,7 @@
             },
             scratch_shapes=scratch,
             cost_estimate=pl.CostEstimate(
-                flops=flops, bytes_accessed=2 * MIB, transcendentals=0
+                flops=FLOPS.get(name, 10**8), bytes_accessed=2 * MIB, transcendentals=0
             ),
             compiler_params=pltpu.CompilerParams(vmem_limit_bytes=limit * MIB),
             name=name,
@@ -324,7 +366,6 @@
             other,
             *x_pieces,
             after=after,
-            flops=3 * matmul,
             limit=20,
         )
         return res[:half], res[half:]
@@ -342,7 +383,6 @@
             *rg_pieces,
             after=after,
             through=through,
-            flops=3 * matmul,
             limit=20,
         )
         return res[:half], res[half:]
@@ -392,6 +432,7 @@
         after=[xf_sib, xn_sib],
     )
     part, d_gates_far, rg_far = to_mirror(res[0]), res[1], within_half(res[2:])
+    grad_far, (gf, df) = backward(rg_far, faf, fbf, "backward_far")
     res = call(
         functools.partial(near_grad_kernel, half),
         "near_grad",
@@ -401,56 +442,37 @@
         teacher,
         part,
         *got_near,
+        after=[df],
     )
     student, d_gates_near, rg_near = res[0], res[1], within_half(res[2:])
 
-    grad_far, (gf, df) = backward(rg_far, faf, fbf, "backward_far")
     back_far = within_half(grad_far)
-    grad_near, (gn, dn) = backward(rg_near, fan, fbn, "backward_near", after=back_far[1:])
+    part_rows = call(
+        far_back_kernel, "far_back", longer, [], far_meta, d_gates_far, *back_far
+    )
+    part = to_mirror(part_rows)
+    grad_near, (gn, dn) = backward(rg_near, fan, fbn, "backward_near", after=[part_rows])
     gf_sib, gn_sib = to_sibling(gf), to_sibling(gn)
-    part_rows, *grad_near = call(
-        far_back_kernel,
-        "far_back",
-        longer,
-        [],
-        far_meta,
-        d_gates_far,
-        *back_far,
-        through=grad_near,
-    )
-    part = to_mirror(part_rows)
     back_near = within_half(grad_near)
 
-    chunk, steps = rows, along
-    columns = pl.BlockSpec((across, rows, rows), lambda i: (0, 0, 0))
-    part_of = lambda first: pl.BlockSpec((1, rows, rows), lambda i: (across + first + i, 0, 0))
-    block = lambda first: pl.BlockSpec((chunk, rows), lambda i: (first + i, 0))
-    specs = [columns] * 8
-    for first in (0, steps, 0):
-        specs += [block(first)] * 2 + [part_of(first)] * 2
-    weight_grads, finished = pl.pallas_call(
-        weight_kernel,
-        grid=(steps,),
-        in_specs=specs,
-        out_specs=[
-            pl.BlockSpec((3, chunk, width), lambda i: (0, i, 0)),
-            pl.BlockSpec((8, 128), lambda i: (0, 0)),
-        ],
-        out_shape=[
+    weight_grads, finished = call(
+        functools.partial(weight_kernel, across),
+        "weight_gradients",
+        [
             jax.ShapeDtypeStruct((3, units, width), BF16),
             jax.ShapeDtypeStruct((8, 128), F32),
         ],
-        cost_estimate=pl.CostEstimate(
-            flops=3 * matmul * 2, bytes_accessed=16 * MIB, transcendentals=0
-        ),
-        compiler_params=pltpu.CompilerParams(vmem_limit_bytes=20 * MIB),
-        name="weight_gradients",
-    )(
+        [],
         *(xf, xn, xf_sib, xn_sib),
         *(gf, gn, gf_sib, gn_sib),
-        *(df, dn, gf_sib, gn_sib),
-        *(df, dn, gf_sib, gn_sib),
-        *(hf, hn, xf_sib, xn_sib),
+        *(df, dn, hf, hn),
+        after=[],
+        limit=24,
+        scratch=[
+            pltpu.VMEM((2, units // 2, width), BF16),
+            pltpu.SemaphoreType.DMA((2,)),
+        ],
+        in_hbm=1,
     )
 
     d_tokens, d_gates = call(

time: 98.7 us -> 91.6 us (0.928)
  waiting for transfers between devices: 26.7 us -> 17.9 us
  Pallas kernels: 25.2 us -> 26.8 us
    pallas_call x11 -> x12, Pallas kernels: 18.6 us -> 26.8 us  [call(): pl.pallas_call(body, in_specs=specs + [aspec] * (len(after) + len(through...]
    pallas_call x1 -> x0, Pallas kernels: 6.65 us -> none  [local(): pl.pallas_call(weight_kernel, grid=(steps,), in_specs=specs, out_specs=[p...]
    ppermute x24, waiting for transfers between devices: 21.4 us -> 16.7 us  [within_half(): lax.ppermute(rows_of[s], 'expert', [(i, i ^ s) for i in range(experts)])]
    ppermute x5, waiting for transfers between devices: 5.3 us -> 1.19 us  [to_mirror(): return lax.ppermute(x, 'expert', [(i, i ^ half) for i in range(experts)])]
    unnamed x12 -> x14, local copies, waits for them, and re-layouts: 4.63 us -> 4.63 us
  transfers between devices with their start and end apart: 34 -> 34, of which waited for: 14 -> 9; matrix products, arithmetic and copies ran while one was open for 0% -> 0% of each run, Pallas kernels for 24% -> 27%
where the time goes in v7:
time: 91.6 us; the launch traced here: 91.3 us
  starting transfers between devices  41.1 us (45%)
  Pallas kernels  26.8 us (29%)
  waiting for transfers between devices  17.9 us (20%)
  local copies, waits for them, and re-layouts  4.63 us (5%)
    ppermute x24, starting transfers between devices, within_half(): lax.ppermute(rows_of[s], 'expert', [(i, i ^ s) for i in range(experts)])  30.6 us
    pallas_call x12, Pallas kernels, call(): pl.pallas_call(body, in_specs=specs + [aspec] * (len(after) + len(through...  26.8 us
    ppermute x24, waiting for transfers between devices, within_half(): lax.ppermute(rows_of[s], 'expert', [(i, i ^ s) for i in range(experts)])  16.7 us
    ppermute x5, starting transfers between devices, to_mirror(): return lax.ppermute(x, 'expert', [(i, i ^ half) for i in range(experts)])  9.89 us
    unnamed x14, local copies, waits for them, and re-layouts  4.63 us
  transfers between devices with their start and end apart: 34, of which 9 were waited for; matrix products, arithmetic and copies ran while one was open for 0% of the time, Pallas kernels for 27%

profile of v7, /device:TPU:0, one launch (start us, length us, event | category | flops | bytes accessed | tf_op | source)
XLA Modules:
  0.0 91.3 jit_solution(11080043995127079832)
XLA Ops:
  0.6 4.1 %collective-permute-start.8 = (bf16[128,768]{1,0:T(8,128)(2,1)}, bf16[128,768]{1,0:T(8,128)(2,1)S(1)}, u32[]{:S(2)}, u32[]{:S(2)}) collective-permute-start(bf16[128,768]{1,0:T(8,128)(2,1)} %refs_3_.1), channel_id=1, source_target_pairs={{0,8},{2,10},{4,12},{6,14},{8,0},{10,2},{12,4},{14,6},{1,9},{3,11}... | collective-permute-start | bytes 589832 | tf_op jit(solution)/shard_map/ppermute | solution.py:350
  4.7 2.3 %copy-done = bf16[1,1024,3,768]{3,1,2,0:T(8,128)(2,1)S(1)} copy-done((bf16[1,1024,3,768]{3,1,2,0:T(8,128)(2,1)S(1)}, bf16[1,1024,3,768]{3,1,2,0:T(8,128)(2,1)}, u32[]{:S(2)}) %copy-start) | copy-done | bytes 4718616
  7.1 0.9 %copy-done.1 = bf16[128,768]{1,0:T(8,128)(2,1)S(1)} copy-done((bf16[128,768]{1,0:T(8,128)(2,1)S(1)}, bf16[128,768]{1,0:T(8,128)(2,1)}, u32[]{:S(2)}) %copy-start.1) | copy-done | bytes 196632
  8.0 0.7 copy-done.3
  8.7 0.7 copy-done.4
  9.4 0.4 pack_near.1
  9.9 1.8 %collective-permute-start.2 = (bf16[64,768]{1,0:T(8,128)(2,1)S(1)}, bf16[64,768]{1,0:T(8,128)(2,1)S(1)}, u32[]{:S(2)}, u32[]{:S(2)}) collective-permute-start(bf16[64,768]{1,0:T(8,128)(2,1)S(1)} %get-tuple-element.64), channel_id=1, source_target_pairs={{0,2},{2,0},{4,6},{6,4},{8,10},{10,8},{12,14},{14,12},{1,3},{3,1},... | collective-permute-start | bytes 294920 | tf_op jit(solution)/shard_map/ppermute | solution.py:346
  11.7 1.6 %collective-permute-start.3 = (bf16[64,768]{1,0:T(8,128)(2,1)S(1)}, bf16[64,768]{1,0:T(8,128)(2,1)S(1)}, u32[]{:S(2)}, u32[]{:S(2)}) collective-permute-start(bf16[64,768]{1,0:T(8,128)(2,1)S(1)} %get-tuple-element.65), channel_id=1, source_target_pairs={{0,4},{2,6},{4,0},{6,2},{8,12},{10,14},{12,8},{14,10},{1,5},{3,7},... | collective-permute-start | bytes 294920 | tf_op jit(solution)/shard_map/ppermute | solution.py:346
  13.2 1.2 %collective-permute-done.refs_0_ = f32[8,128]{1,0:T(8,128)S(1)} collective-permute-done((f32[8,128]{1,0:T(8,128)S(1)}, f32[8,128]{1,0:T(8,128)S(1)}, u32[]{:S(2)}, u32[]{:S(2)}) %collective-permute-start) | collective-permute-done | bytes 4128 | tf_op jit(solution)/shard_map/ppermute | solution.py:350
  14.4 2.5 %collective-permute-start.4 = (bf16[64,768]{1,0:T(8,128)(2,1)S(1)}, bf16[64,768]{1,0:T(8,128)(2,1)S(1)}, u32[]{:S(2)}, u32[]{:S(2)}) collective-permute-start(bf16[64,768]{1,0:T(8,128)(2,1)S(1)} %get-tuple-element.66), channel_id=1, source_target_pairs={{0,6},{2,4},{4,2},{6,0},{8,14},{10,12},{12,10},{14,8},{1,7},{3,5},... | collective-permute-start | bytes 294920 | tf_op jit(solution)/shard_map/ppermute | solution.py:346
  17.3 0.5 collective-permute-start.9
  17.8 0.6 collective-permute-start.10
  18.4 2.5 %collective-permute-start.11 = (bf16[64,768]{1,0:T(8,128)(2,1)S(1)}, bf16[64,768]{1,0:T(8,128)(2,1)S(1)}, u32[]{:S(2)}, u32[]{:S(2)}) collective-permute-start(bf16[64,768]{1,0:T(8,128)(2,1)S(1)} %get-tuple-element.74), channel_id=1, source_target_pairs={{0,6},{2,4},{4,2},{6,0},{8,14},{10,12},{12,10},{14,8},{1,7},{3,5},... | collective-permute-start | bytes 294920 | tf_op jit(solution)/shard_map/ppermute | solution.py:346
  20.9 3.3 %forward_near.1 = (bf16[64,768]{1,0:T(8,128)(2,1)S(1)}, bf16[64,768]{1,0:T(8,128)(2,1)S(1)}, bf16[64,768]{1,0:T(8,128)(2,1)S(1)}, bf16[64,768]{1,0:T(8,128)(2,1)...) custom-call(bf16[3,1024,768]{2,1,0:T(8,128)(2,1)S(1)} %bitcast.13, ...), custom_call_target="tpu_custom_call" | custom-call | flops 100000000 | bytes 2097152 | tf_op jit(solution)/shard_map/forward_near/pallas_call | solution.py:327
  24.2 1.3 %collective-permute-start.5 = (bf16[64,768]{1,0:T(8,128)(2,1)S(1)}, bf16[64,768]{1,0:T(8,128)(2,1)S(1)}, u32[]{:S(2)}, u32[]{:S(2)}) collective-permute-start(bf16[64,768]{1,0:T(8,128)(2,1)S(1)} %get-tuple-element.68), channel_id=1, source_target_pairs={{0,2},{2,0},{4,6},{6,4},{8,10},{10,8},{12,14},{14,12},{1,3},{3,1},... | collective-permute-start | bytes 294920 | tf_op jit(solution)/shard_map/ppermute | solution.py:346
  25.5 1.7 %collective-permute-start.6 = (bf16[64,768]{1,0:T(8,128)(2,1)S(1)}, bf16[64,768]{1,0:T(8,128)(2,1)S(1)}, u32[]{:S(2)}, u32[]{:S(2)}) collective-permute-start(bf16[64,768]{1,0:T(8,128)(2,1)S(1)} %get-tuple-element.69), channel_id=1, source_target_pairs={{0,4},{2,6},{4,0},{6,2},{8,12},{10,14},{12,8},{14,10},{1,5},{3,7},... | collective-permute-start | bytes 294920 | tf_op jit(solution)/shard_map/ppermute | solution.py:346
  27.3 0.5 collective-permute-start.7
  27.8 3.3 %forward_far.1 = (bf16[64,768]{1,0:T(8,128)(2,1)S(1)}, bf16[64,768]{1,0:T(8,128)(2,1)S(1)}, bf16[64,768]{1,0:T(8,128)(2,1)S(1)}, bf16[64,768]{1,0:T(8,128)(2,1)S...) custom-call(bf16[3,1024,768]{2,1,0:T(8,128)(2,1)S(1)} %bitcast.14, ...), custom_call_target="tpu_custom_call" | custom-call | flops 3000000000 | bytes 2097152 | tf_op jit(solution)/shard_map/forward_far/pallas_call | solution.py:327
  31.1 0.6 collective-permute-start.16
  31.7 1.1 %collective-permute-done.7.refs_5_.refs_6_ = bf16[64,768]{1,0:T(8,128)(2,1)S(1)} collective-permute-done((bf16[64,768]{1,0:T(8,128)(2,1)S(1)}, bf16[64,768]{1,0:T(8,128)(2,1)S(1)}, u32[]{:S(2)}, u32[]{:S(2)}) %collective-permute-start.7) | collective-permute-done | bytes 98336 | tf_op jit(solution)/shard_map/ppermute | solution.py:346
  32.8 0.5 near_sum.1
  33.5 2.6 %collective-permute-start.12 = (bf16[128,768]{1,0:T(8,128)(2,1)S(1)}, bf16[128,768]{1,0:T(8,128)(2,1)S(1)}, u32[]{:S(2)}, u32[]{:S(2)}) collective-permute-start(bf16[128,768]{1,0:T(8,128)(2,1)S(1)} %get-tuple-element.80), channel_id=1, source_target_pairs={{0,8},{2,10},{4,12},{6,14},{8,0},{10,2},{12,4},{14,6},{1,9},{3,11}... | collective-permute-start | bytes 589832 | tf_op jit(solution)/shard_map/ppermute | solution.py:350
  36.1 1.8 %collective-permute-start.14 = (bf16[64,768]{1,0:T(8,128)(2,1)S(1)}, bf16[64,768]{1,0:T(8,128)(2,1)S(1)}, u32[]{:S(2)}, u32[]{:S(2)}) collective-permute-start(bf16[64,768]{1,0:T(8,128)(2,1)S(1)} %get-tuple-element.83), channel_id=1, source_target_pairs={{0,4},{2,6},{4,0},{6,2},{8,12},{10,14},{12,8},{14,10},{1,5},{3,7},... | collective-permute-start | bytes 294920 | tf_op jit(solution)/shard_map/ppermute | solution.py:346
  38.0 1.6 %collective-permute-start.15 = (bf16[64,768]{1,0:T(8,128)(2,1)S(1)}, bf16[64,768]{1,0:T(8,128)(2,1)S(1)}, u32[]{:S(2)}, u32[]{:S(2)}) collective-permute-start(bf16[64,768]{1,0:T(8,128)(2,1)S(1)} %get-tuple-element.84), channel_id=1, source_target_pairs={{0,6},{2,4},{4,2},{6,0},{8,14},{10,12},{12,10},{14,8},{1,7},{3,5},... | collective-permute-start | bytes 294920 | tf_op jit(solution)/shard_map/ppermute | solution.py:346
  39.5 3.7 %collective-permute-done.14.refs_4_ = bf16[64,768]{1,0:T(8,128)(2,1)S(1)} collective-permute-done((bf16[64,768]{1,0:T(8,128)(2,1)S(1)}, bf16[64,768]{1,0:T(8,128)(2,1)S(1)}, u32[]{:S(2)}, u32[]{:S(2)}) %collective-permute-start.14) | collective-permute-done | bytes 98336 | tf_op jit(solution)/shard_map/ppermute | solution.py:346
  43.2 3.9 %collective-permute-done.15.refs_5_ = bf16[64,768]{1,0:T(8,128)(2,1)S(1)} collective-permute-done((bf16[64,768]{1,0:T(8,128)(2,1)S(1)}, bf16[64,768]{1,0:T(8,128)(2,1)S(1)}, u32[]{:S(2)}, u32[]{:S(2)}) %collective-permute-start.15) | collective-permute-done | bytes 98336 | tf_op jit(solution)/shard_map/ppermute | solution.py:346
  47.1 0.8 far_grad.1
  47.9 1.1 %collective-permute-start.20 = (bf16[64,768]{1,0:T(8,128)(2,1)S(1)}, bf16[64,768]{1,0:T(8,128)(2,1)S(1)}, u32[]{:S(2)}, u32[]{:S(2)}) collective-permute-start(bf16[64,768]{1,0:T(8,128)(2,1)S(1)} %get-tuple-element.91), channel_id=1, source_target_pairs={{0,4},{2,6},{4,0},{6,2},{8,12},{10,14},{12,8},{14,10},{1,5},{3,7},... | collective-permute-start | bytes 294920 | tf_op jit(solution)/shard_map/ppermute | solution.py:346
  49.1 2.4 %collective-permute-start.21 = (bf16[64,768]{1,0:T(8,128)(2,1)S(1)}, bf16[64,768]{1,0:T(8,128)(2,1)S(1)}, u32[]{:S(2)}, u32[]{:S(2)}) collective-permute-start(bf16[64,768]{1,0:T(8,128)(2,1)S(1)} %get-tuple-element.92), channel_id=1, source_target_pairs={{0,6},{2,4},{4,2},{6,0},{8,14},{10,12},{12,10},{14,8},{1,7},{3,5},... | collective-permute-start | bytes 294920 | tf_op jit(solution)/shard_map/ppermute | solution.py:346
  51.4 0.8 collective-permute-start.18
  52.2 1.1 %collective-permute-done.19.refs_5_ = bf16[64,768]{1,0:T(8,128)(2,1)S(1)} collective-permute-done((bf16[64,768]{1,0:T(8,128)(2,1)S(1)}, bf16[64,768]{1,0:T(8,128)(2,1)S(1)}, u32[]{:S(2)}, u32[]{:S(2)}) %collective-permute-start.19) | collective-permute-done | bytes 98336 | tf_op jit(solution)/shard_map/ppermute | solution.py:346
  53.4 3.6 %collective-permute-done.21.refs_7_ = bf16[64,768]{1,0:T(8,128)(2,1)S(1)} collective-permute-done((bf16[64,768]{1,0:T(8,128)(2,1)S(1)}, bf16[64,768]{1,0:T(8,128)(2,1)S(1)}, u32[]{:S(2)}, u32[]{:S(2)}) %collective-permute-start.21) | collective-permute-done | bytes 98336 | tf_op jit(solution)/shard_map/ppermute | solution.py:346
  56.9 3.7 %backward_far.1 = (bf16[64,768]{1,0:T(8,128)(2,1)S(1)}, bf16[64,768]{1,0:T(8,128)(2,1)S(1)}, bf16[64,768]{1,0:T(8,128)(2,1)S(1)}, bf16[64,768]{1,0:T(8,128)(2,1)...) custom-call(bf16[3,1024,768]{2,1,0:T(8,128)(2,1)S(1)} %bitcast.15, ...), custom_call_target="tpu_custom_call" | custom-call | flops 3000000000 | bytes 2097152 | tf_op jit(solution)/shard_map/backward_far/pallas_call | solution.py:327
  60.6 0.4 collective-permute-start.22
  61.0 1.4 %collective-permute-start.23 = (bf16[64,768]{1,0:T(8,128)(2,1)S(1)}, bf16[64,768]{1,0:T(8,128)(2,1)S(1)}, u32[]{:S(2)}, u32[]{:S(2)}) collective-permute-start(bf16[64,768]{1,0:T(8,128)(2,1)S(1)} %get-tuple-element.98), channel_id=1, source_target_pairs={{0,4},{2,6},{4,0},{6,2},{8,12},{10,14},{12,8},{14,10},{1,5},{3,7},... | collective-permute-start | bytes 294920 | tf_op jit(solution)/shard_map/ppermute | solution.py:346
  62.4 1.8 %collective-permute-start.24 = (bf16[64,768]{1,0:T(8,128)(2,1)S(1)}, bf16[64,768]{1,0:T(8,128)(2,1)S(1)}, u32[]{:S(2)}, u32[]{:S(2)}) collective-permute-start(bf16[64,768]{1,0:T(8,128)(2,1)S(1)} %get-tuple-element.99), channel_id=1, source_target_pairs={{0,6},{2,4},{4,2},{6,0},{8,14},{10,12},{12,10},{14,8},{1,7},{3,5},... | collective-permute-start | bytes 294920 | tf_op jit(solution)/shard_map/ppermute | solution.py:346
  64.2 1.2 %near_grad.1 = (bf16[128,768]{1,0:T(8,128)(2,1)}, f32[2,128]{1,0:T(2,128)S(1)}, bf16[64,768]{1,0:T(8,128)(2,1)S(1)}, bf16[64,768]{1,0:T(8,128)(2,1)S(1)}, bf16[6...) custom-call(f32[8,128]{1,0:T(8,128)S(1)} %get-tuple-element.62.refs_0_, bf16[128,768]{1,0:T(8,128)(2,1)S(1)} %copy-done.2, ...), custom_call_target="tpu_custom_call" | custom-call | flops 30000001024 | bytes 2097152 | tf_op jit(solution)/shard_map/near_grad/pallas_call | solution.py:327
  65.7 1.4 %collective-permute-start.27 = (bf16[64,768]{1,0:T(8,128)(2,1)S(1)}, bf16[64,768]{1,0:T(8,128)(2,1)S(1)}, u32[]{:S(2)}, u32[]{:S(2)}) collective-permute-start(bf16[64,768]{1,0:T(8,128)(2,1)S(1)} %get-tuple-element.105), channel_id=1, source_target_pairs={{0,4},{2,6},{4,0},{6,2},{8,12},{10,14},{12,8},{14,10},{1,5},{3,7},... | collective-permute-start | bytes 294920 | tf_op jit(solution)/shard_map/ppermute | solution.py:346
  67.1 1.8 %collective-permute-start.28 = (bf16[64,768]{1,0:T(8,128)(2,1)S(1)}, bf16[64,768]{1,0:T(8,128)(2,1)S(1)}, u32[]{:S(2)}, u32[]{:S(2)}) collective-permute-start(bf16[64,768]{1,0:T(8,128)(2,1)S(1)} %get-tuple-element.106), channel_id=1, source_target_pairs={{0,6},{2,4},{4,2},{6,0},{8,14},{10,12},{12,10},{14,8},{1,7},{3,5},... | collective-permute-start | bytes 294920 | tf_op jit(solution)/shard_map/ppermute | solution.py:346
  68.9 0.4 far_back.1.refs_8_
  69.3 0.7 collective-permute-done.26.refs_5_
  70.4 2.3 %collective-permute-done.28.refs_7_ = bf16[64,768]{1,0:T(8,128)(2,1)S(1)} collective-permute-done((bf16[64,768]{1,0:T(8,128)(2,1)S(1)}, bf16[64,768]{1,0:T(8,128)(2,1)S(1)}, u32[]{:S(2)}, u32[]{:S(2)}) %collective-permute-start.28) | collective-permute-done | bytes 98336 | tf_op jit(solution)/shard_map/ppermute | solution.py:346
  72.6 3.7 %backward_near.1 = (bf16[64,768]{1,0:T(8,128)(2,1)S(1)}, bf16[64,768]{1,0:T(8,128)(2,1)S(1)}, bf16[64,768]{1,0:T(8,128)(2,1)S(1)}, bf16[64,768]{1,0:T(8,128)(2,1...) custom-call(bf16[3,1024,768]{2,1,0:T(8,128)(2,1)S(1)} %bitcast.16, ...), custom_call_target="tpu_custom_call" | custom-call | flops 10000000000 | bytes 2097152 | tf_op jit(solution)/shard_map/backward_near/pallas_call | solution.py:327
  76.4 2.2 %collective-permute-start.25 = (bf16[144,768]{1,0:T(8,128)(2,1)S(1)}, bf16[144,768]{1,0:T(8,128)(2,1)S(1)}, u32[]{:S(2)}, u32[]{:S(2)}) collective-permute-start(bf16[144,768]{1,0:T(8,128)(2,1)S(1)} %far_back.1.refs_8_), channel_id=1, source_target_pairs={{0,8},{2,10},{4,12},{6,14},{8,0},{10,2},{12,4},{14,6},{1,9},{3,11}... | collective-permute-start | bytes 663560 | tf_op jit(solution)/shard_map/ppermute | solution.py:350
  79.0 1.5 %collective-permute-start.30 = (bf16[64,768]{1,0:T(8,128)(2,1)S(1)}, bf16[64,768]{1,0:T(8,128)(2,1)S(1)}, u32[]{:S(2)}, u32[]{:S(2)}) collective-permute-start(bf16[64,768]{1,0:T(8,128)(2,1)S(1)} %get-tuple-element.109), channel_id=1, source_target_pairs={{0,4},{2,6},{4,0},{6,2},{8,12},{10,14},{12,8},{14,10},{1,5},{3,7},... | collective-permute-start | bytes 294920 | tf_op jit(solution)/shard_map/ppermute | solution.py:346
  80.5 1.6 %collective-permute-start.31 = (bf16[64,768]{1,0:T(8,128)(2,1)S(1)}, bf16[64,768]{1,0:T(8,128)(2,1)S(1)}, u32[]{:S(2)}, u32[]{:S(2)}) collective-permute-start(bf16[64,768]{1,0:T(8,128)(2,1)S(1)} %get-tuple-element.110), channel_id=1, source_target_pairs={{0,6},{2,4},{4,2},{6,0},{8,14},{10,12},{12,10},{14,8},{1,7},{3,5},... | collective-permute-start | bytes 294920 | tf_op jit(solution)/shard_map/ppermute | solution.py:346
  82.1 8.1 %weight_gradients.1 = (bf16[3,1024,768]{2,1,0:T(8,128)(2,1)}, f32[8,128]{1,0:T(8,128)S(1)}) custom-call(bf16[7,256,256]{2,1,0:T(8,128)(2,1)S(1)} %get-tuple-element.85.refs_0_, bf16[7,256,256]{2,1,0:T(8,128)(2,1)S(1)} %get-tuple-element.75.refs_6_.refs_1_, bf16[7,256,256]{2,1,0:T(8,128)(2,1)S(1)} %collective-permute-done.16.refs_6_.refs_2_, ...), custom_call_target="tpu_custom_call" | custom-call | flops 30000001024 | bytes 2097152 | tf_op jit(solution)/shard_map/weight_gradients/pallas_call | solution.py:327
  90.3 1.1 %combine_gradients.1 = (bf16[128,768]{1,0:T(8,128)(2,1)}, f32[2,128]{1,0:T(2,128)}) custom-call(f32[8,128]{1,0:T(8,128)S(1)} %get-tuple-element.62.refs_0_, bf16[144,768]{1,0:T(8,128)(2,1)S(1)} %collective-permute-done.25.refs_1_, f32[2,128]{1,0:T(2,128)S(1)} %get-tuple-element.100.refs_2_, bf16[64,768]{1,0:T(8,128)(2,1)S(1)} %get-tuple-element.107.refs_3_, ...), custom_call_target="tpu_custom_call" | custom-call | flops 30000001024 | bytes 2097152 | tf_op jit(solution)/shard_map/combine_gradients/pallas_call | solution.py:327
  (47 shorter events, 2.1 us)
Async XLA Ops:
  0.6 16.3 %collective-permute-start.8 = (bf16[128,768]{1,0:T(8,128)(2,1)}, bf16[128,768]{1,0:T(8,128)(2,1)S(1)}, u32[]{:S(2)}, u32[]{:S(2)}) collective-permute-start(bf16[128,768]{1,0:T(8,128)(2,1)} %refs_3_.1), channel_id=1, source_target_pairs={{0,8},{2,10},{4,12},{6,14},{8,0},{10,2},{12,4},{14,6},{1,9},{3,11}... | collective-permute-start | bytes 589832 | tf_op jit(solution)/shard_map/ppermute | solution.py:350
  4.7 16.1 %collective-permute-start.1 = (bf16[3,1024,768]{2,1,0:T(8,128)(2,1)}, bf16[3,1024,768]{2,1,0:T(8,128)(2,1)S(1)}, u32[]{:S(2)}, u32[]{:S(2)}) collective-permute-start(bf16[3,1024,768]{2,1,0:T(8,128)(2,1)} %bitcast.9), channel_id=1, source_target_pairs={{0,1},{1,0},{2,3},{3,2},{4,5},{5,4},{6,7},{7,6},{8,9},{9,8},{10,11... | collective-permute-start | bytes 14155784 | tf_op jit(solution)/shard_map/ppermute | solution.py:353
  4.7 2.3 %copy-start = (bf16[1,1024,3,768]{3,1,2,0:T(8,128)(2,1)S(1)}, bf16[1,1024,3,768]{3,1,2,0:T(8,128)(2,1)}, u32[]{:S(2)}) copy-start(bf16[1,1024,3,768]{3,1,2,0:T(8,128)(2,1)} %param.9) | copy-start | bytes 14155780
  7.1 0.9 %copy-start.1 = (bf16[128,768]{1,0:T(8,128)(2,1)S(1)}, bf16[128,768]{1,0:T(8,128)(2,1)}, u32[]{:S(2)}) copy-start(bf16[128,768]{1,0:T(8,128)(2,1)} %refs_3_.1) | copy-start | bytes 589828
  8.0 0.7 copy-start.3
  8.7 0.7 copy-start.4
  9.7 4.7 %collective-permute-start = (f32[8,128]{1,0:T(8,128)S(1)}, f32[8,128]{1,0:T(8,128)S(1)}, u32[]{:S(2)}, u32[]{:S(2)}) collective-permute-start(f32[8,128]{1,0:T(8,128)S(1)} %get-tuple-element.62.refs_0_), channel_id=1, source_target_pairs={{0,8},{2,10},{4,12},{6,14},{8,0},{10,2},{12,4},{14,6},{1,9},{3,11}... | collective-permute-start | bytes 12296 | tf_op jit(solution)/shard_map/ppermute | solution.py:350
  9.9 7.9 %collective-permute-start.2 = (bf16[64,768]{1,0:T(8,128)(2,1)S(1)}, bf16[64,768]{1,0:T(8,128)(2,1)S(1)}, u32[]{:S(2)}, u32[]{:S(2)}) collective-permute-start(bf16[64,768]{1,0:T(8,128)(2,1)S(1)} %get-tuple-element.64), channel_id=1, source_target_pairs={{0,2},{2,0},{4,6},{6,4},{8,10},{10,8},{12,14},{14,12},{1,3},{3,1},... | collective-permute-start | bytes 294920 | tf_op jit(solution)/shard_map/ppermute | solution.py:346
  11.7 6.7 %collective-permute-start.3 = (bf16[64,768]{1,0:T(8,128)(2,1)S(1)}, bf16[64,768]{1,0:T(8,128)(2,1)S(1)}, u32[]{:S(2)}, u32[]{:S(2)}) collective-permute-start(bf16[64,768]{1,0:T(8,128)(2,1)S(1)} %get-tuple-element.65), channel_id=1, source_target_pairs={{0,4},{2,6},{4,0},{6,2},{8,12},{10,14},{12,8},{14,10},{1,5},{3,7},... | collective-permute-start | bytes 294920 | tf_op jit(solution)/shard_map/ppermute | solution.py:346
  14.4 6.4 %slice-start = ((s8[4718592]{0:T(1024)(128)(4,1)}), s8[4194304]{0:T(1024)(128)(4,1)S(1)}, s32[]{:S(2)}) async-start(s8[4718592]{0:T(1024)(128)(4,1)} %bitcast.11), calls=%async_computation | async-start | bytes 8388608
  14.4 6.4 %slice-start.1 = ((s8[4718592]{0:T(1024)(128)(4,1)}), s8[524288]{0:T(1024)(128)(4,1)S(1)}, s32[]{:S(2)}) async-start(s8[4718592]{0:T(1024)(128)(4,1)} %bitcast.11), calls=%async_computation.1 | async-start | bytes 1048576
  14.4 6.4 %collective-permute-start.4 = (bf16[64,768]{1,0:T(8,128)(2,1)S(1)}, bf16[64,768]{1,0:T(8,128)(2,1)S(1)}, u32[]{:S(2)}, u32[]{:S(2)}) collective-permute-start(bf16[64,768]{1,0:T(8,128)(2,1)S(1)} %get-tuple-element.66), channel_id=1, source_target_pairs={{0,6},{2,4},{4,2},{6,0},{8,14},{10,12},{12,10},{14,8},{1,7},{3,5},... | collective-permute-start | bytes 294920 | tf_op jit(solution)/shard_map/ppermute | solution.py:346
  17.3 10.0 %collective-permute-start.9 = (bf16[64,768]{1,0:T(8,128)(2,1)S(1)}, bf16[64,768]{1,0:T(8,128)(2,1)S(1)}, u32[]{:S(2)}, u32[]{:S(2)}) collective-permute-start(bf16[64,768]{1,0:T(8,128)(2,1)S(1)} %get-tuple-element.72), channel_id=1, source_target_pairs={{0,2},{2,0},{4,6},{6,4},{8,10},{10,8},{12,14},{14,12},{1,3},{3,1},... | collective-permute-start | bytes 294920 | tf_op jit(solution)/shard_map/ppermute | solution.py:346
  17.8 9.9 %collective-permute-start.10 = (bf16[64,768]{1,0:T(8,128)(2,1)S(1)}, bf16[64,768]{1,0:T(8,128)(2,1)S(1)}, u32[]{:S(2)}, u32[]{:S(2)}) collective-permute-start(bf16[64,768]{1,0:T(8,128)(2,1)S(1)} %get-tuple-element.73), channel_id=1, source_target_pairs={{0,4},{2,6},{4,0},{6,2},{8,12},{10,14},{12,8},{14,10},{1,5},{3,7},... | collective-permute-start | bytes 294920 | tf_op jit(solution)/shard_map/ppermute | solution.py:346
  18.4 9.4 %collective-permute-start.11 = (bf16[64,768]{1,0:T(8,128)(2,1)S(1)}, bf16[64,768]{1,0:T(8,128)(2,1)S(1)}, u32[]{:S(2)}, u32[]{:S(2)}) collective-permute-start(bf16[64,768]{1,0:T(8,128)(2,1)S(1)} %get-tuple-element.74), channel_id=1, source_target_pairs={{0,6},{2,4},{4,2},{6,0},{8,14},{10,12},{12,10},{14,8},{1,7},{3,5},... | collective-permute-start | bytes 294920 | tf_op jit(solution)/shard_map/ppermute | solution.py:346
  24.2 7.5 %collective-permute-start.5 = (bf16[64,768]{1,0:T(8,128)(2,1)S(1)}, bf16[64,768]{1,0:T(8,128)(2,1)S(1)}, u32[]{:S(2)}, u32[]{:S(2)}) collective-permute-start(bf16[64,768]{1,0:T(8,128)(2,1)S(1)} %get-tuple-element.68), channel_id=1, source_target_pairs={{0,2},{2,0},{4,6},{6,4},{8,10},{10,8},{12,14},{14,12},{1,3},{3,1},... | collective-permute-start | bytes 294920 | tf_op jit(solution)/shard_map/ppermute | solution.py:346
  25.5 6.1 %collective-permute-start.6 = (bf16[64,768]{1,0:T(8,128)(2,1)S(1)}, bf16[64,768]{1,0:T(8,128)(2,1)S(1)}, u32[]{:S(2)}, u32[]{:S(2)}) collective-permute-start(bf16[64,768]{1,0:T(8,128)(2,1)S(1)} %get-tuple-element.69), channel_id=1, source_target_pairs={{0,4},{2,6},{4,0},{6,2},{8,12},{10,14},{12,8},{14,10},{1,5},{3,7},... | collective-permute-start | bytes 294920 | tf_op jit(solution)/shard_map/ppermute | solution.py:346
  27.3 5.5 %collective-permute-start.7 = (bf16[64,768]{1,0:T(8,128)(2,1)S(1)}, bf16[64,768]{1,0:T(8,128)(2,1)S(1)}, u32[]{:S(2)}, u32[]{:S(2)}) collective-permute-start(bf16[64,768]{1,0:T(8,128)(2,1)S(1)} %get-tuple-element.70), channel_id=1, source_target_pairs={{0,6},{2,4},{4,2},{6,0},{8,14},{10,12},{12,10},{14,8},{1,7},{3,5},... | collective-permute-start | bytes 294920 | tf_op jit(solution)/shard_map/ppermute | solution.py:346
  27.8 19.3 %collective-permute-start.17 = (bf16[7,256,256]{2,1,0:T(8,128)(2,1)S(1)}, bf16[7,256,256]{2,1,0:T(8,128)(2,1)S(1)}, u32[]{:S(2)}, u32[]{:S(2)}) collective-permute-start(bf16[7,256,256]{2,1,0:T(8,128)(2,1)S(1)} %get-tuple-element.75.refs_6_.refs_1_), channel_id=1, source_target_pairs={{0,1},{1,0},{2,3},{3,2},{4,5},{5,4},{6,7},{7,6},{8,9},{9,8},{10,11... | collective-permute-start | bytes 2752520 | tf_op jit(solution)/shard_map/ppermute | solution.py:353
  27.8 5.0 %copy-start.2 = (bf16[128,768]{1,0:T(8,128)(2,1)S(1)}, bf16[128,768]{1,0:T(8,128)(2,1)}, u32[]{:S(2)}) copy-start(bf16[128,768]{1,0:T(8,128)(2,1)} %refs_1_.3) | copy-start | bytes 589828
  31.1 16.0 %collective-permute-start.16 = (bf16[7,256,256]{2,1,0:T(8,128)(2,1)S(1)}, bf16[7,256,256]{2,1,0:T(8,128)(2,1)S(1)}, u32[]{:S(2)}, u32[]{:S(2)}) collective-permute-start(bf16[7,256,256]{2,1,0:T(8,128)(2,1)S(1)} %get-tuple-element.85.refs_0_), channel_id=1, source_target_pairs={{0,1},{1,0},{2,3},{3,2},{4,5},{5,4},{6,7},{7,6},{8,9},{9,8},{10,11... | collective-permute-start | bytes 2752520 | tf_op jit(solution)/shard_map/ppermute | solution.py:353
  33.3 4.7 %collective-permute-start.13 = (bf16[64,768]{1,0:T(8,128)(2,1)S(1)}, bf16[64,768]{1,0:T(8,128)(2,1)S(1)}, u32[]{:S(2)}, u32[]{:S(2)}) collective-permute-start(bf16[64,768]{1,0:T(8,128)(2,1)S(1)} %get-tuple-element.82), channel_id=1, source_target_pairs={{0,2},{2,0},{4,6},{6,4},{8,10},{10,8},{12,14},{14,12},{1,3},{3,1},... | collective-permute-start | bytes 294920 | tf_op jit(solution)/shard_map/ppermute | solution.py:346
  33.5 13.6 %collective-permute-start.12 = (bf16[128,768]{1,0:T(8,128)(2,1)S(1)}, bf16[128,768]{1,0:T(8,128)(2,1)S(1)}, u32[]{:S(2)}, u32[]{:S(2)}) collective-permute-start(bf16[128,768]{1,0:T(8,128)(2,1)S(1)} %get-tuple-element.80), channel_id=1, source_target_pairs={{0,8},{2,10},{4,12},{6,14},{8,0},{10,2},{12,4},{14,6},{1,9},{3,11}... | collective-permute-start | bytes 589832 | tf_op jit(solution)/shard_map/ppermute | solution.py:350
  36.1 7.1 %collective-permute-start.14 = (bf16[64,768]{1,0:T(8,128)(2,1)S(1)}, bf16[64,768]{1,0:T(8,128)(2,1)S(1)}, u32[]{:S(2)}, u32[]{:S(2)}) collective-permute-start(bf16[64,768]{1,0:T(8,128)(2,1)S(1)} %get-tuple-element.83), channel_id=1, source_target_pairs={{0,4},{2,6},{4,0},{6,2},{8,12},{10,14},{12,8},{14,10},{1,5},{3,7},... | collective-permute-start | bytes 294920 | tf_op jit(solution)/shard_map/ppermute | solution.py:346
  38.0 9.1 %collective-permute-start.15 = (bf16[64,768]{1,0:T(8,128)(2,1)S(1)}, bf16[64,768]{1,0:T(8,128)(2,1)S(1)}, u32[]{:S(2)}, u32[]{:S(2)}) collective-permute-start(bf16[64,768]{1,0:T(8,128)(2,1)S(1)} %get-tuple-element.84), channel_id=1, source_target_pairs={{0,6},{2,4},{4,2},{6,0},{8,14},{10,12},{12,10},{14,8},{1,7},{3,5},... | collective-permute-start | bytes 294920 | tf_op jit(solution)/shard_map/ppermute | solution.py:346
  47.9 5.5 %collective-permute-start.19 = (bf16[64,768]{1,0:T(8,128)(2,1)S(1)}, bf16[64,768]{1,0:T(8,128)(2,1)S(1)}, u32[]{:S(2)}, u32[]{:S(2)}) collective-permute-start(bf16[64,768]{1,0:T(8,128)(2,1)S(1)} %get-tuple-element.90), channel_id=1, source_target_pairs={{0,2},{2,0},{4,6},{6,4},{8,10},{10,8},{12,14},{14,12},{1,3},{3,1},... | collective-permute-start | bytes 294920 | tf_op jit(solution)/shard_map/ppermute | solution.py:346
  47.9 5.4 %collective-permute-start.20 = (bf16[64,768]{1,0:T(8,128)(2,1)S(1)}, bf16[64,768]{1,0:T(8,128)(2,1)S(1)}, u32[]{:S(2)}, u32[]{:S(2)}) collective-permute-start(bf16[64,768]{1,0:T(8,128)(2,1)S(1)} %get-tuple-element.91), channel_id=1, source_target_pairs={{0,4},{2,6},{4,0},{6,2},{8,12},{10,14},{12,8},{14,10},{1,5},{3,7},... | collective-permute-start | bytes 294920 | tf_op jit(solution)/shard_map/ppermute | solution.py:346
  49.1 7.9 %collective-permute-start.21 = (bf16[64,768]{1,0:T(8,128)(2,1)S(1)}, bf16[64,768]{1,0:T(8,128)(2,1)S(1)}, u32[]{:S(2)}, u32[]{:S(2)}) collective-permute-start(bf16[64,768]{1,0:T(8,128)(2,1)S(1)} %get-tuple-element.92), channel_id=1, source_target_pairs={{0,6},{2,4},{4,2},{6,0},{8,14},{10,12},{12,10},{14,8},{1,7},{3,5},... | collective-permute-start | bytes 294920 | tf_op jit(solution)/shard_map/ppermute | solution.py:346
  51.4 12.7 %collective-permute-start.18 = (bf16[128,768]{1,0:T(8,128)(2,1)S(1)}, bf16[128,768]{1,0:T(8,128)(2,1)S(1)}, u32[]{:S(2)}, u32[]{:S(2)}) collective-permute-start(bf16[128,768]{1,0:T(8,128)(2,1)S(1)} %get-tuple-element.86), channel_id=1, source_target_pairs={{0,8},{2,10},{4,12},{6,14},{8,0},{10,2},{12,4},{14,6},{1,9},{3,11}... | collective-permute-start | bytes 589832 | tf_op jit(solution)/shard_map/ppermute | solution.py:350
  60.6 6.5 %collective-permute-start.22 = (bf16[64,768]{1,0:T(8,128)(2,1)S(1)}, bf16[64,768]{1,0:T(8,128)(2,1)S(1)}, u32[]{:S(2)}, u32[]{:S(2)}) collective-permute-start(bf16[64,768]{1,0:T(8,128)(2,1)S(1)} %get-tuple-element.97), channel_id=1, source_target_pairs={{0,2},{2,0},{4,6},{6,4},{8,10},{10,8},{12,14},{14,12},{1,3},{3,1},... | collective-permute-start | bytes 294920 | tf_op jit(solution)/shard_map/ppermute | solution.py:346
  61.0 7.9 %collective-permute-start.23 = (bf16[64,768]{1,0:T(8,128)(2,1)S(1)}, bf16[64,768]{1,0:T(8,128)(2,1)S(1)}, u32[]{:S(2)}, u32[]{:S(2)}) collective-permute-start(bf16[64,768]{1,0:T(8,128)(2,1)S(1)} %get-tuple-element.98), channel_id=1, source_target_pairs={{0,4},{2,6},{4,0},{6,2},{8,12},{10,14},{12,8},{14,10},{1,5},{3,7},... | collective-permute-start | bytes 294920 | tf_op jit(solution)/shard_map/ppermute | solution.py:346
  62.4 6.5 %collective-permute-start.24 = (bf16[64,768]{1,0:T(8,128)(2,1)S(1)}, bf16[64,768]{1,0:T(8,128)(2,1)S(1)}, u32[]{:S(2)}, u32[]{:S(2)}) collective-permute-start(bf16[64,768]{1,0:T(8,128)(2,1)S(1)} %get-tuple-element.99), channel_id=1, source_target_pairs={{0,6},{2,4},{4,2},{6,0},{8,14},{10,12},{12,10},{14,8},{1,7},{3,5},... | collective-permute-start | bytes 294920 | tf_op jit(solution)/shard_map/ppermute | solution.py:346
  65.4 4.6 %collective-permute-start.26 = (bf16[64,768]{1,0:T(8,128)(2,1)S(1)}, bf16[64,768]{1,0:T(8,128)(2,1)S(1)}, u32[]{:S(2)}, u32[]{:S(2)}) collective-permute-start(bf16[64,768]{1,0:T(8,128)(2,1)S(1)} %get-tuple-element.104), channel_id=1, source_target_pairs={{0,2},{2,0},{4,6},{6,4},{8,10},{10,8},{12,14},{14,12},{1,3},{3,1},... | collective-permute-start | bytes 294920 | tf_op jit(solution)/shard_map/ppermute | solution.py:346
  65.7 4.6 %collective-permute-start.27 = (bf16[64,768]{1,0:T(8,128)(2,1)S(1)}, bf16[64,768]{1,0:T(8,128)(2,1)S(1)}, u32[]{:S(2)}, u32[]{:S(2)}) collective-permute-start(bf16[64,768]{1,0:T(8,128)(2,1)S(1)} %get-tuple-element.105), channel_id=1, source_target_pairs={{0,4},{2,6},{4,0},{6,2},{8,12},{10,14},{12,8},{14,10},{1,5},{3,7},... | collective-permute-start | bytes 294920 | tf_op jit(solution)/shard_map/ppermute | solution.py:346
  67.1 5.5 %collective-permute-start.28 = (bf16[64,768]{1,0:T(8,128)(2,1)S(1)}, bf16[64,768]{1,0:T(8,128)(2,1)S(1)}, u32[]{:S(2)}, u32[]{:S(2)}) collective-permute-start(bf16[64,768]{1,0:T(8,128)(2,1)S(1)} %get-tuple-element.106), channel_id=1, source_target_pairs={{0,6},{2,4},{4,2},{6,0},{8,14},{10,12},{12,10},{14,8},{1,7},{3,5},... | collective-permute-start | bytes 294920 | tf_op jit(solution)/shard_map/ppermute | solution.py:346
  68.9 11.6 %collective-permute-start.32 = (bf16[11,256,256]{2,1,0:T(8,128)(2,1)S(1)}, bf16[11,256,256]{2,1,0:T(8,128)(2,1)S(1)}, u32[]{:S(2)}, u32[]{:S(2)}) collective-permute-start(bf16[11,256,256]{2,1,0:T(8,128)(2,1)S(1)} %get-tuple-element.111.refs_4_), channel_id=1, source_target_pairs={{0,1},{1,0},{2,3},{3,2},{4,5},{5,4},{6,7},{7,6},{8,9},{9,8},{10,11... | collective-permute-start | bytes 4325384 | tf_op jit(solution)/shard_map/ppermute | solution.py:353
  76.3 5.8 %collective-permute-start.33 = (bf16[11,256,256]{2,1,0:T(8,128)(2,1)S(1)}, bf16[11,256,256]{2,1,0:T(8,128)(2,1)S(1)}, u32[]{:S(2)}, u32[]{:S(2)}) collective-permute-start(bf16[11,256,256]{2,1,0:T(8,128)(2,1)S(1)} %get-tuple-element.112.refs_5_), channel_id=1, source_target_pairs={{0,1},{1,0},{2,3},{3,2},{4,5},{5,4},{6,7},{7,6},{8,9},{9,8},{10,11... | collective-permute-start | bytes 4325384 | tf_op jit(solution)/shard_map/ppermute | solution.py:353
  76.4 13.9 %collective-permute-start.25 = (bf16[144,768]{1,0:T(8,128)(2,1)S(1)}, bf16[144,768]{1,0:T(8,128)(2,1)S(1)}, u32[]{:S(2)}, u32[]{:S(2)}) collective-permute-start(bf16[144,768]{1,0:T(8,128)(2,1)S(1)} %far_back.1.refs_8_), channel_id=1, source_target_pairs={{0,8},{2,10},{4,12},{6,14},{8,0},{10,2},{12,4},{14,6},{1,9},{3,11}... | collective-permute-start | bytes 663560 | tf_op jit(solution)/shard_map/ppermute | solution.py:350
  78.6 11.6 %collective-permute-start.29 = (bf16[64,768]{1,0:T(8,128)(2,1)S(1)}, bf16[64,768]{1,0:T(8,128)(2,1)S(1)}, u32[]{:S(2)}, u32[]{:S(2)}) collective-permute-start(bf16[64,768]{1,0:T(8,128)(2,1)S(1)} %get-tuple-element.108), channel_id=1, source_target_pairs={{0,2},{2,0},{4,6},{6,4},{8,10},{10,8},{12,14},{14,12},{1,3},{3,1},... | collective-permute-start | bytes 294920 | tf_op jit(solution)/shard_map/ppermute | solution.py:346
  79.0 11.2 %collective-permute-start.30 = (bf16[64,768]{1,0:T(8,128)(2,1)S(1)}, bf16[64,768]{1,0:T(8,128)(2,1)S(1)}, u32[]{:S(2)}, u32[]{:S(2)}) collective-permute-start(bf16[64,768]{1,0:T(8,128)(2,1)S(1)} %get-tuple-element.109), channel_id=1, source_target_pairs={{0,4},{2,6},{4,0},{6,2},{8,12},{10,14},{12,8},{14,10},{1,5},{3,7},... | collective-permute-start | bytes 294920 | tf_op jit(solution)/shard_map/ppermute | solution.py:346
  80.5 9.7 %collective-permute-start.31 = (bf16[64,768]{1,0:T(8,128)(2,1)S(1)}, bf16[64,768]{1,0:T(8,128)(2,1)S(1)}, u32[]{:S(2)}, u32[]{:S(2)}) collective-permute-start(bf16[64,768]{1,0:T(8,128)(2,1)S(1)} %get-tuple-element.110), channel_id=1, source_target_pairs={{0,6},{2,4},{4,2},{6,0},{8,14},{10,12},{12,10},{14,8},{1,7},{3,5},... | collective-permute-start | bytes 294920 | tf_op jit(solution)/shard_map/ppermute | solution.py:346

commit v8 on v7

--- a/solution.py
+++ b/solution.py
@@ -81,6 +81,7 @@
 
 
 def get(refs):
+    refs = refs[:1] + refs[:0:-1]
     return jnp.concatenate([ref[...] for ref in refs], axis=0)
 
 
@@ -239,40 +240,34 @@
     finished[...] = jnp.zeros_like(finished)
     units = hf.shape[0]
     side = hf.shape[1]
-    part = units // 2
-
-    def columns(*sets):
-        return jnp.concatenate(
-            [jnp.concatenate([r[i] for i in range(across)], axis=1) for r in sets], axis=0
-        )
 
     def acts(own, sent, first):
-        blocks = range(across + first // side, across + (first + part) // side)
+        blocks = range(across + first // side, across + (first + units) // side)
         theirs = [jnp.concatenate([r[i] for i in blocks], axis=0) for r in sent]
-        return jnp.concatenate([r[first : first + part, :] for r in own] + theirs, axis=1)
-
-    x, rg = columns(xf, xn, xfs, xns), columns(gf, gn, gfs, gns)
+        return jnp.concatenate([r[first : first + units, :] for r in own] + theirs, axis=1)
+
+    x, rg = (xf, xn, xfs, xns), (gf, gn, gfs, gns)
     copies = []
-    for m, (own, sent, rows, offset) in enumerate(
+    for m, (own, sent, rows, first) in enumerate(
         (
+            ((hf, hn), (xfs, xns), rg, 0),
             ((df, dn), (gfs, gns), x, 0),
             ((df, dn), (gfs, gns), x, units),
-            ((hf, hn), (xfs, xns), rg, 0),
         )
     ):
-        for first in range(0, units, part):
-            slot = len(copies) % 2
-            if len(copies) > 1:
-                copies[-2].wait()
-            buf[slot] = dot(acts(own, sent, offset + first), rows).astype(BF16)
+        row = (m + 2) % 3
+        for i in range(across):
+            at = pl.ds(i * side, side)
+            column = jnp.concatenate([r[i] for r in rows], axis=0)
+            buf[row, :, at] = dot(acts(own, sent, first), column).astype(BF16)
             copies.append(
                 pltpu.make_async_copy(
-                    buf.at[slot], out_hbm.at[m, pl.ds(first, part)], sems.at[slot]
+                    buf.at[row, :, at], out_hbm.at[row, :, at], sems.at[row, i]
                 )
             )
             copies[-1].start()
-    copies[-2].wait()
-    copies[-1].wait()
+    for copy in copies:
+        copy.wait()
 
 
 def local(tokens, teacher, routes, gate_weights, weights):
@@ -341,10 +336,10 @@
         )(*args, *after, *through)
 
     def within_half(rows_of):
-        got = [rows_of[0]] + [None] * (half - 1)
-        for s in range(1, half):
-            got[s] = lax.ppermute(rows_of[s], "expert", [(i, i ^ s) for i in range(experts)])
-        return got
+        return [rows_of[0]] + [
+            lax.ppermute(rows_of[s], "expert", [(i, i ^ s) for i in range(experts)])
+            for s in range(half - 1, 0, -1)
+        ]
 
     def to_mirror(x):
         return lax.ppermute(x, "expert", [(i, i ^ half) for i in range(experts)])
@@ -451,7 +446,7 @@
         far_back_kernel, "far_back", longer, [], far_meta, d_gates_far, *back_far
     )
     part = to_mirror(part_rows)
-    grad_near, (gn, dn) = backward(rg_near, fan, fbn, "backward_near", after=[part_rows])
+    grad_near, (gn, dn) = backward(rg_near, fan, fbn, "backward_near", after=[part_rows] + back_far[1:])
     gf_sib, gn_sib = to_sibling(gf), to_sibling(gn)
     back_near = within_half(grad_near)
 
@@ -469,8 +464,8 @@
         after=[],
         limit=24,
         scratch=[
-            pltpu.VMEM((2, units // 2, width), BF16),
-            pltpu.SemaphoreType.DMA((2,)),
+            pltpu.VMEM((3, units, width), BF16),
+            pltpu.SemaphoreType.DMA((3, across)),
         ],
         in_hbm=1,
     )

time: 91.6 us -> 89.7 us (0.979)
  waiting for transfers between devices: 17.9 us -> 20.8 us
  starting transfers between devices: 41.1 us -> 38.3 us
  Pallas kernels: 26.8 us -> 25 us
    ppermute x5, starting transfers between devices: 9.89 us -> 7.03 us  [to_mirror(): return lax.ppermute(x, 'expert', [(i, i ^ half) for i in range(experts)])]
    ppermute x5, waiting for transfers between devices: 1.19 us -> 3.98 us  [to_mirror(): return lax.ppermute(x, 'expert', [(i, i ^ half) for i in range(experts)])]
    pallas_call x12, Pallas kernels: 26.8 us -> 25 us  [call(): pl.pallas_call(body, in_specs=specs + [aspec] * (len(after) + len(through...]
  transfers between devices with their start and end apart: 34 -> 34, of which waited for: 9 -> 13; matrix products, arithmetic and copies ran while one was open for 0% -> 0% of each run, Pallas kernels for 27% -> 26%
where the time goes in v8:
time: 89.7 us; the launch traced here: 89.5 us
  starting transfers between devices  38.3 us (43%)
  Pallas kernels  25 us (28%)
  waiting for transfers between devices  20.8 us (23%)
  local copies, waits for them, and re-layouts  4.63 us (5%)
    ppermute x24, starting transfers between devices, within_half(): lax.ppermute(rows_of[s], 'expert', [(i, i ^ s) for i in range(experts)])  30.6 us
    pallas_call x12, Pallas kernels, call(): pl.pallas_call(body, in_specs=specs + [aspec] * (len(after) + len(through...  25 us
    ppermute x24, waiting for transfers between devices, within_half(): lax.ppermute(rows_of[s], 'expert', [(i, i ^ s) for i in range(experts)])  16.8 us
    ppermute x5, starting transfers between devices, to_mirror(): return lax.ppermute(x, 'expert', [(i, i ^ half) for i in range(experts)])  7.03 us
    unnamed x14, local copies, waits for them, and re-layouts  4.63 us
    ppermute x5, waiting for transfers between devices, to_mirror(): return lax.ppermute(x, 'expert', [(i, i ^ half) for i in range(experts)])  3.98 us
  transfers between devices with their start and end apart: 34, of which 13 were waited for; matrix products, arithmetic and copies ran while one was open for 0% of the time, Pallas kernels for 26%

profile of v8, /device:TPU:0, one launch (start us, length us, event | category | flops | bytes accessed | tf_op | source)
XLA Modules:
  0.0 89.5 jit_solution(4702755728063114324)
XLA Ops:
  0.6 4.1 %collective-permute-start.8 = (bf16[128,768]{1,0:T(8,128)(2,1)}, bf16[128,768]{1,0:T(8,128)(2,1)S(1)}, u32[]{:S(2)}, u32[]{:S(2)}) collective-permute-start(bf16[128,768]{1,0:T(8,128)(2,1)} %refs_3_.1), channel_id=1, source_target_pairs={{0,8},{2,10},{4,12},{6,14},{8,0},{10,2},{12,4},{14,6},{1,9},{3,11}... | collective-permute-start | bytes 589832 | tf_op jit(solution)/shard_map/ppermute | solution.py:345
  4.7 2.3 %copy-done = bf16[1,1024,3,768]{3,1,2,0:T(8,128)(2,1)S(1)} copy-done((bf16[1,1024,3,768]{3,1,2,0:T(8,128)(2,1)S(1)}, bf16[1,1024,3,768]{3,1,2,0:T(8,128)(2,1)}, u32[]{:S(2)}) %copy-start) | copy-done | bytes 4718616
  7.1 0.9 %copy-done.1 = bf16[128,768]{1,0:T(8,128)(2,1)S(1)} copy-done((bf16[128,768]{1,0:T(8,128)(2,1)S(1)}, bf16[128,768]{1,0:T(8,128)(2,1)}, u32[]{:S(2)}) %copy-start.1) | copy-done | bytes 196632
  8.0 0.7 copy-done.3
  8.7 0.7 copy-done.4
  9.4 0.4 pack_near.1
  9.9 2.8 %collective-permute-start.2 = (bf16[64,768]{1,0:T(8,128)(2,1)S(1)}, bf16[64,768]{1,0:T(8,128)(2,1)S(1)}, u32[]{:S(2)}, u32[]{:S(2)}) collective-permute-start(bf16[64,768]{1,0:T(8,128)(2,1)S(1)} %get-tuple-element.64), channel_id=1, source_target_pairs={{0,6},{2,4},{4,2},{6,0},{8,14},{10,12},{12,10},{14,8},{1,7},{3,5},... | collective-permute-start | bytes 294920 | tf_op jit(solution)/shard_map/ppermute | solution.py:340
  12.7 0.5 collective-permute-start.3
  13.1 1.2 %collective-permute-done.refs_0_ = f32[8,128]{1,0:T(8,128)S(1)} collective-permute-done((f32[8,128]{1,0:T(8,128)S(1)}, f32[8,128]{1,0:T(8,128)S(1)}, u32[]{:S(2)}, u32[]{:S(2)}) %collective-permute-start) | collective-permute-done | bytes 4128 | tf_op jit(solution)/shard_map/ppermute | solution.py:345
  14.3 1.5 %collective-permute-start.4 = (bf16[64,768]{1,0:T(8,128)(2,1)S(1)}, bf16[64,768]{1,0:T(8,128)(2,1)S(1)}, u32[]{:S(2)}, u32[]{:S(2)}) collective-permute-start(bf16[64,768]{1,0:T(8,128)(2,1)S(1)} %get-tuple-element.66), channel_id=1, source_target_pairs={{0,2},{2,0},{4,6},{6,4},{8,10},{10,8},{12,14},{14,12},{1,3},{3,1},... | collective-permute-start | bytes 294920 | tf_op jit(solution)/shard_map/ppermute | solution.py:340
  16.2 1.6 %collective-permute-start.9 = (bf16[64,768]{1,0:T(8,128)(2,1)S(1)}, bf16[64,768]{1,0:T(8,128)(2,1)S(1)}, u32[]{:S(2)}, u32[]{:S(2)}) collective-permute-start(bf16[64,768]{1,0:T(8,128)(2,1)S(1)} %get-tuple-element.72), channel_id=1, source_target_pairs={{0,6},{2,4},{4,2},{6,0},{8,14},{10,12},{12,10},{14,8},{1,7},{3,5},... | collective-permute-start | bytes 294920 | tf_op jit(solution)/shard_map/ppermute | solution.py:340
  17.8 0.5 collective-permute-start.10
  18.4 1.6 %collective-permute-start.11 = (bf16[64,768]{1,0:T(8,128)(2,1)S(1)}, bf16[64,768]{1,0:T(8,128)(2,1)S(1)}, u32[]{:S(2)}, u32[]{:S(2)}) collective-permute-start(bf16[64,768]{1,0:T(8,128)(2,1)S(1)} %get-tuple-element.74), channel_id=1, source_target_pairs={{0,2},{2,0},{4,6},{6,4},{8,10},{10,8},{12,14},{14,12},{1,3},{3,1},... | collective-permute-start | bytes 294920 | tf_op jit(solution)/shard_map/ppermute | solution.py:340
  20.0 3.3 %forward_near.1 = (bf16[64,768]{1,0:T(8,128)(2,1)S(1)}, bf16[64,768]{1,0:T(8,128)(2,1)S(1)}, bf16[64,768]{1,0:T(8,128)(2,1)S(1)}, bf16[64,768]{1,0:T(8,128)(2,1)...) custom-call(bf16[3,1024,768]{2,1,0:T(8,128)(2,1)S(1)} %bitcast.13, ...), custom_call_target="tpu_custom_call" | custom-call | flops 100000000 | bytes 2097152 | tf_op jit(solution)/shard_map/forward_near/pallas_call | solution.py:322
  23.3 4.2 %collective-permute-start.5 = (bf16[64,768]{1,0:T(8,128)(2,1)S(1)}, bf16[64,768]{1,0:T(8,128)(2,1)S(1)}, u32[]{:S(2)}, u32[]{:S(2)}) collective-permute-start(bf16[64,768]{1,0:T(8,128)(2,1)S(1)} %get-tuple-element.68), channel_id=1, source_target_pairs={{0,6},{2,4},{4,2},{6,0},{8,14},{10,12},{12,10},{14,8},{1,7},{3,5},... | collective-permute-start | bytes 294920 | tf_op jit(solution)/shard_map/ppermute | solution.py:340
  27.5 0.6 collective-permute-start.7
  28.2 3.3 %forward_far.1 = (bf16[64,768]{1,0:T(8,128)(2,1)S(1)}, bf16[64,768]{1,0:T(8,128)(2,1)S(1)}, bf16[64,768]{1,0:T(8,128)(2,1)S(1)}, bf16[64,768]{1,0:T(8,128)(2,1)S...) custom-call(bf16[3,1024,768]{2,1,0:T(8,128)(2,1)S(1)} %bitcast.14, ...), custom_call_target="tpu_custom_call" | custom-call | flops 3000000000 | bytes 2097152 | tf_op jit(solution)/shard_map/forward_far/pallas_call | solution.py:322
  31.5 0.6 collective-permute-start.16
  32.2 0.5 near_sum.1
  32.6 2.9 %collective-permute-start.13 = (bf16[64,768]{1,0:T(8,128)(2,1)S(1)}, bf16[64,768]{1,0:T(8,128)(2,1)S(1)}, u32[]{:S(2)}, u32[]{:S(2)}) collective-permute-start(bf16[64,768]{1,0:T(8,128)(2,1)S(1)} %get-tuple-element.82), channel_id=1, source_target_pairs={{0,6},{2,4},{4,2},{6,0},{8,14},{10,12},{12,10},{14,8},{1,7},{3,5},... | collective-permute-start | bytes 294920 | tf_op jit(solution)/shard_map/ppermute | solution.py:340
  35.5 1.5 %collective-permute-start.12 = (bf16[128,768]{1,0:T(8,128)(2,1)S(1)}, bf16[128,768]{1,0:T(8,128)(2,1)S(1)}, u32[]{:S(2)}, u32[]{:S(2)}) collective-permute-start(bf16[128,768]{1,0:T(8,128)(2,1)S(1)} %get-tuple-element.80), channel_id=1, source_target_pairs={{0,8},{2,10},{4,12},{6,14},{8,0},{10,2},{12,4},{14,6},{1,9},{3,11}... | collective-permute-start | bytes 589832 | tf_op jit(solution)/shard_map/ppermute | solution.py:345
  37.0 2.3 %collective-permute-done.13.refs_3_ = bf16[64,768]{1,0:T(8,128)(2,1)S(1)} collective-permute-done((bf16[64,768]{1,0:T(8,128)(2,1)S(1)}, bf16[64,768]{1,0:T(8,128)(2,1)S(1)}, u32[]{:S(2)}, u32[]{:S(2)}) %collective-permute-start.13) | collective-permute-done | bytes 98336 | tf_op jit(solution)/shard_map/ppermute | solution.py:340
  39.3 0.4 collective-permute-start.15
  39.7 4.4 %collective-permute-done.14.refs_4_ = bf16[64,768]{1,0:T(8,128)(2,1)S(1)} collective-permute-done((bf16[64,768]{1,0:T(8,128)(2,1)S(1)}, bf16[64,768]{1,0:T(8,128)(2,1)S(1)}, u32[]{:S(2)}, u32[]{:S(2)}) %collective-permute-start.14) | collective-permute-done | bytes 98336 | tf_op jit(solution)/shard_map/ppermute | solution.py:340
  44.1 2.8 %collective-permute-done.12.refs_1_ = bf16[128,768]{1,0:T(8,128)(2,1)S(1)} collective-permute-done((bf16[128,768]{1,0:T(8,128)(2,1)S(1)}, bf16[128,768]{1,0:T(8,128)(2,1)S(1)}, u32[]{:S(2)}, u32[]{:S(2)}) %collective-permute-start.12) | collective-permute-done | bytes 196640 | tf_op jit(solution)/shard_map/ppermute | solution.py:345
  46.9 0.8 far_grad.1
  47.8 1.8 %collective-permute-start.20 = (bf16[64,768]{1,0:T(8,128)(2,1)S(1)}, bf16[64,768]{1,0:T(8,128)(2,1)S(1)}, u32[]{:S(2)}, u32[]{:S(2)}) collective-permute-start(bf16[64,768]{1,0:T(8,128)(2,1)S(1)} %get-tuple-element.91), channel_id=1, source_target_pairs={{0,4},{2,6},{4,0},{6,2},{8,12},{10,14},{12,8},{14,10},{1,5},{3,7},... | collective-permute-start | bytes 294920 | tf_op jit(solution)/shard_map/ppermute | solution.py:340
  49.6 1.7 %collective-permute-start.21 = (bf16[64,768]{1,0:T(8,128)(2,1)S(1)}, bf16[64,768]{1,0:T(8,128)(2,1)S(1)}, u32[]{:S(2)}, u32[]{:S(2)}) collective-permute-start(bf16[64,768]{1,0:T(8,128)(2,1)S(1)} %get-tuple-element.92), channel_id=1, source_target_pairs={{0,2},{2,0},{4,6},{6,4},{8,10},{10,8},{12,14},{14,12},{1,3},{3,1},... | collective-permute-start | bytes 294920 | tf_op jit(solution)/shard_map/ppermute | solution.py:340
  51.3 0.6 collective-permute-start.18
  51.9 2.6 %collective-permute-done.19.refs_5_ = bf16[64,768]{1,0:T(8,128)(2,1)S(1)} collective-permute-done((bf16[64,768]{1,0:T(8,128)(2,1)S(1)}, bf16[64,768]{1,0:T(8,128)(2,1)S(1)}, u32[]{:S(2)}, u32[]{:S(2)}) %collective-permute-start.19) | collective-permute-done | bytes 98336 | tf_op jit(solution)/shard_map/ppermute | solution.py:340
  54.5 0.5 collective-permute-done.21.refs_7_
  55.0 3.7 %backward_far.1 = (bf16[64,768]{1,0:T(8,128)(2,1)S(1)}, bf16[64,768]{1,0:T(8,128)(2,1)S(1)}, bf16[64,768]{1,0:T(8,128)(2,1)S(1)}, bf16[64,768]{1,0:T(8,128)(2,1)...) custom-call(bf16[3,1024,768]{2,1,0:T(8,128)(2,1)S(1)} %bitcast.15, ...), custom_call_target="tpu_custom_call" | custom-call | flops 3000000000 | bytes 2097152 | tf_op jit(solution)/shard_map/backward_far/pallas_call | solution.py:322
  58.7 1.5 %collective-permute-start.22 = (bf16[64,768]{1,0:T(8,128)(2,1)S(1)}, bf16[64,768]{1,0:T(8,128)(2,1)S(1)}, u32[]{:S(2)}, u32[]{:S(2)}) collective-permute-start(bf16[64,768]{1,0:T(8,128)(2,1)S(1)} %get-tuple-element.97), channel_id=1, source_target_pairs={{0,6},{2,4},{4,2},{6,0},{8,14},{10,12},{12,10},{14,8},{1,7},{3,5},... | collective-permute-start | bytes 294920 | tf_op jit(solution)/shard_map/ppermute | solution.py:340
  60.2 1.8 %collective-permute-start.23 = (bf16[64,768]{1,0:T(8,128)(2,1)S(1)}, bf16[64,768]{1,0:T(8,128)(2,1)S(1)}, u32[]{:S(2)}, u32[]{:S(2)}) collective-permute-start(bf16[64,768]{1,0:T(8,128)(2,1)S(1)} %get-tuple-element.98), channel_id=1, source_target_pairs={{0,4},{2,6},{4,0},{6,2},{8,12},{10,14},{12,8},{14,10},{1,5},{3,7},... | collective-permute-start | bytes 294920 | tf_op jit(solution)/shard_map/ppermute | solution.py:340
  62.2 1.2 %near_grad.1 = (bf16[128,768]{1,0:T(8,128)(2,1)}, f32[2,128]{1,0:T(2,128)S(1)}, bf16[64,768]{1,0:T(8,128)(2,1)S(1)}, bf16[64,768]{1,0:T(8,128)(2,1)S(1)}, bf16[6...) custom-call(f32[8,128]{1,0:T(8,128)S(1)} %get-tuple-element.62.refs_0_, bf16[128,768]{1,0:T(8,128)(2,1)S(1)} %copy-done.2, ...), custom_call_target="tpu_custom_call" | custom-call | flops 30000001024 | bytes 2097152 | tf_op jit(solution)/shard_map/near_grad/pallas_call | solution.py:322
  63.4 1.5 %collective-permute-start.26 = (bf16[64,768]{1,0:T(8,128)(2,1)S(1)}, bf16[64,768]{1,0:T(8,128)(2,1)S(1)}, u32[]{:S(2)}, u32[]{:S(2)}) collective-permute-start(bf16[64,768]{1,0:T(8,128)(2,1)S(1)} %get-tuple-element.104), channel_id=1, source_target_pairs={{0,6},{2,4},{4,2},{6,0},{8,14},{10,12},{12,10},{14,8},{1,7},{3,5},... | collective-permute-start | bytes 294920 | tf_op jit(solution)/shard_map/ppermute | solution.py:340
  64.9 1.8 %collective-permute-start.27 = (bf16[64,768]{1,0:T(8,128)(2,1)S(1)}, bf16[64,768]{1,0:T(8,128)(2,1)S(1)}, u32[]{:S(2)}, u32[]{:S(2)}) collective-permute-start(bf16[64,768]{1,0:T(8,128)(2,1)S(1)} %get-tuple-element.105), channel_id=1, source_target_pairs={{0,4},{2,6},{4,0},{6,2},{8,12},{10,14},{12,8},{14,10},{1,5},{3,7},... | collective-permute-start | bytes 294920 | tf_op jit(solution)/shard_map/ppermute | solution.py:340
  67.2 2.3 %collective-permute-done.24.refs_5_.refs_11_ = bf16[64,768]{1,0:T(8,128)(2,1)S(1)} collective-permute-done((bf16[64,768]{1,0:T(8,128)(2,1)S(1)}, bf16[64,768]{1,0:T(8,128)(2,1)S(1)}, u32[]{:S(2)}, u32[]{:S(2)}) %collective-permute-start.24) | collective-permute-done | bytes 98336 | tf_op jit(solution)/shard_map/ppermute | solution.py:340
  69.5 0.4 far_back.1.refs_8_
  69.9 0.4 collective-permute-done.27.refs_6_
  70.3 1.0 %collective-permute-done.28.refs_7_ = bf16[64,768]{1,0:T(8,128)(2,1)S(1)} collective-permute-done((bf16[64,768]{1,0:T(8,128)(2,1)S(1)}, bf16[64,768]{1,0:T(8,128)(2,1)S(1)}, u32[]{:S(2)}, u32[]{:S(2)}) %collective-permute-start.28) | collective-permute-done | bytes 98336 | tf_op jit(solution)/shard_map/ppermute | solution.py:340
  71.3 3.7 %backward_near.1 = (bf16[64,768]{1,0:T(8,128)(2,1)S(1)}, bf16[64,768]{1,0:T(8,128)(2,1)S(1)}, bf16[64,768]{1,0:T(8,128)(2,1)S(1)}, bf16[64,768]{1,0:T(8,128)(2,1...) custom-call(bf16[3,1024,768]{2,1,0:T(8,128)(2,1)S(1)} %bitcast.16, ...), custom_call_target="tpu_custom_call" | custom-call | flops 10000000000 | bytes 2097152 | tf_op jit(solution)/shard_map/backward_near/pallas_call | solution.py:322
  75.1 0.7 collective-permute-start.25
  75.8 2.8 %collective-permute-start.29 = (bf16[64,768]{1,0:T(8,128)(2,1)S(1)}, bf16[64,768]{1,0:T(8,128)(2,1)S(1)}, u32[]{:S(2)}, u32[]{:S(2)}) collective-permute-start(bf16[64,768]{1,0:T(8,128)(2,1)S(1)} %get-tuple-element.108), channel_id=1, source_target_pairs={{0,6},{2,4},{4,2},{6,0},{8,14},{10,12},{12,10},{14,8},{1,7},{3,5},... | collective-permute-start | bytes 294920 | tf_op jit(solution)/shard_map/ppermute | solution.py:340
  78.7 0.5 collective-permute-start.31
  79.3 6.3 %weight_gradients.1 = (bf16[3,1024,768]{2,1,0:T(8,128)(2,1)}, f32[8,128]{1,0:T(8,128)S(1)}) custom-call(bf16[7,256,256]{2,1,0:T(8,128)(2,1)S(1)} %get-tuple-element.85.refs_0_, bf16[7,256,256]{2,1,0:T(8,128)(2,1)S(1)} %get-tuple-element.75.refs_6_.refs_1_, bf16[7,256,256]{2,1,0:T(8,128)(2,1)S(1)} %collective-permute-done.16.refs_6_.refs_2_, ...), custom_call_target="tpu_custom_call" | custom-call | flops 30000001024 | bytes 2097152 | tf_op jit(solution)/shard_map/weight_gradients/pallas_call | solution.py:322
  85.6 2.8 %collective-permute-done.30.refs_5_ = bf16[64,768]{1,0:T(8,128)(2,1)S(1)} collective-permute-done((bf16[64,768]{1,0:T(8,128)(2,1)S(1)}, bf16[64,768]{1,0:T(8,128)(2,1)S(1)}, u32[]{:S(2)}, u32[]{:S(2)}) %collective-permute-start.30) | collective-permute-done | bytes 98336 | tf_op jit(solution)/shard_map/ppermute | solution.py:340
  88.4 1.1 %combine_gradients.1 = (bf16[128,768]{1,0:T(8,128)(2,1)}, f32[2,128]{1,0:T(2,128)}) custom-call(f32[8,128]{1,0:T(8,128)S(1)} %get-tuple-element.62.refs_0_, bf16[144,768]{1,0:T(8,128)(2,1)S(1)} %collective-permute-done.25.refs_1_, f32[2,128]{1,0:T(2,128)S(1)} %get-tuple-element.100.refs_2_, bf16[64,768]{1,0:T(8,128)(2,1)S(1)} %get-tuple-element.107.refs_3_, ...), custom_call_target="tpu_custom_call" | custom-call | flops 30000001024 | bytes 2097152 | tf_op jit(solution)/shard_map/combine_gradients/pallas_call | solution.py:322
  (47 shorter events, 1.8 us)
Async XLA Ops:
  0.6 15.2 %collective-permute-start.8 = (bf16[128,768]{1,0:T(8,128)(2,1)}, bf16[128,768]{1,0:T(8,128)(2,1)S(1)}, u32[]{:S(2)}, u32[]{:S(2)}) collective-permute-start(bf16[128,768]{1,0:T(8,128)(2,1)} %refs_3_.1), channel_id=1, source_target_pairs={{0,8},{2,10},{4,12},{6,14},{8,0},{10,2},{12,4},{14,6},{1,9},{3,11}... | collective-permute-start | bytes 589832 | tf_op jit(solution)/shard_map/ppermute | solution.py:345
  4.7 15.2 %collective-permute-start.1 = (bf16[3,1024,768]{2,1,0:T(8,128)(2,1)}, bf16[3,1024,768]{2,1,0:T(8,128)(2,1)S(1)}, u32[]{:S(2)}, u32[]{:S(2)}) collective-permute-start(bf16[3,1024,768]{2,1,0:T(8,128)(2,1)} %bitcast.9), channel_id=1, source_target_pairs={{0,1},{1,0},{2,3},{3,2},{4,5},{5,4},{6,7},{7,6},{8,9},{9,8},{10,11... | collective-permute-start | bytes 14155784 | tf_op jit(solution)/shard_map/ppermute | solution.py:348
  4.7 2.3 %copy-start = (bf16[1,1024,3,768]{3,1,2,0:T(8,128)(2,1)S(1)}, bf16[1,1024,3,768]{3,1,2,0:T(8,128)(2,1)}, u32[]{:S(2)}) copy-start(bf16[1,1024,3,768]{3,1,2,0:T(8,128)(2,1)} %param.9) | copy-start | bytes 14155780
  7.1 0.9 %copy-start.1 = (bf16[128,768]{1,0:T(8,128)(2,1)S(1)}, bf16[128,768]{1,0:T(8,128)(2,1)}, u32[]{:S(2)}) copy-start(bf16[128,768]{1,0:T(8,128)(2,1)} %refs_3_.1) | copy-start | bytes 589828
  8.0 0.7 copy-start.3
  8.7 0.7 copy-start.4
  9.7 4.6 %collective-permute-start = (f32[8,128]{1,0:T(8,128)S(1)}, f32[8,128]{1,0:T(8,128)S(1)}, u32[]{:S(2)}, u32[]{:S(2)}) collective-permute-start(f32[8,128]{1,0:T(8,128)S(1)} %get-tuple-element.62.refs_0_), channel_id=1, source_target_pairs={{0,8},{2,10},{4,12},{6,14},{8,0},{10,2},{12,4},{14,6},{1,9},{3,11}... | collective-permute-start | bytes 12296 | tf_op jit(solution)/shard_map/ppermute | solution.py:345
  9.9 7.9 %collective-permute-start.2 = (bf16[64,768]{1,0:T(8,128)(2,1)S(1)}, bf16[64,768]{1,0:T(8,128)(2,1)S(1)}, u32[]{:S(2)}, u32[]{:S(2)}) collective-permute-start(bf16[64,768]{1,0:T(8,128)(2,1)S(1)} %get-tuple-element.64), channel_id=1, source_target_pairs={{0,6},{2,4},{4,2},{6,0},{8,14},{10,12},{12,10},{14,8},{1,7},{3,5},... | collective-permute-start | bytes 294920 | tf_op jit(solution)/shard_map/ppermute | solution.py:340
  12.7 5.7 %collective-permute-start.3 = (bf16[64,768]{1,0:T(8,128)(2,1)S(1)}, bf16[64,768]{1,0:T(8,128)(2,1)S(1)}, u32[]{:S(2)}, u32[]{:S(2)}) collective-permute-start(bf16[64,768]{1,0:T(8,128)(2,1)S(1)} %get-tuple-element.65), channel_id=1, source_target_pairs={{0,4},{2,6},{4,0},{6,2},{8,12},{10,14},{12,8},{14,10},{1,5},{3,7},... | collective-permute-start | bytes 294920 | tf_op jit(solution)/shard_map/ppermute | solution.py:340
  14.3 5.7 %slice-start = ((s8[4718592]{0:T(1024)(128)(4,1)}), s8[4194304]{0:T(1024)(128)(4,1)S(1)}, s32[]{:S(2)}) async-start(s8[4718592]{0:T(1024)(128)(4,1)} %bitcast.11), calls=%async_computation | async-start | bytes 8388608
  14.3 5.7 %slice-start.1 = ((s8[4718592]{0:T(1024)(128)(4,1)}), s8[524288]{0:T(1024)(128)(4,1)S(1)}, s32[]{:S(2)}) async-start(s8[4718592]{0:T(1024)(128)(4,1)} %bitcast.11), calls=%async_computation.1 | async-start | bytes 1048576
  14.3 5.7 %collective-permute-start.4 = (bf16[64,768]{1,0:T(8,128)(2,1)S(1)}, bf16[64,768]{1,0:T(8,128)(2,1)S(1)}, u32[]{:S(2)}, u32[]{:S(2)}) collective-permute-start(bf16[64,768]{1,0:T(8,128)(2,1)S(1)} %get-tuple-element.66), channel_id=1, source_target_pairs={{0,2},{2,0},{4,6},{6,4},{8,10},{10,8},{12,14},{14,12},{1,3},{3,1},... | collective-permute-start | bytes 294920 | tf_op jit(solution)/shard_map/ppermute | solution.py:340
  16.2 11.3 %collective-permute-start.9 = (bf16[64,768]{1,0:T(8,128)(2,1)S(1)}, bf16[64,768]{1,0:T(8,128)(2,1)S(1)}, u32[]{:S(2)}, u32[]{:S(2)}) collective-permute-start(bf16[64,768]{1,0:T(8,128)(2,1)S(1)} %get-tuple-element.72), channel_id=1, source_target_pairs={{0,6},{2,4},{4,2},{6,0},{8,14},{10,12},{12,10},{14,8},{1,7},{3,5},... | collective-permute-start | bytes 294920 | tf_op jit(solution)/shard_map/ppermute | solution.py:340
  17.8 10.4 %collective-permute-start.10 = (bf16[64,768]{1,0:T(8,128)(2,1)S(1)}, bf16[64,768]{1,0:T(8,128)(2,1)S(1)}, u32[]{:S(2)}, u32[]{:S(2)}) collective-permute-start(bf16[64,768]{1,0:T(8,128)(2,1)S(1)} %get-tuple-element.73), channel_id=1, source_target_pairs={{0,4},{2,6},{4,0},{6,2},{8,12},{10,14},{12,8},{14,10},{1,5},{3,7},... | collective-permute-start | bytes 294920 | tf_op jit(solution)/shard_map/ppermute | solution.py:340
  18.4 9.8 %collective-permute-start.11 = (bf16[64,768]{1,0:T(8,128)(2,1)S(1)}, bf16[64,768]{1,0:T(8,128)(2,1)S(1)}, u32[]{:S(2)}, u32[]{:S(2)}) collective-permute-start(bf16[64,768]{1,0:T(8,128)(2,1)S(1)} %get-tuple-element.74), channel_id=1, source_target_pairs={{0,2},{2,0},{4,6},{6,4},{8,10},{10,8},{12,14},{14,12},{1,3},{3,1},... | collective-permute-start | bytes 294920 | tf_op jit(solution)/shard_map/ppermute | solution.py:340
  23.3 8.8 %collective-permute-start.5 = (bf16[64,768]{1,0:T(8,128)(2,1)S(1)}, bf16[64,768]{1,0:T(8,128)(2,1)S(1)}, u32[]{:S(2)}, u32[]{:S(2)}) collective-permute-start(bf16[64,768]{1,0:T(8,128)(2,1)S(1)} %get-tuple-element.68), channel_id=1, source_target_pairs={{0,6},{2,4},{4,2},{6,0},{8,14},{10,12},{12,10},{14,8},{1,7},{3,5},... | collective-permute-start | bytes 294920 | tf_op jit(solution)/shard_map/ppermute | solution.py:340
  27.5 4.6 %collective-permute-start.6 = (bf16[64,768]{1,0:T(8,128)(2,1)S(1)}, bf16[64,768]{1,0:T(8,128)(2,1)S(1)}, u32[]{:S(2)}, u32[]{:S(2)}) collective-permute-start(bf16[64,768]{1,0:T(8,128)(2,1)S(1)} %get-tuple-element.69), channel_id=1, source_target_pairs={{0,4},{2,6},{4,0},{6,2},{8,12},{10,14},{12,8},{14,10},{1,5},{3,7},... | collective-permute-start | bytes 294920 | tf_op jit(solution)/shard_map/ppermute | solution.py:340
  27.5 4.6 %collective-permute-start.7 = (bf16[64,768]{1,0:T(8,128)(2,1)S(1)}, bf16[64,768]{1,0:T(8,128)(2,1)S(1)}, u32[]{:S(2)}, u32[]{:S(2)}) collective-permute-start(bf16[64,768]{1,0:T(8,128)(2,1)S(1)} %get-tuple-element.70), channel_id=1, source_target_pairs={{0,2},{2,0},{4,6},{6,4},{8,10},{10,8},{12,14},{14,12},{1,3},{3,1},... | collective-permute-start | bytes 294920 | tf_op jit(solution)/shard_map/ppermute | solution.py:340
  28.2 18.7 %collective-permute-start.17 = (bf16[7,256,256]{2,1,0:T(8,128)(2,1)S(1)}, bf16[7,256,256]{2,1,0:T(8,128)(2,1)S(1)}, u32[]{:S(2)}, u32[]{:S(2)}) collective-permute-start(bf16[7,256,256]{2,1,0:T(8,128)(2,1)S(1)} %get-tuple-element.75.refs_6_.refs_1_), channel_id=1, source_target_pairs={{0,1},{1,0},{2,3},{3,2},{4,5},{5,4},{6,7},{7,6},{8,9},{9,8},{10,11... | collective-permute-start | bytes 2752520 | tf_op jit(solution)/shard_map/ppermute | solution.py:348
  28.2 4.0 %copy-start.2 = (bf16[128,768]{1,0:T(8,128)(2,1)S(1)}, bf16[128,768]{1,0:T(8,128)(2,1)}, u32[]{:S(2)}) copy-start(bf16[128,768]{1,0:T(8,128)(2,1)} %refs_1_.3) | copy-start | bytes 589828
  31.5 15.4 %collective-permute-start.16 = (bf16[7,256,256]{2,1,0:T(8,128)(2,1)S(1)}, bf16[7,256,256]{2,1,0:T(8,128)(2,1)S(1)}, u32[]{:S(2)}, u32[]{:S(2)}) collective-permute-start(bf16[7,256,256]{2,1,0:T(8,128)(2,1)S(1)} %get-tuple-element.85.refs_0_), channel_id=1, source_target_pairs={{0,1},{1,0},{2,3},{3,2},{4,5},{5,4},{6,7},{7,6},{8,9},{9,8},{10,11... | collective-permute-start | bytes 2752520 | tf_op jit(solution)/shard_map/ppermute | solution.py:348
  32.6 6.6 %collective-permute-start.13 = (bf16[64,768]{1,0:T(8,128)(2,1)S(1)}, bf16[64,768]{1,0:T(8,128)(2,1)S(1)}, u32[]{:S(2)}, u32[]{:S(2)}) collective-permute-start(bf16[64,768]{1,0:T(8,128)(2,1)S(1)} %get-tuple-element.82), channel_id=1, source_target_pairs={{0,6},{2,4},{4,2},{6,0},{8,14},{10,12},{12,10},{14,8},{1,7},{3,5},... | collective-permute-start | bytes 294920 | tf_op jit(solution)/shard_map/ppermute | solution.py:340
  35.5 11.4 %collective-permute-start.12 = (bf16[128,768]{1,0:T(8,128)(2,1)S(1)}, bf16[128,768]{1,0:T(8,128)(2,1)S(1)}, u32[]{:S(2)}, u32[]{:S(2)}) collective-permute-start(bf16[128,768]{1,0:T(8,128)(2,1)S(1)} %get-tuple-element.80), channel_id=1, source_target_pairs={{0,8},{2,10},{4,12},{6,14},{8,0},{10,2},{12,4},{14,6},{1,9},{3,11}... | collective-permute-start | bytes 589832 | tf_op jit(solution)/shard_map/ppermute | solution.py:345
  37.0 7.1 %collective-permute-start.14 = (bf16[64,768]{1,0:T(8,128)(2,1)S(1)}, bf16[64,768]{1,0:T(8,128)(2,1)S(1)}, u32[]{:S(2)}, u32[]{:S(2)}) collective-permute-start(bf16[64,768]{1,0:T(8,128)(2,1)S(1)} %get-tuple-element.83), channel_id=1, source_target_pairs={{0,4},{2,6},{4,0},{6,2},{8,12},{10,14},{12,8},{14,10},{1,5},{3,7},... | collective-permute-start | bytes 294920 | tf_op jit(solution)/shard_map/ppermute | solution.py:340
  39.3 4.9 %collective-permute-start.15 = (bf16[64,768]{1,0:T(8,128)(2,1)S(1)}, bf16[64,768]{1,0:T(8,128)(2,1)S(1)}, u32[]{:S(2)}, u32[]{:S(2)}) collective-permute-start(bf16[64,768]{1,0:T(8,128)(2,1)S(1)} %get-tuple-element.84), channel_id=1, source_target_pairs={{0,2},{2,0},{4,6},{6,4},{8,10},{10,8},{12,14},{14,12},{1,3},{3,1},... | collective-permute-start | bytes 294920 | tf_op jit(solution)/shard_map/ppermute | solution.py:340
  47.7 6.7 %collective-permute-start.19 = (bf16[64,768]{1,0:T(8,128)(2,1)S(1)}, bf16[64,768]{1,0:T(8,128)(2,1)S(1)}, u32[]{:S(2)}, u32[]{:S(2)}) collective-permute-start(bf16[64,768]{1,0:T(8,128)(2,1)S(1)} %get-tuple-element.90), channel_id=1, source_target_pairs={{0,6},{2,4},{4,2},{6,0},{8,14},{10,12},{12,10},{14,8},{1,7},{3,5},... | collective-permute-start | bytes 294920 | tf_op jit(solution)/shard_map/ppermute | solution.py:340
  47.8 6.7 %collective-permute-start.20 = (bf16[64,768]{1,0:T(8,128)(2,1)S(1)}, bf16[64,768]{1,0:T(8,128)(2,1)S(1)}, u32[]{:S(2)}, u32[]{:S(2)}) collective-permute-start(bf16[64,768]{1,0:T(8,128)(2,1)S(1)} %get-tuple-element.91), channel_id=1, source_target_pairs={{0,4},{2,6},{4,0},{6,2},{8,12},{10,14},{12,8},{14,10},{1,5},{3,7},... | collective-permute-start | bytes 294920 | tf_op jit(solution)/shard_map/ppermute | solution.py:340
  49.6 5.4 %collective-permute-start.21 = (bf16[64,768]{1,0:T(8,128)(2,1)S(1)}, bf16[64,768]{1,0:T(8,128)(2,1)S(1)}, u32[]{:S(2)}, u32[]{:S(2)}) collective-permute-start(bf16[64,768]{1,0:T(8,128)(2,1)S(1)} %get-tuple-element.92), channel_id=1, source_target_pairs={{0,2},{2,0},{4,6},{6,4},{8,10},{10,8},{12,14},{14,12},{1,3},{3,1},... | collective-permute-start | bytes 294920 | tf_op jit(solution)/shard_map/ppermute | solution.py:340
  51.3 10.9 %collective-permute-start.18 = (bf16[128,768]{1,0:T(8,128)(2,1)S(1)}, bf16[128,768]{1,0:T(8,128)(2,1)S(1)}, u32[]{:S(2)}, u32[]{:S(2)}) collective-permute-start(bf16[128,768]{1,0:T(8,128)(2,1)S(1)} %get-tuple-element.86), channel_id=1, source_target_pairs={{0,8},{2,10},{4,12},{6,14},{8,0},{10,2},{12,4},{14,6},{1,9},{3,11}... | collective-permute-start | bytes 589832 | tf_op jit(solution)/shard_map/ppermute | solution.py:345
  58.7 8.0 %collective-permute-start.22 = (bf16[64,768]{1,0:T(8,128)(2,1)S(1)}, bf16[64,768]{1,0:T(8,128)(2,1)S(1)}, u32[]{:S(2)}, u32[]{:S(2)}) collective-permute-start(bf16[64,768]{1,0:T(8,128)(2,1)S(1)} %get-tuple-element.97), channel_id=1, source_target_pairs={{0,6},{2,4},{4,2},{6,0},{8,14},{10,12},{12,10},{14,8},{1,7},{3,5},... | collective-permute-start | bytes 294920 | tf_op jit(solution)/shard_map/ppermute | solution.py:340
  60.2 7.0 %collective-permute-start.23 = (bf16[64,768]{1,0:T(8,128)(2,1)S(1)}, bf16[64,768]{1,0:T(8,128)(2,1)S(1)}, u32[]{:S(2)}, u32[]{:S(2)}) collective-permute-start(bf16[64,768]{1,0:T(8,128)(2,1)S(1)} %get-tuple-element.98), channel_id=1, source_target_pairs={{0,4},{2,6},{4,0},{6,2},{8,12},{10,14},{12,8},{14,10},{1,5},{3,7},... | collective-permute-start | bytes 294920 | tf_op jit(solution)/shard_map/ppermute | solution.py:340
  62.0 7.5 %collective-permute-start.24 = (bf16[64,768]{1,0:T(8,128)(2,1)S(1)}, bf16[64,768]{1,0:T(8,128)(2,1)S(1)}, u32[]{:S(2)}, u32[]{:S(2)}) collective-permute-start(bf16[64,768]{1,0:T(8,128)(2,1)S(1)} %get-tuple-element.99), channel_id=1, source_target_pairs={{0,2},{2,0},{4,6},{6,4},{8,10},{10,8},{12,14},{14,12},{1,3},{3,1},... | collective-permute-start | bytes 294920 | tf_op jit(solution)/shard_map/ppermute | solution.py:340
  63.4 6.4 %collective-permute-start.26 = (bf16[64,768]{1,0:T(8,128)(2,1)S(1)}, bf16[64,768]{1,0:T(8,128)(2,1)S(1)}, u32[]{:S(2)}, u32[]{:S(2)}) collective-permute-start(bf16[64,768]{1,0:T(8,128)(2,1)S(1)} %get-tuple-element.104), channel_id=1, source_target_pairs={{0,6},{2,4},{4,2},{6,0},{8,14},{10,12},{12,10},{14,8},{1,7},{3,5},... | collective-permute-start | bytes 294920 | tf_op jit(solution)/shard_map/ppermute | solution.py:340
  64.9 5.4 %collective-permute-start.27 = (bf16[64,768]{1,0:T(8,128)(2,1)S(1)}, bf16[64,768]{1,0:T(8,128)(2,1)S(1)}, u32[]{:S(2)}, u32[]{:S(2)}) collective-permute-start(bf16[64,768]{1,0:T(8,128)(2,1)S(1)} %get-tuple-element.105), channel_id=1, source_target_pairs={{0,4},{2,6},{4,0},{6,2},{8,12},{10,14},{12,8},{14,10},{1,5},{3,7},... | collective-permute-start | bytes 294920 | tf_op jit(solution)/shard_map/ppermute | solution.py:340
  66.7 4.6 %collective-permute-start.28 = (bf16[64,768]{1,0:T(8,128)(2,1)S(1)}, bf16[64,768]{1,0:T(8,128)(2,1)S(1)}, u32[]{:S(2)}, u32[]{:S(2)}) collective-permute-start(bf16[64,768]{1,0:T(8,128)(2,1)S(1)} %get-tuple-element.106), channel_id=1, source_target_pairs={{0,2},{2,0},{4,6},{6,4},{8,10},{10,8},{12,14},{14,12},{1,3},{3,1},... | collective-permute-start | bytes 294920 | tf_op jit(solution)/shard_map/ppermute | solution.py:340
  67.2 11.6 %collective-permute-start.32 = (bf16[11,256,256]{2,1,0:T(8,128)(2,1)S(1)}, bf16[11,256,256]{2,1,0:T(8,128)(2,1)S(1)}, u32[]{:S(2)}, u32[]{:S(2)}) collective-permute-start(bf16[11,256,256]{2,1,0:T(8,128)(2,1)S(1)} %get-tuple-element.111.refs_4_), channel_id=1, source_target_pairs={{0,1},{1,0},{2,3},{3,2},{4,5},{5,4},{6,7},{7,6},{8,9},{9,8},{10,11... | collective-permute-start | bytes 4325384 | tf_op jit(solution)/shard_map/ppermute | solution.py:348
  75.0 4.3 %collective-permute-start.33 = (bf16[11,256,256]{2,1,0:T(8,128)(2,1)S(1)}, bf16[11,256,256]{2,1,0:T(8,128)(2,1)S(1)}, u32[]{:S(2)}, u32[]{:S(2)}) collective-permute-start(bf16[11,256,256]{2,1,0:T(8,128)(2,1)S(1)} %get-tuple-element.112.refs_5_), channel_id=1, source_target_pairs={{0,1},{1,0},{2,3},{3,2},{4,5},{5,4},{6,7},{7,6},{8,9},{9,8},{10,11... | collective-permute-start | bytes 4325384 | tf_op jit(solution)/shard_map/ppermute | solution.py:348
  75.1 13.3 %collective-permute-start.25 = (bf16[144,768]{1,0:T(8,128)(2,1)S(1)}, bf16[144,768]{1,0:T(8,128)(2,1)S(1)}, u32[]{:S(2)}, u32[]{:S(2)}) collective-permute-start(bf16[144,768]{1,0:T(8,128)(2,1)S(1)} %far_back.1.refs_8_), channel_id=1, source_target_pairs={{0,8},{2,10},{4,12},{6,14},{8,0},{10,2},{12,4},{14,6},{1,9},{3,11}... | collective-permute-start | bytes 663560 | tf_op jit(solution)/shard_map/ppermute | solution.py:345
  75.8 9.8 %collective-permute-start.29 = (bf16[64,768]{1,0:T(8,128)(2,1)S(1)}, bf16[64,768]{1,0:T(8,128)(2,1)S(1)}, u32[]{:S(2)}, u32[]{:S(2)}) collective-permute-start(bf16[64,768]{1,0:T(8,128)(2,1)S(1)} %get-tuple-element.108), channel_id=1, source_target_pairs={{0,6},{2,4},{4,2},{6,0},{8,14},{10,12},{12,10},{14,8},{1,7},{3,5},... | collective-permute-start | bytes 294920 | tf_op jit(solution)/shard_map/ppermute | solution.py:340
  78.6 9.8 %collective-permute-start.30 = (bf16[64,768]{1,0:T(8,128)(2,1)S(1)}, bf16[64,768]{1,0:T(8,128)(2,1)S(1)}, u32[]{:S(2)}, u32[]{:S(2)}) collective-permute-start(bf16[64,768]{1,0:T(8,128)(2,1)S(1)} %get-tuple-element.109), channel_id=1, source_target_pairs={{0,4},{2,6},{4,0},{6,2},{8,12},{10,14},{12,8},{14,10},{1,5},{3,7},... | collective-permute-start | bytes 294920 | tf_op jit(solution)/shard_map/ppermute | solution.py:340
  78.7 9.7 %collective-permute-start.31 = (bf16[64,768]{1,0:T(8,128)(2,1)S(1)}, bf16[64,768]{1,0:T(8,128)(2,1)S(1)}, u32[]{:S(2)}, u32[]{:S(2)}) collective-permute-start(bf16[64,768]{1,0:T(8,128)(2,1)S(1)} %get-tuple-element.110), channel_id=1, source_target_pairs={{0,2},{2,0},{4,6},{6,4},{8,10},{10,8},{12,14},{14,12},{1,3},{3,1},... | collective-permute-start | bytes 294920 | tf_op jit(solution)/shard_map/ppermute | solution.py:340

commit v9 on v8

--- a/solution.py
+++ b/solution.py
@@ -26,6 +26,9 @@
     "far_back": 1000000000,
     "weight_gradients": 30000000000,
     "combine_gradients": 30000000000,
+    "order_rest": 30000000000,
+    "order_back": 30000000000,
+    "order_far": 30000000000,
 }
 
 
@@ -270,6 +273,10 @@
         copy.wait()
 
 
+def order_kernel(tiny_ref):
+    tiny_ref[...] = jnp.zeros_like(tiny_ref)
+
+
 def local(tokens, teacher, routes, gate_weights, weights):
     tok, width = tokens.shape
     experts = lax.axis_size("expert")
@@ -287,6 +294,7 @@
     sent_x = jax.ShapeDtypeStruct((across + along, rows, rows), BF16)
     sent_g = jax.ShapeDtypeStruct((across + 2 * along, rows, rows), BF16)
     acts2 = jax.ShapeDtypeStruct((2 * units, rows), BF16)
+    tiny = jax.ShapeDtypeStruct((8, 128), F32)
     vspec = pl.BlockSpec(memory_space=pltpu.VMEM)
     aspec = pl.BlockSpec(memory_space=pl.ANY)
 
@@ -399,10 +407,13 @@
         call(pack_far_kernel, "pack_far", pieces, [], far_meta, far_tokens)
     )
 
-    out_near, (xn, hn, fan, fbn) = forward(x_near, "forward_near")
+    out_near, (xn, hn, fan, fbn) = forward(x_near, "forward_near", after=[x_far[0]])
+    xn_sib = to_sibling(xn)
+    far_here, hn = call(
+        order_kernel, "order_far", [tiny], [], after=x_far[1:], through=[hn]
+    )
     got_near = within_half(out_near)
-    out_far, (xf, hf, faf, fbf) = forward(x_far, "forward_far", after=[xn])
-    rest_rows, *out_far = call(
+    rest_rows = call(
         near_sum_kernel,
         "near_sum",
         dense,
@@ -410,11 +421,14 @@
         meta,
         teacher,
         *got_near,
-        through=out_far,
     )
     rest = to_mirror(rest_rows)
+    out_far, (xf, hf, faf, fbf) = forward(x_far, "forward_far", after=[far_here, xn_sib, rest_rows])
     got_far = within_half(out_far)
-    xf_sib, xn_sib = to_sibling(xf), to_sibling(xn)
+    _, rest, hf = call(
+        order_kernel, "order_rest", [tiny], [], after=[], through=[rest, hf]
+    )
+    xf_sib = to_sibling(xf)
 
     res = call(
         functools.partial(far_grad_kernel, half),
@@ -442,14 +456,16 @@
     student, d_gates_near, rg_near = res[0], res[1], within_half(res[2:])
 
     back_far = within_half(grad_far)
+    gf_sib = to_sibling(gf)
     part_rows = call(
         far_back_kernel, "far_back", longer, [], far_meta, d_gates_far, *back_far
     )
     part = to_mirror(part_rows)
-    grad_near, (gn, dn) = backward(rg_near, fan, fbn, "backward_near", after=[part_rows] + back_far[1:])
-    gf_sib, gn_sib = to_sibling(gf), to_sibling(gn)
+    grad_near, (gn, dn) = backward(rg_near, fan, fbn, "backward_near", after=[part_rows, gf_sib])
+    gn_sib = to_sibling(gn)
     back_near = within_half(grad_near)
 
+    _, part, dn = call(order_kernel, "order_back", [tiny], [], through=[part, dn])
     weight_grads, finished = call(
         functools.partial(weight_kernel, across),
         "weight_gradients",

time: 89.7 us -> 91 us (1.014)
  Pallas kernels: 25 us -> 26.2 us
    pallas_call x12 -> x15, Pallas kernels: 25 us -> 26.2 us  [call(): pl.pallas_call(body, in_specs=specs + [aspec] * (len(after) + len(through...]
    ppermute x24, starting transfers between devices: 30.6 us -> 29.4 us  [within_half(): lax.ppermute(rows_of[s], 'expert', [(i, i ^ s) for i in range(experts)])]
    unnamed x14 -> x18, local copies, waits for them, and re-layouts: 4.63 us -> 5.09 us
  transfers between devices with their start and end apart: 34 -> 34, of which waited for: 13 -> 14; matrix products, arithmetic and copies ran while one was open for 0% -> 0% of each run, Pallas kernels for 26% -> 27%
where the time goes in v9:
time: 91 us; the launch traced here: 90.7 us
  starting transfers between devices  37.4 us (41%)
  Pallas kernels  26.2 us (29%)
  waiting for transfers between devices  21.2 us (23%)
  local copies, waits for them, and re-layouts  5.09 us (6%)
    ppermute x24, starting transfers between devices, within_half(): lax.ppermute(rows_of[s], 'expert', [(i, i ^ s) for i in range(experts)])  29.4 us
    pallas_call x15, Pallas kernels, call(): pl.pallas_call(body, in_specs=specs + [aspec] * (len(after) + len(through...  26.2 us
    ppermute x24, waiting for transfers between devices, within_half(): lax.ppermute(rows_of[s], 'expert', [(i, i ^ s) for i in range(experts)])  17.3 us
    ppermute x5, starting transfers between devices, to_mirror(): return lax.ppermute(x, 'expert', [(i, i ^ half) for i in range(experts)])  7.77 us
    unnamed x18, local copies, waits for them, and re-layouts  5.09 us
    ppermute x5, waiting for transfers between devices, to_mirror(): return lax.ppermute(x, 'expert', [(i, i ^ half) for i in range(experts)])  3.91 us
  transfers between devices with their start and end apart: 34, of which 14 were waited for; matrix products, arithmetic and copies ran while one was open for 0% of the time, Pallas kernels for 27%

profile of v9, /device:TPU:0, one launch (start us, length us, event | category | flops | bytes accessed | tf_op | source)
XLA Modules:
  0.0 90.7 jit_solution(11914495068327377793)
XLA Ops:
  0.6 4.1 %collective-permute-start.5 = (bf16[128,768]{1,0:T(8,128)(2,1)}, bf16[128,768]{1,0:T(8,128)(2,1)S(1)}, u32[]{:S(2)}, u32[]{:S(2)}) collective-permute-start(bf16[128,768]{1,0:T(8,128)(2,1)} %refs_3_.1), channel_id=1, source_target_pairs={{0,8},{2,10},{4,12},{6,14},{8,0},{10,2},{12,4},{14,6},{1,9},{3,11}... | collective-permute-start | bytes 589832 | tf_op jit(solution)/shard_map/ppermute | solution.py:353
  4.7 2.3 %copy-done = bf16[1,1024,3,768]{3,1,2,0:T(8,128)(2,1)S(1)} copy-done((bf16[1,1024,3,768]{3,1,2,0:T(8,128)(2,1)S(1)}, bf16[1,1024,3,768]{3,1,2,0:T(8,128)(2,1)}, u32[]{:S(2)}) %copy-start) | copy-done | bytes 4718616
  7.1 0.9 %copy-done.3 = bf16[128,768]{1,0:T(8,128)(2,1)S(1)} copy-done((bf16[128,768]{1,0:T(8,128)(2,1)S(1)}, bf16[128,768]{1,0:T(8,128)(2,1)}, u32[]{:S(2)}) %copy-start.3) | copy-done | bytes 196632
  8.0 0.7 copy-done.5
  8.7 0.7 copy-done.6
  9.9 2.8 %collective-permute-start.2 = (bf16[64,768]{1,0:T(8,128)(2,1)S(1)}, bf16[64,768]{1,0:T(8,128)(2,1)S(1)}, u32[]{:S(2)}, u32[]{:S(2)}) collective-permute-start(bf16[64,768]{1,0:T(8,128)(2,1)S(1)} %get-tuple-element.65), channel_id=1, source_target_pairs={{0,6},{2,4},{4,2},{6,0},{8,14},{10,12},{12,10},{14,8},{1,7},{3,5},... | collective-permute-start | bytes 294920 | tf_op jit(solution)/shard_map/ppermute | solution.py:348
  13.1 1.2 %collective-permute-done.refs_0_ = f32[8,128]{1,0:T(8,128)S(1)} collective-permute-done((f32[8,128]{1,0:T(8,128)S(1)}, f32[8,128]{1,0:T(8,128)S(1)}, u32[]{:S(2)}, u32[]{:S(2)}) %collective-permute-start) | collective-permute-done | bytes 4128 | tf_op jit(solution)/shard_map/ppermute | solution.py:353
  14.3 1.5 %collective-permute-start.4 = (bf16[64,768]{1,0:T(8,128)(2,1)S(1)}, bf16[64,768]{1,0:T(8,128)(2,1)S(1)}, u32[]{:S(2)}, u32[]{:S(2)}) collective-permute-start(bf16[64,768]{1,0:T(8,128)(2,1)S(1)} %get-tuple-element.67), channel_id=1, source_target_pairs={{0,2},{2,0},{4,6},{6,4},{8,10},{10,8},{12,14},{14,12},{1,3},{3,1},... | collective-permute-start | bytes 294920 | tf_op jit(solution)/shard_map/ppermute | solution.py:348
  16.2 1.6 %collective-permute-start.10 = (bf16[64,768]{1,0:T(8,128)(2,1)S(1)}, bf16[64,768]{1,0:T(8,128)(2,1)S(1)}, u32[]{:S(2)}, u32[]{:S(2)}) collective-permute-start(bf16[64,768]{1,0:T(8,128)(2,1)S(1)} %get-tuple-element.73), channel_id=1, source_target_pairs={{0,6},{2,4},{4,2},{6,0},{8,14},{10,12},{12,10},{14,8},{1,7},{3,5},... | collective-permute-start | bytes 294920 | tf_op jit(solution)/shard_map/ppermute | solution.py:348
  18.4 1.6 %collective-permute-start.12 = (bf16[64,768]{1,0:T(8,128)(2,1)S(1)}, bf16[64,768]{1,0:T(8,128)(2,1)S(1)}, u32[]{:S(2)}, u32[]{:S(2)}) collective-permute-start(bf16[64,768]{1,0:T(8,128)(2,1)S(1)} %get-tuple-element.75), channel_id=1, source_target_pairs={{0,2},{2,0},{4,6},{6,4},{8,10},{10,8},{12,14},{14,12},{1,3},{3,1},... | collective-permute-start | bytes 294920 | tf_op jit(solution)/shard_map/ppermute | solution.py:348
  20.0 3.3 %forward_near.1 = (bf16[64,768]{1,0:T(8,128)(2,1)S(1)}, bf16[64,768]{1,0:T(8,128)(2,1)S(1)}, bf16[64,768]{1,0:T(8,128)(2,1)S(1)}, bf16[64,768]{1,0:T(8,128)(2,1)...) custom-call(bf16[3,1024,768]{2,1,0:T(8,128)(2,1)S(1)} %bitcast.13, ...), custom_call_target="tpu_custom_call" | custom-call | flops 100000000 | bytes 2097152 | tf_op jit(solution)/shard_map/forward_near/pallas_call | solution.py:330
  23.3 4.2 %collective-permute-start.6 = (bf16[64,768]{1,0:T(8,128)(2,1)S(1)}, bf16[64,768]{1,0:T(8,128)(2,1)S(1)}, u32[]{:S(2)}, u32[]{:S(2)}) collective-permute-start(bf16[64,768]{1,0:T(8,128)(2,1)S(1)} %get-tuple-element.70), channel_id=1, source_target_pairs={{0,6},{2,4},{4,2},{6,0},{8,14},{10,12},{12,10},{14,8},{1,7},{3,5},... | collective-permute-start | bytes 294920 | tf_op jit(solution)/shard_map/ppermute | solution.py:348
  27.5 0.6 collective-permute-start.8
  28.2 1.9 %collective-permute-done.6.refs_3_.refs_4_ = bf16[64,768]{1,0:T(8,128)(2,1)S(1)} collective-permute-done((bf16[64,768]{1,0:T(8,128)(2,1)S(1)}, bf16[64,768]{1,0:T(8,128)(2,1)S(1)}, u32[]{:S(2)}, u32[]{:S(2)}) %collective-permute-start.6) | collective-permute-done | bytes 98336 | tf_op jit(solution)/shard_map/ppermute | solution.py:348
  30.1 2.0 %collective-permute-done.7.refs_4_.refs_5_ = bf16[64,768]{1,0:T(8,128)(2,1)S(1)} collective-permute-done((bf16[64,768]{1,0:T(8,128)(2,1)S(1)}, bf16[64,768]{1,0:T(8,128)(2,1)S(1)}, u32[]{:S(2)}, u32[]{:S(2)}) %collective-permute-start.7) | collective-permute-done | bytes 98336 | tf_op jit(solution)/shard_map/ppermute | solution.py:348
  32.7 1.5 %collective-permute-start.9 = (bf16[128,768]{1,0:T(8,128)(2,1)S(1)}, bf16[128,768]{1,0:T(8,128)(2,1)S(1)}, u32[]{:S(2)}, u32[]{:S(2)}) collective-permute-start(bf16[128,768]{1,0:T(8,128)(2,1)S(1)} %near_sum.1.refs_8_), channel_id=1, source_target_pairs={{0,8},{2,10},{4,12},{6,14},{8,0},{10,2},{12,4},{14,6},{1,9},{3,11}... | collective-permute-start | bytes 589832 | tf_op jit(solution)/shard_map/ppermute | solution.py:353
  34.2 3.3 %forward_far.1 = (bf16[64,768]{1,0:T(8,128)(2,1)S(1)}, bf16[64,768]{1,0:T(8,128)(2,1)S(1)}, bf16[64,768]{1,0:T(8,128)(2,1)S(1)}, bf16[64,768]{1,0:T(8,128)(2,1)S...) custom-call(bf16[3,1024,768]{2,1,0:T(8,128)(2,1)S(1)} %bitcast.14, ...), custom_call_target="tpu_custom_call" | custom-call | flops 3000000000 | bytes 2097152 | tf_op jit(solution)/shard_map/forward_far/pallas_call | solution.py:330
  37.6 2.0 %collective-permute-start.14 = (bf16[64,768]{1,0:T(8,128)(2,1)S(1)}, bf16[64,768]{1,0:T(8,128)(2,1)S(1)}, u32[]{:S(2)}, u32[]{:S(2)}) collective-permute-start(bf16[64,768]{1,0:T(8,128)(2,1)S(1)} %get-tuple-element.82), channel_id=1, source_target_pairs={{0,6},{2,4},{4,2},{6,0},{8,14},{10,12},{12,10},{14,8},{1,7},{3,5},... | collective-permute-start | bytes 294920 | tf_op jit(solution)/shard_map/ppermute | solution.py:348
  39.8 1.4 %collective-permute-start.16 = (bf16[64,768]{1,0:T(8,128)(2,1)S(1)}, bf16[64,768]{1,0:T(8,128)(2,1)S(1)}, u32[]{:S(2)}, u32[]{:S(2)}) collective-permute-start(bf16[64,768]{1,0:T(8,128)(2,1)S(1)} %get-tuple-element.84), channel_id=1, source_target_pairs={{0,2},{2,0},{4,6},{6,4},{8,10},{10,8},{12,14},{14,12},{1,3},{3,1},... | collective-permute-start | bytes 294920 | tf_op jit(solution)/shard_map/ppermute | solution.py:348
  41.2 1.2 %collective-permute-done.9.refs_0_ = bf16[128,768]{1,0:T(8,128)(2,1)S(1)} collective-permute-done((bf16[128,768]{1,0:T(8,128)(2,1)S(1)}, bf16[128,768]{1,0:T(8,128)(2,1)S(1)}, u32[]{:S(2)}, u32[]{:S(2)}) %collective-permute-start.9) | collective-permute-done | bytes 196640 | tf_op jit(solution)/shard_map/ppermute | solution.py:353
  42.4 0.6 order_rest.1
  43.0 2.3 %collective-permute-done.14.refs_3_ = bf16[64,768]{1,0:T(8,128)(2,1)S(1)} collective-permute-done((bf16[64,768]{1,0:T(8,128)(2,1)S(1)}, bf16[64,768]{1,0:T(8,128)(2,1)S(1)}, u32[]{:S(2)}, u32[]{:S(2)}) %collective-permute-start.14) | collective-permute-done | bytes 98336 | tf_op jit(solution)/shard_map/ppermute | solution.py:348
  45.3 1.2 %collective-permute-done.15.refs_4_ = bf16[64,768]{1,0:T(8,128)(2,1)S(1)} collective-permute-done((bf16[64,768]{1,0:T(8,128)(2,1)S(1)}, bf16[64,768]{1,0:T(8,128)(2,1)S(1)}, u32[]{:S(2)}, u32[]{:S(2)}) %collective-permute-start.15) | collective-permute-done | bytes 98336 | tf_op jit(solution)/shard_map/ppermute | solution.py:348
  46.6 0.8 far_grad.1
  47.4 1.3 %collective-permute-start.19 = (bf16[64,768]{1,0:T(8,128)(2,1)S(1)}, bf16[64,768]{1,0:T(8,128)(2,1)S(1)}, u32[]{:S(2)}, u32[]{:S(2)}) collective-permute-start(bf16[64,768]{1,0:T(8,128)(2,1)S(1)} %get-tuple-element.90), channel_id=1, source_target_pairs={{0,6},{2,4},{4,2},{6,0},{8,14},{10,12},{12,10},{14,8},{1,7},{3,5},... | collective-permute-start | bytes 294920 | tf_op jit(solution)/shard_map/ppermute | solution.py:348
  48.7 1.6 %collective-permute-start.20 = (bf16[64,768]{1,0:T(8,128)(2,1)S(1)}, bf16[64,768]{1,0:T(8,128)(2,1)S(1)}, u32[]{:S(2)}, u32[]{:S(2)}) collective-permute-start(bf16[64,768]{1,0:T(8,128)(2,1)S(1)} %get-tuple-element.91), channel_id=1, source_target_pairs={{0,4},{2,6},{4,0},{6,2},{8,12},{10,14},{12,8},{14,10},{1,5},{3,7},... | collective-permute-start | bytes 294920 | tf_op jit(solution)/shard_map/ppermute | solution.py:348
  50.3 0.6 collective-permute-start.21
  50.9 1.4 %collective-permute-start.18 = (bf16[128,768]{1,0:T(8,128)(2,1)S(1)}, bf16[128,768]{1,0:T(8,128)(2,1)S(1)}, u32[]{:S(2)}, u32[]{:S(2)}) collective-permute-start(bf16[128,768]{1,0:T(8,128)(2,1)S(1)} %get-tuple-element.86), channel_id=1, source_target_pairs={{0,8},{2,10},{4,12},{6,14},{8,0},{10,2},{12,4},{14,6},{1,9},{3,11}... | collective-permute-start | bytes 589832 | tf_op jit(solution)/shard_map/ppermute | solution.py:353
  52.4 1.6 %collective-permute-done.19.refs_5_ = bf16[64,768]{1,0:T(8,128)(2,1)S(1)} collective-permute-done((bf16[64,768]{1,0:T(8,128)(2,1)S(1)}, bf16[64,768]{1,0:T(8,128)(2,1)S(1)}, u32[]{:S(2)}, u32[]{:S(2)}) %collective-permute-start.19) | collective-permute-done | bytes 98336 | tf_op jit(solution)/shard_map/ppermute | solution.py:348
  54.0 3.1 %collective-permute-done.20.refs_6_ = bf16[64,768]{1,0:T(8,128)(2,1)S(1)} collective-permute-done((bf16[64,768]{1,0:T(8,128)(2,1)S(1)}, bf16[64,768]{1,0:T(8,128)(2,1)S(1)}, u32[]{:S(2)}, u32[]{:S(2)}) %collective-permute-start.20) | collective-permute-done | bytes 98336 | tf_op jit(solution)/shard_map/ppermute | solution.py:348
  57.1 3.7 %backward_far.1 = (bf16[64,768]{1,0:T(8,128)(2,1)S(1)}, bf16[64,768]{1,0:T(8,128)(2,1)S(1)}, bf16[64,768]{1,0:T(8,128)(2,1)S(1)}, bf16[64,768]{1,0:T(8,128)(2,1)...) custom-call(bf16[3,1024,768]{2,1,0:T(8,128)(2,1)S(1)} %bitcast.15, ...), custom_call_target="tpu_custom_call" | custom-call | flops 3000000000 | bytes 2097152 | tf_op jit(solution)/shard_map/backward_far/pallas_call | solution.py:330
  61.2 1.8 %collective-permute-start.23 = (bf16[64,768]{1,0:T(8,128)(2,1)S(1)}, bf16[64,768]{1,0:T(8,128)(2,1)S(1)}, u32[]{:S(2)}, u32[]{:S(2)}) collective-permute-start(bf16[64,768]{1,0:T(8,128)(2,1)S(1)} %get-tuple-element.98), channel_id=1, source_target_pairs={{0,4},{2,6},{4,0},{6,2},{8,12},{10,14},{12,8},{14,10},{1,5},{3,7},... | collective-permute-start | bytes 294920 | tf_op jit(solution)/shard_map/ppermute | solution.py:348
  63.0 1.5 %collective-permute-start.24 = (bf16[64,768]{1,0:T(8,128)(2,1)S(1)}, bf16[64,768]{1,0:T(8,128)(2,1)S(1)}, u32[]{:S(2)}, u32[]{:S(2)}) collective-permute-start(bf16[64,768]{1,0:T(8,128)(2,1)S(1)} %get-tuple-element.99), channel_id=1, source_target_pairs={{0,2},{2,0},{4,6},{6,4},{8,10},{10,8},{12,14},{14,12},{1,3},{3,1},... | collective-permute-start | bytes 294920 | tf_op jit(solution)/shard_map/ppermute | solution.py:348
  64.5 1.2 %near_grad.1 = (bf16[128,768]{1,0:T(8,128)(2,1)}, f32[2,128]{1,0:T(2,128)S(1)}, bf16[64,768]{1,0:T(8,128)(2,1)S(1)}, bf16[64,768]{1,0:T(8,128)(2,1)S(1)}, bf16[6...) custom-call(f32[8,128]{1,0:T(8,128)S(1)} %get-tuple-element.63.refs_0_, bf16[128,768]{1,0:T(8,128)(2,1)S(1)} %copy-done.4, ...), custom_call_target="tpu_custom_call" | custom-call | flops 30000001024 | bytes 2097152 | tf_op jit(solution)/shard_map/near_grad/pallas_call | solution.py:330
  66.0 1.5 %collective-permute-done.22.refs_3_ = bf16[64,768]{1,0:T(8,128)(2,1)S(1)} collective-permute-done((bf16[64,768]{1,0:T(8,128)(2,1)S(1)}, bf16[64,768]{1,0:T(8,128)(2,1)S(1)}, u32[]{:S(2)}, u32[]{:S(2)}) %collective-permute-start.22) | collective-permute-done | bytes 98336 | tf_op jit(solution)/shard_map/ppermute | solution.py:348
  67.7 0.7 collective-permute-done.23.refs_4_
  68.5 1.5 %collective-permute-start.28 = (bf16[64,768]{1,0:T(8,128)(2,1)S(1)}, bf16[64,768]{1,0:T(8,128)(2,1)S(1)}, u32[]{:S(2)}, u32[]{:S(2)}) collective-permute-start(bf16[64,768]{1,0:T(8,128)(2,1)S(1)} %get-tuple-element.105), channel_id=1, source_target_pairs={{0,2},{2,0},{4,6},{6,4},{8,10},{10,8},{12,14},{14,12},{1,3},{3,1},... | collective-permute-start | bytes 294920 | tf_op jit(solution)/shard_map/ppermute | solution.py:348
  70.3 0.5 collective-permute-start.25
  70.9 1.5 %collective-permute-done.26.refs_5_ = bf16[64,768]{1,0:T(8,128)(2,1)S(1)} collective-permute-done((bf16[64,768]{1,0:T(8,128)(2,1)S(1)}, bf16[64,768]{1,0:T(8,128)(2,1)S(1)}, u32[]{:S(2)}, u32[]{:S(2)}) %collective-permute-start.26) | collective-permute-done | bytes 98336 | tf_op jit(solution)/shard_map/ppermute | solution.py:348
  72.4 1.1 %collective-permute-done.28.refs_7_ = bf16[64,768]{1,0:T(8,128)(2,1)S(1)} collective-permute-done((bf16[64,768]{1,0:T(8,128)(2,1)S(1)}, bf16[64,768]{1,0:T(8,128)(2,1)S(1)}, u32[]{:S(2)}, u32[]{:S(2)}) %collective-permute-start.28) | collective-permute-done | bytes 98336 | tf_op jit(solution)/shard_map/ppermute | solution.py:348
  73.5 3.7 %backward_near.1 = (bf16[64,768]{1,0:T(8,128)(2,1)S(1)}, bf16[64,768]{1,0:T(8,128)(2,1)S(1)}, bf16[64,768]{1,0:T(8,128)(2,1)S(1)}, bf16[64,768]{1,0:T(8,128)(2,1...) custom-call(bf16[3,1024,768]{2,1,0:T(8,128)(2,1)S(1)} %bitcast.16, ...), custom_call_target="tpu_custom_call" | custom-call | flops 10000000000 | bytes 2097152 | tf_op jit(solution)/shard_map/backward_near/pallas_call | solution.py:330
  77.3 0.7 collective-permute-start.30
  77.9 1.9 %collective-permute-start.31 = (bf16[64,768]{1,0:T(8,128)(2,1)S(1)}, bf16[64,768]{1,0:T(8,128)(2,1)S(1)}, u32[]{:S(2)}, u32[]{:S(2)}) collective-permute-start(bf16[64,768]{1,0:T(8,128)(2,1)S(1)} %get-tuple-element.112), channel_id=1, source_target_pairs={{0,4},{2,6},{4,0},{6,2},{8,12},{10,14},{12,8},{14,10},{1,5},{3,7},... | collective-permute-start | bytes 294920 | tf_op jit(solution)/shard_map/ppermute | solution.py:348
  79.9 1.0 %collective-permute-start.32 = (bf16[64,768]{1,0:T(8,128)(2,1)S(1)}, bf16[64,768]{1,0:T(8,128)(2,1)S(1)}, u32[]{:S(2)}, u32[]{:S(2)}) collective-permute-start(bf16[64,768]{1,0:T(8,128)(2,1)S(1)} %get-tuple-element.113), channel_id=1, source_target_pairs={{0,2},{2,0},{4,6},{6,4},{8,10},{10,8},{12,14},{14,12},{1,3},{3,1},... | collective-permute-start | bytes 294920 | tf_op jit(solution)/shard_map/ppermute | solution.py:348
  80.8 1.5 %collective-permute-done.25.refs_0_ = bf16[144,768]{1,0:T(8,128)(2,1)S(1)} collective-permute-done((bf16[144,768]{1,0:T(8,128)(2,1)S(1)}, bf16[144,768]{1,0:T(8,128)(2,1)S(1)}, u32[]{:S(2)}, u32[]{:S(2)}) %collective-permute-start.25) | collective-permute-done | bytes 221216 | tf_op jit(solution)/shard_map/ppermute | solution.py:353
  82.3 0.6 order_back.1
  83.4 6.3 %weight_gradients.1 = (bf16[3,1024,768]{2,1,0:T(8,128)(2,1)}, f32[8,128]{1,0:T(8,128)S(1)}) custom-call(bf16[7,256,256]{2,1,0:T(8,128)(2,1)S(1)} %get-tuple-element.85.refs_0_, bf16[7,256,256]{2,1,0:T(8,128)(2,1)S(1)} %get-tuple-element.78.refs_1_, bf16[7,256,256]{2,1,0:T(8,128)(2,1)S(1)} %collective-permute-done.17.refs_6_.refs_2_, ...), custom_call_target="tpu_custom_call" | custom-call | flops 30000001024 | bytes 2097152 | tf_op jit(solution)/shard_map/weight_gradients/pallas_call | solution.py:330
  89.7 1.1 %combine_gradients.1 = (bf16[128,768]{1,0:T(8,128)(2,1)}, f32[2,128]{1,0:T(2,128)}) custom-call(f32[8,128]{1,0:T(8,128)S(1)} %get-tuple-element.63.refs_0_, bf16[144,768]{1,0:T(8,128)(2,1)S(1)} %get-tuple-element.108.refs_1_, f32[2,128]{1,0:T(2,128)S(1)} %get-tuple-element.109.refs_2_, bf16[64,768]{1,0:T(8,128)(2,1)S(1)} %get-tuple-element.110.refs_3_, ...), custom_call_target="tpu_custom_call" | custom-call | flops 30000001024 | bytes 2097152 | tf_op jit(solution)/shard_map/combine_gradients/pallas_call | solution.py:330
  (54 shorter events, 4.5 us)
Async XLA Ops:
  0.6 15.2 %collective-permute-start.5 = (bf16[128,768]{1,0:T(8,128)(2,1)}, bf16[128,768]{1,0:T(8,128)(2,1)S(1)}, u32[]{:S(2)}, u32[]{:S(2)}) collective-permute-start(bf16[128,768]{1,0:T(8,128)(2,1)} %refs_3_.1), channel_id=1, source_target_pairs={{0,8},{2,10},{4,12},{6,14},{8,0},{10,2},{12,4},{14,6},{1,9},{3,11}... | collective-permute-start | bytes 589832 | tf_op jit(solution)/shard_map/ppermute | solution.py:353
  4.7 15.2 %collective-permute-start.1 = (bf16[3,1024,768]{2,1,0:T(8,128)(2,1)}, bf16[3,1024,768]{2,1,0:T(8,128)(2,1)S(1)}, u32[]{:S(2)}, u32[]{:S(2)}) collective-permute-start(bf16[3,1024,768]{2,1,0:T(8,128)(2,1)} %bitcast.9), channel_id=1, source_target_pairs={{0,1},{1,0},{2,3},{3,2},{4,5},{5,4},{6,7},{7,6},{8,9},{9,8},{10,11... | collective-permute-start | bytes 14155784 | tf_op jit(solution)/shard_map/ppermute | solution.py:356
  4.7 2.3 %copy-start = (bf16[1,1024,3,768]{3,1,2,0:T(8,128)(2,1)S(1)}, bf16[1,1024,3,768]{3,1,2,0:T(8,128)(2,1)}, u32[]{:S(2)}) copy-start(bf16[1,1024,3,768]{3,1,2,0:T(8,128)(2,1)} %param.9) | copy-start | bytes 14155780
  7.1 0.9 %copy-start.3 = (bf16[128,768]{1,0:T(8,128)(2,1)S(1)}, bf16[128,768]{1,0:T(8,128)(2,1)}, u32[]{:S(2)}) copy-start(bf16[128,768]{1,0:T(8,128)(2,1)} %refs_3_.1) | copy-start | bytes 589828
  8.0 0.7 copy-start.5
  8.7 0.7 copy-start.6
  9.7 4.6 %collective-permute-start = (f32[8,128]{1,0:T(8,128)S(1)}, f32[8,128]{1,0:T(8,128)S(1)}, u32[]{:S(2)}, u32[]{:S(2)}) collective-permute-start(f32[8,128]{1,0:T(8,128)S(1)} %get-tuple-element.63.refs_0_), channel_id=1, source_target_pairs={{0,8},{2,10},{4,12},{6,14},{8,0},{10,2},{12,4},{14,6},{1,9},{3,11}... | collective-permute-start | bytes 12296 | tf_op jit(solution)/shard_map/ppermute | solution.py:353
  9.9 7.9 %collective-permute-start.2 = (bf16[64,768]{1,0:T(8,128)(2,1)S(1)}, bf16[64,768]{1,0:T(8,128)(2,1)S(1)}, u32[]{:S(2)}, u32[]{:S(2)}) collective-permute-start(bf16[64,768]{1,0:T(8,128)(2,1)S(1)} %get-tuple-element.65), channel_id=1, source_target_pairs={{0,6},{2,4},{4,2},{6,0},{8,14},{10,12},{12,10},{14,8},{1,7},{3,5},... | collective-permute-start | bytes 294920 | tf_op jit(solution)/shard_map/ppermute | solution.py:348
  12.7 5.7 %collective-permute-start.3 = (bf16[64,768]{1,0:T(8,128)(2,1)S(1)}, bf16[64,768]{1,0:T(8,128)(2,1)S(1)}, u32[]{:S(2)}, u32[]{:S(2)}) collective-permute-start(bf16[64,768]{1,0:T(8,128)(2,1)S(1)} %get-tuple-element.66), channel_id=1, source_target_pairs={{0,4},{2,6},{4,0},{6,2},{8,12},{10,14},{12,8},{14,10},{1,5},{3,7},... | collective-permute-start | bytes 294920 | tf_op jit(solution)/shard_map/ppermute | solution.py:348
  14.3 5.7 %slice-start = ((s8[4718592]{0:T(1024)(128)(4,1)}), s8[4194304]{0:T(1024)(128)(4,1)S(1)}, s32[]{:S(2)}) async-start(s8[4718592]{0:T(1024)(128)(4,1)} %bitcast.11), calls=%async_computation | async-start | bytes 8388608
  14.3 5.7 %slice-start.1 = ((s8[4718592]{0:T(1024)(128)(4,1)}), s8[524288]{0:T(1024)(128)(4,1)S(1)}, s32[]{:S(2)}) async-start(s8[4718592]{0:T(1024)(128)(4,1)} %bitcast.11), calls=%async_computation.1 | async-start | bytes 1048576
  14.3 5.7 %collective-permute-start.4 = (bf16[64,768]{1,0:T(8,128)(2,1)S(1)}, bf16[64,768]{1,0:T(8,128)(2,1)S(1)}, u32[]{:S(2)}, u32[]{:S(2)}) collective-permute-start(bf16[64,768]{1,0:T(8,128)(2,1)S(1)} %get-tuple-element.67), channel_id=1, source_target_pairs={{0,2},{2,0},{4,6},{6,4},{8,10},{10,8},{12,14},{14,12},{1,3},{3,1},... | collective-permute-start | bytes 294920 | tf_op jit(solution)/shard_map/ppermute | solution.py:348
  16.2 11.3 %collective-permute-start.10 = (bf16[64,768]{1,0:T(8,128)(2,1)S(1)}, bf16[64,768]{1,0:T(8,128)(2,1)S(1)}, u32[]{:S(2)}, u32[]{:S(2)}) collective-permute-start(bf16[64,768]{1,0:T(8,128)(2,1)S(1)} %get-tuple-element.73), channel_id=1, source_target_pairs={{0,6},{2,4},{4,2},{6,0},{8,14},{10,12},{12,10},{14,8},{1,7},{3,5},... | collective-permute-start | bytes 294920 | tf_op jit(solution)/shard_map/ppermute | solution.py:348
  17.8 10.4 %collective-permute-start.11 = (bf16[64,768]{1,0:T(8,128)(2,1)S(1)}, bf16[64,768]{1,0:T(8,128)(2,1)S(1)}, u32[]{:S(2)}, u32[]{:S(2)}) collective-permute-start(bf16[64,768]{1,0:T(8,128)(2,1)S(1)} %get-tuple-element.74), channel_id=1, source_target_pairs={{0,4},{2,6},{4,0},{6,2},{8,12},{10,14},{12,8},{14,10},{1,5},{3,7},... | collective-permute-start | bytes 294920 | tf_op jit(solution)/shard_map/ppermute | solution.py:348
  18.4 9.8 %collective-permute-start.12 = (bf16[64,768]{1,0:T(8,128)(2,1)S(1)}, bf16[64,768]{1,0:T(8,128)(2,1)S(1)}, u32[]{:S(2)}, u32[]{:S(2)}) collective-permute-start(bf16[64,768]{1,0:T(8,128)(2,1)S(1)} %get-tuple-element.75), channel_id=1, source_target_pairs={{0,2},{2,0},{4,6},{6,4},{8,10},{10,8},{12,14},{14,12},{1,3},{3,1},... | collective-permute-start | bytes 294920 | tf_op jit(solution)/shard_map/ppermute | solution.py:348
  23.3 6.8 %collective-permute-start.6 = (bf16[64,768]{1,0:T(8,128)(2,1)S(1)}, bf16[64,768]{1,0:T(8,128)(2,1)S(1)}, u32[]{:S(2)}, u32[]{:S(2)}) collective-permute-start(bf16[64,768]{1,0:T(8,128)(2,1)S(1)} %get-tuple-element.70), channel_id=1, source_target_pairs={{0,6},{2,4},{4,2},{6,0},{8,14},{10,12},{12,10},{14,8},{1,7},{3,5},... | collective-permute-start | bytes 294920 | tf_op jit(solution)/shard_map/ppermute | solution.py:348
  27.5 4.6 %collective-permute-start.7 = (bf16[64,768]{1,0:T(8,128)(2,1)S(1)}, bf16[64,768]{1,0:T(8,128)(2,1)S(1)}, u32[]{:S(2)}, u32[]{:S(2)}) collective-permute-start(bf16[64,768]{1,0:T(8,128)(2,1)S(1)} %get-tuple-element.71), channel_id=1, source_target_pairs={{0,4},{2,6},{4,0},{6,2},{8,12},{10,14},{12,8},{14,10},{1,5},{3,7},... | collective-permute-start | bytes 294920 | tf_op jit(solution)/shard_map/ppermute | solution.py:348
  27.5 4.6 %collective-permute-start.8 = (bf16[64,768]{1,0:T(8,128)(2,1)S(1)}, bf16[64,768]{1,0:T(8,128)(2,1)S(1)}, u32[]{:S(2)}, u32[]{:S(2)}) collective-permute-start(bf16[64,768]{1,0:T(8,128)(2,1)S(1)} %get-tuple-element.72), channel_id=1, source_target_pairs={{0,2},{2,0},{4,6},{6,4},{8,10},{10,8},{12,14},{14,12},{1,3},{3,1},... | collective-permute-start | bytes 294920 | tf_op jit(solution)/shard_map/ppermute | solution.py:348
  28.2 6.0 %collective-permute-start.13 = (bf16[7,256,256]{2,1,0:T(8,128)(2,1)S(1)}, bf16[7,256,256]{2,1,0:T(8,128)(2,1)S(1)}, u32[]{:S(2)}, u32[]{:S(2)}) collective-permute-start(bf16[7,256,256]{2,1,0:T(8,128)(2,1)S(1)} %get-tuple-element.78.refs_1_), channel_id=1, source_target_pairs={{0,1},{1,0},{2,3},{3,2},{4,5},{5,4},{6,7},{7,6},{8,9},{9,8},{10,11... | collective-permute-start | bytes 2752520 | tf_op jit(solution)/shard_map/ppermute | solution.py:356
  28.2 4.0 %copy-start.4 = (bf16[128,768]{1,0:T(8,128)(2,1)S(1)}, bf16[128,768]{1,0:T(8,128)(2,1)}, u32[]{:S(2)}) copy-start(bf16[128,768]{1,0:T(8,128)(2,1)} %refs_1_.3) | copy-start | bytes 589828
  28.2 4.4 %copy-start.1 = (bf16[1024,256]{1,0:T(8,128)(2,1)}, bf16[1024,256]{1,0:T(8,128)(2,1)S(1)}, u32[]{:S(2)}) copy-start(bf16[1024,256]{1,0:T(8,128)(2,1)S(1)} %get-tuple-element.117.refs_11_) | copy-start | bytes 1572868
  32.7 9.7 %collective-permute-start.9 = (bf16[128,768]{1,0:T(8,128)(2,1)S(1)}, bf16[128,768]{1,0:T(8,128)(2,1)S(1)}, u32[]{:S(2)}, u32[]{:S(2)}) collective-permute-start(bf16[128,768]{1,0:T(8,128)(2,1)S(1)} %near_sum.1.refs_8_), channel_id=1, source_target_pairs={{0,8},{2,10},{4,12},{6,14},{8,0},{10,2},{12,4},{14,6},{1,9},{3,11}... | collective-permute-start | bytes 589832 | tf_op jit(solution)/shard_map/ppermute | solution.py:353
  37.5 9.1 %collective-permute-start.17 = (bf16[7,256,256]{2,1,0:T(8,128)(2,1)S(1)}, bf16[7,256,256]{2,1,0:T(8,128)(2,1)S(1)}, u32[]{:S(2)}, u32[]{:S(2)}) collective-permute-start(bf16[7,256,256]{2,1,0:T(8,128)(2,1)S(1)} %get-tuple-element.85.refs_0_), channel_id=1, source_target_pairs={{0,1},{1,0},{2,3},{3,2},{4,5},{5,4},{6,7},{7,6},{8,9},{9,8},{10,11... | collective-permute-start | bytes 2752520 | tf_op jit(solution)/shard_map/ppermute | solution.py:356
  37.6 7.7 %collective-permute-start.14 = (bf16[64,768]{1,0:T(8,128)(2,1)S(1)}, bf16[64,768]{1,0:T(8,128)(2,1)S(1)}, u32[]{:S(2)}, u32[]{:S(2)}) collective-permute-start(bf16[64,768]{1,0:T(8,128)(2,1)S(1)} %get-tuple-element.82), channel_id=1, source_target_pairs={{0,6},{2,4},{4,2},{6,0},{8,14},{10,12},{12,10},{14,8},{1,7},{3,5},... | collective-permute-start | bytes 294920 | tf_op jit(solution)/shard_map/ppermute | solution.py:348
  39.6 6.9 %collective-permute-start.15 = (bf16[64,768]{1,0:T(8,128)(2,1)S(1)}, bf16[64,768]{1,0:T(8,128)(2,1)S(1)}, u32[]{:S(2)}, u32[]{:S(2)}) collective-permute-start(bf16[64,768]{1,0:T(8,128)(2,1)S(1)} %get-tuple-element.83), channel_id=1, source_target_pairs={{0,4},{2,6},{4,0},{6,2},{8,12},{10,14},{12,8},{14,10},{1,5},{3,7},... | collective-permute-start | bytes 294920 | tf_op jit(solution)/shard_map/ppermute | solution.py:348
  39.8 6.8 %collective-permute-start.16 = (bf16[64,768]{1,0:T(8,128)(2,1)S(1)}, bf16[64,768]{1,0:T(8,128)(2,1)S(1)}, u32[]{:S(2)}, u32[]{:S(2)}) collective-permute-start(bf16[64,768]{1,0:T(8,128)(2,1)S(1)} %get-tuple-element.84), channel_id=1, source_target_pairs={{0,2},{2,0},{4,6},{6,4},{8,10},{10,8},{12,14},{14,12},{1,3},{3,1},... | collective-permute-start | bytes 294920 | tf_op jit(solution)/shard_map/ppermute | solution.py:348
  47.4 6.6 %collective-permute-start.19 = (bf16[64,768]{1,0:T(8,128)(2,1)S(1)}, bf16[64,768]{1,0:T(8,128)(2,1)S(1)}, u32[]{:S(2)}, u32[]{:S(2)}) collective-permute-start(bf16[64,768]{1,0:T(8,128)(2,1)S(1)} %get-tuple-element.90), channel_id=1, source_target_pairs={{0,6},{2,4},{4,2},{6,0},{8,14},{10,12},{12,10},{14,8},{1,7},{3,5},... | collective-permute-start | bytes 294920 | tf_op jit(solution)/shard_map/ppermute | solution.py:348
  48.7 8.4 %collective-permute-start.20 = (bf16[64,768]{1,0:T(8,128)(2,1)S(1)}, bf16[64,768]{1,0:T(8,128)(2,1)S(1)}, u32[]{:S(2)}, u32[]{:S(2)}) collective-permute-start(bf16[64,768]{1,0:T(8,128)(2,1)S(1)} %get-tuple-element.91), channel_id=1, source_target_pairs={{0,4},{2,6},{4,0},{6,2},{8,12},{10,14},{12,8},{14,10},{1,5},{3,7},... | collective-permute-start | bytes 294920 | tf_op jit(solution)/shard_map/ppermute | solution.py:348
  50.3 6.8 %collective-permute-start.21 = (bf16[64,768]{1,0:T(8,128)(2,1)S(1)}, bf16[64,768]{1,0:T(8,128)(2,1)S(1)}, u32[]{:S(2)}, u32[]{:S(2)}) collective-permute-start(bf16[64,768]{1,0:T(8,128)(2,1)S(1)} %get-tuple-element.92), channel_id=1, source_target_pairs={{0,2},{2,0},{4,6},{6,4},{8,10},{10,8},{12,14},{14,12},{1,3},{3,1},... | collective-permute-start | bytes 294920 | tf_op jit(solution)/shard_map/ppermute | solution.py:348
  50.9 13.5 %collective-permute-start.18 = (bf16[128,768]{1,0:T(8,128)(2,1)S(1)}, bf16[128,768]{1,0:T(8,128)(2,1)S(1)}, u32[]{:S(2)}, u32[]{:S(2)}) collective-permute-start(bf16[128,768]{1,0:T(8,128)(2,1)S(1)} %get-tuple-element.86), channel_id=1, source_target_pairs={{0,8},{2,10},{4,12},{6,14},{8,0},{10,2},{12,4},{14,6},{1,9},{3,11}... | collective-permute-start | bytes 589832 | tf_op jit(solution)/shard_map/ppermute | solution.py:353
  60.8 12.7 %collective-permute-start.29 = (bf16[11,256,256]{2,1,0:T(8,128)(2,1)S(1)}, bf16[11,256,256]{2,1,0:T(8,128)(2,1)S(1)}, u32[]{:S(2)}, u32[]{:S(2)}) collective-permute-start(bf16[11,256,256]{2,1,0:T(8,128)(2,1)S(1)} %get-tuple-element.106.refs_4_), channel_id=1, source_target_pairs={{0,1},{1,0},{2,3},{3,2},{4,5},{5,4},{6,7},{7,6},{8,9},{9,8},{10,11... | collective-permute-start | bytes 4325384 | tf_op jit(solution)/shard_map/ppermute | solution.py:356
  60.9 6.6 %collective-permute-start.22 = (bf16[64,768]{1,0:T(8,128)(2,1)S(1)}, bf16[64,768]{1,0:T(8,128)(2,1)S(1)}, u32[]{:S(2)}, u32[]{:S(2)}) collective-permute-start(bf16[64,768]{1,0:T(8,128)(2,1)S(1)} %get-tuple-element.97), channel_id=1, source_target_pairs={{0,6},{2,4},{4,2},{6,0},{8,14},{10,12},{12,10},{14,8},{1,7},{3,5},... | collective-permute-start | bytes 294920 | tf_op jit(solution)/shard_map/ppermute | solution.py:348
  61.2 7.2 %collective-permute-start.23 = (bf16[64,768]{1,0:T(8,128)(2,1)S(1)}, bf16[64,768]{1,0:T(8,128)(2,1)S(1)}, u32[]{:S(2)}, u32[]{:S(2)}) collective-permute-start(bf16[64,768]{1,0:T(8,128)(2,1)S(1)} %get-tuple-element.98), channel_id=1, source_target_pairs={{0,4},{2,6},{4,0},{6,2},{8,12},{10,14},{12,8},{14,10},{1,5},{3,7},... | collective-permute-start | bytes 294920 | tf_op jit(solution)/shard_map/ppermute | solution.py:348
  63.0 7.0 %collective-permute-start.24 = (bf16[64,768]{1,0:T(8,128)(2,1)S(1)}, bf16[64,768]{1,0:T(8,128)(2,1)S(1)}, u32[]{:S(2)}, u32[]{:S(2)}) collective-permute-start(bf16[64,768]{1,0:T(8,128)(2,1)S(1)} %get-tuple-element.99), channel_id=1, source_target_pairs={{0,2},{2,0},{4,6},{6,4},{8,10},{10,8},{12,14},{14,12},{1,3},{3,1},... | collective-permute-start | bytes 294920 | tf_op jit(solution)/shard_map/ppermute | solution.py:348
  65.7 6.7 %collective-permute-start.26 = (bf16[64,768]{1,0:T(8,128)(2,1)S(1)}, bf16[64,768]{1,0:T(8,128)(2,1)S(1)}, u32[]{:S(2)}, u32[]{:S(2)}) collective-permute-start(bf16[64,768]{1,0:T(8,128)(2,1)S(1)} %get-tuple-element.103), channel_id=1, source_target_pairs={{0,6},{2,4},{4,2},{6,0},{8,14},{10,12},{12,10},{14,8},{1,7},{3,5},... | collective-permute-start | bytes 294920 | tf_op jit(solution)/shard_map/ppermute | solution.py:348
  67.5 5.0 %collective-permute-start.27 = (bf16[64,768]{1,0:T(8,128)(2,1)S(1)}, bf16[64,768]{1,0:T(8,128)(2,1)S(1)}, u32[]{:S(2)}, u32[]{:S(2)}) collective-permute-start(bf16[64,768]{1,0:T(8,128)(2,1)S(1)} %get-tuple-element.104), channel_id=1, source_target_pairs={{0,4},{2,6},{4,0},{6,2},{8,12},{10,14},{12,8},{14,10},{1,5},{3,7},... | collective-permute-start | bytes 294920 | tf_op jit(solution)/shard_map/ppermute | solution.py:348
  68.5 5.0 %collective-permute-start.28 = (bf16[64,768]{1,0:T(8,128)(2,1)S(1)}, bf16[64,768]{1,0:T(8,128)(2,1)S(1)}, u32[]{:S(2)}, u32[]{:S(2)}) collective-permute-start(bf16[64,768]{1,0:T(8,128)(2,1)S(1)} %get-tuple-element.105), channel_id=1, source_target_pairs={{0,2},{2,0},{4,6},{6,4},{8,10},{10,8},{12,14},{14,12},{1,3},{3,1},... | collective-permute-start | bytes 294920 | tf_op jit(solution)/shard_map/ppermute | solution.py:348
  70.3 12.0 %collective-permute-start.25 = (bf16[144,768]{1,0:T(8,128)(2,1)S(1)}, bf16[144,768]{1,0:T(8,128)(2,1)S(1)}, u32[]{:S(2)}, u32[]{:S(2)}) collective-permute-start(bf16[144,768]{1,0:T(8,128)(2,1)S(1)} %far_back.1.refs_8_), channel_id=1, source_target_pairs={{0,8},{2,10},{4,12},{6,14},{8,0},{10,2},{12,4},{14,6},{1,9},{3,11}... | collective-permute-start | bytes 663560 | tf_op jit(solution)/shard_map/ppermute | solution.py:353
  77.2 5.7 %collective-permute-start.33 = (bf16[11,256,256]{2,1,0:T(8,128)(2,1)S(1)}, bf16[11,256,256]{2,1,0:T(8,128)(2,1)S(1)}, u32[]{:S(2)}, u32[]{:S(2)}) collective-permute-start(bf16[11,256,256]{2,1,0:T(8,128)(2,1)S(1)} %get-tuple-element.114.refs_5_), channel_id=1, source_target_pairs={{0,1},{1,0},{2,3},{3,2},{4,5},{5,4},{6,7},{7,6},{8,9},{9,8},{10,11... | collective-permute-start | bytes 4325384 | tf_op jit(solution)/shard_map/ppermute | solution.py:356
  77.3 12.4 %collective-permute-start.30 = (bf16[64,768]{1,0:T(8,128)(2,1)S(1)}, bf16[64,768]{1,0:T(8,128)(2,1)S(1)}, u32[]{:S(2)}, u32[]{:S(2)}) collective-permute-start(bf16[64,768]{1,0:T(8,128)(2,1)S(1)} %get-tuple-element.111), channel_id=1, source_target_pairs={{0,6},{2,4},{4,2},{6,0},{8,14},{10,12},{12,10},{14,8},{1,7},{3,5},... | collective-permute-start | bytes 294920 | tf_op jit(solution)/shard_map/ppermute | solution.py:348
  77.9 11.7 %collective-permute-start.31 = (bf16[64,768]{1,0:T(8,128)(2,1)S(1)}, bf16[64,768]{1,0:T(8,128)(2,1)S(1)}, u32[]{:S(2)}, u32[]{:S(2)}) collective-permute-start(bf16[64,768]{1,0:T(8,128)(2,1)S(1)} %get-tuple-element.112), channel_id=1, source_target_pairs={{0,4},{2,6},{4,0},{6,2},{8,12},{10,14},{12,8},{14,10},{1,5},{3,7},... | collective-permute-start | bytes 294920 | tf_op jit(solution)/shard_map/ppermute | solution.py:348
  79.9 9.8 %collective-permute-start.32 = (bf16[64,768]{1,0:T(8,128)(2,1)S(1)}, bf16[64,768]{1,0:T(8,128)(2,1)S(1)}, u32[]{:S(2)}, u32[]{:S(2)}) collective-permute-start(bf16[64,768]{1,0:T(8,128)(2,1)S(1)} %get-tuple-element.113), channel_id=1, source_target_pairs={{0,2},{2,0},{4,6},{6,4},{8,10},{10,8},{12,14},{14,12},{1,3},{3,1},... | collective-permute-start | bytes 294920 | tf_op jit(solution)/shard_map/ppermute | solution.py:348
  82.3 1.0 %copy-start.2 = (bf16[1024,256]{1,0:T(8,128)(2,1)S(1)}, bf16[1024,256]{1,0:T(8,128)(2,1)}, u32[]{:S(2)}) copy-start(bf16[1024,256]{1,0:T(8,128)(2,1)} %copy-done.1) | copy-start | bytes 1572868

commit v10 on v8

--- a/solution.py
+++ b/solution.py
@@ -23,9 +23,13 @@
     "near_grad": 30000000000,
     "backward_far": 3000000000,
     "backward_near": 10000000000,
-    "far_back": 1000000000,
-    "weight_gradients": 30000000000,
+    "far_back": 10000000000,
+    "weight_near": 30000000000,
     "combine_gradients": 30000000000,
+    "order_rest": 30000000000,
+    "order_back": 30000000000,
+    "order_far": 30000000000,
+    "weight_far": 2400000000,
 }
 
 
@@ -235,39 +239,50 @@
     d_gates_ref[...] = near_ref[...] + (far[0:2] + far[2:4])
 
 
-def weight_kernel(across, *refs):
-    (xf, xn, xfs, xns, gf, gn, gfs, gns, df, dn, hf, hn, out_hbm, finished, buf, sems) = refs
-    finished[...] = jnp.zeros_like(finished)
-    units = hf.shape[0]
-    side = hf.shape[1]
+def weight_blocks(across, x, sent_x, g, sent_g, d, h):
+    units, side = h.shape
 
     def acts(own, sent, first):
         blocks = range(across + first // side, across + (first + units) // side)
-        theirs = [jnp.concatenate([r[i] for i in blocks], axis=0) for r in sent]
-        return jnp.concatenate([r[first : first + units, :] for r in own] + theirs, axis=1)
-
-    x, rg = (xf, xn, xfs, xns), (gf, gn, gfs, gns)
+        theirs = jnp.concatenate([sent[i] for i in blocks], axis=0)
+        return jnp.concatenate([own[first : first + units, :], theirs], axis=1)
+
+    for row, own, sent, rows, first in (
+        (2, h, sent_x, (g, sent_g), 0),
+        (0, d, sent_g, (x, sent_x), 0),
+        (1, d, sent_g, (x, sent_x), units),
+    ):
+        for i in range(across):
+            column = jnp.concatenate([r[i] for r in rows], axis=0)
+            yield row, i, dot(acts(own, sent, first), column)
+
+
+def weight_far_kernel(across, x, sent_x, g, sent_g, d, h, out_ref, tiny_ref):
+    tiny_ref[...] = jnp.zeros_like(tiny_ref)
+    side = h.shape[1]
+    for row, i, value in weight_blocks(across, x, sent_x, g, sent_g, d, h):
+        out_ref[row, :, i * side : (i + 1) * side] = value.astype(BF16)
+
+
+def weight_near_kernel(
+    across, far_ref, x, sent_x, g, sent_g, d, h, out_hbm, tiny_ref, buf, sems
+):
+    tiny_ref[...] = jnp.zeros_like(tiny_ref)
+    side = h.shape[1]
     copies = []
-    for m, (own, sent, rows, first) in enumerate(
-        (
-            ((hf, hn), (xfs, xns), rg, 0),
-            ((df, dn), (gfs, gns), x, 0),
-            ((df, dn), (gfs, gns), x, units),
+    for row, i, value in weight_blocks(across, x, sent_x, g, sent_g, d, h):
+        at = pl.ds(i * side, side)
+        buf[row, :, at] = (value + far_ref[row, :, at].astype(F32)).astype(BF16)
+        copies.append(
+            pltpu.make_async_copy(buf.at[row, :, at], out_hbm.at[row, :, at], sems.at[row, i])
         )
-    ):
-        row = (m + 2) % 3
-        for i in range(across):
-            at = pl.ds(i * side, side)
-            column = jnp.concatenate([r[i] for r in rows], axis=0)
-            buf[row, :, at] = dot(acts(own, sent, first), column).astype(BF16)
-            copies.append(
-                pltpu.make_async_copy(
-                    buf.at[row, :, at], out_hbm.at[row, :, at], sems.at[row, i]
-                )
-            )
-            copies[-1].start()
+        copies[-1].start()
     for copy in copies:
         copy.wait()
+
+
+def order_kernel():
+    pass
 
 
 def local(tokens, teacher, routes, gate_weights, weights):
@@ -287,6 +302,7 @@
     sent_x = jax.ShapeDtypeStruct((across + along, rows, rows), BF16)
     sent_g = jax.ShapeDtypeStruct((across + 2 * along, rows, rows), BF16)
     acts2 = jax.ShapeDtypeStruct((2 * units, rows), BF16)
+    tiny = jax.ShapeDtypeStruct((8, 128), F32)
     vspec = pl.BlockSpec(memory_space=pltpu.VMEM)
     aspec = pl.BlockSpec(memory_space=pl.ANY)
 
@@ -442,26 +458,31 @@
     student, d_gates_near, rg_near = res[0], res[1], within_half(res[2:])
 
     back_far = within_half(grad_far)
+    gf_sib = to_sibling(gf)
+    far_weights, far_done = call(
+        functools.partial(weight_far_kernel, across),
+        "weight_far",
+        [jax.ShapeDtypeStruct((3, units, width), BF16), tiny],
+        [],
+        *(xf, xf_sib, gf, gf_sib, df, hf),
+        after=[back_far[1]],
+        limit=16,
+    )
     part_rows = call(
-        far_back_kernel, "far_back", longer, [], far_meta, d_gates_far, *back_far
+        far_back_kernel, "far_back", longer, [], far_meta, d_gates_far, *back_far, after=[far_done]
     )
     part = to_mirror(part_rows)
-    grad_near, (gn, dn) = backward(rg_near, fan, fbn, "backward_near", after=[part_rows] + back_far[1:])
-    gf_sib, gn_sib = to_sibling(gf), to_sibling(gn)
+    grad_near, (gn, dn) = backward(rg_near, fan, fbn, "backward_near", after=[part_rows, gf_sib, far_done])
+    gn_sib = to_sibling(gn)
     back_near = within_half(grad_near)
 
+    part, dn = call(order_kernel, "order_back", [], [], through=[part, dn])
     weight_grads, finished = call(
-        functools.partial(weight_kernel, across),
-        "weight_gradients",
-        [
-            jax.ShapeDtypeStruct((3, units, width), BF16),
-            jax.ShapeDtypeStruct((8, 128), F32),
-        ],
-        [],
-        *(xf, xn, xf_sib, xn_sib),
-        *(gf, gn, gf_sib, gn_sib),
-        *(df, dn, hf, hn),
-        after=[],
+        functools.partial(weight_near_kernel, across),
+        "weight_near",
+        [jax.ShapeDtypeStruct((3, units, width), BF16), tiny],
+        [],
+        *(far_weights, xn, xn_sib, gn, gn_sib, dn, hn),
         limit=24,
         scratch=[
             pltpu.VMEM((3, units, width), BF16),

time: 89.7 us -> 88.4 us (0.986)
  waiting for transfers between devices: 20.8 us -> 17.6 us
  starting transfers between devices: 38.3 us -> 39.6 us
    ppermute x24, waiting for transfers between devices: 16.8 us -> 10.3 us  [within_half(): lax.ppermute(rows_of[s], 'expert', [(i, i ^ s) for i in range(experts)])]
    ppermute x5, waiting for transfers between devices: 3.98 us -> 7.28 us  [to_mirror(): return lax.ppermute(x, 'expert', [(i, i ^ half) for i in range(experts)])]
    ppermute x5, starting transfers between devices: 7.03 us -> 9.73 us  [to_mirror(): return lax.ppermute(x, 'expert', [(i, i ^ half) for i in range(experts)])]
    ppermute x24, starting transfers between devices: 30.6 us -> 28.6 us  [within_half(): lax.ppermute(rows_of[s], 'expert', [(i, i ^ s) for i in range(experts)])]
    pallas_call x12 -> x14, Pallas kernels: 25 us -> 25.5 us  [call(): pl.pallas_call(body, in_specs=specs + [aspec] * (len(after) + len(through...]
  transfers between devices with their start and end apart: 34 -> 34, of which waited for: 13 -> 10; matrix products, arithmetic and copies ran while one was open for 0% -> 0% of each run, Pallas kernels for 26% -> 27%
where the time goes in v10:
time: 88.4 us; the launch traced here: 88.2 us
  starting transfers between devices  39.6 us (45%)
  Pallas kernels  25.5 us (29%)
  waiting for transfers between devices  17.6 us (20%)
  local copies, waits for them, and re-layouts  4.63 us (5%)
    ppermute x24, starting transfers between devices, within_half(): lax.ppermute(rows_of[s], 'expert', [(i, i ^ s) for i in range(experts)])  28.6 us
    pallas_call x14, Pallas kernels, call(): pl.pallas_call(body, in_specs=specs + [aspec] * (len(after) + len(through...  25.5 us
    ppermute x24, waiting for transfers between devices, within_half(): lax.ppermute(rows_of[s], 'expert', [(i, i ^ s) for i in range(experts)])  10.3 us
    ppermute x5, starting transfers between devices, to_mirror(): return lax.ppermute(x, 'expert', [(i, i ^ half) for i in range(experts)])  9.73 us
    ppermute x5, waiting for transfers between devices, to_mirror(): return lax.ppermute(x, 'expert', [(i, i ^ half) for i in range(experts)])  7.28 us
    unnamed x14, local copies, waits for them, and re-layouts  4.63 us
  transfers between devices with their start and end apart: 34, of which 10 were waited for; matrix products, arithmetic and copies ran while one was open for 0% of the time, Pallas kernels for 27%

profile of v10, /device:TPU:0, one launch (start us, length us, event | category | flops | bytes accessed | tf_op | source)
XLA Modules:
  0.0 88.2 jit_solution(5968167207360762014)
XLA Ops:
  0.6 0.5 collective-permute-start.1
  1.1 3.7 %collective-permute-start.8 = (bf16[128,768]{1,0:T(8,128)(2,1)}, bf16[128,768]{1,0:T(8,128)(2,1)S(1)}, u32[]{:S(2)}, u32[]{:S(2)}) collective-permute-start(bf16[128,768]{1,0:T(8,128)(2,1)} %refs_3_.1), channel_id=1, source_target_pairs={{0,8},{2,10},{4,12},{6,14},{8,0},{10,2},{12,4},{14,6},{1,9},{3,11}... | collective-permute-start | bytes 589832 | tf_op jit(solution)/shard_map/ppermute | solution.py:361
  4.8 2.3 %copy-done = bf16[1,1024,3,768]{3,1,2,0:T(8,128)(2,1)S(1)} copy-done((bf16[1,1024,3,768]{3,1,2,0:T(8,128)(2,1)S(1)}, bf16[1,1024,3,768]{3,1,2,0:T(8,128)(2,1)}, u32[]{:S(2)}) %copy-start) | copy-done | bytes 4718616
  7.2 0.9 %copy-done.1 = bf16[128,768]{1,0:T(8,128)(2,1)S(1)} copy-done((bf16[128,768]{1,0:T(8,128)(2,1)S(1)}, bf16[128,768]{1,0:T(8,128)(2,1)}, u32[]{:S(2)}) %copy-start.1) | copy-done | bytes 196632
  8.1 0.7 copy-done.3
  8.8 0.7 copy-done.4
  9.9 2.9 %collective-permute-start.2 = (bf16[64,768]{1,0:T(8,128)(2,1)S(1)}, bf16[64,768]{1,0:T(8,128)(2,1)S(1)}, u32[]{:S(2)}, u32[]{:S(2)}) collective-permute-start(bf16[64,768]{1,0:T(8,128)(2,1)S(1)} %get-tuple-element.68), channel_id=1, source_target_pairs={{0,6},{2,4},{4,2},{6,0},{8,14},{10,12},{12,10},{14,8},{1,7},{3,5},... | collective-permute-start | bytes 294920 | tf_op jit(solution)/shard_map/ppermute | solution.py:356
  12.8 0.5 collective-permute-start.3
  13.2 1.7 %collective-permute-done.refs_0_ = f32[8,128]{1,0:T(8,128)S(1)} collective-permute-done((f32[8,128]{1,0:T(8,128)S(1)}, f32[8,128]{1,0:T(8,128)S(1)}, u32[]{:S(2)}, u32[]{:S(2)}) %collective-permute-start) | collective-permute-done | bytes 4128 | tf_op jit(solution)/shard_map/ppermute | solution.py:361
  14.9 1.6 %collective-permute-start.4 = (bf16[64,768]{1,0:T(8,128)(2,1)S(1)}, bf16[64,768]{1,0:T(8,128)(2,1)S(1)}, u32[]{:S(2)}, u32[]{:S(2)}) collective-permute-start(bf16[64,768]{1,0:T(8,128)(2,1)S(1)} %get-tuple-element.70), channel_id=1, source_target_pairs={{0,2},{2,0},{4,6},{6,4},{8,10},{10,8},{12,14},{14,12},{1,3},{3,1},... | collective-permute-start | bytes 294920 | tf_op jit(solution)/shard_map/ppermute | solution.py:356
  16.9 1.0 %collective-permute-start.10 = (bf16[64,768]{1,0:T(8,128)(2,1)S(1)}, bf16[64,768]{1,0:T(8,128)(2,1)S(1)}, u32[]{:S(2)}, u32[]{:S(2)}) collective-permute-start(bf16[64,768]{1,0:T(8,128)(2,1)S(1)} %get-tuple-element.77), channel_id=1, source_target_pairs={{0,4},{2,6},{4,0},{6,2},{8,12},{10,14},{12,8},{14,10},{1,5},{3,7},... | collective-permute-start | bytes 294920 | tf_op jit(solution)/shard_map/ppermute | solution.py:356
  18.0 0.5 collective-permute-start.11
  18.5 0.6 collective-permute-done.3.refs_4_
  19.1 1.3 %collective-permute-start.9 = (bf16[64,768]{1,0:T(8,128)(2,1)S(1)}, bf16[64,768]{1,0:T(8,128)(2,1)S(1)}, u32[]{:S(2)}, u32[]{:S(2)}) collective-permute-start(bf16[64,768]{1,0:T(8,128)(2,1)S(1)} %get-tuple-element.76), channel_id=1, source_target_pairs={{0,6},{2,4},{4,2},{6,0},{8,14},{10,12},{12,10},{14,8},{1,7},{3,5},... | collective-permute-start | bytes 294920 | tf_op jit(solution)/shard_map/ppermute | solution.py:356
  20.5 3.4 %forward_near.1 = (bf16[64,768]{1,0:T(8,128)(2,1)S(1)}, bf16[64,768]{1,0:T(8,128)(2,1)S(1)}, bf16[64,768]{1,0:T(8,128)(2,1)S(1)}, bf16[64,768]{1,0:T(8,128)(2,1)...) custom-call(bf16[3,1024,768]{2,1,0:T(8,128)(2,1)S(1)} %bitcast.13, ...), custom_call_target="tpu_custom_call" | custom-call | flops 100000000 | bytes 2097152 | tf_op jit(solution)/shard_map/forward_near/pallas_call | solution.py:338
  23.9 2.0 %collective-permute-start.5 = (bf16[64,768]{1,0:T(8,128)(2,1)S(1)}, bf16[64,768]{1,0:T(8,128)(2,1)S(1)}, u32[]{:S(2)}, u32[]{:S(2)}) collective-permute-start(bf16[64,768]{1,0:T(8,128)(2,1)S(1)} %get-tuple-element.72), channel_id=1, source_target_pairs={{0,6},{2,4},{4,2},{6,0},{8,14},{10,12},{12,10},{14,8},{1,7},{3,5},... | collective-permute-start | bytes 294920 | tf_op jit(solution)/shard_map/ppermute | solution.py:356
  26.3 1.1 %collective-permute-start.7 = (bf16[64,768]{1,0:T(8,128)(2,1)S(1)}, bf16[64,768]{1,0:T(8,128)(2,1)S(1)}, u32[]{:S(2)}, u32[]{:S(2)}) collective-permute-start(bf16[64,768]{1,0:T(8,128)(2,1)S(1)} %get-tuple-element.74), channel_id=1, source_target_pairs={{0,2},{2,0},{4,6},{6,4},{8,10},{10,8},{12,14},{14,12},{1,3},{3,1},... | collective-permute-start | bytes 294920 | tf_op jit(solution)/shard_map/ppermute | solution.py:356
  27.5 3.4 %forward_far.1 = (bf16[64,768]{1,0:T(8,128)(2,1)S(1)}, bf16[64,768]{1,0:T(8,128)(2,1)S(1)}, bf16[64,768]{1,0:T(8,128)(2,1)S(1)}, bf16[64,768]{1,0:T(8,128)(2,1)S...) custom-call(bf16[3,1024,768]{2,1,0:T(8,128)(2,1)S(1)} %bitcast.14, ...), custom_call_target="tpu_custom_call" | custom-call | flops 3000000000 | bytes 2097152 | tf_op jit(solution)/shard_map/forward_far/pallas_call | solution.py:338
  30.9 0.6 collective-permute-start.16
  31.5 0.5 near_sum.1
  32.0 2.1 %collective-permute-start.13 = (bf16[64,768]{1,0:T(8,128)(2,1)S(1)}, bf16[64,768]{1,0:T(8,128)(2,1)S(1)}, u32[]{:S(2)}, u32[]{:S(2)}) collective-permute-start(bf16[64,768]{1,0:T(8,128)(2,1)S(1)} %get-tuple-element.86), channel_id=1, source_target_pairs={{0,6},{2,4},{4,2},{6,0},{8,14},{10,12},{12,10},{14,8},{1,7},{3,5},... | collective-permute-start | bytes 294920 | tf_op jit(solution)/shard_map/ppermute | solution.py:356
  34.0 2.5 %collective-permute-start.12 = (bf16[128,768]{1,0:T(8,128)(2,1)S(1)}, bf16[128,768]{1,0:T(8,128)(2,1)S(1)}, u32[]{:S(2)}, u32[]{:S(2)}) collective-permute-start(bf16[128,768]{1,0:T(8,128)(2,1)S(1)} %get-tuple-element.84), channel_id=1, source_target_pairs={{0,8},{2,10},{4,12},{6,14},{8,0},{10,2},{12,4},{14,6},{1,9},{3,11}... | collective-permute-start | bytes 589832 | tf_op jit(solution)/shard_map/ppermute | solution.py:361
  36.5 1.5 %collective-permute-start.14 = (bf16[64,768]{1,0:T(8,128)(2,1)S(1)}, bf16[64,768]{1,0:T(8,128)(2,1)S(1)}, u32[]{:S(2)}, u32[]{:S(2)}) collective-permute-start(bf16[64,768]{1,0:T(8,128)(2,1)S(1)} %get-tuple-element.87), channel_id=1, source_target_pairs={{0,4},{2,6},{4,0},{6,2},{8,12},{10,14},{12,8},{14,10},{1,5},{3,7},... | collective-permute-start | bytes 294920 | tf_op jit(solution)/shard_map/ppermute | solution.py:356
  38.0 1.3 %collective-permute-start.15 = (bf16[64,768]{1,0:T(8,128)(2,1)S(1)}, bf16[64,768]{1,0:T(8,128)(2,1)S(1)}, u32[]{:S(2)}, u32[]{:S(2)}) collective-permute-start(bf16[64,768]{1,0:T(8,128)(2,1)S(1)} %get-tuple-element.88), channel_id=1, source_target_pairs={{0,2},{2,0},{4,6},{6,4},{8,10},{10,8},{12,14},{14,12},{1,3},{3,1},... | collective-permute-start | bytes 294920 | tf_op jit(solution)/shard_map/ppermute | solution.py:356
  39.3 3.4 %collective-permute-done.14.refs_4_ = bf16[64,768]{1,0:T(8,128)(2,1)S(1)} collective-permute-done((bf16[64,768]{1,0:T(8,128)(2,1)S(1)}, bf16[64,768]{1,0:T(8,128)(2,1)S(1)}, u32[]{:S(2)}, u32[]{:S(2)}) %collective-permute-start.14) | collective-permute-done | bytes 98336 | tf_op jit(solution)/shard_map/ppermute | solution.py:356
  42.7 2.9 %collective-permute-done.12.refs_1_ = bf16[128,768]{1,0:T(8,128)(2,1)S(1)} collective-permute-done((bf16[128,768]{1,0:T(8,128)(2,1)S(1)}, bf16[128,768]{1,0:T(8,128)(2,1)S(1)}, u32[]{:S(2)}, u32[]{:S(2)}) %collective-permute-start.12) | collective-permute-done | bytes 196640 | tf_op jit(solution)/shard_map/ppermute | solution.py:361
  45.7 0.8 far_grad.1
  46.5 1.2 %collective-permute-start.19 = (bf16[64,768]{1,0:T(8,128)(2,1)S(1)}, bf16[64,768]{1,0:T(8,128)(2,1)S(1)}, u32[]{:S(2)}, u32[]{:S(2)}) collective-permute-start(bf16[64,768]{1,0:T(8,128)(2,1)S(1)} %get-tuple-element.94), channel_id=1, source_target_pairs={{0,6},{2,4},{4,2},{6,0},{8,14},{10,12},{12,10},{14,8},{1,7},{3,5},... | collective-permute-start | bytes 294920 | tf_op jit(solution)/shard_map/ppermute | solution.py:356
  47.7 1.5 %collective-permute-start.20 = (bf16[64,768]{1,0:T(8,128)(2,1)S(1)}, bf16[64,768]{1,0:T(8,128)(2,1)S(1)}, u32[]{:S(2)}, u32[]{:S(2)}) collective-permute-start(bf16[64,768]{1,0:T(8,128)(2,1)S(1)} %get-tuple-element.95), channel_id=1, source_target_pairs={{0,4},{2,6},{4,0},{6,2},{8,12},{10,14},{12,8},{14,10},{1,5},{3,7},... | collective-permute-start | bytes 294920 | tf_op jit(solution)/shard_map/ppermute | solution.py:356
  49.2 0.8 collective-permute-start.21
  50.0 1.7 %collective-permute-start.18 = (bf16[128,768]{1,0:T(8,128)(2,1)S(1)}, bf16[128,768]{1,0:T(8,128)(2,1)S(1)}, u32[]{:S(2)}, u32[]{:S(2)}) collective-permute-start(bf16[128,768]{1,0:T(8,128)(2,1)S(1)} %get-tuple-element.90), channel_id=1, source_target_pairs={{0,8},{2,10},{4,12},{6,14},{8,0},{10,2},{12,4},{14,6},{1,9},{3,11}... | collective-permute-start | bytes 589832 | tf_op jit(solution)/shard_map/ppermute | solution.py:361
  51.7 0.4 collective-permute-done.19.refs_5_
  52.1 3.8 %collective-permute-done.20.refs_6_ = bf16[64,768]{1,0:T(8,128)(2,1)S(1)} collective-permute-done((bf16[64,768]{1,0:T(8,128)(2,1)S(1)}, bf16[64,768]{1,0:T(8,128)(2,1)S(1)}, u32[]{:S(2)}, u32[]{:S(2)}) %collective-permute-start.20) | collective-permute-done | bytes 98336 | tf_op jit(solution)/shard_map/ppermute | solution.py:356
  55.9 3.8 %backward_far.1 = (bf16[64,768]{1,0:T(8,128)(2,1)S(1)}, bf16[64,768]{1,0:T(8,128)(2,1)S(1)}, bf16[64,768]{1,0:T(8,128)(2,1)S(1)}, bf16[64,768]{1,0:T(8,128)(2,1)...) custom-call(bf16[3,1024,768]{2,1,0:T(8,128)(2,1)S(1)} %bitcast.15, ...), custom_call_target="tpu_custom_call" | custom-call | flops 3000000000 | bytes 2097152 | tf_op jit(solution)/shard_map/backward_far/pallas_call | solution.py:338
  59.8 1.4 %collective-permute-start.23 = (bf16[64,768]{1,0:T(8,128)(2,1)S(1)}, bf16[64,768]{1,0:T(8,128)(2,1)S(1)}, u32[]{:S(2)}, u32[]{:S(2)}) collective-permute-start(bf16[64,768]{1,0:T(8,128)(2,1)S(1)} %get-tuple-element.102), channel_id=1, source_target_pairs={{0,4},{2,6},{4,0},{6,2},{8,12},{10,14},{12,8},{14,10},{1,5},{3,7},... | collective-permute-start | bytes 294920 | tf_op jit(solution)/shard_map/ppermute | solution.py:356
  61.2 2.1 %collective-permute-start.24 = (bf16[64,768]{1,0:T(8,128)(2,1)S(1)}, bf16[64,768]{1,0:T(8,128)(2,1)S(1)}, u32[]{:S(2)}, u32[]{:S(2)}) collective-permute-start(bf16[64,768]{1,0:T(8,128)(2,1)S(1)} %get-tuple-element.103), channel_id=1, source_target_pairs={{0,2},{2,0},{4,6},{6,4},{8,10},{10,8},{12,14},{14,12},{1,3},{3,1},... | collective-permute-start | bytes 294920 | tf_op jit(solution)/shard_map/ppermute | solution.py:356
  63.3 1.2 %near_grad.1 = (bf16[128,768]{1,0:T(8,128)(2,1)}, f32[2,128]{1,0:T(2,128)S(1)}, bf16[64,768]{1,0:T(8,128)(2,1)S(1)}, bf16[64,768]{1,0:T(8,128)(2,1)S(1)}, bf16[6...) custom-call(f32[8,128]{1,0:T(8,128)S(1)} %get-tuple-element.66.refs_0_, bf16[128,768]{1,0:T(8,128)(2,1)S(1)} %copy-done.2, ...), custom_call_target="tpu_custom_call" | custom-call | flops 30000001024 | bytes 2097152 | tf_op jit(solution)/shard_map/near_grad/pallas_call | solution.py:338
  64.6 1.7 %collective-permute-done.22.refs_6_.refs_3_ = bf16[64,768]{1,0:T(8,128)(2,1)S(1)} collective-permute-done((bf16[64,768]{1,0:T(8,128)(2,1)S(1)}, bf16[64,768]{1,0:T(8,128)(2,1)S(1)}, u32[]{:S(2)}, u32[]{:S(2)}) %collective-permute-start.22) | collective-permute-done | bytes 98336 | tf_op jit(solution)/shard_map/ppermute | solution.py:356
  66.3 1.7 %collective-permute-start.29 = (bf16[64,768]{1,0:T(8,128)(2,1)S(1)}, bf16[64,768]{1,0:T(8,128)(2,1)S(1)}, u32[]{:S(2)}, u32[]{:S(2)}) collective-permute-start(bf16[64,768]{1,0:T(8,128)(2,1)S(1)} %get-tuple-element.112), channel_id=1, source_target_pairs={{0,2},{2,0},{4,6},{6,4},{8,10},{10,8},{12,14},{14,12},{1,3},{3,1},... | collective-permute-start | bytes 294920 | tf_op jit(solution)/shard_map/ppermute | solution.py:356
  68.0 2.6 %weight_far.1 = (bf16[3,1024,768]{2,1,0:T(8,128)(2,1)S(1)}, f32[8,128]{1,0:T(8,128)S(1)}) custom-call(bf16[7,256,256]{2,1,0:T(8,128)(2,1)S(1)} %get-tuple-element.89.refs_0_, bf16[7,256,256]{2,1,0:T(8,128)(2,1)S(1)} %collective-permute-done.16.refs_6_.refs_1_, bf16[11,256,256]{2,1,0:T(8,128)(2,1)S(1)} %get-tuple-element.104.refs_2_, ...), custom_call_target="tpu_custom_call" | custom-call | flops 2400000000 | bytes 2097152 | tf_op jit(solution)/shard_map/weight_far/pallas_call | solution.py:338
  71.1 1.8 %collective-permute-start.26 = (bf16[144,768]{1,0:T(8,128)(2,1)S(1)}, bf16[144,768]{1,0:T(8,128)(2,1)S(1)}, u32[]{:S(2)}, u32[]{:S(2)}) collective-permute-start(bf16[144,768]{1,0:T(8,128)(2,1)S(1)} %far_back.1.refs_8_), channel_id=1, source_target_pairs={{0,8},{2,10},{4,12},{6,14},{8,0},{10,2},{12,4},{14,6},{1,9},{3,11}... | collective-permute-start | bytes 663560 | tf_op jit(solution)/shard_map/ppermute | solution.py:361
  72.9 3.8 %backward_near.1 = (bf16[64,768]{1,0:T(8,128)(2,1)S(1)}, bf16[64,768]{1,0:T(8,128)(2,1)S(1)}, bf16[64,768]{1,0:T(8,128)(2,1)S(1)}, bf16[64,768]{1,0:T(8,128)(2,1...) custom-call(bf16[3,1024,768]{2,1,0:T(8,128)(2,1)S(1)} %bitcast.16, ...), custom_call_target="tpu_custom_call" | custom-call | flops 10000000000 | bytes 2097152 | tf_op jit(solution)/shard_map/backward_near/pallas_call | solution.py:338
  76.7 1.2 %collective-permute-start.30 = (bf16[64,768]{1,0:T(8,128)(2,1)S(1)}, bf16[64,768]{1,0:T(8,128)(2,1)S(1)}, u32[]{:S(2)}, u32[]{:S(2)}) collective-permute-start(bf16[64,768]{1,0:T(8,128)(2,1)S(1)} %get-tuple-element.117), channel_id=1, source_target_pairs={{0,6},{2,4},{4,2},{6,0},{8,14},{10,12},{12,10},{14,8},{1,7},{3,5},... | collective-permute-start | bytes 294920 | tf_op jit(solution)/shard_map/ppermute | solution.py:356
  78.0 1.7 %collective-permute-start.31 = (bf16[64,768]{1,0:T(8,128)(2,1)S(1)}, bf16[64,768]{1,0:T(8,128)(2,1)S(1)}, u32[]{:S(2)}, u32[]{:S(2)}) collective-permute-start(bf16[64,768]{1,0:T(8,128)(2,1)S(1)} %get-tuple-element.118), channel_id=1, source_target_pairs={{0,4},{2,6},{4,0},{6,2},{8,12},{10,14},{12,8},{14,10},{1,5},{3,7},... | collective-permute-start | bytes 294920 | tf_op jit(solution)/shard_map/ppermute | solution.py:356
  79.7 0.6 collective-permute-start.32
  80.3 2.7 %collective-permute-done.26.refs_0_ = bf16[144,768]{1,0:T(8,128)(2,1)S(1)} collective-permute-done((bf16[144,768]{1,0:T(8,128)(2,1)S(1)}, bf16[144,768]{1,0:T(8,128)(2,1)S(1)}, u32[]{:S(2)}, u32[]{:S(2)}) %collective-permute-start.26) | collective-permute-done | bytes 221216 | tf_op jit(solution)/shard_map/ppermute | solution.py:361
  82.9 3.9 %weight_near.1 = (bf16[3,1024,768]{2,1,0:T(8,128)(2,1)}, f32[8,128]{1,0:T(8,128)S(1)}) custom-call(bf16[3,1024,768]{2,1,0:T(8,128)(2,1)S(1)} %get-tuple-element.120.refs_0_, bf16[7,256,256]{2,1,0:T(8,128)(2,1)S(1)} %get-tuple-element.79.refs_6_.refs_1_, bf16[7,256,256]{2,1,0:T(8,128)(2,1)S(1)} %collective-permute-done.17.refs_7_.refs_2_, ...), custom_call_target="tpu_custom_call" | custom-call | flops 30000001024 | bytes 2097152 | tf_op jit(solution)/shard_map/weight_near/pallas_call | solution.py:338
  87.1 1.1 %combine_gradients.1 = (bf16[128,768]{1,0:T(8,128)(2,1)}, f32[2,128]{1,0:T(2,128)}) custom-call(f32[8,128]{1,0:T(8,128)S(1)} %get-tuple-element.66.refs_0_, bf16[144,768]{1,0:T(8,128)(2,1)S(1)} %get-tuple-element.114.refs_1_, f32[2,128]{1,0:T(2,128)S(1)} %get-tuple-element.115.refs_2_, bf16[64,768]{1,0:T(8,128)(2,1)S(1)} %get-tuple-element.116.refs_3_, ...), custom_call_target="tpu_custom_call" | custom-call | flops 30000001024 | bytes 2097152 | tf_op jit(solution)/shard_map/combine_gradients/pallas_call | solution.py:338
  (49 shorter events, 2.3 us)
Async XLA Ops:
  0.6 19.8 %collective-permute-start.1 = (bf16[3,1024,768]{2,1,0:T(8,128)(2,1)}, bf16[3,1024,768]{2,1,0:T(8,128)(2,1)S(1)}, u32[]{:S(2)}, u32[]{:S(2)}) collective-permute-start(bf16[3,1024,768]{2,1,0:T(8,128)(2,1)} %bitcast.9), channel_id=1, source_target_pairs={{0,1},{1,0},{2,3},{3,2},{4,5},{5,4},{6,7},{7,6},{8,9},{9,8},{10,11... | collective-permute-start | bytes 14155784 | tf_op jit(solution)/shard_map/ppermute | solution.py:364
  1.1 15.4 %collective-permute-start.8 = (bf16[128,768]{1,0:T(8,128)(2,1)}, bf16[128,768]{1,0:T(8,128)(2,1)S(1)}, u32[]{:S(2)}, u32[]{:S(2)}) collective-permute-start(bf16[128,768]{1,0:T(8,128)(2,1)} %refs_3_.1), channel_id=1, source_target_pairs={{0,8},{2,10},{4,12},{6,14},{8,0},{10,2},{12,4},{14,6},{1,9},{3,11}... | collective-permute-start | bytes 589832 | tf_op jit(solution)/shard_map/ppermute | solution.py:361
  4.8 2.3 %copy-start = (bf16[1,1024,3,768]{3,1,2,0:T(8,128)(2,1)S(1)}, bf16[1,1024,3,768]{3,1,2,0:T(8,128)(2,1)}, u32[]{:S(2)}) copy-start(bf16[1,1024,3,768]{3,1,2,0:T(8,128)(2,1)} %param.9) | copy-start | bytes 14155780
  7.2 0.9 %copy-start.1 = (bf16[128,768]{1,0:T(8,128)(2,1)S(1)}, bf16[128,768]{1,0:T(8,128)(2,1)}, u32[]{:S(2)}) copy-start(bf16[128,768]{1,0:T(8,128)(2,1)} %refs_3_.1) | copy-start | bytes 589828
  8.1 0.7 copy-start.3
  8.8 0.7 copy-start.4
  9.8 5.1 %collective-permute-start = (f32[8,128]{1,0:T(8,128)S(1)}, f32[8,128]{1,0:T(8,128)S(1)}, u32[]{:S(2)}, u32[]{:S(2)}) collective-permute-start(f32[8,128]{1,0:T(8,128)S(1)} %get-tuple-element.66.refs_0_), channel_id=1, source_target_pairs={{0,8},{2,10},{4,12},{6,14},{8,0},{10,2},{12,4},{14,6},{1,9},{3,11}... | collective-permute-start | bytes 12296 | tf_op jit(solution)/shard_map/ppermute | solution.py:361
  9.9 8.1 %collective-permute-start.2 = (bf16[64,768]{1,0:T(8,128)(2,1)S(1)}, bf16[64,768]{1,0:T(8,128)(2,1)S(1)}, u32[]{:S(2)}, u32[]{:S(2)}) collective-permute-start(bf16[64,768]{1,0:T(8,128)(2,1)S(1)} %get-tuple-element.68), channel_id=1, source_target_pairs={{0,6},{2,4},{4,2},{6,0},{8,14},{10,12},{12,10},{14,8},{1,7},{3,5},... | collective-permute-start | bytes 294920 | tf_op jit(solution)/shard_map/ppermute | solution.py:356
  12.8 6.4 %collective-permute-start.3 = (bf16[64,768]{1,0:T(8,128)(2,1)S(1)}, bf16[64,768]{1,0:T(8,128)(2,1)S(1)}, u32[]{:S(2)}, u32[]{:S(2)}) collective-permute-start(bf16[64,768]{1,0:T(8,128)(2,1)S(1)} %get-tuple-element.69), channel_id=1, source_target_pairs={{0,4},{2,6},{4,0},{6,2},{8,12},{10,14},{12,8},{14,10},{1,5},{3,7},... | collective-permute-start | bytes 294920 | tf_op jit(solution)/shard_map/ppermute | solution.py:356
  14.9 5.5 %slice-start = ((s8[4718592]{0:T(1024)(128)(4,1)}), s8[4194304]{0:T(1024)(128)(4,1)S(1)}, s32[]{:S(2)}) async-start(s8[4718592]{0:T(1024)(128)(4,1)} %bitcast.11), calls=%async_computation | async-start | bytes 8388608
  14.9 5.5 %slice-start.1 = ((s8[4718592]{0:T(1024)(128)(4,1)}), s8[524288]{0:T(1024)(128)(4,1)S(1)}, s32[]{:S(2)}) async-start(s8[4718592]{0:T(1024)(128)(4,1)} %bitcast.11), calls=%async_computation.1 | async-start | bytes 1048576
  14.9 5.5 %collective-permute-start.4 = (bf16[64,768]{1,0:T(8,128)(2,1)S(1)}, bf16[64,768]{1,0:T(8,128)(2,1)S(1)}, u32[]{:S(2)}, u32[]{:S(2)}) collective-permute-start(bf16[64,768]{1,0:T(8,128)(2,1)S(1)} %get-tuple-element.70), channel_id=1, source_target_pairs={{0,2},{2,0},{4,6},{6,4},{8,10},{10,8},{12,14},{14,12},{1,3},{3,1},... | collective-permute-start | bytes 294920 | tf_op jit(solution)/shard_map/ppermute | solution.py:356
  16.9 9.4 %collective-permute-start.10 = (bf16[64,768]{1,0:T(8,128)(2,1)S(1)}, bf16[64,768]{1,0:T(8,128)(2,1)S(1)}, u32[]{:S(2)}, u32[]{:S(2)}) collective-permute-start(bf16[64,768]{1,0:T(8,128)(2,1)S(1)} %get-tuple-element.77), channel_id=1, source_target_pairs={{0,4},{2,6},{4,0},{6,2},{8,12},{10,14},{12,8},{14,10},{1,5},{3,7},... | collective-permute-start | bytes 294920 | tf_op jit(solution)/shard_map/ppermute | solution.py:356
  18.0 9.4 %collective-permute-start.11 = (bf16[64,768]{1,0:T(8,128)(2,1)S(1)}, bf16[64,768]{1,0:T(8,128)(2,1)S(1)}, u32[]{:S(2)}, u32[]{:S(2)}) collective-permute-start(bf16[64,768]{1,0:T(8,128)(2,1)S(1)} %get-tuple-element.78), channel_id=1, source_target_pairs={{0,2},{2,0},{4,6},{6,4},{8,10},{10,8},{12,14},{14,12},{1,3},{3,1},... | collective-permute-start | bytes 294920 | tf_op jit(solution)/shard_map/ppermute | solution.py:356
  19.1 8.3 %collective-permute-start.9 = (bf16[64,768]{1,0:T(8,128)(2,1)S(1)}, bf16[64,768]{1,0:T(8,128)(2,1)S(1)}, u32[]{:S(2)}, u32[]{:S(2)}) collective-permute-start(bf16[64,768]{1,0:T(8,128)(2,1)S(1)} %get-tuple-element.76), channel_id=1, source_target_pairs={{0,6},{2,4},{4,2},{6,0},{8,14},{10,12},{12,10},{14,8},{1,7},{3,5},... | collective-permute-start | bytes 294920 | tf_op jit(solution)/shard_map/ppermute | solution.py:356
  23.9 7.6 %collective-permute-start.5 = (bf16[64,768]{1,0:T(8,128)(2,1)S(1)}, bf16[64,768]{1,0:T(8,128)(2,1)S(1)}, u32[]{:S(2)}, u32[]{:S(2)}) collective-permute-start(bf16[64,768]{1,0:T(8,128)(2,1)S(1)} %get-tuple-element.72), channel_id=1, source_target_pairs={{0,6},{2,4},{4,2},{6,0},{8,14},{10,12},{12,10},{14,8},{1,7},{3,5},... | collective-permute-start | bytes 294920 | tf_op jit(solution)/shard_map/ppermute | solution.py:356
  25.9 5.5 %collective-permute-start.6 = (bf16[64,768]{1,0:T(8,128)(2,1)S(1)}, bf16[64,768]{1,0:T(8,128)(2,1)S(1)}, u32[]{:S(2)}, u32[]{:S(2)}) collective-permute-start(bf16[64,768]{1,0:T(8,128)(2,1)S(1)} %get-tuple-element.73), channel_id=1, source_target_pairs={{0,4},{2,6},{4,0},{6,2},{8,12},{10,14},{12,8},{14,10},{1,5},{3,7},... | collective-permute-start | bytes 294920 | tf_op jit(solution)/shard_map/ppermute | solution.py:356
  26.3 5.1 %collective-permute-start.7 = (bf16[64,768]{1,0:T(8,128)(2,1)S(1)}, bf16[64,768]{1,0:T(8,128)(2,1)S(1)}, u32[]{:S(2)}, u32[]{:S(2)}) collective-permute-start(bf16[64,768]{1,0:T(8,128)(2,1)S(1)} %get-tuple-element.74), channel_id=1, source_target_pairs={{0,2},{2,0},{4,6},{6,4},{8,10},{10,8},{12,14},{14,12},{1,3},{3,1},... | collective-permute-start | bytes 294920 | tf_op jit(solution)/shard_map/ppermute | solution.py:356
  27.5 18.2 %collective-permute-start.17 = (bf16[7,256,256]{2,1,0:T(8,128)(2,1)S(1)}, bf16[7,256,256]{2,1,0:T(8,128)(2,1)S(1)}, u32[]{:S(2)}, u32[]{:S(2)}) collective-permute-start(bf16[7,256,256]{2,1,0:T(8,128)(2,1)S(1)} %get-tuple-element.79.refs_6_.refs_1_), channel_id=1, source_target_pairs={{0,1},{1,0},{2,3},{3,2},{4,5},{5,4},{6,7},{7,6},{8,9},{9,8},{10,11... | collective-permute-start | bytes 2752520 | tf_op jit(solution)/shard_map/ppermute | solution.py:364
  27.5 4.0 %copy-start.2 = (bf16[128,768]{1,0:T(8,128)(2,1)S(1)}, bf16[128,768]{1,0:T(8,128)(2,1)}, u32[]{:S(2)}) copy-start(bf16[128,768]{1,0:T(8,128)(2,1)} %refs_1_.3) | copy-start | bytes 589828
  30.9 14.8 %collective-permute-start.16 = (bf16[7,256,256]{2,1,0:T(8,128)(2,1)S(1)}, bf16[7,256,256]{2,1,0:T(8,128)(2,1)S(1)}, u32[]{:S(2)}, u32[]{:S(2)}) collective-permute-start(bf16[7,256,256]{2,1,0:T(8,128)(2,1)S(1)} %get-tuple-element.89.refs_0_), channel_id=1, source_target_pairs={{0,1},{1,0},{2,3},{3,2},{4,5},{5,4},{6,7},{7,6},{8,9},{9,8},{10,11... | collective-permute-start | bytes 2752520 | tf_op jit(solution)/shard_map/ppermute | solution.py:364
  32.0 6.0 %collective-permute-start.13 = (bf16[64,768]{1,0:T(8,128)(2,1)S(1)}, bf16[64,768]{1,0:T(8,128)(2,1)S(1)}, u32[]{:S(2)}, u32[]{:S(2)}) collective-permute-start(bf16[64,768]{1,0:T(8,128)(2,1)S(1)} %get-tuple-element.86), channel_id=1, source_target_pairs={{0,6},{2,4},{4,2},{6,0},{8,14},{10,12},{12,10},{14,8},{1,7},{3,5},... | collective-permute-start | bytes 294920 | tf_op jit(solution)/shard_map/ppermute | solution.py:356
  34.0 11.6 %collective-permute-start.12 = (bf16[128,768]{1,0:T(8,128)(2,1)S(1)}, bf16[128,768]{1,0:T(8,128)(2,1)S(1)}, u32[]{:S(2)}, u32[]{:S(2)}) collective-permute-start(bf16[128,768]{1,0:T(8,128)(2,1)S(1)} %get-tuple-element.84), channel_id=1, source_target_pairs={{0,8},{2,10},{4,12},{6,14},{8,0},{10,2},{12,4},{14,6},{1,9},{3,11}... | collective-permute-start | bytes 589832 | tf_op jit(solution)/shard_map/ppermute | solution.py:361
  36.5 6.2 %collective-permute-start.14 = (bf16[64,768]{1,0:T(8,128)(2,1)S(1)}, bf16[64,768]{1,0:T(8,128)(2,1)S(1)}, u32[]{:S(2)}, u32[]{:S(2)}) collective-permute-start(bf16[64,768]{1,0:T(8,128)(2,1)S(1)} %get-tuple-element.87), channel_id=1, source_target_pairs={{0,4},{2,6},{4,0},{6,2},{8,12},{10,14},{12,8},{14,10},{1,5},{3,7},... | collective-permute-start | bytes 294920 | tf_op jit(solution)/shard_map/ppermute | solution.py:356
  38.0 4.7 %collective-permute-start.15 = (bf16[64,768]{1,0:T(8,128)(2,1)S(1)}, bf16[64,768]{1,0:T(8,128)(2,1)S(1)}, u32[]{:S(2)}, u32[]{:S(2)}) collective-permute-start(bf16[64,768]{1,0:T(8,128)(2,1)S(1)} %get-tuple-element.88), channel_id=1, source_target_pairs={{0,2},{2,0},{4,6},{6,4},{8,10},{10,8},{12,14},{14,12},{1,3},{3,1},... | collective-permute-start | bytes 294920 | tf_op jit(solution)/shard_map/ppermute | solution.py:356
  46.5 5.7 %collective-permute-start.19 = (bf16[64,768]{1,0:T(8,128)(2,1)S(1)}, bf16[64,768]{1,0:T(8,128)(2,1)S(1)}, u32[]{:S(2)}, u32[]{:S(2)}) collective-permute-start(bf16[64,768]{1,0:T(8,128)(2,1)S(1)} %get-tuple-element.94), channel_id=1, source_target_pairs={{0,6},{2,4},{4,2},{6,0},{8,14},{10,12},{12,10},{14,8},{1,7},{3,5},... | collective-permute-start | bytes 294920 | tf_op jit(solution)/shard_map/ppermute | solution.py:356
  47.7 8.2 %collective-permute-start.20 = (bf16[64,768]{1,0:T(8,128)(2,1)S(1)}, bf16[64,768]{1,0:T(8,128)(2,1)S(1)}, u32[]{:S(2)}, u32[]{:S(2)}) collective-permute-start(bf16[64,768]{1,0:T(8,128)(2,1)S(1)} %get-tuple-element.95), channel_id=1, source_target_pairs={{0,4},{2,6},{4,0},{6,2},{8,12},{10,14},{12,8},{14,10},{1,5},{3,7},... | collective-permute-start | bytes 294920 | tf_op jit(solution)/shard_map/ppermute | solution.py:356
  49.2 6.7 %collective-permute-start.21 = (bf16[64,768]{1,0:T(8,128)(2,1)S(1)}, bf16[64,768]{1,0:T(8,128)(2,1)S(1)}, u32[]{:S(2)}, u32[]{:S(2)}) collective-permute-start(bf16[64,768]{1,0:T(8,128)(2,1)S(1)} %get-tuple-element.96), channel_id=1, source_target_pairs={{0,2},{2,0},{4,6},{6,4},{8,10},{10,8},{12,14},{14,12},{1,3},{3,1},... | collective-permute-start | bytes 294920 | tf_op jit(solution)/shard_map/ppermute | solution.py:356
  50.0 13.3 %collective-permute-start.18 = (bf16[128,768]{1,0:T(8,128)(2,1)S(1)}, bf16[128,768]{1,0:T(8,128)(2,1)S(1)}, u32[]{:S(2)}, u32[]{:S(2)}) collective-permute-start(bf16[128,768]{1,0:T(8,128)(2,1)S(1)} %get-tuple-element.90), channel_id=1, source_target_pairs={{0,8},{2,10},{4,12},{6,14},{8,0},{10,2},{12,4},{14,6},{1,9},{3,11}... | collective-permute-start | bytes 589832 | tf_op jit(solution)/shard_map/ppermute | solution.py:361
  59.7 6.6 %collective-permute-start.25 = (bf16[11,256,256]{2,1,0:T(8,128)(2,1)S(1)}, bf16[11,256,256]{2,1,0:T(8,128)(2,1)S(1)}, u32[]{:S(2)}, u32[]{:S(2)}) collective-permute-start(bf16[11,256,256]{2,1,0:T(8,128)(2,1)S(1)} %get-tuple-element.104.refs_2_), channel_id=1, source_target_pairs={{0,1},{1,0},{2,3},{3,2},{4,5},{5,4},{6,7},{7,6},{8,9},{9,8},{10,11... | collective-permute-start | bytes 4325384 | tf_op jit(solution)/shard_map/ppermute | solution.py:364
  59.7 6.6 %collective-permute-start.22 = (bf16[64,768]{1,0:T(8,128)(2,1)S(1)}, bf16[64,768]{1,0:T(8,128)(2,1)S(1)}, u32[]{:S(2)}, u32[]{:S(2)}) collective-permute-start(bf16[64,768]{1,0:T(8,128)(2,1)S(1)} %get-tuple-element.101), channel_id=1, source_target_pairs={{0,6},{2,4},{4,2},{6,0},{8,14},{10,12},{12,10},{14,8},{1,7},{3,5},... | collective-permute-start | bytes 294920 | tf_op jit(solution)/shard_map/ppermute | solution.py:356
  59.8 10.8 %collective-permute-start.23 = (bf16[64,768]{1,0:T(8,128)(2,1)S(1)}, bf16[64,768]{1,0:T(8,128)(2,1)S(1)}, u32[]{:S(2)}, u32[]{:S(2)}) collective-permute-start(bf16[64,768]{1,0:T(8,128)(2,1)S(1)} %get-tuple-element.102), channel_id=1, source_target_pairs={{0,4},{2,6},{4,0},{6,2},{8,12},{10,14},{12,8},{14,10},{1,5},{3,7},... | collective-permute-start | bytes 294920 | tf_op jit(solution)/shard_map/ppermute | solution.py:356
  61.2 9.4 %collective-permute-start.24 = (bf16[64,768]{1,0:T(8,128)(2,1)S(1)}, bf16[64,768]{1,0:T(8,128)(2,1)S(1)}, u32[]{:S(2)}, u32[]{:S(2)}) collective-permute-start(bf16[64,768]{1,0:T(8,128)(2,1)S(1)} %get-tuple-element.103), channel_id=1, source_target_pairs={{0,2},{2,0},{4,6},{6,4},{8,10},{10,8},{12,14},{14,12},{1,3},{3,1},... | collective-permute-start | bytes 294920 | tf_op jit(solution)/shard_map/ppermute | solution.py:356
  64.5 8.3 %collective-permute-start.27 = (bf16[64,768]{1,0:T(8,128)(2,1)S(1)}, bf16[64,768]{1,0:T(8,128)(2,1)S(1)}, u32[]{:S(2)}, u32[]{:S(2)}) collective-permute-start(bf16[64,768]{1,0:T(8,128)(2,1)S(1)} %get-tuple-element.110), channel_id=1, source_target_pairs={{0,6},{2,4},{4,2},{6,0},{8,14},{10,12},{12,10},{14,8},{1,7},{3,5},... | collective-permute-start | bytes 294920 | tf_op jit(solution)/shard_map/ppermute | solution.py:356
  66.3 6.6 %collective-permute-start.28 = (bf16[64,768]{1,0:T(8,128)(2,1)S(1)}, bf16[64,768]{1,0:T(8,128)(2,1)S(1)}, u32[]{:S(2)}, u32[]{:S(2)}) collective-permute-start(bf16[64,768]{1,0:T(8,128)(2,1)S(1)} %get-tuple-element.111), channel_id=1, source_target_pairs={{0,4},{2,6},{4,0},{6,2},{8,12},{10,14},{12,8},{14,10},{1,5},{3,7},... | collective-permute-start | bytes 294920 | tf_op jit(solution)/shard_map/ppermute | solution.py:356
  66.3 6.6 %collective-permute-start.29 = (bf16[64,768]{1,0:T(8,128)(2,1)S(1)}, bf16[64,768]{1,0:T(8,128)(2,1)S(1)}, u32[]{:S(2)}, u32[]{:S(2)}) collective-permute-start(bf16[64,768]{1,0:T(8,128)(2,1)S(1)} %get-tuple-element.112), channel_id=1, source_target_pairs={{0,2},{2,0},{4,6},{6,4},{8,10},{10,8},{12,14},{14,12},{1,3},{3,1},... | collective-permute-start | bytes 294920 | tf_op jit(solution)/shard_map/ppermute | solution.py:356
  71.1 11.9 %collective-permute-start.26 = (bf16[144,768]{1,0:T(8,128)(2,1)S(1)}, bf16[144,768]{1,0:T(8,128)(2,1)S(1)}, u32[]{:S(2)}, u32[]{:S(2)}) collective-permute-start(bf16[144,768]{1,0:T(8,128)(2,1)S(1)} %far_back.1.refs_8_), channel_id=1, source_target_pairs={{0,8},{2,10},{4,12},{6,14},{8,0},{10,2},{12,4},{14,6},{1,9},{3,11}... | collective-permute-start | bytes 663560 | tf_op jit(solution)/shard_map/ppermute | solution.py:361
  76.7 6.3 %collective-permute-start.33 = (bf16[11,256,256]{2,1,0:T(8,128)(2,1)S(1)}, bf16[11,256,256]{2,1,0:T(8,128)(2,1)S(1)}, u32[]{:S(2)}, u32[]{:S(2)}) collective-permute-start(bf16[11,256,256]{2,1,0:T(8,128)(2,1)S(1)} %get-tuple-element.121.refs_3_), channel_id=1, source_target_pairs={{0,1},{1,0},{2,3},{3,2},{4,5},{5,4},{6,7},{7,6},{8,9},{9,8},{10,11... | collective-permute-start | bytes 4325384 | tf_op jit(solution)/shard_map/ppermute | solution.py:364
  76.7 10.1 %collective-permute-start.30 = (bf16[64,768]{1,0:T(8,128)(2,1)S(1)}, bf16[64,768]{1,0:T(8,128)(2,1)S(1)}, u32[]{:S(2)}, u32[]{:S(2)}) collective-permute-start(bf16[64,768]{1,0:T(8,128)(2,1)S(1)} %get-tuple-element.117), channel_id=1, source_target_pairs={{0,6},{2,4},{4,2},{6,0},{8,14},{10,12},{12,10},{14,8},{1,7},{3,5},... | collective-permute-start | bytes 294920 | tf_op jit(solution)/shard_map/ppermute | solution.py:356
  78.0 9.1 %collective-permute-start.31 = (bf16[64,768]{1,0:T(8,128)(2,1)S(1)}, bf16[64,768]{1,0:T(8,128)(2,1)S(1)}, u32[]{:S(2)}, u32[]{:S(2)}) collective-permute-start(bf16[64,768]{1,0:T(8,128)(2,1)S(1)} %get-tuple-element.118), channel_id=1, source_target_pairs={{0,4},{2,6},{4,0},{6,2},{8,12},{10,14},{12,8},{14,10},{1,5},{3,7},... | collective-permute-start | bytes 294920 | tf_op jit(solution)/shard_map/ppermute | solution.py:356
  79.7 7.4 %collective-permute-start.32 = (bf16[64,768]{1,0:T(8,128)(2,1)S(1)}, bf16[64,768]{1,0:T(8,128)(2,1)S(1)}, u32[]{:S(2)}, u32[]{:S(2)}) collective-permute-start(bf16[64,768]{1,0:T(8,128)(2,1)S(1)} %get-tuple-element.119), channel_id=1, source_target_pairs={{0,2},{2,0},{4,6},{6,4},{8,10},{10,8},{12,14},{14,12},{1,3},{3,1},... | collective-permute-start | bytes 294920 | tf_op jit(solution)/shard_map/ppermute | solution.py:356

commit v11 on v10

--- a/solution.py
+++ b/solution.py
@@ -28,7 +28,7 @@
     "combine_gradients": 30000000000,
     "order_rest": 30000000000,
     "order_back": 30000000000,
-    "order_far": 30000000000,
+    "order_return": 0,
     "weight_far": 2400000000,
 }
 
@@ -429,8 +429,10 @@
         through=out_far,
     )
     rest = to_mirror(rest_rows)
+    xf_sib, xn_sib = to_sibling(xf), to_sibling(xn)
+    out_far = call(order_kernel, "order_return", [], [], after=[xn_sib], through=out_far)
+    (rest,) = call(order_kernel, "order_rest", [], [], after=out_far[:1], through=[rest])
     got_far = within_half(out_far)
-    xf_sib, xn_sib = to_sibling(xf), to_sibling(xn)
 
     res = call(
         functools.partial(far_grad_kernel, half),
@@ -459,19 +461,19 @@
 
     back_far = within_half(grad_far)
     gf_sib = to_sibling(gf)
+    part_rows = call(
+        far_back_kernel, "far_back", longer, [], far_meta, d_gates_far, *back_far
+    )
+    part = to_mirror(part_rows)
     far_weights, far_done = call(
         functools.partial(weight_far_kernel, across),
         "weight_far",
         [jax.ShapeDtypeStruct((3, units, width), BF16), tiny],
         [],
         *(xf, xf_sib, gf, gf_sib, df, hf),
-        after=[back_far[1]],
+        after=[part_rows],
         limit=16,
     )
-    part_rows = call(
-        far_back_kernel, "far_back", longer, [], far_meta, d_gates_far, *back_far, after=[far_done]
-    )
-    part = to_mirror(part_rows)
     grad_near, (gn, dn) = backward(rg_near, fan, fbn, "backward_near", after=[part_rows, gf_sib, far_done])
     gn_sib = to_sibling(gn)
     back_near = within_half(grad_near)

time: 88.4 us -> 86.5 us (0.979)
  starting transfers between devices: 39.6 us -> 36.5 us
  waiting for transfers between devices: 17.6 us -> 18.8 us
    ppermute x5, starting transfers between devices: 9.73 us -> 7.63 us  [to_mirror(): return lax.ppermute(x, 'expert', [(i, i ^ half) for i in range(experts)])]
    ppermute x5, waiting for transfers between devices: 7.28 us -> 8.82 us  [to_mirror(): return lax.ppermute(x, 'expert', [(i, i ^ half) for i in range(experts)])]
    pallas_call x14 -> x16, Pallas kernels: 25.5 us -> 25.5 us  [call(): pl.pallas_call(body, in_specs=specs + [aspec] * (len(after) + len(through...]
  transfers between devices with their start and end apart: 34 -> 34, of which waited for: 10 -> 13; matrix products, arithmetic and copies ran while one was open for 0% -> 0% of each run, Pallas kernels for 27% -> 27%
where the time goes in v11:
time: 86.5 us; the launch traced here: 86.3 us
  starting transfers between devices  36.5 us (42%)
  Pallas kernels  25.5 us (29%)
  waiting for transfers between devices  18.8 us (22%)
  local copies, waits for them, and re-layouts  4.63 us (5%)
    ppermute x24, starting transfers between devices, within_half(): lax.ppermute(rows_of[s], 'expert', [(i, i ^ s) for i in range(experts)])  28.2 us
    pallas_call x16, Pallas kernels, call(): pl.pallas_call(body, in_specs=specs + [aspec] * (len(after) + len(through...  25.5 us
    ppermute x24, waiting for transfers between devices, within_half(): lax.ppermute(rows_of[s], 'expert', [(i, i ^ s) for i in range(experts)])  9.98 us
    ppermute x5, waiting for transfers between devices, to_mirror(): return lax.ppermute(x, 'expert', [(i, i ^ half) for i in range(experts)])  8.82 us
    ppermute x5, starting transfers between devices, to_mirror(): return lax.ppermute(x, 'expert', [(i, i ^ half) for i in range(experts)])  7.63 us
    unnamed x14, local copies, waits for them, and re-layouts  4.63 us
  transfers between devices with their start and end apart: 34, of which 13 were waited for; matrix products, arithmetic and copies ran while one was open for 0% of the time, Pallas kernels for 27%

profile of v11, /device:TPU:0, one launch (start us, length us, event | category | flops | bytes accessed | tf_op | source)
XLA Modules:
  0.0 86.3 jit_solution(13260975232759550080)
XLA Ops:
  0.6 0.5 collective-permute-start.1
  1.1 3.7 %collective-permute-start.9 = (bf16[128,768]{1,0:T(8,128)(2,1)}, bf16[128,768]{1,0:T(8,128)(2,1)S(1)}, u32[]{:S(2)}, u32[]{:S(2)}) collective-permute-start(bf16[128,768]{1,0:T(8,128)(2,1)} %refs_3_.1), channel_id=1, source_target_pairs={{0,8},{2,10},{4,12},{6,14},{8,0},{10,2},{12,4},{14,6},{1,9},{3,11}... | collective-permute-start | bytes 589832 | tf_op jit(solution)/shard_map/ppermute | solution.py:361
  4.8 2.3 %copy-done = bf16[1,1024,3,768]{3,1,2,0:T(8,128)(2,1)S(1)} copy-done((bf16[1,1024,3,768]{3,1,2,0:T(8,128)(2,1)S(1)}, bf16[1,1024,3,768]{3,1,2,0:T(8,128)(2,1)}, u32[]{:S(2)}) %copy-start) | copy-done | bytes 4718616
  7.2 0.9 %copy-done.1 = bf16[128,768]{1,0:T(8,128)(2,1)S(1)} copy-done((bf16[128,768]{1,0:T(8,128)(2,1)S(1)}, bf16[128,768]{1,0:T(8,128)(2,1)}, u32[]{:S(2)}) %copy-start.1) | copy-done | bytes 196632
  8.1 0.7 copy-done.3
  8.8 0.7 copy-done.4
  9.9 2.9 %collective-permute-start.2 = (bf16[64,768]{1,0:T(8,128)(2,1)S(1)}, bf16[64,768]{1,0:T(8,128)(2,1)S(1)}, u32[]{:S(2)}, u32[]{:S(2)}) collective-permute-start(bf16[64,768]{1,0:T(8,128)(2,1)S(1)} %get-tuple-element.72), channel_id=1, source_target_pairs={{0,6},{2,4},{4,2},{6,0},{8,14},{10,12},{12,10},{14,8},{1,7},{3,5},... | collective-permute-start | bytes 294920 | tf_op jit(solution)/shard_map/ppermute | solution.py:356
  12.8 0.5 collective-permute-start.3
  13.2 1.7 %collective-permute-done.refs_0_ = f32[8,128]{1,0:T(8,128)S(1)} collective-permute-done((f32[8,128]{1,0:T(8,128)S(1)}, f32[8,128]{1,0:T(8,128)S(1)}, u32[]{:S(2)}, u32[]{:S(2)}) %collective-permute-start) | collective-permute-done | bytes 4128 | tf_op jit(solution)/shard_map/ppermute | solution.py:361
  14.9 1.6 %collective-permute-start.4 = (bf16[64,768]{1,0:T(8,128)(2,1)S(1)}, bf16[64,768]{1,0:T(8,128)(2,1)S(1)}, u32[]{:S(2)}, u32[]{:S(2)}) collective-permute-start(bf16[64,768]{1,0:T(8,128)(2,1)S(1)} %get-tuple-element.74), channel_id=1, source_target_pairs={{0,2},{2,0},{4,6},{6,4},{8,10},{10,8},{12,14},{14,12},{1,3},{3,1},... | collective-permute-start | bytes 294920 | tf_op jit(solution)/shard_map/ppermute | solution.py:356
  16.9 1.0 %collective-permute-start.10 = (bf16[64,768]{1,0:T(8,128)(2,1)S(1)}, bf16[64,768]{1,0:T(8,128)(2,1)S(1)}, u32[]{:S(2)}, u32[]{:S(2)}) collective-permute-start(bf16[64,768]{1,0:T(8,128)(2,1)S(1)} %get-tuple-element.81), channel_id=1, source_target_pairs={{0,6},{2,4},{4,2},{6,0},{8,14},{10,12},{12,10},{14,8},{1,7},{3,5},... | collective-permute-start | bytes 294920 | tf_op jit(solution)/shard_map/ppermute | solution.py:356
  18.0 0.8 collective-permute-start.11
  19.1 1.6 %collective-permute-start.12 = (bf16[64,768]{1,0:T(8,128)(2,1)S(1)}, bf16[64,768]{1,0:T(8,128)(2,1)S(1)}, u32[]{:S(2)}, u32[]{:S(2)}) collective-permute-start(bf16[64,768]{1,0:T(8,128)(2,1)S(1)} %get-tuple-element.83), channel_id=1, source_target_pairs={{0,2},{2,0},{4,6},{6,4},{8,10},{10,8},{12,14},{14,12},{1,3},{3,1},... | collective-permute-start | bytes 294920 | tf_op jit(solution)/shard_map/ppermute | solution.py:356
  20.7 3.4 %forward_near.1 = (bf16[64,768]{1,0:T(8,128)(2,1)S(1)}, bf16[64,768]{1,0:T(8,128)(2,1)S(1)}, bf16[64,768]{1,0:T(8,128)(2,1)S(1)}, bf16[64,768]{1,0:T(8,128)(2,1)...) custom-call(bf16[3,1024,768]{2,1,0:T(8,128)(2,1)S(1)} %bitcast.13, ...), custom_call_target="tpu_custom_call" | custom-call | flops 100000000 | bytes 2097152 | tf_op jit(solution)/shard_map/forward_near/pallas_call | solution.py:338
  24.1 2.3 %collective-permute-start.6 = (bf16[64,768]{1,0:T(8,128)(2,1)S(1)}, bf16[64,768]{1,0:T(8,128)(2,1)S(1)}, u32[]{:S(2)}, u32[]{:S(2)}) collective-permute-start(bf16[64,768]{1,0:T(8,128)(2,1)S(1)} %get-tuple-element.77), channel_id=1, source_target_pairs={{0,6},{2,4},{4,2},{6,0},{8,14},{10,12},{12,10},{14,8},{1,7},{3,5},... | collective-permute-start | bytes 294920 | tf_op jit(solution)/shard_map/ppermute | solution.py:356
  26.5 1.2 %collective-permute-start.7 = (bf16[64,768]{1,0:T(8,128)(2,1)S(1)}, bf16[64,768]{1,0:T(8,128)(2,1)S(1)}, u32[]{:S(2)}, u32[]{:S(2)}) collective-permute-start(bf16[64,768]{1,0:T(8,128)(2,1)S(1)} %get-tuple-element.78), channel_id=1, source_target_pairs={{0,4},{2,6},{4,0},{6,2},{8,12},{10,14},{12,8},{14,10},{1,5},{3,7},... | collective-permute-start | bytes 294920 | tf_op jit(solution)/shard_map/ppermute | solution.py:356
  27.7 3.4 %forward_far.1 = (bf16[64,768]{1,0:T(8,128)(2,1)S(1)}, bf16[64,768]{1,0:T(8,128)(2,1)S(1)}, bf16[64,768]{1,0:T(8,128)(2,1)S(1)}, bf16[64,768]{1,0:T(8,128)(2,1)S...) custom-call(bf16[3,1024,768]{2,1,0:T(8,128)(2,1)S(1)} %bitcast.14, ...), custom_call_target="tpu_custom_call" | custom-call | flops 3000000000 | bytes 2097152 | tf_op jit(solution)/shard_map/forward_far/pallas_call | solution.py:338
  31.3 1.0 %collective-permute-done.8.refs_5_.refs_6_ = bf16[64,768]{1,0:T(8,128)(2,1)S(1)} collective-permute-done((bf16[64,768]{1,0:T(8,128)(2,1)S(1)}, bf16[64,768]{1,0:T(8,128)(2,1)S(1)}, u32[]{:S(2)}, u32[]{:S(2)}) %collective-permute-start.8) | collective-permute-done | bytes 98336 | tf_op jit(solution)/shard_map/ppermute | solution.py:356
  32.3 0.5 near_sum.1
  32.7 2.2 %collective-permute-start.13 = (bf16[128,768]{1,0:T(8,128)(2,1)S(1)}, bf16[128,768]{1,0:T(8,128)(2,1)S(1)}, u32[]{:S(2)}, u32[]{:S(2)}) collective-permute-start(bf16[128,768]{1,0:T(8,128)(2,1)S(1)} %get-tuple-element.93), channel_id=1, source_target_pairs={{0,8},{2,10},{4,12},{6,14},{8,0},{10,2},{12,4},{14,6},{1,9},{3,11}... | collective-permute-start | bytes 589832 | tf_op jit(solution)/shard_map/ppermute | solution.py:361
  35.0 2.6 %collective-permute-start.14 = (bf16[64,768]{1,0:T(8,128)(2,1)S(1)}, bf16[64,768]{1,0:T(8,128)(2,1)S(1)}, u32[]{:S(2)}, u32[]{:S(2)}) collective-permute-start(bf16[64,768]{1,0:T(8,128)(2,1)S(1)} %get-tuple-element.94), channel_id=1, source_target_pairs={{0,6},{2,4},{4,2},{6,0},{8,14},{10,12},{12,10},{14,8},{1,7},{3,5},... | collective-permute-start | bytes 294920 | tf_op jit(solution)/shard_map/ppermute | solution.py:356
  37.5 0.9 %collective-permute-start.16 = (bf16[64,768]{1,0:T(8,128)(2,1)S(1)}, bf16[64,768]{1,0:T(8,128)(2,1)S(1)}, u32[]{:S(2)}, u32[]{:S(2)}) collective-permute-start(bf16[64,768]{1,0:T(8,128)(2,1)S(1)} %get-tuple-element.96), channel_id=1, source_target_pairs={{0,2},{2,0},{4,6},{6,4},{8,10},{10,8},{12,14},{14,12},{1,3},{3,1},... | collective-permute-start | bytes 294920 | tf_op jit(solution)/shard_map/ppermute | solution.py:356
  38.4 5.9 %collective-permute-done.13.refs_1_ = bf16[128,768]{1,0:T(8,128)(2,1)S(1)} collective-permute-done((bf16[128,768]{1,0:T(8,128)(2,1)S(1)}, bf16[128,768]{1,0:T(8,128)(2,1)S(1)}, u32[]{:S(2)}, u32[]{:S(2)}) %collective-permute-start.13) | collective-permute-done | bytes 196640 | tf_op jit(solution)/shard_map/ppermute | solution.py:361
  44.3 1.5 %collective-permute-done.15.refs_4_ = bf16[64,768]{1,0:T(8,128)(2,1)S(1)} collective-permute-done((bf16[64,768]{1,0:T(8,128)(2,1)S(1)}, bf16[64,768]{1,0:T(8,128)(2,1)S(1)}, u32[]{:S(2)}, u32[]{:S(2)}) %collective-permute-start.15) | collective-permute-done | bytes 98336 | tf_op jit(solution)/shard_map/ppermute | solution.py:356
  45.8 0.8 far_grad.1
  46.6 1.1 %collective-permute-start.19 = (bf16[64,768]{1,0:T(8,128)(2,1)S(1)}, bf16[64,768]{1,0:T(8,128)(2,1)S(1)}, u32[]{:S(2)}, u32[]{:S(2)}) collective-permute-start(bf16[64,768]{1,0:T(8,128)(2,1)S(1)} %get-tuple-element.102), channel_id=1, source_target_pairs={{0,6},{2,4},{4,2},{6,0},{8,14},{10,12},{12,10},{14,8},{1,7},{3,5},... | collective-permute-start | bytes 294920 | tf_op jit(solution)/shard_map/ppermute | solution.py:356
  47.7 1.5 %collective-permute-start.20 = (bf16[64,768]{1,0:T(8,128)(2,1)S(1)}, bf16[64,768]{1,0:T(8,128)(2,1)S(1)}, u32[]{:S(2)}, u32[]{:S(2)}) collective-permute-start(bf16[64,768]{1,0:T(8,128)(2,1)S(1)} %get-tuple-element.103), channel_id=1, source_target_pairs={{0,4},{2,6},{4,0},{6,2},{8,12},{10,14},{12,8},{14,10},{1,5},{3,7},... | collective-permute-start | bytes 294920 | tf_op jit(solution)/shard_map/ppermute | solution.py:356
  49.2 1.0 %collective-permute-start.21 = (bf16[64,768]{1,0:T(8,128)(2,1)S(1)}, bf16[64,768]{1,0:T(8,128)(2,1)S(1)}, u32[]{:S(2)}, u32[]{:S(2)}) collective-permute-start(bf16[64,768]{1,0:T(8,128)(2,1)S(1)} %get-tuple-element.104), channel_id=1, source_target_pairs={{0,2},{2,0},{4,6},{6,4},{8,10},{10,8},{12,14},{14,12},{1,3},{3,1},... | collective-permute-start | bytes 294920 | tf_op jit(solution)/shard_map/ppermute | solution.py:356
  50.1 1.0 %collective-permute-start.18 = (bf16[128,768]{1,0:T(8,128)(2,1)S(1)}, bf16[128,768]{1,0:T(8,128)(2,1)S(1)}, u32[]{:S(2)}, u32[]{:S(2)}) collective-permute-start(bf16[128,768]{1,0:T(8,128)(2,1)S(1)} %get-tuple-element.98), channel_id=1, source_target_pairs={{0,8},{2,10},{4,12},{6,14},{8,0},{10,2},{12,4},{14,6},{1,9},{3,11}... | collective-permute-start | bytes 589832 | tf_op jit(solution)/shard_map/ppermute | solution.py:361
  51.2 1.8 %collective-permute-done.19.refs_5_ = bf16[64,768]{1,0:T(8,128)(2,1)S(1)} collective-permute-done((bf16[64,768]{1,0:T(8,128)(2,1)S(1)}, bf16[64,768]{1,0:T(8,128)(2,1)S(1)}, u32[]{:S(2)}, u32[]{:S(2)}) %collective-permute-start.19) | collective-permute-done | bytes 98336 | tf_op jit(solution)/shard_map/ppermute | solution.py:356
  53.0 2.4 %collective-permute-done.20.refs_6_ = bf16[64,768]{1,0:T(8,128)(2,1)S(1)} collective-permute-done((bf16[64,768]{1,0:T(8,128)(2,1)S(1)}, bf16[64,768]{1,0:T(8,128)(2,1)S(1)}, u32[]{:S(2)}, u32[]{:S(2)}) %collective-permute-start.20) | collective-permute-done | bytes 98336 | tf_op jit(solution)/shard_map/ppermute | solution.py:356
  55.5 3.8 %backward_far.1 = (bf16[64,768]{1,0:T(8,128)(2,1)S(1)}, bf16[64,768]{1,0:T(8,128)(2,1)S(1)}, bf16[64,768]{1,0:T(8,128)(2,1)S(1)}, bf16[64,768]{1,0:T(8,128)(2,1)...) custom-call(bf16[3,1024,768]{2,1,0:T(8,128)(2,1)S(1)} %bitcast.15, ...), custom_call_target="tpu_custom_call" | custom-call | flops 3000000000 | bytes 2097152 | tf_op jit(solution)/shard_map/backward_far/pallas_call | solution.py:338
  59.4 1.8 %collective-permute-start.23 = (bf16[64,768]{1,0:T(8,128)(2,1)S(1)}, bf16[64,768]{1,0:T(8,128)(2,1)S(1)}, u32[]{:S(2)}, u32[]{:S(2)}) collective-permute-start(bf16[64,768]{1,0:T(8,128)(2,1)S(1)} %get-tuple-element.110), channel_id=1, source_target_pairs={{0,4},{2,6},{4,0},{6,2},{8,12},{10,14},{12,8},{14,10},{1,5},{3,7},... | collective-permute-start | bytes 294920 | tf_op jit(solution)/shard_map/ppermute | solution.py:356
  61.2 1.7 %collective-permute-start.24 = (bf16[64,768]{1,0:T(8,128)(2,1)S(1)}, bf16[64,768]{1,0:T(8,128)(2,1)S(1)}, u32[]{:S(2)}, u32[]{:S(2)}) collective-permute-start(bf16[64,768]{1,0:T(8,128)(2,1)S(1)} %get-tuple-element.111), channel_id=1, source_target_pairs={{0,2},{2,0},{4,6},{6,4},{8,10},{10,8},{12,14},{14,12},{1,3},{3,1},... | collective-permute-start | bytes 294920 | tf_op jit(solution)/shard_map/ppermute | solution.py:356
  62.9 1.2 %near_grad.1 = (bf16[128,768]{1,0:T(8,128)(2,1)}, f32[2,128]{1,0:T(2,128)S(1)}, bf16[64,768]{1,0:T(8,128)(2,1)S(1)}, bf16[64,768]{1,0:T(8,128)(2,1)S(1)}, bf16[6...) custom-call(f32[8,128]{1,0:T(8,128)S(1)} %get-tuple-element.70.refs_0_, bf16[128,768]{1,0:T(8,128)(2,1)S(1)} %copy-done.2, ...), custom_call_target="tpu_custom_call" | custom-call | flops 30000001024 | bytes 2097152 | tf_op jit(solution)/shard_map/near_grad/pallas_call | solution.py:338
  64.2 1.7 %collective-permute-done.22.refs_3_ = bf16[64,768]{1,0:T(8,128)(2,1)S(1)} collective-permute-done((bf16[64,768]{1,0:T(8,128)(2,1)S(1)}, bf16[64,768]{1,0:T(8,128)(2,1)S(1)}, u32[]{:S(2)}, u32[]{:S(2)}) %collective-permute-start.22) | collective-permute-done | bytes 98336 | tf_op jit(solution)/shard_map/ppermute | solution.py:356
  65.9 0.7 collective-permute-done.23.refs_4_
  66.7 1.7 %collective-permute-start.28 = (bf16[64,768]{1,0:T(8,128)(2,1)S(1)}, bf16[64,768]{1,0:T(8,128)(2,1)S(1)}, u32[]{:S(2)}, u32[]{:S(2)}) collective-permute-start(bf16[64,768]{1,0:T(8,128)(2,1)S(1)} %get-tuple-element.117), channel_id=1, source_target_pairs={{0,2},{2,0},{4,6},{6,4},{8,10},{10,8},{12,14},{14,12},{1,3},{3,1},... | collective-permute-start | bytes 294920 | tf_op jit(solution)/shard_map/ppermute | solution.py:356
  68.3 0.4 far_back.1.refs_6_.refs_8_
  68.7 0.6 collective-permute-start.25
  69.4 2.6 %weight_far.1 = (bf16[3,1024,768]{2,1,0:T(8,128)(2,1)S(1)}, f32[8,128]{1,0:T(8,128)S(1)}) custom-call(bf16[7,256,256]{2,1,0:T(8,128)(2,1)S(1)} %get-tuple-element.97.refs_0_, bf16[7,256,256]{2,1,0:T(8,128)(2,1)S(1)} %collective-permute-done.17.refs_6_.refs_1_, bf16[11,256,256]{2,1,0:T(8,128)(2,1)S(1)} %get-tuple-element.118.refs_2_, ...), custom_call_target="tpu_custom_call" | custom-call | flops 2400000000 | bytes 2097152 | tf_op jit(solution)/shard_map/weight_far/pallas_call | solution.py:338
  72.0 3.8 %backward_near.1 = (bf16[64,768]{1,0:T(8,128)(2,1)S(1)}, bf16[64,768]{1,0:T(8,128)(2,1)S(1)}, bf16[64,768]{1,0:T(8,128)(2,1)S(1)}, bf16[64,768]{1,0:T(8,128)(2,1...) custom-call(bf16[3,1024,768]{2,1,0:T(8,128)(2,1)S(1)} %bitcast.16, ...), custom_call_target="tpu_custom_call" | custom-call | flops 10000000000 | bytes 2097152 | tf_op jit(solution)/shard_map/backward_near/pallas_call | solution.py:338
  75.9 3.0 %collective-permute-start.30 = (bf16[64,768]{1,0:T(8,128)(2,1)S(1)}, bf16[64,768]{1,0:T(8,128)(2,1)S(1)}, u32[]{:S(2)}, u32[]{:S(2)}) collective-permute-start(bf16[64,768]{1,0:T(8,128)(2,1)S(1)} %get-tuple-element.125), channel_id=1, source_target_pairs={{0,6},{2,4},{4,2},{6,0},{8,14},{10,12},{12,10},{14,8},{1,7},{3,5},... | collective-permute-start | bytes 294920 | tf_op jit(solution)/shard_map/ppermute | solution.py:356
  78.8 0.6 collective-permute-start.31
  79.4 0.4 collective-permute-start.32
  79.8 1.2 %collective-permute-done.25.refs_0_ = bf16[144,768]{1,0:T(8,128)(2,1)S(1)} collective-permute-done((bf16[144,768]{1,0:T(8,128)(2,1)S(1)}, bf16[144,768]{1,0:T(8,128)(2,1)S(1)}, u32[]{:S(2)}, u32[]{:S(2)}) %collective-permute-start.25) | collective-permute-done | bytes 221216 | tf_op jit(solution)/shard_map/ppermute | solution.py:361
  81.1 3.9 %weight_near.1 = (bf16[3,1024,768]{2,1,0:T(8,128)(2,1)}, f32[8,128]{1,0:T(8,128)S(1)}) custom-call(bf16[3,1024,768]{2,1,0:T(8,128)(2,1)S(1)} %get-tuple-element.128.refs_0_, bf16[7,256,256]{2,1,0:T(8,128)(2,1)S(1)} %get-tuple-element.75.refs_6_.refs_1_, bf16[7,256,256]{2,1,0:T(8,128)(2,1)S(1)} %collective-permute-done.5.refs_0_.refs_7_.refs_2_, ...), custom_call_target="tpu_custom_call" | custom-call | flops 30000001024 | bytes 2097152 | tf_op jit(solution)/shard_map/weight_near/pallas_call | solution.py:338
  85.3 1.1 %combine_gradients.1 = (bf16[128,768]{1,0:T(8,128)(2,1)}, f32[2,128]{1,0:T(2,128)}) custom-call(f32[8,128]{1,0:T(8,128)S(1)} %get-tuple-element.70.refs_0_, bf16[144,768]{1,0:T(8,128)(2,1)S(1)} %get-tuple-element.122.refs_1_, f32[2,128]{1,0:T(2,128)S(1)} %get-tuple-element.123.refs_2_, bf16[64,768]{1,0:T(8,128)(2,1)S(1)} %get-tuple-element.124.refs_3_, ...), custom_call_target="tpu_custom_call" | custom-call | flops 30000001024 | bytes 2097152 | tf_op jit(solution)/shard_map/combine_gradients/pallas_call | solution.py:338
  (51 shorter events, 2.2 us)
Async XLA Ops:
  0.6 20.1 %collective-permute-start.1 = (bf16[3,1024,768]{2,1,0:T(8,128)(2,1)}, bf16[3,1024,768]{2,1,0:T(8,128)(2,1)S(1)}, u32[]{:S(2)}, u32[]{:S(2)}) collective-permute-start(bf16[3,1024,768]{2,1,0:T(8,128)(2,1)} %bitcast.9), channel_id=1, source_target_pairs={{0,1},{1,0},{2,3},{3,2},{4,5},{5,4},{6,7},{7,6},{8,9},{9,8},{10,11... | collective-permute-start | bytes 14155784 | tf_op jit(solution)/shard_map/ppermute | solution.py:364
  1.1 15.4 %collective-permute-start.9 = (bf16[128,768]{1,0:T(8,128)(2,1)}, bf16[128,768]{1,0:T(8,128)(2,1)S(1)}, u32[]{:S(2)}, u32[]{:S(2)}) collective-permute-start(bf16[128,768]{1,0:T(8,128)(2,1)} %refs_3_.1), channel_id=1, source_target_pairs={{0,8},{2,10},{4,12},{6,14},{8,0},{10,2},{12,4},{14,6},{1,9},{3,11}... | collective-permute-start | bytes 589832 | tf_op jit(solution)/shard_map/ppermute | solution.py:361
  4.8 2.3 %copy-start = (bf16[1,1024,3,768]{3,1,2,0:T(8,128)(2,1)S(1)}, bf16[1,1024,3,768]{3,1,2,0:T(8,128)(2,1)}, u32[]{:S(2)}) copy-start(bf16[1,1024,3,768]{3,1,2,0:T(8,128)(2,1)} %param.9) | copy-start | bytes 14155780
  7.2 0.9 %copy-start.1 = (bf16[128,768]{1,0:T(8,128)(2,1)S(1)}, bf16[128,768]{1,0:T(8,128)(2,1)}, u32[]{:S(2)}) copy-start(bf16[128,768]{1,0:T(8,128)(2,1)} %refs_3_.1) | copy-start | bytes 589828
  8.1 0.7 copy-start.3
  8.8 0.7 copy-start.4
  9.8 5.1 %collective-permute-start = (f32[8,128]{1,0:T(8,128)S(1)}, f32[8,128]{1,0:T(8,128)S(1)}, u32[]{:S(2)}, u32[]{:S(2)}) collective-permute-start(f32[8,128]{1,0:T(8,128)S(1)} %get-tuple-element.70.refs_0_), channel_id=1, source_target_pairs={{0,8},{2,10},{4,12},{6,14},{8,0},{10,2},{12,4},{14,6},{1,9},{3,11}... | collective-permute-start | bytes 12296 | tf_op jit(solution)/shard_map/ppermute | solution.py:361
  9.9 8.1 %collective-permute-start.2 = (bf16[64,768]{1,0:T(8,128)(2,1)S(1)}, bf16[64,768]{1,0:T(8,128)(2,1)S(1)}, u32[]{:S(2)}, u32[]{:S(2)}) collective-permute-start(bf16[64,768]{1,0:T(8,128)(2,1)S(1)} %get-tuple-element.72), channel_id=1, source_target_pairs={{0,6},{2,4},{4,2},{6,0},{8,14},{10,12},{12,10},{14,8},{1,7},{3,5},... | collective-permute-start | bytes 294920 | tf_op jit(solution)/shard_map/ppermute | solution.py:356
  12.8 6.4 %collective-permute-start.3 = (bf16[64,768]{1,0:T(8,128)(2,1)S(1)}, bf16[64,768]{1,0:T(8,128)(2,1)S(1)}, u32[]{:S(2)}, u32[]{:S(2)}) collective-permute-start(bf16[64,768]{1,0:T(8,128)(2,1)S(1)} %get-tuple-element.73), channel_id=1, source_target_pairs={{0,4},{2,6},{4,0},{6,2},{8,12},{10,14},{12,8},{14,10},{1,5},{3,7},... | collective-permute-start | bytes 294920 | tf_op jit(solution)/shard_map/ppermute | solution.py:356
  14.9 5.8 %slice-start = ((s8[4718592]{0:T(1024)(128)(4,1)}), s8[4194304]{0:T(1024)(128)(4,1)S(1)}, s32[]{:S(2)}) async-start(s8[4718592]{0:T(1024)(128)(4,1)} %bitcast.11), calls=%async_computation | async-start | bytes 8388608
  14.9 5.8 %slice-start.1 = ((s8[4718592]{0:T(1024)(128)(4,1)}), s8[524288]{0:T(1024)(128)(4,1)S(1)}, s32[]{:S(2)}) async-start(s8[4718592]{0:T(1024)(128)(4,1)} %bitcast.11), calls=%async_computation.1 | async-start | bytes 1048576
  14.9 5.8 %collective-permute-start.4 = (bf16[64,768]{1,0:T(8,128)(2,1)S(1)}, bf16[64,768]{1,0:T(8,128)(2,1)S(1)}, u32[]{:S(2)}, u32[]{:S(2)}) collective-permute-start(bf16[64,768]{1,0:T(8,128)(2,1)S(1)} %get-tuple-element.74), channel_id=1, source_target_pairs={{0,2},{2,0},{4,6},{6,4},{8,10},{10,8},{12,14},{14,12},{1,3},{3,1},... | collective-permute-start | bytes 294920 | tf_op jit(solution)/shard_map/ppermute | solution.py:356
  16.9 10.7 %collective-permute-start.10 = (bf16[64,768]{1,0:T(8,128)(2,1)S(1)}, bf16[64,768]{1,0:T(8,128)(2,1)S(1)}, u32[]{:S(2)}, u32[]{:S(2)}) collective-permute-start(bf16[64,768]{1,0:T(8,128)(2,1)S(1)} %get-tuple-element.81), channel_id=1, source_target_pairs={{0,6},{2,4},{4,2},{6,0},{8,14},{10,12},{12,10},{14,8},{1,7},{3,5},... | collective-permute-start | bytes 294920 | tf_op jit(solution)/shard_map/ppermute | solution.py:356
  18.0 9.7 %collective-permute-start.11 = (bf16[64,768]{1,0:T(8,128)(2,1)S(1)}, bf16[64,768]{1,0:T(8,128)(2,1)S(1)}, u32[]{:S(2)}, u32[]{:S(2)}) collective-permute-start(bf16[64,768]{1,0:T(8,128)(2,1)S(1)} %get-tuple-element.82), channel_id=1, source_target_pairs={{0,4},{2,6},{4,0},{6,2},{8,12},{10,14},{12,8},{14,10},{1,5},{3,7},... | collective-permute-start | bytes 294920 | tf_op jit(solution)/shard_map/ppermute | solution.py:356
  19.1 8.6 %collective-permute-start.12 = (bf16[64,768]{1,0:T(8,128)(2,1)S(1)}, bf16[64,768]{1,0:T(8,128)(2,1)S(1)}, u32[]{:S(2)}, u32[]{:S(2)}) collective-permute-start(bf16[64,768]{1,0:T(8,128)(2,1)S(1)} %get-tuple-element.83), channel_id=1, source_target_pairs={{0,2},{2,0},{4,6},{6,4},{8,10},{10,8},{12,14},{14,12},{1,3},{3,1},... | collective-permute-start | bytes 294920 | tf_op jit(solution)/shard_map/ppermute | solution.py:356
  24.1 7.0 %collective-permute-start.6 = (bf16[64,768]{1,0:T(8,128)(2,1)S(1)}, bf16[64,768]{1,0:T(8,128)(2,1)S(1)}, u32[]{:S(2)}, u32[]{:S(2)}) collective-permute-start(bf16[64,768]{1,0:T(8,128)(2,1)S(1)} %get-tuple-element.77), channel_id=1, source_target_pairs={{0,6},{2,4},{4,2},{6,0},{8,14},{10,12},{12,10},{14,8},{1,7},{3,5},... | collective-permute-start | bytes 294920 | tf_op jit(solution)/shard_map/ppermute | solution.py:356
  26.5 4.8 %collective-permute-start.7 = (bf16[64,768]{1,0:T(8,128)(2,1)S(1)}, bf16[64,768]{1,0:T(8,128)(2,1)S(1)}, u32[]{:S(2)}, u32[]{:S(2)}) collective-permute-start(bf16[64,768]{1,0:T(8,128)(2,1)S(1)} %get-tuple-element.78), channel_id=1, source_target_pairs={{0,4},{2,6},{4,0},{6,2},{8,12},{10,14},{12,8},{14,10},{1,5},{3,7},... | collective-permute-start | bytes 294920 | tf_op jit(solution)/shard_map/ppermute | solution.py:356
  27.6 4.6 %collective-permute-start.8 = (bf16[64,768]{1,0:T(8,128)(2,1)S(1)}, bf16[64,768]{1,0:T(8,128)(2,1)S(1)}, u32[]{:S(2)}, u32[]{:S(2)}) collective-permute-start(bf16[64,768]{1,0:T(8,128)(2,1)S(1)} %get-tuple-element.79), channel_id=1, source_target_pairs={{0,2},{2,0},{4,6},{6,4},{8,10},{10,8},{12,14},{14,12},{1,3},{3,1},... | collective-permute-start | bytes 294920 | tf_op jit(solution)/shard_map/ppermute | solution.py:356
  27.7 7.3 %collective-permute-start.5 = (bf16[7,256,256]{2,1,0:T(8,128)(2,1)S(1)}, bf16[7,256,256]{2,1,0:T(8,128)(2,1)S(1)}, u32[]{:S(2)}, u32[]{:S(2)}) collective-permute-start(bf16[7,256,256]{2,1,0:T(8,128)(2,1)S(1)} %get-tuple-element.75.refs_6_.refs_1_), channel_id=1, source_target_pairs={{0,1},{1,0},{2,3},{3,2},{4,5},{5,4},{6,7},{7,6},{8,9},{9,8},{10,11... | collective-permute-start | bytes 2752520 | tf_op jit(solution)/shard_map/ppermute | solution.py:364
  27.7 4.5 %copy-start.2 = (bf16[128,768]{1,0:T(8,128)(2,1)S(1)}, bf16[128,768]{1,0:T(8,128)(2,1)}, u32[]{:S(2)}) copy-start(bf16[128,768]{1,0:T(8,128)(2,1)} %refs_1_.3) | copy-start | bytes 589828
  32.7 11.6 %collective-permute-start.13 = (bf16[128,768]{1,0:T(8,128)(2,1)S(1)}, bf16[128,768]{1,0:T(8,128)(2,1)S(1)}, u32[]{:S(2)}, u32[]{:S(2)}) collective-permute-start(bf16[128,768]{1,0:T(8,128)(2,1)S(1)} %get-tuple-element.93), channel_id=1, source_target_pairs={{0,8},{2,10},{4,12},{6,14},{8,0},{10,2},{12,4},{14,6},{1,9},{3,11}... | collective-permute-start | bytes 589832 | tf_op jit(solution)/shard_map/ppermute | solution.py:361
  34.9 9.4 %collective-permute-start.17 = (bf16[7,256,256]{2,1,0:T(8,128)(2,1)S(1)}, bf16[7,256,256]{2,1,0:T(8,128)(2,1)S(1)}, u32[]{:S(2)}, u32[]{:S(2)}) collective-permute-start(bf16[7,256,256]{2,1,0:T(8,128)(2,1)S(1)} %get-tuple-element.97.refs_0_), channel_id=1, source_target_pairs={{0,1},{1,0},{2,3},{3,2},{4,5},{5,4},{6,7},{7,6},{8,9},{9,8},{10,11... | collective-permute-start | bytes 2752520 | tf_op jit(solution)/shard_map/ppermute | solution.py:364
  35.0 9.4 %collective-permute-start.14 = (bf16[64,768]{1,0:T(8,128)(2,1)S(1)}, bf16[64,768]{1,0:T(8,128)(2,1)S(1)}, u32[]{:S(2)}, u32[]{:S(2)}) collective-permute-start(bf16[64,768]{1,0:T(8,128)(2,1)S(1)} %get-tuple-element.94), channel_id=1, source_target_pairs={{0,6},{2,4},{4,2},{6,0},{8,14},{10,12},{12,10},{14,8},{1,7},{3,5},... | collective-permute-start | bytes 294920 | tf_op jit(solution)/shard_map/ppermute | solution.py:356
  37.5 8.3 %collective-permute-start.15 = (bf16[64,768]{1,0:T(8,128)(2,1)S(1)}, bf16[64,768]{1,0:T(8,128)(2,1)S(1)}, u32[]{:S(2)}, u32[]{:S(2)}) collective-permute-start(bf16[64,768]{1,0:T(8,128)(2,1)S(1)} %get-tuple-element.95), channel_id=1, source_target_pairs={{0,4},{2,6},{4,0},{6,2},{8,12},{10,14},{12,8},{14,10},{1,5},{3,7},... | collective-permute-start | bytes 294920 | tf_op jit(solution)/shard_map/ppermute | solution.py:356
  37.5 8.3 %collective-permute-start.16 = (bf16[64,768]{1,0:T(8,128)(2,1)S(1)}, bf16[64,768]{1,0:T(8,128)(2,1)S(1)}, u32[]{:S(2)}, u32[]{:S(2)}) collective-permute-start(bf16[64,768]{1,0:T(8,128)(2,1)S(1)} %get-tuple-element.96), channel_id=1, source_target_pairs={{0,2},{2,0},{4,6},{6,4},{8,10},{10,8},{12,14},{14,12},{1,3},{3,1},... | collective-permute-start | bytes 294920 | tf_op jit(solution)/shard_map/ppermute | solution.py:356
  46.6 6.4 %collective-permute-start.19 = (bf16[64,768]{1,0:T(8,128)(2,1)S(1)}, bf16[64,768]{1,0:T(8,128)(2,1)S(1)}, u32[]{:S(2)}, u32[]{:S(2)}) collective-permute-start(bf16[64,768]{1,0:T(8,128)(2,1)S(1)} %get-tuple-element.102), channel_id=1, source_target_pairs={{0,6},{2,4},{4,2},{6,0},{8,14},{10,12},{12,10},{14,8},{1,7},{3,5},... | collective-permute-start | bytes 294920 | tf_op jit(solution)/shard_map/ppermute | solution.py:356
  47.7 7.7 %collective-permute-start.20 = (bf16[64,768]{1,0:T(8,128)(2,1)S(1)}, bf16[64,768]{1,0:T(8,128)(2,1)S(1)}, u32[]{:S(2)}, u32[]{:S(2)}) collective-permute-start(bf16[64,768]{1,0:T(8,128)(2,1)S(1)} %get-tuple-element.103), channel_id=1, source_target_pairs={{0,4},{2,6},{4,0},{6,2},{8,12},{10,14},{12,8},{14,10},{1,5},{3,7},... | collective-permute-start | bytes 294920 | tf_op jit(solution)/shard_map/ppermute | solution.py:356
  49.2 6.3 %collective-permute-start.21 = (bf16[64,768]{1,0:T(8,128)(2,1)S(1)}, bf16[64,768]{1,0:T(8,128)(2,1)S(1)}, u32[]{:S(2)}, u32[]{:S(2)}) collective-permute-start(bf16[64,768]{1,0:T(8,128)(2,1)S(1)} %get-tuple-element.104), channel_id=1, source_target_pairs={{0,2},{2,0},{4,6},{6,4},{8,10},{10,8},{12,14},{14,12},{1,3},{3,1},... | collective-permute-start | bytes 294920 | tf_op jit(solution)/shard_map/ppermute | solution.py:356
  50.1 12.7 %collective-permute-start.18 = (bf16[128,768]{1,0:T(8,128)(2,1)S(1)}, bf16[128,768]{1,0:T(8,128)(2,1)S(1)}, u32[]{:S(2)}, u32[]{:S(2)}) collective-permute-start(bf16[128,768]{1,0:T(8,128)(2,1)S(1)} %get-tuple-element.98), channel_id=1, source_target_pairs={{0,8},{2,10},{4,12},{6,14},{8,0},{10,2},{12,4},{14,6},{1,9},{3,11}... | collective-permute-start | bytes 589832 | tf_op jit(solution)/shard_map/ppermute | solution.py:361
  59.2 10.1 %collective-permute-start.29 = (bf16[11,256,256]{2,1,0:T(8,128)(2,1)S(1)}, bf16[11,256,256]{2,1,0:T(8,128)(2,1)S(1)}, u32[]{:S(2)}, u32[]{:S(2)}) collective-permute-start(bf16[11,256,256]{2,1,0:T(8,128)(2,1)S(1)} %get-tuple-element.118.refs_2_), channel_id=1, source_target_pairs={{0,1},{1,0},{2,3},{3,2},{4,5},{5,4},{6,7},{7,6},{8,9},{9,8},{10,11... | collective-permute-start | bytes 4325384 | tf_op jit(solution)/shard_map/ppermute | solution.py:364
  59.3 6.6 %collective-permute-start.22 = (bf16[64,768]{1,0:T(8,128)(2,1)S(1)}, bf16[64,768]{1,0:T(8,128)(2,1)S(1)}, u32[]{:S(2)}, u32[]{:S(2)}) collective-permute-start(bf16[64,768]{1,0:T(8,128)(2,1)S(1)} %get-tuple-element.109), channel_id=1, source_target_pairs={{0,6},{2,4},{4,2},{6,0},{8,14},{10,12},{12,10},{14,8},{1,7},{3,5},... | collective-permute-start | bytes 294920 | tf_op jit(solution)/shard_map/ppermute | solution.py:356
  59.4 7.3 %collective-permute-start.23 = (bf16[64,768]{1,0:T(8,128)(2,1)S(1)}, bf16[64,768]{1,0:T(8,128)(2,1)S(1)}, u32[]{:S(2)}, u32[]{:S(2)}) collective-permute-start(bf16[64,768]{1,0:T(8,128)(2,1)S(1)} %get-tuple-element.110), channel_id=1, source_target_pairs={{0,4},{2,6},{4,0},{6,2},{8,12},{10,14},{12,8},{14,10},{1,5},{3,7},... | collective-permute-start | bytes 294920 | tf_op jit(solution)/shard_map/ppermute | solution.py:356
  61.2 7.2 %collective-permute-start.24 = (bf16[64,768]{1,0:T(8,128)(2,1)S(1)}, bf16[64,768]{1,0:T(8,128)(2,1)S(1)}, u32[]{:S(2)}, u32[]{:S(2)}) collective-permute-start(bf16[64,768]{1,0:T(8,128)(2,1)S(1)} %get-tuple-element.111), channel_id=1, source_target_pairs={{0,2},{2,0},{4,6},{6,4},{8,10},{10,8},{12,14},{14,12},{1,3},{3,1},... | collective-permute-start | bytes 294920 | tf_op jit(solution)/shard_map/ppermute | solution.py:356
  64.1 7.9 %collective-permute-start.26 = (bf16[64,768]{1,0:T(8,128)(2,1)S(1)}, bf16[64,768]{1,0:T(8,128)(2,1)S(1)}, u32[]{:S(2)}, u32[]{:S(2)}) collective-permute-start(bf16[64,768]{1,0:T(8,128)(2,1)S(1)} %get-tuple-element.115), channel_id=1, source_target_pairs={{0,6},{2,4},{4,2},{6,0},{8,14},{10,12},{12,10},{14,8},{1,7},{3,5},... | collective-permute-start | bytes 294920 | tf_op jit(solution)/shard_map/ppermute | solution.py:356
  65.9 6.1 %collective-permute-start.27 = (bf16[64,768]{1,0:T(8,128)(2,1)S(1)}, bf16[64,768]{1,0:T(8,128)(2,1)S(1)}, u32[]{:S(2)}, u32[]{:S(2)}) collective-permute-start(bf16[64,768]{1,0:T(8,128)(2,1)S(1)} %get-tuple-element.116), channel_id=1, source_target_pairs={{0,4},{2,6},{4,0},{6,2},{8,12},{10,14},{12,8},{14,10},{1,5},{3,7},... | collective-permute-start | bytes 294920 | tf_op jit(solution)/shard_map/ppermute | solution.py:356
  66.7 5.3 %collective-permute-start.28 = (bf16[64,768]{1,0:T(8,128)(2,1)S(1)}, bf16[64,768]{1,0:T(8,128)(2,1)S(1)}, u32[]{:S(2)}, u32[]{:S(2)}) collective-permute-start(bf16[64,768]{1,0:T(8,128)(2,1)S(1)} %get-tuple-element.117), channel_id=1, source_target_pairs={{0,2},{2,0},{4,6},{6,4},{8,10},{10,8},{12,14},{14,12},{1,3},{3,1},... | collective-permute-start | bytes 294920 | tf_op jit(solution)/shard_map/ppermute | solution.py:356
  68.7 12.3 %collective-permute-start.25 = (bf16[144,768]{1,0:T(8,128)(2,1)S(1)}, bf16[144,768]{1,0:T(8,128)(2,1)S(1)}, u32[]{:S(2)}, u32[]{:S(2)}) collective-permute-start(bf16[144,768]{1,0:T(8,128)(2,1)S(1)} %far_back.1.refs_6_.refs_8_), channel_id=1, source_target_pairs={{0,8},{2,10},{4,12},{6,14},{8,0},{10,2},{12,4},{14,6},{1,9},{3,11}... | collective-permute-start | bytes 663560 | tf_op jit(solution)/shard_map/ppermute | solution.py:361
  75.8 5.3 %collective-permute-start.33 = (bf16[11,256,256]{2,1,0:T(8,128)(2,1)S(1)}, bf16[11,256,256]{2,1,0:T(8,128)(2,1)S(1)}, u32[]{:S(2)}, u32[]{:S(2)}) collective-permute-start(bf16[11,256,256]{2,1,0:T(8,128)(2,1)S(1)} %get-tuple-element.129.refs_3_), channel_id=1, source_target_pairs={{0,1},{1,0},{2,3},{3,2},{4,5},{5,4},{6,7},{7,6},{8,9},{9,8},{10,11... | collective-permute-start | bytes 4325384 | tf_op jit(solution)/shard_map/ppermute | solution.py:364
  75.9 9.1 %collective-permute-start.30 = (bf16[64,768]{1,0:T(8,128)(2,1)S(1)}, bf16[64,768]{1,0:T(8,128)(2,1)S(1)}, u32[]{:S(2)}, u32[]{:S(2)}) collective-permute-start(bf16[64,768]{1,0:T(8,128)(2,1)S(1)} %get-tuple-element.125), channel_id=1, source_target_pairs={{0,6},{2,4},{4,2},{6,0},{8,14},{10,12},{12,10},{14,8},{1,7},{3,5},... | collective-permute-start | bytes 294920 | tf_op jit(solution)/shard_map/ppermute | solution.py:356
  78.8 6.4 %collective-permute-start.31 = (bf16[64,768]{1,0:T(8,128)(2,1)S(1)}, bf16[64,768]{1,0:T(8,128)(2,1)S(1)}, u32[]{:S(2)}, u32[]{:S(2)}) collective-permute-start(bf16[64,768]{1,0:T(8,128)(2,1)S(1)} %get-tuple-element.126), channel_id=1, source_target_pairs={{0,4},{2,6},{4,0},{6,2},{8,12},{10,14},{12,8},{14,10},{1,5},{3,7},... | collective-permute-start | bytes 294920 | tf_op jit(solution)/shard_map/ppermute | solution.py:356
  79.4 5.9 %collective-permute-start.32 = (bf16[64,768]{1,0:T(8,128)(2,1)S(1)}, bf16[64,768]{1,0:T(8,128)(2,1)S(1)}, u32[]{:S(2)}, u32[]{:S(2)}) collective-permute-start(bf16[64,768]{1,0:T(8,128)(2,1)S(1)} %get-tuple-element.127), channel_id=1, source_target_pairs={{0,2},{2,0},{4,6},{6,4},{8,10},{10,8},{12,14},{14,12},{1,3},{3,1},... | collective-permute-start | bytes 294920 | tf_op jit(solution)/shard_map/ppermute | solution.py:356

commit v12 on v11

--- a/solution.py
+++ b/solution.py
@@ -89,8 +89,11 @@
     return jnp.concatenate([ref[...] for ref in refs], axis=0)
 
 
-def masks_of(meta, refs):
-    return slot_masks(lax.axis_index("expert"), meta, len(refs), refs[0].shape[0])
+def keep_masks(masks_ref, meta, refs):
+    m0, m1 = slot_masks(lax.axis_index("expert"), meta, len(refs), refs[0].shape[0])
+    masks_ref[0] = m0
+    masks_ref[1] = m1
+    return m0 + m1
 
 
 def gate_columns(meta):
@@ -98,8 +101,8 @@
     return columns[:, 2:3], columns[:, 3:4]
 
 
-def route_sums(meta, refs):
-    m0, m1 = masks_of(meta, refs)
+def route_sums(meta, masks_ref, refs):
+    m0, m1 = masks_ref[0], masks_ref[1]
     got = get(refs)
     g0, g1 = gate_columns(meta)
     o0, o1 = dot(m0, got, FIRST), dot(m1, got, FIRST)
@@ -119,7 +122,9 @@
     put(refs, dot(jnp.concatenate([m0, m1], axis=1), grads))
 
 
-def pack_near_kernel(own_ref, routes_ref, gates_ref, tokens_ref, meta_ref, *rows_refs):
+def pack_near_kernel(
+    own_ref, routes_ref, gates_ref, tokens_ref, meta_ref, masks_ref, *rows_refs
+):
     del own_ref
     meta = jnp.concatenate(
         [
@@ -130,13 +135,11 @@
         axis=0,
     )
     meta_ref[...] = meta
-    m0, m1 = masks_of(meta, rows_refs)
-    put(rows_refs, dot(m0 + m1, tokens_ref[...]))
-
-
-def pack_far_kernel(meta_ref, tokens_ref, *rows_refs):
-    m0, m1 = masks_of(meta_ref[...], rows_refs)
-    put(rows_refs, dot(m0 + m1, tokens_ref[...]))
+    put(rows_refs, dot(keep_masks(masks_ref, meta, rows_refs), tokens_ref[...]))
+
+
+def pack_far_kernel(meta_ref, tokens_ref, masks_ref, *rows_refs):
+    put(rows_refs, dot(keep_masks(masks_ref, meta_ref[...], rows_refs), tokens_ref[...]))
 
 
 def forward_kernel(pieces, own_ref, other_ref, *refs):
@@ -181,34 +184,34 @@
     )
 
 
-def near_sum_kernel(meta_ref, teacher_ref, *refs):
+def near_sum_kernel(meta_ref, masks_ref, teacher_ref, *refs):
     ins, out_ref = refs[:-1], refs[-1]
-    total = route_sums(meta_ref[...], ins)[-1]
+    total = route_sums(meta_ref[...], masks_ref, ins)[-1]
     out_ref[...] = (total - teacher_ref[...].astype(F32)).astype(BF16)
 
 
-def far_grad_kernel(pieces, meta_ref, rest_ref, *refs):
+def far_grad_kernel(pieces, meta_ref, masks_ref, rest_ref, *refs):
     ins, part_ref, d_gates_ref, outs = (
         refs[:pieces],
         refs[pieces],
         refs[pieces + 1],
         refs[pieces + 2 :],
     )
-    m0, m1, g0, g1, o0, o1, total = route_sums(meta_ref[...], ins)
+    m0, m1, g0, g1, o0, o1, total = route_sums(meta_ref[...], masks_ref, ins)
     part_ref[...] = total.astype(BF16)
     diff = total + rest_ref[...].astype(F32)
     put_route_grads(outs, m0, m1, g0, g1, diff)
     put_d_gates(d_gates_ref, diff, o0, o1)
 
 
-def near_grad_kernel(pieces, meta_ref, teacher_ref, part_ref, *refs):
+def near_grad_kernel(pieces, meta_ref, masks_ref, teacher_ref, part_ref, *refs):
     ins, student_ref, d_gates_ref, outs = (
         refs[:pieces],
         refs[pieces],
         refs[pieces + 1],
         refs[pieces + 2 :],
     )
-    m0, m1, g0, g1, o0, o1, total = route_sums(meta_ref[...], ins)
+    m0, m1, g0, g1, o0, o1, total = route_sums(meta_ref[...], masks_ref, ins)
     total = total + part_ref[...].astype(F32)
     student_ref[...] = total.astype(BF16)
     diff = total - teacher_ref[...].astype(F32)
@@ -216,11 +219,10 @@
     put_d_gates(d_gates_ref, diff, o0, o1)
 
 
-def far_back_kernel(meta_ref, d_gates_ref, *refs):
+def far_back_kernel(masks_ref, d_gates_ref, *refs):
     ins, out_ref = refs[:-1], refs[-1]
-    m0, m1 = masks_of(meta_ref[...], ins)
-    tok = m0.shape[1]
-    out_ref[:tok, :] = dot(m0 + m1, get(ins), FIRST).astype(BF16)
+    tok = masks_ref.shape[2]
+    out_ref[:tok, :] = dot(masks_ref[0] + masks_ref[1], get(ins), FIRST).astype(BF16)
     value = d_gates_ref[...]
     high = value.astype(BF16)
     low = (value - high.astype(F32)).astype(BF16)
@@ -229,14 +231,16 @@
     out_ref[tok:, tok:] = jnp.zeros((out_ref.shape[0] - tok, out_ref.shape[1] - tok), BF16)
 
 
-def final_kernel(pieces, meta_ref, part_ref, near_ref, *refs):
-    ins, out_ref, d_gates_ref = refs[:pieces], refs[pieces], refs[pieces + 1]
-    m0, m1 = masks_of(meta_ref[...], ins)
-    tok = m0.shape[1]
-    total = dot(m0 + m1, get(ins), FIRST) + part_ref[:tok, :].astype(F32)
+def final_kernel(pieces, masks_ref, part_ref, near_ref, student_ref, *refs):
+    ins, student_hbm, out_ref, d_gates_ref, sem = refs[:pieces], *refs[pieces:]
+    copy = pltpu.make_async_copy(student_ref, student_hbm, sem)
+    copy.start()
+    tok = masks_ref.shape[2]
+    total = dot(masks_ref[0] + masks_ref[1], get(ins), FIRST) + part_ref[:tok, :].astype(F32)
     out_ref[...] = total.astype(BF16)
     far = part_ref[tok:, :tok].astype(F32)
     d_gates_ref[...] = near_ref[...] + (far[0:2] + far[2:4])
+    copy.wait()
 
 
 def weight_blocks(across, x, sent_x, g, sent_g, d, h):
@@ -303,6 +307,7 @@
     sent_g = jax.ShapeDtypeStruct((across + 2 * along, rows, rows), BF16)
     acts2 = jax.ShapeDtypeStruct((2 * units, rows), BF16)
     tiny = jax.ShapeDtypeStruct((8, 128), F32)
+    masks = jax.ShapeDtypeStruct((2, rows, tok), BF16)
     vspec = pl.BlockSpec(memory_space=pltpu.VMEM)
     aspec = pl.BlockSpec(memory_space=pl.ANY)
 
@@ -401,7 +406,7 @@
     res = call(
         pack_near_kernel,
         "pack_near",
-        [jax.ShapeDtypeStruct((8, tok), F32)] + pieces,
+        [jax.ShapeDtypeStruct((8, tok), F32), masks] + pieces,
         [],
         own,
         routes.T,
@@ -409,11 +414,10 @@
         tokens,
         limit=10,
     )
-    meta, x_near = res[0], within_half(res[1:])
+    meta, near_masks, x_near = res[0], res[1], within_half(res[2:])
     far_meta = to_mirror(meta)
-    x_far = within_half(
-        call(pack_far_kernel, "pack_far", pieces, [], far_meta, far_tokens)
-    )
+    res = call(pack_far_kernel, "pack_far", [masks] + pieces, [], far_meta, far_tokens)
+    far_masks, x_far = res[0], within_half(res[1:])
 
     out_near, (xn, hn, fan, fbn) = forward(x_near, "forward_near")
     got_near = within_half(out_near)
@@ -424,6 +428,7 @@
         dense,
         [],
         meta,
+        near_masks,
         teacher,
         *got_near,
         through=out_far,
@@ -440,6 +445,7 @@
         [dense, pair] + pieces,
         [],
         far_meta,
+        far_masks,
         rest,
         *got_far,
         after=[xf_sib, xn_sib],
@@ -452,6 +458,7 @@
         [dense, pair] + pieces,
         [],
         meta,
+        near_masks,
         teacher,
         part,
         *got_near,
@@ -462,7 +469,7 @@
     back_far = within_half(grad_far)
     gf_sib = to_sibling(gf)
     part_rows = call(
-        far_back_kernel, "far_back", longer, [], far_meta, d_gates_far, *back_far
+        far_back_kernel, "far_back", longer, [], far_masks, d_gates_far, *back_far
     )
     part = to_mirror(part_rows)
     far_weights, far_done = call(
@@ -493,16 +500,19 @@
         in_hbm=1,
     )
 
-    d_tokens, d_gates = call(
+    student, d_tokens, d_gates = call(
         functools.partial(final_kernel, half),
         "combine_gradients",
-        [dense, pair],
-        [],
-        meta,
+        [dense, dense, pair],
+        [],
+        near_masks,
         part,
         d_gates_near,
+        student,
         *back_near,
         after=[finished],
+        scratch=[pltpu.SemaphoreType.DMA],
+        in_hbm=1,
     )
     return (student, d_tokens, d_gates.T, weight_grads.transpose(1, 0, 2)[None])
 

time: 86.5 us -> 86.9 us (level)
  transfers between devices with their start and end apart: 34 -> 34, of which waited for: 13 -> 13; matrix products, arithmetic and copies ran while one was open for 0% -> 0% of each run, Pallas kernels for 27% -> 26%
where the time goes in v12:
time: 86.9 us; the launch traced here: 86.7 us
  starting transfers between devices  36.5 us (42%)
  Pallas kernels  24.9 us (29%)
  waiting for transfers between devices  19.5 us (22%)
  local copies, waits for them, and re-layouts  4.63 us (5%)
  between operations  1.01 us (1%)
    ppermute x24, starting transfers between devices, within_half(): lax.ppermute(rows_of[s], 'expert', [(i, i ^ s) for i in range(experts)])  28.3 us
    pallas_call x16, Pallas kernels, call(): pl.pallas_call(body, in_specs=specs + [aspec] * (len(after) + len(through...  24.9 us
    ppermute x24, waiting for transfers between devices, within_half(): lax.ppermute(rows_of[s], 'expert', [(i, i ^ s) for i in range(experts)])  10.7 us
    ppermute x5, waiting for transfers between devices, to_mirror(): return lax.ppermute(x, 'expert', [(i, i ^ half) for i in range(experts)])  8.8 us
    ppermute x5, starting transfers between devices, to_mirror(): return lax.ppermute(x, 'expert', [(i, i ^ half) for i in range(experts)])  7.61 us
    unnamed x14, local copies, waits for them, and re-layouts  4.63 us
  transfers between devices with their start and end apart: 34, of which 13 were waited for; matrix products, arithmetic and copies ran while one was open for 0% of the time, Pallas kernels for 26%

profile of v12, /device:TPU:0, one launch (start us, length us, event | category | flops | bytes accessed | tf_op | source)
XLA Modules:
  0.0 86.7 jit_solution(2803161182248654773)
XLA Ops:
  0.6 0.5 collective-permute-start.2
  1.1 3.7 %collective-permute-start.1 = (bf16[128,768]{1,0:T(8,128)(2,1)}, bf16[128,768]{1,0:T(8,128)(2,1)S(1)}, u32[]{:S(2)}, u32[]{:S(2)}) collective-permute-start(bf16[128,768]{1,0:T(8,128)(2,1)} %refs_3_.1), channel_id=1, source_target_pairs={{0,8},{2,10},{4,12},{6,14},{8,0},{10,2},{12,4},{14,6},{1,9},{3,11}... | collective-permute-start | bytes 589832 | tf_op jit(solution)/shard_map/ppermute | solution.py:366
  4.8 2.3 %copy-done = bf16[1,1024,3,768]{3,1,2,0:T(8,128)(2,1)S(1)} copy-done((bf16[1,1024,3,768]{3,1,2,0:T(8,128)(2,1)S(1)}, bf16[1,1024,3,768]{3,1,2,0:T(8,128)(2,1)}, u32[]{:S(2)}) %copy-start) | copy-done | bytes 4718616
  7.2 0.9 %copy-done.1 = bf16[128,768]{1,0:T(8,128)(2,1)S(1)} copy-done((bf16[128,768]{1,0:T(8,128)(2,1)S(1)}, bf16[128,768]{1,0:T(8,128)(2,1)}, u32[]{:S(2)}) %copy-start.1) | copy-done | bytes 196632
  8.1 0.7 copy-done.3
  8.8 0.7 copy-done.4
  9.4 0.4 pack_near.1
  9.9 2.9 %collective-permute-start.3 = (bf16[64,768]{1,0:T(8,128)(2,1)S(1)}, bf16[64,768]{1,0:T(8,128)(2,1)S(1)}, u32[]{:S(2)}, u32[]{:S(2)}) collective-permute-start(bf16[64,768]{1,0:T(8,128)(2,1)S(1)} %get-tuple-element.77), channel_id=1, source_target_pairs={{0,6},{2,4},{4,2},{6,0},{8,14},{10,12},{12,10},{14,8},{1,7},{3,5},... | collective-permute-start | bytes 294920 | tf_op jit(solution)/shard_map/ppermute | solution.py:361
  12.8 0.5 collective-permute-start.4
  13.2 1.7 %collective-permute-done.refs_0_ = f32[8,128]{1,0:T(8,128)S(1)} collective-permute-done((f32[8,128]{1,0:T(8,128)S(1)}, f32[8,128]{1,0:T(8,128)S(1)}, u32[]{:S(2)}, u32[]{:S(2)}) %collective-permute-start) | collective-permute-done | bytes 4128 | tf_op jit(solution)/shard_map/ppermute | solution.py:366
  14.9 1.6 %collective-permute-start.5 = (bf16[64,768]{1,0:T(8,128)(2,1)S(1)}, bf16[64,768]{1,0:T(8,128)(2,1)S(1)}, u32[]{:S(2)}, u32[]{:S(2)}) collective-permute-start(bf16[64,768]{1,0:T(8,128)(2,1)S(1)} %get-tuple-element.79), channel_id=1, source_target_pairs={{0,2},{2,0},{4,6},{6,4},{8,10},{10,8},{12,14},{14,12},{1,3},{3,1},... | collective-permute-start | bytes 294920 | tf_op jit(solution)/shard_map/ppermute | solution.py:361
  16.5 0.4 pack_far.1
  16.9 1.0 %collective-permute-start.10 = (bf16[64,768]{1,0:T(8,128)(2,1)S(1)}, bf16[64,768]{1,0:T(8,128)(2,1)S(1)}, u32[]{:S(2)}, u32[]{:S(2)}) collective-permute-start(bf16[64,768]{1,0:T(8,128)(2,1)S(1)} %get-tuple-element.86), channel_id=1, source_target_pairs={{0,6},{2,4},{4,2},{6,0},{8,14},{10,12},{12,10},{14,8},{1,7},{3,5},... | collective-permute-start | bytes 294920 | tf_op jit(solution)/shard_map/ppermute | solution.py:361
  18.0 0.8 collective-permute-start.11
  19.1 1.6 %collective-permute-start.12 = (bf16[64,768]{1,0:T(8,128)(2,1)S(1)}, bf16[64,768]{1,0:T(8,128)(2,1)S(1)}, u32[]{:S(2)}, u32[]{:S(2)}) collective-permute-start(bf16[64,768]{1,0:T(8,128)(2,1)S(1)} %get-tuple-element.88), channel_id=1, source_target_pairs={{0,2},{2,0},{4,6},{6,4},{8,10},{10,8},{12,14},{14,12},{1,3},{3,1},... | collective-permute-start | bytes 294920 | tf_op jit(solution)/shard_map/ppermute | solution.py:361
  20.7 3.4 %forward_near.1 = (bf16[64,768]{1,0:T(8,128)(2,1)S(1)}, bf16[64,768]{1,0:T(8,128)(2,1)S(1)}, bf16[64,768]{1,0:T(8,128)(2,1)S(1)}, bf16[64,768]{1,0:T(8,128)(2,1)...) custom-call(bf16[3,1024,768]{2,1,0:T(8,128)(2,1)S(1)} %bitcast.13, ...), custom_call_target="tpu_custom_call" | custom-call | flops 100000000 | bytes 2097152 | tf_op jit(solution)/shard_map/forward_near/pallas_call | solution.py:343
  24.1 2.3 %collective-permute-start.7 = (bf16[64,768]{1,0:T(8,128)(2,1)S(1)}, bf16[64,768]{1,0:T(8,128)(2,1)S(1)}, u32[]{:S(2)}, u32[]{:S(2)}) collective-permute-start(bf16[64,768]{1,0:T(8,128)(2,1)S(1)} %get-tuple-element.82), channel_id=1, source_target_pairs={{0,6},{2,4},{4,2},{6,0},{8,14},{10,12},{12,10},{14,8},{1,7},{3,5},... | collective-permute-start | bytes 294920 | tf_op jit(solution)/shard_map/ppermute | solution.py:361
  26.5 1.2 %collective-permute-start.8 = (bf16[64,768]{1,0:T(8,128)(2,1)S(1)}, bf16[64,768]{1,0:T(8,128)(2,1)S(1)}, u32[]{:S(2)}, u32[]{:S(2)}) collective-permute-start(bf16[64,768]{1,0:T(8,128)(2,1)S(1)} %get-tuple-element.83), channel_id=1, source_target_pairs={{0,4},{2,6},{4,0},{6,2},{8,12},{10,14},{12,8},{14,10},{1,5},{3,7},... | collective-permute-start | bytes 294920 | tf_op jit(solution)/shard_map/ppermute | solution.py:361
  27.7 3.4 %forward_far.1 = (bf16[64,768]{1,0:T(8,128)(2,1)S(1)}, bf16[64,768]{1,0:T(8,128)(2,1)S(1)}, bf16[64,768]{1,0:T(8,128)(2,1)S(1)}, bf16[64,768]{1,0:T(8,128)(2,1)S...) custom-call(bf16[3,1024,768]{2,1,0:T(8,128)(2,1)S(1)} %bitcast.14, ...), custom_call_target="tpu_custom_call" | custom-call | flops 3000000000 | bytes 2097152 | tf_op jit(solution)/shard_map/forward_far/pallas_call | solution.py:343
  31.3 1.0 %collective-permute-done.9.refs_6_.refs_7_ = bf16[64,768]{1,0:T(8,128)(2,1)S(1)} collective-permute-done((bf16[64,768]{1,0:T(8,128)(2,1)S(1)}, bf16[64,768]{1,0:T(8,128)(2,1)S(1)}, u32[]{:S(2)}, u32[]{:S(2)}) %collective-permute-start.9) | collective-permute-done | bytes 98336 | tf_op jit(solution)/shard_map/ppermute | solution.py:361
  32.6 2.2 %collective-permute-start.13 = (bf16[128,768]{1,0:T(8,128)(2,1)S(1)}, bf16[128,768]{1,0:T(8,128)(2,1)S(1)}, u32[]{:S(2)}, u32[]{:S(2)}) collective-permute-start(bf16[128,768]{1,0:T(8,128)(2,1)S(1)} %get-tuple-element.98), channel_id=1, source_target_pairs={{0,8},{2,10},{4,12},{6,14},{8,0},{10,2},{12,4},{14,6},{1,9},{3,11}... | collective-permute-start | bytes 589832 | tf_op jit(solution)/shard_map/ppermute | solution.py:366
  34.8 2.6 %collective-permute-start.14 = (bf16[64,768]{1,0:T(8,128)(2,1)S(1)}, bf16[64,768]{1,0:T(8,128)(2,1)S(1)}, u32[]{:S(2)}, u32[]{:S(2)}) collective-permute-start(bf16[64,768]{1,0:T(8,128)(2,1)S(1)} %get-tuple-element.99), channel_id=1, source_target_pairs={{0,6},{2,4},{4,2},{6,0},{8,14},{10,12},{12,10},{14,8},{1,7},{3,5},... | collective-permute-start | bytes 294920 | tf_op jit(solution)/shard_map/ppermute | solution.py:361
  37.4 0.9 %collective-permute-start.16 = (bf16[64,768]{1,0:T(8,128)(2,1)S(1)}, bf16[64,768]{1,0:T(8,128)(2,1)S(1)}, u32[]{:S(2)}, u32[]{:S(2)}) collective-permute-start(bf16[64,768]{1,0:T(8,128)(2,1)S(1)} %get-tuple-element.101), channel_id=1, source_target_pairs={{0,2},{2,0},{4,6},{6,4},{8,10},{10,8},{12,14},{14,12},{1,3},{3,1},... | collective-permute-start | bytes 294920 | tf_op jit(solution)/shard_map/ppermute | solution.py:361
  38.3 5.9 %collective-permute-done.13.refs_1_ = bf16[128,768]{1,0:T(8,128)(2,1)S(1)} collective-permute-done((bf16[128,768]{1,0:T(8,128)(2,1)S(1)}, bf16[128,768]{1,0:T(8,128)(2,1)S(1)}, u32[]{:S(2)}, u32[]{:S(2)}) %collective-permute-start.13) | collective-permute-done | bytes 196640 | tf_op jit(solution)/shard_map/ppermute | solution.py:366
  44.2 1.5 %collective-permute-done.15.refs_5_ = bf16[64,768]{1,0:T(8,128)(2,1)S(1)} collective-permute-done((bf16[64,768]{1,0:T(8,128)(2,1)S(1)}, bf16[64,768]{1,0:T(8,128)(2,1)S(1)}, u32[]{:S(2)}, u32[]{:S(2)}) %collective-permute-start.15) | collective-permute-done | bytes 98336 | tf_op jit(solution)/shard_map/ppermute | solution.py:361
  45.7 0.6 far_grad.1
  46.3 1.1 %collective-permute-start.18 = (bf16[64,768]{1,0:T(8,128)(2,1)S(1)}, bf16[64,768]{1,0:T(8,128)(2,1)S(1)}, u32[]{:S(2)}, u32[]{:S(2)}) collective-permute-start(bf16[64,768]{1,0:T(8,128)(2,1)S(1)} %get-tuple-element.107), channel_id=1, source_target_pairs={{0,6},{2,4},{4,2},{6,0},{8,14},{10,12},{12,10},{14,8},{1,7},{3,5},... | collective-permute-start | bytes 294920 | tf_op jit(solution)/shard_map/ppermute | solution.py:361
  47.4 1.5 %collective-permute-start.19 = (bf16[64,768]{1,0:T(8,128)(2,1)S(1)}, bf16[64,768]{1,0:T(8,128)(2,1)S(1)}, u32[]{:S(2)}, u32[]{:S(2)}) collective-permute-start(bf16[64,768]{1,0:T(8,128)(2,1)S(1)} %get-tuple-element.108), channel_id=1, source_target_pairs={{0,4},{2,6},{4,0},{6,2},{8,12},{10,14},{12,8},{14,10},{1,5},{3,7},... | collective-permute-start | bytes 294920 | tf_op jit(solution)/shard_map/ppermute | solution.py:361
  48.9 0.9 %collective-permute-start.20 = (bf16[64,768]{1,0:T(8,128)(2,1)S(1)}, bf16[64,768]{1,0:T(8,128)(2,1)S(1)}, u32[]{:S(2)}, u32[]{:S(2)}) collective-permute-start(bf16[64,768]{1,0:T(8,128)(2,1)S(1)} %get-tuple-element.109), channel_id=1, source_target_pairs={{0,2},{2,0},{4,6},{6,4},{8,10},{10,8},{12,14},{14,12},{1,3},{3,1},... | collective-permute-start | bytes 294920 | tf_op jit(solution)/shard_map/ppermute | solution.py:361
  49.9 1.1 %collective-permute-start.25 = (bf16[128,768]{1,0:T(8,128)(2,1)S(1)}, bf16[128,768]{1,0:T(8,128)(2,1)S(1)}, u32[]{:S(2)}, u32[]{:S(2)}) collective-permute-start(bf16[128,768]{1,0:T(8,128)(2,1)S(1)} %get-tuple-element.116), channel_id=1, source_target_pairs={{0,8},{2,10},{4,12},{6,14},{8,0},{10,2},{12,4},{14,6},{1,9},{3,11}... | collective-permute-start | bytes 589832 | tf_op jit(solution)/shard_map/ppermute | solution.py:366
  50.9 1.8 %collective-permute-done.18.refs_5_ = bf16[64,768]{1,0:T(8,128)(2,1)S(1)} collective-permute-done((bf16[64,768]{1,0:T(8,128)(2,1)S(1)}, bf16[64,768]{1,0:T(8,128)(2,1)S(1)}, u32[]{:S(2)}, u32[]{:S(2)}) %collective-permute-start.18) | collective-permute-done | bytes 98336 | tf_op jit(solution)/shard_map/ppermute | solution.py:361
  52.7 2.4 %collective-permute-done.19.refs_6_ = bf16[64,768]{1,0:T(8,128)(2,1)S(1)} collective-permute-done((bf16[64,768]{1,0:T(8,128)(2,1)S(1)}, bf16[64,768]{1,0:T(8,128)(2,1)S(1)}, u32[]{:S(2)}, u32[]{:S(2)}) %collective-permute-start.19) | collective-permute-done | bytes 98336 | tf_op jit(solution)/shard_map/ppermute | solution.py:361
  55.2 3.8 %backward_far.1 = (bf16[64,768]{1,0:T(8,128)(2,1)S(1)}, bf16[64,768]{1,0:T(8,128)(2,1)S(1)}, bf16[64,768]{1,0:T(8,128)(2,1)S(1)}, bf16[64,768]{1,0:T(8,128)(2,1)...) custom-call(bf16[3,1024,768]{2,1,0:T(8,128)(2,1)S(1)} %bitcast.15, ...), custom_call_target="tpu_custom_call" | custom-call | flops 3000000000 | bytes 2097152 | tf_op jit(solution)/shard_map/backward_far/pallas_call | solution.py:343
  59.1 1.8 %collective-permute-start.22 = (bf16[64,768]{1,0:T(8,128)(2,1)S(1)}, bf16[64,768]{1,0:T(8,128)(2,1)S(1)}, u32[]{:S(2)}, u32[]{:S(2)}) collective-permute-start(bf16[64,768]{1,0:T(8,128)(2,1)S(1)} %get-tuple-element.112), channel_id=1, source_target_pairs={{0,4},{2,6},{4,0},{6,2},{8,12},{10,14},{12,8},{14,10},{1,5},{3,7},... | collective-permute-start | bytes 294920 | tf_op jit(solution)/shard_map/ppermute | solution.py:361
  60.9 1.7 %collective-permute-start.23 = (bf16[64,768]{1,0:T(8,128)(2,1)S(1)}, bf16[64,768]{1,0:T(8,128)(2,1)S(1)}, u32[]{:S(2)}, u32[]{:S(2)}) collective-permute-start(bf16[64,768]{1,0:T(8,128)(2,1)S(1)} %get-tuple-element.113), channel_id=1, source_target_pairs={{0,2},{2,0},{4,6},{6,4},{8,10},{10,8},{12,14},{14,12},{1,3},{3,1},... | collective-permute-start | bytes 294920 | tf_op jit(solution)/shard_map/ppermute | solution.py:361
  62.6 0.7 near_grad.1
  63.4 2.2 %collective-permute-done.21.refs_3_ = bf16[64,768]{1,0:T(8,128)(2,1)S(1)} collective-permute-done((bf16[64,768]{1,0:T(8,128)(2,1)S(1)}, bf16[64,768]{1,0:T(8,128)(2,1)S(1)}, u32[]{:S(2)}, u32[]{:S(2)}) %collective-permute-start.21) | collective-permute-done | bytes 98336 | tf_op jit(solution)/shard_map/ppermute | solution.py:361
  65.6 1.0 %collective-permute-done.22.refs_4_ = bf16[64,768]{1,0:T(8,128)(2,1)S(1)} collective-permute-done((bf16[64,768]{1,0:T(8,128)(2,1)S(1)}, bf16[64,768]{1,0:T(8,128)(2,1)S(1)}, u32[]{:S(2)}, u32[]{:S(2)}) %collective-permute-start.22) | collective-permute-done | bytes 98336 | tf_op jit(solution)/shard_map/ppermute | solution.py:361
  66.6 1.7 %collective-permute-start.28 = (bf16[64,768]{1,0:T(8,128)(2,1)S(1)}, bf16[64,768]{1,0:T(8,128)(2,1)S(1)}, u32[]{:S(2)}, u32[]{:S(2)}) collective-permute-start(bf16[64,768]{1,0:T(8,128)(2,1)S(1)} %get-tuple-element.121), channel_id=1, source_target_pairs={{0,2},{2,0},{4,6},{6,4},{8,10},{10,8},{12,14},{14,12},{1,3},{3,1},... | collective-permute-start | bytes 294920 | tf_op jit(solution)/shard_map/ppermute | solution.py:361
  68.6 0.6 collective-permute-start.24
  69.2 2.6 %weight_far.1 = (bf16[3,1024,768]{2,1,0:T(8,128)(2,1)S(1)}, f32[8,128]{1,0:T(8,128)S(1)}) custom-call(bf16[7,256,256]{2,1,0:T(8,128)(2,1)S(1)} %get-tuple-element.102.refs_0_, bf16[7,256,256]{2,1,0:T(8,128)(2,1)S(1)} %collective-permute-done.17.refs_7_.refs_1_, bf16[11,256,256]{2,1,0:T(8,128)(2,1)S(1)} %get-tuple-element.122.refs_2_, ...), custom_call_target="tpu_custom_call" | custom-call | flops 2400000000 | bytes 2097152 | tf_op jit(solution)/shard_map/weight_far/pallas_call | solution.py:343
  71.8 3.8 %backward_near.1 = (bf16[64,768]{1,0:T(8,128)(2,1)S(1)}, bf16[64,768]{1,0:T(8,128)(2,1)S(1)}, bf16[64,768]{1,0:T(8,128)(2,1)S(1)}, bf16[64,768]{1,0:T(8,128)(2,1...) custom-call(bf16[3,1024,768]{2,1,0:T(8,128)(2,1)S(1)} %bitcast.16, ...), custom_call_target="tpu_custom_call" | custom-call | flops 10000000000 | bytes 2097152 | tf_op jit(solution)/shard_map/backward_near/pallas_call | solution.py:343
  75.7 2.9 %collective-permute-start.30 = (bf16[64,768]{1,0:T(8,128)(2,1)S(1)}, bf16[64,768]{1,0:T(8,128)(2,1)S(1)}, u32[]{:S(2)}, u32[]{:S(2)}) collective-permute-start(bf16[64,768]{1,0:T(8,128)(2,1)S(1)} %get-tuple-element.130), channel_id=1, source_target_pairs={{0,6},{2,4},{4,2},{6,0},{8,14},{10,12},{12,10},{14,8},{1,7},{3,5},... | collective-permute-start | bytes 294920 | tf_op jit(solution)/shard_map/ppermute | solution.py:361
  78.6 0.5 collective-permute-start.31
  79.1 0.6 collective-permute-start.32
  79.7 1.2 %collective-permute-done.24.refs_0_ = bf16[144,768]{1,0:T(8,128)(2,1)S(1)} collective-permute-done((bf16[144,768]{1,0:T(8,128)(2,1)S(1)}, bf16[144,768]{1,0:T(8,128)(2,1)S(1)}, u32[]{:S(2)}, u32[]{:S(2)}) %collective-permute-start.24) | collective-permute-done | bytes 221216 | tf_op jit(solution)/shard_map/ppermute | solution.py:366
  80.9 3.9 %weight_near.1 = (bf16[3,1024,768]{2,1,0:T(8,128)(2,1)}, f32[8,128]{1,0:T(8,128)S(1)}) custom-call(bf16[3,1024,768]{2,1,0:T(8,128)(2,1)S(1)} %get-tuple-element.133.refs_0_, bf16[7,256,256]{2,1,0:T(8,128)(2,1)S(1)} %get-tuple-element.80.refs_6_.refs_1_, bf16[7,256,256]{2,1,0:T(8,128)(2,1)S(1)} %collective-permute-done.6.refs_0_.refs_8_.refs_2_, ...), custom_call_target="tpu_custom_call" | custom-call | flops 30000001024 | bytes 2097152 | tf_op jit(solution)/shard_map/weight_near/pallas_call | solution.py:343
  85.1 1.4 %combine_gradients.1 = (bf16[128,768]{1,0:T(8,128)(2,1)}, bf16[128,768]{1,0:T(8,128)(2,1)}, f32[2,128]{1,0:T(2,128)}) custom-call(bf16[2,256,128]{2,1,0:T(8,128)(2,1)S(1)} %get-tuple-element.73.refs_1_.refs_0_, bf16[144,768]{1,0:T(8,128)(2,1)S(1)} %get-tuple-element.126.refs_1_, f32[2,128]{1,0:T(2,128)S(1)} %get-tuple-element.127.refs_2_, ...), custom_call_target="tpu_custom_call" | custom-call | flops 30000001024 | bytes 2097152 | tf_op jit(solution)/shard_map/combine_gradients/pallas_call | solution.py:343
  (51 shorter events, 2.1 us)
Async XLA Ops:
  0.6 20.1 %collective-permute-start.2 = (bf16[3,1024,768]{2,1,0:T(8,128)(2,1)}, bf16[3,1024,768]{2,1,0:T(8,128)(2,1)S(1)}, u32[]{:S(2)}, u32[]{:S(2)}) collective-permute-start(bf16[3,1024,768]{2,1,0:T(8,128)(2,1)} %bitcast.9), channel_id=1, source_target_pairs={{0,1},{1,0},{2,3},{3,2},{4,5},{5,4},{6,7},{7,6},{8,9},{9,8},{10,11... | collective-permute-start | bytes 14155784 | tf_op jit(solution)/shard_map/ppermute | solution.py:369
  1.1 15.4 %collective-permute-start.1 = (bf16[128,768]{1,0:T(8,128)(2,1)}, bf16[128,768]{1,0:T(8,128)(2,1)S(1)}, u32[]{:S(2)}, u32[]{:S(2)}) collective-permute-start(bf16[128,768]{1,0:T(8,128)(2,1)} %refs_3_.1), channel_id=1, source_target_pairs={{0,8},{2,10},{4,12},{6,14},{8,0},{10,2},{12,4},{14,6},{1,9},{3,11}... | collective-permute-start | bytes 589832 | tf_op jit(solution)/shard_map/ppermute | solution.py:366
  4.8 2.3 %copy-start = (bf16[1,1024,3,768]{3,1,2,0:T(8,128)(2,1)S(1)}, bf16[1,1024,3,768]{3,1,2,0:T(8,128)(2,1)}, u32[]{:S(2)}) copy-start(bf16[1,1024,3,768]{3,1,2,0:T(8,128)(2,1)} %param.9) | copy-start | bytes 14155780
  7.2 0.9 %copy-start.1 = (bf16[128,768]{1,0:T(8,128)(2,1)S(1)}, bf16[128,768]{1,0:T(8,128)(2,1)}, u32[]{:S(2)}) copy-start(bf16[128,768]{1,0:T(8,128)(2,1)} %refs_3_.1) | copy-start | bytes 589828
  8.1 0.7 copy-start.3
  8.8 0.7 copy-start.4
  9.8 5.1 %collective-permute-start = (f32[8,128]{1,0:T(8,128)S(1)}, f32[8,128]{1,0:T(8,128)S(1)}, u32[]{:S(2)}, u32[]{:S(2)}) collective-permute-start(f32[8,128]{1,0:T(8,128)S(1)} %get-tuple-element.74.refs_0_), channel_id=1, source_target_pairs={{0,8},{2,10},{4,12},{6,14},{8,0},{10,2},{12,4},{14,6},{1,9},{3,11}... | collective-permute-start | bytes 12296 | tf_op jit(solution)/shard_map/ppermute | solution.py:366
  9.9 8.1 %collective-permute-start.3 = (bf16[64,768]{1,0:T(8,128)(2,1)S(1)}, bf16[64,768]{1,0:T(8,128)(2,1)S(1)}, u32[]{:S(2)}, u32[]{:S(2)}) collective-permute-start(bf16[64,768]{1,0:T(8,128)(2,1)S(1)} %get-tuple-element.77), channel_id=1, source_target_pairs={{0,6},{2,4},{4,2},{6,0},{8,14},{10,12},{12,10},{14,8},{1,7},{3,5},... | collective-permute-start | bytes 294920 | tf_op jit(solution)/shard_map/ppermute | solution.py:361
  12.8 6.4 %collective-permute-start.4 = (bf16[64,768]{1,0:T(8,128)(2,1)S(1)}, bf16[64,768]{1,0:T(8,128)(2,1)S(1)}, u32[]{:S(2)}, u32[]{:S(2)}) collective-permute-start(bf16[64,768]{1,0:T(8,128)(2,1)S(1)} %get-tuple-element.78), channel_id=1, source_target_pairs={{0,4},{2,6},{4,0},{6,2},{8,12},{10,14},{12,8},{14,10},{1,5},{3,7},... | collective-permute-start | bytes 294920 | tf_op jit(solution)/shard_map/ppermute | solution.py:361
  14.9 5.8 %slice-start = ((s8[4718592]{0:T(1024)(128)(4,1)}), s8[4194304]{0:T(1024)(128)(4,1)S(1)}, s32[]{:S(2)}) async-start(s8[4718592]{0:T(1024)(128)(4,1)} %bitcast.11), calls=%async_computation | async-start | bytes 8388608
  14.9 5.8 %slice-start.1 = ((s8[4718592]{0:T(1024)(128)(4,1)}), s8[524288]{0:T(1024)(128)(4,1)S(1)}, s32[]{:S(2)}) async-start(s8[4718592]{0:T(1024)(128)(4,1)} %bitcast.11), calls=%async_computation.1 | async-start | bytes 1048576
  14.9 5.8 %collective-permute-start.5 = (bf16[64,768]{1,0:T(8,128)(2,1)S(1)}, bf16[64,768]{1,0:T(8,128)(2,1)S(1)}, u32[]{:S(2)}, u32[]{:S(2)}) collective-permute-start(bf16[64,768]{1,0:T(8,128)(2,1)S(1)} %get-tuple-element.79), channel_id=1, source_target_pairs={{0,2},{2,0},{4,6},{6,4},{8,10},{10,8},{12,14},{14,12},{1,3},{3,1},... | collective-permute-start | bytes 294920 | tf_op jit(solution)/shard_map/ppermute | solution.py:361
  16.9 10.7 %collective-permute-start.10 = (bf16[64,768]{1,0:T(8,128)(2,1)S(1)}, bf16[64,768]{1,0:T(8,128)(2,1)S(1)}, u32[]{:S(2)}, u32[]{:S(2)}) collective-permute-start(bf16[64,768]{1,0:T(8,128)(2,1)S(1)} %get-tuple-element.86), channel_id=1, source_target_pairs={{0,6},{2,4},{4,2},{6,0},{8,14},{10,12},{12,10},{14,8},{1,7},{3,5},... | collective-permute-start | bytes 294920 | tf_op jit(solution)/shard_map/ppermute | solution.py:361
  18.0 9.7 %collective-permute-start.11 = (bf16[64,768]{1,0:T(8,128)(2,1)S(1)}, bf16[64,768]{1,0:T(8,128)(2,1)S(1)}, u32[]{:S(2)}, u32[]{:S(2)}) collective-permute-start(bf16[64,768]{1,0:T(8,128)(2,1)S(1)} %get-tuple-element.87), channel_id=1, source_target_pairs={{0,4},{2,6},{4,0},{6,2},{8,12},{10,14},{12,8},{14,10},{1,5},{3,7},... | collective-permute-start | bytes 294920 | tf_op jit(solution)/shard_map/ppermute | solution.py:361
  19.1 8.6 %collective-permute-start.12 = (bf16[64,768]{1,0:T(8,128)(2,1)S(1)}, bf16[64,768]{1,0:T(8,128)(2,1)S(1)}, u32[]{:S(2)}, u32[]{:S(2)}) collective-permute-start(bf16[64,768]{1,0:T(8,128)(2,1)S(1)} %get-tuple-element.88), channel_id=1, source_target_pairs={{0,2},{2,0},{4,6},{6,4},{8,10},{10,8},{12,14},{14,12},{1,3},{3,1},... | collective-permute-start | bytes 294920 | tf_op jit(solution)/shard_map/ppermute | solution.py:361
  24.1 7.0 %collective-permute-start.7 = (bf16[64,768]{1,0:T(8,128)(2,1)S(1)}, bf16[64,768]{1,0:T(8,128)(2,1)S(1)}, u32[]{:S(2)}, u32[]{:S(2)}) collective-permute-start(bf16[64,768]{1,0:T(8,128)(2,1)S(1)} %get-tuple-element.82), channel_id=1, source_target_pairs={{0,6},{2,4},{4,2},{6,0},{8,14},{10,12},{12,10},{14,8},{1,7},{3,5},... | collective-permute-start | bytes 294920 | tf_op jit(solution)/shard_map/ppermute | solution.py:361
  26.5 4.8 %collective-permute-start.8 = (bf16[64,768]{1,0:T(8,128)(2,1)S(1)}, bf16[64,768]{1,0:T(8,128)(2,1)S(1)}, u32[]{:S(2)}, u32[]{:S(2)}) collective-permute-start(bf16[64,768]{1,0:T(8,128)(2,1)S(1)} %get-tuple-element.83), channel_id=1, source_target_pairs={{0,4},{2,6},{4,0},{6,2},{8,12},{10,14},{12,8},{14,10},{1,5},{3,7},... | collective-permute-start | bytes 294920 | tf_op jit(solution)/shard_map/ppermute | solution.py:361
  27.6 4.6 %collective-permute-start.9 = (bf16[64,768]{1,0:T(8,128)(2,1)S(1)}, bf16[64,768]{1,0:T(8,128)(2,1)S(1)}, u32[]{:S(2)}, u32[]{:S(2)}) collective-permute-start(bf16[64,768]{1,0:T(8,128)(2,1)S(1)} %get-tuple-element.84), channel_id=1, source_target_pairs={{0,2},{2,0},{4,6},{6,4},{8,10},{10,8},{12,14},{14,12},{1,3},{3,1},... | collective-permute-start | bytes 294920 | tf_op jit(solution)/shard_map/ppermute | solution.py:361
  27.7 7.1 %collective-permute-start.6 = (bf16[7,256,256]{2,1,0:T(8,128)(2,1)S(1)}, bf16[7,256,256]{2,1,0:T(8,128)(2,1)S(1)}, u32[]{:S(2)}, u32[]{:S(2)}) collective-permute-start(bf16[7,256,256]{2,1,0:T(8,128)(2,1)S(1)} %get-tuple-element.80.refs_6_.refs_1_), channel_id=1, source_target_pairs={{0,1},{1,0},{2,3},{3,2},{4,5},{5,4},{6,7},{7,6},{8,9},{9,8},{10,11... | collective-permute-start | bytes 2752520 | tf_op jit(solution)/shard_map/ppermute | solution.py:369
  27.7 4.5 %copy-start.2 = (bf16[128,768]{1,0:T(8,128)(2,1)S(1)}, bf16[128,768]{1,0:T(8,128)(2,1)}, u32[]{:S(2)}) copy-start(bf16[128,768]{1,0:T(8,128)(2,1)} %refs_2_.3) | copy-start | bytes 589828
  32.6 11.6 %collective-permute-start.13 = (bf16[128,768]{1,0:T(8,128)(2,1)S(1)}, bf16[128,768]{1,0:T(8,128)(2,1)S(1)}, u32[]{:S(2)}, u32[]{:S(2)}) collective-permute-start(bf16[128,768]{1,0:T(8,128)(2,1)S(1)} %get-tuple-element.98), channel_id=1, source_target_pairs={{0,8},{2,10},{4,12},{6,14},{8,0},{10,2},{12,4},{14,6},{1,9},{3,11}... | collective-permute-start | bytes 589832 | tf_op jit(solution)/shard_map/ppermute | solution.py:366
  34.8 9.4 %collective-permute-start.17 = (bf16[7,256,256]{2,1,0:T(8,128)(2,1)S(1)}, bf16[7,256,256]{2,1,0:T(8,128)(2,1)S(1)}, u32[]{:S(2)}, u32[]{:S(2)}) collective-permute-start(bf16[7,256,256]{2,1,0:T(8,128)(2,1)S(1)} %get-tuple-element.102.refs_0_), channel_id=1, source_target_pairs={{0,1},{1,0},{2,3},{3,2},{4,5},{5,4},{6,7},{7,6},{8,9},{9,8},{10,11... | collective-permute-start | bytes 2752520 | tf_op jit(solution)/shard_map/ppermute | solution.py:369
  34.8 9.4 %collective-permute-start.14 = (bf16[64,768]{1,0:T(8,128)(2,1)S(1)}, bf16[64,768]{1,0:T(8,128)(2,1)S(1)}, u32[]{:S(2)}, u32[]{:S(2)}) collective-permute-start(bf16[64,768]{1,0:T(8,128)(2,1)S(1)} %get-tuple-element.99), channel_id=1, source_target_pairs={{0,6},{2,4},{4,2},{6,0},{8,14},{10,12},{12,10},{14,8},{1,7},{3,5},... | collective-permute-start | bytes 294920 | tf_op jit(solution)/shard_map/ppermute | solution.py:361
  37.4 8.3 %collective-permute-start.15 = (bf16[64,768]{1,0:T(8,128)(2,1)S(1)}, bf16[64,768]{1,0:T(8,128)(2,1)S(1)}, u32[]{:S(2)}, u32[]{:S(2)}) collective-permute-start(bf16[64,768]{1,0:T(8,128)(2,1)S(1)} %get-tuple-element.100), channel_id=1, source_target_pairs={{0,4},{2,6},{4,0},{6,2},{8,12},{10,14},{12,8},{14,10},{1,5},{3,7},... | collective-permute-start | bytes 294920 | tf_op jit(solution)/shard_map/ppermute | solution.py:361
  37.4 8.3 %collective-permute-start.16 = (bf16[64,768]{1,0:T(8,128)(2,1)S(1)}, bf16[64,768]{1,0:T(8,128)(2,1)S(1)}, u32[]{:S(2)}, u32[]{:S(2)}) collective-permute-start(bf16[64,768]{1,0:T(8,128)(2,1)S(1)} %get-tuple-element.101), channel_id=1, source_target_pairs={{0,2},{2,0},{4,6},{6,4},{8,10},{10,8},{12,14},{14,12},{1,3},{3,1},... | collective-permute-start | bytes 294920 | tf_op jit(solution)/shard_map/ppermute | solution.py:361
  46.3 6.4 %collective-permute-start.18 = (bf16[64,768]{1,0:T(8,128)(2,1)S(1)}, bf16[64,768]{1,0:T(8,128)(2,1)S(1)}, u32[]{:S(2)}, u32[]{:S(2)}) collective-permute-start(bf16[64,768]{1,0:T(8,128)(2,1)S(1)} %get-tuple-element.107), channel_id=1, source_target_pairs={{0,6},{2,4},{4,2},{6,0},{8,14},{10,12},{12,10},{14,8},{1,7},{3,5},... | collective-permute-start | bytes 294920 | tf_op jit(solution)/shard_map/ppermute | solution.py:361
  47.4 7.7 %collective-permute-start.19 = (bf16[64,768]{1,0:T(8,128)(2,1)S(1)}, bf16[64,768]{1,0:T(8,128)(2,1)S(1)}, u32[]{:S(2)}, u32[]{:S(2)}) collective-permute-start(bf16[64,768]{1,0:T(8,128)(2,1)S(1)} %get-tuple-element.108), channel_id=1, source_target_pairs={{0,4},{2,6},{4,0},{6,2},{8,12},{10,14},{12,8},{14,10},{1,5},{3,7},... | collective-permute-start | bytes 294920 | tf_op jit(solution)/shard_map/ppermute | solution.py:361
  48.9 6.3 %collective-permute-start.20 = (bf16[64,768]{1,0:T(8,128)(2,1)S(1)}, bf16[64,768]{1,0:T(8,128)(2,1)S(1)}, u32[]{:S(2)}, u32[]{:S(2)}) collective-permute-start(bf16[64,768]{1,0:T(8,128)(2,1)S(1)} %get-tuple-element.109), channel_id=1, source_target_pairs={{0,2},{2,0},{4,6},{6,4},{8,10},{10,8},{12,14},{14,12},{1,3},{3,1},... | collective-permute-start | bytes 294920 | tf_op jit(solution)/shard_map/ppermute | solution.py:361
  49.9 12.7 %collective-permute-start.25 = (bf16[128,768]{1,0:T(8,128)(2,1)S(1)}, bf16[128,768]{1,0:T(8,128)(2,1)S(1)}, u32[]{:S(2)}, u32[]{:S(2)}) collective-permute-start(bf16[128,768]{1,0:T(8,128)(2,1)S(1)} %get-tuple-element.116), channel_id=1, source_target_pairs={{0,8},{2,10},{4,12},{6,14},{8,0},{10,2},{12,4},{14,6},{1,9},{3,11}... | collective-permute-start | bytes 589832 | tf_op jit(solution)/shard_map/ppermute | solution.py:366
  58.9 10.2 %collective-permute-start.29 = (bf16[11,256,256]{2,1,0:T(8,128)(2,1)S(1)}, bf16[11,256,256]{2,1,0:T(8,128)(2,1)S(1)}, u32[]{:S(2)}, u32[]{:S(2)}) collective-permute-start(bf16[11,256,256]{2,1,0:T(8,128)(2,1)S(1)} %get-tuple-element.122.refs_2_), channel_id=1, source_target_pairs={{0,1},{1,0},{2,3},{3,2},{4,5},{5,4},{6,7},{7,6},{8,9},{9,8},{10,11... | collective-permute-start | bytes 4325384 | tf_op jit(solution)/shard_map/ppermute | solution.py:369
  59.0 6.6 %collective-permute-start.21 = (bf16[64,768]{1,0:T(8,128)(2,1)S(1)}, bf16[64,768]{1,0:T(8,128)(2,1)S(1)}, u32[]{:S(2)}, u32[]{:S(2)}) collective-permute-start(bf16[64,768]{1,0:T(8,128)(2,1)S(1)} %get-tuple-element.111), channel_id=1, source_target_pairs={{0,6},{2,4},{4,2},{6,0},{8,14},{10,12},{12,10},{14,8},{1,7},{3,5},... | collective-permute-start | bytes 294920 | tf_op jit(solution)/shard_map/ppermute | solution.py:361
  59.1 7.5 %collective-permute-start.22 = (bf16[64,768]{1,0:T(8,128)(2,1)S(1)}, bf16[64,768]{1,0:T(8,128)(2,1)S(1)}, u32[]{:S(2)}, u32[]{:S(2)}) collective-permute-start(bf16[64,768]{1,0:T(8,128)(2,1)S(1)} %get-tuple-element.112), channel_id=1, source_target_pairs={{0,4},{2,6},{4,0},{6,2},{8,12},{10,14},{12,8},{14,10},{1,5},{3,7},... | collective-permute-start | bytes 294920 | tf_op jit(solution)/shard_map/ppermute | solution.py:361
  60.9 7.3 %collective-permute-start.23 = (bf16[64,768]{1,0:T(8,128)(2,1)S(1)}, bf16[64,768]{1,0:T(8,128)(2,1)S(1)}, u32[]{:S(2)}, u32[]{:S(2)}) collective-permute-start(bf16[64,768]{1,0:T(8,128)(2,1)S(1)} %get-tuple-element.113), channel_id=1, source_target_pairs={{0,2},{2,0},{4,6},{6,4},{8,10},{10,8},{12,14},{14,12},{1,3},{3,1},... | collective-permute-start | bytes 294920 | tf_op jit(solution)/shard_map/ppermute | solution.py:361
  63.2 8.6 %collective-permute-start.26 = (bf16[64,768]{1,0:T(8,128)(2,1)S(1)}, bf16[64,768]{1,0:T(8,128)(2,1)S(1)}, u32[]{:S(2)}, u32[]{:S(2)}) collective-permute-start(bf16[64,768]{1,0:T(8,128)(2,1)S(1)} %get-tuple-element.119), channel_id=1, source_target_pairs={{0,6},{2,4},{4,2},{6,0},{8,14},{10,12},{12,10},{14,8},{1,7},{3,5},... | collective-permute-start | bytes 294920 | tf_op jit(solution)/shard_map/ppermute | solution.py:361
  65.6 6.2 %collective-permute-start.27 = (bf16[64,768]{1,0:T(8,128)(2,1)S(1)}, bf16[64,768]{1,0:T(8,128)(2,1)S(1)}, u32[]{:S(2)}, u32[]{:S(2)}) collective-permute-start(bf16[64,768]{1,0:T(8,128)(2,1)S(1)} %get-tuple-element.120), channel_id=1, source_target_pairs={{0,4},{2,6},{4,0},{6,2},{8,12},{10,14},{12,8},{14,10},{1,5},{3,7},... | collective-permute-start | bytes 294920 | tf_op jit(solution)/shard_map/ppermute | solution.py:361
  66.6 5.2 %collective-permute-start.28 = (bf16[64,768]{1,0:T(8,128)(2,1)S(1)}, bf16[64,768]{1,0:T(8,128)(2,1)S(1)}, u32[]{:S(2)}, u32[]{:S(2)}) collective-permute-start(bf16[64,768]{1,0:T(8,128)(2,1)S(1)} %get-tuple-element.121), channel_id=1, source_target_pairs={{0,2},{2,0},{4,6},{6,4},{8,10},{10,8},{12,14},{14,12},{1,3},{3,1},... | collective-permute-start | bytes 294920 | tf_op jit(solution)/shard_map/ppermute | solution.py:361
  68.6 12.3 %collective-permute-start.24 = (bf16[144,768]{1,0:T(8,128)(2,1)S(1)}, bf16[144,768]{1,0:T(8,128)(2,1)S(1)}, u32[]{:S(2)}, u32[]{:S(2)}) collective-permute-start(bf16[144,768]{1,0:T(8,128)(2,1)S(1)} %far_back.1.refs_6_.refs_8_), channel_id=1, source_target_pairs={{0,8},{2,10},{4,12},{6,14},{8,0},{10,2},{12,4},{14,6},{1,9},{3,11}... | collective-permute-start | bytes 663560 | tf_op jit(solution)/shard_map/ppermute | solution.py:366
  75.6 5.3 %collective-permute-start.33 = (bf16[11,256,256]{2,1,0:T(8,128)(2,1)S(1)}, bf16[11,256,256]{2,1,0:T(8,128)(2,1)S(1)}, u32[]{:S(2)}, u32[]{:S(2)}) collective-permute-start(bf16[11,256,256]{2,1,0:T(8,128)(2,1)S(1)} %get-tuple-element.134.refs_3_), channel_id=1, source_target_pairs={{0,1},{1,0},{2,3},{3,2},{4,5},{5,4},{6,7},{7,6},{8,9},{9,8},{10,11... | collective-permute-start | bytes 4325384 | tf_op jit(solution)/shard_map/ppermute | solution.py:369
  75.7 9.1 %collective-permute-start.30 = (bf16[64,768]{1,0:T(8,128)(2,1)S(1)}, bf16[64,768]{1,0:T(8,128)(2,1)S(1)}, u32[]{:S(2)}, u32[]{:S(2)}) collective-permute-start(bf16[64,768]{1,0:T(8,128)(2,1)S(1)} %get-tuple-element.130), channel_id=1, source_target_pairs={{0,6},{2,4},{4,2},{6,0},{8,14},{10,12},{12,10},{14,8},{1,7},{3,5},... | collective-permute-start | bytes 294920 | tf_op jit(solution)/shard_map/ppermute | solution.py:361
  78.6 6.5 %collective-permute-start.31 = (bf16[64,768]{1,0:T(8,128)(2,1)S(1)}, bf16[64,768]{1,0:T(8,128)(2,1)S(1)}, u32[]{:S(2)}, u32[]{:S(2)}) collective-permute-start(bf16[64,768]{1,0:T(8,128)(2,1)S(1)} %get-tuple-element.131), channel_id=1, source_target_pairs={{0,4},{2,6},{4,0},{6,2},{8,12},{10,14},{12,8},{14,10},{1,5},{3,7},... | collective-permute-start | bytes 294920 | tf_op jit(solution)/shard_map/ppermute | solution.py:361
  79.1 6.0 %collective-permute-start.32 = (bf16[64,768]{1,0:T(8,128)(2,1)S(1)}, bf16[64,768]{1,0:T(8,128)(2,1)S(1)}, u32[]{:S(2)}, u32[]{:S(2)}) collective-permute-start(bf16[64,768]{1,0:T(8,128)(2,1)S(1)} %get-tuple-element.132), channel_id=1, source_target_pairs={{0,2},{2,0},{4,6},{6,4},{8,10},{10,8},{12,14},{14,12},{1,3},{3,1},... | collective-permute-start | bytes 294920 | tf_op jit(solution)/shard_map/ppermute | solution.py:361

commit v13 on v12

--- a/solution.py
+++ b/solution.py
@@ -148,18 +148,23 @@
     x = get(ins)
     put_columns(sent_ref, x)
     units, width = other_ref.shape[1:]
-    hidden = []
-    for w_ref, first in ((own_ref, 0), (other_ref, units)):
-        both = dot(w_ref[0:2].reshape(2 * units, width), x, LAST)
+    halves = ((own_ref, 0), (other_ref, units))
+    products = [dot(w_ref[0:2].reshape(2 * units, width), x, LAST) for w_ref, _ in halves]
+    total = None
+    for (w_ref, first), both in zip(halves, products):
         gate, up = both[:units], both[units:]
         sig = 0.5 * jnp.tanh(0.5 * gate) + 0.5
         silu = gate * sig
-        hidden.append((silu * up).astype(BF16))
+        hidden = (silu * up).astype(BF16)
         fa_ref[first : first + units, :] = (up * (sig + silu * (1.0 - sig))).astype(BF16)
         fb_ref[first : first + units, :] = silu.astype(BF16)
-    hid_own_ref[...] = hidden[0]
-    put_rows(sent_ref, width // x.shape[0], hidden[1])
-    put(outs, dot(hidden[0], own_ref[2], FIRST) + dot(hidden[1], other_ref[2], FIRST))
+        if w_ref is own_ref:
+            hid_own_ref[...] = hidden
+        else:
+            put_rows(sent_ref, width // x.shape[0], hidden)
+        out = dot(hidden, w_ref[2], FIRST)
+        total = out if total is None else total + out
+    put(outs, total)
 
 
 def backward_kernel(pieces, own_ref, other_ref, fa_ref, fb_ref, *refs):
@@ -168,20 +173,21 @@
     rg = get(ins)
     put_columns(sent_ref, rg)
     units, width = own_ref.shape[1:]
-    both = []
-    for w_ref, first in ((own_ref, 0), (other_ref, units)):
+    halves = ((own_ref, 0), (other_ref, units))
+    products = [dot(w_ref[2], rg, LAST) for w_ref, _ in halves]
+    total = None
+    for (w_ref, first), dh in zip(halves, products):
         at = slice(first, first + units)
-        dh = dot(w_ref[2], rg, LAST)
         dg = (dh * fa_ref[at, :].astype(F32)).astype(BF16)
         du = (dh * fb_ref[at, :].astype(F32)).astype(BF16)
-        both.append(jnp.concatenate([dg, du], axis=0))
-    dgu_own_ref[...] = both[0]
-    put_rows(sent_ref, width // rg.shape[0], both[1])
-    put(
-        outs,
-        dot(both[0], own_ref[0:2].reshape(2 * units, width), FIRST)
-        + dot(both[1], other_ref[0:2].reshape(2 * units, width), FIRST),
-    )
+        dgu = jnp.concatenate([dg, du], axis=0)
+        if w_ref is own_ref:
+            dgu_own_ref[...] = dgu
+        else:
+            put_rows(sent_ref, width // rg.shape[0], dgu)
+        out = dot(dgu, w_ref[0:2].reshape(2 * units, width), FIRST)
+        total = out if total is None else total + out
+    put(outs, total)
 
 
 def near_sum_kernel(meta_ref, masks_ref, teacher_ref, *refs):
@@ -231,16 +237,13 @@
     out_ref[tok:, tok:] = jnp.zeros((out_ref.shape[0] - tok, out_ref.shape[1] - tok), BF16)
 
 
-def final_kernel(pieces, masks_ref, part_ref, near_ref, student_ref, *refs):
-    ins, student_hbm, out_ref, d_gates_ref, sem = refs[:pieces], *refs[pieces:]
-    copy = pltpu.make_async_copy(student_ref, student_hbm, sem)
-    copy.start()
+def final_kernel(pieces, masks_ref, part_ref, near_ref, *refs):
+    ins, out_ref, d_gates_ref = refs[:pieces], refs[pieces], refs[pieces + 1]
     tok = masks_ref.shape[2]
     total = dot(masks_ref[0] + masks_ref[1], get(ins), FIRST) + part_ref[:tok, :].astype(F32)
     out_ref[...] = total.astype(BF16)
     far = part_ref[tok:, :tok].astype(F32)
     d_gates_ref[...] = near_ref[...] + (far[0:2] + far[2:4])
-    copy.wait()
 
 
 def weight_blocks(across, x, sent_x, g, sent_g, d, h):
@@ -500,19 +503,16 @@
         in_hbm=1,
     )
 
-    student, d_tokens, d_gates = call(
+    d_tokens, d_gates = call(
         functools.partial(final_kernel, half),
         "combine_gradients",
-        [dense, dense, pair],
+        [dense, pair],
         [],
         near_masks,
         part,
         d_gates_near,
-        student,
         *back_near,
         after=[finished],
-        scratch=[pltpu.SemaphoreType.DMA],
-        in_hbm=1,
     )
     return (student, d_tokens, d_gates.T, weight_grads.transpose(1, 0, 2)[None])
 

time: 86.9 us -> 86.2 us (level)
  transfers between devices with their start and end apart: 34 -> 34, of which waited for: 13 -> 13; matrix products, arithmetic and copies ran while one was open for 0% -> 0% of each run, Pallas kernels for 26% -> 27%
where the time goes in v13:
time: 86.2 us; the launch traced here: 85.9 us
  starting transfers between devices  36.4 us (42%)
  Pallas kernels  25 us (29%)
  waiting for transfers between devices  19.1 us (22%)
  local copies, waits for them, and re-layouts  4.63 us (5%)
    ppermute x24, starting transfers between devices, within_half(): lax.ppermute(rows_of[s], 'expert', [(i, i ^ s) for i in range(experts)])  28.2 us
    pallas_call x16, Pallas kernels, call(): pl.pallas_call(body, in_specs=specs + [aspec] * (len(after) + len(through...  25 us
    ppermute x24, waiting for transfers between devices, within_half(): lax.ppermute(rows_of[s], 'expert', [(i, i ^ s) for i in range(experts)])  10.3 us
    ppermute x5, waiting for transfers between devices, to_mirror(): return lax.ppermute(x, 'expert', [(i, i ^ half) for i in range(experts)])  8.78 us
    ppermute x5, starting transfers between devices, to_mirror(): return lax.ppermute(x, 'expert', [(i, i ^ half) for i in range(experts)])  7.56 us
    unnamed x14, local copies, waits for them, and re-layouts  4.63 us
  transfers between devices with their start and end apart: 34, of which 13 were waited for; matrix products, arithmetic and copies ran while one was open for 0% of the time, Pallas kernels for 27%

profile of v13, /device:TPU:0, one launch (start us, length us, event | category | flops | bytes accessed | tf_op | source)
XLA Modules:
  0.0 85.9 jit_solution(11138506416398356112)
XLA Ops:
  0.6 0.5 collective-permute-start.2
  1.1 3.7 %collective-permute-start.1 = (bf16[128,768]{1,0:T(8,128)(2,1)}, bf16[128,768]{1,0:T(8,128)(2,1)S(1)}, u32[]{:S(2)}, u32[]{:S(2)}) collective-permute-start(bf16[128,768]{1,0:T(8,128)(2,1)} %refs_3_.1), channel_id=1, source_target_pairs={{0,8},{2,10},{4,12},{6,14},{8,0},{10,2},{12,4},{14,6},{1,9},{3,11}... | collective-permute-start | bytes 589832 | tf_op jit(solution)/shard_map/ppermute | solution.py:369
  4.8 2.3 %copy-done = bf16[1,1024,3,768]{3,1,2,0:T(8,128)(2,1)S(1)} copy-done((bf16[1,1024,3,768]{3,1,2,0:T(8,128)(2,1)S(1)}, bf16[1,1024,3,768]{3,1,2,0:T(8,128)(2,1)}, u32[]{:S(2)}) %copy-start) | copy-done | bytes 4718616
  7.2 0.9 %copy-done.1 = bf16[128,768]{1,0:T(8,128)(2,1)S(1)} copy-done((bf16[128,768]{1,0:T(8,128)(2,1)S(1)}, bf16[128,768]{1,0:T(8,128)(2,1)}, u32[]{:S(2)}) %copy-start.1) | copy-done | bytes 196632
  8.1 0.7 copy-done.3
  8.8 0.7 copy-done.4
  9.9 2.9 %collective-permute-start.3 = (bf16[64,768]{1,0:T(8,128)(2,1)S(1)}, bf16[64,768]{1,0:T(8,128)(2,1)S(1)}, u32[]{:S(2)}, u32[]{:S(2)}) collective-permute-start(bf16[64,768]{1,0:T(8,128)(2,1)S(1)} %get-tuple-element.76), channel_id=1, source_target_pairs={{0,6},{2,4},{4,2},{6,0},{8,14},{10,12},{12,10},{14,8},{1,7},{3,5},... | collective-permute-start | bytes 294920 | tf_op jit(solution)/shard_map/ppermute | solution.py:364
  12.8 0.5 collective-permute-start.4
  13.2 1.7 %collective-permute-done.refs_0_ = f32[8,128]{1,0:T(8,128)S(1)} collective-permute-done((f32[8,128]{1,0:T(8,128)S(1)}, f32[8,128]{1,0:T(8,128)S(1)}, u32[]{:S(2)}, u32[]{:S(2)}) %collective-permute-start) | collective-permute-done | bytes 4128 | tf_op jit(solution)/shard_map/ppermute | solution.py:369
  14.9 1.6 %collective-permute-start.5 = (bf16[64,768]{1,0:T(8,128)(2,1)S(1)}, bf16[64,768]{1,0:T(8,128)(2,1)S(1)}, u32[]{:S(2)}, u32[]{:S(2)}) collective-permute-start(bf16[64,768]{1,0:T(8,128)(2,1)S(1)} %get-tuple-element.78), channel_id=1, source_target_pairs={{0,2},{2,0},{4,6},{6,4},{8,10},{10,8},{12,14},{14,12},{1,3},{3,1},... | collective-permute-start | bytes 294920 | tf_op jit(solution)/shard_map/ppermute | solution.py:364
  16.5 0.4 pack_far.1
  16.9 1.0 %collective-permute-start.10 = (bf16[64,768]{1,0:T(8,128)(2,1)S(1)}, bf16[64,768]{1,0:T(8,128)(2,1)S(1)}, u32[]{:S(2)}, u32[]{:S(2)}) collective-permute-start(bf16[64,768]{1,0:T(8,128)(2,1)S(1)} %get-tuple-element.85), channel_id=1, source_target_pairs={{0,6},{2,4},{4,2},{6,0},{8,14},{10,12},{12,10},{14,8},{1,7},{3,5},... | collective-permute-start | bytes 294920 | tf_op jit(solution)/shard_map/ppermute | solution.py:364
  18.0 0.8 collective-permute-start.11
  19.1 1.6 %collective-permute-start.12 = (bf16[64,768]{1,0:T(8,128)(2,1)S(1)}, bf16[64,768]{1,0:T(8,128)(2,1)S(1)}, u32[]{:S(2)}, u32[]{:S(2)}) collective-permute-start(bf16[64,768]{1,0:T(8,128)(2,1)S(1)} %get-tuple-element.87), channel_id=1, source_target_pairs={{0,2},{2,0},{4,6},{6,4},{8,10},{10,8},{12,14},{14,12},{1,3},{3,1},... | collective-permute-start | bytes 294920 | tf_op jit(solution)/shard_map/ppermute | solution.py:364
  20.7 3.4 %forward_near.1 = (bf16[64,768]{1,0:T(8,128)(2,1)S(1)}, bf16[64,768]{1,0:T(8,128)(2,1)S(1)}, bf16[64,768]{1,0:T(8,128)(2,1)S(1)}, bf16[64,768]{1,0:T(8,128)(2,1)...) custom-call(bf16[3,1024,768]{2,1,0:T(8,128)(2,1)S(1)} %bitcast.13, ...), custom_call_target="tpu_custom_call" | custom-call | flops 100000000 | bytes 2097152 | tf_op jit(solution)/shard_map/forward_near/pallas_call | solution.py:346
  24.1 2.3 %collective-permute-start.7 = (bf16[64,768]{1,0:T(8,128)(2,1)S(1)}, bf16[64,768]{1,0:T(8,128)(2,1)S(1)}, u32[]{:S(2)}, u32[]{:S(2)}) collective-permute-start(bf16[64,768]{1,0:T(8,128)(2,1)S(1)} %get-tuple-element.81), channel_id=1, source_target_pairs={{0,6},{2,4},{4,2},{6,0},{8,14},{10,12},{12,10},{14,8},{1,7},{3,5},... | collective-permute-start | bytes 294920 | tf_op jit(solution)/shard_map/ppermute | solution.py:364
  26.5 1.2 %collective-permute-start.8 = (bf16[64,768]{1,0:T(8,128)(2,1)S(1)}, bf16[64,768]{1,0:T(8,128)(2,1)S(1)}, u32[]{:S(2)}, u32[]{:S(2)}) collective-permute-start(bf16[64,768]{1,0:T(8,128)(2,1)S(1)} %get-tuple-element.82), channel_id=1, source_target_pairs={{0,4},{2,6},{4,0},{6,2},{8,12},{10,14},{12,8},{14,10},{1,5},{3,7},... | collective-permute-start | bytes 294920 | tf_op jit(solution)/shard_map/ppermute | solution.py:364
  27.7 3.4 %forward_far.1 = (bf16[64,768]{1,0:T(8,128)(2,1)S(1)}, bf16[64,768]{1,0:T(8,128)(2,1)S(1)}, bf16[64,768]{1,0:T(8,128)(2,1)S(1)}, bf16[64,768]{1,0:T(8,128)(2,1)S...) custom-call(bf16[3,1024,768]{2,1,0:T(8,128)(2,1)S(1)} %bitcast.14, ...), custom_call_target="tpu_custom_call" | custom-call | flops 3000000000 | bytes 2097152 | tf_op jit(solution)/shard_map/forward_far/pallas_call | solution.py:346
  31.3 1.0 %collective-permute-done.9.refs_6_.refs_7_ = bf16[64,768]{1,0:T(8,128)(2,1)S(1)} collective-permute-done((bf16[64,768]{1,0:T(8,128)(2,1)S(1)}, bf16[64,768]{1,0:T(8,128)(2,1)S(1)}, u32[]{:S(2)}, u32[]{:S(2)}) %collective-permute-start.9) | collective-permute-done | bytes 98336 | tf_op jit(solution)/shard_map/ppermute | solution.py:364
  32.6 2.2 %collective-permute-start.13 = (bf16[128,768]{1,0:T(8,128)(2,1)S(1)}, bf16[128,768]{1,0:T(8,128)(2,1)S(1)}, u32[]{:S(2)}, u32[]{:S(2)}) collective-permute-start(bf16[128,768]{1,0:T(8,128)(2,1)S(1)} %get-tuple-element.97), channel_id=1, source_target_pairs={{0,8},{2,10},{4,12},{6,14},{8,0},{10,2},{12,4},{14,6},{1,9},{3,11}... | collective-permute-start | bytes 589832 | tf_op jit(solution)/shard_map/ppermute | solution.py:369
  34.8 2.6 %collective-permute-start.14 = (bf16[64,768]{1,0:T(8,128)(2,1)S(1)}, bf16[64,768]{1,0:T(8,128)(2,1)S(1)}, u32[]{:S(2)}, u32[]{:S(2)}) collective-permute-start(bf16[64,768]{1,0:T(8,128)(2,1)S(1)} %get-tuple-element.98), channel_id=1, source_target_pairs={{0,6},{2,4},{4,2},{6,0},{8,14},{10,12},{12,10},{14,8},{1,7},{3,5},... | collective-permute-start | bytes 294920 | tf_op jit(solution)/shard_map/ppermute | solution.py:364
  37.4 0.9 %collective-permute-start.16 = (bf16[64,768]{1,0:T(8,128)(2,1)S(1)}, bf16[64,768]{1,0:T(8,128)(2,1)S(1)}, u32[]{:S(2)}, u32[]{:S(2)}) collective-permute-start(bf16[64,768]{1,0:T(8,128)(2,1)S(1)} %get-tuple-element.100), channel_id=1, source_target_pairs={{0,2},{2,0},{4,6},{6,4},{8,10},{10,8},{12,14},{14,12},{1,3},{3,1},... | collective-permute-start | bytes 294920 | tf_op jit(solution)/shard_map/ppermute | solution.py:364
  38.3 5.9 %collective-permute-done.13.refs_1_ = bf16[128,768]{1,0:T(8,128)(2,1)S(1)} collective-permute-done((bf16[128,768]{1,0:T(8,128)(2,1)S(1)}, bf16[128,768]{1,0:T(8,128)(2,1)S(1)}, u32[]{:S(2)}, u32[]{:S(2)}) %collective-permute-start.13) | collective-permute-done | bytes 196640 | tf_op jit(solution)/shard_map/ppermute | solution.py:369
  44.2 1.5 %collective-permute-done.15.refs_5_ = bf16[64,768]{1,0:T(8,128)(2,1)S(1)} collective-permute-done((bf16[64,768]{1,0:T(8,128)(2,1)S(1)}, bf16[64,768]{1,0:T(8,128)(2,1)S(1)}, u32[]{:S(2)}, u32[]{:S(2)}) %collective-permute-start.15) | collective-permute-done | bytes 98336 | tf_op jit(solution)/shard_map/ppermute | solution.py:364
  45.7 0.6 far_grad.1
  46.3 1.1 %collective-permute-start.19 = (bf16[64,768]{1,0:T(8,128)(2,1)S(1)}, bf16[64,768]{1,0:T(8,128)(2,1)S(1)}, u32[]{:S(2)}, u32[]{:S(2)}) collective-permute-start(bf16[64,768]{1,0:T(8,128)(2,1)S(1)} %get-tuple-element.106), channel_id=1, source_target_pairs={{0,6},{2,4},{4,2},{6,0},{8,14},{10,12},{12,10},{14,8},{1,7},{3,5},... | collective-permute-start | bytes 294920 | tf_op jit(solution)/shard_map/ppermute | solution.py:364
  47.4 1.5 %collective-permute-start.20 = (bf16[64,768]{1,0:T(8,128)(2,1)S(1)}, bf16[64,768]{1,0:T(8,128)(2,1)S(1)}, u32[]{:S(2)}, u32[]{:S(2)}) collective-permute-start(bf16[64,768]{1,0:T(8,128)(2,1)S(1)} %get-tuple-element.107), channel_id=1, source_target_pairs={{0,4},{2,6},{4,0},{6,2},{8,12},{10,14},{12,8},{14,10},{1,5},{3,7},... | collective-permute-start | bytes 294920 | tf_op jit(solution)/shard_map/ppermute | solution.py:364
  48.9 0.9 %collective-permute-start.21 = (bf16[64,768]{1,0:T(8,128)(2,1)S(1)}, bf16[64,768]{1,0:T(8,128)(2,1)S(1)}, u32[]{:S(2)}, u32[]{:S(2)}) collective-permute-start(bf16[64,768]{1,0:T(8,128)(2,1)S(1)} %get-tuple-element.108), channel_id=1, source_target_pairs={{0,2},{2,0},{4,6},{6,4},{8,10},{10,8},{12,14},{14,12},{1,3},{3,1},... | collective-permute-start | bytes 294920 | tf_op jit(solution)/shard_map/ppermute | solution.py:364
  49.9 1.1 %collective-permute-start.18 = (bf16[128,768]{1,0:T(8,128)(2,1)S(1)}, bf16[128,768]{1,0:T(8,128)(2,1)S(1)}, u32[]{:S(2)}, u32[]{:S(2)}) collective-permute-start(bf16[128,768]{1,0:T(8,128)(2,1)S(1)} %get-tuple-element.102), channel_id=1, source_target_pairs={{0,8},{2,10},{4,12},{6,14},{8,0},{10,2},{12,4},{14,6},{1,9},{3,11}... | collective-permute-start | bytes 589832 | tf_op jit(solution)/shard_map/ppermute | solution.py:369
  50.9 1.8 %collective-permute-done.19.refs_5_ = bf16[64,768]{1,0:T(8,128)(2,1)S(1)} collective-permute-done((bf16[64,768]{1,0:T(8,128)(2,1)S(1)}, bf16[64,768]{1,0:T(8,128)(2,1)S(1)}, u32[]{:S(2)}, u32[]{:S(2)}) %collective-permute-start.19) | collective-permute-done | bytes 98336 | tf_op jit(solution)/shard_map/ppermute | solution.py:364
  52.7 2.4 %collective-permute-done.20.refs_6_ = bf16[64,768]{1,0:T(8,128)(2,1)S(1)} collective-permute-done((bf16[64,768]{1,0:T(8,128)(2,1)S(1)}, bf16[64,768]{1,0:T(8,128)(2,1)S(1)}, u32[]{:S(2)}, u32[]{:S(2)}) %collective-permute-start.20) | collective-permute-done | bytes 98336 | tf_op jit(solution)/shard_map/ppermute | solution.py:364
  55.2 3.8 %backward_far.1 = (bf16[64,768]{1,0:T(8,128)(2,1)S(1)}, bf16[64,768]{1,0:T(8,128)(2,1)S(1)}, bf16[64,768]{1,0:T(8,128)(2,1)S(1)}, bf16[64,768]{1,0:T(8,128)(2,1)...) custom-call(bf16[3,1024,768]{2,1,0:T(8,128)(2,1)S(1)} %bitcast.15, ...), custom_call_target="tpu_custom_call" | custom-call | flops 3000000000 | bytes 2097152 | tf_op jit(solution)/shard_map/backward_far/pallas_call | solution.py:346
  59.1 1.8 %collective-permute-start.23 = (bf16[64,768]{1,0:T(8,128)(2,1)S(1)}, bf16[64,768]{1,0:T(8,128)(2,1)S(1)}, u32[]{:S(2)}, u32[]{:S(2)}) collective-permute-start(bf16[64,768]{1,0:T(8,128)(2,1)S(1)} %get-tuple-element.114), channel_id=1, source_target_pairs={{0,4},{2,6},{4,0},{6,2},{8,12},{10,14},{12,8},{14,10},{1,5},{3,7},... | collective-permute-start | bytes 294920 | tf_op jit(solution)/shard_map/ppermute | solution.py:364
  60.9 1.7 %collective-permute-start.24 = (bf16[64,768]{1,0:T(8,128)(2,1)S(1)}, bf16[64,768]{1,0:T(8,128)(2,1)S(1)}, u32[]{:S(2)}, u32[]{:S(2)}) collective-permute-start(bf16[64,768]{1,0:T(8,128)(2,1)S(1)} %get-tuple-element.115), channel_id=1, source_target_pairs={{0,2},{2,0},{4,6},{6,4},{8,10},{10,8},{12,14},{14,12},{1,3},{3,1},... | collective-permute-start | bytes 294920 | tf_op jit(solution)/shard_map/ppermute | solution.py:364
  62.6 1.1 %near_grad.1 = (bf16[128,768]{1,0:T(8,128)(2,1)}, f32[2,128]{1,0:T(2,128)S(1)}, bf16[64,768]{1,0:T(8,128)(2,1)S(1)}, bf16[64,768]{1,0:T(8,128)(2,1)S(1)}, bf16[6...) custom-call(f32[8,128]{1,0:T(8,128)S(1)} %get-tuple-element.72.refs_0_, ...), custom_call_target="tpu_custom_call" | custom-call | flops 30000001024 | bytes 2097152 | tf_op jit(solution)/shard_map/near_grad/pallas_call | solution.py:346
  63.8 1.8 %collective-permute-done.22.refs_3_ = bf16[64,768]{1,0:T(8,128)(2,1)S(1)} collective-permute-done((bf16[64,768]{1,0:T(8,128)(2,1)S(1)}, bf16[64,768]{1,0:T(8,128)(2,1)S(1)}, u32[]{:S(2)}, u32[]{:S(2)}) %collective-permute-start.22) | collective-permute-done | bytes 98336 | tf_op jit(solution)/shard_map/ppermute | solution.py:364
  65.6 0.9 %collective-permute-done.23.refs_4_ = bf16[64,768]{1,0:T(8,128)(2,1)S(1)} collective-permute-done((bf16[64,768]{1,0:T(8,128)(2,1)S(1)}, bf16[64,768]{1,0:T(8,128)(2,1)S(1)}, u32[]{:S(2)}, u32[]{:S(2)}) %collective-permute-start.23) | collective-permute-done | bytes 98336 | tf_op jit(solution)/shard_map/ppermute | solution.py:364
  66.5 1.7 %collective-permute-start.28 = (bf16[64,768]{1,0:T(8,128)(2,1)S(1)}, bf16[64,768]{1,0:T(8,128)(2,1)S(1)}, u32[]{:S(2)}, u32[]{:S(2)}) collective-permute-start(bf16[64,768]{1,0:T(8,128)(2,1)S(1)} %get-tuple-element.121), channel_id=1, source_target_pairs={{0,2},{2,0},{4,6},{6,4},{8,10},{10,8},{12,14},{14,12},{1,3},{3,1},... | collective-permute-start | bytes 294920 | tf_op jit(solution)/shard_map/ppermute | solution.py:364
  68.2 0.4 far_back.1.refs_6_.refs_8_
  68.6 0.5 collective-permute-start.25
  69.1 2.6 %weight_far.1 = (bf16[3,1024,768]{2,1,0:T(8,128)(2,1)S(1)}, f32[8,128]{1,0:T(8,128)S(1)}) custom-call(bf16[7,256,256]{2,1,0:T(8,128)(2,1)S(1)} %get-tuple-element.101.refs_0_, bf16[7,256,256]{2,1,0:T(8,128)(2,1)S(1)} %collective-permute-done.17.refs_7_.refs_1_, bf16[11,256,256]{2,1,0:T(8,128)(2,1)S(1)} %get-tuple-element.122.refs_2_, ...), custom_call_target="tpu_custom_call" | custom-call | flops 2400000000 | bytes 2097152 | tf_op jit(solution)/shard_map/weight_far/pallas_call | solution.py:346
  71.8 3.8 %backward_near.1 = (bf16[64,768]{1,0:T(8,128)(2,1)S(1)}, bf16[64,768]{1,0:T(8,128)(2,1)S(1)}, bf16[64,768]{1,0:T(8,128)(2,1)S(1)}, bf16[64,768]{1,0:T(8,128)(2,1...) custom-call(bf16[3,1024,768]{2,1,0:T(8,128)(2,1)S(1)} %bitcast.16, ...), custom_call_target="tpu_custom_call" | custom-call | flops 10000000000 | bytes 2097152 | tf_op jit(solution)/shard_map/backward_near/pallas_call | solution.py:346
  75.6 2.9 %collective-permute-start.30 = (bf16[64,768]{1,0:T(8,128)(2,1)S(1)}, bf16[64,768]{1,0:T(8,128)(2,1)S(1)}, u32[]{:S(2)}, u32[]{:S(2)}) collective-permute-start(bf16[64,768]{1,0:T(8,128)(2,1)S(1)} %get-tuple-element.129), channel_id=1, source_target_pairs={{0,6},{2,4},{4,2},{6,0},{8,14},{10,12},{12,10},{14,8},{1,7},{3,5},... | collective-permute-start | bytes 294920 | tf_op jit(solution)/shard_map/ppermute | solution.py:364
  78.6 0.5 collective-permute-start.31
  79.1 0.6 collective-permute-start.32
  79.6 1.2 %collective-permute-done.25.refs_0_ = bf16[144,768]{1,0:T(8,128)(2,1)S(1)} collective-permute-done((bf16[144,768]{1,0:T(8,128)(2,1)S(1)}, bf16[144,768]{1,0:T(8,128)(2,1)S(1)}, u32[]{:S(2)}, u32[]{:S(2)}) %collective-permute-start.25) | collective-permute-done | bytes 221216 | tf_op jit(solution)/shard_map/ppermute | solution.py:369
  80.8 3.9 %weight_near.1 = (bf16[3,1024,768]{2,1,0:T(8,128)(2,1)}, f32[8,128]{1,0:T(8,128)S(1)}) custom-call(bf16[3,1024,768]{2,1,0:T(8,128)(2,1)S(1)} %get-tuple-element.132.refs_0_, bf16[7,256,256]{2,1,0:T(8,128)(2,1)S(1)} %get-tuple-element.79.refs_6_.refs_1_, bf16[7,256,256]{2,1,0:T(8,128)(2,1)S(1)} %collective-permute-done.6.refs_0_.refs_8_.refs_2_, ...), custom_call_target="tpu_custom_call" | custom-call | flops 30000001024 | bytes 2097152 | tf_op jit(solution)/shard_map/weight_near/pallas_call | solution.py:346
  85.0 0.9 %combine_gradients.1 = (bf16[128,768]{1,0:T(8,128)(2,1)}, f32[2,128]{1,0:T(2,128)}) custom-call(bf16[2,256,128]{2,1,0:T(8,128)(2,1)S(1)} %get-tuple-element.73.refs_1_.refs_0_, bf16[144,768]{1,0:T(8,128)(2,1)S(1)} %get-tuple-element.126.refs_1_, f32[2,128]{1,0:T(2,128)S(1)} %get-tuple-element.127.refs_2_, bf16[64,768]{1,0:T(8,128)(2,1)S(1)} %get-tuple-element.128.refs_3_, ...), custom_call_target="tpu_custom_call" | custom-call | flops 30000001024 | bytes 2097152 | tf_op jit(solution)/shard_map/combine_gradients/pallas_call | solution.py:346
  (51 shorter events, 2.1 us)
Async XLA Ops:
  0.6 20.1 %collective-permute-start.2 = (bf16[3,1024,768]{2,1,0:T(8,128)(2,1)}, bf16[3,1024,768]{2,1,0:T(8,128)(2,1)S(1)}, u32[]{:S(2)}, u32[]{:S(2)}) collective-permute-start(bf16[3,1024,768]{2,1,0:T(8,128)(2,1)} %bitcast.9), channel_id=1, source_target_pairs={{0,1},{1,0},{2,3},{3,2},{4,5},{5,4},{6,7},{7,6},{8,9},{9,8},{10,11... | collective-permute-start | bytes 14155784 | tf_op jit(solution)/shard_map/ppermute | solution.py:372
  1.1 15.4 %collective-permute-start.1 = (bf16[128,768]{1,0:T(8,128)(2,1)}, bf16[128,768]{1,0:T(8,128)(2,1)S(1)}, u32[]{:S(2)}, u32[]{:S(2)}) collective-permute-start(bf16[128,768]{1,0:T(8,128)(2,1)} %refs_3_.1), channel_id=1, source_target_pairs={{0,8},{2,10},{4,12},{6,14},{8,0},{10,2},{12,4},{14,6},{1,9},{3,11}... | collective-permute-start | bytes 589832 | tf_op jit(solution)/shard_map/ppermute | solution.py:369
  4.8 2.3 %copy-start = (bf16[1,1024,3,768]{3,1,2,0:T(8,128)(2,1)S(1)}, bf16[1,1024,3,768]{3,1,2,0:T(8,128)(2,1)}, u32[]{:S(2)}) copy-start(bf16[1,1024,3,768]{3,1,2,0:T(8,128)(2,1)} %param.9) | copy-start | bytes 14155780
  7.2 0.9 %copy-start.1 = (bf16[128,768]{1,0:T(8,128)(2,1)S(1)}, bf16[128,768]{1,0:T(8,128)(2,1)}, u32[]{:S(2)}) copy-start(bf16[128,768]{1,0:T(8,128)(2,1)} %refs_3_.1) | copy-start | bytes 589828
  8.1 0.7 copy-start.3
  8.8 0.7 copy-start.4
  9.8 5.1 %collective-permute-start = (f32[8,128]{1,0:T(8,128)S(1)}, f32[8,128]{1,0:T(8,128)S(1)}, u32[]{:S(2)}, u32[]{:S(2)}) collective-permute-start(f32[8,128]{1,0:T(8,128)S(1)} %get-tuple-element.72.refs_0_), channel_id=1, source_target_pairs={{0,8},{2,10},{4,12},{6,14},{8,0},{10,2},{12,4},{14,6},{1,9},{3,11}... | collective-permute-start | bytes 12296 | tf_op jit(solution)/shard_map/ppermute | solution.py:369
  9.9 8.1 %collective-permute-start.3 = (bf16[64,768]{1,0:T(8,128)(2,1)S(1)}, bf16[64,768]{1,0:T(8,128)(2,1)S(1)}, u32[]{:S(2)}, u32[]{:S(2)}) collective-permute-start(bf16[64,768]{1,0:T(8,128)(2,1)S(1)} %get-tuple-element.76), channel_id=1, source_target_pairs={{0,6},{2,4},{4,2},{6,0},{8,14},{10,12},{12,10},{14,8},{1,7},{3,5},... | collective-permute-start | bytes 294920 | tf_op jit(solution)/shard_map/ppermute | solution.py:364
  12.8 6.4 %collective-permute-start.4 = (bf16[64,768]{1,0:T(8,128)(2,1)S(1)}, bf16[64,768]{1,0:T(8,128)(2,1)S(1)}, u32[]{:S(2)}, u32[]{:S(2)}) collective-permute-start(bf16[64,768]{1,0:T(8,128)(2,1)S(1)} %get-tuple-element.77), channel_id=1, source_target_pairs={{0,4},{2,6},{4,0},{6,2},{8,12},{10,14},{12,8},{14,10},{1,5},{3,7},... | collective-permute-start | bytes 294920 | tf_op jit(solution)/shard_map/ppermute | solution.py:364
  14.9 5.8 %slice-start = ((s8[4718592]{0:T(1024)(128)(4,1)}), s8[4194304]{0:T(1024)(128)(4,1)S(1)}, s32[]{:S(2)}) async-start(s8[4718592]{0:T(1024)(128)(4,1)} %bitcast.11), calls=%async_computation | async-start | bytes 8388608
  14.9 5.8 %slice-start.1 = ((s8[4718592]{0:T(1024)(128)(4,1)}), s8[524288]{0:T(1024)(128)(4,1)S(1)}, s32[]{:S(2)}) async-start(s8[4718592]{0:T(1024)(128)(4,1)} %bitcast.11), calls=%async_computation.1 | async-start | bytes 1048576
  14.9 5.8 %collective-permute-start.5 = (bf16[64,768]{1,0:T(8,128)(2,1)S(1)}, bf16[64,768]{1,0:T(8,128)(2,1)S(1)}, u32[]{:S(2)}, u32[]{:S(2)}) collective-permute-start(bf16[64,768]{1,0:T(8,128)(2,1)S(1)} %get-tuple-element.78), channel_id=1, source_target_pairs={{0,2},{2,0},{4,6},{6,4},{8,10},{10,8},{12,14},{14,12},{1,3},{3,1},... | collective-permute-start | bytes 294920 | tf_op jit(solution)/shard_map/ppermute | solution.py:364
  16.9 10.7 %collective-permute-start.10 = (bf16[64,768]{1,0:T(8,128)(2,1)S(1)}, bf16[64,768]{1,0:T(8,128)(2,1)S(1)}, u32[]{:S(2)}, u32[]{:S(2)}) collective-permute-start(bf16[64,768]{1,0:T(8,128)(2,1)S(1)} %get-tuple-element.85), channel_id=1, source_target_pairs={{0,6},{2,4},{4,2},{6,0},{8,14},{10,12},{12,10},{14,8},{1,7},{3,5},... | collective-permute-start | bytes 294920 | tf_op jit(solution)/shard_map/ppermute | solution.py:364
  18.0 9.7 %collective-permute-start.11 = (bf16[64,768]{1,0:T(8,128)(2,1)S(1)}, bf16[64,768]{1,0:T(8,128)(2,1)S(1)}, u32[]{:S(2)}, u32[]{:S(2)}) collective-permute-start(bf16[64,768]{1,0:T(8,128)(2,1)S(1)} %get-tuple-element.86), channel_id=1, source_target_pairs={{0,4},{2,6},{4,0},{6,2},{8,12},{10,14},{12,8},{14,10},{1,5},{3,7},... | collective-permute-start | bytes 294920 | tf_op jit(solution)/shard_map/ppermute | solution.py:364
  19.1 8.6 %collective-permute-start.12 = (bf16[64,768]{1,0:T(8,128)(2,1)S(1)}, bf16[64,768]{1,0:T(8,128)(2,1)S(1)}, u32[]{:S(2)}, u32[]{:S(2)}) collective-permute-start(bf16[64,768]{1,0:T(8,128)(2,1)S(1)} %get-tuple-element.87), channel_id=1, source_target_pairs={{0,2},{2,0},{4,6},{6,4},{8,10},{10,8},{12,14},{14,12},{1,3},{3,1},... | collective-permute-start | bytes 294920 | tf_op jit(solution)/shard_map/ppermute | solution.py:364
  24.1 7.0 %collective-permute-start.7 = (bf16[64,768]{1,0:T(8,128)(2,1)S(1)}, bf16[64,768]{1,0:T(8,128)(2,1)S(1)}, u32[]{:S(2)}, u32[]{:S(2)}) collective-permute-start(bf16[64,768]{1,0:T(8,128)(2,1)S(1)} %get-tuple-element.81), channel_id=1, source_target_pairs={{0,6},{2,4},{4,2},{6,0},{8,14},{10,12},{12,10},{14,8},{1,7},{3,5},... | collective-permute-start | bytes 294920 | tf_op jit(solution)/shard_map/ppermute | solution.py:364
  26.5 4.8 %collective-permute-start.8 = (bf16[64,768]{1,0:T(8,128)(2,1)S(1)}, bf16[64,768]{1,0:T(8,128)(2,1)S(1)}, u32[]{:S(2)}, u32[]{:S(2)}) collective-permute-start(bf16[64,768]{1,0:T(8,128)(2,1)S(1)} %get-tuple-element.82), channel_id=1, source_target_pairs={{0,4},{2,6},{4,0},{6,2},{8,12},{10,14},{12,8},{14,10},{1,5},{3,7},... | collective-permute-start | bytes 294920 | tf_op jit(solution)/shard_map/ppermute | solution.py:364
  27.6 4.6 %collective-permute-start.9 = (bf16[64,768]{1,0:T(8,128)(2,1)S(1)}, bf16[64,768]{1,0:T(8,128)(2,1)S(1)}, u32[]{:S(2)}, u32[]{:S(2)}) collective-permute-start(bf16[64,768]{1,0:T(8,128)(2,1)S(1)} %get-tuple-element.83), channel_id=1, source_target_pairs={{0,2},{2,0},{4,6},{6,4},{8,10},{10,8},{12,14},{14,12},{1,3},{3,1},... | collective-permute-start | bytes 294920 | tf_op jit(solution)/shard_map/ppermute | solution.py:364
  27.7 7.1 %collective-permute-start.6 = (bf16[7,256,256]{2,1,0:T(8,128)(2,1)S(1)}, bf16[7,256,256]{2,1,0:T(8,128)(2,1)S(1)}, u32[]{:S(2)}, u32[]{:S(2)}) collective-permute-start(bf16[7,256,256]{2,1,0:T(8,128)(2,1)S(1)} %get-tuple-element.79.refs_6_.refs_1_), channel_id=1, source_target_pairs={{0,1},{1,0},{2,3},{3,2},{4,5},{5,4},{6,7},{7,6},{8,9},{9,8},{10,11... | collective-permute-start | bytes 2752520 | tf_op jit(solution)/shard_map/ppermute | solution.py:372
  27.7 4.5 %copy-start.2 = (bf16[128,768]{1,0:T(8,128)(2,1)S(1)}, bf16[128,768]{1,0:T(8,128)(2,1)}, u32[]{:S(2)}) copy-start(bf16[128,768]{1,0:T(8,128)(2,1)} %refs_2_.3) | copy-start | bytes 589828
  32.6 11.6 %collective-permute-start.13 = (bf16[128,768]{1,0:T(8,128)(2,1)S(1)}, bf16[128,768]{1,0:T(8,128)(2,1)S(1)}, u32[]{:S(2)}, u32[]{:S(2)}) collective-permute-start(bf16[128,768]{1,0:T(8,128)(2,1)S(1)} %get-tuple-element.97), channel_id=1, source_target_pairs={{0,8},{2,10},{4,12},{6,14},{8,0},{10,2},{12,4},{14,6},{1,9},{3,11}... | collective-permute-start | bytes 589832 | tf_op jit(solution)/shard_map/ppermute | solution.py:369
  34.8 9.4 %collective-permute-start.17 = (bf16[7,256,256]{2,1,0:T(8,128)(2,1)S(1)}, bf16[7,256,256]{2,1,0:T(8,128)(2,1)S(1)}, u32[]{:S(2)}, u32[]{:S(2)}) collective-permute-start(bf16[7,256,256]{2,1,0:T(8,128)(2,1)S(1)} %get-tuple-element.101.refs_0_), channel_id=1, source_target_pairs={{0,1},{1,0},{2,3},{3,2},{4,5},{5,4},{6,7},{7,6},{8,9},{9,8},{10,11... | collective-permute-start | bytes 2752520 | tf_op jit(solution)/shard_map/ppermute | solution.py:372
  34.8 9.4 %collective-permute-start.14 = (bf16[64,768]{1,0:T(8,128)(2,1)S(1)}, bf16[64,768]{1,0:T(8,128)(2,1)S(1)}, u32[]{:S(2)}, u32[]{:S(2)}) collective-permute-start(bf16[64,768]{1,0:T(8,128)(2,1)S(1)} %get-tuple-element.98), channel_id=1, source_target_pairs={{0,6},{2,4},{4,2},{6,0},{8,14},{10,12},{12,10},{14,8},{1,7},{3,5},... | collective-permute-start | bytes 294920 | tf_op jit(solution)/shard_map/ppermute | solution.py:364
  37.4 8.3 %collective-permute-start.15 = (bf16[64,768]{1,0:T(8,128)(2,1)S(1)}, bf16[64,768]{1,0:T(8,128)(2,1)S(1)}, u32[]{:S(2)}, u32[]{:S(2)}) collective-permute-start(bf16[64,768]{1,0:T(8,128)(2,1)S(1)} %get-tuple-element.99), channel_id=1, source_target_pairs={{0,4},{2,6},{4,0},{6,2},{8,12},{10,14},{12,8},{14,10},{1,5},{3,7},... | collective-permute-start | bytes 294920 | tf_op jit(solution)/shard_map/ppermute | solution.py:364
  37.4 8.3 %collective-permute-start.16 = (bf16[64,768]{1,0:T(8,128)(2,1)S(1)}, bf16[64,768]{1,0:T(8,128)(2,1)S(1)}, u32[]{:S(2)}, u32[]{:S(2)}) collective-permute-start(bf16[64,768]{1,0:T(8,128)(2,1)S(1)} %get-tuple-element.100), channel_id=1, source_target_pairs={{0,2},{2,0},{4,6},{6,4},{8,10},{10,8},{12,14},{14,12},{1,3},{3,1},... | collective-permute-start | bytes 294920 | tf_op jit(solution)/shard_map/ppermute | solution.py:364
  46.3 6.4 %collective-permute-start.19 = (bf16[64,768]{1,0:T(8,128)(2,1)S(1)}, bf16[64,768]{1,0:T(8,128)(2,1)S(1)}, u32[]{:S(2)}, u32[]{:S(2)}) collective-permute-start(bf16[64,768]{1,0:T(8,128)(2,1)S(1)} %get-tuple-element.106), channel_id=1, source_target_pairs={{0,6},{2,4},{4,2},{6,0},{8,14},{10,12},{12,10},{14,8},{1,7},{3,5},... | collective-permute-start | bytes 294920 | tf_op jit(solution)/shard_map/ppermute | solution.py:364
  47.4 7.7 %collective-permute-start.20 = (bf16[64,768]{1,0:T(8,128)(2,1)S(1)}, bf16[64,768]{1,0:T(8,128)(2,1)S(1)}, u32[]{:S(2)}, u32[]{:S(2)}) collective-permute-start(bf16[64,768]{1,0:T(8,128)(2,1)S(1)} %get-tuple-element.107), channel_id=1, source_target_pairs={{0,4},{2,6},{4,0},{6,2},{8,12},{10,14},{12,8},{14,10},{1,5},{3,7},... | collective-permute-start | bytes 294920 | tf_op jit(solution)/shard_map/ppermute | solution.py:364
  48.9 6.3 %collective-permute-start.21 = (bf16[64,768]{1,0:T(8,128)(2,1)S(1)}, bf16[64,768]{1,0:T(8,128)(2,1)S(1)}, u32[]{:S(2)}, u32[]{:S(2)}) collective-permute-start(bf16[64,768]{1,0:T(8,128)(2,1)S(1)} %get-tuple-element.108), channel_id=1, source_target_pairs={{0,2},{2,0},{4,6},{6,4},{8,10},{10,8},{12,14},{14,12},{1,3},{3,1},... | collective-permute-start | bytes 294920 | tf_op jit(solution)/shard_map/ppermute | solution.py:364
  49.9 12.7 %collective-permute-start.18 = (bf16[128,768]{1,0:T(8,128)(2,1)S(1)}, bf16[128,768]{1,0:T(8,128)(2,1)S(1)}, u32[]{:S(2)}, u32[]{:S(2)}) collective-permute-start(bf16[128,768]{1,0:T(8,128)(2,1)S(1)} %get-tuple-element.102), channel_id=1, source_target_pairs={{0,8},{2,10},{4,12},{6,14},{8,0},{10,2},{12,4},{14,6},{1,9},{3,11}... | collective-permute-start | bytes 589832 | tf_op jit(solution)/shard_map/ppermute | solution.py:369
  58.9 10.2 %collective-permute-start.29 = (bf16[11,256,256]{2,1,0:T(8,128)(2,1)S(1)}, bf16[11,256,256]{2,1,0:T(8,128)(2,1)S(1)}, u32[]{:S(2)}, u32[]{:S(2)}) collective-permute-start(bf16[11,256,256]{2,1,0:T(8,128)(2,1)S(1)} %get-tuple-element.122.refs_2_), channel_id=1, source_target_pairs={{0,1},{1,0},{2,3},{3,2},{4,5},{5,4},{6,7},{7,6},{8,9},{9,8},{10,11... | collective-permute-start | bytes 4325384 | tf_op jit(solution)/shard_map/ppermute | solution.py:372
  59.0 6.6 %collective-permute-start.22 = (bf16[64,768]{1,0:T(8,128)(2,1)S(1)}, bf16[64,768]{1,0:T(8,128)(2,1)S(1)}, u32[]{:S(2)}, u32[]{:S(2)}) collective-permute-start(bf16[64,768]{1,0:T(8,128)(2,1)S(1)} %get-tuple-element.113), channel_id=1, source_target_pairs={{0,6},{2,4},{4,2},{6,0},{8,14},{10,12},{12,10},{14,8},{1,7},{3,5},... | collective-permute-start | bytes 294920 | tf_op jit(solution)/shard_map/ppermute | solution.py:364
  59.1 7.4 %collective-permute-start.23 = (bf16[64,768]{1,0:T(8,128)(2,1)S(1)}, bf16[64,768]{1,0:T(8,128)(2,1)S(1)}, u32[]{:S(2)}, u32[]{:S(2)}) collective-permute-start(bf16[64,768]{1,0:T(8,128)(2,1)S(1)} %get-tuple-element.114), channel_id=1, source_target_pairs={{0,4},{2,6},{4,0},{6,2},{8,12},{10,14},{12,8},{14,10},{1,5},{3,7},... | collective-permute-start | bytes 294920 | tf_op jit(solution)/shard_map/ppermute | solution.py:364
  60.9 7.3 %collective-permute-start.24 = (bf16[64,768]{1,0:T(8,128)(2,1)S(1)}, bf16[64,768]{1,0:T(8,128)(2,1)S(1)}, u32[]{:S(2)}, u32[]{:S(2)}) collective-permute-start(bf16[64,768]{1,0:T(8,128)(2,1)S(1)} %get-tuple-element.115), channel_id=1, source_target_pairs={{0,2},{2,0},{4,6},{6,4},{8,10},{10,8},{12,14},{14,12},{1,3},{3,1},... | collective-permute-start | bytes 294920 | tf_op jit(solution)/shard_map/ppermute | solution.py:364
  63.7 8.0 %collective-permute-start.26 = (bf16[64,768]{1,0:T(8,128)(2,1)S(1)}, bf16[64,768]{1,0:T(8,128)(2,1)S(1)}, u32[]{:S(2)}, u32[]{:S(2)}) collective-permute-start(bf16[64,768]{1,0:T(8,128)(2,1)S(1)} %get-tuple-element.119), channel_id=1, source_target_pairs={{0,6},{2,4},{4,2},{6,0},{8,14},{10,12},{12,10},{14,8},{1,7},{3,5},... | collective-permute-start | bytes 294920 | tf_op jit(solution)/shard_map/ppermute | solution.py:364
  65.6 6.2 %collective-permute-start.27 = (bf16[64,768]{1,0:T(8,128)(2,1)S(1)}, bf16[64,768]{1,0:T(8,128)(2,1)S(1)}, u32[]{:S(2)}, u32[]{:S(2)}) collective-permute-start(bf16[64,768]{1,0:T(8,128)(2,1)S(1)} %get-tuple-element.120), channel_id=1, source_target_pairs={{0,4},{2,6},{4,0},{6,2},{8,12},{10,14},{12,8},{14,10},{1,5},{3,7},... | collective-permute-start | bytes 294920 | tf_op jit(solution)/shard_map/ppermute | solution.py:364
  66.5 5.3 %collective-permute-start.28 = (bf16[64,768]{1,0:T(8,128)(2,1)S(1)}, bf16[64,768]{1,0:T(8,128)(2,1)S(1)}, u32[]{:S(2)}, u32[]{:S(2)}) collective-permute-start(bf16[64,768]{1,0:T(8,128)(2,1)S(1)} %get-tuple-element.121), channel_id=1, source_target_pairs={{0,2},{2,0},{4,6},{6,4},{8,10},{10,8},{12,14},{14,12},{1,3},{3,1},... | collective-permute-start | bytes 294920 | tf_op jit(solution)/shard_map/ppermute | solution.py:364
  68.6 12.3 %collective-permute-start.25 = (bf16[144,768]{1,0:T(8,128)(2,1)S(1)}, bf16[144,768]{1,0:T(8,128)(2,1)S(1)}, u32[]{:S(2)}, u32[]{:S(2)}) collective-permute-start(bf16[144,768]{1,0:T(8,128)(2,1)S(1)} %far_back.1.refs_6_.refs_8_), channel_id=1, source_target_pairs={{0,8},{2,10},{4,12},{6,14},{8,0},{10,2},{12,4},{14,6},{1,9},{3,11}... | collective-permute-start | bytes 663560 | tf_op jit(solution)/shard_map/ppermute | solution.py:369
  75.5 5.3 %collective-permute-start.33 = (bf16[11,256,256]{2,1,0:T(8,128)(2,1)S(1)}, bf16[11,256,256]{2,1,0:T(8,128)(2,1)S(1)}, u32[]{:S(2)}, u32[]{:S(2)}) collective-permute-start(bf16[11,256,256]{2,1,0:T(8,128)(2,1)S(1)} %get-tuple-element.133.refs_3_), channel_id=1, source_target_pairs={{0,1},{1,0},{2,3},{3,2},{4,5},{5,4},{6,7},{7,6},{8,9},{9,8},{10,11... | collective-permute-start | bytes 4325384 | tf_op jit(solution)/shard_map/ppermute | solution.py:372
  75.6 9.1 %collective-permute-start.30 = (bf16[64,768]{1,0:T(8,128)(2,1)S(1)}, bf16[64,768]{1,0:T(8,128)(2,1)S(1)}, u32[]{:S(2)}, u32[]{:S(2)}) collective-permute-start(bf16[64,768]{1,0:T(8,128)(2,1)S(1)} %get-tuple-element.129), channel_id=1, source_target_pairs={{0,6},{2,4},{4,2},{6,0},{8,14},{10,12},{12,10},{14,8},{1,7},{3,5},... | collective-permute-start | bytes 294920 | tf_op jit(solution)/shard_map/ppermute | solution.py:364
  78.6 6.5 %collective-permute-start.31 = (bf16[64,768]{1,0:T(8,128)(2,1)S(1)}, bf16[64,768]{1,0:T(8,128)(2,1)S(1)}, u32[]{:S(2)}, u32[]{:S(2)}) collective-permute-start(bf16[64,768]{1,0:T(8,128)(2,1)S(1)} %get-tuple-element.130), channel_id=1, source_target_pairs={{0,4},{2,6},{4,0},{6,2},{8,12},{10,14},{12,8},{14,10},{1,5},{3,7},... | collective-permute-start | bytes 294920 | tf_op jit(solution)/shard_map/ppermute | solution.py:364
  79.1 5.9 %collective-permute-start.32 = (bf16[64,768]{1,0:T(8,128)(2,1)S(1)}, bf16[64,768]{1,0:T(8,128)(2,1)S(1)}, u32[]{:S(2)}, u32[]{:S(2)}) collective-permute-start(bf16[64,768]{1,0:T(8,128)(2,1)S(1)} %get-tuple-element.131), channel_id=1, source_target_pairs={{0,2},{2,0},{4,6},{6,4},{8,10},{10,8},{12,14},{14,12},{1,3},{3,1},... | collective-permute-start | bytes 294920 | tf_op jit(solution)/shard_map/ppermute | solution.py:364

commit v14 on v13

--- a/solution.py
+++ b/solution.py
@@ -109,12 +109,12 @@
     return m0, m1, g0, g1, o0, o1, g0 * o0 + g1 * o1
 
 
-def put_d_gates(ref, diff, o0, o1):
+def d_gates_of(diff, o0, o1):
     tok = diff.shape[0]
     lane = lax.broadcasted_iota(jnp.int32, (tok, 128), 1)
     d0 = jnp.sum(diff * o0, axis=1, keepdims=True)
     d1 = jnp.sum(diff * o1, axis=1, keepdims=True)
-    ref[...] = jnp.where(lane == 0, d0, jnp.where(lane == 1, d1, 0.0)).T[0:2, :]
+    return jnp.where(lane == 0, d0, jnp.where(lane == 1, d1, 0.0)).T[0:2, :]
 
 
 def put_route_grads(refs, m0, m1, g0, g1, diff):
@@ -197,17 +197,18 @@
 
 
 def far_grad_kernel(pieces, meta_ref, masks_ref, rest_ref, *refs):
-    ins, part_ref, d_gates_ref, outs = (
-        refs[:pieces],
-        refs[pieces],
-        refs[pieces + 1],
-        refs[pieces + 2 :],
-    )
+    ins, part_ref, outs = refs[:pieces], refs[pieces], refs[pieces + 1 :]
     m0, m1, g0, g1, o0, o1, total = route_sums(meta_ref[...], masks_ref, ins)
-    part_ref[...] = total.astype(BF16)
+    tok = total.shape[0]
+    part_ref[:tok, :] = total.astype(BF16)
     diff = total + rest_ref[...].astype(F32)
     put_route_grads(outs, m0, m1, g0, g1, diff)
-    put_d_gates(d_gates_ref, diff, o0, o1)
+    value = d_gates_of(diff, o0, o1)
+    high = value.astype(BF16)
+    low = (value - high.astype(F32)).astype(BF16)
+    rest = jnp.zeros((part_ref.shape[0] - tok - 4, tok), BF16)
+    part_ref[tok:, :tok] = jnp.concatenate([high, low, rest], axis=0)
+    part_ref[tok:, tok:] = jnp.zeros((part_ref.shape[0] - tok, part_ref.shape[1] - tok), BF16)
 
 
 def near_grad_kernel(pieces, meta_ref, masks_ref, teacher_ref, part_ref, *refs):
@@ -218,32 +219,24 @@
         refs[pieces + 2 :],
     )
     m0, m1, g0, g1, o0, o1, total = route_sums(meta_ref[...], masks_ref, ins)
-    total = total + part_ref[...].astype(F32)
+    tok = total.shape[0]
+    total = total + part_ref[:tok, :].astype(F32)
     student_ref[...] = total.astype(BF16)
     diff = total - teacher_ref[...].astype(F32)
     put_route_grads(outs, m0, m1, g0, g1, diff)
-    put_d_gates(d_gates_ref, diff, o0, o1)
-
-
-def far_back_kernel(masks_ref, d_gates_ref, *refs):
+    far = part_ref[tok:, :tok].astype(F32)
+    d_gates_ref[...] = d_gates_of(diff, o0, o1) + (far[0:2] + far[2:4])
+
+
+def far_back_kernel(masks_ref, *refs):
     ins, out_ref = refs[:-1], refs[-1]
-    tok = masks_ref.shape[2]
-    out_ref[:tok, :] = dot(masks_ref[0] + masks_ref[1], get(ins), FIRST).astype(BF16)
-    value = d_gates_ref[...]
-    high = value.astype(BF16)
-    low = (value - high.astype(F32)).astype(BF16)
-    rest = jnp.zeros((out_ref.shape[0] - tok - 4, tok), BF16)
-    out_ref[tok:, :tok] = jnp.concatenate([high, low, rest], axis=0)
-    out_ref[tok:, tok:] = jnp.zeros((out_ref.shape[0] - tok, out_ref.shape[1] - tok), BF16)
-
-
-def final_kernel(pieces, masks_ref, part_ref, near_ref, *refs):
-    ins, out_ref, d_gates_ref = refs[:pieces], refs[pieces], refs[pieces + 1]
-    tok = masks_ref.shape[2]
-    total = dot(masks_ref[0] + masks_ref[1], get(ins), FIRST) + part_ref[:tok, :].astype(F32)
+    out_ref[...] = dot(masks_ref[0] + masks_ref[1], get(ins), FIRST).astype(BF16)
+
+
+def final_kernel(masks_ref, part_ref, *refs):
+    ins, out_ref = refs[:-1], refs[-1]
+    total = dot(masks_ref[0] + masks_ref[1], get(ins), FIRST) + part_ref[...].astype(F32)
     out_ref[...] = total.astype(BF16)
-    far = part_ref[tok:, :tok].astype(F32)
-    d_gates_ref[...] = near_ref[...] + (far[0:2] + far[2:4])
 
 
 def weight_blocks(across, x, sent_x, g, sent_g, d, h):
@@ -445,7 +438,7 @@
     res = call(
         functools.partial(far_grad_kernel, half),
         "far_grad",
-        [dense, pair] + pieces,
+        [longer] + pieces,
         [],
         far_meta,
         far_masks,
@@ -453,7 +446,7 @@
         *got_far,
         after=[xf_sib, xn_sib],
     )
-    part, d_gates_far, rg_far = to_mirror(res[0]), res[1], within_half(res[2:])
+    part, rg_far = to_mirror(res[0]), within_half(res[1:])
     grad_far, (gf, df) = backward(rg_far, faf, fbf, "backward_far")
     res = call(
         functools.partial(near_grad_kernel, half),
@@ -467,12 +460,12 @@
         *got_near,
         after=[df],
     )
-    student, d_gates_near, rg_near = res[0], res[1], within_half(res[2:])
+    student, d_gates, rg_near = res[0], res[1], within_half(res[2:])
 
     back_far = within_half(grad_far)
     gf_sib = to_sibling(gf)
     part_rows = call(
-        far_back_kernel, "far_back", longer, [], far_masks, d_gates_far, *back_far
+        far_back_kernel, "far_back", dense, [], far_masks, *back_far, after=[rg_near[0]]
     )
     part = to_mirror(part_rows)
     far_weights, far_done = call(
@@ -503,14 +496,13 @@
         in_hbm=1,
     )
 
-    d_tokens, d_gates = call(
-        functools.partial(final_kernel, half),
+    d_tokens = call(
+        final_kernel,
         "combine_gradients",
-        [dense, pair],
+        dense,
         [],
         near_masks,
         part,
-        d_gates_near,
         *back_near,
         after=[finished],
     )

time: 86.2 us -> 85.5 us (level)
    ppermute x5, waiting for transfers between devices: 8.78 us -> 7.68 us  [to_mirror(): return lax.ppermute(x, 'expert', [(i, i ^ half) for i in range(experts)])]
where the time goes in v14:
time: 85.5 us; the launch traced here: 85.2 us
  starting transfers between devices  36.5 us (43%)
  Pallas kernels  25 us (29%)
  waiting for transfers between devices  18.3 us (21%)
  local copies, waits for them, and re-layouts  4.63 us (5%)
    ppermute x24, starting transfers between devices, within_half(): lax.ppermute(rows_of[s], 'expert', [(i, i ^ s) for i in range(experts)])  28.2 us
    pallas_call x16, Pallas kernels, call(): pl.pallas_call(body, in_specs=specs + [aspec] * (len(after) + len(through...  25 us
    ppermute x24, waiting for transfers between devices, within_half(): lax.ppermute(rows_of[s], 'expert', [(i, i ^ s) for i in range(experts)])  10.6 us
    ppermute x5, waiting for transfers between devices, to_mirror(): return lax.ppermute(x, 'expert', [(i, i ^ half) for i in range(experts)])  7.68 us
    ppermute x5, starting transfers between devices, to_mirror(): return lax.ppermute(x, 'expert', [(i, i ^ half) for i in range(experts)])  7.63 us
    unnamed x14, local copies, waits for them, and re-layouts  4.63 us
  transfers between devices with their start and end apart: 34, of which 13 were waited for; matrix products, arithmetic and copies ran while one was open for 0% of the time, Pallas kernels for 27%

profile of v14, /device:TPU:0, one launch (start us, length us, event | category | flops | bytes accessed | tf_op | source)
XLA Modules:
  0.0 85.2 jit_solution(9253360907307659164)
XLA Ops:
  0.6 0.5 collective-permute-start.2
  1.1 3.7 %collective-permute-start.1 = (bf16[128,768]{1,0:T(8,128)(2,1)}, bf16[128,768]{1,0:T(8,128)(2,1)S(1)}, u32[]{:S(2)}, u32[]{:S(2)}) collective-permute-start(bf16[128,768]{1,0:T(8,128)(2,1)} %refs_3_.1), channel_id=1, source_target_pairs={{0,8},{2,10},{4,12},{6,14},{8,0},{10,2},{12,4},{14,6},{1,9},{3,11}... | collective-permute-start | bytes 589832 | tf_op jit(solution)/shard_map/ppermute | solution.py:362
  4.8 2.3 %copy-done = bf16[1,1024,3,768]{3,1,2,0:T(8,128)(2,1)S(1)} copy-done((bf16[1,1024,3,768]{3,1,2,0:T(8,128)(2,1)S(1)}, bf16[1,1024,3,768]{3,1,2,0:T(8,128)(2,1)}, u32[]{:S(2)}) %copy-start) | copy-done | bytes 4718616
  7.2 0.9 %copy-done.1 = bf16[128,768]{1,0:T(8,128)(2,1)S(1)} copy-done((bf16[128,768]{1,0:T(8,128)(2,1)S(1)}, bf16[128,768]{1,0:T(8,128)(2,1)}, u32[]{:S(2)}) %copy-start.1) | copy-done | bytes 196632
  8.1 0.7 copy-done.3
  8.8 0.7 copy-done.4
  9.9 2.9 %collective-permute-start.3 = (bf16[64,768]{1,0:T(8,128)(2,1)S(1)}, bf16[64,768]{1,0:T(8,128)(2,1)S(1)}, u32[]{:S(2)}, u32[]{:S(2)}) collective-permute-start(bf16[64,768]{1,0:T(8,128)(2,1)S(1)} %get-tuple-element.73), channel_id=1, source_target_pairs={{0,6},{2,4},{4,2},{6,0},{8,14},{10,12},{12,10},{14,8},{1,7},{3,5},... | collective-permute-start | bytes 294920 | tf_op jit(solution)/shard_map/ppermute | solution.py:357
  12.8 0.5 collective-permute-start.4
  13.2 1.7 %collective-permute-done.refs_0_ = f32[8,128]{1,0:T(8,128)S(1)} collective-permute-done((f32[8,128]{1,0:T(8,128)S(1)}, f32[8,128]{1,0:T(8,128)S(1)}, u32[]{:S(2)}, u32[]{:S(2)}) %collective-permute-start) | collective-permute-done | bytes 4128 | tf_op jit(solution)/shard_map/ppermute | solution.py:362
  14.9 1.6 %collective-permute-start.5 = (bf16[64,768]{1,0:T(8,128)(2,1)S(1)}, bf16[64,768]{1,0:T(8,128)(2,1)S(1)}, u32[]{:S(2)}, u32[]{:S(2)}) collective-permute-start(bf16[64,768]{1,0:T(8,128)(2,1)S(1)} %get-tuple-element.75), channel_id=1, source_target_pairs={{0,2},{2,0},{4,6},{6,4},{8,10},{10,8},{12,14},{14,12},{1,3},{3,1},... | collective-permute-start | bytes 294920 | tf_op jit(solution)/shard_map/ppermute | solution.py:357
  16.5 0.4 pack_far.1
  16.9 1.0 %collective-permute-start.10 = (bf16[64,768]{1,0:T(8,128)(2,1)S(1)}, bf16[64,768]{1,0:T(8,128)(2,1)S(1)}, u32[]{:S(2)}, u32[]{:S(2)}) collective-permute-start(bf16[64,768]{1,0:T(8,128)(2,1)S(1)} %get-tuple-element.82), channel_id=1, source_target_pairs={{0,6},{2,4},{4,2},{6,0},{8,14},{10,12},{12,10},{14,8},{1,7},{3,5},... | collective-permute-start | bytes 294920 | tf_op jit(solution)/shard_map/ppermute | solution.py:357
  18.0 0.8 collective-permute-start.11
  19.1 1.6 %collective-permute-start.12 = (bf16[64,768]{1,0:T(8,128)(2,1)S(1)}, bf16[64,768]{1,0:T(8,128)(2,1)S(1)}, u32[]{:S(2)}, u32[]{:S(2)}) collective-permute-start(bf16[64,768]{1,0:T(8,128)(2,1)S(1)} %get-tuple-element.84), channel_id=1, source_target_pairs={{0,2},{2,0},{4,6},{6,4},{8,10},{10,8},{12,14},{14,12},{1,3},{3,1},... | collective-permute-start | bytes 294920 | tf_op jit(solution)/shard_map/ppermute | solution.py:357
  20.7 3.4 %forward_near.1 = (bf16[64,768]{1,0:T(8,128)(2,1)S(1)}, bf16[64,768]{1,0:T(8,128)(2,1)S(1)}, bf16[64,768]{1,0:T(8,128)(2,1)S(1)}, bf16[64,768]{1,0:T(8,128)(2,1)...) custom-call(bf16[3,1024,768]{2,1,0:T(8,128)(2,1)S(1)} %bitcast.13, ...), custom_call_target="tpu_custom_call" | custom-call | flops 100000000 | bytes 2097152 | tf_op jit(solution)/shard_map/forward_near/pallas_call | solution.py:339
  24.1 2.3 %collective-permute-start.7 = (bf16[64,768]{1,0:T(8,128)(2,1)S(1)}, bf16[64,768]{1,0:T(8,128)(2,1)S(1)}, u32[]{:S(2)}, u32[]{:S(2)}) collective-permute-start(bf16[64,768]{1,0:T(8,128)(2,1)S(1)} %get-tuple-element.78), channel_id=1, source_target_pairs={{0,6},{2,4},{4,2},{6,0},{8,14},{10,12},{12,10},{14,8},{1,7},{3,5},... | collective-permute-start | bytes 294920 | tf_op jit(solution)/shard_map/ppermute | solution.py:357
  26.5 1.2 %collective-permute-start.8 = (bf16[64,768]{1,0:T(8,128)(2,1)S(1)}, bf16[64,768]{1,0:T(8,128)(2,1)S(1)}, u32[]{:S(2)}, u32[]{:S(2)}) collective-permute-start(bf16[64,768]{1,0:T(8,128)(2,1)S(1)} %get-tuple-element.79), channel_id=1, source_target_pairs={{0,4},{2,6},{4,0},{6,2},{8,12},{10,14},{12,8},{14,10},{1,5},{3,7},... | collective-permute-start | bytes 294920 | tf_op jit(solution)/shard_map/ppermute | solution.py:357
  27.7 3.4 %forward_far.1 = (bf16[64,768]{1,0:T(8,128)(2,1)S(1)}, bf16[64,768]{1,0:T(8,128)(2,1)S(1)}, bf16[64,768]{1,0:T(8,128)(2,1)S(1)}, bf16[64,768]{1,0:T(8,128)(2,1)S...) custom-call(bf16[3,1024,768]{2,1,0:T(8,128)(2,1)S(1)} %bitcast.14, ...), custom_call_target="tpu_custom_call" | custom-call | flops 3000000000 | bytes 2097152 | tf_op jit(solution)/shard_map/forward_far/pallas_call | solution.py:339
  31.3 1.0 %collective-permute-done.9.refs_6_.refs_7_ = bf16[64,768]{1,0:T(8,128)(2,1)S(1)} collective-permute-done((bf16[64,768]{1,0:T(8,128)(2,1)S(1)}, bf16[64,768]{1,0:T(8,128)(2,1)S(1)}, u32[]{:S(2)}, u32[]{:S(2)}) %collective-permute-start.9) | collective-permute-done | bytes 98336 | tf_op jit(solution)/shard_map/ppermute | solution.py:357
  32.6 2.2 %collective-permute-start.13 = (bf16[128,768]{1,0:T(8,128)(2,1)S(1)}, bf16[128,768]{1,0:T(8,128)(2,1)S(1)}, u32[]{:S(2)}, u32[]{:S(2)}) collective-permute-start(bf16[128,768]{1,0:T(8,128)(2,1)S(1)} %get-tuple-element.94), channel_id=1, source_target_pairs={{0,8},{2,10},{4,12},{6,14},{8,0},{10,2},{12,4},{14,6},{1,9},{3,11}... | collective-permute-start | bytes 589832 | tf_op jit(solution)/shard_map/ppermute | solution.py:362
  34.8 2.6 %collective-permute-start.14 = (bf16[64,768]{1,0:T(8,128)(2,1)S(1)}, bf16[64,768]{1,0:T(8,128)(2,1)S(1)}, u32[]{:S(2)}, u32[]{:S(2)}) collective-permute-start(bf16[64,768]{1,0:T(8,128)(2,1)S(1)} %get-tuple-element.95), channel_id=1, source_target_pairs={{0,6},{2,4},{4,2},{6,0},{8,14},{10,12},{12,10},{14,8},{1,7},{3,5},... | collective-permute-start | bytes 294920 | tf_op jit(solution)/shard_map/ppermute | solution.py:357
  37.4 0.9 %collective-permute-start.16 = (bf16[64,768]{1,0:T(8,128)(2,1)S(1)}, bf16[64,768]{1,0:T(8,128)(2,1)S(1)}, u32[]{:S(2)}, u32[]{:S(2)}) collective-permute-start(bf16[64,768]{1,0:T(8,128)(2,1)S(1)} %get-tuple-element.97), channel_id=1, source_target_pairs={{0,2},{2,0},{4,6},{6,4},{8,10},{10,8},{12,14},{14,12},{1,3},{3,1},... | collective-permute-start | bytes 294920 | tf_op jit(solution)/shard_map/ppermute | solution.py:357
  38.3 5.9 %collective-permute-done.13.refs_1_ = bf16[128,768]{1,0:T(8,128)(2,1)S(1)} collective-permute-done((bf16[128,768]{1,0:T(8,128)(2,1)S(1)}, bf16[128,768]{1,0:T(8,128)(2,1)S(1)}, u32[]{:S(2)}, u32[]{:S(2)}) %collective-permute-start.13) | collective-permute-done | bytes 196640 | tf_op jit(solution)/shard_map/ppermute | solution.py:362
  44.2 1.5 %collective-permute-done.15.refs_5_ = bf16[64,768]{1,0:T(8,128)(2,1)S(1)} collective-permute-done((bf16[64,768]{1,0:T(8,128)(2,1)S(1)}, bf16[64,768]{1,0:T(8,128)(2,1)S(1)}, u32[]{:S(2)}, u32[]{:S(2)}) %collective-permute-start.15) | collective-permute-done | bytes 98336 | tf_op jit(solution)/shard_map/ppermute | solution.py:357
  45.7 0.6 far_grad.1
  46.3 1.1 %collective-permute-start.19 = (bf16[64,768]{1,0:T(8,128)(2,1)S(1)}, bf16[64,768]{1,0:T(8,128)(2,1)S(1)}, u32[]{:S(2)}, u32[]{:S(2)}) collective-permute-start(bf16[64,768]{1,0:T(8,128)(2,1)S(1)} %get-tuple-element.103), channel_id=1, source_target_pairs={{0,6},{2,4},{4,2},{6,0},{8,14},{10,12},{12,10},{14,8},{1,7},{3,5},... | collective-permute-start | bytes 294920 | tf_op jit(solution)/shard_map/ppermute | solution.py:357
  47.5 1.5 %collective-permute-start.20 = (bf16[64,768]{1,0:T(8,128)(2,1)S(1)}, bf16[64,768]{1,0:T(8,128)(2,1)S(1)}, u32[]{:S(2)}, u32[]{:S(2)}) collective-permute-start(bf16[64,768]{1,0:T(8,128)(2,1)S(1)} %get-tuple-element.104), channel_id=1, source_target_pairs={{0,4},{2,6},{4,0},{6,2},{8,12},{10,14},{12,8},{14,10},{1,5},{3,7},... | collective-permute-start | bytes 294920 | tf_op jit(solution)/shard_map/ppermute | solution.py:357
  48.9 1.0 %collective-permute-start.21 = (bf16[64,768]{1,0:T(8,128)(2,1)S(1)}, bf16[64,768]{1,0:T(8,128)(2,1)S(1)}, u32[]{:S(2)}, u32[]{:S(2)}) collective-permute-start(bf16[64,768]{1,0:T(8,128)(2,1)S(1)} %get-tuple-element.105), channel_id=1, source_target_pairs={{0,2},{2,0},{4,6},{6,4},{8,10},{10,8},{12,14},{14,12},{1,3},{3,1},... | collective-permute-start | bytes 294920 | tf_op jit(solution)/shard_map/ppermute | solution.py:357
  49.9 1.0 %collective-permute-start.18 = (bf16[144,768]{1,0:T(8,128)(2,1)S(1)}, bf16[144,768]{1,0:T(8,128)(2,1)S(1)}, u32[]{:S(2)}, u32[]{:S(2)}) collective-permute-start(bf16[144,768]{1,0:T(8,128)(2,1)S(1)} %get-tuple-element.99), channel_id=1, source_target_pairs={{0,8},{2,10},{4,12},{6,14},{8,0},{10,2},{12,4},{14,6},{1,9},{3,11}... | collective-permute-start | bytes 663560 | tf_op jit(solution)/shard_map/ppermute | solution.py:362
  50.9 1.8 %collective-permute-done.19.refs_5_ = bf16[64,768]{1,0:T(8,128)(2,1)S(1)} collective-permute-done((bf16[64,768]{1,0:T(8,128)(2,1)S(1)}, bf16[64,768]{1,0:T(8,128)(2,1)S(1)}, u32[]{:S(2)}, u32[]{:S(2)}) %collective-permute-start.19) | collective-permute-done | bytes 98336 | tf_op jit(solution)/shard_map/ppermute | solution.py:357
  52.7 2.4 %collective-permute-done.20.refs_6_ = bf16[64,768]{1,0:T(8,128)(2,1)S(1)} collective-permute-done((bf16[64,768]{1,0:T(8,128)(2,1)S(1)}, bf16[64,768]{1,0:T(8,128)(2,1)S(1)}, u32[]{:S(2)}, u32[]{:S(2)}) %collective-permute-start.20) | collective-permute-done | bytes 98336 | tf_op jit(solution)/shard_map/ppermute | solution.py:357
  55.1 3.7 %backward_far.1 = (bf16[64,768]{1,0:T(8,128)(2,1)S(1)}, bf16[64,768]{1,0:T(8,128)(2,1)S(1)}, bf16[64,768]{1,0:T(8,128)(2,1)S(1)}, bf16[64,768]{1,0:T(8,128)(2,1)...) custom-call(bf16[3,1024,768]{2,1,0:T(8,128)(2,1)S(1)} %bitcast.15, ...), custom_call_target="tpu_custom_call" | custom-call | flops 3000000000 | bytes 2097152 | tf_op jit(solution)/shard_map/backward_far/pallas_call | solution.py:339
  59.0 1.8 %collective-permute-start.23 = (bf16[64,768]{1,0:T(8,128)(2,1)S(1)}, bf16[64,768]{1,0:T(8,128)(2,1)S(1)}, u32[]{:S(2)}, u32[]{:S(2)}) collective-permute-start(bf16[64,768]{1,0:T(8,128)(2,1)S(1)} %get-tuple-element.110), channel_id=1, source_target_pairs={{0,4},{2,6},{4,0},{6,2},{8,12},{10,14},{12,8},{14,10},{1,5},{3,7},... | collective-permute-start | bytes 294920 | tf_op jit(solution)/shard_map/ppermute | solution.py:357
  60.9 1.6 %collective-permute-start.24 = (bf16[64,768]{1,0:T(8,128)(2,1)S(1)}, bf16[64,768]{1,0:T(8,128)(2,1)S(1)}, u32[]{:S(2)}, u32[]{:S(2)}) collective-permute-start(bf16[64,768]{1,0:T(8,128)(2,1)S(1)} %get-tuple-element.111), channel_id=1, source_target_pairs={{0,2},{2,0},{4,6},{6,4},{8,10},{10,8},{12,14},{14,12},{1,3},{3,1},... | collective-permute-start | bytes 294920 | tf_op jit(solution)/shard_map/ppermute | solution.py:357
  62.5 1.1 %near_grad.1 = (bf16[128,768]{1,0:T(8,128)(2,1)}, f32[2,128]{1,0:T(2,128)}, bf16[64,768]{1,0:T(8,128)(2,1)S(1)}, bf16[64,768]{1,0:T(8,128)(2,1)S(1)}, bf16[64,76...) custom-call(f32[8,128]{1,0:T(8,128)S(1)} %get-tuple-element.69.refs_0_, ...), custom_call_target="tpu_custom_call" | custom-call | flops 30000001024 | bytes 2097152 | tf_op jit(solution)/shard_map/near_grad/pallas_call | solution.py:339
  63.7 1.8 %collective-permute-done.22.refs_2_ = bf16[64,768]{1,0:T(8,128)(2,1)S(1)} collective-permute-done((bf16[64,768]{1,0:T(8,128)(2,1)S(1)}, bf16[64,768]{1,0:T(8,128)(2,1)S(1)}, u32[]{:S(2)}, u32[]{:S(2)}) %collective-permute-start.22) | collective-permute-done | bytes 98336 | tf_op jit(solution)/shard_map/ppermute | solution.py:357
  65.6 0.9 %collective-permute-done.23.refs_3_ = bf16[64,768]{1,0:T(8,128)(2,1)S(1)} collective-permute-done((bf16[64,768]{1,0:T(8,128)(2,1)S(1)}, bf16[64,768]{1,0:T(8,128)(2,1)S(1)}, u32[]{:S(2)}, u32[]{:S(2)}) %collective-permute-start.23) | collective-permute-done | bytes 98336 | tf_op jit(solution)/shard_map/ppermute | solution.py:357
  66.5 1.6 %collective-permute-start.28 = (bf16[64,768]{1,0:T(8,128)(2,1)S(1)}, bf16[64,768]{1,0:T(8,128)(2,1)S(1)}, u32[]{:S(2)}, u32[]{:S(2)}) collective-permute-start(bf16[64,768]{1,0:T(8,128)(2,1)S(1)} %get-tuple-element.117), channel_id=1, source_target_pairs={{0,2},{2,0},{4,6},{6,4},{8,10},{10,8},{12,14},{14,12},{1,3},{3,1},... | collective-permute-start | bytes 294920 | tf_op jit(solution)/shard_map/ppermute | solution.py:357
  68.1 0.4 far_back.1.refs_6_.refs_8_
  68.5 0.6 collective-permute-start.25
  69.1 2.6 %weight_far.1 = (bf16[3,1024,768]{2,1,0:T(8,128)(2,1)S(1)}, f32[8,128]{1,0:T(8,128)S(1)}) custom-call(bf16[7,256,256]{2,1,0:T(8,128)(2,1)S(1)} %get-tuple-element.98.refs_0_, bf16[7,256,256]{2,1,0:T(8,128)(2,1)S(1)} %collective-permute-done.17.refs_7_.refs_1_, bf16[11,256,256]{2,1,0:T(8,128)(2,1)S(1)} %get-tuple-element.118.refs_2_, ...), custom_call_target="tpu_custom_call" | custom-call | flops 2400000000 | bytes 2097152 | tf_op jit(solution)/shard_map/weight_far/pallas_call | solution.py:339
  71.8 3.7 %backward_near.1 = (bf16[64,768]{1,0:T(8,128)(2,1)S(1)}, bf16[64,768]{1,0:T(8,128)(2,1)S(1)}, bf16[64,768]{1,0:T(8,128)(2,1)S(1)}, bf16[64,768]{1,0:T(8,128)(2,1...) custom-call(bf16[3,1024,768]{2,1,0:T(8,128)(2,1)S(1)} %bitcast.16, ...), custom_call_target="tpu_custom_call" | custom-call | flops 10000000000 | bytes 2097152 | tf_op jit(solution)/shard_map/backward_near/pallas_call | solution.py:339
  75.6 2.3 %collective-permute-start.30 = (bf16[64,768]{1,0:T(8,128)(2,1)S(1)}, bf16[64,768]{1,0:T(8,128)(2,1)S(1)}, u32[]{:S(2)}, u32[]{:S(2)}) collective-permute-start(bf16[64,768]{1,0:T(8,128)(2,1)S(1)} %get-tuple-element.124), channel_id=1, source_target_pairs={{0,6},{2,4},{4,2},{6,0},{8,14},{10,12},{12,10},{14,8},{1,7},{3,5},... | collective-permute-start | bytes 294920 | tf_op jit(solution)/shard_map/ppermute | solution.py:357
  77.9 1.2 %collective-permute-start.31 = (bf16[64,768]{1,0:T(8,128)(2,1)S(1)}, bf16[64,768]{1,0:T(8,128)(2,1)S(1)}, u32[]{:S(2)}, u32[]{:S(2)}) collective-permute-start(bf16[64,768]{1,0:T(8,128)(2,1)S(1)} %get-tuple-element.125), channel_id=1, source_target_pairs={{0,4},{2,6},{4,0},{6,2},{8,12},{10,14},{12,8},{14,10},{1,5},{3,7},... | collective-permute-start | bytes 294920 | tf_op jit(solution)/shard_map/ppermute | solution.py:357
  79.1 0.5 collective-permute-start.32
  79.7 3.9 %weight_near.1 = (bf16[3,1024,768]{2,1,0:T(8,128)(2,1)}, f32[8,128]{1,0:T(8,128)S(1)}) custom-call(bf16[3,1024,768]{2,1,0:T(8,128)(2,1)S(1)} %get-tuple-element.127.refs_0_, bf16[7,256,256]{2,1,0:T(8,128)(2,1)S(1)} %get-tuple-element.76.refs_6_.refs_1_, bf16[7,256,256]{2,1,0:T(8,128)(2,1)S(1)} %collective-permute-done.6.refs_0_.refs_8_.refs_2_, ...), custom_call_target="tpu_custom_call" | custom-call | flops 30000001024 | bytes 2097152 | tf_op jit(solution)/shard_map/weight_near/pallas_call | solution.py:339
  83.6 0.7 collective-permute-done.31.refs_4_
  84.3 0.9 %combine_gradients.1 = bf16[128,768]{1,0:T(8,128)(2,1)} custom-call(bf16[2,256,128]{2,1,0:T(8,128)(2,1)S(1)} %get-tuple-element.70.refs_1_.refs_0_, bf16[128,768]{1,0:T(8,128)(2,1)S(1)} %get-tuple-element.122.refs_1_, bf16[64,768]{1,0:T(8,128)(2,1)S(1)} %get-tuple-element.123.refs_2_, bf16[64,768]{1,0:T(8,128)(2,1)S(1)} %collective-permute-done.30.refs_3_, ...), custom_call_target="tpu_custom_call" | custom-call | flops 30000001024 | bytes 2097152 | tf_op jit(solution)/shard_map/combine_gradients/pallas_call | solution.py:339
  (51 shorter events, 1.9 us)
Async XLA Ops:
  0.6 20.1 %collective-permute-start.2 = (bf16[3,1024,768]{2,1,0:T(8,128)(2,1)}, bf16[3,1024,768]{2,1,0:T(8,128)(2,1)S(1)}, u32[]{:S(2)}, u32[]{:S(2)}) collective-permute-start(bf16[3,1024,768]{2,1,0:T(8,128)(2,1)} %bitcast.9), channel_id=1, source_target_pairs={{0,1},{1,0},{2,3},{3,2},{4,5},{5,4},{6,7},{7,6},{8,9},{9,8},{10,11... | collective-permute-start | bytes 14155784 | tf_op jit(solution)/shard_map/ppermute | solution.py:365
  1.1 15.4 %collective-permute-start.1 = (bf16[128,768]{1,0:T(8,128)(2,1)}, bf16[128,768]{1,0:T(8,128)(2,1)S(1)}, u32[]{:S(2)}, u32[]{:S(2)}) collective-permute-start(bf16[128,768]{1,0:T(8,128)(2,1)} %refs_3_.1), channel_id=1, source_target_pairs={{0,8},{2,10},{4,12},{6,14},{8,0},{10,2},{12,4},{14,6},{1,9},{3,11}... | collective-permute-start | bytes 589832 | tf_op jit(solution)/shard_map/ppermute | solution.py:362
  4.8 2.3 %copy-start = (bf16[1,1024,3,768]{3,1,2,0:T(8,128)(2,1)S(1)}, bf16[1,1024,3,768]{3,1,2,0:T(8,128)(2,1)}, u32[]{:S(2)}) copy-start(bf16[1,1024,3,768]{3,1,2,0:T(8,128)(2,1)} %param.9) | copy-start | bytes 14155780
  7.2 0.9 %copy-start.1 = (bf16[128,768]{1,0:T(8,128)(2,1)S(1)}, bf16[128,768]{1,0:T(8,128)(2,1)}, u32[]{:S(2)}) copy-start(bf16[128,768]{1,0:T(8,128)(2,1)} %refs_3_.1) | copy-start | bytes 589828
  8.1 0.7 copy-start.3
  8.8 0.7 copy-start.4
  9.8 5.1 %collective-permute-start = (f32[8,128]{1,0:T(8,128)S(1)}, f32[8,128]{1,0:T(8,128)S(1)}, u32[]{:S(2)}, u32[]{:S(2)}) collective-permute-start(f32[8,128]{1,0:T(8,128)S(1)} %get-tuple-element.69.refs_0_), channel_id=1, source_target_pairs={{0,8},{2,10},{4,12},{6,14},{8,0},{10,2},{12,4},{14,6},{1,9},{3,11}... | collective-permute-start | bytes 12296 | tf_op jit(solution)/shard_map/ppermute | solution.py:362
  9.9 8.1 %collective-permute-start.3 = (bf16[64,768]{1,0:T(8,128)(2,1)S(1)}, bf16[64,768]{1,0:T(8,128)(2,1)S(1)}, u32[]{:S(2)}, u32[]{:S(2)}) collective-permute-start(bf16[64,768]{1,0:T(8,128)(2,1)S(1)} %get-tuple-element.73), channel_id=1, source_target_pairs={{0,6},{2,4},{4,2},{6,0},{8,14},{10,12},{12,10},{14,8},{1,7},{3,5},... | collective-permute-start | bytes 294920 | tf_op jit(solution)/shard_map/ppermute | solution.py:357
  12.8 6.4 %collective-permute-start.4 = (bf16[64,768]{1,0:T(8,128)(2,1)S(1)}, bf16[64,768]{1,0:T(8,128)(2,1)S(1)}, u32[]{:S(2)}, u32[]{:S(2)}) collective-permute-start(bf16[64,768]{1,0:T(8,128)(2,1)S(1)} %get-tuple-element.74), channel_id=1, source_target_pairs={{0,4},{2,6},{4,0},{6,2},{8,12},{10,14},{12,8},{14,10},{1,5},{3,7},... | collective-permute-start | bytes 294920 | tf_op jit(solution)/shard_map/ppermute | solution.py:357
  14.9 5.8 %slice-start = ((s8[4718592]{0:T(1024)(128)(4,1)}), s8[4194304]{0:T(1024)(128)(4,1)S(1)}, s32[]{:S(2)}) async-start(s8[4718592]{0:T(1024)(128)(4,1)} %bitcast.11), calls=%async_computation | async-start | bytes 8388608
  14.9 5.8 %slice-start.1 = ((s8[4718592]{0:T(1024)(128)(4,1)}), s8[524288]{0:T(1024)(128)(4,1)S(1)}, s32[]{:S(2)}) async-start(s8[4718592]{0:T(1024)(128)(4,1)} %bitcast.11), calls=%async_computation.1 | async-start | bytes 1048576
  14.9 5.8 %collective-permute-start.5 = (bf16[64,768]{1,0:T(8,128)(2,1)S(1)}, bf16[64,768]{1,0:T(8,128)(2,1)S(1)}, u32[]{:S(2)}, u32[]{:S(2)}) collective-permute-start(bf16[64,768]{1,0:T(8,128)(2,1)S(1)} %get-tuple-element.75), channel_id=1, source_target_pairs={{0,2},{2,0},{4,6},{6,4},{8,10},{10,8},{12,14},{14,12},{1,3},{3,1},... | collective-permute-start | bytes 294920 | tf_op jit(solution)/shard_map/ppermute | solution.py:357
  16.9 10.7 %collective-permute-start.10 = (bf16[64,768]{1,0:T(8,128)(2,1)S(1)}, bf16[64,768]{1,0:T(8,128)(2,1)S(1)}, u32[]{:S(2)}, u32[]{:S(2)}) collective-permute-start(bf16[64,768]{1,0:T(8,128)(2,1)S(1)} %get-tuple-element.82), channel_id=1, source_target_pairs={{0,6},{2,4},{4,2},{6,0},{8,14},{10,12},{12,10},{14,8},{1,7},{3,5},... | collective-permute-start | bytes 294920 | tf_op jit(solution)/shard_map/ppermute | solution.py:357
  18.0 9.7 %collective-permute-start.11 = (bf16[64,768]{1,0:T(8,128)(2,1)S(1)}, bf16[64,768]{1,0:T(8,128)(2,1)S(1)}, u32[]{:S(2)}, u32[]{:S(2)}) collective-permute-start(bf16[64,768]{1,0:T(8,128)(2,1)S(1)} %get-tuple-element.83), channel_id=1, source_target_pairs={{0,4},{2,6},{4,0},{6,2},{8,12},{10,14},{12,8},{14,10},{1,5},{3,7},... | collective-permute-start | bytes 294920 | tf_op jit(solution)/shard_map/ppermute | solution.py:357
  19.1 8.6 %collective-permute-start.12 = (bf16[64,768]{1,0:T(8,128)(2,1)S(1)}, bf16[64,768]{1,0:T(8,128)(2,1)S(1)}, u32[]{:S(2)}, u32[]{:S(2)}) collective-permute-start(bf16[64,768]{1,0:T(8,128)(2,1)S(1)} %get-tuple-element.84), channel_id=1, source_target_pairs={{0,2},{2,0},{4,6},{6,4},{8,10},{10,8},{12,14},{14,12},{1,3},{3,1},... | collective-permute-start | bytes 294920 | tf_op jit(solution)/shard_map/ppermute | solution.py:357
  24.1 7.0 %collective-permute-start.7 = (bf16[64,768]{1,0:T(8,128)(2,1)S(1)}, bf16[64,768]{1,0:T(8,128)(2,1)S(1)}, u32[]{:S(2)}, u32[]{:S(2)}) collective-permute-start(bf16[64,768]{1,0:T(8,128)(2,1)S(1)} %get-tuple-element.78), channel_id=1, source_target_pairs={{0,6},{2,4},{4,2},{6,0},{8,14},{10,12},{12,10},{14,8},{1,7},{3,5},... | collective-permute-start | bytes 294920 | tf_op jit(solution)/shard_map/ppermute | solution.py:357
  26.5 4.8 %collective-permute-start.8 = (bf16[64,768]{1,0:T(8,128)(2,1)S(1)}, bf16[64,768]{1,0:T(8,128)(2,1)S(1)}, u32[]{:S(2)}, u32[]{:S(2)}) collective-permute-start(bf16[64,768]{1,0:T(8,128)(2,1)S(1)} %get-tuple-element.79), channel_id=1, source_target_pairs={{0,4},{2,6},{4,0},{6,2},{8,12},{10,14},{12,8},{14,10},{1,5},{3,7},... | collective-permute-start | bytes 294920 | tf_op jit(solution)/shard_map/ppermute | solution.py:357
  27.6 4.6 %collective-permute-start.9 = (bf16[64,768]{1,0:T(8,128)(2,1)S(1)}, bf16[64,768]{1,0:T(8,128)(2,1)S(1)}, u32[]{:S(2)}, u32[]{:S(2)}) collective-permute-start(bf16[64,768]{1,0:T(8,128)(2,1)S(1)} %get-tuple-element.80), channel_id=1, source_target_pairs={{0,2},{2,0},{4,6},{6,4},{8,10},{10,8},{12,14},{14,12},{1,3},{3,1},... | collective-permute-start | bytes 294920 | tf_op jit(solution)/shard_map/ppermute | solution.py:357
  27.7 7.1 %collective-permute-start.6 = (bf16[7,256,256]{2,1,0:T(8,128)(2,1)S(1)}, bf16[7,256,256]{2,1,0:T(8,128)(2,1)S(1)}, u32[]{:S(2)}, u32[]{:S(2)}) collective-permute-start(bf16[7,256,256]{2,1,0:T(8,128)(2,1)S(1)} %get-tuple-element.76.refs_6_.refs_1_), channel_id=1, source_target_pairs={{0,1},{1,0},{2,3},{3,2},{4,5},{5,4},{6,7},{7,6},{8,9},{9,8},{10,11... | collective-permute-start | bytes 2752520 | tf_op jit(solution)/shard_map/ppermute | solution.py:365
  27.7 4.5 %copy-start.2 = (bf16[128,768]{1,0:T(8,128)(2,1)S(1)}, bf16[128,768]{1,0:T(8,128)(2,1)}, u32[]{:S(2)}) copy-start(bf16[128,768]{1,0:T(8,128)(2,1)} %refs_2_.3) | copy-start | bytes 589828
  32.6 11.6 %collective-permute-start.13 = (bf16[128,768]{1,0:T(8,128)(2,1)S(1)}, bf16[128,768]{1,0:T(8,128)(2,1)S(1)}, u32[]{:S(2)}, u32[]{:S(2)}) collective-permute-start(bf16[128,768]{1,0:T(8,128)(2,1)S(1)} %get-tuple-element.94), channel_id=1, source_target_pairs={{0,8},{2,10},{4,12},{6,14},{8,0},{10,2},{12,4},{14,6},{1,9},{3,11}... | collective-permute-start | bytes 589832 | tf_op jit(solution)/shard_map/ppermute | solution.py:362
  34.8 9.4 %collective-permute-start.17 = (bf16[7,256,256]{2,1,0:T(8,128)(2,1)S(1)}, bf16[7,256,256]{2,1,0:T(8,128)(2,1)S(1)}, u32[]{:S(2)}, u32[]{:S(2)}) collective-permute-start(bf16[7,256,256]{2,1,0:T(8,128)(2,1)S(1)} %get-tuple-element.98.refs_0_), channel_id=1, source_target_pairs={{0,1},{1,0},{2,3},{3,2},{4,5},{5,4},{6,7},{7,6},{8,9},{9,8},{10,11... | collective-permute-start | bytes 2752520 | tf_op jit(solution)/shard_map/ppermute | solution.py:365
  34.8 9.4 %collective-permute-start.14 = (bf16[64,768]{1,0:T(8,128)(2,1)S(1)}, bf16[64,768]{1,0:T(8,128)(2,1)S(1)}, u32[]{:S(2)}, u32[]{:S(2)}) collective-permute-start(bf16[64,768]{1,0:T(8,128)(2,1)S(1)} %get-tuple-element.95), channel_id=1, source_target_pairs={{0,6},{2,4},{4,2},{6,0},{8,14},{10,12},{12,10},{14,8},{1,7},{3,5},... | collective-permute-start | bytes 294920 | tf_op jit(solution)/shard_map/ppermute | solution.py:357
  37.4 8.3 %collective-permute-start.15 = (bf16[64,768]{1,0:T(8,128)(2,1)S(1)}, bf16[64,768]{1,0:T(8,128)(2,1)S(1)}, u32[]{:S(2)}, u32[]{:S(2)}) collective-permute-start(bf16[64,768]{1,0:T(8,128)(2,1)S(1)} %get-tuple-element.96), channel_id=1, source_target_pairs={{0,4},{2,6},{4,0},{6,2},{8,12},{10,14},{12,8},{14,10},{1,5},{3,7},... | collective-permute-start | bytes 294920 | tf_op jit(solution)/shard_map/ppermute | solution.py:357
  37.4 8.3 %collective-permute-start.16 = (bf16[64,768]{1,0:T(8,128)(2,1)S(1)}, bf16[64,768]{1,0:T(8,128)(2,1)S(1)}, u32[]{:S(2)}, u32[]{:S(2)}) collective-permute-start(bf16[64,768]{1,0:T(8,128)(2,1)S(1)} %get-tuple-element.97), channel_id=1, source_target_pairs={{0,2},{2,0},{4,6},{6,4},{8,10},{10,8},{12,14},{14,12},{1,3},{3,1},... | collective-permute-start | bytes 294920 | tf_op jit(solution)/shard_map/ppermute | solution.py:357
  46.3 6.4 %collective-permute-start.19 = (bf16[64,768]{1,0:T(8,128)(2,1)S(1)}, bf16[64,768]{1,0:T(8,128)(2,1)S(1)}, u32[]{:S(2)}, u32[]{:S(2)}) collective-permute-start(bf16[64,768]{1,0:T(8,128)(2,1)S(1)} %get-tuple-element.103), channel_id=1, source_target_pairs={{0,6},{2,4},{4,2},{6,0},{8,14},{10,12},{12,10},{14,8},{1,7},{3,5},... | collective-permute-start | bytes 294920 | tf_op jit(solution)/shard_map/ppermute | solution.py:357
  47.5 7.7 %collective-permute-start.20 = (bf16[64,768]{1,0:T(8,128)(2,1)S(1)}, bf16[64,768]{1,0:T(8,128)(2,1)S(1)}, u32[]{:S(2)}, u32[]{:S(2)}) collective-permute-start(bf16[64,768]{1,0:T(8,128)(2,1)S(1)} %get-tuple-element.104), channel_id=1, source_target_pairs={{0,4},{2,6},{4,0},{6,2},{8,12},{10,14},{12,8},{14,10},{1,5},{3,7},... | collective-permute-start | bytes 294920 | tf_op jit(solution)/shard_map/ppermute | solution.py:357
  48.9 6.2 %collective-permute-start.21 = (bf16[64,768]{1,0:T(8,128)(2,1)S(1)}, bf16[64,768]{1,0:T(8,128)(2,1)S(1)}, u32[]{:S(2)}, u32[]{:S(2)}) collective-permute-start(bf16[64,768]{1,0:T(8,128)(2,1)S(1)} %get-tuple-element.105), channel_id=1, source_target_pairs={{0,2},{2,0},{4,6},{6,4},{8,10},{10,8},{12,14},{14,12},{1,3},{3,1},... | collective-permute-start | bytes 294920 | tf_op jit(solution)/shard_map/ppermute | solution.py:357
  49.9 12.6 %collective-permute-start.18 = (bf16[144,768]{1,0:T(8,128)(2,1)S(1)}, bf16[144,768]{1,0:T(8,128)(2,1)S(1)}, u32[]{:S(2)}, u32[]{:S(2)}) collective-permute-start(bf16[144,768]{1,0:T(8,128)(2,1)S(1)} %get-tuple-element.99), channel_id=1, source_target_pairs={{0,8},{2,10},{4,12},{6,14},{8,0},{10,2},{12,4},{14,6},{1,9},{3,11}... | collective-permute-start | bytes 663560 | tf_op jit(solution)/shard_map/ppermute | solution.py:362
  58.9 10.3 %collective-permute-start.29 = (bf16[11,256,256]{2,1,0:T(8,128)(2,1)S(1)}, bf16[11,256,256]{2,1,0:T(8,128)(2,1)S(1)}, u32[]{:S(2)}, u32[]{:S(2)}) collective-permute-start(bf16[11,256,256]{2,1,0:T(8,128)(2,1)S(1)} %get-tuple-element.118.refs_2_), channel_id=1, source_target_pairs={{0,1},{1,0},{2,3},{3,2},{4,5},{5,4},{6,7},{7,6},{8,9},{9,8},{10,11... | collective-permute-start | bytes 4325384 | tf_op jit(solution)/shard_map/ppermute | solution.py:365
  59.0 6.6 %collective-permute-start.22 = (bf16[64,768]{1,0:T(8,128)(2,1)S(1)}, bf16[64,768]{1,0:T(8,128)(2,1)S(1)}, u32[]{:S(2)}, u32[]{:S(2)}) collective-permute-start(bf16[64,768]{1,0:T(8,128)(2,1)S(1)} %get-tuple-element.109), channel_id=1, source_target_pairs={{0,6},{2,4},{4,2},{6,0},{8,14},{10,12},{12,10},{14,8},{1,7},{3,5},... | collective-permute-start | bytes 294920 | tf_op jit(solution)/shard_map/ppermute | solution.py:357
  59.0 7.4 %collective-permute-start.23 = (bf16[64,768]{1,0:T(8,128)(2,1)S(1)}, bf16[64,768]{1,0:T(8,128)(2,1)S(1)}, u32[]{:S(2)}, u32[]{:S(2)}) collective-permute-start(bf16[64,768]{1,0:T(8,128)(2,1)S(1)} %get-tuple-element.110), channel_id=1, source_target_pairs={{0,4},{2,6},{4,0},{6,2},{8,12},{10,14},{12,8},{14,10},{1,5},{3,7},... | collective-permute-start | bytes 294920 | tf_op jit(solution)/shard_map/ppermute | solution.py:357
  60.9 7.2 %collective-permute-start.24 = (bf16[64,768]{1,0:T(8,128)(2,1)S(1)}, bf16[64,768]{1,0:T(8,128)(2,1)S(1)}, u32[]{:S(2)}, u32[]{:S(2)}) collective-permute-start(bf16[64,768]{1,0:T(8,128)(2,1)S(1)} %get-tuple-element.111), channel_id=1, source_target_pairs={{0,2},{2,0},{4,6},{6,4},{8,10},{10,8},{12,14},{14,12},{1,3},{3,1},... | collective-permute-start | bytes 294920 | tf_op jit(solution)/shard_map/ppermute | solution.py:357
  63.7 8.1 %collective-permute-start.26 = (bf16[64,768]{1,0:T(8,128)(2,1)S(1)}, bf16[64,768]{1,0:T(8,128)(2,1)S(1)}, u32[]{:S(2)}, u32[]{:S(2)}) collective-permute-start(bf16[64,768]{1,0:T(8,128)(2,1)S(1)} %get-tuple-element.115), channel_id=1, source_target_pairs={{0,6},{2,4},{4,2},{6,0},{8,14},{10,12},{12,10},{14,8},{1,7},{3,5},... | collective-permute-start | bytes 294920 | tf_op jit(solution)/shard_map/ppermute | solution.py:357
  65.5 6.2 %collective-permute-start.27 = (bf16[64,768]{1,0:T(8,128)(2,1)S(1)}, bf16[64,768]{1,0:T(8,128)(2,1)S(1)}, u32[]{:S(2)}, u32[]{:S(2)}) collective-permute-start(bf16[64,768]{1,0:T(8,128)(2,1)S(1)} %get-tuple-element.116), channel_id=1, source_target_pairs={{0,4},{2,6},{4,0},{6,2},{8,12},{10,14},{12,8},{14,10},{1,5},{3,7},... | collective-permute-start | bytes 294920 | tf_op jit(solution)/shard_map/ppermute | solution.py:357
  66.5 5.3 %collective-permute-start.28 = (bf16[64,768]{1,0:T(8,128)(2,1)S(1)}, bf16[64,768]{1,0:T(8,128)(2,1)S(1)}, u32[]{:S(2)}, u32[]{:S(2)}) collective-permute-start(bf16[64,768]{1,0:T(8,128)(2,1)S(1)} %get-tuple-element.117), channel_id=1, source_target_pairs={{0,2},{2,0},{4,6},{6,4},{8,10},{10,8},{12,14},{14,12},{1,3},{3,1},... | collective-permute-start | bytes 294920 | tf_op jit(solution)/shard_map/ppermute | solution.py:357
  68.5 11.2 %collective-permute-start.25 = (bf16[128,768]{1,0:T(8,128)(2,1)S(1)}, bf16[128,768]{1,0:T(8,128)(2,1)S(1)}, u32[]{:S(2)}, u32[]{:S(2)}) collective-permute-start(bf16[128,768]{1,0:T(8,128)(2,1)S(1)} %far_back.1.refs_6_.refs_8_), channel_id=1, source_target_pairs={{0,8},{2,10},{4,12},{6,14},{8,0},{10,2},{12,4},{14,6},{1,9},{3,11}... | collective-permute-start | bytes 589832 | tf_op jit(solution)/shard_map/ppermute | solution.py:362
  75.5 4.2 %collective-permute-start.33 = (bf16[11,256,256]{2,1,0:T(8,128)(2,1)S(1)}, bf16[11,256,256]{2,1,0:T(8,128)(2,1)S(1)}, u32[]{:S(2)}, u32[]{:S(2)}) collective-permute-start(bf16[11,256,256]{2,1,0:T(8,128)(2,1)S(1)} %get-tuple-element.128.refs_3_), channel_id=1, source_target_pairs={{0,1},{1,0},{2,3},{3,2},{4,5},{5,4},{6,7},{7,6},{8,9},{9,8},{10,11... | collective-permute-start | bytes 4325384 | tf_op jit(solution)/shard_map/ppermute | solution.py:365
  75.6 8.0 %collective-permute-start.30 = (bf16[64,768]{1,0:T(8,128)(2,1)S(1)}, bf16[64,768]{1,0:T(8,128)(2,1)S(1)}, u32[]{:S(2)}, u32[]{:S(2)}) collective-permute-start(bf16[64,768]{1,0:T(8,128)(2,1)S(1)} %get-tuple-element.124), channel_id=1, source_target_pairs={{0,6},{2,4},{4,2},{6,0},{8,14},{10,12},{12,10},{14,8},{1,7},{3,5},... | collective-permute-start | bytes 294920 | tf_op jit(solution)/shard_map/ppermute | solution.py:357
  77.9 6.4 %collective-permute-start.31 = (bf16[64,768]{1,0:T(8,128)(2,1)S(1)}, bf16[64,768]{1,0:T(8,128)(2,1)S(1)}, u32[]{:S(2)}, u32[]{:S(2)}) collective-permute-start(bf16[64,768]{1,0:T(8,128)(2,1)S(1)} %get-tuple-element.125), channel_id=1, source_target_pairs={{0,4},{2,6},{4,0},{6,2},{8,12},{10,14},{12,8},{14,10},{1,5},{3,7},... | collective-permute-start | bytes 294920 | tf_op jit(solution)/shard_map/ppermute | solution.py:357
  79.1 5.2 %collective-permute-start.32 = (bf16[64,768]{1,0:T(8,128)(2,1)S(1)}, bf16[64,768]{1,0:T(8,128)(2,1)S(1)}, u32[]{:S(2)}, u32[]{:S(2)}) collective-permute-start(bf16[64,768]{1,0:T(8,128)(2,1)S(1)} %get-tuple-element.126), channel_id=1, source_target_pairs={{0,2},{2,0},{4,6},{6,4},{8,10},{10,8},{12,14},{14,12},{1,3},{3,1},... | collective-permute-start | bytes 294920 | tf_op jit(solution)/shard_map/ppermute | solution.py:357

commit v15 on v14

--- a/solution.py
+++ b/solution.py
@@ -123,9 +123,8 @@
 
 
 def pack_near_kernel(
-    own_ref, routes_ref, gates_ref, tokens_ref, meta_ref, masks_ref, *rows_refs
+    routes_ref, gates_ref, tokens_ref, meta_ref, masks_ref, *rows_refs
 ):
-    del own_ref
     meta = jnp.concatenate(
         [
             routes_ref[...].astype(F32),
@@ -404,7 +403,6 @@
         "pack_near",
         [jax.ShapeDtypeStruct((8, tok), F32), masks] + pieces,
         [],
-        own,
         routes.T,
         gate_weights.T,
         tokens,

time: 85.5 us -> 85.2 us (level)
  local copies, waits for them, and re-layouts: 4.63 us -> 2.33 us
  waiting for transfers between devices: 18.3 us -> 20.4 us
    ppermute x5, waiting for transfers between devices: 7.68 us -> 10.3 us  [to_mirror(): return lax.ppermute(x, 'expert', [(i, i ^ half) for i in range(experts)])]
    unnamed x14 -> x12, local copies, waits for them, and re-layouts: 4.63 us -> 2.33 us
    ppermute x5, starting transfers between devices: 7.63 us -> 6.73 us  [to_mirror(): return lax.ppermute(x, 'expert', [(i, i ^ half) for i in range(experts)])]
    ppermute x24, starting transfers between devices: 28.2 us -> 29.1 us  [within_half(): lax.ppermute(rows_of[s], 'expert', [(i, i ^ s) for i in range(experts)])]
  transfers between devices with their start and end apart: 34 -> 34, of which waited for: 13 -> 11; matrix products, arithmetic and copies ran while one was open for 0% -> 0% of each run, Pallas kernels for 27% -> 27%
where the time goes in v15:
time: 85.2 us; the launch traced here: 85.1 us
  starting transfers between devices  36.6 us (43%)
  Pallas kernels  24.9 us (29%)
  waiting for transfers between devices  20.4 us (24%)
  local copies, waits for them, and re-layouts  2.33 us (3%)
  between operations  0.86 us (1%)
    ppermute x24, starting transfers between devices, within_half(): lax.ppermute(rows_of[s], 'expert', [(i, i ^ s) for i in range(experts)])  29.1 us
    pallas_call x16, Pallas kernels, call(): pl.pallas_call(body, in_specs=specs + [aspec] * (len(after) + len(through...  24.9 us
    ppermute x5, waiting for transfers between devices, to_mirror(): return lax.ppermute(x, 'expert', [(i, i ^ half) for i in range(experts)])  10.3 us
    ppermute x24, waiting for transfers between devices, within_half(): lax.ppermute(rows_of[s], 'expert', [(i, i ^ s) for i in range(experts)])  10.1 us
    ppermute x5, starting transfers between devices, to_mirror(): return lax.ppermute(x, 'expert', [(i, i ^ half) for i in range(experts)])  6.73 us
    unnamed x12, local copies, waits for them, and re-layouts  2.33 us
  transfers between devices with their start and end apart: 34, of which 11 were waited for; matrix products, arithmetic and copies ran while one was open for 0% of the time, Pallas kernels for 27%

profile of v15, /device:TPU:0, one launch (start us, length us, event | category | flops | bytes accessed | tf_op | source)
XLA Modules:
  0.0 85.1 jit_solution(17964187426549156423)
XLA Ops:
  0.6 0.5 collective-permute-start.2
  1.1 3.7 %collective-permute-start.1 = (bf16[128,768]{1,0:T(8,128)(2,1)}, bf16[128,768]{1,0:T(8,128)(2,1)S(1)}, u32[]{:S(2)}, u32[]{:S(2)}) collective-permute-start(bf16[128,768]{1,0:T(8,128)(2,1)} %refs_2_.3), channel_id=1, source_target_pairs={{0,8},{2,10},{4,12},{6,14},{8,0},{10,2},{12,4},{14,6},{1,9},{3,11}... | collective-permute-start | bytes 589832 | tf_op jit(solution)/shard_map/ppermute | solution.py:361
  4.8 1.0 %copy-done = bf16[128,768]{1,0:T(8,128)(2,1)S(1)} copy-done((bf16[128,768]{1,0:T(8,128)(2,1)S(1)}, bf16[128,768]{1,0:T(8,128)(2,1)}, u32[]{:S(2)}) %copy-start) | copy-done | bytes 196632
  5.8 0.7 copy-done.2
  6.5 0.7 copy-done.3
  7.1 0.4 pack_near.1
  7.6 2.9 %collective-permute-start.3 = (bf16[64,768]{1,0:T(8,128)(2,1)S(1)}, bf16[64,768]{1,0:T(8,128)(2,1)S(1)}, u32[]{:S(2)}, u32[]{:S(2)}) collective-permute-start(bf16[64,768]{1,0:T(8,128)(2,1)S(1)} %get-tuple-element.73), channel_id=1, source_target_pairs={{0,6},{2,4},{4,2},{6,0},{8,14},{10,12},{12,10},{14,8},{1,7},{3,5},... | collective-permute-start | bytes 294920 | tf_op jit(solution)/shard_map/ppermute | solution.py:356
  10.4 0.4 collective-permute-start.4
  10.9 4.0 %collective-permute-done.refs_0_ = f32[8,128]{1,0:T(8,128)S(1)} collective-permute-done((f32[8,128]{1,0:T(8,128)S(1)}, f32[8,128]{1,0:T(8,128)S(1)}, u32[]{:S(2)}, u32[]{:S(2)}) %collective-permute-start) | collective-permute-done | bytes 4128 | tf_op jit(solution)/shard_map/ppermute | solution.py:361
  14.9 1.6 %collective-permute-start.5 = (bf16[64,768]{1,0:T(8,128)(2,1)S(1)}, bf16[64,768]{1,0:T(8,128)(2,1)S(1)}, u32[]{:S(2)}, u32[]{:S(2)}) collective-permute-start(bf16[64,768]{1,0:T(8,128)(2,1)S(1)} %get-tuple-element.75), channel_id=1, source_target_pairs={{0,2},{2,0},{4,6},{6,4},{8,10},{10,8},{12,14},{14,12},{1,3},{3,1},... | collective-permute-start | bytes 294920 | tf_op jit(solution)/shard_map/ppermute | solution.py:356
  16.5 0.4 pack_far.1
  16.9 0.8 collective-permute-start.10
  17.7 1.2 %collective-permute-start.11 = (bf16[64,768]{1,0:T(8,128)(2,1)S(1)}, bf16[64,768]{1,0:T(8,128)(2,1)S(1)}, u32[]{:S(2)}, u32[]{:S(2)}) collective-permute-start(bf16[64,768]{1,0:T(8,128)(2,1)S(1)} %get-tuple-element.83), channel_id=1, source_target_pairs={{0,4},{2,6},{4,0},{6,2},{8,12},{10,14},{12,8},{14,10},{1,5},{3,7},... | collective-permute-start | bytes 294920 | tf_op jit(solution)/shard_map/ppermute | solution.py:356
  18.9 1.6 %collective-permute-start.12 = (bf16[64,768]{1,0:T(8,128)(2,1)S(1)}, bf16[64,768]{1,0:T(8,128)(2,1)S(1)}, u32[]{:S(2)}, u32[]{:S(2)}) collective-permute-start(bf16[64,768]{1,0:T(8,128)(2,1)S(1)} %get-tuple-element.84), channel_id=1, source_target_pairs={{0,2},{2,0},{4,6},{6,4},{8,10},{10,8},{12,14},{14,12},{1,3},{3,1},... | collective-permute-start | bytes 294920 | tf_op jit(solution)/shard_map/ppermute | solution.py:356
  20.5 3.4 %forward_near.1 = (bf16[64,768]{1,0:T(8,128)(2,1)S(1)}, bf16[64,768]{1,0:T(8,128)(2,1)S(1)}, bf16[64,768]{1,0:T(8,128)(2,1)S(1)}, bf16[64,768]{1,0:T(8,128)(2,1)...) custom-call(bf16[3,1024,768]{2,1,0:T(8,128)(2,1)S(1)} %bitcast.12, ...), custom_call_target="tpu_custom_call" | custom-call | flops 100000000 | bytes 2097152 | tf_op jit(solution)/shard_map/forward_near/pallas_call | solution.py:338
  23.9 2.7 %collective-permute-start.7 = (bf16[64,768]{1,0:T(8,128)(2,1)S(1)}, bf16[64,768]{1,0:T(8,128)(2,1)S(1)}, u32[]{:S(2)}, u32[]{:S(2)}) collective-permute-start(bf16[64,768]{1,0:T(8,128)(2,1)S(1)} %get-tuple-element.78), channel_id=1, source_target_pairs={{0,6},{2,4},{4,2},{6,0},{8,14},{10,12},{12,10},{14,8},{1,7},{3,5},... | collective-permute-start | bytes 294920 | tf_op jit(solution)/shard_map/ppermute | solution.py:356
  26.6 1.3 %collective-permute-start.8 = (bf16[64,768]{1,0:T(8,128)(2,1)S(1)}, bf16[64,768]{1,0:T(8,128)(2,1)S(1)}, u32[]{:S(2)}, u32[]{:S(2)}) collective-permute-start(bf16[64,768]{1,0:T(8,128)(2,1)S(1)} %get-tuple-element.79), channel_id=1, source_target_pairs={{0,4},{2,6},{4,0},{6,2},{8,12},{10,14},{12,8},{14,10},{1,5},{3,7},... | collective-permute-start | bytes 294920 | tf_op jit(solution)/shard_map/ppermute | solution.py:356
  28.0 3.4 %forward_far.1 = (bf16[64,768]{1,0:T(8,128)(2,1)S(1)}, bf16[64,768]{1,0:T(8,128)(2,1)S(1)}, bf16[64,768]{1,0:T(8,128)(2,1)S(1)}, bf16[64,768]{1,0:T(8,128)(2,1)S...) custom-call(bf16[3,1024,768]{2,1,0:T(8,128)(2,1)S(1)} %bitcast.13, ...), custom_call_target="tpu_custom_call" | custom-call | flops 3000000000 | bytes 2097152 | tf_op jit(solution)/shard_map/forward_far/pallas_call | solution.py:338
  31.6 1.0 %collective-permute-done.9.refs_6_.refs_7_ = bf16[64,768]{1,0:T(8,128)(2,1)S(1)} collective-permute-done((bf16[64,768]{1,0:T(8,128)(2,1)S(1)}, bf16[64,768]{1,0:T(8,128)(2,1)S(1)}, u32[]{:S(2)}, u32[]{:S(2)}) %collective-permute-start.9) | collective-permute-done | bytes 98336 | tf_op jit(solution)/shard_map/ppermute | solution.py:356
  32.5 0.3 near_sum.1
  32.9 1.8 %collective-permute-start.13 = (bf16[128,768]{1,0:T(8,128)(2,1)S(1)}, bf16[128,768]{1,0:T(8,128)(2,1)S(1)}, u32[]{:S(2)}, u32[]{:S(2)}) collective-permute-start(bf16[128,768]{1,0:T(8,128)(2,1)S(1)} %get-tuple-element.94), channel_id=1, source_target_pairs={{0,8},{2,10},{4,12},{6,14},{8,0},{10,2},{12,4},{14,6},{1,9},{3,11}... | collective-permute-start | bytes 589832 | tf_op jit(solution)/shard_map/ppermute | solution.py:361
  34.7 2.6 %collective-permute-start.14 = (bf16[64,768]{1,0:T(8,128)(2,1)S(1)}, bf16[64,768]{1,0:T(8,128)(2,1)S(1)}, u32[]{:S(2)}, u32[]{:S(2)}) collective-permute-start(bf16[64,768]{1,0:T(8,128)(2,1)S(1)} %get-tuple-element.95), channel_id=1, source_target_pairs={{0,6},{2,4},{4,2},{6,0},{8,14},{10,12},{12,10},{14,8},{1,7},{3,5},... | collective-permute-start | bytes 294920 | tf_op jit(solution)/shard_map/ppermute | solution.py:356
  37.3 0.9 %collective-permute-start.16 = (bf16[64,768]{1,0:T(8,128)(2,1)S(1)}, bf16[64,768]{1,0:T(8,128)(2,1)S(1)}, u32[]{:S(2)}, u32[]{:S(2)}) collective-permute-start(bf16[64,768]{1,0:T(8,128)(2,1)S(1)} %get-tuple-element.97), channel_id=1, source_target_pairs={{0,2},{2,0},{4,6},{6,4},{8,10},{10,8},{12,14},{14,12},{1,3},{3,1},... | collective-permute-start | bytes 294920 | tf_op jit(solution)/shard_map/ppermute | solution.py:356
  38.2 6.2 %collective-permute-done.13.refs_1_ = bf16[128,768]{1,0:T(8,128)(2,1)S(1)} collective-permute-done((bf16[128,768]{1,0:T(8,128)(2,1)S(1)}, bf16[128,768]{1,0:T(8,128)(2,1)S(1)}, u32[]{:S(2)}, u32[]{:S(2)}) %collective-permute-start.13) | collective-permute-done | bytes 196640 | tf_op jit(solution)/shard_map/ppermute | solution.py:361
  44.4 1.5 %collective-permute-done.15.refs_5_ = bf16[64,768]{1,0:T(8,128)(2,1)S(1)} collective-permute-done((bf16[64,768]{1,0:T(8,128)(2,1)S(1)}, bf16[64,768]{1,0:T(8,128)(2,1)S(1)}, u32[]{:S(2)}, u32[]{:S(2)}) %collective-permute-start.15) | collective-permute-done | bytes 98336 | tf_op jit(solution)/shard_map/ppermute | solution.py:356
  45.9 0.6 far_grad.1
  46.5 0.8 collective-permute-start.19
  47.3 1.9 %collective-permute-start.20 = (bf16[64,768]{1,0:T(8,128)(2,1)S(1)}, bf16[64,768]{1,0:T(8,128)(2,1)S(1)}, u32[]{:S(2)}, u32[]{:S(2)}) collective-permute-start(bf16[64,768]{1,0:T(8,128)(2,1)S(1)} %get-tuple-element.104), channel_id=1, source_target_pairs={{0,4},{2,6},{4,0},{6,2},{8,12},{10,14},{12,8},{14,10},{1,5},{3,7},... | collective-permute-start | bytes 294920 | tf_op jit(solution)/shard_map/ppermute | solution.py:356
  49.2 0.9 %collective-permute-start.21 = (bf16[64,768]{1,0:T(8,128)(2,1)S(1)}, bf16[64,768]{1,0:T(8,128)(2,1)S(1)}, u32[]{:S(2)}, u32[]{:S(2)}) collective-permute-start(bf16[64,768]{1,0:T(8,128)(2,1)S(1)} %get-tuple-element.105), channel_id=1, source_target_pairs={{0,2},{2,0},{4,6},{6,4},{8,10},{10,8},{12,14},{14,12},{1,3},{3,1},... | collective-permute-start | bytes 294920 | tf_op jit(solution)/shard_map/ppermute | solution.py:356
  50.1 0.7 collective-permute-start.18
  50.8 2.1 %collective-permute-done.19.refs_5_ = bf16[64,768]{1,0:T(8,128)(2,1)S(1)} collective-permute-done((bf16[64,768]{1,0:T(8,128)(2,1)S(1)}, bf16[64,768]{1,0:T(8,128)(2,1)S(1)}, u32[]{:S(2)}, u32[]{:S(2)}) %collective-permute-start.19) | collective-permute-done | bytes 98336 | tf_op jit(solution)/shard_map/ppermute | solution.py:356
  52.9 2.2 %collective-permute-done.20.refs_6_ = bf16[64,768]{1,0:T(8,128)(2,1)S(1)} collective-permute-done((bf16[64,768]{1,0:T(8,128)(2,1)S(1)}, bf16[64,768]{1,0:T(8,128)(2,1)S(1)}, u32[]{:S(2)}, u32[]{:S(2)}) %collective-permute-start.20) | collective-permute-done | bytes 98336 | tf_op jit(solution)/shard_map/ppermute | solution.py:356
  55.2 3.7 %backward_far.1 = (bf16[64,768]{1,0:T(8,128)(2,1)S(1)}, bf16[64,768]{1,0:T(8,128)(2,1)S(1)}, bf16[64,768]{1,0:T(8,128)(2,1)S(1)}, bf16[64,768]{1,0:T(8,128)(2,1)...) custom-call(bf16[3,1024,768]{2,1,0:T(8,128)(2,1)S(1)} %bitcast.14, ...), custom_call_target="tpu_custom_call" | custom-call | flops 3000000000 | bytes 2097152 | tf_op jit(solution)/shard_map/backward_far/pallas_call | solution.py:338
  59.1 1.5 %collective-permute-start.23 = (bf16[64,768]{1,0:T(8,128)(2,1)S(1)}, bf16[64,768]{1,0:T(8,128)(2,1)S(1)}, u32[]{:S(2)}, u32[]{:S(2)}) collective-permute-start(bf16[64,768]{1,0:T(8,128)(2,1)S(1)} %get-tuple-element.110), channel_id=1, source_target_pairs={{0,4},{2,6},{4,0},{6,2},{8,12},{10,14},{12,8},{14,10},{1,5},{3,7},... | collective-permute-start | bytes 294920 | tf_op jit(solution)/shard_map/ppermute | solution.py:356
  60.6 1.9 %collective-permute-start.24 = (bf16[64,768]{1,0:T(8,128)(2,1)S(1)}, bf16[64,768]{1,0:T(8,128)(2,1)S(1)}, u32[]{:S(2)}, u32[]{:S(2)}) collective-permute-start(bf16[64,768]{1,0:T(8,128)(2,1)S(1)} %get-tuple-element.111), channel_id=1, source_target_pairs={{0,2},{2,0},{4,6},{6,4},{8,10},{10,8},{12,14},{14,12},{1,3},{3,1},... | collective-permute-start | bytes 294920 | tf_op jit(solution)/shard_map/ppermute | solution.py:356
  62.6 1.1 %near_grad.1 = (bf16[128,768]{1,0:T(8,128)(2,1)}, f32[2,128]{1,0:T(2,128)}, bf16[64,768]{1,0:T(8,128)(2,1)S(1)}, bf16[64,768]{1,0:T(8,128)(2,1)S(1)}, bf16[64,76...) custom-call(f32[8,128]{1,0:T(8,128)S(1)} %get-tuple-element.69.refs_0_, ...), custom_call_target="tpu_custom_call" | custom-call | flops 30000001024 | bytes 2097152 | tf_op jit(solution)/shard_map/near_grad/pallas_call | solution.py:338
  63.8 1.8 %collective-permute-done.22.refs_2_ = bf16[64,768]{1,0:T(8,128)(2,1)S(1)} collective-permute-done((bf16[64,768]{1,0:T(8,128)(2,1)S(1)}, bf16[64,768]{1,0:T(8,128)(2,1)S(1)}, u32[]{:S(2)}, u32[]{:S(2)}) %collective-permute-start.22) | collective-permute-done | bytes 98336 | tf_op jit(solution)/shard_map/ppermute | solution.py:356
  65.7 0.6 collective-permute-done.23.refs_3_
  66.3 1.8 %collective-permute-start.28 = (bf16[64,768]{1,0:T(8,128)(2,1)S(1)}, bf16[64,768]{1,0:T(8,128)(2,1)S(1)}, u32[]{:S(2)}, u32[]{:S(2)}) collective-permute-start(bf16[64,768]{1,0:T(8,128)(2,1)S(1)} %get-tuple-element.117), channel_id=1, source_target_pairs={{0,2},{2,0},{4,6},{6,4},{8,10},{10,8},{12,14},{14,12},{1,3},{3,1},... | collective-permute-start | bytes 294920 | tf_op jit(solution)/shard_map/ppermute | solution.py:356
  68.5 0.5 collective-permute-start.25
  69.0 2.6 %weight_far.1 = (bf16[3,1024,768]{2,1,0:T(8,128)(2,1)S(1)}, f32[8,128]{1,0:T(8,128)S(1)}) custom-call(bf16[7,256,256]{2,1,0:T(8,128)(2,1)S(1)} %get-tuple-element.98.refs_0_, bf16[7,256,256]{2,1,0:T(8,128)(2,1)S(1)} %collective-permute-done.17.refs_7_.refs_1_, bf16[11,256,256]{2,1,0:T(8,128)(2,1)S(1)} %get-tuple-element.118.refs_2_, ...), custom_call_target="tpu_custom_call" | custom-call | flops 2400000000 | bytes 2097152 | tf_op jit(solution)/shard_map/weight_far/pallas_call | solution.py:338
  71.6 3.7 %backward_near.1 = (bf16[64,768]{1,0:T(8,128)(2,1)S(1)}, bf16[64,768]{1,0:T(8,128)(2,1)S(1)}, bf16[64,768]{1,0:T(8,128)(2,1)S(1)}, bf16[64,768]{1,0:T(8,128)(2,1...) custom-call(bf16[3,1024,768]{2,1,0:T(8,128)(2,1)S(1)} %bitcast.15, ...), custom_call_target="tpu_custom_call" | custom-call | flops 10000000000 | bytes 2097152 | tf_op jit(solution)/shard_map/backward_near/pallas_call | solution.py:338
  75.4 2.3 %collective-permute-start.30 = (bf16[64,768]{1,0:T(8,128)(2,1)S(1)}, bf16[64,768]{1,0:T(8,128)(2,1)S(1)}, u32[]{:S(2)}, u32[]{:S(2)}) collective-permute-start(bf16[64,768]{1,0:T(8,128)(2,1)S(1)} %get-tuple-element.124), channel_id=1, source_target_pairs={{0,6},{2,4},{4,2},{6,0},{8,14},{10,12},{12,10},{14,8},{1,7},{3,5},... | collective-permute-start | bytes 294920 | tf_op jit(solution)/shard_map/ppermute | solution.py:356
  77.7 1.2 %collective-permute-start.31 = (bf16[64,768]{1,0:T(8,128)(2,1)S(1)}, bf16[64,768]{1,0:T(8,128)(2,1)S(1)}, u32[]{:S(2)}, u32[]{:S(2)}) collective-permute-start(bf16[64,768]{1,0:T(8,128)(2,1)S(1)} %get-tuple-element.125), channel_id=1, source_target_pairs={{0,4},{2,6},{4,0},{6,2},{8,12},{10,14},{12,8},{14,10},{1,5},{3,7},... | collective-permute-start | bytes 294920 | tf_op jit(solution)/shard_map/ppermute | solution.py:356
  78.9 0.5 collective-permute-start.32
  79.5 3.9 %weight_near.1 = (bf16[3,1024,768]{2,1,0:T(8,128)(2,1)}, f32[8,128]{1,0:T(8,128)S(1)}) custom-call(bf16[3,1024,768]{2,1,0:T(8,128)(2,1)S(1)} %get-tuple-element.127.refs_0_, bf16[7,256,256]{2,1,0:T(8,128)(2,1)S(1)} %get-tuple-element.76.refs_6_.refs_1_, bf16[7,256,256]{2,1,0:T(8,128)(2,1)S(1)} %collective-permute-done.6.refs_0_.refs_8_.refs_2_, ...), custom_call_target="tpu_custom_call" | custom-call | flops 30000001024 | bytes 2097152 | tf_op jit(solution)/shard_map/weight_near/pallas_call | solution.py:338
  83.4 0.7 collective-permute-done.31.refs_4_
  84.1 0.9 %combine_gradients.1 = bf16[128,768]{1,0:T(8,128)(2,1)} custom-call(bf16[2,256,128]{2,1,0:T(8,128)(2,1)S(1)} %get-tuple-element.70.refs_1_.refs_0_, bf16[128,768]{1,0:T(8,128)(2,1)S(1)} %get-tuple-element.122.refs_1_, bf16[64,768]{1,0:T(8,128)(2,1)S(1)} %get-tuple-element.123.refs_2_, bf16[64,768]{1,0:T(8,128)(2,1)S(1)} %collective-permute-done.30.refs_3_, ...), custom_call_target="tpu_custom_call" | custom-call | flops 30000001024 | bytes 2097152 | tf_op jit(solution)/shard_map/combine_gradients/pallas_call | solution.py:338
  (49 shorter events, 1.2 us)
Async XLA Ops:
  0.6 19.8 %collective-permute-start.2 = (bf16[3,1024,768]{2,1,0:T(8,128)(2,1)}, bf16[3,1024,768]{2,1,0:T(8,128)(2,1)S(1)}, u32[]{:S(2)}, u32[]{:S(2)}) collective-permute-start(bf16[3,1024,768]{2,1,0:T(8,128)(2,1)} %bitcast.9), channel_id=1, source_target_pairs={{0,1},{1,0},{2,3},{3,2},{4,5},{5,4},{6,7},{7,6},{8,9},{9,8},{10,11... | collective-permute-start | bytes 14155784 | tf_op jit(solution)/shard_map/ppermute | solution.py:364
  1.1 15.4 %collective-permute-start.1 = (bf16[128,768]{1,0:T(8,128)(2,1)}, bf16[128,768]{1,0:T(8,128)(2,1)S(1)}, u32[]{:S(2)}, u32[]{:S(2)}) collective-permute-start(bf16[128,768]{1,0:T(8,128)(2,1)} %refs_2_.3), channel_id=1, source_target_pairs={{0,8},{2,10},{4,12},{6,14},{8,0},{10,2},{12,4},{14,6},{1,9},{3,11}... | collective-permute-start | bytes 589832 | tf_op jit(solution)/shard_map/ppermute | solution.py:361
  4.8 1.0 %copy-start = (bf16[128,768]{1,0:T(8,128)(2,1)S(1)}, bf16[128,768]{1,0:T(8,128)(2,1)}, u32[]{:S(2)}) copy-start(bf16[128,768]{1,0:T(8,128)(2,1)} %refs_2_.3) | copy-start | bytes 589828
  5.8 0.7 copy-start.2
  6.5 0.7 copy-start.3
  7.5 7.4 %collective-permute-start = (f32[8,128]{1,0:T(8,128)S(1)}, f32[8,128]{1,0:T(8,128)S(1)}, u32[]{:S(2)}, u32[]{:S(2)}) collective-permute-start(f32[8,128]{1,0:T(8,128)S(1)} %get-tuple-element.69.refs_0_), channel_id=1, source_target_pairs={{0,8},{2,10},{4,12},{6,14},{8,0},{10,2},{12,4},{14,6},{1,9},{3,11}... | collective-permute-start | bytes 12296 | tf_op jit(solution)/shard_map/ppermute | solution.py:361
  7.6 10.1 %collective-permute-start.3 = (bf16[64,768]{1,0:T(8,128)(2,1)S(1)}, bf16[64,768]{1,0:T(8,128)(2,1)S(1)}, u32[]{:S(2)}, u32[]{:S(2)}) collective-permute-start(bf16[64,768]{1,0:T(8,128)(2,1)S(1)} %get-tuple-element.73), channel_id=1, source_target_pairs={{0,6},{2,4},{4,2},{6,0},{8,14},{10,12},{12,10},{14,8},{1,7},{3,5},... | collective-permute-start | bytes 294920 | tf_op jit(solution)/shard_map/ppermute | solution.py:356
  10.4 8.4 %collective-permute-start.4 = (bf16[64,768]{1,0:T(8,128)(2,1)S(1)}, bf16[64,768]{1,0:T(8,128)(2,1)S(1)}, u32[]{:S(2)}, u32[]{:S(2)}) collective-permute-start(bf16[64,768]{1,0:T(8,128)(2,1)S(1)} %get-tuple-element.74), channel_id=1, source_target_pairs={{0,4},{2,6},{4,0},{6,2},{8,12},{10,14},{12,8},{14,10},{1,5},{3,7},... | collective-permute-start | bytes 294920 | tf_op jit(solution)/shard_map/ppermute | solution.py:356
  14.9 5.5 %slice-start = ((s8[4718592]{0:T(1024)(128)(4,1)}), s8[4194304]{0:T(1024)(128)(4,1)S(1)}, s32[]{:S(2)}) async-start(s8[4718592]{0:T(1024)(128)(4,1)} %bitcast.10), calls=%async_computation | async-start | bytes 8388608
  14.9 5.5 %slice-start.1 = ((s8[4718592]{0:T(1024)(128)(4,1)}), s8[524288]{0:T(1024)(128)(4,1)S(1)}, s32[]{:S(2)}) async-start(s8[4718592]{0:T(1024)(128)(4,1)} %bitcast.10), calls=%async_computation.1 | async-start | bytes 1048576
  14.9 5.5 %collective-permute-start.5 = (bf16[64,768]{1,0:T(8,128)(2,1)S(1)}, bf16[64,768]{1,0:T(8,128)(2,1)S(1)}, u32[]{:S(2)}, u32[]{:S(2)}) collective-permute-start(bf16[64,768]{1,0:T(8,128)(2,1)S(1)} %get-tuple-element.75), channel_id=1, source_target_pairs={{0,2},{2,0},{4,6},{6,4},{8,10},{10,8},{12,14},{14,12},{1,3},{3,1},... | collective-permute-start | bytes 294920 | tf_op jit(solution)/shard_map/ppermute | solution.py:356
  16.9 11.0 %collective-permute-start.10 = (bf16[64,768]{1,0:T(8,128)(2,1)S(1)}, bf16[64,768]{1,0:T(8,128)(2,1)S(1)}, u32[]{:S(2)}, u32[]{:S(2)}) collective-permute-start(bf16[64,768]{1,0:T(8,128)(2,1)S(1)} %get-tuple-element.82), channel_id=1, source_target_pairs={{0,6},{2,4},{4,2},{6,0},{8,14},{10,12},{12,10},{14,8},{1,7},{3,5},... | collective-permute-start | bytes 294920 | tf_op jit(solution)/shard_map/ppermute | solution.py:356
  17.7 10.2 %collective-permute-start.11 = (bf16[64,768]{1,0:T(8,128)(2,1)S(1)}, bf16[64,768]{1,0:T(8,128)(2,1)S(1)}, u32[]{:S(2)}, u32[]{:S(2)}) collective-permute-start(bf16[64,768]{1,0:T(8,128)(2,1)S(1)} %get-tuple-element.83), channel_id=1, source_target_pairs={{0,4},{2,6},{4,0},{6,2},{8,12},{10,14},{12,8},{14,10},{1,5},{3,7},... | collective-permute-start | bytes 294920 | tf_op jit(solution)/shard_map/ppermute | solution.py:356
  18.9 9.1 %collective-permute-start.12 = (bf16[64,768]{1,0:T(8,128)(2,1)S(1)}, bf16[64,768]{1,0:T(8,128)(2,1)S(1)}, u32[]{:S(2)}, u32[]{:S(2)}) collective-permute-start(bf16[64,768]{1,0:T(8,128)(2,1)S(1)} %get-tuple-element.84), channel_id=1, source_target_pairs={{0,2},{2,0},{4,6},{6,4},{8,10},{10,8},{12,14},{14,12},{1,3},{3,1},... | collective-permute-start | bytes 294920 | tf_op jit(solution)/shard_map/ppermute | solution.py:356
  23.9 7.5 %collective-permute-start.7 = (bf16[64,768]{1,0:T(8,128)(2,1)S(1)}, bf16[64,768]{1,0:T(8,128)(2,1)S(1)}, u32[]{:S(2)}, u32[]{:S(2)}) collective-permute-start(bf16[64,768]{1,0:T(8,128)(2,1)S(1)} %get-tuple-element.78), channel_id=1, source_target_pairs={{0,6},{2,4},{4,2},{6,0},{8,14},{10,12},{12,10},{14,8},{1,7},{3,5},... | collective-permute-start | bytes 294920 | tf_op jit(solution)/shard_map/ppermute | solution.py:356
  26.6 5.0 %collective-permute-start.8 = (bf16[64,768]{1,0:T(8,128)(2,1)S(1)}, bf16[64,768]{1,0:T(8,128)(2,1)S(1)}, u32[]{:S(2)}, u32[]{:S(2)}) collective-permute-start(bf16[64,768]{1,0:T(8,128)(2,1)S(1)} %get-tuple-element.79), channel_id=1, source_target_pairs={{0,4},{2,6},{4,0},{6,2},{8,12},{10,14},{12,8},{14,10},{1,5},{3,7},... | collective-permute-start | bytes 294920 | tf_op jit(solution)/shard_map/ppermute | solution.py:356
  27.9 4.6 %collective-permute-start.9 = (bf16[64,768]{1,0:T(8,128)(2,1)S(1)}, bf16[64,768]{1,0:T(8,128)(2,1)S(1)}, u32[]{:S(2)}, u32[]{:S(2)}) collective-permute-start(bf16[64,768]{1,0:T(8,128)(2,1)S(1)} %get-tuple-element.80), channel_id=1, source_target_pairs={{0,2},{2,0},{4,6},{6,4},{8,10},{10,8},{12,14},{14,12},{1,3},{3,1},... | collective-permute-start | bytes 294920 | tf_op jit(solution)/shard_map/ppermute | solution.py:356
  27.9 6.8 %collective-permute-start.6 = (bf16[7,256,256]{2,1,0:T(8,128)(2,1)S(1)}, bf16[7,256,256]{2,1,0:T(8,128)(2,1)S(1)}, u32[]{:S(2)}, u32[]{:S(2)}) collective-permute-start(bf16[7,256,256]{2,1,0:T(8,128)(2,1)S(1)} %get-tuple-element.76.refs_6_.refs_1_), channel_id=1, source_target_pairs={{0,1},{1,0},{2,3},{3,2},{4,5},{5,4},{6,7},{7,6},{8,9},{9,8},{10,11... | collective-permute-start | bytes 2752520 | tf_op jit(solution)/shard_map/ppermute | solution.py:364
  28.0 4.5 %copy-start.1 = (bf16[128,768]{1,0:T(8,128)(2,1)S(1)}, bf16[128,768]{1,0:T(8,128)(2,1)}, u32[]{:S(2)}) copy-start(bf16[128,768]{1,0:T(8,128)(2,1)} %refs_2_.5) | copy-start | bytes 589828
  32.9 11.5 %collective-permute-start.13 = (bf16[128,768]{1,0:T(8,128)(2,1)S(1)}, bf16[128,768]{1,0:T(8,128)(2,1)S(1)}, u32[]{:S(2)}, u32[]{:S(2)}) collective-permute-start(bf16[128,768]{1,0:T(8,128)(2,1)S(1)} %get-tuple-element.94), channel_id=1, source_target_pairs={{0,8},{2,10},{4,12},{6,14},{8,0},{10,2},{12,4},{14,6},{1,9},{3,11}... | collective-permute-start | bytes 589832 | tf_op jit(solution)/shard_map/ppermute | solution.py:361
  34.7 9.7 %collective-permute-start.17 = (bf16[7,256,256]{2,1,0:T(8,128)(2,1)S(1)}, bf16[7,256,256]{2,1,0:T(8,128)(2,1)S(1)}, u32[]{:S(2)}, u32[]{:S(2)}) collective-permute-start(bf16[7,256,256]{2,1,0:T(8,128)(2,1)S(1)} %get-tuple-element.98.refs_0_), channel_id=1, source_target_pairs={{0,1},{1,0},{2,3},{3,2},{4,5},{5,4},{6,7},{7,6},{8,9},{9,8},{10,11... | collective-permute-start | bytes 2752520 | tf_op jit(solution)/shard_map/ppermute | solution.py:364
  34.7 9.7 %collective-permute-start.14 = (bf16[64,768]{1,0:T(8,128)(2,1)S(1)}, bf16[64,768]{1,0:T(8,128)(2,1)S(1)}, u32[]{:S(2)}, u32[]{:S(2)}) collective-permute-start(bf16[64,768]{1,0:T(8,128)(2,1)S(1)} %get-tuple-element.95), channel_id=1, source_target_pairs={{0,6},{2,4},{4,2},{6,0},{8,14},{10,12},{12,10},{14,8},{1,7},{3,5},... | collective-permute-start | bytes 294920 | tf_op jit(solution)/shard_map/ppermute | solution.py:356
  37.3 8.6 %collective-permute-start.15 = (bf16[64,768]{1,0:T(8,128)(2,1)S(1)}, bf16[64,768]{1,0:T(8,128)(2,1)S(1)}, u32[]{:S(2)}, u32[]{:S(2)}) collective-permute-start(bf16[64,768]{1,0:T(8,128)(2,1)S(1)} %get-tuple-element.96), channel_id=1, source_target_pairs={{0,4},{2,6},{4,0},{6,2},{8,12},{10,14},{12,8},{14,10},{1,5},{3,7},... | collective-permute-start | bytes 294920 | tf_op jit(solution)/shard_map/ppermute | solution.py:356
  37.3 8.6 %collective-permute-start.16 = (bf16[64,768]{1,0:T(8,128)(2,1)S(1)}, bf16[64,768]{1,0:T(8,128)(2,1)S(1)}, u32[]{:S(2)}, u32[]{:S(2)}) collective-permute-start(bf16[64,768]{1,0:T(8,128)(2,1)S(1)} %get-tuple-element.97), channel_id=1, source_target_pairs={{0,2},{2,0},{4,6},{6,4},{8,10},{10,8},{12,14},{14,12},{1,3},{3,1},... | collective-permute-start | bytes 294920 | tf_op jit(solution)/shard_map/ppermute | solution.py:356
  46.5 6.4 %collective-permute-start.19 = (bf16[64,768]{1,0:T(8,128)(2,1)S(1)}, bf16[64,768]{1,0:T(8,128)(2,1)S(1)}, u32[]{:S(2)}, u32[]{:S(2)}) collective-permute-start(bf16[64,768]{1,0:T(8,128)(2,1)S(1)} %get-tuple-element.103), channel_id=1, source_target_pairs={{0,6},{2,4},{4,2},{6,0},{8,14},{10,12},{12,10},{14,8},{1,7},{3,5},... | collective-permute-start | bytes 294920 | tf_op jit(solution)/shard_map/ppermute | solution.py:356
  47.3 7.9 %collective-permute-start.20 = (bf16[64,768]{1,0:T(8,128)(2,1)S(1)}, bf16[64,768]{1,0:T(8,128)(2,1)S(1)}, u32[]{:S(2)}, u32[]{:S(2)}) collective-permute-start(bf16[64,768]{1,0:T(8,128)(2,1)S(1)} %get-tuple-element.104), channel_id=1, source_target_pairs={{0,4},{2,6},{4,0},{6,2},{8,12},{10,14},{12,8},{14,10},{1,5},{3,7},... | collective-permute-start | bytes 294920 | tf_op jit(solution)/shard_map/ppermute | solution.py:356
  49.2 6.0 %collective-permute-start.21 = (bf16[64,768]{1,0:T(8,128)(2,1)S(1)}, bf16[64,768]{1,0:T(8,128)(2,1)S(1)}, u32[]{:S(2)}, u32[]{:S(2)}) collective-permute-start(bf16[64,768]{1,0:T(8,128)(2,1)S(1)} %get-tuple-element.105), channel_id=1, source_target_pairs={{0,2},{2,0},{4,6},{6,4},{8,10},{10,8},{12,14},{14,12},{1,3},{3,1},... | collective-permute-start | bytes 294920 | tf_op jit(solution)/shard_map/ppermute | solution.py:356
  50.1 12.5 %collective-permute-start.18 = (bf16[144,768]{1,0:T(8,128)(2,1)S(1)}, bf16[144,768]{1,0:T(8,128)(2,1)S(1)}, u32[]{:S(2)}, u32[]{:S(2)}) collective-permute-start(bf16[144,768]{1,0:T(8,128)(2,1)S(1)} %get-tuple-element.99), channel_id=1, source_target_pairs={{0,8},{2,10},{4,12},{6,14},{8,0},{10,2},{12,4},{14,6},{1,9},{3,11}... | collective-permute-start | bytes 663560 | tf_op jit(solution)/shard_map/ppermute | solution.py:361
  58.9 10.0 %collective-permute-start.29 = (bf16[11,256,256]{2,1,0:T(8,128)(2,1)S(1)}, bf16[11,256,256]{2,1,0:T(8,128)(2,1)S(1)}, u32[]{:S(2)}, u32[]{:S(2)}) collective-permute-start(bf16[11,256,256]{2,1,0:T(8,128)(2,1)S(1)} %get-tuple-element.118.refs_2_), channel_id=1, source_target_pairs={{0,1},{1,0},{2,3},{3,2},{4,5},{5,4},{6,7},{7,6},{8,9},{9,8},{10,11... | collective-permute-start | bytes 4325384 | tf_op jit(solution)/shard_map/ppermute | solution.py:364
  59.0 6.6 %collective-permute-start.22 = (bf16[64,768]{1,0:T(8,128)(2,1)S(1)}, bf16[64,768]{1,0:T(8,128)(2,1)S(1)}, u32[]{:S(2)}, u32[]{:S(2)}) collective-permute-start(bf16[64,768]{1,0:T(8,128)(2,1)S(1)} %get-tuple-element.109), channel_id=1, source_target_pairs={{0,6},{2,4},{4,2},{6,0},{8,14},{10,12},{12,10},{14,8},{1,7},{3,5},... | collective-permute-start | bytes 294920 | tf_op jit(solution)/shard_map/ppermute | solution.py:356
  59.1 7.2 %collective-permute-start.23 = (bf16[64,768]{1,0:T(8,128)(2,1)S(1)}, bf16[64,768]{1,0:T(8,128)(2,1)S(1)}, u32[]{:S(2)}, u32[]{:S(2)}) collective-permute-start(bf16[64,768]{1,0:T(8,128)(2,1)S(1)} %get-tuple-element.110), channel_id=1, source_target_pairs={{0,4},{2,6},{4,0},{6,2},{8,12},{10,14},{12,8},{14,10},{1,5},{3,7},... | collective-permute-start | bytes 294920 | tf_op jit(solution)/shard_map/ppermute | solution.py:356
  60.6 7.5 %collective-permute-start.24 = (bf16[64,768]{1,0:T(8,128)(2,1)S(1)}, bf16[64,768]{1,0:T(8,128)(2,1)S(1)}, u32[]{:S(2)}, u32[]{:S(2)}) collective-permute-start(bf16[64,768]{1,0:T(8,128)(2,1)S(1)} %get-tuple-element.111), channel_id=1, source_target_pairs={{0,2},{2,0},{4,6},{6,4},{8,10},{10,8},{12,14},{14,12},{1,3},{3,1},... | collective-permute-start | bytes 294920 | tf_op jit(solution)/shard_map/ppermute | solution.py:356
  63.7 7.9 %collective-permute-start.26 = (bf16[64,768]{1,0:T(8,128)(2,1)S(1)}, bf16[64,768]{1,0:T(8,128)(2,1)S(1)}, u32[]{:S(2)}, u32[]{:S(2)}) collective-permute-start(bf16[64,768]{1,0:T(8,128)(2,1)S(1)} %get-tuple-element.115), channel_id=1, source_target_pairs={{0,6},{2,4},{4,2},{6,0},{8,14},{10,12},{12,10},{14,8},{1,7},{3,5},... | collective-permute-start | bytes 294920 | tf_op jit(solution)/shard_map/ppermute | solution.py:356
  65.6 6.0 %collective-permute-start.27 = (bf16[64,768]{1,0:T(8,128)(2,1)S(1)}, bf16[64,768]{1,0:T(8,128)(2,1)S(1)}, u32[]{:S(2)}, u32[]{:S(2)}) collective-permute-start(bf16[64,768]{1,0:T(8,128)(2,1)S(1)} %get-tuple-element.116), channel_id=1, source_target_pairs={{0,4},{2,6},{4,0},{6,2},{8,12},{10,14},{12,8},{14,10},{1,5},{3,7},... | collective-permute-start | bytes 294920 | tf_op jit(solution)/shard_map/ppermute | solution.py:356
  66.3 5.3 %collective-permute-start.28 = (bf16[64,768]{1,0:T(8,128)(2,1)S(1)}, bf16[64,768]{1,0:T(8,128)(2,1)S(1)}, u32[]{:S(2)}, u32[]{:S(2)}) collective-permute-start(bf16[64,768]{1,0:T(8,128)(2,1)S(1)} %get-tuple-element.117), channel_id=1, source_target_pairs={{0,2},{2,0},{4,6},{6,4},{8,10},{10,8},{12,14},{14,12},{1,3},{3,1},... | collective-permute-start | bytes 294920 | tf_op jit(solution)/shard_map/ppermute | solution.py:356
  68.5 11.1 %collective-permute-start.25 = (bf16[128,768]{1,0:T(8,128)(2,1)S(1)}, bf16[128,768]{1,0:T(8,128)(2,1)S(1)}, u32[]{:S(2)}, u32[]{:S(2)}) collective-permute-start(bf16[128,768]{1,0:T(8,128)(2,1)S(1)} %far_back.1.refs_6_.refs_8_), channel_id=1, source_target_pairs={{0,8},{2,10},{4,12},{6,14},{8,0},{10,2},{12,4},{14,6},{1,9},{3,11}... | collective-permute-start | bytes 589832 | tf_op jit(solution)/shard_map/ppermute | solution.py:361
  75.4 4.2 %collective-permute-start.33 = (bf16[11,256,256]{2,1,0:T(8,128)(2,1)S(1)}, bf16[11,256,256]{2,1,0:T(8,128)(2,1)S(1)}, u32[]{:S(2)}, u32[]{:S(2)}) collective-permute-start(bf16[11,256,256]{2,1,0:T(8,128)(2,1)S(1)} %get-tuple-element.128.refs_3_), channel_id=1, source_target_pairs={{0,1},{1,0},{2,3},{3,2},{4,5},{5,4},{6,7},{7,6},{8,9},{9,8},{10,11... | collective-permute-start | bytes 4325384 | tf_op jit(solution)/shard_map/ppermute | solution.py:364
  75.4 8.0 %collective-permute-start.30 = (bf16[64,768]{1,0:T(8,128)(2,1)S(1)}, bf16[64,768]{1,0:T(8,128)(2,1)S(1)}, u32[]{:S(2)}, u32[]{:S(2)}) collective-permute-start(bf16[64,768]{1,0:T(8,128)(2,1)S(1)} %get-tuple-element.124), channel_id=1, source_target_pairs={{0,6},{2,4},{4,2},{6,0},{8,14},{10,12},{12,10},{14,8},{1,7},{3,5},... | collective-permute-start | bytes 294920 | tf_op jit(solution)/shard_map/ppermute | solution.py:356
  77.7 6.4 %collective-permute-start.31 = (bf16[64,768]{1,0:T(8,128)(2,1)S(1)}, bf16[64,768]{1,0:T(8,128)(2,1)S(1)}, u32[]{:S(2)}, u32[]{:S(2)}) collective-permute-start(bf16[64,768]{1,0:T(8,128)(2,1)S(1)} %get-tuple-element.125), channel_id=1, source_target_pairs={{0,4},{2,6},{4,0},{6,2},{8,12},{10,14},{12,8},{14,10},{1,5},{3,7},... | collective-permute-start | bytes 294920 | tf_op jit(solution)/shard_map/ppermute | solution.py:356
  78.9 5.2 %collective-permute-start.32 = (bf16[64,768]{1,0:T(8,128)(2,1)S(1)}, bf16[64,768]{1,0:T(8,128)(2,1)S(1)}, u32[]{:S(2)}, u32[]{:S(2)}) collective-permute-start(bf16[64,768]{1,0:T(8,128)(2,1)S(1)} %get-tuple-element.126), channel_id=1, source_target_pairs={{0,2},{2,0},{4,6},{6,4},{8,10},{10,8},{12,14},{14,12},{1,3},{3,1},... | collective-permute-start | bytes 294920 | tf_op jit(solution)/shard_map/ppermute | solution.py:356

commit v16 on v15

--- a/solution.py
+++ b/solution.py
@@ -234,7 +234,8 @@
 
 def final_kernel(masks_ref, part_ref, *refs):
     ins, out_ref = refs[:-1], refs[-1]
-    total = dot(masks_ref[0] + masks_ref[1], get(ins), FIRST) + part_ref[...].astype(F32)
+    got = jnp.concatenate([ref[...] for ref in ins], axis=0)
+    total = dot(masks_ref[0] + masks_ref[1], got, FIRST) + part_ref[...].astype(F32)
     out_ref[...] = total.astype(BF16)
 
 
@@ -501,7 +502,7 @@
         [],
         near_masks,
         part,
-        *back_near,
+        *(back_near[:1] + back_near[:0:-1]),
         after=[finished],
     )
     return (student, d_tokens, d_gates.T, weight_grads.transpose(1, 0, 2)[None])

time: 85.2 us -> 85.8 us (level)
  no operation moved by 1% of the time
where the time goes in v16:
time: 85.8 us; the launch traced here: 85.6 us
  starting transfers between devices  36.6 us (43%)
  Pallas kernels  24.9 us (29%)
  waiting for transfers between devices  20.9 us (24%)
  local copies, waits for them, and re-layouts  2.33 us (3%)
  between operations  0.86 us (1%)
    ppermute x24, starting transfers between devices, within_half(): lax.ppermute(rows_of[s], 'expert', [(i, i ^ s) for i in range(experts)])  29.1 us
    pallas_call x16, Pallas kernels, call(): pl.pallas_call(body, in_specs=specs + [aspec] * (len(after) + len(through...  24.9 us
    ppermute x24, waiting for transfers between devices, within_half(): lax.ppermute(rows_of[s], 'expert', [(i, i ^ s) for i in range(experts)])  10.6 us
    ppermute x5, waiting for transfers between devices, to_mirror(): return lax.ppermute(x, 'expert', [(i, i ^ half) for i in range(experts)])  10.3 us
    ppermute x5, starting transfers between devices, to_mirror(): return lax.ppermute(x, 'expert', [(i, i ^ half) for i in range(experts)])  6.73 us
    unnamed x12, local copies, waits for them, and re-layouts  2.33 us
  transfers between devices with their start and end apart: 34, of which 11 were waited for; matrix products, arithmetic and copies ran while one was open for 0% of the time, Pallas kernels for 27%

profile of v16, /device:TPU:0, one launch (start us, length us, event | category | flops | bytes accessed | tf_op | source)
XLA Modules:
  0.0 85.6 jit_solution(2979393543235523055)
XLA Ops:
  0.6 0.5 collective-permute-start.2
  1.1 3.7 %collective-permute-start.1 = (bf16[128,768]{1,0:T(8,128)(2,1)}, bf16[128,768]{1,0:T(8,128)(2,1)S(1)}, u32[]{:S(2)}, u32[]{:S(2)}) collective-permute-start(bf16[128,768]{1,0:T(8,128)(2,1)} %refs_2_.3), channel_id=1, source_target_pairs={{0,8},{2,10},{4,12},{6,14},{8,0},{10,2},{12,4},{14,6},{1,9},{3,11}... | collective-permute-start | bytes 589832 | tf_op jit(solution)/shard_map/ppermute | solution.py:362
  4.8 1.0 %copy-done = bf16[128,768]{1,0:T(8,128)(2,1)S(1)} copy-done((bf16[128,768]{1,0:T(8,128)(2,1)S(1)}, bf16[128,768]{1,0:T(8,128)(2,1)}, u32[]{:S(2)}) %copy-start) | copy-done | bytes 196632
  5.8 0.7 copy-done.2
  6.5 0.7 copy-done.3
  7.1 0.4 pack_near.1
  7.6 2.9 %collective-permute-start.3 = (bf16[64,768]{1,0:T(8,128)(2,1)S(1)}, bf16[64,768]{1,0:T(8,128)(2,1)S(1)}, u32[]{:S(2)}, u32[]{:S(2)}) collective-permute-start(bf16[64,768]{1,0:T(8,128)(2,1)S(1)} %get-tuple-element.73), channel_id=1, source_target_pairs={{0,6},{2,4},{4,2},{6,0},{8,14},{10,12},{12,10},{14,8},{1,7},{3,5},... | collective-permute-start | bytes 294920 | tf_op jit(solution)/shard_map/ppermute | solution.py:357
  10.4 0.4 collective-permute-start.4
  10.9 4.0 %collective-permute-done.refs_0_ = f32[8,128]{1,0:T(8,128)S(1)} collective-permute-done((f32[8,128]{1,0:T(8,128)S(1)}, f32[8,128]{1,0:T(8,128)S(1)}, u32[]{:S(2)}, u32[]{:S(2)}) %collective-permute-start) | collective-permute-done | bytes 4128 | tf_op jit(solution)/shard_map/ppermute | solution.py:362
  14.9 1.6 %collective-permute-start.5 = (bf16[64,768]{1,0:T(8,128)(2,1)S(1)}, bf16[64,768]{1,0:T(8,128)(2,1)S(1)}, u32[]{:S(2)}, u32[]{:S(2)}) collective-permute-start(bf16[64,768]{1,0:T(8,128)(2,1)S(1)} %get-tuple-element.75), channel_id=1, source_target_pairs={{0,2},{2,0},{4,6},{6,4},{8,10},{10,8},{12,14},{14,12},{1,3},{3,1},... | collective-permute-start | bytes 294920 | tf_op jit(solution)/shard_map/ppermute | solution.py:357
  16.5 0.4 pack_far.1
  16.9 0.8 collective-permute-start.10
  17.7 1.2 %collective-permute-start.11 = (bf16[64,768]{1,0:T(8,128)(2,1)S(1)}, bf16[64,768]{1,0:T(8,128)(2,1)S(1)}, u32[]{:S(2)}, u32[]{:S(2)}) collective-permute-start(bf16[64,768]{1,0:T(8,128)(2,1)S(1)} %get-tuple-element.83), channel_id=1, source_target_pairs={{0,4},{2,6},{4,0},{6,2},{8,12},{10,14},{12,8},{14,10},{1,5},{3,7},... | collective-permute-start | bytes 294920 | tf_op jit(solution)/shard_map/ppermute | solution.py:357
  18.9 1.6 %collective-permute-start.12 = (bf16[64,768]{1,0:T(8,128)(2,1)S(1)}, bf16[64,768]{1,0:T(8,128)(2,1)S(1)}, u32[]{:S(2)}, u32[]{:S(2)}) collective-permute-start(bf16[64,768]{1,0:T(8,128)(2,1)S(1)} %get-tuple-element.84), channel_id=1, source_target_pairs={{0,2},{2,0},{4,6},{6,4},{8,10},{10,8},{12,14},{14,12},{1,3},{3,1},... | collective-permute-start | bytes 294920 | tf_op jit(solution)/shard_map/ppermute | solution.py:357
  20.5 3.4 %forward_near.1 = (bf16[64,768]{1,0:T(8,128)(2,1)S(1)}, bf16[64,768]{1,0:T(8,128)(2,1)S(1)}, bf16[64,768]{1,0:T(8,128)(2,1)S(1)}, bf16[64,768]{1,0:T(8,128)(2,1)...) custom-call(bf16[3,1024,768]{2,1,0:T(8,128)(2,1)S(1)} %bitcast.12, ...), custom_call_target="tpu_custom_call" | custom-call | flops 100000000 | bytes 2097152 | tf_op jit(solution)/shard_map/forward_near/pallas_call | solution.py:339
  23.9 2.7 %collective-permute-start.7 = (bf16[64,768]{1,0:T(8,128)(2,1)S(1)}, bf16[64,768]{1,0:T(8,128)(2,1)S(1)}, u32[]{:S(2)}, u32[]{:S(2)}) collective-permute-start(bf16[64,768]{1,0:T(8,128)(2,1)S(1)} %get-tuple-element.78), channel_id=1, source_target_pairs={{0,6},{2,4},{4,2},{6,0},{8,14},{10,12},{12,10},{14,8},{1,7},{3,5},... | collective-permute-start | bytes 294920 | tf_op jit(solution)/shard_map/ppermute | solution.py:357
  26.6 1.3 %collective-permute-start.8 = (bf16[64,768]{1,0:T(8,128)(2,1)S(1)}, bf16[64,768]{1,0:T(8,128)(2,1)S(1)}, u32[]{:S(2)}, u32[]{:S(2)}) collective-permute-start(bf16[64,768]{1,0:T(8,128)(2,1)S(1)} %get-tuple-element.79), channel_id=1, source_target_pairs={{0,4},{2,6},{4,0},{6,2},{8,12},{10,14},{12,8},{14,10},{1,5},{3,7},... | collective-permute-start | bytes 294920 | tf_op jit(solution)/shard_map/ppermute | solution.py:357
  28.0 3.4 %forward_far.1 = (bf16[64,768]{1,0:T(8,128)(2,1)S(1)}, bf16[64,768]{1,0:T(8,128)(2,1)S(1)}, bf16[64,768]{1,0:T(8,128)(2,1)S(1)}, bf16[64,768]{1,0:T(8,128)(2,1)S...) custom-call(bf16[3,1024,768]{2,1,0:T(8,128)(2,1)S(1)} %bitcast.13, ...), custom_call_target="tpu_custom_call" | custom-call | flops 3000000000 | bytes 2097152 | tf_op jit(solution)/shard_map/forward_far/pallas_call | solution.py:339
  31.6 1.0 %collective-permute-done.9.refs_6_.refs_7_ = bf16[64,768]{1,0:T(8,128)(2,1)S(1)} collective-permute-done((bf16[64,768]{1,0:T(8,128)(2,1)S(1)}, bf16[64,768]{1,0:T(8,128)(2,1)S(1)}, u32[]{:S(2)}, u32[]{:S(2)}) %collective-permute-start.9) | collective-permute-done | bytes 98336 | tf_op jit(solution)/shard_map/ppermute | solution.py:357
  32.5 0.3 near_sum.1
  32.9 1.8 %collective-permute-start.13 = (bf16[128,768]{1,0:T(8,128)(2,1)S(1)}, bf16[128,768]{1,0:T(8,128)(2,1)S(1)}, u32[]{:S(2)}, u32[]{:S(2)}) collective-permute-start(bf16[128,768]{1,0:T(8,128)(2,1)S(1)} %get-tuple-element.94), channel_id=1, source_target_pairs={{0,8},{2,10},{4,12},{6,14},{8,0},{10,2},{12,4},{14,6},{1,9},{3,11}... | collective-permute-start | bytes 589832 | tf_op jit(solution)/shard_map/ppermute | solution.py:362
  34.7 2.6 %collective-permute-start.14 = (bf16[64,768]{1,0:T(8,128)(2,1)S(1)}, bf16[64,768]{1,0:T(8,128)(2,1)S(1)}, u32[]{:S(2)}, u32[]{:S(2)}) collective-permute-start(bf16[64,768]{1,0:T(8,128)(2,1)S(1)} %get-tuple-element.95), channel_id=1, source_target_pairs={{0,6},{2,4},{4,2},{6,0},{8,14},{10,12},{12,10},{14,8},{1,7},{3,5},... | collective-permute-start | bytes 294920 | tf_op jit(solution)/shard_map/ppermute | solution.py:357
  37.3 0.9 %collective-permute-start.16 = (bf16[64,768]{1,0:T(8,128)(2,1)S(1)}, bf16[64,768]{1,0:T(8,128)(2,1)S(1)}, u32[]{:S(2)}, u32[]{:S(2)}) collective-permute-start(bf16[64,768]{1,0:T(8,128)(2,1)S(1)} %get-tuple-element.97), channel_id=1, source_target_pairs={{0,2},{2,0},{4,6},{6,4},{8,10},{10,8},{12,14},{14,12},{1,3},{3,1},... | collective-permute-start | bytes 294920 | tf_op jit(solution)/shard_map/ppermute | solution.py:357
  38.2 6.2 %collective-permute-done.13.refs_1_ = bf16[128,768]{1,0:T(8,128)(2,1)S(1)} collective-permute-done((bf16[128,768]{1,0:T(8,128)(2,1)S(1)}, bf16[128,768]{1,0:T(8,128)(2,1)S(1)}, u32[]{:S(2)}, u32[]{:S(2)}) %collective-permute-start.13) | collective-permute-done | bytes 196640 | tf_op jit(solution)/shard_map/ppermute | solution.py:362
  44.4 1.5 %collective-permute-done.15.refs_5_ = bf16[64,768]{1,0:T(8,128)(2,1)S(1)} collective-permute-done((bf16[64,768]{1,0:T(8,128)(2,1)S(1)}, bf16[64,768]{1,0:T(8,128)(2,1)S(1)}, u32[]{:S(2)}, u32[]{:S(2)}) %collective-permute-start.15) | collective-permute-done | bytes 98336 | tf_op jit(solution)/shard_map/ppermute | solution.py:357
  45.9 0.6 far_grad.1
  46.5 0.8 collective-permute-start.19
  47.3 1.9 %collective-permute-start.20 = (bf16[64,768]{1,0:T(8,128)(2,1)S(1)}, bf16[64,768]{1,0:T(8,128)(2,1)S(1)}, u32[]{:S(2)}, u32[]{:S(2)}) collective-permute-start(bf16[64,768]{1,0:T(8,128)(2,1)S(1)} %get-tuple-element.104), channel_id=1, source_target_pairs={{0,4},{2,6},{4,0},{6,2},{8,12},{10,14},{12,8},{14,10},{1,5},{3,7},... | collective-permute-start | bytes 294920 | tf_op jit(solution)/shard_map/ppermute | solution.py:357
  49.2 0.9 %collective-permute-start.21 = (bf16[64,768]{1,0:T(8,128)(2,1)S(1)}, bf16[64,768]{1,0:T(8,128)(2,1)S(1)}, u32[]{:S(2)}, u32[]{:S(2)}) collective-permute-start(bf16[64,768]{1,0:T(8,128)(2,1)S(1)} %get-tuple-element.105), channel_id=1, source_target_pairs={{0,2},{2,0},{4,6},{6,4},{8,10},{10,8},{12,14},{14,12},{1,3},{3,1},... | collective-permute-start | bytes 294920 | tf_op jit(solution)/shard_map/ppermute | solution.py:357
  50.1 0.7 collective-permute-start.18
  50.8 2.1 %collective-permute-done.19.refs_5_ = bf16[64,768]{1,0:T(8,128)(2,1)S(1)} collective-permute-done((bf16[64,768]{1,0:T(8,128)(2,1)S(1)}, bf16[64,768]{1,0:T(8,128)(2,1)S(1)}, u32[]{:S(2)}, u32[]{:S(2)}) %collective-permute-start.19) | collective-permute-done | bytes 98336 | tf_op jit(solution)/shard_map/ppermute | solution.py:357
  52.9 2.2 %collective-permute-done.20.refs_6_ = bf16[64,768]{1,0:T(8,128)(2,1)S(1)} collective-permute-done((bf16[64,768]{1,0:T(8,128)(2,1)S(1)}, bf16[64,768]{1,0:T(8,128)(2,1)S(1)}, u32[]{:S(2)}, u32[]{:S(2)}) %collective-permute-start.20) | collective-permute-done | bytes 98336 | tf_op jit(solution)/shard_map/ppermute | solution.py:357
  55.2 3.7 %backward_far.1 = (bf16[64,768]{1,0:T(8,128)(2,1)S(1)}, bf16[64,768]{1,0:T(8,128)(2,1)S(1)}, bf16[64,768]{1,0:T(8,128)(2,1)S(1)}, bf16[64,768]{1,0:T(8,128)(2,1)...) custom-call(bf16[3,1024,768]{2,1,0:T(8,128)(2,1)S(1)} %bitcast.14, ...), custom_call_target="tpu_custom_call" | custom-call | flops 3000000000 | bytes 2097152 | tf_op jit(solution)/shard_map/backward_far/pallas_call | solution.py:339
  59.1 1.5 %collective-permute-start.23 = (bf16[64,768]{1,0:T(8,128)(2,1)S(1)}, bf16[64,768]{1,0:T(8,128)(2,1)S(1)}, u32[]{:S(2)}, u32[]{:S(2)}) collective-permute-start(bf16[64,768]{1,0:T(8,128)(2,1)S(1)} %get-tuple-element.110), channel_id=1, source_target_pairs={{0,4},{2,6},{4,0},{6,2},{8,12},{10,14},{12,8},{14,10},{1,5},{3,7},... | collective-permute-start | bytes 294920 | tf_op jit(solution)/shard_map/ppermute | solution.py:357
  60.6 1.9 %collective-permute-start.24 = (bf16[64,768]{1,0:T(8,128)(2,1)S(1)}, bf16[64,768]{1,0:T(8,128)(2,1)S(1)}, u32[]{:S(2)}, u32[]{:S(2)}) collective-permute-start(bf16[64,768]{1,0:T(8,128)(2,1)S(1)} %get-tuple-element.111), channel_id=1, source_target_pairs={{0,2},{2,0},{4,6},{6,4},{8,10},{10,8},{12,14},{14,12},{1,3},{3,1},... | collective-permute-start | bytes 294920 | tf_op jit(solution)/shard_map/ppermute | solution.py:357
  62.6 1.1 %near_grad.1 = (bf16[128,768]{1,0:T(8,128)(2,1)}, f32[2,128]{1,0:T(2,128)}, bf16[64,768]{1,0:T(8,128)(2,1)S(1)}, bf16[64,768]{1,0:T(8,128)(2,1)S(1)}, bf16[64,76...) custom-call(f32[8,128]{1,0:T(8,128)S(1)} %get-tuple-element.69.refs_0_, ...), custom_call_target="tpu_custom_call" | custom-call | flops 30000001024 | bytes 2097152 | tf_op jit(solution)/shard_map/near_grad/pallas_call | solution.py:339
  63.8 1.8 %collective-permute-done.22.refs_2_ = bf16[64,768]{1,0:T(8,128)(2,1)S(1)} collective-permute-done((bf16[64,768]{1,0:T(8,128)(2,1)S(1)}, bf16[64,768]{1,0:T(8,128)(2,1)S(1)}, u32[]{:S(2)}, u32[]{:S(2)}) %collective-permute-start.22) | collective-permute-done | bytes 98336 | tf_op jit(solution)/shard_map/ppermute | solution.py:357
  65.7 0.6 collective-permute-done.23.refs_3_
  66.3 1.8 %collective-permute-start.28 = (bf16[64,768]{1,0:T(8,128)(2,1)S(1)}, bf16[64,768]{1,0:T(8,128)(2,1)S(1)}, u32[]{:S(2)}, u32[]{:S(2)}) collective-permute-start(bf16[64,768]{1,0:T(8,128)(2,1)S(1)} %get-tuple-element.117), channel_id=1, source_target_pairs={{0,2},{2,0},{4,6},{6,4},{8,10},{10,8},{12,14},{14,12},{1,3},{3,1},... | collective-permute-start | bytes 294920 | tf_op jit(solution)/shard_map/ppermute | solution.py:357
  68.5 0.5 collective-permute-start.25
  69.0 2.6 %weight_far.1 = (bf16[3,1024,768]{2,1,0:T(8,128)(2,1)S(1)}, f32[8,128]{1,0:T(8,128)S(1)}) custom-call(bf16[7,256,256]{2,1,0:T(8,128)(2,1)S(1)} %get-tuple-element.98.refs_0_, bf16[7,256,256]{2,1,0:T(8,128)(2,1)S(1)} %collective-permute-done.17.refs_7_.refs_1_, bf16[11,256,256]{2,1,0:T(8,128)(2,1)S(1)} %get-tuple-element.118.refs_2_, ...), custom_call_target="tpu_custom_call" | custom-call | flops 2400000000 | bytes 2097152 | tf_op jit(solution)/shard_map/weight_far/pallas_call | solution.py:339
  71.6 3.7 %backward_near.1 = (bf16[64,768]{1,0:T(8,128)(2,1)S(1)}, bf16[64,768]{1,0:T(8,128)(2,1)S(1)}, bf16[64,768]{1,0:T(8,128)(2,1)S(1)}, bf16[64,768]{1,0:T(8,128)(2,1...) custom-call(bf16[3,1024,768]{2,1,0:T(8,128)(2,1)S(1)} %bitcast.15, ...), custom_call_target="tpu_custom_call" | custom-call | flops 10000000000 | bytes 2097152 | tf_op jit(solution)/shard_map/backward_near/pallas_call | solution.py:339
  75.4 2.0 %collective-permute-start.30 = (bf16[64,768]{1,0:T(8,128)(2,1)S(1)}, bf16[64,768]{1,0:T(8,128)(2,1)S(1)}, u32[]{:S(2)}, u32[]{:S(2)}) collective-permute-start(bf16[64,768]{1,0:T(8,128)(2,1)S(1)} %get-tuple-element.124), channel_id=1, source_target_pairs={{0,2},{2,0},{4,6},{6,4},{8,10},{10,8},{12,14},{14,12},{1,3},{3,1},... | collective-permute-start | bytes 294920 | tf_op jit(solution)/shard_map/ppermute | solution.py:357
  77.4 0.8 collective-permute-start.31
  78.3 1.2 %collective-permute-start.32 = (bf16[64,768]{1,0:T(8,128)(2,1)S(1)}, bf16[64,768]{1,0:T(8,128)(2,1)S(1)}, u32[]{:S(2)}, u32[]{:S(2)}) collective-permute-start(bf16[64,768]{1,0:T(8,128)(2,1)S(1)} %get-tuple-element.126), channel_id=1, source_target_pairs={{0,6},{2,4},{4,2},{6,0},{8,14},{10,12},{12,10},{14,8},{1,7},{3,5},... | collective-permute-start | bytes 294920 | tf_op jit(solution)/shard_map/ppermute | solution.py:357
  79.5 3.9 %weight_near.1 = (bf16[3,1024,768]{2,1,0:T(8,128)(2,1)}, f32[8,128]{1,0:T(8,128)S(1)}) custom-call(bf16[3,1024,768]{2,1,0:T(8,128)(2,1)S(1)} %get-tuple-element.127.refs_0_, bf16[7,256,256]{2,1,0:T(8,128)(2,1)S(1)} %get-tuple-element.76.refs_6_.refs_1_, bf16[7,256,256]{2,1,0:T(8,128)(2,1)S(1)} %collective-permute-done.6.refs_0_.refs_8_.refs_2_, ...), custom_call_target="tpu_custom_call" | custom-call | flops 30000001024 | bytes 2097152 | tf_op jit(solution)/shard_map/weight_near/pallas_call | solution.py:339
  83.4 1.2 %collective-permute-done.32.refs_5_ = bf16[64,768]{1,0:T(8,128)(2,1)S(1)} collective-permute-done((bf16[64,768]{1,0:T(8,128)(2,1)S(1)}, bf16[64,768]{1,0:T(8,128)(2,1)S(1)}, u32[]{:S(2)}, u32[]{:S(2)}) %collective-permute-start.32) | collective-permute-done | bytes 98336 | tf_op jit(solution)/shard_map/ppermute | solution.py:357
  84.7 0.9 %combine_gradients.1 = bf16[128,768]{1,0:T(8,128)(2,1)} custom-call(bf16[2,256,128]{2,1,0:T(8,128)(2,1)S(1)} %get-tuple-element.70.refs_1_.refs_0_, bf16[128,768]{1,0:T(8,128)(2,1)S(1)} %get-tuple-element.122.refs_1_, bf16[64,768]{1,0:T(8,128)(2,1)S(1)} %get-tuple-element.123.refs_2_, bf16[64,768]{1,0:T(8,128)(2,1)S(1)} %collective-permute-done.30.refs_3_, ...), custom_call_target="tpu_custom_call" | custom-call | flops 30000001024 | bytes 2097152 | tf_op jit(solution)/shard_map/combine_gradients/pallas_call | solution.py:339
  (49 shorter events, 1.2 us)
Async XLA Ops:
  0.6 19.8 %collective-permute-start.2 = (bf16[3,1024,768]{2,1,0:T(8,128)(2,1)}, bf16[3,1024,768]{2,1,0:T(8,128)(2,1)S(1)}, u32[]{:S(2)}, u32[]{:S(2)}) collective-permute-start(bf16[3,1024,768]{2,1,0:T(8,128)(2,1)} %bitcast.9), channel_id=1, source_target_pairs={{0,1},{1,0},{2,3},{3,2},{4,5},{5,4},{6,7},{7,6},{8,9},{9,8},{10,11... | collective-permute-start | bytes 14155784 | tf_op jit(solution)/shard_map/ppermute | solution.py:365
  1.1 15.4 %collective-permute-start.1 = (bf16[128,768]{1,0:T(8,128)(2,1)}, bf16[128,768]{1,0:T(8,128)(2,1)S(1)}, u32[]{:S(2)}, u32[]{:S(2)}) collective-permute-start(bf16[128,768]{1,0:T(8,128)(2,1)} %refs_2_.3), channel_id=1, source_target_pairs={{0,8},{2,10},{4,12},{6,14},{8,0},{10,2},{12,4},{14,6},{1,9},{3,11}... | collective-permute-start | bytes 589832 | tf_op jit(solution)/shard_map/ppermute | solution.py:362
  4.8 1.0 %copy-start = (bf16[128,768]{1,0:T(8,128)(2,1)S(1)}, bf16[128,768]{1,0:T(8,128)(2,1)}, u32[]{:S(2)}) copy-start(bf16[128,768]{1,0:T(8,128)(2,1)} %refs_2_.3) | copy-start | bytes 589828
  5.8 0.7 copy-start.2
  6.5 0.7 copy-start.3
  7.5 7.4 %collective-permute-start = (f32[8,128]{1,0:T(8,128)S(1)}, f32[8,128]{1,0:T(8,128)S(1)}, u32[]{:S(2)}, u32[]{:S(2)}) collective-permute-start(f32[8,128]{1,0:T(8,128)S(1)} %get-tuple-element.69.refs_0_), channel_id=1, source_target_pairs={{0,8},{2,10},{4,12},{6,14},{8,0},{10,2},{12,4},{14,6},{1,9},{3,11}... | collective-permute-start | bytes 12296 | tf_op jit(solution)/shard_map/ppermute | solution.py:362
  7.6 10.1 %collective-permute-start.3 = (bf16[64,768]{1,0:T(8,128)(2,1)S(1)}, bf16[64,768]{1,0:T(8,128)(2,1)S(1)}, u32[]{:S(2)}, u32[]{:S(2)}) collective-permute-start(bf16[64,768]{1,0:T(8,128)(2,1)S(1)} %get-tuple-element.73), channel_id=1, source_target_pairs={{0,6},{2,4},{4,2},{6,0},{8,14},{10,12},{12,10},{14,8},{1,7},{3,5},... | collective-permute-start | bytes 294920 | tf_op jit(solution)/shard_map/ppermute | solution.py:357
  10.4 8.4 %collective-permute-start.4 = (bf16[64,768]{1,0:T(8,128)(2,1)S(1)}, bf16[64,768]{1,0:T(8,128)(2,1)S(1)}, u32[]{:S(2)}, u32[]{:S(2)}) collective-permute-start(bf16[64,768]{1,0:T(8,128)(2,1)S(1)} %get-tuple-element.74), channel_id=1, source_target_pairs={{0,4},{2,6},{4,0},{6,2},{8,12},{10,14},{12,8},{14,10},{1,5},{3,7},... | collective-permute-start | bytes 294920 | tf_op jit(solution)/shard_map/ppermute | solution.py:357
  14.9 5.5 %slice-start = ((s8[4718592]{0:T(1024)(128)(4,1)}), s8[4194304]{0:T(1024)(128)(4,1)S(1)}, s32[]{:S(2)}) async-start(s8[4718592]{0:T(1024)(128)(4,1)} %bitcast.10), calls=%async_computation | async-start | bytes 8388608
  14.9 5.5 %slice-start.1 = ((s8[4718592]{0:T(1024)(128)(4,1)}), s8[524288]{0:T(1024)(128)(4,1)S(1)}, s32[]{:S(2)}) async-start(s8[4718592]{0:T(1024)(128)(4,1)} %bitcast.10), calls=%async_computation.1 | async-start | bytes 1048576
  14.9 5.5 %collective-permute-start.5 = (bf16[64,768]{1,0:T(8,128)(2,1)S(1)}, bf16[64,768]{1,0:T(8,128)(2,1)S(1)}, u32[]{:S(2)}, u32[]{:S(2)}) collective-permute-start(bf16[64,768]{1,0:T(8,128)(2,1)S(1)} %get-tuple-element.75), channel_id=1, source_target_pairs={{0,2},{2,0},{4,6},{6,4},{8,10},{10,8},{12,14},{14,12},{1,3},{3,1},... | collective-permute-start | bytes 294920 | tf_op jit(solution)/shard_map/ppermute | solution.py:357
  16.9 11.0 %collective-permute-start.10 = (bf16[64,768]{1,0:T(8,128)(2,1)S(1)}, bf16[64,768]{1,0:T(8,128)(2,1)S(1)}, u32[]{:S(2)}, u32[]{:S(2)}) collective-permute-start(bf16[64,768]{1,0:T(8,128)(2,1)S(1)} %get-tuple-element.82), channel_id=1, source_target_pairs={{0,6},{2,4},{4,2},{6,0},{8,14},{10,12},{12,10},{14,8},{1,7},{3,5},... | collective-permute-start | bytes 294920 | tf_op jit(solution)/shard_map/ppermute | solution.py:357
  17.7 10.2 %collective-permute-start.11 = (bf16[64,768]{1,0:T(8,128)(2,1)S(1)}, bf16[64,768]{1,0:T(8,128)(2,1)S(1)}, u32[]{:S(2)}, u32[]{:S(2)}) collective-permute-start(bf16[64,768]{1,0:T(8,128)(2,1)S(1)} %get-tuple-element.83), channel_id=1, source_target_pairs={{0,4},{2,6},{4,0},{6,2},{8,12},{10,14},{12,8},{14,10},{1,5},{3,7},... | collective-permute-start | bytes 294920 | tf_op jit(solution)/shard_map/ppermute | solution.py:357
  18.9 9.1 %collective-permute-start.12 = (bf16[64,768]{1,0:T(8,128)(2,1)S(1)}, bf16[64,768]{1,0:T(8,128)(2,1)S(1)}, u32[]{:S(2)}, u32[]{:S(2)}) collective-permute-start(bf16[64,768]{1,0:T(8,128)(2,1)S(1)} %get-tuple-element.84), channel_id=1, source_target_pairs={{0,2},{2,0},{4,6},{6,4},{8,10},{10,8},{12,14},{14,12},{1,3},{3,1},... | collective-permute-start | bytes 294920 | tf_op jit(solution)/shard_map/ppermute | solution.py:357
  23.9 7.5 %collective-permute-start.7 = (bf16[64,768]{1,0:T(8,128)(2,1)S(1)}, bf16[64,768]{1,0:T(8,128)(2,1)S(1)}, u32[]{:S(2)}, u32[]{:S(2)}) collective-permute-start(bf16[64,768]{1,0:T(8,128)(2,1)S(1)} %get-tuple-element.78), channel_id=1, source_target_pairs={{0,6},{2,4},{4,2},{6,0},{8,14},{10,12},{12,10},{14,8},{1,7},{3,5},... | collective-permute-start | bytes 294920 | tf_op jit(solution)/shard_map/ppermute | solution.py:357
  26.6 5.0 %collective-permute-start.8 = (bf16[64,768]{1,0:T(8,128)(2,1)S(1)}, bf16[64,768]{1,0:T(8,128)(2,1)S(1)}, u32[]{:S(2)}, u32[]{:S(2)}) collective-permute-start(bf16[64,768]{1,0:T(8,128)(2,1)S(1)} %get-tuple-element.79), channel_id=1, source_target_pairs={{0,4},{2,6},{4,0},{6,2},{8,12},{10,14},{12,8},{14,10},{1,5},{3,7},... | collective-permute-start | bytes 294920 | tf_op jit(solution)/shard_map/ppermute | solution.py:357
  27.9 4.6 %collective-permute-start.9 = (bf16[64,768]{1,0:T(8,128)(2,1)S(1)}, bf16[64,768]{1,0:T(8,128)(2,1)S(1)}, u32[]{:S(2)}, u32[]{:S(2)}) collective-permute-start(bf16[64,768]{1,0:T(8,128)(2,1)S(1)} %get-tuple-element.80), channel_id=1, source_target_pairs={{0,2},{2,0},{4,6},{6,4},{8,10},{10,8},{12,14},{14,12},{1,3},{3,1},... | collective-permute-start | bytes 294920 | tf_op jit(solution)/shard_map/ppermute | solution.py:357
  27.9 6.8 %collective-permute-start.6 = (bf16[7,256,256]{2,1,0:T(8,128)(2,1)S(1)}, bf16[7,256,256]{2,1,0:T(8,128)(2,1)S(1)}, u32[]{:S(2)}, u32[]{:S(2)}) collective-permute-start(bf16[7,256,256]{2,1,0:T(8,128)(2,1)S(1)} %get-tuple-element.76.refs_6_.refs_1_), channel_id=1, source_target_pairs={{0,1},{1,0},{2,3},{3,2},{4,5},{5,4},{6,7},{7,6},{8,9},{9,8},{10,11... | collective-permute-start | bytes 2752520 | tf_op jit(solution)/shard_map/ppermute | solution.py:365
  28.0 4.5 %copy-start.1 = (bf16[128,768]{1,0:T(8,128)(2,1)S(1)}, bf16[128,768]{1,0:T(8,128)(2,1)}, u32[]{:S(2)}) copy-start(bf16[128,768]{1,0:T(8,128)(2,1)} %refs_2_.5) | copy-start | bytes 589828
  32.9 11.5 %collective-permute-start.13 = (bf16[128,768]{1,0:T(8,128)(2,1)S(1)}, bf16[128,768]{1,0:T(8,128)(2,1)S(1)}, u32[]{:S(2)}, u32[]{:S(2)}) collective-permute-start(bf16[128,768]{1,0:T(8,128)(2,1)S(1)} %get-tuple-element.94), channel_id=1, source_target_pairs={{0,8},{2,10},{4,12},{6,14},{8,0},{10,2},{12,4},{14,6},{1,9},{3,11}... | collective-permute-start | bytes 589832 | tf_op jit(solution)/shard_map/ppermute | solution.py:362
  34.7 9.7 %collective-permute-start.17 = (bf16[7,256,256]{2,1,0:T(8,128)(2,1)S(1)}, bf16[7,256,256]{2,1,0:T(8,128)(2,1)S(1)}, u32[]{:S(2)}, u32[]{:S(2)}) collective-permute-start(bf16[7,256,256]{2,1,0:T(8,128)(2,1)S(1)} %get-tuple-element.98.refs_0_), channel_id=1, source_target_pairs={{0,1},{1,0},{2,3},{3,2},{4,5},{5,4},{6,7},{7,6},{8,9},{9,8},{10,11... | collective-permute-start | bytes 2752520 | tf_op jit(solution)/shard_map/ppermute | solution.py:365
  34.7 9.7 %collective-permute-start.14 = (bf16[64,768]{1,0:T(8,128)(2,1)S(1)}, bf16[64,768]{1,0:T(8,128)(2,1)S(1)}, u32[]{:S(2)}, u32[]{:S(2)}) collective-permute-start(bf16[64,768]{1,0:T(8,128)(2,1)S(1)} %get-tuple-element.95), channel_id=1, source_target_pairs={{0,6},{2,4},{4,2},{6,0},{8,14},{10,12},{12,10},{14,8},{1,7},{3,5},... | collective-permute-start | bytes 294920 | tf_op jit(solution)/shard_map/ppermute | solution.py:357
  37.3 8.6 %collective-permute-start.15 = (bf16[64,768]{1,0:T(8,128)(2,1)S(1)}, bf16[64,768]{1,0:T(8,128)(2,1)S(1)}, u32[]{:S(2)}, u32[]{:S(2)}) collective-permute-start(bf16[64,768]{1,0:T(8,128)(2,1)S(1)} %get-tuple-element.96), channel_id=1, source_target_pairs={{0,4},{2,6},{4,0},{6,2},{8,12},{10,14},{12,8},{14,10},{1,5},{3,7},... | collective-permute-start | bytes 294920 | tf_op jit(solution)/shard_map/ppermute | solution.py:357
  37.3 8.6 %collective-permute-start.16 = (bf16[64,768]{1,0:T(8,128)(2,1)S(1)}, bf16[64,768]{1,0:T(8,128)(2,1)S(1)}, u32[]{:S(2)}, u32[]{:S(2)}) collective-permute-start(bf16[64,768]{1,0:T(8,128)(2,1)S(1)} %get-tuple-element.97), channel_id=1, source_target_pairs={{0,2},{2,0},{4,6},{6,4},{8,10},{10,8},{12,14},{14,12},{1,3},{3,1},... | collective-permute-start | bytes 294920 | tf_op jit(solution)/shard_map/ppermute | solution.py:357
  46.5 6.4 %collective-permute-start.19 = (bf16[64,768]{1,0:T(8,128)(2,1)S(1)}, bf16[64,768]{1,0:T(8,128)(2,1)S(1)}, u32[]{:S(2)}, u32[]{:S(2)}) collective-permute-start(bf16[64,768]{1,0:T(8,128)(2,1)S(1)} %get-tuple-element.103), channel_id=1, source_target_pairs={{0,6},{2,4},{4,2},{6,0},{8,14},{10,12},{12,10},{14,8},{1,7},{3,5},... | collective-permute-start | bytes 294920 | tf_op jit(solution)/shard_map/ppermute | solution.py:357
  47.3 7.9 %collective-permute-start.20 = (bf16[64,768]{1,0:T(8,128)(2,1)S(1)}, bf16[64,768]{1,0:T(8,128)(2,1)S(1)}, u32[]{:S(2)}, u32[]{:S(2)}) collective-permute-start(bf16[64,768]{1,0:T(8,128)(2,1)S(1)} %get-tuple-element.104), channel_id=1, source_target_pairs={{0,4},{2,6},{4,0},{6,2},{8,12},{10,14},{12,8},{14,10},{1,5},{3,7},... | collective-permute-start | bytes 294920 | tf_op jit(solution)/shard_map/ppermute | solution.py:357
  49.2 6.0 %collective-permute-start.21 = (bf16[64,768]{1,0:T(8,128)(2,1)S(1)}, bf16[64,768]{1,0:T(8,128)(2,1)S(1)}, u32[]{:S(2)}, u32[]{:S(2)}) collective-permute-start(bf16[64,768]{1,0:T(8,128)(2,1)S(1)} %get-tuple-element.105), channel_id=1, source_target_pairs={{0,2},{2,0},{4,6},{6,4},{8,10},{10,8},{12,14},{14,12},{1,3},{3,1},... | collective-permute-start | bytes 294920 | tf_op jit(solution)/shard_map/ppermute | solution.py:357
  50.1 12.5 %collective-permute-start.18 = (bf16[144,768]{1,0:T(8,128)(2,1)S(1)}, bf16[144,768]{1,0:T(8,128)(2,1)S(1)}, u32[]{:S(2)}, u32[]{:S(2)}) collective-permute-start(bf16[144,768]{1,0:T(8,128)(2,1)S(1)} %get-tuple-element.99), channel_id=1, source_target_pairs={{0,8},{2,10},{4,12},{6,14},{8,0},{10,2},{12,4},{14,6},{1,9},{3,11}... | collective-permute-start | bytes 663560 | tf_op jit(solution)/shard_map/ppermute | solution.py:362
  58.9 10.0 %collective-permute-start.29 = (bf16[11,256,256]{2,1,0:T(8,128)(2,1)S(1)}, bf16[11,256,256]{2,1,0:T(8,128)(2,1)S(1)}, u32[]{:S(2)}, u32[]{:S(2)}) collective-permute-start(bf16[11,256,256]{2,1,0:T(8,128)(2,1)S(1)} %get-tuple-element.118.refs_2_), channel_id=1, source_target_pairs={{0,1},{1,0},{2,3},{3,2},{4,5},{5,4},{6,7},{7,6},{8,9},{9,8},{10,11... | collective-permute-start | bytes 4325384 | tf_op jit(solution)/shard_map/ppermute | solution.py:365
  59.0 6.6 %collective-permute-start.22 = (bf16[64,768]{1,0:T(8,128)(2,1)S(1)}, bf16[64,768]{1,0:T(8,128)(2,1)S(1)}, u32[]{:S(2)}, u32[]{:S(2)}) collective-permute-start(bf16[64,768]{1,0:T(8,128)(2,1)S(1)} %get-tuple-element.109), channel_id=1, source_target_pairs={{0,6},{2,4},{4,2},{6,0},{8,14},{10,12},{12,10},{14,8},{1,7},{3,5},... | collective-permute-start | bytes 294920 | tf_op jit(solution)/shard_map/ppermute | solution.py:357
  59.1 7.2 %collective-permute-start.23 = (bf16[64,768]{1,0:T(8,128)(2,1)S(1)}, bf16[64,768]{1,0:T(8,128)(2,1)S(1)}, u32[]{:S(2)}, u32[]{:S(2)}) collective-permute-start(bf16[64,768]{1,0:T(8,128)(2,1)S(1)} %get-tuple-element.110), channel_id=1, source_target_pairs={{0,4},{2,6},{4,0},{6,2},{8,12},{10,14},{12,8},{14,10},{1,5},{3,7},... | collective-permute-start | bytes 294920 | tf_op jit(solution)/shard_map/ppermute | solution.py:357
  60.6 7.5 %collective-permute-start.24 = (bf16[64,768]{1,0:T(8,128)(2,1)S(1)}, bf16[64,768]{1,0:T(8,128)(2,1)S(1)}, u32[]{:S(2)}, u32[]{:S(2)}) collective-permute-start(bf16[64,768]{1,0:T(8,128)(2,1)S(1)} %get-tuple-element.111), channel_id=1, source_target_pairs={{0,2},{2,0},{4,6},{6,4},{8,10},{10,8},{12,14},{14,12},{1,3},{3,1},... | collective-permute-start | bytes 294920 | tf_op jit(solution)/shard_map/ppermute | solution.py:357
  63.7 7.9 %collective-permute-start.26 = (bf16[64,768]{1,0:T(8,128)(2,1)S(1)}, bf16[64,768]{1,0:T(8,128)(2,1)S(1)}, u32[]{:S(2)}, u32[]{:S(2)}) collective-permute-start(bf16[64,768]{1,0:T(8,128)(2,1)S(1)} %get-tuple-element.115), channel_id=1, source_target_pairs={{0,6},{2,4},{4,2},{6,0},{8,14},{10,12},{12,10},{14,8},{1,7},{3,5},... | collective-permute-start | bytes 294920 | tf_op jit(solution)/shard_map/ppermute | solution.py:357
  65.6 6.0 %collective-permute-start.27 = (bf16[64,768]{1,0:T(8,128)(2,1)S(1)}, bf16[64,768]{1,0:T(8,128)(2,1)S(1)}, u32[]{:S(2)}, u32[]{:S(2)}) collective-permute-start(bf16[64,768]{1,0:T(8,128)(2,1)S(1)} %get-tuple-element.116), channel_id=1, source_target_pairs={{0,4},{2,6},{4,0},{6,2},{8,12},{10,14},{12,8},{14,10},{1,5},{3,7},... | collective-permute-start | bytes 294920 | tf_op jit(solution)/shard_map/ppermute | solution.py:357
  66.3 5.3 %collective-permute-start.28 = (bf16[64,768]{1,0:T(8,128)(2,1)S(1)}, bf16[64,768]{1,0:T(8,128)(2,1)S(1)}, u32[]{:S(2)}, u32[]{:S(2)}) collective-permute-start(bf16[64,768]{1,0:T(8,128)(2,1)S(1)} %get-tuple-element.117), channel_id=1, source_target_pairs={{0,2},{2,0},{4,6},{6,4},{8,10},{10,8},{12,14},{14,12},{1,3},{3,1},... | collective-permute-start | bytes 294920 | tf_op jit(solution)/shard_map/ppermute | solution.py:357
  68.5 11.1 %collective-permute-start.25 = (bf16[128,768]{1,0:T(8,128)(2,1)S(1)}, bf16[128,768]{1,0:T(8,128)(2,1)S(1)}, u32[]{:S(2)}, u32[]{:S(2)}) collective-permute-start(bf16[128,768]{1,0:T(8,128)(2,1)S(1)} %far_back.1.refs_6_.refs_8_), channel_id=1, source_target_pairs={{0,8},{2,10},{4,12},{6,14},{8,0},{10,2},{12,4},{14,6},{1,9},{3,11}... | collective-permute-start | bytes 589832 | tf_op jit(solution)/shard_map/ppermute | solution.py:362
  75.4 4.2 %collective-permute-start.33 = (bf16[11,256,256]{2,1,0:T(8,128)(2,1)S(1)}, bf16[11,256,256]{2,1,0:T(8,128)(2,1)S(1)}, u32[]{:S(2)}, u32[]{:S(2)}) collective-permute-start(bf16[11,256,256]{2,1,0:T(8,128)(2,1)S(1)} %get-tuple-element.128.refs_3_), channel_id=1, source_target_pairs={{0,1},{1,0},{2,3},{3,2},{4,5},{5,4},{6,7},{7,6},{8,9},{9,8},{10,11... | collective-permute-start | bytes 4325384 | tf_op jit(solution)/shard_map/ppermute | solution.py:365
  75.4 8.0 %collective-permute-start.30 = (bf16[64,768]{1,0:T(8,128)(2,1)S(1)}, bf16[64,768]{1,0:T(8,128)(2,1)S(1)}, u32[]{:S(2)}, u32[]{:S(2)}) collective-permute-start(bf16[64,768]{1,0:T(8,128)(2,1)S(1)} %get-tuple-element.124), channel_id=1, source_target_pairs={{0,2},{2,0},{4,6},{6,4},{8,10},{10,8},{12,14},{14,12},{1,3},{3,1},... | collective-permute-start | bytes 294920 | tf_op jit(solution)/shard_map/ppermute | solution.py:357
  77.4 6.0 %collective-permute-start.31 = (bf16[64,768]{1,0:T(8,128)(2,1)S(1)}, bf16[64,768]{1,0:T(8,128)(2,1)S(1)}, u32[]{:S(2)}, u32[]{:S(2)}) collective-permute-start(bf16[64,768]{1,0:T(8,128)(2,1)S(1)} %get-tuple-element.125), channel_id=1, source_target_pairs={{0,4},{2,6},{4,0},{6,2},{8,12},{10,14},{12,8},{14,10},{1,5},{3,7},... | collective-permute-start | bytes 294920 | tf_op jit(solution)/shard_map/ppermute | solution.py:357
  78.3 6.4 %collective-permute-start.32 = (bf16[64,768]{1,0:T(8,128)(2,1)S(1)}, bf16[64,768]{1,0:T(8,128)(2,1)S(1)}, u32[]{:S(2)}, u32[]{:S(2)}) collective-permute-start(bf16[64,768]{1,0:T(8,128)(2,1)S(1)} %get-tuple-element.126), channel_id=1, source_target_pairs={{0,6},{2,4},{4,2},{6,0},{8,14},{10,12},{12,10},{14,8},{1,7},{3,5},... | collective-permute-start | bytes 294920 | tf_op jit(solution)/shard_map/ppermute | solution.py:357
